TPU v7x, 32 devices: a whole 2x2x4 slice. The times are simulated.
32 devices in a mesh: parts: 2 (over x), rep: 8 (over z, y), tp: 2 (over core).
Axes of the slice: x: 2, y: 2, z: 4, core: 2. Of those that a mesh axis runs over, the one named last changes fastest.
Arguments:
- tokens: bfloat16 [4096, 8192], P(('parts', 'rep'), 'tp'), parts along dimension 0, may hold values from -6 to 6
- base_weight: bfloat16 [8192, 1024], P('tp'), may hold values from -0.0625 to 0.0625
- shrink_panels: bfloat16 [32, 8192, 64], P('rep', 'tp'), may hold values from -0.0625 to 0.0625
- expand_panels: bfloat16 [32, 64, 1024], P('rep'), may hold values from -0.75 to 0.75
- adapter_home: int32 [32], replicated, may hold values from 0 to 31, as said below
- fetch_list: int32 [8, 8], replicated, may hold values from 0 to 31, as said below
- seg_len: int32 [16, 8], P(('parts', 'rep')), parts along dimension 0, may hold values from 1 to 64, 256 in all within a row
Outputs:
- projected: bfloat16 [4096, 1024], P(('parts', 'rep'), 'tp'), parts along dimension 0
There are 2 independent parts, one for each index of `parts`. A program takes and returns all parts, laid end to end along the dimension named above; an argument that names none is the same for every part. Nothing has to cross between parts.
Inputs may be any that keep to these rules, and one draw needn't show every extreme that they name: `adapter_home`: a permutation: every adapter has its own storage position. `fetch_list`: each row names 8 different adapters; at most 1 adapters of one row have storage positions with the same value of position // 4, and every row has such a group of exactly 1. `seg_len`: each row sums to 256 and holds one entry of exactly 64.
All inputs are finite; a program needn't handle non-finite values.
Results may differ from a plain program's by a relative error of at most 0.001.
Values may be sent and summed in bfloat16 or wider, within the bound.
No kernel may reach another device: no remote copies, remote signals or barrier semaphores. Data moves between devices by JAX's collectives and lax.ppermute only.
A program may use at most 128 MiB of HBM per device.

v0:
```python
import jax
import jax.numpy as jnp
from jax import lax
from jax.sharding import PartitionSpec as P

adapter_scale = 2.0


def list_tables(adapter_home, fetch_list, per_home):
    adapter_count = adapter_home.shape[0]
    matches = fetch_list[:, :, None] == jnp.arange(adapter_count, dtype=jnp.int32)[None, None, :]
    stored = jnp.sum(jnp.where(matches, adapter_home[None, None, :], 0), axis=2)
    owners = stored // per_home
    within = stored % per_home
    ordinal = jnp.arange(fetch_list.shape[1], dtype=jnp.int32)
    same_home = (owners[:, :, None] == owners[:, None, :]) & (
        ordinal[None, None, :] < ordinal[None, :, None]
    )
    ranking = jnp.sum(same_home.astype(jnp.int32), axis=2)
    return (owners, within, ranking)


def served_slots(owners, within, ranking, my_index, per_peer):
    copies = jnp.arange(per_peer, dtype=jnp.int32)
    chosen = (owners[:, None, :] == my_index) & (ranking[:, None, :] == copies[None, :, None])
    present = jnp.any(chosen, axis=2)
    local_slot = jnp.sum(jnp.where(chosen, within[:, None, :], 0), axis=2)
    return (local_slot, present)


def pack_panels(panels, local_slot, present):
    picked = jnp.take(panels, local_slot.reshape(-1), axis=0)
    picked = jnp.where(present.reshape(-1)[:, None, None], picked, jnp.zeros((), panels.dtype))
    return picked.reshape(local_slot.shape + panels.shape[1:])


def on_device(tokens, base_weight, shrink_panels, expand_panels, adapter_home, fetch_list, seg_len):
    per_home = shrink_panels.shape[0]
    replicas = lax.axis_size("rep")
    listed_entries = fetch_list.shape[1]
    per_peer = (listed_entries + replicas - 1) // replicas
    slot_count = replicas * per_peer
    tok_count = tokens.shape[0]
    segment_largest = 2 * tok_count // replicas
    my_index = lax.axis_index("rep")
    owners, within, ranking = list_tables(adapter_home, fetch_list, per_home)
    my_owners = lax.dynamic_index_in_dim(owners, my_index, 0, keepdims=False)
    my_ranks = lax.dynamic_index_in_dim(ranking, my_index, 0, keepdims=False)
    entry_index = my_owners * per_peer + my_ranks
    local_slot, present = served_slots(owners, within, ranking, my_index, per_peer)
    lengths = seg_len[0]
    seg_ends = jnp.cumsum(lengths)
    starts = seg_ends - lengths
    padded = jnp.arange(segment_largest, dtype=jnp.int32)
    seg_index = jnp.minimum(starts[:, None] + padded[None, :], tok_count - 1)
    seg_valid = padded[None, :] < lengths[:, None]
    positions = jnp.arange(tok_count, dtype=jnp.int32)
    member = (positions[:, None] >= starts[None, :]) & (positions[:, None] < seg_ends[None, :])
    ordinal = jnp.arange(listed_entries, dtype=jnp.int32)
    tok_segment = jnp.sum(jnp.where(member, ordinal[None, :], 0), axis=1)
    tok_start = jnp.sum(jnp.where(member, starts[None, :], 0), axis=1)
    token_placement = tok_segment * segment_largest + positions - tok_start
    seg_tokens = jnp.take(tokens, seg_index.reshape(-1), axis=0).reshape(
        listed_entries, segment_largest, tokens.shape[1]
    )
    seg_tokens = jnp.where(seg_valid[:, :, None], seg_tokens, jnp.zeros((), tokens.dtype))
    column_count = expand_panels.shape[2] // lax.axis_size("tp")
    expand_part = lax.dynamic_slice_in_dim(
        expand_panels, lax.axis_index("tp") * column_count, column_count, 2
    )
    shrink_send = pack_panels(shrink_panels, local_slot, present)
    expand_send = pack_panels(expand_part, local_slot, present)
    shrink_recv, expand_recv = (
        lax.all_to_all(shrink_send, "rep", split_axis=0, concat_axis=0, tiled=True),
        lax.all_to_all(expand_send, "rep", split_axis=0, concat_axis=0, tiled=True),
    )
    shrink_cat = jnp.take(
        shrink_recv.reshape((slot_count,) + shrink_panels.shape[1:]), entry_index, axis=0
    )
    seg_shrink = jnp.einsum(
        "fpd,fdr->fpr", seg_tokens, shrink_cat, preferred_element_type=jnp.float32
    )
    expand_cat = jnp.take(
        expand_recv.reshape((slot_count,) + expand_part.shape[1:]), entry_index, axis=0
    )
    expand_wide = expand_cat.astype(jnp.float32)
    base_part = jnp.dot(tokens, base_weight, preferred_element_type=jnp.float32)
    shrink_full = lax.psum(seg_shrink, "tp")
    segment_adapter = jnp.einsum(
        "fpr,frc->fpc",
        shrink_full,
        expand_wide,
        precision=lax.Precision.HIGHEST,
        preferred_element_type=jnp.float32,
    )
    adapter_output = jnp.take(
        segment_adapter.reshape(listed_entries * segment_largest, segment_adapter.shape[2]),
        token_placement,
        axis=0,
    )
    base_output = lax.psum_scatter(base_part, "tp", scatter_dimension=1, tiled=True)
    summed_output = base_output + adapter_scale * adapter_output
    return summed_output.astype(jnp.bfloat16)


def solution(mesh):
    return jax.shard_map(
        on_device,
        mesh=mesh,
        in_specs=(
            P(("parts", "rep"), "tp"),
            P("tp", None),
            P("rep", "tp", None),
            P("rep", None, None),
            P(),
            P(),
            P(("parts", "rep"), None),
        ),
        out_specs=P(("parts", "rep"), "tp"),
        check_vma=False,
    )
```

profile of v0, /device:TPU:0, one launch (start us, length us, event | category | flops | bytes accessed | tf_op | source)
XLA Modules:
  0.0 169.1 jit_solution(17417847654108839626)
XLA Ops:
  6.5 0.0 copy-start
  6.5 1.1 select_reduce_fusion
  7.7 0.3 convert_reduce_fusion
  8.0 0.1 fusion.29
  8.1 0.1 fusion.18
  8.3 4.4 %gather_fusion.1 = bf16[8,4096,64]{1,2,0:T(8,128)(2,1)} fusion(bf16[4,4096,64]{1,2,0:T(8,128)(2,1)} %param.9, s32[1024]{0:T(1024)S(1)} %pad_clamp_fusion.2), kind=kCustom, calls=%fused_computation.1 | custom fusion | bytes 8388640 | tf_op jit(solution)/shard_map/jit(_take)/gather | solution.py:32
  12.6 4.7 %fusion = bf16[8,1,4096,64]{2,3,1,0:T(8,128)(2,1)} fusion(bf16[8,4096,64]{1,2,0:T(8,128)(2,1)} %gather_fusion.1, pred[8]{0:T(512)(128)(4,1)S(1)} %compare_and_fusion.2, pred[8]{0:T(512)(128)(4,1)S(1)} %get-tuple-element.9), kind=kLoop, calls=%fused_computation.7 | loop fusion | flops 4194304 | bytes 8388624 | tf_op jit(solution)/shard_map/jit(_where)/select_n | solution.py:33
  17.3 7.4 %all-to-all-start = ((bf16[8,1,4096,64]{2,3,1,0:T(8,128)(2,1)}), bf16[8,1,4096,64]{2,3,1,0:T(8,128)(2,1)}, u32[]{:S(2)}, u32[]{:S(2)}) async-start(bf16[8,1,4096,64]{2,3,1,0:T(8,128)(2,1)} %fusion), calls=%async_computation.1 | async-start | bytes 8388608 | tf_op jit(solution)/shard_map/all_to_all | solution.py:74
  24.7 0.0 all-reduce.2.cloned.1.call-start
  24.8 0.0 copy-done.2
  24.8 0.2 reduce-window.4
  25.0 0.1 add_minimum_fusion
  25.1 0.1 min.22
  25.2 4.4 %gather_fusion = bf16[512,4096]{1,0:T(8,128)(2,1)} fusion(bf16[256,4096]{1,0:T(8,128)(2,1)S(1)} %copy-done, s32[1024]{0:T(1024)S(1)} %pad_clamp_fusion.3), kind=kCustom, calls=%fused_computation | custom fusion | bytes 8390656 | tf_op jit(solution)/shard_map/jit(_take)/gather | solution.py:63
  29.6 0.1 iota_compare_fusion.4
  29.7 88.3 %all-to-all-done = bf16[8,1,4096,64]{2,3,1,0:T(8,128)(2,1)} async-done(((bf16[8,1,4096,64]{2,3,1,0:T(8,128)(2,1)}), bf16[8,1,4096,64]{2,3,1,0:T(8,128)(2,1)}, u32[]{:S(2)}, u32[]{:S(2)}) %all-to-all-start) | async-done | bytes 4194336 | tf_op jit(solution)/shard_map/all_to_all | solution.py:74
  118.0 5.0 %gather_fusion.2 = bf16[8,4096,64]{1,2,0:T(8,128)(2,1)} fusion(bf16[8,4096,64]{1,2,0:T(8,128)(2,1)} %bitcast.11, s32[1024]{0:T(1024)S(1)} %pad_clamp_fusion.1), kind=kCustom, calls=%fused_computation.2 | custom fusion | bytes 8388640 | tf_op jit(solution)/shard_map/jit(_take)/gather | solution.py:77
  123.0 5.5 %fusion.1 = f32[8,64,64]{2,1,0:T(8,128)} fusion(bf16[8,4096,64]{1,2,0:T(8,128)(2,1)} %gather_fusion.2, bf16[8,64,4096]{2,1,0:T(8,128)(2,1)} %bitcast.41, pred[8]{0:T(512)(128)(4,1)S(1)} %get-tuple-element.7, pred[8,64]{1,0:T(8,128)(4,1)S(1)} %get-tuple-element.12, pred[8,64]{1,0:T(8,128)(4,1)S(1)} %get-tuple-element.11), kind=kOutput, calls=%fused_computation.8 | convolution fusion | flops 274726912 | bytes 8520712 | tf_op jit(solution)/shard_map/fpd,fdr->fpr/dot_general | solution.py:80
  128.5 0.0 all-reduce.2.cloned.1.call-update
  128.5 0.0 copy-start.1
  128.6 0.0 reduce-scatter.2.cloned.1.call-start
  128.6 6.7 %fusion.30 = f32[256,1024]{1,0:T(8,128)} fusion(bf16[256,4096]{1,0:T(8,128)(2,1)S(1)} %copy-done, bf16[4096,1024]{1,0:T(8,128)(2,1)} %param.8), kind=kOutput, calls=%fused_computation.77 | convolution fusion | flops 2147483648 | bytes 11534336 | tf_op jit(solution)/shard_map/dot_general | solution.py:87
  135.3 0.0 reduce-scatter.2.cloned.1.call-update
  135.4 0.6 gather_fusion.3
  136.0 1.0 fusion.11
  137.0 3.6 %all-to-all-start.1 = ((bf16[8,1,64,512]{3,2,1,0:T(8,128)(2,1)}), bf16[8,1,64,512]{3,2,1,0:T(8,128)(2,1)S(1)}, u32[]{:S(2)}, u32[]{:S(2)}) async-start(bf16[8,1,64,512]{3,2,1,0:T(8,128)(2,1)} %fusion.11), calls=%async_computation.2 | async-start | bytes 1048576 | tf_op jit(solution)/shard_map/all_to_all | solution.py:75
  140.6 0.1 select_reduce_fusion.2
  140.7 14.5 %all-to-all-done.1 = bf16[8,1,64,512]{3,2,1,0:T(8,128)(2,1)S(1)} async-done(((bf16[8,1,64,512]{3,2,1,0:T(8,128)(2,1)}), bf16[8,1,64,512]{3,2,1,0:T(8,128)(2,1)S(1)}, u32[]{:S(2)}, u32[]{:S(2)}) %all-to-all-start.1) | async-done | bytes 524320 | tf_op jit(solution)/shard_map/all_to_all | solution.py:75
  155.3 1.4 gather_fusion.4
  156.7 1.8 %fusion.12 = f32[8,64,512]{2,1,0:T(8,128)S(1)} fusion(f32[8,64,64]{2,1,0:T(8,128)} %all-reduce.2.cloned.1.call-done, bf16[8,64,512]{2,1,0:T(8,128)(2,1)} %gather_fusion.4, pred[8]{0:T(512)(128)(4,1)S(1)} %get-tuple-element.7), kind=kOutput, calls=%fused_computation.21 | convolution fusion | flops 201588736 | bytes 1703944 | tf_op jit(solution)/shard_map/fpr,frc->fpc/dot_general | solution.py:89
  158.4 1.8 %gather_fusion.5 = f32[256,512]{1,0:T(8,128)} fusion(f32[512,512]{1,0:T(8,128)S(1)} %bitcast.40, s32[1024]{0:T(1024)S(1)} %pad_clamp_fusion), kind=kCustom, calls=%fused_computation.5 | custom fusion | bytes 1049600 | tf_op jit(solution)/shard_map/jit(_take)/gather | solution.py:96
  160.2 2.0 %add_convert_fusion = bf16[256,512]{1,0:T(8,128)(2,1)} fusion(f32[256,512]{1,0:T(8,128)} %reduce-scatter.2.cloned.1.call-done, f32[256,512]{1,0:T(8,128)} %gather_fusion.5, pred[256]{0:T(512)(128)(4,1)S(1)} %compare_and_fusion.4), kind=kLoop, calls=%fused_computation.20 | loop fusion | flops 524288 | bytes 1310976 | tf_op jit(solution)/shard_map/convert_element_type | solution.py:103
  (22 shorter events, 0.1 us)
Async XLA Ops:
  6.5 18.6 %copy-start = (bf16[256,4096]{1,0:T(8,128)(2,1)S(1)}, bf16[256,4096]{1,0:T(8,128)(2,1)}, u32[]{:S(2)}) copy-start(bf16[256,4096]{1,0:T(8,128)(2,1)} %param.7) | copy-start | bytes 6291460
  17.3 7.5 %copy-start.2 = (s32[1,8]{1,0:T(1,128)S(1)}, s32[1,8]{1,0:T(1,128)}, u32[]{:S(2)}) copy-start(s32[1,8]{1,0:T(1,128)} %param.13) | copy-start | bytes 100
  17.3 100.7 %all-to-all-start = ((bf16[8,1,4096,64]{2,3,1,0:T(8,128)(2,1)}), bf16[8,1,4096,64]{2,3,1,0:T(8,128)(2,1)}, u32[]{:S(2)}, u32[]{:S(2)}) async-start(bf16[8,1,4096,64]{2,3,1,0:T(8,128)(2,1)} %fusion), calls=%async_computation.1 | async-start | bytes 8388608 | tf_op jit(solution)/shard_map/all_to_all | solution.py:74
  24.7 131.9 %all-reduce.2.cloned.1.call-start = ((), (), s32[]{:S(2)}) async-start(), calls=%async_computation.4 | async-start | bytes 524288 | tf_op jit(solution)/shard_map/psum | solution.py:88
  128.5 6.8 %copy-start.1 = (bf16[4,64,1024]{2,1,0:T(8,128)(2,1)S(1)}, bf16[4,64,1024]{2,1,0:T(8,128)(2,1)}, u32[]{:S(2)}) copy-start(bf16[4,64,1024]{2,1,0:T(8,128)(2,1)} %param.10) | copy-start | bytes 1572868
  128.6 31.7 %reduce-scatter.2.cloned.1.call-start = ((), (), s32[]{:S(2)}) async-start(), calls=%async_computation.3 | async-start | bytes 1572864 | tf_op jit(solution)/shard_map/reduce_scatter | solution.py:101
  137.0 18.3 %all-to-all-start.1 = ((bf16[8,1,64,512]{3,2,1,0:T(8,128)(2,1)}), bf16[8,1,64,512]{3,2,1,0:T(8,128)(2,1)S(1)}, u32[]{:S(2)}, u32[]{:S(2)}) async-start(bf16[8,1,64,512]{3,2,1,0:T(8,128)(2,1)} %fusion.11), calls=%async_computation.2 | async-start | bytes 1048576 | tf_op jit(solution)/shard_map/all_to_all | solution.py:75
Sparse Core Ops, SparseCore 0:
  128.7 17.3 all-reduce.1
  148.3 9.6 reduce-scatter.1
where the time goes:
time: 170 us; the launch traced here: 169 us
  waiting for transfers between devices  103 us (61%)
  local copies, waits for them, and re-layouts  17.6 us (10%)
  matrix products  14 us (8%)
  between operations  13.6 us (8%)
  starting transfers between devices  11.1 us (7%)
  other arithmetic  9.87 us (6%)
    all_to_all x1, waiting for transfers between devices, on_device(): lax.all_to_all(shrink_send, 'rep', split_axis=0, concat_axis=0, tiled=True)  88.3 us
    all_to_all x1, waiting for transfers between devices, on_device(): lax.all_to_all(expand_send, 'rep', split_axis=0, concat_axis=0, tiled=True)  14.5 us
    all_to_all x1, starting transfers between devices, on_device(): lax.all_to_all(shrink_send, 'rep', split_axis=0, concat_axis=0, tiled=True)  7.41 us
    dot_general x1, matrix products, on_device(): base_part = jnp.dot(tokens, base_weight, preferred_element_type=jnp.float32)  6.75 us
    select_n x2, other arithmetic, pack_panels(): jnp.where(present.reshape(-1)[:, None, None], picked, jnp.zeros((), panel...  5.64 us
    dot_general x1, matrix products, on_device(): jnp.einsum('fpd,fdr->fpr', seg_tokens, shrink_cat, preferred_element_type...  5.51 us
    gather x1, local copies, waits for them, and re-layouts, on_device(): jnp.take(shrink_recv.reshape((slot_count,) + shrink_panels.shape[1:]), en...  4.98 us
    gather x2, local copies, waits for them, and re-layouts, pack_panels(): picked = jnp.take(panels, local_slot.reshape(-1), axis=0)  4.96 us
  transfers between devices with their start and end apart: 4, of which 2 were waited for; matrix products, arithmetic and copies ran while one was open for 11% of the time, Pallas kernels for 0%

commit v1 on v0

v1 whole, which is shorter than its diff:
```python
import functools
import jax
import jax.numpy as jnp
from jax import lax
from jax.experimental import pallas as pl
from jax.experimental.pallas import tpu as pltpu
from jax.sharding import PartitionSpec as P

adapter_scale = 2.0


def pack_kernel(steps, rows, home_ref, fetch_ref, shrink_ref, expand_ref, *refs):
    outs, sems = refs[: len(steps)], refs[len(steps)]
    me, part, half = lax.axis_index("rep"), lax.axis_index("parts"), lax.axis_index("tp")
    per_home, rank, depth = shrink_ref.shape
    listed = fetch_ref.shape[1]
    columns = outs[0].shape[1] - depth
    first = 0 if rows == rank else pl.multiple_of(part * rows, 16)
    left = pl.multiple_of(half * columns, 128)
    copies = []
    for at, step in enumerate(steps):
        peer = me ^ step

        def look(j, slot):
            position = home_ref[fetch_ref[peer, j]]
            return jnp.where(position // per_home == me, position % per_home, slot)

        slot = lax.fori_loop(0, listed, look, jnp.int32(0), unroll=listed <= 8)
        for n, (source, target) in enumerate(
            (
                (shrink_ref.at[slot, pl.ds(first, rows), :], outs[at].at[:, pl.ds(0, depth)]),
                (
                    expand_ref.at[slot, pl.ds(first, rows), pl.ds(left, columns)],
                    outs[at].at[:, pl.ds(depth, columns)],
                ),
            )
        ):
            copy = pltpu.make_async_copy(source, target, sems.at[at, n])
            copy.start()
            copies.append(copy)
    for copy in copies:
        copy.wait()


def pack(steps, rows, columns, adapter_home, fetch_list, panels, expand_panels):
    width = panels.shape[2] + columns
    return pl.pallas_call(
        functools.partial(pack_kernel, steps, rows),
        out_shape=[jax.ShapeDtypeStruct((rows, width), panels.dtype)] * len(steps),
        in_specs=[pl.BlockSpec(memory_space=pltpu.SMEM)] * 2 + [pl.BlockSpec(memory_space=pl.ANY)] * 2,
        out_specs=[pl.BlockSpec(memory_space=pl.ANY)] * len(steps),
        scratch_shapes=[pltpu.SemaphoreType.DMA((len(steps), 2))],
        cost_estimate=pl.CostEstimate(
            flops=0, bytes_accessed=4 * len(steps) * rows * width, transcendentals=0
        ),
    )(adapter_home, fetch_list, panels, expand_panels)


def on_device(tokens, base_weight, shrink_panels, expand_panels, adapter_home, fetch_list, seg_len):
    per_home, depth, rank = shrink_panels.shape
    replicas, parts, cores = lax.axis_size("rep"), lax.axis_size("parts"), lax.axis_size("tp")
    me = lax.axis_index("rep")
    tok_count = tokens.shape[0]
    columns = expand_panels.shape[2] // cores
    panels = jnp.swapaxes(shrink_panels, 1, 2)
    far = tuple(range(replicas // 2, replicas))
    near = tuple(range(1, replicas // 2))
    share = rank // parts

    args = (columns, adapter_home, fetch_list, panels, expand_panels)
    far_send = pack(far, share, *args)
    near_send = pack(near, rank, *args)
    own = pack((0,), rank, *args)[0]

    tokens, far_send, near_send, own = lax.optimization_barrier((tokens, far_send, near_send, own))

    def hop(x, step):
        return lax.ppermute(x, "rep", [(i, i ^ step) for i in range(replicas)])

    def across(x, shift):
        return lax.ppermute(x, "parts", [(i, (i + shift) % parts) for i in range(parts)])

    far_recv = [hop(x, step) for x, step in zip(far_send, far)]
    near_recv = [hop(x, step) for x, step in zip(near_send, near)]
    passed = [[across(x, shift) for x in far_recv] for shift in range(1, parts)]

    stored = jnp.take(adapter_home, lax.dynamic_index_in_dim(fetch_list, me, 0, keepdims=False))
    owners = stored // per_home
    lengths = seg_len[0]
    ordinal = jnp.arange(lengths.shape[0])
    starts = jnp.sum(jnp.where(ordinal[None, :] < ordinal[:, None], lengths[None, :], 0), axis=1)
    rows = jnp.arange(tok_count, dtype=jnp.int32)
    member = (rows[:, None] >= starts[None, :]) & (rows[:, None] < (starts + lengths)[None, :])
    row_owner = jnp.sum(jnp.where(member, owners[None, :], 0), axis=1)

    base_part = jnp.dot(tokens, base_weight, preferred_element_type=jnp.float32)
    base = lax.psum_scatter(base_part, "tp", scatter_dimension=1, tiled=True)

    def low_rank(blocks, steps):
        scores = [
            jnp.where(
                (row_owner == (me ^ step))[:, None],
                lax.dot_general(
                    tokens,
                    block[:, :depth],
                    (((1,), (1,)), ((), ())),
                    preferred_element_type=jnp.float32,
                ),
                0.0,
            )
            for block, step in zip(blocks, steps)
        ]
        scores = jnp.concatenate(scores, axis=1)
        for shift in range(1, cores):
            scores = scores + lax.ppermute(
                scores, "tp", [(i, (i + shift) % cores) for i in range(cores)]
            )
        expand = jnp.concatenate([block[:, depth:] for block in blocks], axis=0)
        return jnp.dot(
            scores,
            expand.astype(jnp.float32),
            precision=lax.Precision.HIGHEST,
            preferred_element_type=jnp.float32,
        )

    lora = low_rank([own] + near_recv, (0,) + near)
    lora = lora + low_rank(far_recv, far)
    for group in passed:
        lora = lora + low_rank(group, far)
    return (base + adapter_scale * lora).astype(jnp.bfloat16)


def solution(mesh):
    return jax.shard_map(
        on_device,
        mesh=mesh,
        in_specs=(
            P(("parts", "rep"), "tp"),
            P("tp", None),
            P("rep", "tp", None),
            P("rep", None, None),
            P(),
            P(),
            P(("parts", "rep"), None),
        ),
        out_specs=P(("parts", "rep"), "tp"),
        check_vma=False,
    )
```

time: 170 us -> 218 us (1.28)
  the two profiles are of different devices: /device:TPU:0 before, /device:TPU:19 now
where the time goes in v1:
time: 218 us
  Pallas kernels  113 us (52%)
  waiting for transfers between devices  37.4 us (17%)
  starting transfers between devices  24 us (11%)
  matrix products  22.6 us (10%)
  between operations  13.7 us (6%)
  local copies, waits for them, and re-layouts  5.08 us (2%)
    pallas_call x3, Pallas kernels, pack(): pl.pallas_call(functools.partial(pack_kernel, steps, rows), out_shape=[ja...  113 us
    ppermute x7, waiting for transfers between devices, hop(): return lax.ppermute(x, 'rep', [(i, i ^ step) for i in range(replicas)])  27.1 us
    ppermute x7, starting transfers between devices, hop(): return lax.ppermute(x, 'rep', [(i, i ^ step) for i in range(replicas)])  16.8 us
    dot_general x12, matrix products, low_rank(): lax.dot_general(tokens, block[:, :depth], (((1,), (1,)), ((), ())), prefe...  12.7 us
    ppermute x4, waiting for transfers between devices, across(): lax.ppermute(x, 'parts', [(i, (i + shift) % parts) for i in range(parts)])  10.3 us
    dot_general x1, matrix products, on_device(): base_part = jnp.dot(tokens, base_weight, preferred_element_type=jnp.float32)  6.7 us
    ppermute x3, starting transfers between devices, low_rank(): lax.ppermute(scores, 'tp', [(i, (i + shift) % cores) for i in range(cores)])  5.12 us
    slice x13, local copies, waits for them, and re-layouts, low_rank(): expand = jnp.concatenate([block[:, depth:] for block in blocks], axis=0)  4.41 us
  transfers between devices with their start and end apart: 15, of which 6 were waited for; matrix products, arithmetic and copies ran while one was open for 12% of the time, Pallas kernels for 0%

profile of v1, /device:TPU:19, one launch (start us, length us, event | category | flops | bytes accessed | tf_op | source)
XLA Modules:
  0.0 217.8 jit_solution(11944707798890653390)
XLA Ops:
  6.5 19.9 %shard_map.75 = bf16[64,4608]{1,0:T(8,128)(2,1)} custom-call(s32[32]{0:T(128)} %home_ref.5, s32[8,8]{1,0:T(8,128)} %fetch_ref.5, bf16[4,64,4096]{2,1,0:T(8,128)(2,1)} %bitcast.32, bf16[4,64,1024]{2,1,0:T(8,128)(2,1)} %expand_ref.5), custom_call_target="tpu_custom_call" | custom-call | bytes 1179648 | tf_op jit(solution)/shard_map/pallas_call | solution.py:47
  26.5 37.7 %shard_map.73 = (bf16[32,4608]{1,0:T(8,128)(2,1)}, bf16[32,4608]{1,0:T(8,128)(2,1)}, bf16[32,4608]{1,0:T(8,128)(2,1)}, bf16[32,4608]{1,0:T(8,128)(2,1)}) custom-call(s32[32]{0:T(128)} %home_ref.5, s32[8,8]{1,0:T(8,128)} %fetch_ref.5, bf16[4,64,4096]{2,1,0:T(8,128)(2,1)} %bitcast.33, bf16[4,64,1024]{2,1,0:T(8,128)(2,1)} %expand_ref.5), custom_call_target="tpu_custom_call" | custom-call | bytes 2359296 | tf_op jit(solution)/shard_map/pallas_call | solution.py:47
  64.2 55.6 %shard_map.74 = (bf16[64,4608]{1,0:T(8,128)(2,1)}, bf16[64,4608]{1,0:T(8,128)(2,1)}, bf16[64,4608]{1,0:T(8,128)(2,1)}) custom-call(s32[32]{0:T(128)} %home_ref.5, s32[8,8]{1,0:T(8,128)} %fetch_ref.5, bf16[4,64,4096]{2,1,0:T(8,128)(2,1)} %bitcast.34, bf16[4,64,1024]{2,1,0:T(8,128)(2,1)} %expand_ref.5), custom_call_target="tpu_custom_call" | custom-call | bytes 3538944 | tf_op jit(solution)/shard_map/pallas_call | solution.py:47
  119.9 3.3 %collective-permute-start.5 = (bf16[32,4608]{1,0:T(8,128)(2,1)}, bf16[32,4608]{1,0:T(8,128)(2,1)}, u32[]{:S(2)}, u32[]{:S(2)}) collective-permute-start(bf16[32,4608]{1,0:T(8,128)(2,1)} %get-tuple-element.34), channel_id=1, source_target_pairs={{0,10},{2,8},{4,14},{6,12},{8,2},{10,0},{12,6},{14,4},{1,11},{3,9}... | collective-permute-start | bytes 884744 | tf_op jit(solution)/shard_map/ppermute | solution.py:78
  123.4 1.2 collective-permute-start.7
  124.6 1.2 collective-permute-start
  125.8 6.7 %fusion.49 = f32[256,1024]{1,0:T(8,128)} fusion(bf16[256,4096]{1,0:T(8,128)(2,1)S(1)} %copy-done, bf16[4096,1024]{1,0:T(8,128)(2,1)} %param.8), kind=kOutput, calls=%fused_computation.89 | convolution fusion | flops 2147483648 | bytes 11534336 | tf_op jit(solution)/shard_map/dot_general | solution.py:96
  134.0 0.8 fusion.44
  134.9 0.8 convolution_select_fusion.3
  135.7 15.5 %collective-permute-done.4 = bf16[32,4608]{1,0:T(8,128)(2,1)} collective-permute-done((bf16[32,4608]{1,0:T(8,128)(2,1)}, bf16[32,4608]{1,0:T(8,128)(2,1)}, u32[]{:S(2)}, u32[]{:S(2)}) %collective-permute-start.4) | collective-permute-done | bytes 294944 | tf_op jit(solution)/shard_map/ppermute | solution.py:78
  151.2 5.3 %collective-permute-start.1 = (bf16[64,4608]{1,0:T(8,128)(2,1)S(1)}, bf16[64,4608]{1,0:T(8,128)(2,1)S(1)}, u32[]{:S(2)}, u32[]{:S(2)}) collective-permute-start(bf16[64,4608]{1,0:T(8,128)(2,1)S(1)} %copy-done.5), channel_id=1, source_target_pairs={{0,4},{2,6},{4,0},{6,2},{8,12},{10,14},{12,8},{14,10},{1,5},{3,7},... | collective-permute-start | bytes 1769480 | tf_op jit(solution)/shard_map/ppermute | solution.py:78
  156.4 1.7 convolution_select_fusion.11
  158.2 5.6 %collective-permute-start.2 = (bf16[64,4608]{1,0:T(8,128)(2,1)S(1)}, bf16[64,4608]{1,0:T(8,128)(2,1)S(1)}, u32[]{:S(2)}, u32[]{:S(2)}) collective-permute-start(bf16[64,4608]{1,0:T(8,128)(2,1)S(1)} %copy-done.4), channel_id=1, source_target_pairs={{0,6},{2,4},{4,2},{6,0},{8,14},{10,12},{12,10},{14,8},{1,7},{3,5},... | collective-permute-start | bytes 1769480 | tf_op jit(solution)/shard_map/ppermute | solution.py:78
  163.7 1.7 convolution_select_fusion.10
  165.4 2.5 %collective-permute-done.6 = bf16[32,4608]{1,0:T(8,128)(2,1)} collective-permute-done((bf16[32,4608]{1,0:T(8,128)(2,1)}, bf16[32,4608]{1,0:T(8,128)(2,1)}, u32[]{:S(2)}, u32[]{:S(2)}) %collective-permute-start.6) | collective-permute-done | bytes 294944 | tf_op jit(solution)/shard_map/ppermute | solution.py:78
  168.2 1.7 convolution_select_fusion.9
  169.9 9.1 %collective-permute-done.7 = bf16[32,4608]{1,0:T(8,128)(2,1)S(1)} collective-permute-done((bf16[32,4608]{1,0:T(8,128)(2,1)}, bf16[32,4608]{1,0:T(8,128)(2,1)S(1)}, u32[]{:S(2)}, u32[]{:S(2)}) %collective-permute-start.7) | collective-permute-done | bytes 294944 | tf_op jit(solution)/shard_map/ppermute | solution.py:78
  179.2 0.7 convolution_select_fusion.8
  180.0 0.8 slice.108
  180.7 0.8 slice.109
  181.5 0.8 slice.110
  182.3 1.3 collective-permute-start.11
  184.3 2.5 %collective-permute-done.10 = bf16[32,4608]{1,0:T(8,128)(2,1)S(1)} collective-permute-done((bf16[32,4608]{1,0:T(8,128)(2,1)}, bf16[32,4608]{1,0:T(8,128)(2,1)S(1)}, u32[]{:S(2)}, u32[]{:S(2)}) %collective-permute-start.10) | collective-permute-done | bytes 294944 | tf_op jit(solution)/shard_map/ppermute | solution.py:81
  187.8 5.3 %collective-permute-done.11 = bf16[32,4608]{1,0:T(8,128)(2,1)S(1)} collective-permute-done((bf16[32,4608]{1,0:T(8,128)(2,1)}, bf16[32,4608]{1,0:T(8,128)(2,1)S(1)}, u32[]{:S(2)}, u32[]{:S(2)}) %collective-permute-start.11) | collective-permute-done | bytes 294944 | tf_op jit(solution)/shard_map/ppermute | solution.py:81
  193.1 3.2 %collective-permute-start.8 = (f32[256,128]{0,1:T(8,128)S(1)}, f32[256,128]{0,1:T(8,128)S(1)}, u32[]{:S(2)}, u32[]{:S(2)}) collective-permute-start(f32[256,128]{0,1:T(8,128)S(1)} %pad_maximum_fusion.1), channel_id=1, source_target_pairs={{0,1},{1,0},{2,3},{3,2},{4,5},{5,4},{6,7},{7,6},{8,9},{9,8},{10,11... | collective-permute-start | bytes 393224 | tf_op jit(solution)/shard_map/ppermute | solution.py:115
  197.0 2.4 %collective-permute-done.12 = bf16[32,4608]{1,0:T(8,128)(2,1)S(1)} collective-permute-done((bf16[32,4608]{1,0:T(8,128)(2,1)S(1)}, bf16[32,4608]{1,0:T(8,128)(2,1)S(1)}, u32[]{:S(2)}, u32[]{:S(2)}) %collective-permute-start.12) | collective-permute-done | bytes 294944 | tf_op jit(solution)/shard_map/ppermute | solution.py:81
  200.2 1.9 collective-permute-start.13
  202.1 1.8 convolution_select_fusion.2
  203.9 0.8 convolution_select_fusion.1
  204.6 0.8 convolution_select_fusion
  206.0 0.8 slice.101
  208.6 2.4 %fusion.3 = bf16[256,512]{1,0:T(8,128)(2,1)} fusion(f32[256,512]{1,0:T(8,128)} %reduce-scatter.2.cloned.1.call-done, f32[256,512]{1,0:T(8,128)S(1)} %fusion.32, f32[256,512]{1,0:T(8,128)S(1)} %fusion.24, bf16[64,512]{1,0:T(8,128)(2,1)} %slice.103, bf16[64,512]{1,0:T(8,128)(2,1)} %slice.102, bf16[64,512]{1,0:T(8,128)(2,1)S(1)} %slice.101, ...), kind=kOutput, calls=%fused_computation.5 | convolution fusion | flops 404619264 | bytes 2621440 | tf_op jit(solution)/shard_map/dot_general | solution.py:119
  (53 shorter events, 7.9 us)
Async XLA Ops:
  6.5 119.3 %copy-start = (bf16[256,4096]{1,0:T(8,128)(2,1)S(1)}, bf16[256,4096]{1,0:T(8,128)(2,1)}, u32[]{:S(2)}) copy-start(bf16[256,4096]{1,0:T(8,128)(2,1)} %param.7) | copy-start | bytes 6291460
  6.5 202.0 %reduce-scatter.2.cloned.1.call-start = ((), (), s32[]{:S(2)}) async-start(), calls=%async_computation.1 | async-start | bytes 1572864 | tf_op jit(solution)/shard_map/reduce_scatter | solution.py:97
  119.7 12.8 %copy-start.3 = (s32[1,8]{1,0:T(1,128)S(1)}, s32[1,8]{1,0:T(1,128)}, u32[]{:S(2)}) copy-start(s32[1,8]{1,0:T(1,128)} %param.13) | copy-start | bytes 100
  119.8 13.6 %copy-start.1 = (s32[32]{0:T(128)S(1)}, s32[32]{0:T(128)}, u32[]{:S(2)}) copy-start(s32[32]{0:T(128)} %home_ref.5) | copy-start | bytes 388
  119.8 15.1 %copy-start.2 = (bf16[64,4608]{1,0:T(8,128)(2,1)S(1)}, bf16[64,4608]{1,0:T(8,128)(2,1)}, u32[]{:S(2)}) copy-start(bf16[64,4608]{1,0:T(8,128)(2,1)} %shard_map.75) | copy-start | bytes 1769476
  119.8 31.4 %collective-permute-start.4 = (bf16[32,4608]{1,0:T(8,128)(2,1)}, bf16[32,4608]{1,0:T(8,128)(2,1)}, u32[]{:S(2)}, u32[]{:S(2)}) collective-permute-start(bf16[32,4608]{1,0:T(8,128)(2,1)} %get-tuple-element.33), channel_id=1, source_target_pairs={{0,8},{2,10},{4,12},{6,14},{8,0},{10,2},{12,4},{14,6},{1,9},{3,11}... | collective-permute-start | bytes 884744 | tf_op jit(solution)/shard_map/ppermute | solution.py:78
  119.9 38.2 %collective-permute-start.5 = (bf16[32,4608]{1,0:T(8,128)(2,1)}, bf16[32,4608]{1,0:T(8,128)(2,1)}, u32[]{:S(2)}, u32[]{:S(2)}) collective-permute-start(bf16[32,4608]{1,0:T(8,128)(2,1)} %get-tuple-element.34), channel_id=1, source_target_pairs={{0,10},{2,8},{4,14},{6,12},{8,2},{10,0},{12,6},{14,4},{1,11},{3,9}... | collective-permute-start | bytes 884744 | tf_op jit(solution)/shard_map/ppermute | solution.py:78
  123.2 44.8 %collective-permute-start.6 = (bf16[32,4608]{1,0:T(8,128)(2,1)}, bf16[32,4608]{1,0:T(8,128)(2,1)}, u32[]{:S(2)}, u32[]{:S(2)}) collective-permute-start(bf16[32,4608]{1,0:T(8,128)(2,1)} %get-tuple-element.35), channel_id=1, source_target_pairs={{0,12},{2,14},{4,8},{6,10},{8,4},{10,6},{12,0},{14,2},{1,13},{3,15... | collective-permute-start | bytes 884744 | tf_op jit(solution)/shard_map/ppermute | solution.py:78
  123.4 55.6 %collective-permute-start.7 = (bf16[32,4608]{1,0:T(8,128)(2,1)}, bf16[32,4608]{1,0:T(8,128)(2,1)S(1)}, u32[]{:S(2)}, u32[]{:S(2)}) collective-permute-start(bf16[32,4608]{1,0:T(8,128)(2,1)} %get-tuple-element.36), channel_id=1, source_target_pairs={{0,14},{2,12},{4,10},{6,8},{8,6},{10,4},{12,2},{14,0},{1,15},{3,13... | collective-permute-start | bytes 884744 | tf_op jit(solution)/shard_map/ppermute | solution.py:78
  124.6 77.5 %collective-permute-start = (bf16[64,4608]{1,0:T(8,128)(2,1)}, bf16[64,4608]{1,0:T(8,128)(2,1)}, u32[]{:S(2)}, u32[]{:S(2)}) collective-permute-start(bf16[64,4608]{1,0:T(8,128)(2,1)} %get-tuple-element.30), channel_id=1, source_target_pairs={{0,2},{2,0},{4,6},{6,4},{8,10},{10,8},{12,14},{14,12},{1,3},{3,1},... | collective-permute-start | bytes 1769480 | tf_op jit(solution)/shard_map/ppermute | solution.py:78
  134.0 17.2 %copy-start.5 = (bf16[64,4608]{1,0:T(8,128)(2,1)S(1)}, bf16[64,4608]{1,0:T(8,128)(2,1)}, u32[]{:S(2)}) copy-start(bf16[64,4608]{1,0:T(8,128)(2,1)} %get-tuple-element.31) | copy-start | bytes 1769476
  134.9 23.2 %copy-start.4 = (bf16[64,4608]{1,0:T(8,128)(2,1)S(1)}, bf16[64,4608]{1,0:T(8,128)(2,1)}, u32[]{:S(2)}) copy-start(bf16[64,4608]{1,0:T(8,128)(2,1)} %get-tuple-element.32) | copy-start | bytes 1769476
  151.2 52.7 %collective-permute-start.1 = (bf16[64,4608]{1,0:T(8,128)(2,1)S(1)}, bf16[64,4608]{1,0:T(8,128)(2,1)S(1)}, u32[]{:S(2)}, u32[]{:S(2)}) collective-permute-start(bf16[64,4608]{1,0:T(8,128)(2,1)S(1)} %copy-done.5), channel_id=1, source_target_pairs={{0,4},{2,6},{4,0},{6,2},{8,12},{10,14},{12,8},{14,10},{1,5},{3,7},... | collective-permute-start | bytes 1769480 | tf_op jit(solution)/shard_map/ppermute | solution.py:78
  158.2 46.5 %collective-permute-start.2 = (bf16[64,4608]{1,0:T(8,128)(2,1)S(1)}, bf16[64,4608]{1,0:T(8,128)(2,1)S(1)}, u32[]{:S(2)}, u32[]{:S(2)}) collective-permute-start(bf16[64,4608]{1,0:T(8,128)(2,1)S(1)} %copy-done.4), channel_id=1, source_target_pairs={{0,6},{2,4},{4,2},{6,0},{8,14},{10,12},{12,10},{14,8},{1,7},{3,5},... | collective-permute-start | bytes 1769480 | tf_op jit(solution)/shard_map/ppermute | solution.py:78
  167.9 14.3 %collective-permute-start.9 = (bf16[32,4608]{1,0:T(8,128)(2,1)}, bf16[32,4608]{1,0:T(8,128)(2,1)S(1)}, u32[]{:S(2)}, u32[]{:S(2)}) collective-permute-start(bf16[32,4608]{1,0:T(8,128)(2,1)} %collective-permute-done.4), channel_id=1, source_target_pairs={{0,16},{16,0},{1,17},{17,1},{2,18},{18,2},{3,19},{19,3},{4,20},{20... | collective-permute-start | bytes 884744 | tf_op jit(solution)/shard_map/ppermute | solution.py:81
  179.0 7.8 %collective-permute-start.10 = (bf16[32,4608]{1,0:T(8,128)(2,1)}, bf16[32,4608]{1,0:T(8,128)(2,1)S(1)}, u32[]{:S(2)}, u32[]{:S(2)}) collective-permute-start(bf16[32,4608]{1,0:T(8,128)(2,1)} %collective-permute-done.5), channel_id=1, source_target_pairs={{0,16},{16,0},{1,17},{17,1},{2,18},{18,2},{3,19},{19,3},{4,20},{20... | collective-permute-start | bytes 884744 | tf_op jit(solution)/shard_map/ppermute | solution.py:81
  182.3 10.9 %collective-permute-start.11 = (bf16[32,4608]{1,0:T(8,128)(2,1)}, bf16[32,4608]{1,0:T(8,128)(2,1)S(1)}, u32[]{:S(2)}, u32[]{:S(2)}) collective-permute-start(bf16[32,4608]{1,0:T(8,128)(2,1)} %collective-permute-done.6), channel_id=1, source_target_pairs={{0,16},{16,0},{1,17},{17,1},{2,18},{18,2},{3,19},{19,3},{4,20},{20... | collective-permute-start | bytes 884744 | tf_op jit(solution)/shard_map/ppermute | solution.py:81
  186.8 12.6 %collective-permute-start.12 = (bf16[32,4608]{1,0:T(8,128)(2,1)S(1)}, bf16[32,4608]{1,0:T(8,128)(2,1)S(1)}, u32[]{:S(2)}, u32[]{:S(2)}) collective-permute-start(bf16[32,4608]{1,0:T(8,128)(2,1)S(1)} %collective-permute-done.7), channel_id=1, source_target_pairs={{0,16},{16,0},{1,17},{17,1},{2,18},{18,2},{3,19},{19,3},{4,20},{20... | collective-permute-start | bytes 884744 | tf_op jit(solution)/shard_map/ppermute | solution.py:81
  193.1 12.4 %collective-permute-start.8 = (f32[256,128]{0,1:T(8,128)S(1)}, f32[256,128]{0,1:T(8,128)S(1)}, u32[]{:S(2)}, u32[]{:S(2)}) collective-permute-start(f32[256,128]{0,1:T(8,128)S(1)} %pad_maximum_fusion.1), channel_id=1, source_target_pairs={{0,1},{1,0},{2,3},{3,2},{4,5},{5,4},{6,7},{7,6},{8,9},{9,8},{10,11... | collective-permute-start | bytes 393224 | tf_op jit(solution)/shard_map/ppermute | solution.py:115
  200.2 7.9 %collective-permute-start.13 = (f32[256,128]{0,1:T(8,128)S(1)}, f32[256,128]{0,1:T(8,128)S(1)}, u32[]{:S(2)}, u32[]{:S(2)}) collective-permute-start(f32[256,128]{0,1:T(8,128)S(1)} %pad_maximum_fusion.2), channel_id=1, source_target_pairs={{0,1},{1,0},{2,3},{3,2},{4,5},{5,4},{6,7},{7,6},{8,9},{9,8},{10,11... | collective-permute-start | bytes 393224 | tf_op jit(solution)/shard_map/ppermute | solution.py:115
  205.4 3.2 %slice-start = ((bf16[64,4608]{1,0:T(8,128)(2,1)}), bf16[64,512]{1,0:T(8,128)(2,1)S(1)}, s32[]{:S(2)}) async-start(bf16[64,4608]{1,0:T(8,128)(2,1)} %shard_map.75), calls=%async_computation.2 | async-start | bytes 131072 | tf_op jit(solution)/shard_map/slice | solution.py:118
  205.4 3.1 %collective-permute-start.3 = (f32[256,256]{0,1:T(8,128)S(1)}, f32[256,256]{0,1:T(8,128)}, u32[]{:S(2)}, u32[]{:S(2)}) collective-permute-start(f32[256,256]{0,1:T(8,128)S(1)} %pad_maximum_fusion), channel_id=1, source_target_pairs={{0,1},{1,0},{2,3},{3,2},{4,5},{5,4},{6,7},{7,6},{8,9},{9,8},{10,11... | collective-permute-start | bytes 786440 | tf_op jit(solution)/shard_map/ppermute | solution.py:115
Sparse Core Ops, SparseCore 0:
  132.7 12.5 reduce-scatter.1

commit v2 on v1

v2 whole, which is shorter than its diff:
```python
import functools
import jax
import jax.numpy as jnp
from jax import lax
from jax.experimental import pallas as pl
from jax.experimental.pallas import tpu as pltpu
from jax.sharding import PartitionSpec as P

adapter_scale = 2.0


def pack_kernel(plan, home_ref, fetch_ref, shrink_ref, expand_ref, *refs):
    outs, sems = refs[:-1], refs[-1]
    me, part, half = lax.axis_index("rep"), lax.axis_index("parts"), lax.axis_index("tp")
    per_home, rank, depth = shrink_ref.shape
    listed = fetch_ref.shape[1]
    columns = outs[0].shape[1] - depth
    left = pl.multiple_of(half * columns, 128)
    copies, slots = [], {}
    for at, (step, first, rows, share) in enumerate(plan):
        peer = me ^ step

        def look(j, slot):
            position = home_ref[fetch_ref[peer, j]]
            return jnp.where(position // per_home == me, position % per_home, slot)

        if step not in slots:
            slots[step] = lax.fori_loop(0, listed, look, jnp.int32(0), unroll=listed <= 8)
        slot = slots[step]
        start = pl.multiple_of(part * share + first, 16)
        for n, (source, target) in enumerate(
            (
                (shrink_ref.at[slot, pl.ds(start, rows), :], outs[at].at[:, pl.ds(0, depth)]),
                (
                    expand_ref.at[slot, pl.ds(start, rows), pl.ds(left, columns)],
                    outs[at].at[:, pl.ds(depth, columns)],
                ),
            )
        ):
            copy = pltpu.make_async_copy(source, target, sems.at[at, n])
            copy.start()
            copies.append(copy)
    for copy in copies:
        copy.wait()


def pack(plan, columns, adapter_home, fetch_list, panels, expand_panels):
    width = panels.shape[2] + columns
    size = 2 * width * sum(rows for _, _, rows, _ in plan)
    return pl.pallas_call(
        functools.partial(pack_kernel, plan),
        out_shape=[jax.ShapeDtypeStruct((rows, width), panels.dtype) for _, _, rows, _ in plan],
        in_specs=[pl.BlockSpec(memory_space=pltpu.SMEM)] * 2 + [pl.BlockSpec(memory_space=pl.ANY)] * 2,
        out_specs=[pl.BlockSpec(memory_space=pltpu.VMEM)] * len(plan),
        scratch_shapes=[pltpu.SemaphoreType.DMA((len(plan), 2))],
        compiler_params=pltpu.CompilerParams(vmem_limit_bytes=2 * size + (1 << 20)),
        cost_estimate=pl.CostEstimate(flops=0, bytes_accessed=2 * size, transcendentals=0),
    )(adapter_home, fetch_list, panels, expand_panels)


def on_device(tokens, base_weight, shrink_panels, expand_panels, adapter_home, fetch_list, seg_len):
    per_home, depth, rank = shrink_panels.shape
    replicas, parts, cores = lax.axis_size("rep"), lax.axis_size("parts"), lax.axis_size("tp")
    me = lax.axis_index("rep")
    tok_count = tokens.shape[0]
    columns = expand_panels.shape[2] // cores
    panels = jnp.swapaxes(shrink_panels, 1, 2)
    share = rank // parts

    shared = [step for step in range(replicas // 2, replicas)]
    shared += [step for step in range(2, replicas // 2)]
    order = shared[: replicas // 2 - 1] + shared[replicas // 2 :] + shared[replicas // 2 - 1 : replicas // 2]
    cut = max(16, share // 2)
    plan = [(step, 0, share, share) for step in order[:-1]]
    plan += [(order[-1], first, cut, share) for first in range(0, share, cut)]
    window = 2

    args = (columns, adapter_home, fetch_list, panels, expand_panels)
    first_send = pack(plan[:window], *args)
    panels, first_send = lax.optimization_barrier((panels, first_send))
    args = (columns, adapter_home, fetch_list, panels, expand_panels)
    *rest_send, whole_send, own = pack(plan[window:] + [(1, 0, rank, 0), (0, 0, rank, 0)], *args)
    tokens, rest_send, whole_send, own = lax.optimization_barrier(
        (tokens, rest_send, whole_send, own)
    )
    send = list(first_send) + list(rest_send)

    def hop(x, step):
        return lax.ppermute(x, "rep", [(i, i ^ step) for i in range(replicas)])

    def across(x, shift):
        return lax.ppermute(x, "parts", [(i, (i + shift) % parts) for i in range(parts)])

    received = []
    whole = hop(whole_send, 1)
    for at, (step, *_) in enumerate(plan):
        block = send[at]
        if at >= window:
            block, received[at - window] = lax.optimization_barrier((block, received[at - window]))
        if at == len(plan) // 2:
            block, whole = lax.optimization_barrier((block, whole))
        received.append(hop(block, step))
    passed = [[across(x, shift) for shift in range(1, parts)] for x in received]

    stored = jnp.take(adapter_home, lax.dynamic_index_in_dim(fetch_list, me, 0, keepdims=False))
    owners = stored // per_home
    lengths = seg_len[0]
    ordinal = jnp.arange(lengths.shape[0])
    starts = jnp.sum(jnp.where(ordinal[None, :] < ordinal[:, None], lengths[None, :], 0), axis=1)
    rows = jnp.arange(tok_count, dtype=jnp.int32)
    member = (rows[:, None] >= starts[None, :]) & (rows[:, None] < (starts + lengths)[None, :])
    row_owner = jnp.sum(jnp.where(member, owners[None, :], 0), axis=1)

    base_part = jnp.dot(tokens, base_weight, preferred_element_type=jnp.float32)
    base = lax.psum_scatter(base_part, "tp", scatter_dimension=1, tiled=True)

    def low_rank(blocks):
        scores = [
            jnp.where(
                (row_owner == (me ^ step))[:, None],
                lax.dot_general(
                    tokens,
                    block[:, :depth],
                    (((1,), (1,)), ((), ())),
                    preferred_element_type=jnp.float32,
                ),
                0.0,
            )
            for step, block in blocks
        ]
        scores = jnp.concatenate(scores, axis=1)
        for shift in range(1, cores):
            scores = scores + lax.ppermute(
                scores, "tp", [(i, (i + shift) % cores) for i in range(cores)]
            )
        expand = jnp.concatenate([block[:, depth:] for _, block in blocks], axis=0)
        return jnp.dot(
            scores,
            expand.astype(jnp.float32),
            precision=lax.Precision.HIGHEST,
            preferred_element_type=jnp.float32,
        )

    steps = [step for step, *_ in plan]
    late = len(plan) - 2
    lora = low_rank([(0, own), (1, whole)] + list(zip(steps[:late], received[:late])))
    lora = lora + low_rank(
        [(step, x) for step, group in zip(steps[:late], passed[:late]) for x in group]
    )
    lora = lora + low_rank(
        list(zip(steps[late:], received[late:]))
        + [(step, x) for step, group in zip(steps[late:], passed[late:]) for x in group]
    )
    return (base + adapter_scale * lora).astype(jnp.bfloat16)


def solution(mesh):
    return jax.shard_map(
        on_device,
        mesh=mesh,
        in_specs=(
            P(("parts", "rep"), "tp"),
            P("tp", None),
            P("rep", "tp", None),
            P("rep", None, None),
            P(),
            P(),
            P(("parts", "rep"), None),
        ),
        out_specs=P(("parts", "rep"), "tp"),
        check_vma=False,
    )
```

time: 218 us -> 112 us (0.51)
  the two profiles are of different devices: /device:TPU:19 before, /device:TPU:9 now
where the time goes in v2:
time: 112 us; the launch traced here: 111 us
  waiting for transfers between devices  40.9 us (37%)
  matrix products  24.5 us (22%)
  starting transfers between devices  18.7 us (17%)
  between operations  13.8 us (12%)
  local copies, waits for them, and re-layouts  10.1 us (9%)
  Pallas kernels  3.12 us (3%)
    ppermute x8, waiting for transfers between devices, hop(): return lax.ppermute(x, 'rep', [(i, i ^ step) for i in range(replicas)])  38.2 us
    dot_general x16, matrix products, low_rank(): lax.dot_general(tokens, block[:, :depth], (((1,), (1,)), ((), ())), prefe...  14.3 us
    unnamed x52, local copies, waits for them, and re-layouts  9.4 us
    ppermute x8, starting transfers between devices, hop(): return lax.ppermute(x, 'rep', [(i, i ^ step) for i in range(replicas)])  7.51 us
    dot_general x1, matrix products, on_device(): base_part = jnp.dot(tokens, base_weight, preferred_element_type=jnp.float32)  6.7 us
    ppermute x7, starting transfers between devices, across(): lax.ppermute(x, 'parts', [(i, (i + shift) % parts) for i in range(parts)])  6.63 us
    ppermute x3, starting transfers between devices, low_rank(): lax.ppermute(scores, 'tp', [(i, (i + shift) % cores) for i in range(cores)])  4.6 us
    dot_general x3, matrix products, low_rank(): jnp.dot(scores, expand.astype(jnp.float32), precision=lax.Precision.HIGHE...  3.53 us
  transfers between devices with their start and end apart: 19, of which 7 were waited for; matrix products, arithmetic and copies ran while one was open for 23% of the time, Pallas kernels for 1%

profile of v2, /device:TPU:9, one launch (start us, length us, event | category | flops | bytes accessed | tf_op | source)
XLA Modules:
  0.0 111.4 jit_solution(11155525384771419804)
XLA Ops:
  6.5 0.8 copy-done.1
  7.4 1.6 %copy-done.3 = bf16[4,4096,64]{1,2,0:T(8,128)(2,1)S(1)} copy-done((bf16[4,4096,64]{1,2,0:T(8,128)(2,1)S(1)}, bf16[4,4096,64]{1,2,0:T(8,128)(2,1)}, u32[]{:S(2)}) %copy-start.3) | copy-done | bytes 2097176
  9.0 1.0 copy-done.5
  10.7 1.6 %shard_map.73 = (bf16[32,4608]{1,0:T(8,128)(2,1)}, bf16[32,4608]{1,0:T(8,128)(2,1)}) custom-call(s32[32]{0:T(128)S(1)} %copy-done.1, s32[8,8]{1,0:T(8,128)S(1)} %copy-done.7, bf16[4,64,4096]{2,1,0:T(8,128)(2,1)S(1)} %bitcast.38, bf16[4,64,1024]{2,1,0:T(8,128)(2,1)S(1)} %copy-done.5), custom_call_target="tpu_custom_call" | custom-call | bytes 1179648 | tf_op jit(solution)/shard_map/pallas_call | solution.py:50
  12.3 3.3 %collective-permute-start = (bf16[32,4608]{1,0:T(8,128)(2,1)}, bf16[32,4608]{1,0:T(8,128)(2,1)}, u32[]{:S(2)}, u32[]{:S(2)}) collective-permute-start(bf16[32,4608]{1,0:T(8,128)(2,1)} %get-tuple-element.50), channel_id=1, source_target_pairs={{0,10},{2,8},{4,14},{6,12},{8,2},{10,0},{12,6},{14,4},{1,11},{3,9}... | collective-permute-start | bytes 884744 | tf_op jit(solution)/shard_map/ppermute | solution.py:89
  15.7 1.5 %shard_map.74 = (bf16[32,4608]{1,0:T(8,128)(2,1)S(1)}, bf16[32,4608]{1,0:T(8,128)(2,1)S(1)}, bf16[32,4608]{1,0:T(8,128)(2,1)S(1)}, bf16[16,4608]{1,0:T(8,128)(2,...) custom-call(s32[32]{0:T(128)S(1)} %copy-done.2, ...), custom_call_target="tpu_custom_call" | custom-call | bytes 4718592 | tf_op jit(solution)/shard_map/pallas_call | solution.py:50
  20.3 6.7 %fusion.49 = f32[256,1024]{1,0:T(8,128)} fusion(bf16[256,4096]{1,0:T(8,128)(2,1)S(1)} %copy-done, bf16[4096,1024]{1,0:T(8,128)(2,1)} %param.8), kind=kOutput, calls=%fused_computation.103 | convolution fusion | flops 2147483648 | bytes 11534336 | tf_op jit(solution)/shard_map/dot_general | solution.py:114
  28.0 13.6 %collective-permute-done.2 = bf16[32,4608]{1,0:T(8,128)(2,1)} collective-permute-done((bf16[32,4608]{1,0:T(8,128)(2,1)}, bf16[32,4608]{1,0:T(8,128)(2,1)}, u32[]{:S(2)}, u32[]{:S(2)}) %collective-permute-start.2) | collective-permute-done | bytes 294944 | tf_op jit(solution)/shard_map/ppermute | solution.py:89
  41.6 0.8 fusion.5
  42.3 1.3 %collective-permute-start.7 = (bf16[32,4608]{1,0:T(8,128)(2,1)}, bf16[32,4608]{1,0:T(8,128)(2,1)S(1)}, u32[]{:S(2)}, u32[]{:S(2)}) collective-permute-start(bf16[32,4608]{1,0:T(8,128)(2,1)} %collective-permute-done.2), channel_id=1, source_target_pairs={{0,16},{16,0},{1,17},{17,1},{2,18},{18,2},{3,19},{19,3},{4,20},{20... | collective-permute-start | bytes 884744 | tf_op jit(solution)/shard_map/ppermute | solution.py:92
  43.9 12.3 %collective-permute-done.3 = bf16[32,4608]{1,0:T(8,128)(2,1)S(1)} collective-permute-done((bf16[32,4608]{1,0:T(8,128)(2,1)}, bf16[32,4608]{1,0:T(8,128)(2,1)S(1)}, u32[]{:S(2)}, u32[]{:S(2)}) %collective-permute-start.3) | collective-permute-done | bytes 294944 | tf_op jit(solution)/shard_map/ppermute | solution.py:89
  56.2 1.4 %collective-permute-start.5 = (bf16[32,4608]{1,0:T(8,128)(2,1)S(1)}, bf16[32,4608]{1,0:T(8,128)(2,1)S(1)}, u32[]{:S(2)}, u32[]{:S(2)}) collective-permute-start(bf16[32,4608]{1,0:T(8,128)(2,1)S(1)} %copy-done.10), channel_id=1, source_target_pairs={{0,6},{2,4},{4,2},{6,0},{8,14},{10,12},{12,10},{14,8},{1,7},{3,5},... | collective-permute-start | bytes 884744 | tf_op jit(solution)/shard_map/ppermute | solution.py:89
  57.6 0.8 slice_dynamic-update-slice_fusion
  58.4 0.8 constant_dynamic-update-slice_fusion.4
  59.2 0.8 constant_dynamic-update-slice_fusion.3
  60.0 1.2 %collective-permute-start.9 = (bf16[32,4608]{1,0:T(8,128)(2,1)S(1)}, bf16[32,4608]{1,0:T(8,128)(2,1)S(1)}, u32[]{:S(2)}, u32[]{:S(2)}) collective-permute-start(bf16[32,4608]{1,0:T(8,128)(2,1)S(1)} %collective-permute-done.3), channel_id=1, source_target_pairs={{0,16},{16,0},{1,17},{17,1},{2,18},{18,2},{3,19},{19,3},{4,20},{20... | collective-permute-start | bytes 884744 | tf_op jit(solution)/shard_map/ppermute | solution.py:92
  61.2 1.8 %fusion.4 = f32[256,288]{0,1:T(8,128)S(1)} fusion(f32[256,288]{0,1:T(8,128)S(1)} %fusion.5, bf16[256,4096]{1,0:T(8,128)(2,1)S(1)} %copy-done, bf16[64,4608]{1,0:T(8,128)(2,1)} %collective-permute-done.1, pred[256]{0:T(512)(128)(4,1)S(1)} %get-tuple-element.69), kind=kOutput, calls=%fused_computation.7 | convolution fusion | flops 134234112 | bytes 2687488 | tf_op jit(solution)/shard_map/dot_general | solution.py:121
  63.0 1.7 %fusion.15 = f32[256,288]{0,1:T(8,128)S(1)} fusion(f32[256,288]{0,1:T(8,128)S(1)} %fusion.4, bf16[256,4096]{1,0:T(8,128)(2,1)S(1)} %copy-done, bf16[32,4608]{1,0:T(8,128)(2,1)} %collective-permute-done.2, pred[256]{0:T(512)(128)(4,1)S(1)} %get-tuple-element.75), kind=kOutput, calls=%fused_computation.29 | convolution fusion | flops 67117056 | bytes 2392576 | tf_op jit(solution)/shard_map/dot_general | solution.py:121
  64.7 1.7 %fusion.14 = f32[256,288]{0,1:T(8,128)S(1)} fusion(f32[256,288]{0,1:T(8,128)S(1)} %fusion.15, bf16[256,4096]{1,0:T(8,128)(2,1)S(1)} %copy-done, bf16[32,4608]{1,0:T(8,128)(2,1)} %collective-permute-done, pred[256]{0:T(512)(128)(4,1)S(1)} %get-tuple-element.74), kind=kOutput, calls=%fused_computation.27 | convolution fusion | flops 67117056 | bytes 2392576 | tf_op jit(solution)/shard_map/dot_general | solution.py:121
  68.6 1.0 collective-permute-done.5
  69.6 1.2 %collective-permute-start.10 = (bf16[32,4608]{1,0:T(8,128)(2,1)S(1)}, bf16[32,4608]{1,0:T(8,128)(2,1)S(1)}, u32[]{:S(2)}, u32[]{:S(2)}) collective-permute-start(bf16[32,4608]{1,0:T(8,128)(2,1)S(1)} %collective-permute-done.4), channel_id=1, source_target_pairs={{0,16},{16,0},{1,17},{17,1},{2,18},{18,2},{3,19},{19,3},{4,20},{20... | collective-permute-start | bytes 884744 | tf_op jit(solution)/shard_map/ppermute | solution.py:92
  72.6 2.9 %collective-permute-start.6 = (f32[256,288]{0,1:T(8,128)S(1)}, f32[256,288]{0,1:T(8,128)}, u32[]{:S(2)}, u32[]{:S(2)}) collective-permute-start(f32[256,288]{0,1:T(8,128)S(1)} %fusion.11), channel_id=1, source_target_pairs={{0,1},{1,0},{2,3},{3,2},{4,5},{5,4},{6,7},{7,6},{8,9},{9,8},{10,11... | collective-permute-start | bytes 884744 | tf_op jit(solution)/shard_map/ppermute | solution.py:133
  75.4 1.3 %collective-permute-start.13 = (bf16[16,4608]{1,0:T(8,128)(2,1)S(1)}, bf16[16,4608]{1,0:T(8,128)(2,1)S(1)}, u32[]{:S(2)}, u32[]{:S(2)}) collective-permute-start(bf16[16,4608]{1,0:T(8,128)(2,1)S(1)} %copy-done.15), channel_id=1, source_target_pairs={{0,14},{2,12},{4,10},{6,8},{8,6},{10,4},{12,2},{14,0},{1,15},{3,13... | collective-permute-start | bytes 442376 | tf_op jit(solution)/shard_map/ppermute | solution.py:89
  76.8 1.2 %collective-permute-start.14 = (bf16[16,4608]{1,0:T(8,128)(2,1)S(1)}, bf16[16,4608]{1,0:T(8,128)(2,1)S(1)}, u32[]{:S(2)}, u32[]{:S(2)}) collective-permute-start(bf16[16,4608]{1,0:T(8,128)(2,1)S(1)} %get-tuple-element.68), channel_id=1, source_target_pairs={{0,14},{2,12},{4,10},{6,8},{8,6},{10,4},{12,2},{14,0},{1,15},{3,13... | collective-permute-start | bytes 442376 | tf_op jit(solution)/shard_map/ppermute | solution.py:89
  78.7 9.4 %collective-permute-done.13 = bf16[16,4608]{1,0:T(8,128)(2,1)S(1)} collective-permute-done((bf16[16,4608]{1,0:T(8,128)(2,1)S(1)}, bf16[16,4608]{1,0:T(8,128)(2,1)S(1)}, u32[]{:S(2)}, u32[]{:S(2)}) %collective-permute-start.13) | collective-permute-done | bytes 147488 | tf_op jit(solution)/shard_map/ppermute | solution.py:89
  88.1 1.2 %collective-permute-start.15 = (bf16[16,4608]{1,0:T(8,128)(2,1)S(1)}, bf16[16,4608]{1,0:T(8,128)(2,1)S(1)}, u32[]{:S(2)}, u32[]{:S(2)}) collective-permute-start(bf16[16,4608]{1,0:T(8,128)(2,1)S(1)} %collective-permute-done.13), channel_id=1, source_target_pairs={{0,16},{16,0},{1,17},{17,1},{2,18},{18,2},{3,19},{19,3},{4,20},{20... | collective-permute-start | bytes 442376 | tf_op jit(solution)/shard_map/ppermute | solution.py:92
  89.3 1.9 %collective-permute-done.14 = bf16[16,4608]{1,0:T(8,128)(2,1)S(1)} collective-permute-done((bf16[16,4608]{1,0:T(8,128)(2,1)S(1)}, bf16[16,4608]{1,0:T(8,128)(2,1)S(1)}, u32[]{:S(2)}, u32[]{:S(2)}) %collective-permute-start.14) | collective-permute-done | bytes 147488 | tf_op jit(solution)/shard_map/ppermute | solution.py:89
  91.2 1.2 %collective-permute-start.16 = (bf16[16,4608]{1,0:T(8,128)(2,1)S(1)}, bf16[16,4608]{1,0:T(8,128)(2,1)S(1)}, u32[]{:S(2)}, u32[]{:S(2)}) collective-permute-start(bf16[16,4608]{1,0:T(8,128)(2,1)S(1)} %collective-permute-done.14), channel_id=1, source_target_pairs={{0,16},{16,0},{1,17},{17,1},{2,18},{18,2},{3,19},{19,3},{4,20},{20... | collective-permute-start | bytes 442376 | tf_op jit(solution)/shard_map/ppermute | solution.py:92
  94.4 1.7 %collective-permute-done.16 = bf16[16,4608]{1,0:T(8,128)(2,1)S(1)} collective-permute-done((bf16[16,4608]{1,0:T(8,128)(2,1)S(1)}, bf16[16,4608]{1,0:T(8,128)(2,1)S(1)}, u32[]{:S(2)}, u32[]{:S(2)}) %collective-permute-start.16) | collective-permute-done | bytes 147488 | tf_op jit(solution)/shard_map/ppermute | solution.py:92
  96.8 1.6 %collective-permute-start.17 = (f32[256,64]{0,1:T(8,128)S(1)}, f32[256,64]{0,1:T(8,128)S(1)}, u32[]{:S(2)}, u32[]{:S(2)}) collective-permute-start(f32[256,64]{0,1:T(8,128)S(1)} %pad_maximum_fusion), channel_id=1, source_target_pairs={{0,1},{1,0},{2,3},{3,2},{4,5},{5,4},{6,7},{7,6},{8,9},{9,8},{10,11... | collective-permute-start | bytes 196616 | tf_op jit(solution)/shard_map/ppermute | solution.py:133
  100.5 0.9 collective-permute-done.12
  101.9 2.7 %fusion.3 = bf16[256,512]{1,0:T(8,128)(2,1)} fusion(f32[256,512]{1,0:T(8,128)} %reduce-scatter.2.cloned.1.call-done, f32[256,512]{1,0:T(8,128)S(1)} %fusion.35, f32[256,512]{1,0:T(8,128)S(1)} %fusion.29, bf16[288,512]{1,0:T(8,128)(2,1)} %copy-done.16, f32[256,288]{0,1:T(8,128)} %copy-done.17, f32[256,288]{0,1:T(8,128)} %collective-permute-done.6), kind=kOutput, calls=%fused_computation.5 | convolution fusion | flops 453713920 | bytes 2719744 | tf_op jit(solution)/shard_map/dot_general | solution.py:137
  (97 shorter events, 14.7 us)
Async XLA Ops:
  6.5 13.8 %copy-start = (bf16[256,4096]{1,0:T(8,128)(2,1)S(1)}, bf16[256,4096]{1,0:T(8,128)(2,1)}, u32[]{:S(2)}) copy-start(bf16[256,4096]{1,0:T(8,128)(2,1)} %param.7) | copy-start | bytes 6291460
  6.5 9.1 %copy-start.2 = (s32[32]{0:T(128)S(1)}, s32[32]{0:T(128)}, u32[]{:S(2)}) copy-start(s32[32]{0:T(128)} %home_ref.3) | copy-start | bytes 388
  6.5 95.4 %reduce-scatter.2.cloned.1.call-start = ((), (), s32[]{:S(2)}) async-start(), calls=%async_computation.1 | async-start | bytes 1572864 | tf_op jit(solution)/shard_map/reduce_scatter | solution.py:115
  10.7 5.0 %copy-start.4 = (bf16[4,4096,64]{1,2,0:T(8,128)(2,1)S(1)}, bf16[4,4096,64]{1,2,0:T(8,128)(2,1)}, u32[]{:S(2)}) copy-start(bf16[4,4096,64]{1,2,0:T(8,128)(2,1)} %param.9) | copy-start | bytes 6291460
  10.7 5.0 %copy-start.6 = (bf16[4,64,1024]{2,1,0:T(8,128)(2,1)S(1)}, bf16[4,64,1024]{2,1,0:T(8,128)(2,1)}, u32[]{:S(2)}) copy-start(bf16[4,64,1024]{2,1,0:T(8,128)(2,1)} %expand_ref.3) | copy-start | bytes 1572868
  10.7 5.0 %copy-start.8 = (s32[8,8]{1,0:T(8,128)S(1)}, s32[8,8]{1,0:T(8,128)}, u32[]{:S(2)}) copy-start(s32[8,8]{1,0:T(8,128)} %fetch_ref.3) | copy-start | bytes 772
  12.3 30.0 %collective-permute-start = (bf16[32,4608]{1,0:T(8,128)(2,1)}, bf16[32,4608]{1,0:T(8,128)(2,1)}, u32[]{:S(2)}, u32[]{:S(2)}) collective-permute-start(bf16[32,4608]{1,0:T(8,128)(2,1)} %get-tuple-element.50), channel_id=1, source_target_pairs={{0,10},{2,8},{4,14},{6,12},{8,2},{10,0},{12,6},{14,4},{1,11},{3,9}... | collective-permute-start | bytes 884744 | tf_op jit(solution)/shard_map/ppermute | solution.py:89
  20.0 7.7 %copy-start.20 = (s32[1,8]{1,0:T(1,128)S(1)}, s32[1,8]{1,0:T(1,128)}, u32[]{:S(2)}) copy-start(s32[1,8]{1,0:T(1,128)} %param.13) | copy-start | bytes 100
  20.0 23.9 %collective-permute-start.1 = (bf16[64,4608]{1,0:T(8,128)(2,1)S(1)}, bf16[64,4608]{1,0:T(8,128)(2,1)}, u32[]{:S(2)}, u32[]{:S(2)}) collective-permute-start(bf16[64,4608]{1,0:T(8,128)(2,1)S(1)} %get-tuple-element.52), channel_id=1, source_target_pairs={{0,2},{2,0},{4,6},{6,4},{8,10},{10,8},{12,14},{14,12},{1,3},{3,1},... | collective-permute-start | bytes 1769480 | tf_op jit(solution)/shard_map/ppermute | solution.py:89
  20.2 21.4 %collective-permute-start.2 = (bf16[32,4608]{1,0:T(8,128)(2,1)}, bf16[32,4608]{1,0:T(8,128)(2,1)}, u32[]{:S(2)}, u32[]{:S(2)}) collective-permute-start(bf16[32,4608]{1,0:T(8,128)(2,1)} %get-tuple-element.55), channel_id=1, source_target_pairs={{0,8},{2,10},{4,12},{6,14},{8,0},{10,2},{12,4},{14,6},{1,9},{3,11}... | collective-permute-start | bytes 884744 | tf_op jit(solution)/shard_map/ppermute | solution.py:89
  27.8 28.3 %copy-start.12 = (bf16[32,4608]{1,0:T(8,128)(2,1)S(1)}, bf16[32,4608]{1,0:T(8,128)(2,1)}, u32[]{:S(2)}) copy-start(bf16[32,4608]{1,0:T(8,128)(2,1)} %copy-done.11) | copy-start | bytes 884740
  27.8 28.3 %copy-start.10 = (bf16[32,4608]{1,0:T(8,128)(2,1)S(1)}, bf16[32,4608]{1,0:T(8,128)(2,1)}, u32[]{:S(2)}) copy-start(bf16[32,4608]{1,0:T(8,128)(2,1)} %copy-done.9) | copy-start | bytes 884740
  41.6 14.6 %collective-permute-start.3 = (bf16[32,4608]{1,0:T(8,128)(2,1)}, bf16[32,4608]{1,0:T(8,128)(2,1)S(1)}, u32[]{:S(2)}, u32[]{:S(2)}) collective-permute-start(bf16[32,4608]{1,0:T(8,128)(2,1)} %copy-done.13), channel_id=1, source_target_pairs={{0,12},{2,14},{4,8},{6,10},{8,4},{10,6},{12,0},{14,2},{1,13},{3,15... | collective-permute-start | bytes 884744 | tf_op jit(solution)/shard_map/ppermute | solution.py:89
  42.3 24.8 %collective-permute-start.7 = (bf16[32,4608]{1,0:T(8,128)(2,1)}, bf16[32,4608]{1,0:T(8,128)(2,1)S(1)}, u32[]{:S(2)}, u32[]{:S(2)}) collective-permute-start(bf16[32,4608]{1,0:T(8,128)(2,1)} %collective-permute-done.2), channel_id=1, source_target_pairs={{0,16},{16,0},{1,17},{17,1},{2,18},{18,2},{3,19},{19,3},{4,20},{20... | collective-permute-start | bytes 884744 | tf_op jit(solution)/shard_map/ppermute | solution.py:92
  43.6 24.2 %collective-permute-start.8 = (bf16[32,4608]{1,0:T(8,128)(2,1)}, bf16[32,4608]{1,0:T(8,128)(2,1)S(1)}, u32[]{:S(2)}, u32[]{:S(2)}) collective-permute-start(bf16[32,4608]{1,0:T(8,128)(2,1)} %collective-permute-done), channel_id=1, source_target_pairs={{0,16},{16,0},{1,17},{17,1},{2,18},{18,2},{3,19},{19,3},{4,20},{20... | collective-permute-start | bytes 884744 | tf_op jit(solution)/shard_map/ppermute | solution.py:92
  56.2 12.5 %collective-permute-start.4 = (bf16[32,4608]{1,0:T(8,128)(2,1)S(1)}, bf16[32,4608]{1,0:T(8,128)(2,1)S(1)}, u32[]{:S(2)}, u32[]{:S(2)}) collective-permute-start(bf16[32,4608]{1,0:T(8,128)(2,1)S(1)} %copy-done.12), channel_id=1, source_target_pairs={{0,4},{2,6},{4,0},{6,2},{8,12},{10,14},{12,8},{14,10},{1,5},{3,7},... | collective-permute-start | bytes 884744 | tf_op jit(solution)/shard_map/ppermute | solution.py:89
  56.2 13.4 %collective-permute-start.5 = (bf16[32,4608]{1,0:T(8,128)(2,1)S(1)}, bf16[32,4608]{1,0:T(8,128)(2,1)S(1)}, u32[]{:S(2)}, u32[]{:S(2)}) collective-permute-start(bf16[32,4608]{1,0:T(8,128)(2,1)S(1)} %copy-done.10), channel_id=1, source_target_pairs={{0,6},{2,4},{4,2},{6,0},{8,14},{10,12},{12,10},{14,8},{1,7},{3,5},... | collective-permute-start | bytes 884744 | tf_op jit(solution)/shard_map/ppermute | solution.py:89
  60.0 16.8 %collective-permute-start.9 = (bf16[32,4608]{1,0:T(8,128)(2,1)S(1)}, bf16[32,4608]{1,0:T(8,128)(2,1)S(1)}, u32[]{:S(2)}, u32[]{:S(2)}) collective-permute-start(bf16[32,4608]{1,0:T(8,128)(2,1)S(1)} %collective-permute-done.3), channel_id=1, source_target_pairs={{0,16},{16,0},{1,17},{17,1},{2,18},{18,2},{3,19},{19,3},{4,20},{20... | collective-permute-start | bytes 884744 | tf_op jit(solution)/shard_map/ppermute | solution.py:92
  69.6 28.9 %collective-permute-start.10 = (bf16[32,4608]{1,0:T(8,128)(2,1)S(1)}, bf16[32,4608]{1,0:T(8,128)(2,1)S(1)}, u32[]{:S(2)}, u32[]{:S(2)}) collective-permute-start(bf16[32,4608]{1,0:T(8,128)(2,1)S(1)} %collective-permute-done.4), channel_id=1, source_target_pairs={{0,16},{16,0},{1,17},{17,1},{2,18},{18,2},{3,19},{19,3},{4,20},{20... | collective-permute-start | bytes 884744 | tf_op jit(solution)/shard_map/ppermute | solution.py:92
  70.8 28.4 %collective-permute-start.11 = (bf16[32,4608]{1,0:T(8,128)(2,1)S(1)}, bf16[32,4608]{1,0:T(8,128)(2,1)S(1)}, u32[]{:S(2)}, u32[]{:S(2)}) collective-permute-start(bf16[32,4608]{1,0:T(8,128)(2,1)S(1)} %collective-permute-done.5), channel_id=1, source_target_pairs={{0,16},{16,0},{1,17},{17,1},{2,18},{18,2},{3,19},{19,3},{4,20},{20... | collective-permute-start | bytes 884744 | tf_op jit(solution)/shard_map/ppermute | solution.py:92
  71.1 4.4 %copy-start.15 = (bf16[16,4608]{1,0:T(8,128)(2,1)S(1)}, bf16[16,4608]{1,0:T(8,128)(2,1)}, u32[]{:S(2)}) copy-start(bf16[16,4608]{1,0:T(8,128)(2,1)} %copy-done.14) | copy-start | bytes 442372
  72.5 20.5 %copy-start.17 = (f32[256,288]{0,1:T(8,128)}, f32[256,288]{0,1:T(8,128)S(1)}, u32[]{:S(2)}) copy-start(f32[256,288]{0,1:T(8,128)S(1)} %fusion.11) | copy-start | bytes 884740
  72.6 29.3 %collective-permute-start.6 = (f32[256,288]{0,1:T(8,128)S(1)}, f32[256,288]{0,1:T(8,128)}, u32[]{:S(2)}, u32[]{:S(2)}) collective-permute-start(f32[256,288]{0,1:T(8,128)S(1)} %fusion.11), channel_id=1, source_target_pairs={{0,1},{1,0},{2,3},{3,2},{4,5},{5,4},{6,7},{7,6},{8,9},{9,8},{10,11... | collective-permute-start | bytes 884744 | tf_op jit(solution)/shard_map/ppermute | solution.py:133
  75.4 12.6 %collective-permute-start.13 = (bf16[16,4608]{1,0:T(8,128)(2,1)S(1)}, bf16[16,4608]{1,0:T(8,128)(2,1)S(1)}, u32[]{:S(2)}, u32[]{:S(2)}) collective-permute-start(bf16[16,4608]{1,0:T(8,128)(2,1)S(1)} %copy-done.15), channel_id=1, source_target_pairs={{0,14},{2,12},{4,10},{6,8},{8,6},{10,4},{12,2},{14,0},{1,15},{3,13... | collective-permute-start | bytes 442376 | tf_op jit(solution)/shard_map/ppermute | solution.py:89
  76.7 16.4 %copy-start.16 = (bf16[288,512]{1,0:T(8,128)(2,1)}, bf16[288,512]{1,0:T(8,128)(2,1)S(1)}, u32[]{:S(2)}) copy-start(bf16[288,512]{1,0:T(8,128)(2,1)S(1)} %constant_dynamic-update-slice_fusion) | copy-start | bytes 884740
  76.8 14.5 %collective-permute-start.14 = (bf16[16,4608]{1,0:T(8,128)(2,1)S(1)}, bf16[16,4608]{1,0:T(8,128)(2,1)S(1)}, u32[]{:S(2)}, u32[]{:S(2)}) collective-permute-start(bf16[16,4608]{1,0:T(8,128)(2,1)S(1)} %get-tuple-element.68), channel_id=1, source_target_pairs={{0,14},{2,12},{4,10},{6,8},{8,6},{10,4},{12,2},{14,0},{1,15},{3,13... | collective-permute-start | bytes 442376 | tf_op jit(solution)/shard_map/ppermute | solution.py:89
  88.1 5.7 %collective-permute-start.15 = (bf16[16,4608]{1,0:T(8,128)(2,1)S(1)}, bf16[16,4608]{1,0:T(8,128)(2,1)S(1)}, u32[]{:S(2)}, u32[]{:S(2)}) collective-permute-start(bf16[16,4608]{1,0:T(8,128)(2,1)S(1)} %collective-permute-done.13), channel_id=1, source_target_pairs={{0,16},{16,0},{1,17},{17,1},{2,18},{18,2},{3,19},{19,3},{4,20},{20... | collective-permute-start | bytes 442376 | tf_op jit(solution)/shard_map/ppermute | solution.py:92
  91.2 4.9 %collective-permute-start.16 = (bf16[16,4608]{1,0:T(8,128)(2,1)S(1)}, bf16[16,4608]{1,0:T(8,128)(2,1)S(1)}, u32[]{:S(2)}, u32[]{:S(2)}) collective-permute-start(bf16[16,4608]{1,0:T(8,128)(2,1)S(1)} %collective-permute-done.14), channel_id=1, source_target_pairs={{0,16},{16,0},{1,17},{17,1},{2,18},{18,2},{3,19},{19,3},{4,20},{20... | collective-permute-start | bytes 442376 | tf_op jit(solution)/shard_map/ppermute | solution.py:92
  93.8 4.7 %copy-start.18 = (bf16[16,4608]{1,0:T(8,128)(2,1)}, bf16[16,4608]{1,0:T(8,128)(2,1)S(1)}, u32[]{:S(2)}) copy-start(bf16[16,4608]{1,0:T(8,128)(2,1)S(1)} %collective-permute-done.15) | copy-start | bytes 442372
  96.2 3.0 %copy-start.19 = (bf16[16,4608]{1,0:T(8,128)(2,1)}, bf16[16,4608]{1,0:T(8,128)(2,1)S(1)}, u32[]{:S(2)}) copy-start(bf16[16,4608]{1,0:T(8,128)(2,1)S(1)} %collective-permute-done.16) | copy-start | bytes 442372
  96.8 3.2 %collective-permute-start.17 = (f32[256,64]{0,1:T(8,128)S(1)}, f32[256,64]{0,1:T(8,128)S(1)}, u32[]{:S(2)}, u32[]{:S(2)}) collective-permute-start(f32[256,64]{0,1:T(8,128)S(1)} %pad_maximum_fusion), channel_id=1, source_target_pairs={{0,1},{1,0},{2,3},{3,2},{4,5},{5,4},{6,7},{7,6},{8,9},{9,8},{10,11... | collective-permute-start | bytes 196616 | tf_op jit(solution)/shard_map/ppermute | solution.py:133
  100.0 1.5 %collective-permute-start.12 = (f32[256,160]{0,1:T(8,128)S(1)}, f32[256,160]{0,1:T(8,128)S(1)}, u32[]{:S(2)}, u32[]{:S(2)}) collective-permute-start(f32[256,160]{0,1:T(8,128)S(1)} %fusion.6), channel_id=1, source_target_pairs={{0,1},{1,0},{2,3},{3,2},{4,5},{5,4},{6,7},{7,6},{8,9},{9,8},{10,11... | collective-permute-start | bytes 491528 | tf_op jit(solution)/shard_map/ppermute | solution.py:133
  (10 other events, 9.4 us)
Sparse Core Ops, SparseCore 0:
  27.1 11.2 reduce-scatter.1

commit v3 on v2

v3 whole, which is shorter than its diff:
```python
import functools
import jax
import jax.numpy as jnp
from jax import lax
from jax.experimental import pallas as pl
from jax.experimental.pallas import tpu as pltpu
from jax.sharding import PartitionSpec as P

adapter_scale = 2.0


def pack_kernel(plan, home_ref, fetch_ref, shrink_ref, expand_ref, *refs):
    outs, sems = refs[:-1], refs[-1]
    me, part, half = lax.axis_index("rep"), lax.axis_index("parts"), lax.axis_index("tp")
    per_home, rank, depth = shrink_ref.shape
    listed = fetch_ref.shape[1]
    columns = outs[0].shape[1] - depth
    left = pl.multiple_of(half * columns, 128)
    copies, slots = [], {}
    for at, (step, first, rows, share) in enumerate(plan):
        peer = me ^ step

        def look(j, slot):
            position = home_ref[fetch_ref[peer, j]]
            return jnp.where(position // per_home == me, position % per_home, slot)

        if step not in slots:
            slots[step] = lax.fori_loop(0, listed, look, jnp.int32(0), unroll=listed <= 8)
        slot = slots[step]
        start = pl.multiple_of(part * share + first, 16)
        for n, (source, target) in enumerate(
            (
                (shrink_ref.at[slot, pl.ds(start, rows), :], outs[at].at[:, pl.ds(0, depth)]),
                (
                    expand_ref.at[slot, pl.ds(start, rows), pl.ds(left, columns)],
                    outs[at].at[:, pl.ds(depth, columns)],
                ),
            )
        ):
            copy = pltpu.make_async_copy(source, target, sems.at[at, n])
            copy.start()
            copies.append(copy)
    for copy in copies:
        copy.wait()


def pack(plan, columns, adapter_home, fetch_list, panels, expand_panels):
    width = panels.shape[2] + columns
    size = 2 * width * sum(rows for _, _, rows, _ in plan)
    return pl.pallas_call(
        functools.partial(pack_kernel, plan),
        out_shape=[jax.ShapeDtypeStruct((rows, width), panels.dtype) for _, _, rows, _ in plan],
        in_specs=[pl.BlockSpec(memory_space=pltpu.SMEM)] * 2 + [pl.BlockSpec(memory_space=pl.ANY)] * 2,
        out_specs=[pl.BlockSpec(memory_space=pltpu.VMEM)] * len(plan),
        scratch_shapes=[pltpu.SemaphoreType.DMA((len(plan), 2))],
        compiler_params=pltpu.CompilerParams(vmem_limit_bytes=56 << 20),
        cost_estimate=pl.CostEstimate(flops=0, bytes_accessed=2 * size, transcendentals=0),
    )(adapter_home, fetch_list, panels, expand_panels)


def on_device(tokens, base_weight, shrink_panels, expand_panels, adapter_home, fetch_list, seg_len):
    per_home, depth, rank = shrink_panels.shape
    replicas, parts, cores = lax.axis_size("rep"), lax.axis_size("parts"), lax.axis_size("tp")
    me = lax.axis_index("rep")
    tok_count = tokens.shape[0]
    columns = expand_panels.shape[2] // cores
    panels = jnp.swapaxes(shrink_panels, 1, 2)
    share = rank // parts

    half = replicas // 2
    cut = max(16, share // 2)
    far = [(step, 0, share, share) for step in range(half, replicas - 1)]
    far += [(replicas - 1, first, cut, share) for first in range(0, share, cut)]
    near = [(step, 0, share, share) for step in range(2, half)]
    plan = far + near + [(1, 0, rank, 0), (0, 0, rank, 0)]
    send = pack(plan, columns, adapter_home, fetch_list, panels, expand_panels)
    tokens, send = lax.optimization_barrier((tokens, list(send)))
    far_send, near_send = send[: len(far)], send[len(far) : -2]
    whole_send, own = send[-2:]

    def hop(x, step):
        return lax.ppermute(x, "rep", [(i, i ^ step) for i in range(replicas)])

    def across(x):
        return [
            lax.ppermute(x, "parts", [(i, (i + shift) % parts) for i in range(parts)])
            for shift in range(1, parts)
        ]

    def trade(x):
        for shift in range(1, cores):
            x = x + lax.ppermute(x, "tp", [(i, (i + shift) % cores) for i in range(cores)])
        return x

    stored = jnp.take(adapter_home, lax.dynamic_index_in_dim(fetch_list, me, 0, keepdims=False))
    owners = stored // per_home
    lengths = seg_len[0]
    ordinal = jnp.arange(lengths.shape[0])
    starts = jnp.sum(jnp.where(ordinal[None, :] < ordinal[:, None], lengths[None, :], 0), axis=1)
    rows = jnp.arange(tok_count, dtype=jnp.int32)
    member = (rows[:, None] >= starts[None, :]) & (rows[:, None] < (starts + lengths)[None, :])
    row_owner = jnp.sum(jnp.where(member, owners[None, :], 0), axis=1)

    def score(block, step, tokens):
        product = lax.dot_general(
            tokens, block[:, :depth], (((1,), (1,)), ((), ())), preferred_element_type=jnp.float32
        )
        return jnp.where((row_owner == (me ^ step))[:, None], product, 0.0)

    def spread(scores, blocks):
        return jnp.dot(
            trade(jnp.concatenate(scores, axis=1)),
            jnp.concatenate([block[:, depth:] for block in blocks], axis=0).astype(jnp.float32),
            precision=lax.Precision.HIGHEST,
            preferred_element_type=jnp.float32,
        )

    tie = lax.optimization_barrier
    window = 2
    far_recv = [hop(far_send[at], far[at][0]) for at in range(window)]
    near_recv = [hop(near_send[0], near[0][0])]
    for at in range(window, len(far)):
        block = far_send[at]
        before = at - window
        if before < len(near):
            block, near_recv[before] = tie((block, near_recv[before]))
        if at == len(far) - 1:
            block, far_recv[before:] = tie((block, far_recv[before:]))
        else:
            block, far_recv[before] = tie((block, far_recv[before]))
        far_recv.append(hop(block, far[at][0]))
        if before + 1 < len(near):
            block, near_recv[before] = tie((near_send[before + 1], near_recv[before]))
            near_recv.append(hop(block, near[before + 1][0]))
    whole_send, near_recv[-1] = tie((whole_send, near_recv[-1]))
    whole = hop(whole_send, 1)

    arrived = [(x, step) for x, (step, *_) in zip(far_recv, far)]
    arrived_near = [(x, step) for x, (step, *_) in zip(near_recv, near)]
    arrived = arrived_near[:1] + arrived[:window] + arrived_near[1:] + arrived[window:]
    base_part = jnp.dot(tokens, base_weight, preferred_element_type=jnp.float32)
    base = lax.psum_scatter(base_part, "tp", scatter_dimension=1, tiled=True)

    done_scores, done_blocks, passed = [], [], []

    def multiply(blocks, step):
        for block in blocks:
            done_scores.append(score(block, step, tokens))
            done_blocks.append(block)

    multiply([own], 0)
    for at, (block, step) in enumerate(arrived):
        if at >= window:
            block, passed[at - window] = tie((block, passed[at - window]))
        block, done_scores = tie((block, done_scores))
        passed.append(across(block))
        multiply([block], step)
        if at >= window:
            multiply(passed[at - window], arrived[at - window][1])
        if at == len(arrived) - 2:
            multiply([whole], 1)
    for at in range(len(arrived) - window, len(arrived) - 1):
        multiply(passed[at], arrived[at][1])
    done_scores = tie(done_scores)
    total = base + adapter_scale * spread(done_scores, done_blocks)
    tokens, total = tie((tokens, total))
    last = [score(block, arrived[-1][1], tokens) for block in passed[-1]]
    total = total + adapter_scale * spread(last, passed[-1])
    return total.astype(jnp.bfloat16)


def solution(mesh):
    return jax.shard_map(
        on_device,
        mesh=mesh,
        in_specs=(
            P(("parts", "rep"), "tp"),
            P("tp", None),
            P("rep", "tp", None),
            P("rep", None, None),
            P(),
            P(),
            P(("parts", "rep"), None),
        ),
        out_specs=P(("parts", "rep"), "tp"),
        check_vma=False,
    )
```

time: 112 us -> 98.9 us (0.88)
  the two profiles are of different devices: /device:TPU:9 before, /device:TPU:0 now
where the time goes in v3:
time: 98.9 us; the launch traced here: 97.7 us
  starting transfers between devices  29.9 us (30%)
  matrix products  23.2 us (23%)
  waiting for transfers between devices  20.6 us (21%)
  between operations  13.9 us (14%)
  Pallas kernels  4.57 us (5%)
  local copies, waits for them, and re-layouts  3.07 us (3%)
  other arithmetic  2.41 us (2%)
    ppermute x8, starting transfers between devices, hop(): return lax.ppermute(x, 'rep', [(i, i ^ step) for i in range(replicas)])  19 us
    dot_general x16, matrix products, score(): lax.dot_general(tokens, block[:, :depth], (((1,), (1,)), ((), ())), prefe...  14.2 us
    ppermute x8, waiting for transfers between devices, hop(): return lax.ppermute(x, 'rep', [(i, i ^ step) for i in range(replicas)])  12.9 us
    ppermute x7, starting transfers between devices, across(): lax.ppermute(x, 'parts', [(i, (i + shift) % parts) for i in range(parts)])  10.7 us
    dot_general x1, matrix products, on_device(): base_part = jnp.dot(tokens, base_weight, preferred_element_type=jnp.float32)  6.71 us
    ppermute x7, waiting for transfers between devices, across(): lax.ppermute(x, 'parts', [(i, (i + shift) % parts) for i in range(parts)])  5.4 us
    pallas_call x1, Pallas kernels, pack(): pl.pallas_call(functools.partial(pack_kernel, plan), out_shape=[jax.Shape...  4.57 us
    unnamed x44, local copies, waits for them, and re-layouts  2.42 us
  transfers between devices with their start and end apart: 18, of which 7 were waited for; matrix products, arithmetic and copies ran while one was open for 27% of the time, Pallas kernels for 0%

profile of v3, /device:TPU:0, one launch (start us, length us, event | category | flops | bytes accessed | tf_op | source)
XLA Modules:
  0.0 97.7 jit_solution(17915521271999679404)
XLA Ops:
  6.5 4.6 %shard_map.73 = (bf16[32,4608]{1,0:T(8,128)(2,1)}, bf16[32,4608]{1,0:T(8,128)(2,1)}, bf16[32,4608]{1,0:T(8,128)(2,1)}, bf16[16,4608]{1,0:T(8,128)(2,1)}, bf16[16...) custom-call(s32[32]{0:T(128)} %home_ref.1, ...), custom_call_target="tpu_custom_call" | custom-call | bytes 5898240 | tf_op jit(solution)/shard_map/pallas_call | solution.py:50
  11.2 3.1 %collective-permute-start = (bf16[32,4608]{1,0:T(8,128)(2,1)}, bf16[32,4608]{1,0:T(8,128)(2,1)}, u32[]{:S(2)}, u32[]{:S(2)}) collective-permute-start(bf16[32,4608]{1,0:T(8,128)(2,1)} %get-tuple-element.124), channel_id=1, source_target_pairs={{0,4},{2,6},{4,0},{6,2},{8,12},{10,14},{12,8},{14,10},{1,5},{3,7},... | collective-permute-start | bytes 884744 | tf_op jit(solution)/shard_map/ppermute | solution.py:82
  14.2 2.7 %collective-permute-start.1 = (bf16[32,4608]{1,0:T(8,128)(2,1)}, bf16[32,4608]{1,0:T(8,128)(2,1)}, u32[]{:S(2)}, u32[]{:S(2)}) collective-permute-start(bf16[32,4608]{1,0:T(8,128)(2,1)} %get-tuple-element.126), channel_id=1, source_target_pairs={{0,8},{2,10},{4,12},{6,14},{8,0},{10,2},{12,4},{14,6},{1,9},{3,11}... | collective-permute-start | bytes 884744 | tf_op jit(solution)/shard_map/ppermute | solution.py:82
  17.0 1.2 %collective-permute-start.4 = (bf16[32,4608]{1,0:T(8,128)(2,1)}, bf16[32,4608]{1,0:T(8,128)(2,1)S(1)}, u32[]{:S(2)}, u32[]{:S(2)}) collective-permute-start(bf16[32,4608]{1,0:T(8,128)(2,1)} %get-tuple-element.133), channel_id=1, source_target_pairs={{0,10},{2,8},{4,14},{6,12},{8,2},{10,0},{12,6},{14,4},{1,11},{3,9}... | collective-permute-start | bytes 884744 | tf_op jit(solution)/shard_map/ppermute | solution.py:82
  18.1 6.7 %fusion.24 = f32[256,1024]{1,0:T(8,128)} fusion(bf16[256,4096]{1,0:T(8,128)(2,1)S(1)} %copy-done, bf16[4096,1024]{1,0:T(8,128)(2,1)} %param.8), kind=kOutput, calls=%fused_computation.97 | convolution fusion | flops 2147483648 | bytes 11534336 | tf_op jit(solution)/shard_map/dot_general | solution.py:141
  27.2 0.8 convolution_select_fusion.1
  28.0 1.6 %collective-permute-start.7 = (bf16[32,4608]{1,0:T(8,128)(2,1)}, bf16[32,4608]{1,0:T(8,128)(2,1)S(1)}, u32[]{:S(2)}, u32[]{:S(2)}) collective-permute-start(bf16[32,4608]{1,0:T(8,128)(2,1)} %collective-permute-done), channel_id=1, source_target_pairs={{0,16},{16,0},{1,17},{17,1},{2,18},{18,2},{3,19},{19,3},{4,20},{20... | collective-permute-start | bytes 884744 | tf_op jit(solution)/shard_map/ppermute | solution.py:86
  30.0 1.7 %convolution_select_fusion.11 = f32[256,32]{0,1:T(8,128)S(1)} fusion(bf16[256,4096]{1,0:T(8,128)(2,1)S(1)} %copy-done, bf16[32,4608]{1,0:T(8,128)(2,1)} %collective-permute-done, pred[256]{0:T(512)(128)(4,1)S(1)} %get-tuple-element.225), kind=kOutput, calls=%fused_computation.15 | convolution fusion | flops 67117056 | bytes 2392320 | tf_op jit(solution)/shard_map/dot_general | solution.py:105
  31.8 6.4 %collective-permute-done.1 = bf16[32,4608]{1,0:T(8,128)(2,1)} collective-permute-done((bf16[32,4608]{1,0:T(8,128)(2,1)}, bf16[32,4608]{1,0:T(8,128)(2,1)}, u32[]{:S(2)}, u32[]{:S(2)}) %collective-permute-start.1) | collective-permute-done | bytes 294944 | tf_op jit(solution)/shard_map/ppermute | solution.py:82
  38.1 1.5 %collective-permute-start.9 = (bf16[32,4608]{1,0:T(8,128)(2,1)}, bf16[32,4608]{1,0:T(8,128)(2,1)S(1)}, u32[]{:S(2)}, u32[]{:S(2)}) collective-permute-start(bf16[32,4608]{1,0:T(8,128)(2,1)} %collective-permute-done.1), channel_id=1, source_target_pairs={{0,16},{16,0},{1,17},{17,1},{2,18},{18,2},{3,19},{19,3},{4,20},{20... | collective-permute-start | bytes 884744 | tf_op jit(solution)/shard_map/ppermute | solution.py:86
  39.6 1.7 %convolution_select_fusion.10 = f32[256,32]{0,1:T(8,128)S(1)} fusion(bf16[256,4096]{1,0:T(8,128)(2,1)S(1)} %copy-done, bf16[32,4608]{1,0:T(8,128)(2,1)} %collective-permute-done.1, pred[256]{0:T(512)(128)(4,1)S(1)} %get-tuple-element.224), kind=kOutput, calls=%fused_computation.14 | convolution fusion | flops 67117056 | bytes 2392320 | tf_op jit(solution)/shard_map/dot_general | solution.py:105
  41.3 0.8 constant_dynamic-update-slice_fusion.27
  42.1 0.8 constant_dynamic-update-slice_fusion.26
  42.9 2.5 %collective-permute-start.2 = (bf16[32,4608]{1,0:T(8,128)(2,1)S(1)}, bf16[32,4608]{1,0:T(8,128)(2,1)S(1)}, u32[]{:S(2)}, u32[]{:S(2)}) collective-permute-start(bf16[32,4608]{1,0:T(8,128)(2,1)S(1)} %copy-done.5), channel_id=1, source_target_pairs={{0,12},{2,14},{4,8},{6,10},{8,4},{10,6},{12,0},{14,2},{1,13},{3,15... | collective-permute-start | bytes 884744 | tf_op jit(solution)/shard_map/ppermute | solution.py:82
  45.4 1.9 %collective-permute-done.3 = bf16[32,4608]{1,0:T(8,128)(2,1)S(1)} collective-permute-done((bf16[32,4608]{1,0:T(8,128)(2,1)}, bf16[32,4608]{1,0:T(8,128)(2,1)S(1)}, u32[]{:S(2)}, u32[]{:S(2)}) %collective-permute-start.3) | collective-permute-done | bytes 294944 | tf_op jit(solution)/shard_map/ppermute | solution.py:82
  47.3 1.2 %collective-permute-done.4 = bf16[32,4608]{1,0:T(8,128)(2,1)S(1)} collective-permute-done((bf16[32,4608]{1,0:T(8,128)(2,1)}, bf16[32,4608]{1,0:T(8,128)(2,1)S(1)}, u32[]{:S(2)}, u32[]{:S(2)}) %collective-permute-start.4) | collective-permute-done | bytes 294944 | tf_op jit(solution)/shard_map/ppermute | solution.py:82
  48.4 0.7 convolution_select_fusion.6
  49.2 4.7 %collective-permute-start.8 = (bf16[32,4608]{1,0:T(8,128)(2,1)S(1)}, bf16[32,4608]{1,0:T(8,128)(2,1)S(1)}, u32[]{:S(2)}, u32[]{:S(2)}) collective-permute-start(bf16[32,4608]{1,0:T(8,128)(2,1)S(1)} %collective-permute-done.4), channel_id=1, source_target_pairs={{0,16},{16,0},{1,17},{17,1},{2,18},{18,2},{3,19},{19,3},{4,20},{20... | collective-permute-start | bytes 884744 | tf_op jit(solution)/shard_map/ppermute | solution.py:86
  54.6 0.7 convolution_select_fusion.9
  56.2 4.5 %collective-permute-start.5 = (bf16[16,4608]{1,0:T(8,128)(2,1)S(1)}, bf16[16,4608]{1,0:T(8,128)(2,1)S(1)}, u32[]{:S(2)}, u32[]{:S(2)}) collective-permute-start(bf16[16,4608]{1,0:T(8,128)(2,1)S(1)} %copy-done.7), channel_id=1, source_target_pairs={{0,14},{2,12},{4,10},{6,8},{8,6},{10,4},{12,2},{14,0},{1,15},{3,13... | collective-permute-start | bytes 442376 | tf_op jit(solution)/shard_map/ppermute | solution.py:82
  60.7 3.5 %collective-permute-done.5 = bf16[16,4608]{1,0:T(8,128)(2,1)S(1)} collective-permute-done((bf16[16,4608]{1,0:T(8,128)(2,1)S(1)}, bf16[16,4608]{1,0:T(8,128)(2,1)S(1)}, u32[]{:S(2)}, u32[]{:S(2)}) %collective-permute-start.5) | collective-permute-done | bytes 147488 | tf_op jit(solution)/shard_map/ppermute | solution.py:82
  64.2 4.5 %collective-permute-start.6 = (bf16[16,4608]{1,0:T(8,128)(2,1)S(1)}, bf16[16,4608]{1,0:T(8,128)(2,1)}, u32[]{:S(2)}, u32[]{:S(2)}) collective-permute-start(bf16[16,4608]{1,0:T(8,128)(2,1)S(1)} %copy-done.6), channel_id=1, source_target_pairs={{0,14},{2,12},{4,10},{6,8},{8,6},{10,4},{12,2},{14,0},{1,15},{3,13... | collective-permute-start | bytes 442376 | tf_op jit(solution)/shard_map/ppermute | solution.py:82
  70.7 0.7 convolution_select_fusion.5
  71.5 1.6 %collective-permute-start.13 = (bf16[16,4608]{1,0:T(8,128)(2,1)S(1)}, bf16[16,4608]{1,0:T(8,128)(2,1)S(1)}, u32[]{:S(2)}, u32[]{:S(2)}) collective-permute-start(bf16[16,4608]{1,0:T(8,128)(2,1)S(1)} %collective-permute-done.5), channel_id=1, source_target_pairs={{0,16},{16,0},{1,17},{17,1},{2,18},{18,2},{3,19},{19,3},{4,20},{20... | collective-permute-start | bytes 442376 | tf_op jit(solution)/shard_map/ppermute | solution.py:86
  73.8 5.4 %collective-permute-done.13 = bf16[16,4608]{1,0:T(8,128)(2,1)S(1)} collective-permute-done((bf16[16,4608]{1,0:T(8,128)(2,1)S(1)}, bf16[16,4608]{1,0:T(8,128)(2,1)S(1)}, u32[]{:S(2)}, u32[]{:S(2)}) %collective-permute-start.13) | collective-permute-done | bytes 147488 | tf_op jit(solution)/shard_map/ppermute | solution.py:86
  79.8 0.8 convolution_select_fusion
  80.6 1.5 %convolution_select_fusion.14 = f32[256,16]{0,1:T(8,128)S(1)} fusion(bf16[256,4096]{1,0:T(8,128)(2,1)S(1)} %copy-done, bf16[16,4608]{1,0:T(8,128)(2,1)} %collective-permute-done.6, pred[256]{0:T(512)(128)(4,1)S(1)} %get-tuple-element.220), kind=kOutput, calls=%fused_computation.18 | convolution fusion | flops 33558528 | bytes 2244864 | tf_op jit(solution)/shard_map/dot_general | solution.py:105
  82.1 0.8 collective-permute-start.15
  84.6 1.3 %collective-permute-done.14 = f32[256,496]{0,1:T(8,128)} collective-permute-done((f32[256,496]{0,1:T(8,128)S(1)}, f32[256,496]{0,1:T(8,128)}, u32[]{:S(2)}, u32[]{:S(2)}) %collective-permute-start.14) | collective-permute-done | bytes 507936 | tf_op jit(solution)/shard_map/ppermute | solution.py:92
  85.9 1.9 %fusion = f32[256,512]{1,0:T(8,128)S(1)} fusion(f32[256,512]{1,0:T(8,128)} %reduce-scatter.2.cloned.1.call-done, bf16[496,512]{1,0:T(8,128)(2,1)S(1)} %constant_dynamic-update-slice_fusion.15, f32[256,496]{0,1:T(8,128)S(1)} %constant_dynamic-update-slice_fusion, f32[256,496]{0,1:T(8,128)} %collective-permute-done.14), kind=kOutput, calls=%fused_computation.3 | convolution fusion | flops 780529664 | bytes 2572288 | tf_op jit(solution)/shard_map/dot_general | solution.py:111
  88.6 1.0 %collective-permute-done.16 = f32[256,16]{0,1:T(8,128)S(1)} collective-permute-done((f32[256,16]{0,1:T(8,128)S(1)}, f32[256,16]{0,1:T(8,128)S(1)}, u32[]{:S(2)}, u32[]{:S(2)}) %collective-permute-start.16) | collective-permute-done | bytes 16416 | tf_op jit(solution)/shard_map/ppermute | solution.py:92
  90.1 0.8 add_convert_fusion
  (79 shorter events, 10.6 us)
Async XLA Ops:
  6.5 11.6 %copy-start = (bf16[256,4096]{1,0:T(8,128)(2,1)S(1)}, bf16[256,4096]{1,0:T(8,128)(2,1)}, u32[]{:S(2)}) copy-start(bf16[256,4096]{1,0:T(8,128)(2,1)} %param.7) | copy-start | bytes 6291460
  6.5 79.4 %reduce-scatter.2.cloned.1.call-start = ((), (), s32[]{:S(2)}) async-start(), calls=%async_computation.1 | async-start | bytes 1572864 | tf_op jit(solution)/shard_map/reduce_scatter | solution.py:142
  11.1 13.7 %copy-start.3 = (s32[1,8]{1,0:T(1,128)S(1)}, s32[1,8]{1,0:T(1,128)}, u32[]{:S(2)}) copy-start(s32[1,8]{1,0:T(1,128)} %param.13) | copy-start | bytes 100
  11.1 14.6 %copy-start.1 = (s32[32]{0:T(128)S(1)}, s32[32]{0:T(128)}, u32[]{:S(2)}) copy-start(s32[32]{0:T(128)} %home_ref.1) | copy-start | bytes 388
  11.1 16.0 %copy-start.2 = (bf16[64,4608]{1,0:T(8,128)(2,1)S(1)}, bf16[64,4608]{1,0:T(8,128)(2,1)}, u32[]{:S(2)}) copy-start(bf16[64,4608]{1,0:T(8,128)(2,1)} %get-tuple-element.139) | copy-start | bytes 1769476
  11.2 16.8 %collective-permute-start = (bf16[32,4608]{1,0:T(8,128)(2,1)}, bf16[32,4608]{1,0:T(8,128)(2,1)}, u32[]{:S(2)}, u32[]{:S(2)}) collective-permute-start(bf16[32,4608]{1,0:T(8,128)(2,1)} %get-tuple-element.124), channel_id=1, source_target_pairs={{0,4},{2,6},{4,0},{6,2},{8,12},{10,14},{12,8},{14,10},{1,5},{3,7},... | collective-permute-start | bytes 884744 | tf_op jit(solution)/shard_map/ppermute | solution.py:82
  14.2 23.9 %collective-permute-start.1 = (bf16[32,4608]{1,0:T(8,128)(2,1)}, bf16[32,4608]{1,0:T(8,128)(2,1)}, u32[]{:S(2)}, u32[]{:S(2)}) collective-permute-start(bf16[32,4608]{1,0:T(8,128)(2,1)} %get-tuple-element.126), channel_id=1, source_target_pairs={{0,8},{2,10},{4,12},{6,14},{8,0},{10,2},{12,4},{14,6},{1,9},{3,11}... | collective-permute-start | bytes 884744 | tf_op jit(solution)/shard_map/ppermute | solution.py:82
  17.0 31.4 %collective-permute-start.4 = (bf16[32,4608]{1,0:T(8,128)(2,1)}, bf16[32,4608]{1,0:T(8,128)(2,1)S(1)}, u32[]{:S(2)}, u32[]{:S(2)}) collective-permute-start(bf16[32,4608]{1,0:T(8,128)(2,1)} %get-tuple-element.133), channel_id=1, source_target_pairs={{0,10},{2,8},{4,14},{6,12},{8,2},{10,0},{12,6},{14,4},{1,11},{3,9}... | collective-permute-start | bytes 884744 | tf_op jit(solution)/shard_map/ppermute | solution.py:82
  28.0 21.2 %collective-permute-start.7 = (bf16[32,4608]{1,0:T(8,128)(2,1)}, bf16[32,4608]{1,0:T(8,128)(2,1)S(1)}, u32[]{:S(2)}, u32[]{:S(2)}) collective-permute-start(bf16[32,4608]{1,0:T(8,128)(2,1)} %collective-permute-done), channel_id=1, source_target_pairs={{0,16},{16,0},{1,17},{17,1},{2,18},{18,2},{3,19},{19,3},{4,20},{20... | collective-permute-start | bytes 884744 | tf_op jit(solution)/shard_map/ppermute | solution.py:86
  29.5 17.7 %collective-permute-start.3 = (bf16[32,4608]{1,0:T(8,128)(2,1)}, bf16[32,4608]{1,0:T(8,128)(2,1)S(1)}, u32[]{:S(2)}, u32[]{:S(2)}) collective-permute-start(bf16[32,4608]{1,0:T(8,128)(2,1)} %get-tuple-element.131), channel_id=1, source_target_pairs={{0,6},{2,4},{4,2},{6,0},{8,14},{10,12},{12,10},{14,8},{1,7},{3,5},... | collective-permute-start | bytes 884744 | tf_op jit(solution)/shard_map/ppermute | solution.py:82
  30.0 12.8 %copy-start.5 = (bf16[32,4608]{1,0:T(8,128)(2,1)S(1)}, bf16[32,4608]{1,0:T(8,128)(2,1)}, u32[]{:S(2)}) copy-start(bf16[32,4608]{1,0:T(8,128)(2,1)} %get-tuple-element.127) | copy-start | bytes 884740
  38.1 9.1 %collective-permute-start.9 = (bf16[32,4608]{1,0:T(8,128)(2,1)}, bf16[32,4608]{1,0:T(8,128)(2,1)S(1)}, u32[]{:S(2)}, u32[]{:S(2)}) collective-permute-start(bf16[32,4608]{1,0:T(8,128)(2,1)} %collective-permute-done.1), channel_id=1, source_target_pairs={{0,16},{16,0},{1,17},{17,1},{2,18},{18,2},{3,19},{19,3},{4,20},{20... | collective-permute-start | bytes 884744 | tf_op jit(solution)/shard_map/ppermute | solution.py:86
  42.9 17.8 %collective-permute-start.2 = (bf16[32,4608]{1,0:T(8,128)(2,1)S(1)}, bf16[32,4608]{1,0:T(8,128)(2,1)S(1)}, u32[]{:S(2)}, u32[]{:S(2)}) collective-permute-start(bf16[32,4608]{1,0:T(8,128)(2,1)S(1)} %copy-done.5), channel_id=1, source_target_pairs={{0,12},{2,14},{4,8},{6,10},{8,4},{10,6},{12,0},{14,2},{1,13},{3,15... | collective-permute-start | bytes 884744 | tf_op jit(solution)/shard_map/ppermute | solution.py:82
  49.2 20.3 %collective-permute-start.8 = (bf16[32,4608]{1,0:T(8,128)(2,1)S(1)}, bf16[32,4608]{1,0:T(8,128)(2,1)S(1)}, u32[]{:S(2)}, u32[]{:S(2)}) collective-permute-start(bf16[32,4608]{1,0:T(8,128)(2,1)S(1)} %collective-permute-done.4), channel_id=1, source_target_pairs={{0,16},{16,0},{1,17},{17,1},{2,18},{18,2},{3,19},{19,3},{4,20},{20... | collective-permute-start | bytes 884744 | tf_op jit(solution)/shard_map/ppermute | solution.py:86
  54.6 1.6 %copy-start.7 = (bf16[16,4608]{1,0:T(8,128)(2,1)S(1)}, bf16[16,4608]{1,0:T(8,128)(2,1)}, u32[]{:S(2)}) copy-start(bf16[16,4608]{1,0:T(8,128)(2,1)} %get-tuple-element.134) | copy-start | bytes 442372
  54.6 6.1 %copy-start.4 = (bf16[64,4608]{1,0:T(8,128)(2,1)S(1)}, bf16[64,4608]{1,0:T(8,128)(2,1)}, u32[]{:S(2)}) copy-start(bf16[64,4608]{1,0:T(8,128)(2,1)} %get-tuple-element.187) | copy-start | bytes 1769476
  54.6 9.6 %copy-start.6 = (bf16[16,4608]{1,0:T(8,128)(2,1)S(1)}, bf16[16,4608]{1,0:T(8,128)(2,1)}, u32[]{:S(2)}) copy-start(bf16[16,4608]{1,0:T(8,128)(2,1)} %get-tuple-element.135) | copy-start | bytes 442372
  55.3 13.4 %collective-permute-start.11 = (bf16[32,4608]{1,0:T(8,128)(2,1)S(1)}, bf16[32,4608]{1,0:T(8,128)(2,1)S(1)}, u32[]{:S(2)}, u32[]{:S(2)}) collective-permute-start(bf16[32,4608]{1,0:T(8,128)(2,1)S(1)} %collective-permute-done.3), channel_id=1, source_target_pairs={{0,16},{16,0},{1,17},{17,1},{2,18},{18,2},{3,19},{19,3},{4,20},{20... | collective-permute-start | bytes 884744 | tf_op jit(solution)/shard_map/ppermute | solution.py:86
  56.2 8.0 %collective-permute-start.5 = (bf16[16,4608]{1,0:T(8,128)(2,1)S(1)}, bf16[16,4608]{1,0:T(8,128)(2,1)S(1)}, u32[]{:S(2)}, u32[]{:S(2)}) collective-permute-start(bf16[16,4608]{1,0:T(8,128)(2,1)S(1)} %copy-done.7), channel_id=1, source_target_pairs={{0,14},{2,12},{4,10},{6,8},{8,6},{10,4},{12,2},{14,0},{1,15},{3,13... | collective-permute-start | bytes 442376 | tf_op jit(solution)/shard_map/ppermute | solution.py:82
  60.7 19.1 %collective-permute-start.12 = (bf16[64,4608]{1,0:T(8,128)(2,1)S(1)}, bf16[64,4608]{1,0:T(8,128)(2,1)S(1)}, u32[]{:S(2)}, u32[]{:S(2)}) collective-permute-start(bf16[64,4608]{1,0:T(8,128)(2,1)S(1)} %copy-done.4), channel_id=1, source_target_pairs={{0,2},{2,0},{4,6},{6,4},{8,10},{10,8},{12,14},{14,12},{1,3},{3,1},... | collective-permute-start | bytes 1769480 | tf_op jit(solution)/shard_map/ppermute | solution.py:82
  64.2 15.6 %collective-permute-start.6 = (bf16[16,4608]{1,0:T(8,128)(2,1)S(1)}, bf16[16,4608]{1,0:T(8,128)(2,1)}, u32[]{:S(2)}, u32[]{:S(2)}) collective-permute-start(bf16[16,4608]{1,0:T(8,128)(2,1)S(1)} %copy-done.6), channel_id=1, source_target_pairs={{0,14},{2,12},{4,10},{6,8},{8,6},{10,4},{12,2},{14,0},{1,15},{3,13... | collective-permute-start | bytes 442376 | tf_op jit(solution)/shard_map/ppermute | solution.py:82
  69.4 10.3 %collective-permute-start.10 = (bf16[32,4608]{1,0:T(8,128)(2,1)S(1)}, bf16[32,4608]{1,0:T(8,128)(2,1)S(1)}, u32[]{:S(2)}, u32[]{:S(2)}) collective-permute-start(bf16[32,4608]{1,0:T(8,128)(2,1)S(1)} %collective-permute-done.2), channel_id=1, source_target_pairs={{0,16},{16,0},{1,17},{17,1},{2,18},{18,2},{3,19},{19,3},{4,20},{20... | collective-permute-start | bytes 884744 | tf_op jit(solution)/shard_map/ppermute | solution.py:86
  71.5 7.7 %collective-permute-start.13 = (bf16[16,4608]{1,0:T(8,128)(2,1)S(1)}, bf16[16,4608]{1,0:T(8,128)(2,1)S(1)}, u32[]{:S(2)}, u32[]{:S(2)}) collective-permute-start(bf16[16,4608]{1,0:T(8,128)(2,1)S(1)} %collective-permute-done.5), channel_id=1, source_target_pairs={{0,16},{16,0},{1,17},{17,1},{2,18},{18,2},{3,19},{19,3},{4,20},{20... | collective-permute-start | bytes 442376 | tf_op jit(solution)/shard_map/ppermute | solution.py:86
  82.1 5.6 %collective-permute-start.15 = (bf16[16,4608]{1,0:T(8,128)(2,1)}, bf16[16,4608]{1,0:T(8,128)(2,1)S(1)}, u32[]{:S(2)}, u32[]{:S(2)}) collective-permute-start(bf16[16,4608]{1,0:T(8,128)(2,1)} %collective-permute-done.6), channel_id=1, source_target_pairs={{0,16},{16,0},{1,17},{17,1},{2,18},{18,2},{3,19},{19,3},{4,20},{20... | collective-permute-start | bytes 442376 | tf_op jit(solution)/shard_map/ppermute | solution.py:86
  83.8 2.1 %collective-permute-start.14 = (f32[256,496]{0,1:T(8,128)S(1)}, f32[256,496]{0,1:T(8,128)}, u32[]{:S(2)}, u32[]{:S(2)}) collective-permute-start(f32[256,496]{0,1:T(8,128)S(1)} %constant_dynamic-update-slice_fusion), channel_id=1, source_target_pairs={{0,1},{1,0},{2,3},{3,2},{4,5},{5,4},{6,7},{7,6},{8,9},{9,8},{10,11... | collective-permute-start | bytes 1523720 | tf_op jit(solution)/shard_map/ppermute | solution.py:92
  88.4 1.2 %collective-permute-start.16 = (f32[256,16]{0,1:T(8,128)S(1)}, f32[256,16]{0,1:T(8,128)S(1)}, u32[]{:S(2)}, u32[]{:S(2)}) collective-permute-start(f32[256,16]{0,1:T(8,128)S(1)} %convolution_select_fusion.12), channel_id=1, source_target_pairs={{0,1},{1,0},{2,3},{3,2},{4,5},{5,4},{6,7},{7,6},{8,9},{9,8},{10,11... | collective-permute-start | bytes 49160 | tf_op jit(solution)/shard_map/ppermute | solution.py:92
Sparse Core Ops, SparseCore 0:
  25.0 7.9 reduce-scatter.1

commit v4 on v1

v4 whole, which is shorter than its diff:
```python
import functools
import jax
import jax.numpy as jnp
from jax import lax
from jax.experimental import pallas as pl
from jax.experimental.pallas import tpu as pltpu
from jax.sharding import PartitionSpec as P

adapter_scale = 2.0


def pack_kernel(groups, home_ref, fetch_ref, shrink_ref, expand_ref, *refs):
    outs, sems = refs[:-1], refs[-1]
    me, part, half = lax.axis_index("rep"), lax.axis_index("parts"), lax.axis_index("tp")
    per_home = shrink_ref.shape[0]
    listed = fetch_ref.shape[1]
    copies = []
    for at, (group, kind) in enumerate(groups):
        step = jnp.int32(group[0])
        for p, other in enumerate(group):
            step = jnp.where(part == p, other, step)
        peer = me ^ step

        def look(j, slot):
            position = home_ref[fetch_ref[peer, j]]
            return jnp.where(position // per_home == me, position % per_home, slot)

        slot = lax.fori_loop(0, listed, look, jnp.int32(0), unroll=listed <= 8)
        if kind == "shrink":
            source = shrink_ref.at[slot]
        else:
            columns = outs[at].shape[1]
            source = expand_ref.at[slot, :, pl.ds(pl.multiple_of(half * columns, 128), columns)]
        copy = pltpu.make_async_copy(source, outs[at], sems.at[at])
        copy.start()
        copies.append(copy)
    for copy in copies:
        copy.wait()


def pack(groups, columns, adapter_home, fetch_list, panels, expand_panels):
    rank, depth = panels.shape[1:]
    widths = [depth if kind == "shrink" else columns for _, kind in groups]
    return list(
        pl.pallas_call(
            functools.partial(pack_kernel, groups),
            out_shape=[jax.ShapeDtypeStruct((rank, width), panels.dtype) for width in widths],
            in_specs=[pl.BlockSpec(memory_space=pltpu.SMEM)] * 2 + [pl.BlockSpec(memory_space=pl.ANY)] * 2,
            out_specs=[pl.BlockSpec(memory_space=pltpu.VMEM)] * len(groups),
            scratch_shapes=[pltpu.SemaphoreType.DMA((len(groups),))],
            compiler_params=pltpu.CompilerParams(vmem_limit_bytes=56 << 20),
            cost_estimate=pl.CostEstimate(
                flops=0, bytes_accessed=4 * rank * sum(widths), transcendentals=0
            ),
        )(adapter_home, fetch_list, panels, expand_panels)
    )


def on_device(tokens, base_weight, shrink_panels, expand_panels, adapter_home, fetch_list, seg_len):
    per_home = shrink_panels.shape[0]
    replicas, parts, cores = lax.axis_size("rep"), lax.axis_size("parts"), lax.axis_size("tp")
    me, part = lax.axis_index("rep"), lax.axis_index("parts")
    tok_count = tokens.shape[0]
    columns = expand_panels.shape[2] // cores
    panels = jnp.swapaxes(shrink_panels, 1, 2)
    tie = lax.optimization_barrier

    alone, half = max(2, parts), replicas // 2

    def grouped(steps):
        size = len(steps) // parts
        return [tuple(steps[p * size + g] for p in range(parts)) for g in range(size)]

    far = grouped(list(range(half, replicas)))
    near = grouped(list(range(alone, half)))
    groups = far + near
    solo = [(step,) * parts for step in range(1, alone)]

    def hop(x, group):
        pairs = [
            (p * replicas + i, p * replicas + (i ^ group[p]))
            for p in range(parts)
            for i in range(replicas)
        ]
        return lax.ppermute(x, ("parts", "rep"), pairs)

    def shift_parts(x, shift, turn=0):
        pairs = [
            (p * cores + t, ((p + shift) % parts) * cores + (t + turn) % cores)
            for p in range(parts)
            for t in range(cores)
        ]
        return lax.ppermute(x, ("parts", "tp"), pairs)

    def packed(kind, groups, panels):
        kinds = [(group, kind) for group in groups]
        return pack(kinds, columns, adapter_home, fetch_list, panels, expand_panels)

    others = near + solo
    own_group = (0,) * parts
    far_send = packed("shrink", far, panels)
    panels, far_send = tie((panels, far_send))
    near_send = packed("shrink", others, panels)
    tokens, far_send, near_send = tie((tokens, far_send, near_send))

    far_recv = [hop(x, group) for x, group in zip(far_send, far)]
    tokens_of = [tokens] + [shift_parts(tokens, shift) for shift in range(1, parts)]
    near_recv = [hop(x, group) for x, group in zip(near_send, others)]
    panels, seg_len, near_recv = tie((panels, seg_len, near_recv))
    own, *expand_send = pack(
        [(own_group, "shrink")] + [(group, "expand") for group in far + others + [own_group]],
        columns,
        adapter_home,
        fetch_list,
        panels,
        expand_panels,
    )
    own_expand = expand_send.pop()
    expand_recv = [hop(x, group) for x, group in zip(expand_send, far)]
    seg_len, expand_send, expand_recv = tie((seg_len, expand_send, expand_recv))
    lengths_of = [seg_len[0]] + [shift_parts(seg_len, shift)[0] for shift in range(1, parts)]
    expand_recv += [hop(x, group) for x, group in zip(expand_send[len(far) :], others)]

    stored = jnp.take(adapter_home, lax.dynamic_index_in_dim(fetch_list, me, 0, keepdims=False))
    steps = (stored // per_home) ^ me
    rows = jnp.arange(tok_count, dtype=jnp.int32)

    def steps_of_rows(lengths):
        ordinal = jnp.arange(lengths.shape[0])
        starts = jnp.sum(jnp.where(ordinal[None, :] < ordinal[:, None], lengths[None, :], 0), axis=1)
        member = (rows[:, None] >= starts[None, :]) & (rows[:, None] < (starts + lengths)[None, :])
        return jnp.sum(jnp.where(member, steps[None, :], 0), axis=1)[:, None]

    row_steps = [steps_of_rows(lengths) for lengths in lengths_of]

    def step_of(group, shift=0):
        step = jnp.int32(0)
        for p in range(parts):
            step = jnp.where(part == p, group[(p - shift) % parts], step)
        return step

    def score(block, step, shift):
        product = lax.dot_general(
            tokens_of[shift], block, (((1,), (1,)), ((), ())), preferred_element_type=jnp.float32
        )
        return jnp.where(row_steps[shift] == step, product, 0.0)

    base_part = jnp.dot(tokens, base_weight, preferred_element_type=jnp.float32)
    base = lax.psum_scatter(base_part, "tp", scatter_dimension=1, tiled=True)

    count = len(far) + len(near)
    expands = [own_expand] + expand_recv
    expand_steps = [0] + [step_of(group) for group in far + others]
    mine = jnp.concatenate(expand_recv[:count], axis=0)
    for shift in range(1, parts):
        expands.append(shift_parts(mine, shift))
        expand_steps += [step_of(group, shift) for group in far + near]
    expand = jnp.concatenate(expands, axis=0).astype(jnp.float32)

    scores = [score(own, 0, 0)] + [None] * (parts - 1)
    for block, group in zip(near_recv[len(near) :], solo):
        scores[0] = scores[0] + score(block, group[0], 0)
    for at, (block, group) in enumerate(zip(near_recv[: len(near)] + far_recv, near + far)):
        if at == len(near):
            tokens_of, expand, scores = tie((tokens_of, expand, scores))
        for shift in range(parts):
            term = score(block, step_of(group), shift)
            scores[shift] = term if scores[shift] is None else scores[shift] + term
    shrink = scores[0]
    for turn in range(cores):
        for shift in range(parts):
            if shift or turn:
                shrink = shrink + shift_parts(scores[shift], -shift, turn)
    wide = jnp.concatenate(
        [jnp.where(row_steps[0] == step, shrink, 0.0) for step in expand_steps], axis=1
    )
    lora = jnp.dot(
        wide, expand, precision=lax.Precision.HIGHEST, preferred_element_type=jnp.float32
    )
    return (base + adapter_scale * lora).astype(jnp.bfloat16)


def solution(mesh):
    return jax.shard_map(
        on_device,
        mesh=mesh,
        in_specs=(
            P(("parts", "rep"), "tp"),
            P("tp", None),
            P("rep", "tp", None),
            P("rep", None, None),
            P(),
            P(),
            P(("parts", "rep"), None),
        ),
        out_specs=P(("parts", "rep"), "tp"),
        check_vma=False,
    )
```

time: 218 us -> 114 us (0.52)
  the two profiles are of different devices: /device:TPU:19 before, /device:TPU:0 now
where the time goes in v4:
time: 114 us; the launch traced here: 113 us
  waiting for transfers between devices  45.6 us (40%)
  matrix products  23.7 us (21%)
  starting transfers between devices  17.3 us (15%)
  between operations  13.7 us (12%)
  Pallas kernels  9.1 us (8%)
  other arithmetic  1.99 us (2%)
  local copies, waits for them, and re-layouts  1.54 us (1%)
    ppermute x8, waiting for transfers between devices, hop(): return lax.ppermute(x, ('parts', 'rep'), pairs)  34 us
    dot_general x8, matrix products, score(): lax.dot_general(tokens_of[shift], block, (((1,), (1,)), ((), ())), prefer...  14.2 us
    ppermute x8, starting transfers between devices, hop(): return lax.ppermute(x, ('parts', 'rep'), pairs)  13.9 us
    ppermute x6, waiting for transfers between devices, shift_parts(): return lax.ppermute(x, ('parts', 'tp'), pairs)  11.6 us
    pallas_call x3, Pallas kernels, pack(): pl.pallas_call(functools.partial(pack_kernel, groups), out_shape=[jax.Sha...  9.1 us
    dot_general x1, matrix products, on_device(): base_part = jnp.dot(tokens, base_weight, preferred_element_type=jnp.float32)  6.74 us
    ppermute x6, starting transfers between devices, shift_parts(): return lax.ppermute(x, ('parts', 'tp'), pairs)  3.44 us
    dot_general x1, matrix products, on_device(): jnp.dot(wide, expand, precision=lax.Precision.HIGHEST, preferred_element_...  2.83 us
  transfers between devices with their start and end apart: 15, of which 8 were waited for; matrix products, arithmetic and copies ran while one was open for 22% of the time, Pallas kernels for 3%

profile of v4, /device:TPU:0, one launch (start us, length us, event | category | flops | bytes accessed | tf_op | source)
XLA Modules:
  0.0 113.0 jit_solution(1257166394689756933)
XLA Ops:
  6.5 3.1 %shard_map.73 = (bf16[64,4096]{1,0:T(8,128)(2,1)}, bf16[64,4096]{1,0:T(8,128)(2,1)}) custom-call(s32[32]{0:T(128)} %home_ref.5, s32[8,8]{1,0:T(8,128)} %fetch_ref.5, bf16[4,64,4096]{2,1,0:T(8,128)(2,1)} %bitcast.45, bf16[4,64,1024]{2,1,0:T(8,128)(2,1)} %expand_ref.5), custom_call_target="tpu_custom_call" | custom-call | bytes 2097152 | tf_op jit(solution)/shard_map/pallas_call | solution.py:45
  9.7 3.0 %shard_map.74 = (bf16[64,4096]{1,0:T(8,128)(2,1)}, bf16[64,4096]{1,0:T(8,128)(2,1)}) custom-call(s32[32]{0:T(128)} %home_ref.5, s32[8,8]{1,0:T(8,128)} %fetch_ref.5, bf16[4,64,4096]{2,1,0:T(8,128)(2,1)} %bitcast.46, bf16[4,64,1024]{2,1,0:T(8,128)(2,1)} %expand_ref.5), custom_call_target="tpu_custom_call" | custom-call | bytes 2097152 | tf_op jit(solution)/shard_map/pallas_call | solution.py:45
  12.7 3.1 %collective-permute-start = (bf16[64,4096]{1,0:T(8,128)(2,1)}, bf16[64,4096]{1,0:T(8,128)(2,1)S(1)}, u32[]{:S(2)}, u32[]{:S(2)}) collective-permute-start(bf16[64,4096]{1,0:T(8,128)(2,1)} %get-tuple-element.45), channel_id=1, source_target_pairs={{0,4},{2,6},{4,0},{6,2},{8,12},{10,14},{12,8},{14,10},{16,22},{18,... | collective-permute-start | bytes 1572872 | tf_op jit(solution)/shard_map/ppermute | solution.py:85
  15.8 1.6 %collective-permute-start.1 = (bf16[64,4096]{1,0:T(8,128)(2,1)}, bf16[64,4096]{1,0:T(8,128)(2,1)S(1)}, u32[]{:S(2)}, u32[]{:S(2)}) collective-permute-start(bf16[64,4096]{1,0:T(8,128)(2,1)} %get-tuple-element.46), channel_id=1, source_target_pairs={{0,2},{2,0},{4,6},{6,4},{8,10},{10,8},{12,14},{14,12},{16,18},{18,... | collective-permute-start | bytes 1572872 | tf_op jit(solution)/shard_map/ppermute | solution.py:85
  17.4 1.4 %collective-permute-start.4 = (bf16[256,4096]{1,0:T(8,128)(2,1)S(1)}, bf16[256,4096]{1,0:T(8,128)(2,1)}, u32[]{:S(2)}, u32[]{:S(2)}) collective-permute-start(bf16[256,4096]{1,0:T(8,128)(2,1)S(1)} %copy-done.1), channel_id=1, source_target_pairs={{0,16},{1,17},{16,0},{17,1},{2,18},{3,19},{18,2},{19,3},{4,20},{5,... | collective-permute-start | bytes 6291464 | tf_op jit(solution)/shard_map/ppermute | solution.py:93
  18.8 2.6 %collective-permute-start.9 = (bf16[64,4096]{1,0:T(8,128)(2,1)}, bf16[64,4096]{1,0:T(8,128)(2,1)}, u32[]{:S(2)}, u32[]{:S(2)}) collective-permute-start(bf16[64,4096]{1,0:T(8,128)(2,1)} %get-tuple-element.64), channel_id=1, source_target_pairs={{0,8},{2,10},{4,12},{6,14},{8,0},{10,2},{12,4},{14,6},{16,28},{18,... | collective-permute-start | bytes 1572872 | tf_op jit(solution)/shard_map/ppermute | solution.py:85
  21.4 1.3 %collective-permute-start.10 = (bf16[64,4096]{1,0:T(8,128)(2,1)}, bf16[64,4096]{1,0:T(8,128)(2,1)}, u32[]{:S(2)}, u32[]{:S(2)}) collective-permute-start(bf16[64,4096]{1,0:T(8,128)(2,1)} %get-tuple-element.65), channel_id=1, source_target_pairs={{0,10},{2,8},{4,14},{6,12},{8,2},{10,0},{12,6},{14,4},{16,30},{18,... | collective-permute-start | bytes 1572872 | tf_op jit(solution)/shard_map/ppermute | solution.py:85
  22.7 6.7 %fusion.9 = f32[256,1024]{1,0:T(8,128)} fusion(bf16[256,4096]{1,0:T(8,128)(2,1)S(1)} %copy-done.1, bf16[4096,1024]{1,0:T(8,128)(2,1)} %param.8), kind=kOutput, calls=%fused_computation.70 | convolution fusion | flops 2147483648 | bytes 11534336 | tf_op jit(solution)/shard_map/dot_general | solution.py:148
  29.4 0.7 fusion.6
  30.1 0.6 gather_fusion
  30.8 0.7 xor_bitcast_fusion
  31.5 5.2 %collective-permute-done = bf16[64,4096]{1,0:T(8,128)(2,1)S(1)} collective-permute-done((bf16[64,4096]{1,0:T(8,128)(2,1)}, bf16[64,4096]{1,0:T(8,128)(2,1)S(1)}, u32[]{:S(2)}, u32[]{:S(2)}) %collective-permute-start) | collective-permute-done | bytes 524320 | tf_op jit(solution)/shard_map/ppermute | solution.py:85
  36.8 2.9 %shard_map.75 = (bf16[64,4096]{1,0:T(8,128)(2,1)}, bf16[64,512]{1,0:T(8,128)(2,1)}, bf16[64,512]{1,0:T(8,128)(2,1)}, bf16[64,512]{1,0:T(8,128)(2,1)}, bf16[64,512]{1,0:T(8,128)(2,1)}, /*index=5*/bf16[64,512]{1,0:T(8,128)(2,1)}) custom-call(s32[32]{0:T(128)} %home_ref.5, s32[8,8]{1,0:T(8,128)} %fetch_ref.5, bf16[4,64,4096]{2,1,0:T(8,128)(2,1)} %bitcast.47, ...), custom_call_target="tpu_custom_call" | custom-call | bytes 1703936 | tf_op jit(solution)/shard_map/pallas_call | solution.py:45
  39.7 0.8 collective-permute-start.2
  40.5 3.2 %collective-permute-start.3 = (bf16[64,512]{1,0:T(8,128)(2,1)}, bf16[64,512]{1,0:T(8,128)(2,1)S(1)}, u32[]{:S(2)}, u32[]{:S(2)}) collective-permute-start(bf16[64,512]{1,0:T(8,128)(2,1)} %get-tuple-element.50), channel_id=1, source_target_pairs={{0,10},{2,8},{4,14},{6,12},{8,2},{10,0},{12,6},{14,4},{16,30},{18,... | collective-permute-start | bytes 196616 | tf_op jit(solution)/shard_map/ppermute | solution.py:85
  43.7 0.8 constant_dynamic-update-slice_fusion.5
  44.6 26.8 %collective-permute-done.2 = bf16[64,512]{1,0:T(8,128)(2,1)S(1)} collective-permute-done((bf16[64,512]{1,0:T(8,128)(2,1)}, bf16[64,512]{1,0:T(8,128)(2,1)S(1)}, u32[]{:S(2)}, u32[]{:S(2)}) %collective-permute-start.2) | collective-permute-done | bytes 65568 | tf_op jit(solution)/shard_map/ppermute | solution.py:85
  71.4 1.7 %collective-permute-done.3 = bf16[64,512]{1,0:T(8,128)(2,1)S(1)} collective-permute-done((bf16[64,512]{1,0:T(8,128)(2,1)}, bf16[64,512]{1,0:T(8,128)(2,1)S(1)}, u32[]{:S(2)}, u32[]{:S(2)}) %collective-permute-start.3) | collective-permute-done | bytes 65568 | tf_op jit(solution)/shard_map/ppermute | solution.py:85
  73.2 0.9 collective-permute-start.5
  74.0 2.5 %collective-permute-done.8 = s32[1,8]{1,0:T(1,128)S(1)} collective-permute-done((s32[1,8]{1,0:T(1,128)S(1)}, s32[1,8]{1,0:T(1,128)S(1)}, u32[]{:S(2)}, u32[]{:S(2)}) %collective-permute-start.8) | collective-permute-done | bytes 64 | tf_op jit(solution)/shard_map/ppermute | solution.py:93
  77.3 1.8 %convolution_select_fusion.7 = f32[256,64]{0,1:T(8,128)S(1)} fusion(bf16[256,4096]{1,0:T(8,128)(2,1)S(1)} %copy-done.1, bf16[64,4096]{1,0:T(8,128)(2,1)} %get-tuple-element.59, pred[256]{0:T(512)(128)(4,1)S(1)} %get-tuple-element.81), kind=kOutput, calls=%fused_computation.13 | convolution fusion | flops 134234112 | bytes 2687232 | tf_op jit(solution)/shard_map/dot_general | solution.py:143
  79.1 0.8 fusion.3
  79.9 0.8 fusion.2
  81.1 5.4 %collective-permute-done.7 = bf16[192,512]{1,0:T(8,128)(2,1)S(1)} collective-permute-done((bf16[192,512]{1,0:T(8,128)(2,1)S(1)}, bf16[192,512]{1,0:T(8,128)(2,1)S(1)}, u32[]{:S(2)}, u32[]{:S(2)}) %collective-permute-start.7) | collective-permute-done | bytes 196640 | tf_op jit(solution)/shard_map/ppermute | solution.py:93
  86.6 2.4 %convolution_select_fusion.4 = f32[256,64]{0,1:T(8,128)S(1)} fusion(bf16[256,4096]{1,0:T(8,128)(2,1)} %collective-permute-done.4, bf16[64,4096]{1,0:T(8,128)(2,1)S(1)} %copy-done.3, pred[256]{0:T(512)(128)(4,1)S(1)} %get-tuple-element.84), kind=kOutput, calls=%fused_computation.8 | convolution fusion | flops 134234112 | bytes 2687232 | tf_op jit(solution)/shard_map/dot_general | solution.py:143
  89.0 1.8 %convolution_select_fusion.3 = f32[256,64]{0,1:T(8,128)S(1)} fusion(bf16[256,4096]{1,0:T(8,128)(2,1)S(1)} %copy-done.1, bf16[64,4096]{1,0:T(8,128)(2,1)} %collective-permute-done.9, pred[256]{0:T(512)(128)(4,1)S(1)} %get-tuple-element.78), kind=kOutput, calls=%fused_computation.7 | convolution fusion | flops 134234112 | bytes 2687232 | tf_op jit(solution)/shard_map/dot_general | solution.py:143
  90.8 1.8 %add_add_fusion.2 = f32[256,64]{0,1:T(8,128)S(1)} fusion(f32[256,64]{0,1:T(8,128)S(1)} %fusion.2, f32[256,64]{0,1:T(8,128)S(1)} %convolution_select_fusion.3, bf16[256,4096]{1,0:T(8,128)(2,1)S(1)} %copy-done.1, bf16[64,4096]{1,0:T(8,128)(2,1)} %collective-permute-done.10, pred[256]{0:T(512)(128)(4,1)S(1)} %get-tuple-element.77), kind=kOutput, calls=%fused_computation.25 | convolution fusion | flops 134266880 | bytes 2818304 | tf_op jit(solution)/shard_map/dot_general | solution.py:143
  92.7 2.4 %convolution_select_fusion.1 = f32[256,64]{0,1:T(8,128)S(1)} fusion(bf16[256,4096]{1,0:T(8,128)(2,1)} %collective-permute-done.4, bf16[64,4096]{1,0:T(8,128)(2,1)} %collective-permute-done.9, pred[256]{0:T(512)(128)(4,1)S(1)} %get-tuple-element.83), kind=kOutput, calls=%fused_computation.5 | convolution fusion | flops 134234112 | bytes 2687232 | tf_op jit(solution)/shard_map/dot_general | solution.py:143
  95.1 2.4 %add_add_fusion.1 = f32[256,64]{0,1:T(8,128)S(1)} fusion(f32[256,64]{0,1:T(8,128)S(1)} %convolution_select_fusion.4, f32[256,64]{0,1:T(8,128)S(1)} %convolution_select_fusion.1, bf16[256,4096]{1,0:T(8,128)(2,1)} %collective-permute-done.4, bf16[64,4096]{1,0:T(8,128)(2,1)} %collective-permute-done.10, pred[256]{0:T(512)(128)(4,1)S(1)} %get-tuple-element.82), kind=kOutput, calls=%fused_computation.24 | convolution fusion | flops 134266880 | bytes 2818304 | tf_op jit(solution)/shard_map/dot_general | solution.py:143
  97.6 1.8 %collective-permute-start.13 = (f32[256,64]{0,1:T(8,128)S(1)}, f32[256,64]{0,1:T(8,128)S(1)}, u32[]{:S(2)}, u32[]{:S(2)}) collective-permute-start(f32[256,64]{0,1:T(8,128)S(1)} %add_add_fusion.1), channel_id=1, source_target_pairs={{0,17},{1,16},{16,1},{17,0},{2,19},{3,18},{18,3},{19,2},{4,21},{5,... | collective-permute-start | bytes 196616 | tf_op jit(solution)/shard_map/ppermute | solution.py:93
  99.5 3.0 %collective-permute-done.11 = f32[256,64]{0,1:T(8,128)S(1)} collective-permute-done((f32[256,64]{0,1:T(8,128)S(1)}, f32[256,64]{0,1:T(8,128)S(1)}, u32[]{:S(2)}, u32[]{:S(2)}) %collective-permute-start.11) | collective-permute-done | bytes 65568 | tf_op jit(solution)/shard_map/ppermute | solution.py:93
  103.3 2.8 %fusion.1 = bf16[256,512]{1,0:T(8,128)(2,1)} fusion(f32[256,512]{1,0:T(8,128)} %reduce-scatter.2.cloned.1.call-done, f32[256,512]{0,1:T(8,128)S(1)} %select_dynamic-update-slice_fusion, f32[512,512]{1,0:T(8,128)S(1)} %convert_element_type.6), kind=kOutput, calls=%fused_computation.3 | convolution fusion | flops 805699584 | bytes 2359296 | tf_op jit(solution)/shard_map/dot_general | solution.py:177
  (49 shorter events, 2.3 us)
Async XLA Ops:
  6.5 96.8 %reduce-scatter.2.cloned.1.call-start = ((), (), s32[]{:S(2)}) async-start(), calls=%async_computation.1 | async-start | bytes 1572864 | tf_op jit(solution)/shard_map/reduce_scatter | solution.py:149
  6.5 10.9 %copy-start.1 = (bf16[256,4096]{1,0:T(8,128)(2,1)S(1)}, bf16[256,4096]{1,0:T(8,128)(2,1)}, u32[]{:S(2)}) copy-start(bf16[256,4096]{1,0:T(8,128)(2,1)} %param.7) | copy-start | bytes 6291460
  12.7 17.4 %copy-start = (s32[32]{0:T(128)S(1)}, s32[32]{0:T(128)}, u32[]{:S(2)}) copy-start(s32[32]{0:T(128)} %home_ref.5) | copy-start | bytes 388
  12.7 24.0 %collective-permute-start = (bf16[64,4096]{1,0:T(8,128)(2,1)}, bf16[64,4096]{1,0:T(8,128)(2,1)S(1)}, u32[]{:S(2)}, u32[]{:S(2)}) collective-permute-start(bf16[64,4096]{1,0:T(8,128)(2,1)} %get-tuple-element.45), channel_id=1, source_target_pairs={{0,4},{2,6},{4,0},{6,2},{8,12},{10,14},{12,8},{14,10},{16,22},{18,... | collective-permute-start | bytes 1572872 | tf_op jit(solution)/shard_map/ppermute | solution.py:85
  15.8 21.0 %collective-permute-start.1 = (bf16[64,4096]{1,0:T(8,128)(2,1)}, bf16[64,4096]{1,0:T(8,128)(2,1)S(1)}, u32[]{:S(2)}, u32[]{:S(2)}) collective-permute-start(bf16[64,4096]{1,0:T(8,128)(2,1)} %get-tuple-element.46), channel_id=1, source_target_pairs={{0,2},{2,0},{4,6},{6,4},{8,10},{10,8},{12,14},{14,12},{16,18},{18,... | collective-permute-start | bytes 1572872 | tf_op jit(solution)/shard_map/ppermute | solution.py:85
  17.4 69.2 %collective-permute-start.4 = (bf16[256,4096]{1,0:T(8,128)(2,1)S(1)}, bf16[256,4096]{1,0:T(8,128)(2,1)}, u32[]{:S(2)}, u32[]{:S(2)}) collective-permute-start(bf16[256,4096]{1,0:T(8,128)(2,1)S(1)} %copy-done.1), channel_id=1, source_target_pairs={{0,16},{1,17},{16,0},{17,1},{2,18},{3,19},{18,2},{19,3},{4,20},{5,... | collective-permute-start | bytes 6291464 | tf_op jit(solution)/shard_map/ppermute | solution.py:93
  18.8 70.2 %collective-permute-start.9 = (bf16[64,4096]{1,0:T(8,128)(2,1)}, bf16[64,4096]{1,0:T(8,128)(2,1)}, u32[]{:S(2)}, u32[]{:S(2)}) collective-permute-start(bf16[64,4096]{1,0:T(8,128)(2,1)} %get-tuple-element.64), channel_id=1, source_target_pairs={{0,8},{2,10},{4,12},{6,14},{8,0},{10,2},{12,4},{14,6},{16,28},{18,... | collective-permute-start | bytes 1572872 | tf_op jit(solution)/shard_map/ppermute | solution.py:85
  21.4 69.4 %collective-permute-start.10 = (bf16[64,4096]{1,0:T(8,128)(2,1)}, bf16[64,4096]{1,0:T(8,128)(2,1)}, u32[]{:S(2)}, u32[]{:S(2)}) collective-permute-start(bf16[64,4096]{1,0:T(8,128)(2,1)} %get-tuple-element.65), channel_id=1, source_target_pairs={{0,10},{2,8},{4,14},{6,12},{8,2},{10,0},{12,6},{14,4},{16,30},{18,... | collective-permute-start | bytes 1572872 | tf_op jit(solution)/shard_map/ppermute | solution.py:85
  29.4 43.6 %copy-start.4 = (s32[1,8]{1,0:T(1,128)S(1)}, s32[1,8]{1,0:T(1,128)}, u32[]{:S(2)}) copy-start(s32[1,8]{1,0:T(1,128)} %param.13) | copy-start | bytes 100
  36.8 43.1 %copy-start.2 = (bf16[64,4096]{1,0:T(8,128)(2,1)}, bf16[64,4096]{1,0:T(8,128)(2,1)S(1)}, u32[]{:S(2)}) copy-start(bf16[64,4096]{1,0:T(8,128)(2,1)S(1)} %collective-permute-done) | copy-start | bytes 1572868
  39.7 31.6 %collective-permute-start.2 = (bf16[64,512]{1,0:T(8,128)(2,1)}, bf16[64,512]{1,0:T(8,128)(2,1)S(1)}, u32[]{:S(2)}, u32[]{:S(2)}) collective-permute-start(bf16[64,512]{1,0:T(8,128)(2,1)} %get-tuple-element.49), channel_id=1, source_target_pairs={{0,8},{2,10},{4,12},{6,14},{8,0},{10,2},{12,4},{14,6},{16,28},{18,... | collective-permute-start | bytes 196616 | tf_op jit(solution)/shard_map/ppermute | solution.py:85
  40.5 32.5 %collective-permute-start.3 = (bf16[64,512]{1,0:T(8,128)(2,1)}, bf16[64,512]{1,0:T(8,128)(2,1)S(1)}, u32[]{:S(2)}, u32[]{:S(2)}) collective-permute-start(bf16[64,512]{1,0:T(8,128)(2,1)} %get-tuple-element.50), channel_id=1, source_target_pairs={{0,10},{2,8},{4,14},{6,12},{8,2},{10,0},{12,6},{14,4},{16,30},{18,... | collective-permute-start | bytes 196616 | tf_op jit(solution)/shard_map/ppermute | solution.py:85
  73.0 3.5 %collective-permute-start.8 = (s32[1,8]{1,0:T(1,128)S(1)}, s32[1,8]{1,0:T(1,128)S(1)}, u32[]{:S(2)}, u32[]{:S(2)}) collective-permute-start(s32[1,8]{1,0:T(1,128)S(1)} %copy-done.4), channel_id=1, source_target_pairs={{0,16},{1,17},{16,0},{17,1},{2,18},{3,19},{18,2},{19,3},{4,20},{5,... | collective-permute-start | bytes 104 | tf_op jit(solution)/shard_map/ppermute | solution.py:93
  73.2 7.5 %collective-permute-start.5 = (bf16[64,512]{1,0:T(8,128)(2,1)}, bf16[64,512]{1,0:T(8,128)(2,1)S(1)}, u32[]{:S(2)}, u32[]{:S(2)}) collective-permute-start(bf16[64,512]{1,0:T(8,128)(2,1)} %get-tuple-element.57), channel_id=1, source_target_pairs={{0,4},{2,6},{4,0},{6,2},{8,12},{10,14},{12,8},{14,10},{16,22},{18,... | collective-permute-start | bytes 196616 | tf_op jit(solution)/shard_map/ppermute | solution.py:85
  76.6 4.5 %collective-permute-start.6 = (bf16[64,512]{1,0:T(8,128)(2,1)}, bf16[64,512]{1,0:T(8,128)(2,1)S(1)}, u32[]{:S(2)}, u32[]{:S(2)}) collective-permute-start(bf16[64,512]{1,0:T(8,128)(2,1)} %get-tuple-element.58), channel_id=1, source_target_pairs={{0,2},{2,0},{4,6},{6,4},{8,10},{10,8},{12,14},{14,12},{16,18},{18,... | collective-permute-start | bytes 196616 | tf_op jit(solution)/shard_map/ppermute | solution.py:85
  80.7 5.9 %copy-start.3 = (bf16[64,4096]{1,0:T(8,128)(2,1)S(1)}, bf16[64,4096]{1,0:T(8,128)(2,1)}, u32[]{:S(2)}) copy-start(bf16[64,4096]{1,0:T(8,128)(2,1)} %copy-done.2) | copy-start | bytes 1572868
  80.7 5.7 %collective-permute-start.7 = (bf16[192,512]{1,0:T(8,128)(2,1)S(1)}, bf16[192,512]{1,0:T(8,128)(2,1)S(1)}, u32[]{:S(2)}, u32[]{:S(2)}) collective-permute-start(bf16[192,512]{1,0:T(8,128)(2,1)S(1)} %pad_maximum_fusion), channel_id=1, source_target_pairs={{0,16},{1,17},{16,0},{17,1},{2,18},{3,19},{18,2},{19,3},{4,20},{5,... | collective-permute-start | bytes 589832 | tf_op jit(solution)/shard_map/ppermute | solution.py:93
  92.6 6.9 %collective-permute-start.12 = (f32[256,64]{0,1:T(8,128)S(1)}, f32[256,64]{0,1:T(8,128)S(1)}, u32[]{:S(2)}, u32[]{:S(2)}) collective-permute-start(f32[256,64]{0,1:T(8,128)S(1)} %add_add_fusion.2), channel_id=1, source_target_pairs={{0,1},{1,0},{16,17},{17,16},{2,3},{3,2},{18,19},{19,18},{4,5},{5,4... | collective-permute-start | bytes 196616 | tf_op jit(solution)/shard_map/ppermute | solution.py:93
  97.5 4.9 %collective-permute-start.11 = (f32[256,64]{0,1:T(8,128)S(1)}, f32[256,64]{0,1:T(8,128)S(1)}, u32[]{:S(2)}, u32[]{:S(2)}) collective-permute-start(f32[256,64]{0,1:T(8,128)S(1)} %add_add_fusion.1), channel_id=1, source_target_pairs={{0,16},{1,17},{16,0},{17,1},{2,18},{3,19},{18,2},{19,3},{4,20},{5,... | collective-permute-start | bytes 196616 | tf_op jit(solution)/shard_map/ppermute | solution.py:93
  97.6 5.5 %collective-permute-start.13 = (f32[256,64]{0,1:T(8,128)S(1)}, f32[256,64]{0,1:T(8,128)S(1)}, u32[]{:S(2)}, u32[]{:S(2)}) collective-permute-start(f32[256,64]{0,1:T(8,128)S(1)} %add_add_fusion.1), channel_id=1, source_target_pairs={{0,17},{1,16},{16,1},{17,0},{2,19},{3,18},{18,3},{19,2},{4,21},{5,... | collective-permute-start | bytes 196616 | tf_op jit(solution)/shard_map/ppermute | solution.py:93
Sparse Core Ops, SparseCore 0:
  29.5 7.6 reduce-scatter.1

commit v5 on v4

v5 whole, which is shorter than its diff:
```python
import functools
import jax
import jax.numpy as jnp
from jax import lax
from jax.experimental import pallas as pl
from jax.experimental.pallas import tpu as pltpu
from jax.sharding import PartitionSpec as P

adapter_scale = 2.0


def pack_kernel(blocks, home_ref, fetch_ref, shrink_ref, expand_ref, *refs):
    outs, sems = refs[:-1], refs[-1]
    me, part, half = lax.axis_index("rep"), lax.axis_index("parts"), lax.axis_index("tp")
    per_home, _, depth = shrink_ref.shape
    columns = expand_ref.shape[2] // lax.axis_size("tp")
    listed = fetch_ref.shape[1]
    copies, slots = [], {}
    for at, (group, shrink, expand) in enumerate(blocks):
        if group not in slots:
            step = jnp.int32(group[0])
            for p, other in enumerate(group):
                step = jnp.where(part == p, other, step)
            peer = me ^ step

            def look(j, slot):
                position = home_ref[fetch_ref[peer, j]]
                return jnp.where(position // per_home == me, position % per_home, slot)

            slots[group] = lax.fori_loop(0, listed, look, jnp.int32(0), unroll=listed <= 8)
        slot = slots[group]
        pieces = []
        if shrink:
            pieces.append((shrink_ref.at[slot], outs[at].at[:, pl.ds(0, depth)]))
        if expand:
            left = pl.multiple_of(half * columns, 128)
            pieces.append(
                (
                    expand_ref.at[slot, :, pl.ds(left, columns)],
                    outs[at].at[:, pl.ds(depth * shrink, columns)],
                )
            )
        for n, (source, target) in enumerate(pieces):
            copy = pltpu.make_async_copy(source, target, sems.at[at, n])
            copy.start()
            copies.append(copy)
    for copy in copies:
        copy.wait()


def pack(blocks, columns, adapter_home, fetch_list, panels, expand_panels):
    rank, depth = panels.shape[1:]
    shapes = [(rank, depth * shrink + columns * expand) for _, shrink, expand in blocks]
    return list(
        pl.pallas_call(
            functools.partial(pack_kernel, blocks),
            out_shape=[jax.ShapeDtypeStruct(shape, panels.dtype) for shape in shapes],
            in_specs=[pl.BlockSpec(memory_space=pltpu.SMEM)] * 2 + [pl.BlockSpec(memory_space=pl.ANY)] * 2,
            out_specs=[pl.BlockSpec(memory_space=pltpu.VMEM)] * len(blocks),
            scratch_shapes=[pltpu.SemaphoreType.DMA((len(blocks), 2))],
            compiler_params=pltpu.CompilerParams(vmem_limit_bytes=56 << 20),
            cost_estimate=pl.CostEstimate(
                flops=0, bytes_accessed=4 * sum(r * w for r, w in shapes), transcendentals=0
            ),
        )(adapter_home, fetch_list, panels, expand_panels)
    )


def on_device(tokens, base_weight, shrink_panels, expand_panels, adapter_home, fetch_list, seg_len):
    per_home, depth, _ = shrink_panels.shape
    replicas, parts, cores = lax.axis_size("rep"), lax.axis_size("parts"), lax.axis_size("tp")
    me, part = lax.axis_index("rep"), lax.axis_index("parts")
    tok_count = tokens.shape[0]
    columns = expand_panels.shape[2] // cores
    panels = jnp.swapaxes(shrink_panels, 1, 2)
    tie = lax.optimization_barrier

    alone, half = max(2, parts), replicas // 2

    def grouped(steps):
        size = len(steps) // parts
        return [tuple(steps[p * size + g] for p in range(parts)) for g in range(size)]

    far = grouped(list(range(half, replicas)))
    near = grouped(list(range(alone, half)))
    groups = far + near
    solo = [(step,) * parts for step in range(1, alone)]

    def hop(x, group):
        pairs = [
            (p * replicas + i, p * replicas + (i ^ group[p]))
            for p in range(parts)
            for i in range(replicas)
        ]
        return lax.ppermute(x, ("parts", "rep"), pairs)

    def shift_parts(x, shift, turn=0):
        pairs = [
            (p * cores + t, ((p + shift) % parts) * cores + (t + turn) % cores)
            for p in range(parts)
            for t in range(cores)
        ]
        return lax.ppermute(x, ("parts", "tp"), pairs)

    rank = panels.shape[1]
    others, own_group = near + solo, (0,) * parts
    tables = (columns, adapter_home, fetch_list, panels, expand_panels)
    blocks = [(group, True, True) for group in others + far[:-1]]
    blocks += [(far[-1], True, False), (far[-1], False, True)]
    send = pack(blocks, *tables)
    tokens, send = tie((tokens, send))
    last_expand = hop(send.pop(), far[-1])
    recv = [hop(x, group) for x, group in zip(send[:-1], others + far[:-1])]
    last_send, last_expand = tie((send[-1], last_expand))
    recv.append(hop(last_send, far[-1]))
    every_tokens = lax.all_gather(tokens, "parts", axis=0, tiled=True)
    every_seg_len = lax.all_gather(seg_len, "parts", axis=0, tiled=True)
    base_part = jnp.dot(tokens, base_weight, preferred_element_type=jnp.float32)
    base = lax.psum_scatter(base_part, "tp", scatter_dimension=1, tiled=True)
    panels, base_part = tie((panels, base_part))
    tables = (columns, adapter_home, fetch_list, panels, expand_panels)
    (own,) = pack([(own_group, True, True)], *tables)

    stored = jnp.take(adapter_home, lax.dynamic_index_in_dim(fetch_list, me, 0, keepdims=False))
    steps = (stored // per_home) ^ me
    rows = jnp.arange(tok_count, dtype=jnp.int32)

    def steps_of_rows(lengths):
        ends = jnp.cumsum(lengths, axis=1)[:, None, :]
        starts = ends - lengths[:, None, :]
        member = (rows[None, :, None] >= starts) & (rows[None, :, None] < ends)
        return jnp.sum(jnp.where(member, steps[None, None, :], 0), axis=2).reshape(-1, 1)

    row_steps, every_row_steps = steps_of_rows(seg_len), steps_of_rows(every_seg_len)

    def step_of(group, shift=0):
        step = jnp.int32(0)
        for p in range(parts):
            step = jnp.where(part == p, group[(p - shift) % parts], step)
        return step

    def score(block, step, tokens, row_steps):
        product = lax.dot_general(
            tokens,
            block[:, :depth],
            (((1,), (1,)), ((), ())),
            preferred_element_type=jnp.float32,
        )
        return jnp.where(row_steps == step, product, 0.0)

    def total(scores, solo_scores=None):
        shrink = solo_scores
        for shift in range(parts):
            at = ((part + shift) % parts) * tok_count
            piece = lax.dynamic_slice_in_dim(scores, at, tok_count, 0)
            if shift == 0 and solo_scores is not None:
                piece = piece + solo_scores
            for turn in range(cores):
                term = shift_parts(piece, shift, turn) if shift or turn else piece
                shrink = term if shift == 0 and turn == 0 else shrink + term
        return shrink

    def spread(shrink, steps, expands):
        wide = jnp.concatenate([jnp.where(row_steps == step, shrink, 0.0) for step in steps], axis=1)
        return adapter_scale * jnp.dot(
            wide,
            jnp.concatenate(expands, axis=0).astype(jnp.float32),
            precision=lax.Precision.HIGHEST,
            preferred_element_type=jnp.float32,
        )

    shared = recv[: len(near)] + recv[len(others) :]
    shared_groups = near + far
    mine = [x[:, depth:] for x in shared[:-1]] + [last_expand]
    alone_blocks = [own] + recv[len(near) : len(others)]
    alone_steps = [0] + [group[0] for group in solo]
    expands = [x[:, depth:] for x in alone_blocks] + mine[:-1]
    expand_steps = alone_steps + [step_of(group) for group in shared_groups[:-1]]
    last_expands, last_steps = mine[-1:], [step_of(far[-1])]
    sent = jnp.concatenate(mine, axis=0)
    for shift in range(1, parts):
        came = shift_parts(sent, shift)
        expands.append(came[:-rank])
        expand_steps += [step_of(group, shift) for group in shared_groups[:-1]]
        last_expands.append(came[-rank:])
        last_steps.append(step_of(far[-1], shift))

    solo_scores = sum(
        score(block, step, tokens, row_steps) for block, step in zip(alone_blocks, alone_steps)
    )
    scores = sum(
        score(block, step_of(group), every_tokens, every_row_steps)
        for block, group in zip(shared[:-1], shared_groups)
    )
    result = base + spread(total(scores, solo_scores), expand_steps, expands)

    every_tokens, result, last_expands = tie((every_tokens, result, last_expands))
    scores = score(shared[-1], step_of(far[-1]), every_tokens, every_row_steps)
    result = result + spread(total(scores), last_steps, last_expands)
    return result.astype(jnp.bfloat16)


def solution(mesh):
    return jax.shard_map(
        on_device,
        mesh=mesh,
        in_specs=(
            P(("parts", "rep"), "tp"),
            P("tp", None),
            P("rep", "tp", None),
            P("rep", None, None),
            P(),
            P(),
            P(("parts", "rep"), None),
        ),
        out_specs=P(("parts", "rep"), "tp"),
        check_vma=False,
    )
```

time: 114 us -> 107 us (0.939)
  waiting for transfers between devices: 45.6 us -> 31.7 us
  local copies, waits for them, and re-layouts: 1.54 us -> 7.32 us
  blocking collectives: 0 us -> 4.58 us
  Pallas kernels: 9.1 us -> 6.78 us
  other arithmetic: 1.99 us -> 4.25 us
  matrix products: 23.7 us -> 21.5 us
  starting transfers between devices: 17.3 us -> 15.5 us
  between operations: 13.7 us -> 15.1 us
    ppermute x8 -> x5, waiting for transfers between devices: 34 us -> 13.7 us  [hop(): return lax.ppermute(x, ('parts', 'rep'), pairs)]
    all_gather x0 -> x1, waiting for transfers between devices: none -> 13.5 us  [on_device(): every_tokens = lax.all_gather(tokens, 'parts', axis=0, tiled=True)]
    ppermute x6 -> x7, waiting for transfers between devices: 11.6 us -> 4.45 us  [shift_parts(): return lax.ppermute(x, ('parts', 'tp'), pairs)]
    all_gather x0 -> x1, blocking collectives: none -> 4.58 us  [on_device(): every_seg_len = lax.all_gather(seg_len, 'parts', axis=0, tiled=True)]
    ppermute x8 -> x5, starting transfers between devices: 13.9 us -> 10.6 us  [hop(): return lax.ppermute(x, ('parts', 'rep'), pairs)]
    dot_general x9 -> x7, matrix products: 17 us -> 13.7 us  [the longest x5 11.5 us: score(): lax.dot_general(tokens, block[:, :depth], (((1,), (1,)), ((), ())), prefe...]
    slice x0 -> x3, local copies, waits for them, and re-layouts: none -> 2.94 us  [the longest x2 2.1 us: on_device(): mine = [x[:, depth:] for x in shared[:-1]] + [last_expand]]
    pallas_call x3 -> x2, Pallas kernels: 9.1 us -> 6.78 us  [pack(): pl.pallas_call(functools.partial(pack_kernel, blocks), out_shape=[jax.Sha...]
  transfers between devices with their start and end apart: 15 -> 14, of which waited for: 8 -> 5; matrix products, arithmetic and copies ran while one was open for 22% -> 26% of each run, Pallas kernels for 3% -> 3%
where the time goes in v5:
time: 107 us
  waiting for transfers between devices  31.7 us (30%)
  matrix products  21.5 us (20%)
  starting transfers between devices  15.5 us (14%)
  between operations  15.1 us (14%)
  local copies, waits for them, and re-layouts  7.32 us (7%)
  Pallas kernels  6.78 us (6%)
  blocking collectives  4.58 us (4%)
  other arithmetic  4.25 us (4%)
    ppermute x5, waiting for transfers between devices, hop(): return lax.ppermute(x, ('parts', 'rep'), pairs)  13.7 us
    all_gather x1, waiting for transfers between devices, on_device(): every_tokens = lax.all_gather(tokens, 'parts', axis=0, tiled=True)  13.5 us
    dot_general x5, matrix products, score(): lax.dot_general(tokens, block[:, :depth], (((1,), (1,)), ((), ())), prefe...  11.5 us
    ppermute x5, starting transfers between devices, hop(): return lax.ppermute(x, ('parts', 'rep'), pairs)  10.6 us
    dot_general x1, matrix products, on_device(): base_part = jnp.dot(tokens, base_weight, preferred_element_type=jnp.float32)  7.77 us
    pallas_call x2, Pallas kernels, pack(): pl.pallas_call(functools.partial(pack_kernel, blocks), out_shape=[jax.Sha...  6.78 us
    ppermute x7, starting transfers between devices, shift_parts(): return lax.ppermute(x, ('parts', 'tp'), pairs)  4.88 us
    all_gather x1, blocking collectives, on_device(): every_seg_len = lax.all_gather(seg_len, 'parts', axis=0, tiled=True)  4.58 us
  transfers between devices with their start and end apart: 14, of which 5 were waited for; matrix products, arithmetic and copies ran while one was open for 26% of the time, Pallas kernels for 3%

profile of v5, /device:TPU:0, one launch (start us, length us, event | category | flops | bytes accessed | tf_op | source)
XLA Modules:
  0.0 106.7 jit_solution(1804530710266693106)
XLA Ops:
  7.4 4.1 %shard_map.73 = (bf16[64,4608]{1,0:T(8,128)(2,1)}, bf16[64,4608]{1,0:T(8,128)(2,1)}, bf16[64,4608]{1,0:T(8,128)(2,1)}, bf16[64,4096]{1,0:T(8,128)(2,1)}, bf16[64,512]{1,0:T(8,128)(2,1)}) custom-call(s32[32]{0:T(128)} %home_ref.3, s32[8,8]{1,0:T(8,128)} %fetch_ref.3, bf16[4,64,4096]{2,1,0:T(8,128)(2,1)} %bitcast.32, bf16[4,64,1024]{2,1,0:T(8,128)(2,1)} %expand_ref.3), custom_call_target="tpu_custom_call" | custom-call | bytes 4718592 | tf_op jit(solution)/shard_map/pallas_call | solution.py:55
  11.5 5.1 %collective-permute-start.6 = (bf16[64,512]{1,0:T(8,128)(2,1)}, bf16[64,512]{1,0:T(8,128)(2,1)S(1)}, u32[]{:S(2)}, u32[]{:S(2)}) collective-permute-start(bf16[64,512]{1,0:T(8,128)(2,1)} %get-tuple-element.34), channel_id=1, source_target_pairs={{0,10},{2,8},{4,14},{6,12},{8,2},{10,0},{12,6},{14,4},{16,30},{18,... | collective-permute-start | bytes 196616 | tf_op jit(solution)/shard_map/ppermute | solution.py:95
  16.6 1.6 %collective-permute-start = (bf16[64,4608]{1,0:T(8,128)(2,1)}, bf16[64,4608]{1,0:T(8,128)(2,1)S(1)}, u32[]{:S(2)}, u32[]{:S(2)}) collective-permute-start(bf16[64,4608]{1,0:T(8,128)(2,1)} %get-tuple-element.29), channel_id=1, source_target_pairs={{0,4},{2,6},{4,0},{6,2},{8,12},{10,14},{12,8},{14,10},{16,22},{18,... | collective-permute-start | bytes 1769480 | tf_op jit(solution)/shard_map/ppermute | solution.py:95
  19.1 7.8 %fusion.23 = f32[256,1024]{1,0:T(8,128)} fusion(bf16[256,4096]{1,0:T(8,128)(2,1)S(1)} %copy-done.2, bf16[4096,1024]{1,0:T(8,128)(2,1)} %param.8), kind=kOutput, calls=%fused_computation.84 | convolution fusion | flops 2147483648 | bytes 11534336 | tf_op jit(solution)/shard_map/dot_general | solution.py:118
  27.1 0.7 fusion.17
  27.8 0.6 gather_fusion
  28.5 0.7 xor_bitcast_fusion
  29.2 2.7 %shard_map.74 = bf16[64,4608]{1,0:T(8,128)(2,1)} custom-call(s32[32]{0:T(128)} %home_ref.3, s32[8,8]{1,0:T(8,128)} %fetch_ref.3, bf16[4,64,4096]{2,1,0:T(8,128)(2,1)} %bitcast.33, bf16[4,64,1024]{2,1,0:T(8,128)(2,1)} %expand_ref.3), custom_call_target="tpu_custom_call" | custom-call | bytes 1179648 | tf_op jit(solution)/shard_map/pallas_call | solution.py:55
  32.0 1.8 %convolution_select_fusion.4 = f32[256,64]{0,1:T(8,128)S(1)} fusion(bf16[256,4096]{1,0:T(8,128)(2,1)S(1)} %copy-done.2, bf16[64,4608]{1,0:T(8,128)(2,1)} %shard_map.74, pred[256]{0:T(512)(128)(4,1)S(1)} %get-tuple-element.61), kind=kOutput, calls=%fused_computation.10 | convolution fusion | flops 134234112 | bytes 2687232 | tf_op jit(solution)/shard_map/dot_general | solution.py:143
  33.8 1.5 %slice_dynamic-update-slice_fusion.2 = bf16[384,512]{1,0:T(8,128)(2,1)} fusion(bf16[64,4608]{1,0:T(8,128)(2,1)} %shard_map.74), kind=kLoop, calls=%fused_computation.25 | loop fusion | bytes 131072
  35.3 0.7 fusion.18
  36.0 4.6 %all-gather = s32[2,1,8]{2,1,0:T(1,128)S(1)} all-gather(s32[1,1,8]{2,1,0:T(1,128)S(1)} %bitcast.38), channel_id=1, replica_groups=mesh['parts'=2,'rep'=8,'tp'=2] {'parts'}, dimensions={0}, use_global_device_ids=true | all-gather | bytes 96 | tf_op jit(solution)/shard_map/all_gather | solution.py:117
  41.0 3.0 %collective-permute-start.8 = (bf16[64,4096]{1,0:T(8,128)(2,1)}, bf16[64,4096]{1,0:T(8,128)(2,1)}, u32[]{:S(2)}, u32[]{:S(2)}) collective-permute-start(bf16[64,4096]{1,0:T(8,128)(2,1)} %get-tuple-element.38), channel_id=1, source_target_pairs={{0,10},{2,8},{4,14},{6,12},{8,2},{10,0},{12,6},{14,4},{16,30},{18,... | collective-permute-start | bytes 1572872 | tf_op jit(solution)/shard_map/ppermute | solution.py:95
  44.6 0.6 fusion.21
  45.2 13.7 %collective-permute-done.1 = bf16[64,4608]{1,0:T(8,128)(2,1)} collective-permute-done((bf16[64,4608]{1,0:T(8,128)(2,1)}, bf16[64,4608]{1,0:T(8,128)(2,1)}, u32[]{:S(2)}, u32[]{:S(2)}) %collective-permute-start.1) | collective-permute-done | bytes 589856 | tf_op jit(solution)/shard_map/ppermute | solution.py:95
  58.9 1.5 %fusion.22 = (bf16[64,512]{1,0:T(8,128)(2,1)S(1)}, bf16[384,512]{1,0:T(8,128)(2,1)}) fusion(bf16[64,4608]{1,0:T(8,128)(2,1)} %collective-permute-done.1, bf16[384,512]{1,0:T(8,128)(2,1)} %get-tuple-element.46), kind=kLoop, calls=%fused_computation.83 | loop fusion | bytes 196608 | tf_op jit(solution)/shard_map/slice | solution.py:174
  60.4 0.7 pad_maximum_fusion
  61.1 0.7 collective-permute-start.7
  61.7 13.5 %all-gather.3.cloned.1.call-done = bf16[512,4096]{1,0:T(8,128)(2,1)} async-done(((bf16[256,4096]{1,0:T(8,128)(2,1)}), bf16[512,4096]{1,0:T(8,128)(2,1)}) %all-gather.3.cloned.1.call-update) | async-done | bytes 4194320 | tf_op jit(solution)/shard_map/all_gather | solution.py:116
  75.3 3.8 %convolution_select_fusion.1 = f32[512,64]{0,1:T(8,128)S(1)} fusion(bf16[512,4096]{1,0:T(8,128)(2,1)} %all-gather.3.cloned.1.call-done, bf16[64,4608]{1,0:T(8,128)(2,1)} %collective-permute-done.1, pred[512]{0:T(512)(128)(4,1)S(1)} %eq.161), kind=kOutput, calls=%fused_computation.5 | convolution fusion | flops 268468224 | bytes 4850176 | tf_op jit(solution)/shard_map/dot_general | solution.py:143
  79.1 1.4 %fusion.1 = f32[512,64]{0,1:T(8,128)S(1)} fusion(f32[512,64]{0,1:T(8,128)S(1)} %convolution_select_fusion.1, bf16[512,4096]{1,0:T(8,128)(2,1)S(1)} %copy-done.1, bf16[64,4608]{1,0:T(8,128)(2,1)S(1)} %collective-permute-done, pred[512]{0:T(512)(128)(4,1)S(1)} %eq.158), kind=kOutput, calls=%fused_computation.7 | convolution fusion | flops 268500992 | bytes 4981248 | tf_op jit(solution)/shard_map/dot_general | solution.py:143
  80.6 1.5 %collective-permute-start.4 = (f32[256,64]{0,1:T(8,128)S(1)}, f32[256,64]{0,1:T(8,128)S(1)}, u32[]{:S(2)}, u32[]{:S(2)}) collective-permute-start(f32[256,64]{0,1:T(8,128)S(1)} %constant_dynamic-slice_fusion.1), channel_id=1, source_target_pairs={{0,16},{1,17},{16,0},{17,1},{2,18},{3,19},{18,2},{19,3},{4,20},{5,... | collective-permute-start | bytes 196616 | tf_op jit(solution)/shard_map/ppermute | solution.py:103
  82.1 0.8 dynamic-slice_add_fusion
  83.3 1.6 %slice_dynamic-update-slice_fusion = bf16[384,512]{1,0:T(8,128)(2,1)} fusion(bf16[384,512]{1,0:T(8,128)(2,1)} %get-tuple-element.48, bf16[192,512]{1,0:T(8,128)(2,1)} %collective-permute-done.7), kind=kLoop, calls=%fused_computation.17 | loop fusion | bytes 262144 | tf_op jit(solution)/shard_map/concatenate | solution.py:167
  84.9 0.8 slice.51
  85.7 0.7 collective-permute-done.4
  86.6 1.8 %fusion = f32[256,512]{1,0:T(8,128)S(1)} fusion(f32[256,512]{1,0:T(8,128)} %reduce-scatter.2.cloned.1.call-done, f32[256,384]{0,1:T(8,128)S(1)} %select_dynamic-update-slice_fusion, bf16[384,512]{1,0:T(8,128)(2,1)} %slice_dynamic-update-slice_fusion), kind=kOutput, calls=%fused_computation.3 | convolution fusion | flops 604241920 | bytes 1835008 | tf_op jit(solution)/shard_map/dot_general | solution.py:165
  88.4 3.7 %convolution_select_fusion = f32[512,64]{0,1:T(8,128)S(1)} fusion(bf16[512,4096]{1,0:T(8,128)(2,1)} %all-gather.3.cloned.1.call-done, bf16[64,4096]{1,0:T(8,128)(2,1)} %collective-permute-done.8, pred[512]{0:T(512)(128)(4,1)S(1)} %eq.175), kind=kOutput, calls=%fused_computation.4 | convolution fusion | flops 268468224 | bytes 4850176 | tf_op jit(solution)/shard_map/dot_general | solution.py:143
  92.6 1.7 %collective-permute-start.10 = (f32[256,64]{0,1:T(8,128)S(1)}, f32[256,64]{0,1:T(8,128)S(1)}, u32[]{:S(2)}, u32[]{:S(2)}) collective-permute-start(f32[256,64]{0,1:T(8,128)S(1)} %get-tuple-element.50), channel_id=1, source_target_pairs={{0,16},{1,17},{16,0},{17,1},{2,18},{3,19},{18,2},{19,3},{4,20},{5,... | collective-permute-start | bytes 196616 | tf_op jit(solution)/shard_map/ppermute | solution.py:103
  94.3 1.8 %collective-permute-done.11 = f32[256,64]{0,1:T(8,128)S(1)} collective-permute-done((f32[256,64]{0,1:T(8,128)S(1)}, f32[256,64]{0,1:T(8,128)S(1)}, u32[]{:S(2)}, u32[]{:S(2)}) %collective-permute-start.11) | collective-permute-done | bytes 65568 | tf_op jit(solution)/shard_map/ppermute | solution.py:103
  96.1 2.0 %collective-permute-done.10 = f32[256,64]{0,1:T(8,128)S(1)} collective-permute-done((f32[256,64]{0,1:T(8,128)S(1)}, f32[256,64]{0,1:T(8,128)S(1)}, u32[]{:S(2)}, u32[]{:S(2)}) %collective-permute-start.10) | collective-permute-done | bytes 65568 | tf_op jit(solution)/shard_map/ppermute | solution.py:103
  98.5 0.8 add_convert_fusion
  (51 shorter events, 3.9 us)
Async XLA Ops:
  7.4 11.7 %copy-start.2 = (bf16[256,4096]{1,0:T(8,128)(2,1)S(1)}, bf16[256,4096]{1,0:T(8,128)(2,1)}, u32[]{:S(2)}) copy-start(bf16[256,4096]{1,0:T(8,128)(2,1)} %param.7) | copy-start | bytes 6291460
  7.4 67.9 %all-gather.3.cloned.1.call-start = ((), (), s32[]{:S(2)}) async-start(), calls=%async_computation.1 | async-start | bytes 6291456 | tf_op jit(solution)/shard_map/all_gather | solution.py:116
  11.5 15.5 %copy-start.3 = (s32[1,8]{1,0:T(1,128)S(1)}, s32[1,8]{1,0:T(1,128)}, u32[]{:S(2)}) copy-start(s32[1,8]{1,0:T(1,128)} %param.13) | copy-start | bytes 100
  11.5 16.3 %copy-start = (s32[32]{0:T(128)S(1)}, s32[32]{0:T(128)}, u32[]{:S(2)}) copy-start(s32[32]{0:T(128)} %home_ref.3) | copy-start | bytes 388
  11.5 75.1 %reduce-scatter.2.cloned.1.call-start = ((), (), s32[]{:S(2)}) async-start(), calls=%async_computation.2 | async-start | bytes 1572864 | tf_op jit(solution)/shard_map/reduce_scatter | solution.py:119
  11.5 29.4 %collective-permute-start.6 = (bf16[64,512]{1,0:T(8,128)(2,1)}, bf16[64,512]{1,0:T(8,128)(2,1)S(1)}, u32[]{:S(2)}, u32[]{:S(2)}) collective-permute-start(bf16[64,512]{1,0:T(8,128)(2,1)} %get-tuple-element.34), channel_id=1, source_target_pairs={{0,10},{2,8},{4,14},{6,12},{8,2},{10,0},{12,6},{14,4},{16,30},{18,... | collective-permute-start | bytes 196616 | tf_op jit(solution)/shard_map/ppermute | solution.py:95
  16.6 28.0 %collective-permute-start = (bf16[64,4608]{1,0:T(8,128)(2,1)}, bf16[64,4608]{1,0:T(8,128)(2,1)S(1)}, u32[]{:S(2)}, u32[]{:S(2)}) collective-permute-start(bf16[64,4608]{1,0:T(8,128)(2,1)} %get-tuple-element.29), channel_id=1, source_target_pairs={{0,4},{2,6},{4,0},{6,2},{8,12},{10,14},{12,8},{14,10},{16,22},{18,... | collective-permute-start | bytes 1769480 | tf_op jit(solution)/shard_map/ppermute | solution.py:95
  18.2 40.7 %collective-permute-start.1 = (bf16[64,4608]{1,0:T(8,128)(2,1)}, bf16[64,4608]{1,0:T(8,128)(2,1)}, u32[]{:S(2)}, u32[]{:S(2)}) collective-permute-start(bf16[64,4608]{1,0:T(8,128)(2,1)} %get-tuple-element.30), channel_id=1, source_target_pairs={{0,8},{2,10},{4,12},{6,14},{8,0},{10,2},{12,4},{14,6},{16,28},{18,... | collective-permute-start | bytes 1769480 | tf_op jit(solution)/shard_map/ppermute | solution.py:95
  18.6 25.4 %collective-permute-start.2 = (bf16[64,4608]{1,0:T(8,128)(2,1)}, bf16[64,4608]{1,0:T(8,128)(2,1)S(1)}, u32[]{:S(2)}, u32[]{:S(2)}) collective-permute-start(bf16[64,4608]{1,0:T(8,128)(2,1)} %get-tuple-element.32), channel_id=1, source_target_pairs={{0,2},{2,0},{4,6},{6,4},{8,10},{10,8},{12,14},{14,12},{16,18},{18,... | collective-permute-start | bytes 1769480 | tf_op jit(solution)/shard_map/ppermute | solution.py:95
  41.0 47.4 %collective-permute-start.8 = (bf16[64,4096]{1,0:T(8,128)(2,1)}, bf16[64,4096]{1,0:T(8,128)(2,1)}, u32[]{:S(2)}, u32[]{:S(2)}) collective-permute-start(bf16[64,4096]{1,0:T(8,128)(2,1)} %get-tuple-element.38), channel_id=1, source_target_pairs={{0,10},{2,8},{4,14},{6,12},{8,2},{10,0},{12,6},{14,4},{16,30},{18,... | collective-permute-start | bytes 1572872 | tf_op jit(solution)/shard_map/ppermute | solution.py:95
  61.1 22.2 %collective-permute-start.7 = (bf16[192,512]{1,0:T(8,128)(2,1)}, bf16[192,512]{1,0:T(8,128)(2,1)}, u32[]{:S(2)}, u32[]{:S(2)}) collective-permute-start(bf16[192,512]{1,0:T(8,128)(2,1)} %pad_maximum_fusion), channel_id=1, source_target_pairs={{0,16},{1,17},{16,0},{17,1},{2,18},{3,19},{18,2},{19,3},{4,20},{5,... | collective-permute-start | bytes 589832 | tf_op jit(solution)/shard_map/ppermute | solution.py:103
  75.3 3.9 %copy-start.1 = (bf16[512,4096]{1,0:T(8,128)(2,1)S(1)}, bf16[512,4096]{1,0:T(8,128)(2,1)}, u32[]{:S(2)}) copy-start(bf16[512,4096]{1,0:T(8,128)(2,1)} %all-gather.3.cloned.1.call-done) | copy-start | bytes 12582916
  80.6 5.2 %collective-permute-start.5 = (f32[256,64]{0,1:T(8,128)S(1)}, f32[256,64]{0,1:T(8,128)S(1)}, u32[]{:S(2)}, u32[]{:S(2)}) collective-permute-start(f32[256,64]{0,1:T(8,128)S(1)} %constant_dynamic-slice_fusion.1), channel_id=1, source_target_pairs={{0,17},{1,16},{16,1},{17,0},{2,19},{3,18},{18,3},{19,2},{4,21},{5,... | collective-permute-start | bytes 196616 | tf_op jit(solution)/shard_map/ppermute | solution.py:103
  80.6 5.8 %collective-permute-start.4 = (f32[256,64]{0,1:T(8,128)S(1)}, f32[256,64]{0,1:T(8,128)S(1)}, u32[]{:S(2)}, u32[]{:S(2)}) collective-permute-start(f32[256,64]{0,1:T(8,128)S(1)} %constant_dynamic-slice_fusion.1), channel_id=1, source_target_pairs={{0,16},{1,17},{16,0},{17,1},{2,18},{3,19},{18,2},{19,3},{4,20},{5,... | collective-permute-start | bytes 196616 | tf_op jit(solution)/shard_map/ppermute | solution.py:103
  82.8 3.6 %collective-permute-start.3 = (f32[256,64]{0,1:T(8,128)S(1)}, f32[256,64]{0,1:T(8,128)S(1)}, u32[]{:S(2)}, u32[]{:S(2)}) collective-permute-start(f32[256,64]{0,1:T(8,128)S(1)} %dynamic-slice_add_fusion), channel_id=1, source_target_pairs={{0,1},{1,0},{16,17},{17,16},{2,3},{3,2},{18,19},{19,18},{4,5},{5,4... | collective-permute-start | bytes 196616 | tf_op jit(solution)/shard_map/ppermute | solution.py:103
  92.1 2.2 %collective-permute-start.9 = (f32[256,64]{0,1:T(8,128)S(1)}, f32[256,64]{0,1:T(8,128)S(1)}, u32[]{:S(2)}, u32[]{:S(2)}) collective-permute-start(f32[256,64]{0,1:T(8,128)S(1)} %get-tuple-element.49), channel_id=1, source_target_pairs={{0,1},{1,0},{16,17},{17,16},{2,3},{3,2},{18,19},{19,18},{4,5},{5,4... | collective-permute-start | bytes 196616 | tf_op jit(solution)/shard_map/ppermute | solution.py:103
  92.3 3.8 %collective-permute-start.11 = (f32[256,64]{0,1:T(8,128)S(1)}, f32[256,64]{0,1:T(8,128)S(1)}, u32[]{:S(2)}, u32[]{:S(2)}) collective-permute-start(f32[256,64]{0,1:T(8,128)S(1)} %get-tuple-element.50), channel_id=1, source_target_pairs={{0,17},{1,16},{16,1},{17,0},{2,19},{3,18},{18,3},{19,2},{4,21},{5,... | collective-permute-start | bytes 196616 | tf_op jit(solution)/shard_map/ppermute | solution.py:103
  92.6 5.4 %collective-permute-start.10 = (f32[256,64]{0,1:T(8,128)S(1)}, f32[256,64]{0,1:T(8,128)S(1)}, u32[]{:S(2)}, u32[]{:S(2)}) collective-permute-start(f32[256,64]{0,1:T(8,128)S(1)} %get-tuple-element.50), channel_id=1, source_target_pairs={{0,16},{1,17},{16,0},{17,1},{2,18},{3,19},{18,2},{19,3},{4,20},{5,... | collective-permute-start | bytes 196616 | tf_op jit(solution)/shard_map/ppermute | solution.py:103
Sparse Core Ops, SparseCore 0:
  11.6 63.6 all-gather.2
Sparse Core Ops, SparseCore 1:
  27.0 8.7 reduce-scatter.1

commit v6 on v5

v6 whole, which is shorter than its diff:
```python
import functools
import jax
import jax.numpy as jnp
from jax import lax
from jax.experimental import pallas as pl
from jax.experimental.pallas import tpu as pltpu
from jax.sharding import PartitionSpec as P

adapter_scale = 2.0


def pack_kernel(blocks, home_ref, fetch_ref, shrink_ref, expand_ref, *refs):
    outs, sems = refs[:-1], refs[-1]
    me, part, half = lax.axis_index("rep"), lax.axis_index("parts"), lax.axis_index("tp")
    per_home, _, depth = shrink_ref.shape
    columns = expand_ref.shape[2] // lax.axis_size("tp")
    listed = fetch_ref.shape[1]
    copies, slots = [], {}
    for at, (group, first, rows) in enumerate(blocks):
        if group not in slots:
            step = jnp.int32(group[0])
            for p, other in enumerate(group):
                step = jnp.where(part == p, other, step)
            peer = me ^ step

            def look(j, slot):
                position = home_ref[fetch_ref[peer, j]]
                return jnp.where(position // per_home == me, position % per_home, slot)

            slots[group] = lax.fori_loop(0, listed, look, jnp.int32(0), unroll=listed <= 8)
        slot = slots[group]
        left = pl.multiple_of(half * columns, 128)
        pieces = (
            (shrink_ref.at[slot, pl.ds(first, rows)], outs[at].at[:, pl.ds(0, depth)]),
            (
                expand_ref.at[slot, pl.ds(first, rows), pl.ds(left, columns)],
                outs[at].at[:, pl.ds(depth, columns)],
            ),
        )
        for n, (source, target) in enumerate(pieces):
            copy = pltpu.make_async_copy(source, target, sems.at[at, n])
            copy.start()
            copies.append(copy)
    for copy in copies:
        copy.wait()


def pack(blocks, columns, adapter_home, fetch_list, panels, expand_panels):
    shapes = [(rows, panels.shape[2] + columns) for _, _, rows in blocks]
    return list(
        pl.pallas_call(
            functools.partial(pack_kernel, blocks),
            out_shape=[jax.ShapeDtypeStruct(shape, panels.dtype) for shape in shapes],
            in_specs=[pl.BlockSpec(memory_space=pltpu.SMEM)] * 2 + [pl.BlockSpec(memory_space=pl.ANY)] * 2,
            out_specs=[pl.BlockSpec(memory_space=pltpu.VMEM)] * len(blocks),
            scratch_shapes=[pltpu.SemaphoreType.DMA((len(blocks), 2))],
            compiler_params=pltpu.CompilerParams(vmem_limit_bytes=56 << 20),
            cost_estimate=pl.CostEstimate(
                flops=0, bytes_accessed=4 * sum(r * w for r, w in shapes), transcendentals=0
            ),
        )(adapter_home, fetch_list, panels, expand_panels)
    )


def on_device(tokens, base_weight, shrink_panels, expand_panels, adapter_home, fetch_list, seg_len):
    per_home, depth, _ = shrink_panels.shape
    replicas, parts, cores = lax.axis_size("rep"), lax.axis_size("parts"), lax.axis_size("tp")
    me, part = lax.axis_index("rep"), lax.axis_index("parts")
    tok_count = tokens.shape[0]
    columns = expand_panels.shape[2] // cores
    panels = jnp.swapaxes(shrink_panels, 1, 2)
    tie = lax.optimization_barrier

    alone, half = max(2, parts), replicas // 2

    def grouped(steps):
        size = len(steps) // parts
        return [tuple(steps[p * size + g] for p in range(parts)) for g in range(size)]

    far = grouped(list(range(half, replicas)))
    near = grouped(list(range(alone, half)))
    groups = far + near
    solo = [(step,) * parts for step in range(1, alone)]

    def hop(x, group):
        pairs = [
            (p * replicas + i, p * replicas + (i ^ group[p]))
            for p in range(parts)
            for i in range(replicas)
        ]
        return lax.ppermute(x, ("parts", "rep"), pairs)

    def across(x):
        return [
            lax.ppermute(x, "parts", [(i, (i + shift) % parts) for i in range(parts)])
            for shift in range(1, parts)
        ]

    def trade(x):
        for shift in range(1, cores):
            x = x + lax.ppermute(x, "tp", [(i, (i + shift) % cores) for i in range(cores)])
        return x

    rank = panels.shape[1]
    cut = rank - 16
    early = near + solo + far[:-1]
    tables = (columns, adapter_home, fetch_list, panels, expand_panels)
    send = pack([(group, 0, rank) for group in early], *tables)
    tokens, send = tie((tokens, send))
    recv = [hop(x, group) for x, group in zip(send, early)]
    base_part = jnp.dot(tokens, base_weight, preferred_element_type=jnp.float32)
    base = lax.psum_scatter(base_part, "tp", scatter_dimension=1, tiled=True)
    panels, base_part = tie((panels, base_part))
    tables = (columns, adapter_home, fetch_list, panels, expand_panels)
    last_low, last_high, own = pack(
        [(far[-1], 0, cut), (far[-1], cut, rank - cut), ((0,) * parts, 0, rank)], *tables
    )
    last_low, recv[: len(near)] = tie((last_low, recv[: len(near)]))
    last_low = hop(last_low, far[-1])
    passed = [across(x) for x in recv[: len(near)]]
    last_high, recv[len(near) :] = tie((last_high, recv[len(near) :]))
    last_high = hop(last_high, far[-1])
    passed += [across(x) for x in recv[len(near) + len(solo) :] + [last_low]]
    last_passed = across(last_high)

    stored = jnp.take(adapter_home, lax.dynamic_index_in_dim(fetch_list, me, 0, keepdims=False))
    steps = (stored // per_home) ^ me
    lengths = seg_len[0]
    ordinal = jnp.arange(lengths.shape[0])
    starts = jnp.sum(jnp.where(ordinal[None, :] < ordinal[:, None], lengths[None, :], 0), axis=1)
    rows = jnp.arange(tok_count, dtype=jnp.int32)
    member = (rows[:, None] >= starts[None, :]) & (rows[:, None] < (starts + lengths)[None, :])
    row_steps = jnp.sum(jnp.where(member, steps[None, :], 0), axis=1)[:, None]

    def step_of(group, shift=0):
        step = jnp.int32(0)
        for p in range(parts):
            step = jnp.where(part == p, group[(p - shift) % parts], step)
        return step

    def score(block, step, tokens):
        product = lax.dot_general(
            tokens,
            block[:, :depth],
            (((1,), (1,)), ((), ())),
            preferred_element_type=jnp.float32,
        )
        return jnp.where(row_steps == step, product, 0.0)

    def spread(scores, blocks):
        return adapter_scale * jnp.dot(
            trade(jnp.concatenate(scores, axis=1)),
            jnp.concatenate([block[:, depth:] for block in blocks], axis=0).astype(jnp.float32),
            precision=lax.Precision.HIGHEST,
            preferred_element_type=jnp.float32,
        )

    blocks = [(own, 0)] + [(x, step_of(group)) for x, group in zip(recv, early)]
    blocks += [(last_low, step_of(far[-1])), (last_high, step_of(far[-1]))]
    for group, came in zip(near + far, passed):
        blocks += [(x, step_of(group, shift + 1)) for shift, x in enumerate(came)]
    scores = tie([score(block, step, tokens) for block, step in blocks])
    result = base + spread(scores, [block for block, _ in blocks])
    tokens, result = tie((tokens, result))
    scores = [score(x, step_of(far[-1], shift + 1), tokens) for shift, x in enumerate(last_passed)]
    result = result + spread(scores, last_passed)
    return result.astype(jnp.bfloat16)


def solution(mesh):
    return jax.shard_map(
        on_device,
        mesh=mesh,
        in_specs=(
            P(("parts", "rep"), "tp"),
            P("tp", None),
            P("rep", "tp", None),
            P("rep", None, None),
            P(),
            P(),
            P(("parts", "rep"), None),
        ),
        out_specs=P(("parts", "rep"), "tp"),
        check_vma=False,
    )
```

time: 107 us -> 104 us (0.972)
  waiting for transfers between devices: 31.7 us -> 44.6 us
  blocking collectives: 4.58 us -> 0 us
  local copies, waits for them, and re-layouts: 7.32 us -> 3.3 us
  other arithmetic: 4.25 us -> 1.63 us
  starting transfers between devices: 15.5 us -> 13.3 us
  between operations: 15.1 us -> 13.7 us
  matrix products: 21.5 us -> 20.3 us
    ppermute x5, waiting for transfers between devices: 13.7 us -> 32.9 us  [hop(): return lax.ppermute(x, ('parts', 'rep'), pairs)]
    all_gather x1 -> x0, waiting for transfers between devices: 13.5 us -> none  [on_device(): every_tokens = lax.all_gather(tokens, 'parts', axis=0, tiled=True)]
    ppermute x7 -> x6, waiting for transfers between devices: 4.45 us -> 11.7 us  [the longest x4 8.69 us: across(): lax.ppermute(x, 'parts', [(i, (i + shift) % parts) for i in range(parts)])]
    all_gather x1 -> x0, blocking collectives: 4.58 us -> none  [on_device(): every_seg_len = lax.all_gather(seg_len, 'parts', axis=0, tiled=True)]
    slice x3 -> x0, local copies, waits for them, and re-layouts: 2.94 us -> none  [the longest x2 2.1 us: on_device(): mine = [x[:, depth:] for x in shared[:-1]] + [last_expand]]
    ppermute x7 -> x6, starting transfers between devices: 4.88 us -> 2.32 us  [the longest x4 2.1 us: across(): lax.ppermute(x, 'parts', [(i, (i + shift) % parts) for i in range(parts)])]
    concatenate x1 -> x2, local copies, waits for them, and re-layouts: 1.55 us -> 0.01 us  [the longest x1 0.01 us: spread(): jnp.concatenate(scores, axis=1)]
    dot_general x1, matrix products: 7.77 us -> 6.69 us  [on_device(): base_part = jnp.dot(tokens, base_weight, preferred_element_type=jnp.float32)]
  transfers between devices with their start and end apart: 14 -> 12, of which waited for: 5 -> 7; matrix products, arithmetic and copies ran while one was open for 26% -> 23% of each run, Pallas kernels for 3% -> 3%
where the time goes in v6:
time: 104 us
  waiting for transfers between devices  44.6 us (43%)
  matrix products  20.3 us (20%)
  between operations  13.7 us (13%)
  starting transfers between devices  13.3 us (13%)
  Pallas kernels  6.79 us (7%)
  local copies, waits for them, and re-layouts  3.3 us (3%)
  other arithmetic  1.63 us (2%)
    ppermute x5, waiting for transfers between devices, hop(): return lax.ppermute(x, ('parts', 'rep'), pairs)  32.9 us
    ppermute x5, starting transfers between devices, hop(): return lax.ppermute(x, ('parts', 'rep'), pairs)  11 us
    dot_general x10, matrix products, score(): lax.dot_general(tokens, block[:, :depth], (((1,), (1,)), ((), ())), prefe...  10.6 us
    ppermute x4, waiting for transfers between devices, across(): lax.ppermute(x, 'parts', [(i, (i + shift) % parts) for i in range(parts)])  8.69 us
    pallas_call x2, Pallas kernels, pack(): pl.pallas_call(functools.partial(pack_kernel, blocks), out_shape=[jax.Sha...  6.79 us
    dot_general x1, matrix products, on_device(): base_part = jnp.dot(tokens, base_weight, preferred_element_type=jnp.float32)  6.69 us
    ppermute x2, waiting for transfers between devices, trade(): lax.ppermute(x, 'tp', [(i, (i + shift) % cores) for i in range(cores)])  3.01 us
    dot_general x2, matrix products, spread(): jnp.dot(trade(jnp.concatenate(scores, axis=1)), jnp.concatenate([block[:,...  2.98 us
  transfers between devices with their start and end apart: 12, of which 7 were waited for; matrix products, arithmetic and copies ran while one was open for 23% of the time, Pallas kernels for 3%

profile of v6, /device:TPU:0, one launch (start us, length us, event | category | flops | bytes accessed | tf_op | source)
XLA Modules:
  0.0 103.6 jit_solution(8181801045681349495)
XLA Ops:
  6.5 3.6 %shard_map.73 = (bf16[64,4608]{1,0:T(8,128)(2,1)}, bf16[64,4608]{1,0:T(8,128)(2,1)}, bf16[64,4608]{1,0:T(8,128)(2,1)}) custom-call(s32[32]{0:T(128)} %home_ref.3, s32[8,8]{1,0:T(8,128)} %fetch_ref.3, bf16[4,64,4096]{2,1,0:T(8,128)(2,1)} %bitcast.31, bf16[4,64,1024]{2,1,0:T(8,128)(2,1)} %expand_ref.3), custom_call_target="tpu_custom_call" | custom-call | bytes 3538944 | tf_op jit(solution)/shard_map/pallas_call | solution.py:51
  10.2 3.1 %collective-permute-start = (bf16[64,4608]{1,0:T(8,128)(2,1)}, bf16[64,4608]{1,0:T(8,128)(2,1)S(1)}, u32[]{:S(2)}, u32[]{:S(2)}) collective-permute-start(bf16[64,4608]{1,0:T(8,128)(2,1)} %get-tuple-element.39), channel_id=1, source_target_pairs={{0,4},{2,6},{4,0},{6,2},{8,12},{10,14},{12,8},{14,10},{16,22},{18,... | collective-permute-start | bytes 1769480 | tf_op jit(solution)/shard_map/ppermute | solution.py:91
  13.3 1.5 %collective-permute-start.1 = (bf16[64,4608]{1,0:T(8,128)(2,1)}, bf16[64,4608]{1,0:T(8,128)(2,1)}, u32[]{:S(2)}, u32[]{:S(2)}) collective-permute-start(bf16[64,4608]{1,0:T(8,128)(2,1)} %get-tuple-element.42), channel_id=1, source_target_pairs={{0,2},{2,0},{4,6},{6,4},{8,10},{10,8},{12,14},{14,12},{16,18},{18,... | collective-permute-start | bytes 1769480 | tf_op jit(solution)/shard_map/ppermute | solution.py:91
  14.8 2.6 %collective-permute-start.2 = (bf16[64,4608]{1,0:T(8,128)(2,1)}, bf16[64,4608]{1,0:T(8,128)(2,1)}, u32[]{:S(2)}, u32[]{:S(2)}) collective-permute-start(bf16[64,4608]{1,0:T(8,128)(2,1)} %get-tuple-element.43), channel_id=1, source_target_pairs={{0,8},{2,10},{4,12},{6,14},{8,0},{10,2},{12,4},{14,6},{16,28},{18,... | collective-permute-start | bytes 1769480 | tf_op jit(solution)/shard_map/ppermute | solution.py:91
  17.4 6.7 %fusion.19 = f32[256,1024]{1,0:T(8,128)} fusion(bf16[256,4096]{1,0:T(8,128)(2,1)S(1)} %copy-done, bf16[4096,1024]{1,0:T(8,128)(2,1)} %param.8), kind=kOutput, calls=%fused_computation.74 | convolution fusion | flops 2147483648 | bytes 11534336 | tf_op jit(solution)/shard_map/dot_general | solution.py:111
  24.3 0.7 fusion.17
  25.6 0.7 fusion.18
  26.4 3.2 %shard_map.74 = (bf16[48,4608]{1,0:T(8,128)(2,1)}, bf16[16,4608]{1,0:T(8,128)(2,1)}, bf16[64,4608]{1,0:T(8,128)(2,1)}) custom-call(s32[32]{0:T(128)} %home_ref.3, s32[8,8]{1,0:T(8,128)} %fetch_ref.3, bf16[4,64,4096]{2,1,0:T(8,128)(2,1)} %bitcast.32, bf16[4,64,1024]{2,1,0:T(8,128)(2,1)} %expand_ref.3), custom_call_target="tpu_custom_call" | custom-call | bytes 2359296 | tf_op jit(solution)/shard_map/pallas_call | solution.py:51
  29.6 0.8 slice_dynamic-update-slice_fusion.5
  30.5 1.8 %convolution_select_fusion.5 = f32[256,64]{0,1:T(8,128)S(1)} fusion(bf16[256,4096]{1,0:T(8,128)(2,1)S(1)} %copy-done, bf16[64,4608]{1,0:T(8,128)(2,1)} %get-tuple-element.37, pred[256]{0:T(512)(128)(4,1)S(1)} %get-tuple-element.66), kind=kOutput, calls=%fused_computation.11 | convolution fusion | flops 134234112 | bytes 2687232 | tf_op jit(solution)/shard_map/dot_general | solution.py:142
  32.3 6.0 %collective-permute-done = bf16[64,4608]{1,0:T(8,128)(2,1)S(1)} collective-permute-done((bf16[64,4608]{1,0:T(8,128)(2,1)}, bf16[64,4608]{1,0:T(8,128)(2,1)S(1)}, u32[]{:S(2)}, u32[]{:S(2)}) %collective-permute-start) | collective-permute-done | bytes 589856 | tf_op jit(solution)/shard_map/ppermute | solution.py:91
  38.2 5.0 %collective-permute-done.2 = bf16[64,4608]{1,0:T(8,128)(2,1)} collective-permute-done((bf16[64,4608]{1,0:T(8,128)(2,1)}, bf16[64,4608]{1,0:T(8,128)(2,1)}, u32[]{:S(2)}, u32[]{:S(2)}) %collective-permute-start.2) | collective-permute-done | bytes 589856 | tf_op jit(solution)/shard_map/ppermute | solution.py:91
  43.2 1.1 %collective-permute-start.6 = (bf16[64,4608]{1,0:T(8,128)(2,1)}, bf16[64,4608]{1,0:T(8,128)(2,1)S(1)}, u32[]{:S(2)}, u32[]{:S(2)}) collective-permute-start(bf16[64,4608]{1,0:T(8,128)(2,1)} %collective-permute-done.2), channel_id=1, source_target_pairs={{0,16},{16,0},{1,17},{17,1},{2,18},{18,2},{3,19},{19,3},{4,20},{20... | collective-permute-start | bytes 1769480 | tf_op jit(solution)/shard_map/ppermute | solution.py:95
  44.4 1.8 %convolution_select_fusion.2 = f32[256,64]{0,1:T(8,128)S(1)} fusion(bf16[256,4096]{1,0:T(8,128)(2,1)S(1)} %copy-done, bf16[64,4608]{1,0:T(8,128)(2,1)} %collective-permute-done.2, pred[256]{0:T(512)(128)(4,1)S(1)} %get-tuple-element.63), kind=kOutput, calls=%fused_computation.8 | convolution fusion | flops 134234112 | bytes 2687232 | tf_op jit(solution)/shard_map/dot_general | solution.py:142
  46.2 0.9 collective-permute-start.5
  47.1 0.8 convolution_select_fusion.4
  47.9 1.9 %convolution_select_fusion.3 = f32[256,64]{0,1:T(8,128)S(1)} fusion(bf16[256,4096]{1,0:T(8,128)(2,1)S(1)} %copy-done, bf16[64,4608]{1,0:T(8,128)(2,1)} %collective-permute-done.1, pred[256]{0:T(512)(128)(4,1)S(1)} %get-tuple-element.64), kind=kOutput, calls=%fused_computation.9 | convolution fusion | flops 134234112 | bytes 2687232 | tf_op jit(solution)/shard_map/dot_general | solution.py:142
  49.8 0.8 slice_dynamic-update-slice_fusion.3
  50.6 2.0 %collective-permute-start.4 = (bf16[16,4608]{1,0:T(8,128)(2,1)S(1)}, bf16[16,4608]{1,0:T(8,128)(2,1)S(1)}, u32[]{:S(2)}, u32[]{:S(2)}) collective-permute-start(bf16[16,4608]{1,0:T(8,128)(2,1)S(1)} %copy-done.4), channel_id=1, source_target_pairs={{0,10},{2,8},{4,14},{6,12},{8,2},{10,0},{12,6},{14,4},{16,30},{18,... | collective-permute-start | bytes 442376 | tf_op jit(solution)/shard_map/ppermute | solution.py:91
  52.7 1.8 %collective-permute-start.3 = (bf16[48,4608]{1,0:T(8,128)(2,1)S(1)}, bf16[48,4608]{1,0:T(8,128)(2,1)S(1)}, u32[]{:S(2)}, u32[]{:S(2)}) collective-permute-start(bf16[48,4608]{1,0:T(8,128)(2,1)S(1)} %copy-done.3), channel_id=1, source_target_pairs={{0,10},{2,8},{4,14},{6,12},{8,2},{10,0},{12,6},{14,4},{16,30},{18,... | collective-permute-start | bytes 1327112 | tf_op jit(solution)/shard_map/ppermute | solution.py:91
  54.5 0.8 slice_dynamic-update-slice_fusion.2
  55.3 14.3 %collective-permute-done.4 = bf16[16,4608]{1,0:T(8,128)(2,1)S(1)} collective-permute-done((bf16[16,4608]{1,0:T(8,128)(2,1)S(1)}, bf16[16,4608]{1,0:T(8,128)(2,1)S(1)}, u32[]{:S(2)}, u32[]{:S(2)}) %collective-permute-start.4) | collective-permute-done | bytes 147488 | tf_op jit(solution)/shard_map/ppermute | solution.py:91
  70.3 7.7 %collective-permute-done.3 = bf16[48,4608]{1,0:T(8,128)(2,1)S(1)} collective-permute-done((bf16[48,4608]{1,0:T(8,128)(2,1)S(1)}, bf16[48,4608]{1,0:T(8,128)(2,1)S(1)}, u32[]{:S(2)}, u32[]{:S(2)}) %collective-permute-start.3) | collective-permute-done | bytes 442400 | tf_op jit(solution)/shard_map/ppermute | solution.py:91
  78.0 0.7 convolution_select_fusion.7
  78.8 0.8 convolution_select_fusion
  79.5 0.8 convolution_select_fusion.1
  80.3 8.7 %collective-permute-done.7 = bf16[48,4608]{1,0:T(8,128)(2,1)S(1)} collective-permute-done((bf16[48,4608]{1,0:T(8,128)(2,1)S(1)}, bf16[48,4608]{1,0:T(8,128)(2,1)S(1)}, u32[]{:S(2)}, u32[]{:S(2)}) %collective-permute-start.7) | collective-permute-done | bytes 442400 | tf_op jit(solution)/shard_map/ppermute | solution.py:95
  89.0 0.7 convolution_select_fusion.6
  90.0 2.0 %collective-permute-done.8 = f32[256,496]{0,1:T(8,128)} collective-permute-done((f32[256,496]{0,1:T(8,128)S(1)}, f32[256,496]{0,1:T(8,128)}, u32[]{:S(2)}, u32[]{:S(2)}) %collective-permute-start.8) | collective-permute-done | bytes 507936 | tf_op jit(solution)/shard_map/ppermute | solution.py:101
  91.9 1.8 %fusion = f32[256,512]{1,0:T(8,128)S(1)} fusion(f32[256,512]{1,0:T(8,128)} %reduce-scatter.2.cloned.1.call-done, bf16[496,512]{1,0:T(8,128)(2,1)S(1)} %slice_dynamic-update-slice_fusion.6, f32[256,496]{0,1:T(8,128)S(1)} %constant_dynamic-update-slice_fusion, f32[256,496]{0,1:T(8,128)} %collective-permute-done.8), kind=kOutput, calls=%fused_computation.3 | convolution fusion | flops 780529664 | bytes 2572288 | tf_op jit(solution)/shard_map/dot_general | solution.py:151
  94.6 1.0 %collective-permute-done.10 = f32[256,16]{0,1:T(8,128)S(1)} collective-permute-done((f32[256,16]{0,1:T(8,128)S(1)}, f32[256,16]{0,1:T(8,128)S(1)}, u32[]{:S(2)}, u32[]{:S(2)}) %collective-permute-start.10) | collective-permute-done | bytes 16416 | tf_op jit(solution)/shard_map/ppermute | solution.py:101
  95.7 1.1 %fusion.2 = bf16[256,512]{1,0:T(8,128)(2,1)} fusion(f32[256,512]{1,0:T(8,128)S(1)} %fusion, bf16[16,4608]{1,0:T(8,128)(2,1)S(1)} %collective-permute-done.9, f32[256,16]{0,1:T(8,128)S(1)} %convolution_select_fusion.8, f32[256,16]{0,1:T(8,128)S(1)} %collective-permute-done.10), kind=kOutput, calls=%fused_computation.5 | convolution fusion | flops 25563136 | bytes 835584 | tf_op jit(solution)/shard_map/dot_general | solution.py:151
  (43 shorter events, 2.5 us)
Async XLA Ops:
  6.5 10.9 %copy-start = (bf16[256,4096]{1,0:T(8,128)(2,1)S(1)}, bf16[256,4096]{1,0:T(8,128)(2,1)}, u32[]{:S(2)}) copy-start(bf16[256,4096]{1,0:T(8,128)(2,1)} %param.7) | copy-start | bytes 6291460
  6.5 85.4 %reduce-scatter.2.cloned.1.call-start = ((), (), s32[]{:S(2)}) async-start(), calls=%async_computation.1 | async-start | bytes 1572864 | tf_op jit(solution)/shard_map/reduce_scatter | solution.py:112
  10.2 14.0 %copy-start.2 = (s32[1,8]{1,0:T(1,128)S(1)}, s32[1,8]{1,0:T(1,128)}, u32[]{:S(2)}) copy-start(s32[1,8]{1,0:T(1,128)} %param.13) | copy-start | bytes 100
  10.2 14.8 %copy-start.1 = (s32[32]{0:T(128)S(1)}, s32[32]{0:T(128)}, u32[]{:S(2)}) copy-start(s32[32]{0:T(128)} %home_ref.3) | copy-start | bytes 388
  10.2 28.0 %collective-permute-start = (bf16[64,4608]{1,0:T(8,128)(2,1)}, bf16[64,4608]{1,0:T(8,128)(2,1)S(1)}, u32[]{:S(2)}, u32[]{:S(2)}) collective-permute-start(bf16[64,4608]{1,0:T(8,128)(2,1)} %get-tuple-element.39), channel_id=1, source_target_pairs={{0,4},{2,6},{4,0},{6,2},{8,12},{10,14},{12,8},{14,10},{16,22},{18,... | collective-permute-start | bytes 1769480 | tf_op jit(solution)/shard_map/ppermute | solution.py:91
  13.3 25.0 %collective-permute-start.1 = (bf16[64,4608]{1,0:T(8,128)(2,1)}, bf16[64,4608]{1,0:T(8,128)(2,1)}, u32[]{:S(2)}, u32[]{:S(2)}) collective-permute-start(bf16[64,4608]{1,0:T(8,128)(2,1)} %get-tuple-element.42), channel_id=1, source_target_pairs={{0,2},{2,0},{4,6},{6,4},{8,10},{10,8},{12,14},{14,12},{16,18},{18,... | collective-permute-start | bytes 1769480 | tf_op jit(solution)/shard_map/ppermute | solution.py:91
  14.8 28.4 %collective-permute-start.2 = (bf16[64,4608]{1,0:T(8,128)(2,1)}, bf16[64,4608]{1,0:T(8,128)(2,1)}, u32[]{:S(2)}, u32[]{:S(2)}) collective-permute-start(bf16[64,4608]{1,0:T(8,128)(2,1)} %get-tuple-element.43), channel_id=1, source_target_pairs={{0,8},{2,10},{4,12},{6,14},{8,0},{10,2},{12,4},{14,6},{16,28},{18,... | collective-permute-start | bytes 1769480 | tf_op jit(solution)/shard_map/ppermute | solution.py:91
  43.2 35.5 %collective-permute-start.6 = (bf16[64,4608]{1,0:T(8,128)(2,1)}, bf16[64,4608]{1,0:T(8,128)(2,1)S(1)}, u32[]{:S(2)}, u32[]{:S(2)}) collective-permute-start(bf16[64,4608]{1,0:T(8,128)(2,1)} %collective-permute-done.2), channel_id=1, source_target_pairs={{0,16},{16,0},{1,17},{17,1},{2,18},{18,2},{3,19},{19,3},{4,20},{20... | collective-permute-start | bytes 1769480 | tf_op jit(solution)/shard_map/ppermute | solution.py:95
  46.2 33.3 %collective-permute-start.5 = (bf16[64,4608]{1,0:T(8,128)(2,1)S(1)}, bf16[64,4608]{1,0:T(8,128)(2,1)S(1)}, u32[]{:S(2)}, u32[]{:S(2)}) collective-permute-start(bf16[64,4608]{1,0:T(8,128)(2,1)S(1)} %collective-permute-done), channel_id=1, source_target_pairs={{0,16},{16,0},{1,17},{17,1},{2,18},{18,2},{3,19},{19,3},{4,20},{20... | collective-permute-start | bytes 1769480 | tf_op jit(solution)/shard_map/ppermute | solution.py:95
  47.9 2.8 %copy-start.4 = (bf16[16,4608]{1,0:T(8,128)(2,1)S(1)}, bf16[16,4608]{1,0:T(8,128)(2,1)}, u32[]{:S(2)}) copy-start(bf16[16,4608]{1,0:T(8,128)(2,1)} %get-tuple-element.47) | copy-start | bytes 442372
  47.9 4.8 %copy-start.3 = (bf16[48,4608]{1,0:T(8,128)(2,1)S(1)}, bf16[48,4608]{1,0:T(8,128)(2,1)}, u32[]{:S(2)}) copy-start(bf16[48,4608]{1,0:T(8,128)(2,1)} %get-tuple-element.46) | copy-start | bytes 1327108
  50.6 19.0 %collective-permute-start.4 = (bf16[16,4608]{1,0:T(8,128)(2,1)S(1)}, bf16[16,4608]{1,0:T(8,128)(2,1)S(1)}, u32[]{:S(2)}, u32[]{:S(2)}) collective-permute-start(bf16[16,4608]{1,0:T(8,128)(2,1)S(1)} %copy-done.4), channel_id=1, source_target_pairs={{0,10},{2,8},{4,14},{6,12},{8,2},{10,0},{12,6},{14,4},{16,30},{18,... | collective-permute-start | bytes 442376 | tf_op jit(solution)/shard_map/ppermute | solution.py:91
  52.7 25.3 %collective-permute-start.3 = (bf16[48,4608]{1,0:T(8,128)(2,1)S(1)}, bf16[48,4608]{1,0:T(8,128)(2,1)S(1)}, u32[]{:S(2)}, u32[]{:S(2)}) collective-permute-start(bf16[48,4608]{1,0:T(8,128)(2,1)S(1)} %copy-done.3), channel_id=1, source_target_pairs={{0,10},{2,8},{4,14},{6,12},{8,2},{10,0},{12,6},{14,4},{16,30},{18,... | collective-permute-start | bytes 1327112 | tf_op jit(solution)/shard_map/ppermute | solution.py:91
  69.7 24.1 %collective-permute-start.9 = (bf16[16,4608]{1,0:T(8,128)(2,1)S(1)}, bf16[16,4608]{1,0:T(8,128)(2,1)S(1)}, u32[]{:S(2)}, u32[]{:S(2)}) collective-permute-start(bf16[16,4608]{1,0:T(8,128)(2,1)S(1)} %collective-permute-done.4), channel_id=1, source_target_pairs={{0,16},{16,0},{1,17},{17,1},{2,18},{18,2},{3,19},{19,3},{4,20},{20... | collective-permute-start | bytes 442376 | tf_op jit(solution)/shard_map/ppermute | solution.py:95
  78.0 11.0 %collective-permute-start.7 = (bf16[48,4608]{1,0:T(8,128)(2,1)S(1)}, bf16[48,4608]{1,0:T(8,128)(2,1)S(1)}, u32[]{:S(2)}, u32[]{:S(2)}) collective-permute-start(bf16[48,4608]{1,0:T(8,128)(2,1)S(1)} %collective-permute-done.3), channel_id=1, source_target_pairs={{0,16},{16,0},{1,17},{17,1},{2,18},{18,2},{3,19},{19,3},{4,20},{20... | collective-permute-start | bytes 1327112 | tf_op jit(solution)/shard_map/ppermute | solution.py:95
  89.9 2.1 %collective-permute-start.8 = (f32[256,496]{0,1:T(8,128)S(1)}, f32[256,496]{0,1:T(8,128)}, u32[]{:S(2)}, u32[]{:S(2)}) collective-permute-start(f32[256,496]{0,1:T(8,128)S(1)} %constant_dynamic-update-slice_fusion), channel_id=1, source_target_pairs={{0,1},{1,0},{2,3},{3,2},{4,5},{5,4},{6,7},{7,6},{8,9},{9,8},{10,11... | collective-permute-start | bytes 1523720 | tf_op jit(solution)/shard_map/ppermute | solution.py:101
  94.5 1.2 %collective-permute-start.10 = (f32[256,16]{0,1:T(8,128)S(1)}, f32[256,16]{0,1:T(8,128)S(1)}, u32[]{:S(2)}, u32[]{:S(2)}) collective-permute-start(f32[256,16]{0,1:T(8,128)S(1)} %convolution_select_fusion.8), channel_id=1, source_target_pairs={{0,1},{1,0},{2,3},{3,2},{4,5},{5,4},{6,7},{7,6},{8,9},{9,8},{10,11... | collective-permute-start | bytes 49160 | tf_op jit(solution)/shard_map/ppermute | solution.py:101
Sparse Core Ops, SparseCore 0:
  24.2 7.3 reduce-scatter.1

commit v7 on v6

--- a/solution.py
+++ b/solution.py
@@ -103,11 +103,12 @@
 
     rank = panels.shape[1]
     cut = rank - 16
-    early = near + solo + far[:-1]
+    early = near + far[:-1] + solo
     tables = (columns, adapter_home, fetch_list, panels, expand_panels)
     send = pack([(group, 0, rank) for group in early], *tables)
     tokens, send = tie((tokens, send))
-    recv = [hop(x, group) for x, group in zip(send, early)]
+    recv = [hop(x, group) for x, group in zip(send[: -len(solo)], early)]
+    near_recv, far_recv = recv[: len(near)], recv[len(near) :]
     base_part = jnp.dot(tokens, base_weight, preferred_element_type=jnp.float32)
     base = lax.psum_scatter(base_part, "tp", scatter_dimension=1, tiled=True)
     panels, base_part = tie((panels, base_part))
@@ -115,12 +116,13 @@
     last_low, last_high, own = pack(
         [(far[-1], 0, cut), (far[-1], cut, rank - cut), ((0,) * parts, 0, rank)], *tables
     )
-    last_low, recv[: len(near)] = tie((last_low, recv[: len(near)]))
+    last_low, solo_send, near_recv = tie((last_low, send[-len(solo) :], near_recv))
     last_low = hop(last_low, far[-1])
-    passed = [across(x) for x in recv[: len(near)]]
-    last_high, recv[len(near) :] = tie((last_high, recv[len(near) :]))
+    solo_recv = [hop(x, group) for x, group in zip(solo_send, solo)]
+    passed = [across(x) for x in near_recv]
+    last_high, passed = tie((last_high, passed))
     last_high = hop(last_high, far[-1])
-    passed += [across(x) for x in recv[len(near) + len(solo) :] + [last_low]]
+    passed += [across(x) for x in far_recv + [last_low]]
     last_passed = across(last_high)
 
     stored = jnp.take(adapter_home, lax.dynamic_index_in_dim(fetch_list, me, 0, keepdims=False))
@@ -155,7 +157,7 @@
             preferred_element_type=jnp.float32,
         )
 
-    blocks = [(own, 0)] + [(x, step_of(group)) for x, group in zip(recv, early)]
+    blocks = [(own, 0)] + [(x, step_of(group)) for x, group in zip(near_recv + far_recv + solo_recv, early)]
     blocks += [(last_low, step_of(far[-1])), (last_high, step_of(far[-1]))]
     for group, came in zip(near + far, passed):
         blocks += [(x, step_of(group, shift + 1)) for shift, x in enumerate(came)]

time: 104 us -> 95.2 us (0.915)
  waiting for transfers between devices: 44.6 us -> 28.2 us
  starting transfers between devices: 13.3 us -> 22.6 us
  matrix products: 20.3 us -> 19.2 us
    ppermute x5, waiting for transfers between devices: 32.9 us -> 16 us  [hop(): return lax.ppermute(x, ('parts', 'rep'), pairs)]
    ppermute x4, starting transfers between devices: 2.1 us -> 10.7 us  [across(): lax.ppermute(x, 'parts', [(i, (i + shift) % parts) for i in range(parts)])]
    dot_general x10, matrix products: 10.6 us -> 9.49 us  [score(): lax.dot_general(tokens, block[:, :depth], (((1,), (1,)), ((), ())), prefe...]
    unnamed x26 -> x28, local copies, waits for them, and re-layouts: 2.64 us -> 1.84 us
  transfers between devices with their start and end apart: 12 -> 12, of which waited for: 7 -> 8; matrix products, arithmetic and copies ran while one was open for 23% -> 23% of each run, Pallas kernels for 3% -> 3%
where the time goes in v7:
time: 95.2 us; the launch traced here: 94.7 us
  waiting for transfers between devices  28.2 us (30%)
  starting transfers between devices  22.6 us (24%)
  matrix products  19.2 us (20%)
  between operations  13.7 us (14%)
  Pallas kernels  6.97 us (7%)
  local copies, waits for them, and re-layouts  2.49 us (3%)
  other arithmetic  1.63 us (2%)
    ppermute x5, waiting for transfers between devices, hop(): return lax.ppermute(x, ('parts', 'rep'), pairs)  16 us
    ppermute x5, starting transfers between devices, hop(): return lax.ppermute(x, ('parts', 'rep'), pairs)  11.8 us
    ppermute x4, starting transfers between devices, across(): lax.ppermute(x, 'parts', [(i, (i + shift) % parts) for i in range(parts)])  10.7 us
    dot_general x10, matrix products, score(): lax.dot_general(tokens, block[:, :depth], (((1,), (1,)), ((), ())), prefe...  9.49 us
    ppermute x4, waiting for transfers between devices, across(): lax.ppermute(x, 'parts', [(i, (i + shift) % parts) for i in range(parts)])  9.36 us
    pallas_call x2, Pallas kernels, pack(): pl.pallas_call(functools.partial(pack_kernel, blocks), out_shape=[jax.Sha...  6.97 us
    dot_general x1, matrix products, on_device(): base_part = jnp.dot(tokens, base_weight, preferred_element_type=jnp.float32)  6.69 us
    dot_general x2, matrix products, spread(): jnp.dot(trade(jnp.concatenate(scores, axis=1)), jnp.concatenate([block[:,...  2.98 us
  transfers between devices with their start and end apart: 12, of which 8 were waited for; matrix products, arithmetic and copies ran while one was open for 23% of the time, Pallas kernels for 3%

profile of v7, /device:TPU:0, one launch (start us, length us, event | category | flops | bytes accessed | tf_op | source)
XLA Modules:
  0.0 94.7 jit_solution(9473338859875850858)
XLA Ops:
  6.5 3.7 %shard_map.73 = (bf16[64,4608]{1,0:T(8,128)(2,1)}, bf16[64,4608]{1,0:T(8,128)(2,1)}, bf16[64,4608]{1,0:T(8,128)(2,1)}) custom-call(s32[32]{0:T(128)} %home_ref.3, s32[8,8]{1,0:T(8,128)} %fetch_ref.3, bf16[4,64,4096]{2,1,0:T(8,128)(2,1)} %bitcast.31, bf16[4,64,1024]{2,1,0:T(8,128)(2,1)} %expand_ref.3), custom_call_target="tpu_custom_call" | custom-call | bytes 3538944 | tf_op jit(solution)/shard_map/pallas_call | solution.py:51
  10.2 3.1 %collective-permute-start = (bf16[64,4608]{1,0:T(8,128)(2,1)}, bf16[64,4608]{1,0:T(8,128)(2,1)}, u32[]{:S(2)}, u32[]{:S(2)}) collective-permute-start(bf16[64,4608]{1,0:T(8,128)(2,1)} %get-tuple-element.40), channel_id=1, source_target_pairs={{0,4},{2,6},{4,0},{6,2},{8,12},{10,14},{12,8},{14,10},{16,22},{18,... | collective-permute-start | bytes 1769480 | tf_op jit(solution)/shard_map/ppermute | solution.py:91
  13.3 2.6 %collective-permute-start.1 = (bf16[64,4608]{1,0:T(8,128)(2,1)}, bf16[64,4608]{1,0:T(8,128)(2,1)S(1)}, u32[]{:S(2)}, u32[]{:S(2)}) collective-permute-start(bf16[64,4608]{1,0:T(8,128)(2,1)} %get-tuple-element.42), channel_id=1, source_target_pairs={{0,8},{2,10},{4,12},{6,14},{8,0},{10,2},{12,4},{14,6},{16,28},{18,... | collective-permute-start | bytes 1769480 | tf_op jit(solution)/shard_map/ppermute | solution.py:91
  15.9 6.7 %fusion.19 = f32[256,1024]{1,0:T(8,128)} fusion(bf16[256,4096]{1,0:T(8,128)(2,1)S(1)} %copy-done, bf16[4096,1024]{1,0:T(8,128)(2,1)} %param.8), kind=kOutput, calls=%fused_computation.74 | convolution fusion | flops 2147483648 | bytes 11534336 | tf_op jit(solution)/shard_map/dot_general | solution.py:112
  22.8 0.7 fusion.17
  23.5 0.6 gather_fusion
  24.1 0.7 fusion.18
  25.0 3.3 %shard_map.74 = (bf16[48,4608]{1,0:T(8,128)(2,1)}, bf16[16,4608]{1,0:T(8,128)(2,1)}, bf16[64,4608]{1,0:T(8,128)(2,1)}) custom-call(s32[32]{0:T(128)} %home_ref.3, s32[8,8]{1,0:T(8,128)} %fetch_ref.3, bf16[4,64,4096]{2,1,0:T(8,128)(2,1)} %bitcast.32, bf16[4,64,1024]{2,1,0:T(8,128)(2,1)} %expand_ref.3), custom_call_target="tpu_custom_call" | custom-call | bytes 2359296 | tf_op jit(solution)/shard_map/pallas_call | solution.py:51
  28.3 1.9 %convolution_select_fusion.5 = f32[256,64]{0,1:T(8,128)S(1)} fusion(bf16[256,4096]{1,0:T(8,128)(2,1)S(1)} %copy-done, bf16[64,4608]{1,0:T(8,128)(2,1)} %get-tuple-element.37, pred[256]{0:T(512)(128)(4,1)S(1)} %get-tuple-element.66), kind=kOutput, calls=%fused_computation.11 | convolution fusion | flops 134234112 | bytes 2687232 | tf_op jit(solution)/shard_map/dot_general | solution.py:144
  30.2 0.8 slice_dynamic-update-slice_fusion.5
  31.0 8.5 %collective-permute-done = bf16[64,4608]{1,0:T(8,128)(2,1)} collective-permute-done((bf16[64,4608]{1,0:T(8,128)(2,1)}, bf16[64,4608]{1,0:T(8,128)(2,1)}, u32[]{:S(2)}, u32[]{:S(2)}) %collective-permute-start) | collective-permute-done | bytes 589856 | tf_op jit(solution)/shard_map/ppermute | solution.py:91
  39.5 1.7 %collective-permute-start.3 = (bf16[48,4608]{1,0:T(8,128)(2,1)S(1)}, bf16[48,4608]{1,0:T(8,128)(2,1)S(1)}, u32[]{:S(2)}, u32[]{:S(2)}) collective-permute-start(bf16[48,4608]{1,0:T(8,128)(2,1)S(1)} %copy-done.4), channel_id=1, source_target_pairs={{0,10},{2,8},{4,14},{6,12},{8,2},{10,0},{12,6},{14,4},{16,30},{18,... | collective-permute-start | bytes 1327112 | tf_op jit(solution)/shard_map/ppermute | solution.py:91
  41.7 10.3 %collective-permute-start.4 = (bf16[64,4608]{1,0:T(8,128)(2,1)}, bf16[64,4608]{1,0:T(8,128)(2,1)S(1)}, u32[]{:S(2)}, u32[]{:S(2)}) collective-permute-start(bf16[64,4608]{1,0:T(8,128)(2,1)} %collective-permute-done), channel_id=1, source_target_pairs={{0,16},{16,0},{1,17},{17,1},{2,18},{18,2},{3,19},{19,3},{4,20},{20... | collective-permute-start | bytes 1769480 | tf_op jit(solution)/shard_map/ppermute | solution.py:95
  52.0 0.9 slice_dynamic-update-slice_fusion.4
  52.8 1.8 %convolution_select_fusion.4 = f32[256,64]{0,1:T(8,128)S(1)} fusion(bf16[256,4096]{1,0:T(8,128)(2,1)S(1)} %copy-done, bf16[64,4608]{1,0:T(8,128)(2,1)} %collective-permute-done, pred[256]{0:T(512)(128)(4,1)S(1)} %get-tuple-element.65), kind=kOutput, calls=%fused_computation.10 | convolution fusion | flops 134234112 | bytes 2687232 | tf_op jit(solution)/shard_map/dot_general | solution.py:144
  54.8 0.8 convolution_select_fusion.3
  55.5 6.4 %collective-permute-done.3 = bf16[48,4608]{1,0:T(8,128)(2,1)S(1)} collective-permute-done((bf16[48,4608]{1,0:T(8,128)(2,1)S(1)}, bf16[48,4608]{1,0:T(8,128)(2,1)S(1)}, u32[]{:S(2)}, u32[]{:S(2)}) %collective-permute-start.3) | collective-permute-done | bytes 442400 | tf_op jit(solution)/shard_map/ppermute | solution.py:91
  62.0 0.7 convolution_select_fusion.7
  62.7 3.9 %collective-permute-start.5 = (bf16[16,4608]{1,0:T(8,128)(2,1)S(1)}, bf16[16,4608]{1,0:T(8,128)(2,1)S(1)}, u32[]{:S(2)}, u32[]{:S(2)}) collective-permute-start(bf16[16,4608]{1,0:T(8,128)(2,1)S(1)} %copy-done.5), channel_id=1, source_target_pairs={{0,10},{2,8},{4,14},{6,12},{8,2},{10,0},{12,6},{14,4},{16,30},{18,... | collective-permute-start | bytes 442376 | tf_op jit(solution)/shard_map/ppermute | solution.py:91
  66.7 0.8 convolution_select_fusion.1
  67.5 0.8 convolution_select_fusion.2
  68.2 3.5 %collective-permute-done.6 = bf16[64,4608]{1,0:T(8,128)(2,1)S(1)} collective-permute-done((bf16[64,4608]{1,0:T(8,128)(2,1)S(1)}, bf16[64,4608]{1,0:T(8,128)(2,1)S(1)}, u32[]{:S(2)}, u32[]{:S(2)}) %collective-permute-start.6) | collective-permute-done | bytes 589856 | tf_op jit(solution)/shard_map/ppermute | solution.py:95
  71.7 0.8 convolution_select_fusion
  72.5 1.1 %collective-permute-done.5 = bf16[16,4608]{1,0:T(8,128)(2,1)S(1)} collective-permute-done((bf16[16,4608]{1,0:T(8,128)(2,1)S(1)}, bf16[16,4608]{1,0:T(8,128)(2,1)S(1)}, u32[]{:S(2)}, u32[]{:S(2)}) %collective-permute-start.5) | collective-permute-done | bytes 147488 | tf_op jit(solution)/shard_map/ppermute | solution.py:91
  74.2 3.5 %collective-permute-done.7 = bf16[48,4608]{1,0:T(8,128)(2,1)S(1)} collective-permute-done((bf16[48,4608]{1,0:T(8,128)(2,1)S(1)}, bf16[48,4608]{1,0:T(8,128)(2,1)S(1)}, u32[]{:S(2)}, u32[]{:S(2)}) %collective-permute-start.7) | collective-permute-done | bytes 442400 | tf_op jit(solution)/shard_map/ppermute | solution.py:95
  77.7 0.7 convolution_select_fusion.6
  79.0 1.6 %collective-permute-done.8 = f32[256,496]{0,1:T(8,128)} collective-permute-done((f32[256,496]{0,1:T(8,128)S(1)}, f32[256,496]{0,1:T(8,128)}, u32[]{:S(2)}, u32[]{:S(2)}) %collective-permute-start.8) | collective-permute-done | bytes 507936 | tf_op jit(solution)/shard_map/ppermute | solution.py:101
  80.6 1.8 %fusion = f32[256,512]{1,0:T(8,128)S(1)} fusion(f32[256,512]{1,0:T(8,128)} %reduce-scatter.2.cloned.1.call-done, bf16[496,512]{1,0:T(8,128)(2,1)S(1)} %slice_dynamic-update-slice_fusion.6, f32[256,496]{0,1:T(8,128)S(1)} %constant_dynamic-update-slice_fusion, f32[256,496]{0,1:T(8,128)} %collective-permute-done.8), kind=kOutput, calls=%fused_computation.3 | convolution fusion | flops 780529664 | bytes 2572288 | tf_op jit(solution)/shard_map/dot_general | solution.py:153
  82.5 2.4 %collective-permute-done.9 = bf16[16,4608]{1,0:T(8,128)(2,1)S(1)} collective-permute-done((bf16[16,4608]{1,0:T(8,128)(2,1)S(1)}, bf16[16,4608]{1,0:T(8,128)(2,1)S(1)}, u32[]{:S(2)}, u32[]{:S(2)}) %collective-permute-start.9) | collective-permute-done | bytes 147488 | tf_op jit(solution)/shard_map/ppermute | solution.py:95
  84.9 0.6 convolution_select_fusion.8
  85.5 1.2 %collective-permute-done.10 = f32[256,16]{0,1:T(8,128)S(1)} collective-permute-done((f32[256,16]{0,1:T(8,128)S(1)}, f32[256,16]{0,1:T(8,128)S(1)}, u32[]{:S(2)}, u32[]{:S(2)}) %collective-permute-start.10) | collective-permute-done | bytes 16416 | tf_op jit(solution)/shard_map/ppermute | solution.py:101
  86.7 1.1 %fusion.2 = bf16[256,512]{1,0:T(8,128)(2,1)} fusion(f32[256,512]{1,0:T(8,128)S(1)} %fusion, bf16[16,4608]{1,0:T(8,128)(2,1)S(1)} %collective-permute-done.9, f32[256,16]{0,1:T(8,128)S(1)} %convolution_select_fusion.8, f32[256,16]{0,1:T(8,128)S(1)} %collective-permute-done.10), kind=kOutput, calls=%fused_computation.5 | convolution fusion | flops 25563136 | bytes 835584 | tf_op jit(solution)/shard_map/dot_general | solution.py:153
  (45 shorter events, 2.0 us)
Async XLA Ops:
  6.5 9.4 %copy-start = (bf16[256,4096]{1,0:T(8,128)(2,1)S(1)}, bf16[256,4096]{1,0:T(8,128)(2,1)}, u32[]{:S(2)}) copy-start(bf16[256,4096]{1,0:T(8,128)(2,1)} %param.7) | copy-start | bytes 6291460
  6.5 74.1 %reduce-scatter.2.cloned.1.call-start = ((), (), s32[]{:S(2)}) async-start(), calls=%async_computation.1 | async-start | bytes 1572864 | tf_op jit(solution)/shard_map/reduce_scatter | solution.py:113
  10.2 12.5 %copy-start.2 = (s32[1,8]{1,0:T(1,128)S(1)}, s32[1,8]{1,0:T(1,128)}, u32[]{:S(2)}) copy-start(s32[1,8]{1,0:T(1,128)} %param.13) | copy-start | bytes 100
  10.2 13.3 %copy-start.1 = (s32[32]{0:T(128)S(1)}, s32[32]{0:T(128)}, u32[]{:S(2)}) copy-start(s32[32]{0:T(128)} %home_ref.3) | copy-start | bytes 388
  10.2 29.3 %collective-permute-start = (bf16[64,4608]{1,0:T(8,128)(2,1)}, bf16[64,4608]{1,0:T(8,128)(2,1)}, u32[]{:S(2)}, u32[]{:S(2)}) collective-permute-start(bf16[64,4608]{1,0:T(8,128)(2,1)} %get-tuple-element.40), channel_id=1, source_target_pairs={{0,4},{2,6},{4,0},{6,2},{8,12},{10,14},{12,8},{14,10},{16,22},{18,... | collective-permute-start | bytes 1769480 | tf_op jit(solution)/shard_map/ppermute | solution.py:91
  13.3 41.3 %collective-permute-start.1 = (bf16[64,4608]{1,0:T(8,128)(2,1)}, bf16[64,4608]{1,0:T(8,128)(2,1)S(1)}, u32[]{:S(2)}, u32[]{:S(2)}) collective-permute-start(bf16[64,4608]{1,0:T(8,128)(2,1)} %get-tuple-element.42), channel_id=1, source_target_pairs={{0,8},{2,10},{4,12},{6,14},{8,0},{10,2},{12,4},{14,6},{16,28},{18,... | collective-permute-start | bytes 1769480 | tf_op jit(solution)/shard_map/ppermute | solution.py:91
  25.0 16.2 %copy-start.3 = (bf16[64,4608]{1,0:T(8,128)(2,1)S(1)}, bf16[64,4608]{1,0:T(8,128)(2,1)}, u32[]{:S(2)}) copy-start(bf16[64,4608]{1,0:T(8,128)(2,1)} %get-tuple-element.43) | copy-start | bytes 1769476
  28.3 11.2 %copy-start.4 = (bf16[48,4608]{1,0:T(8,128)(2,1)S(1)}, bf16[48,4608]{1,0:T(8,128)(2,1)}, u32[]{:S(2)}) copy-start(bf16[48,4608]{1,0:T(8,128)(2,1)} %get-tuple-element.44) | copy-start | bytes 1327108
  39.5 22.5 %collective-permute-start.3 = (bf16[48,4608]{1,0:T(8,128)(2,1)S(1)}, bf16[48,4608]{1,0:T(8,128)(2,1)S(1)}, u32[]{:S(2)}, u32[]{:S(2)}) collective-permute-start(bf16[48,4608]{1,0:T(8,128)(2,1)S(1)} %copy-done.4), channel_id=1, source_target_pairs={{0,10},{2,8},{4,14},{6,12},{8,2},{10,0},{12,6},{14,4},{16,30},{18,... | collective-permute-start | bytes 1327112 | tf_op jit(solution)/shard_map/ppermute | solution.py:91
  41.2 25.5 %collective-permute-start.2 = (bf16[64,4608]{1,0:T(8,128)(2,1)S(1)}, bf16[64,4608]{1,0:T(8,128)(2,1)S(1)}, u32[]{:S(2)}, u32[]{:S(2)}) collective-permute-start(bf16[64,4608]{1,0:T(8,128)(2,1)S(1)} %copy-done.3), channel_id=1, source_target_pairs={{0,2},{2,0},{4,6},{6,4},{8,10},{10,8},{12,14},{14,12},{16,18},{18,... | collective-permute-start | bytes 1769480 | tf_op jit(solution)/shard_map/ppermute | solution.py:91
  41.7 21.1 %collective-permute-start.4 = (bf16[64,4608]{1,0:T(8,128)(2,1)}, bf16[64,4608]{1,0:T(8,128)(2,1)S(1)}, u32[]{:S(2)}, u32[]{:S(2)}) collective-permute-start(bf16[64,4608]{1,0:T(8,128)(2,1)} %collective-permute-done), channel_id=1, source_target_pairs={{0,16},{16,0},{1,17},{17,1},{2,18},{18,2},{3,19},{19,3},{4,20},{20... | collective-permute-start | bytes 1769480 | tf_op jit(solution)/shard_map/ppermute | solution.py:95
  54.7 17.1 %collective-permute-start.6 = (bf16[64,4608]{1,0:T(8,128)(2,1)S(1)}, bf16[64,4608]{1,0:T(8,128)(2,1)S(1)}, u32[]{:S(2)}, u32[]{:S(2)}) collective-permute-start(bf16[64,4608]{1,0:T(8,128)(2,1)S(1)} %collective-permute-done.1), channel_id=1, source_target_pairs={{0,16},{16,0},{1,17},{17,1},{2,18},{18,2},{3,19},{19,3},{4,20},{20... | collective-permute-start | bytes 1769480 | tf_op jit(solution)/shard_map/ppermute | solution.py:95
  54.7 8.0 %copy-start.5 = (bf16[16,4608]{1,0:T(8,128)(2,1)S(1)}, bf16[16,4608]{1,0:T(8,128)(2,1)}, u32[]{:S(2)}) copy-start(bf16[16,4608]{1,0:T(8,128)(2,1)} %get-tuple-element.46) | copy-start | bytes 442372
  62.0 15.7 %collective-permute-start.7 = (bf16[48,4608]{1,0:T(8,128)(2,1)S(1)}, bf16[48,4608]{1,0:T(8,128)(2,1)S(1)}, u32[]{:S(2)}, u32[]{:S(2)}) collective-permute-start(bf16[48,4608]{1,0:T(8,128)(2,1)S(1)} %collective-permute-done.3), channel_id=1, source_target_pairs={{0,16},{16,0},{1,17},{17,1},{2,18},{18,2},{3,19},{19,3},{4,20},{20... | collective-permute-start | bytes 1327112 | tf_op jit(solution)/shard_map/ppermute | solution.py:95
  62.7 10.8 %collective-permute-start.5 = (bf16[16,4608]{1,0:T(8,128)(2,1)S(1)}, bf16[16,4608]{1,0:T(8,128)(2,1)S(1)}, u32[]{:S(2)}, u32[]{:S(2)}) collective-permute-start(bf16[16,4608]{1,0:T(8,128)(2,1)S(1)} %copy-done.5), channel_id=1, source_target_pairs={{0,10},{2,8},{4,14},{6,12},{8,2},{10,0},{12,6},{14,4},{16,30},{18,... | collective-permute-start | bytes 442376 | tf_op jit(solution)/shard_map/ppermute | solution.py:91
  78.5 2.1 %collective-permute-start.8 = (f32[256,496]{0,1:T(8,128)S(1)}, f32[256,496]{0,1:T(8,128)}, u32[]{:S(2)}, u32[]{:S(2)}) collective-permute-start(f32[256,496]{0,1:T(8,128)S(1)} %constant_dynamic-update-slice_fusion), channel_id=1, source_target_pairs={{0,1},{1,0},{2,3},{3,2},{4,5},{5,4},{6,7},{7,6},{8,9},{9,8},{10,11... | collective-permute-start | bytes 1523720 | tf_op jit(solution)/shard_map/ppermute | solution.py:101
  78.6 6.3 %collective-permute-start.9 = (bf16[16,4608]{1,0:T(8,128)(2,1)S(1)}, bf16[16,4608]{1,0:T(8,128)(2,1)S(1)}, u32[]{:S(2)}, u32[]{:S(2)}) collective-permute-start(bf16[16,4608]{1,0:T(8,128)(2,1)S(1)} %collective-permute-done.5), channel_id=1, source_target_pairs={{0,16},{16,0},{1,17},{17,1},{2,18},{18,2},{3,19},{19,3},{4,20},{20... | collective-permute-start | bytes 442376 | tf_op jit(solution)/shard_map/ppermute | solution.py:95
  85.5 1.2 %collective-permute-start.10 = (f32[256,16]{0,1:T(8,128)S(1)}, f32[256,16]{0,1:T(8,128)S(1)}, u32[]{:S(2)}, u32[]{:S(2)}) collective-permute-start(f32[256,16]{0,1:T(8,128)S(1)} %convolution_select_fusion.8), channel_id=1, source_target_pairs={{0,1},{1,0},{2,3},{3,2},{4,5},{5,4},{6,7},{7,6},{8,9},{9,8},{10,11... | collective-permute-start | bytes 49160 | tf_op jit(solution)/shard_map/ppermute | solution.py:101
Sparse Core Ops, SparseCore 0:
  22.7 7.4 reduce-scatter.1

commit v8 on v5

v8 whole, which is shorter than its diff:
```python
import functools
import jax
import jax.numpy as jnp
from jax import lax
from jax.experimental import pallas as pl
from jax.experimental.pallas import tpu as pltpu
from jax.sharding import PartitionSpec as P

adapter_scale = 2.0


def pack_kernel(blocks, home_ref, fetch_ref, shrink_ref, expand_ref, *refs):
    outs, sems = refs[:-1], refs[-1]
    me, part, half = lax.axis_index("rep"), lax.axis_index("parts"), lax.axis_index("tp")
    per_home, _, depth = shrink_ref.shape
    columns = expand_ref.shape[2] // lax.axis_size("tp")
    left = pl.multiple_of(half * columns, 128)
    listed = fetch_ref.shape[1]
    copies, slots = [], {}
    for at, (group, shrink, expand) in enumerate(blocks):
        if group not in slots:
            step = jnp.int32(group[0])
            for p, other in enumerate(group):
                step = jnp.where(part == p, other, step)
            peer = me ^ step

            def look(j, slot):
                position = home_ref[fetch_ref[peer, j]]
                return jnp.where(position // per_home == me, position % per_home, slot)

            slots[group] = lax.fori_loop(0, listed, look, jnp.int32(0), unroll=listed <= 8)
        slot = slots[group]
        pieces = []
        if shrink:
            pieces.append((shrink_ref.at[slot], outs[at].at[:, pl.ds(0, depth)]))
        if expand:
            target = outs[at].at[:, pl.ds(depth * shrink, columns)]
            pieces.append((expand_ref.at[slot, :, pl.ds(left, columns)], target))
        for n, (source, target) in enumerate(pieces):
            copies.append(pltpu.make_async_copy(source, target, sems.at[at, n]))
            copies[-1].start()
    for copy in copies:
        copy.wait()


def pack(blocks, columns, adapter_home, fetch_list, panels, expand_panels):
    rank, depth = panels.shape[1:]
    shapes = [(rank, depth * shrink + columns * expand) for _, shrink, expand in blocks]
    return list(
        pl.pallas_call(
            functools.partial(pack_kernel, blocks),
            out_shape=[jax.ShapeDtypeStruct(shape, panels.dtype) for shape in shapes],
            in_specs=[pl.BlockSpec(memory_space=pltpu.SMEM)] * 2 + [pl.BlockSpec(memory_space=pl.ANY)] * 2,
            out_specs=[pl.BlockSpec(memory_space=pltpu.VMEM)] * len(blocks),
            scratch_shapes=[pltpu.SemaphoreType.DMA((len(blocks), 2))],
            compiler_params=pltpu.CompilerParams(vmem_limit_bytes=56 << 20),
            cost_estimate=pl.CostEstimate(
                flops=0, bytes_accessed=4 * sum(r * w for r, w in shapes), transcendentals=0
            ),
        )(adapter_home, fetch_list, panels, expand_panels)
    )


def on_device(tokens, base_weight, shrink_panels, expand_panels, adapter_home, fetch_list, seg_len):
    per_home, depth, _ = shrink_panels.shape
    replicas, parts, cores = lax.axis_size("rep"), lax.axis_size("parts"), lax.axis_size("tp")
    me, part = lax.axis_index("rep"), lax.axis_index("parts")
    tok_count = tokens.shape[0]
    columns = expand_panels.shape[2] // cores
    panels = jnp.swapaxes(shrink_panels, 1, 2)
    tie = lax.optimization_barrier

    alone, half = max(2, parts), replicas // 2

    def grouped(steps):
        size = len(steps) // parts
        return [tuple(steps[p * size + g] for p in range(parts)) for g in range(size)]

    far = grouped(list(range(half, replicas)))
    near = grouped(list(range(alone, half)))
    groups = far + near
    solo = [(step,) * parts for step in range(1, alone)]

    def hop(x, group):
        pairs = [
            (p * replicas + i, p * replicas + (i ^ group[p]))
            for p in range(parts)
            for i in range(replicas)
        ]
        return lax.ppermute(x, ("parts", "rep"), pairs)

    def shift_parts(x, shift, turn=0):
        pairs = [
            (p * cores + t, ((p + shift) % parts) * cores + (t + turn) % cores)
            for p in range(parts)
            for t in range(cores)
        ]
        return lax.ppermute(x, ("parts", "tp"), pairs)

    rank = panels.shape[1]
    others = near + solo
    blocks = [(group, False, True) for group in far] + [(group, True, False) for group in far]
    blocks += [(group, True, True) for group in others]
    send = pack(blocks, columns, adapter_home, fetch_list, panels, expand_panels)
    tokens, send = tie((tokens, send))
    count = len(far)
    far_expand = [hop(x, group) for x, group in zip(send, far)]
    far_recv = [hop(x, group) for x, group in zip(send[count:], far)]
    tokens_of = [tokens] + [shift_parts(tokens, shift) for shift in range(1, parts)]
    other_send, far_expand = tie((send[2 * count :], far_expand))
    recv = [hop(x, group) for x, group in zip(other_send, others)]
    base_part = jnp.dot(tokens, base_weight, preferred_element_type=jnp.float32)
    base = lax.psum_scatter(base_part, "tp", scatter_dimension=1, tiled=True)
    panels, base_part = tie((panels, base_part))
    tables = (columns, adapter_home, fetch_list, panels, expand_panels)
    (own,) = pack([((0,) * parts, True, True)], *tables)

    def step_of(group, shift=0):
        step = jnp.int32(0)
        for p in range(parts):
            step = jnp.where(part == p, group[(p - shift) % parts], step)
        return step

    mine = [x[:, depth:] for x in recv[: len(near)]] + far_expand
    expands = [own[:, depth:]] + [x[:, depth:] for x in recv[len(near) :]] + mine
    expand_steps = [0] + [group[0] for group in solo] + [step_of(group) for group in near + far]
    sent = jnp.concatenate(mine, axis=0)
    for shift in range(1, parts):
        expands.append(shift_parts(sent, shift))
        expand_steps += [step_of(group, shift) for group in near + far]
    expand = jnp.concatenate(expands, axis=0)
    lengths_of = [seg_len[0]]
    for shift in range(1, parts):
        seg_len, tokens_of[shift] = tie((seg_len, tokens_of[shift]))
        lengths_of.append(shift_parts(seg_len, shift)[0])

    stored = jnp.take(adapter_home, lax.dynamic_index_in_dim(fetch_list, me, 0, keepdims=False))
    steps = (stored // per_home) ^ me
    rows = jnp.arange(tok_count, dtype=jnp.int32)

    def steps_of_rows(lengths):
        ordinal = jnp.arange(lengths.shape[0])
        starts = jnp.sum(jnp.where(ordinal[None, :] < ordinal[:, None], lengths[None, :], 0), axis=1)
        member = (rows[:, None] >= starts[None, :]) & (rows[:, None] < (starts + lengths)[None, :])
        return jnp.sum(jnp.where(member, steps[None, :], 0), axis=1)[:, None]

    row_steps = [steps_of_rows(lengths) for lengths in lengths_of]

    def score(block, step, shift):
        product = lax.dot_general(
            tokens_of[shift],
            block[:, :depth],
            (((1,), (1,)), ((), ())),
            preferred_element_type=jnp.float32,
        )
        return jnp.where(row_steps[shift] == step, product, 0.0)

    scores = [score(own, 0, 0)] + [0.0] * (parts - 1)
    for block, group in zip(recv[len(near) :], solo):
        scores[0] = scores[0] + score(block, group[0], 0)
    for block, group in zip(recv, near):
        for shift in range(parts):
            scores[shift] = scores[shift] + score(block, step_of(group), shift)
    tokens_of, scores, expand, base = tie((tokens_of, scores, expand, base))
    for block, group in zip(far_recv, far):
        for shift in range(parts):
            scores[shift] = scores[shift] + score(block, step_of(group), shift)
    shrink = scores[0]
    for turn in range(cores):
        for shift in range(parts):
            if shift or turn:
                shrink = shrink + shift_parts(scores[shift], -shift, turn)
    wide = jnp.concatenate(
        [jnp.where(row_steps[0] == step, shrink, 0.0) for step in expand_steps], axis=1
    )
    lora = jnp.dot(
        wide,
        expand.astype(jnp.float32),
        precision=lax.Precision.HIGHEST,
        preferred_element_type=jnp.float32,
    )
    return (base + adapter_scale * lora).astype(jnp.bfloat16)


def solution(mesh):
    return jax.shard_map(
        on_device,
        mesh=mesh,
        in_specs=(
            P(("parts", "rep"), "tp"),
            P("tp", None),
            P("rep", "tp", None),
            P("rep", None, None),
            P(),
            P(),
            P(("parts", "rep"), None),
        ),
        out_specs=P(("parts", "rep"), "tp"),
        check_vma=False,
    )
```

time: 107 us -> 119 us (1.11)
  waiting for transfers between devices: 31.7 us -> 55.8 us
  blocking collectives: 4.58 us -> 0 us
  local copies, waits for them, and re-layouts: 7.32 us -> 3.19 us
  other arithmetic: 4.25 us -> 2.63 us
  between operations: 15.1 us -> 13.7 us
  matrix products: 21.5 us -> 20.3 us
    ppermute x5 -> x6, waiting for transfers between devices: 13.7 us -> 42 us  [hop(): return lax.ppermute(x, ('parts', 'rep'), pairs)]
    all_gather x1 -> x0, waiting for transfers between devices: 13.5 us -> none  [on_device(): every_tokens = lax.all_gather(tokens, 'parts', axis=0, tiled=True)]
    ppermute x7 -> x6, waiting for transfers between devices: 4.45 us -> 13.7 us  [shift_parts(): return lax.ppermute(x, ('parts', 'tp'), pairs)]
    all_gather x1 -> x0, blocking collectives: 4.58 us -> none  [on_device(): every_seg_len = lax.all_gather(seg_len, 'parts', axis=0, tiled=True)]
    slice x3 -> x1, local copies, waits for them, and re-layouts: 2.94 us -> 0.01 us  [on_device(): mine = [x[:, depth:] for x in recv[:len(near)]] + far_expand]
    concatenate x1, local copies, waits for them, and re-layouts: 1.55 us -> 0.01 us  [on_device(): expand = jnp.concatenate(expands, axis=0)]
    ppermute x7 -> x6, starting transfers between devices: 4.88 us -> 6.32 us  [shift_parts(): return lax.ppermute(x, ('parts', 'tp'), pairs)]
    ppermute x5 -> x6, starting transfers between devices: 10.6 us -> 9.53 us  [hop(): return lax.ppermute(x, ('parts', 'rep'), pairs)]
  transfers between devices with their start and end apart: 14 -> 13, of which waited for: 5 -> 7; matrix products, arithmetic and copies ran while one was open for 26% -> 20% of each run, Pallas kernels for 3% -> 2%
where the time goes in v8:
time: 119 us; the launch traced here: 118 us
  waiting for transfers between devices  55.8 us (47%)
  matrix products  20.3 us (17%)
  starting transfers between devices  15.9 us (13%)
  between operations  13.7 us (12%)
  Pallas kernels  6.93 us (6%)
  local copies, waits for them, and re-layouts  3.19 us (3%)
  other arithmetic  2.63 us (2%)
    ppermute x6, waiting for transfers between devices, hop(): return lax.ppermute(x, ('parts', 'rep'), pairs)  42 us
    ppermute x6, waiting for transfers between devices, shift_parts(): return lax.ppermute(x, ('parts', 'tp'), pairs)  13.7 us
    dot_general x8, matrix products, score(): lax.dot_general(tokens_of[shift], block[:, :depth], (((1,), (1,)), ((), (...  13 us
    ppermute x6, starting transfers between devices, hop(): return lax.ppermute(x, ('parts', 'rep'), pairs)  9.53 us
    pallas_call x2, Pallas kernels, pack(): pl.pallas_call(functools.partial(pack_kernel, blocks), out_shape=[jax.Sha...  6.93 us
    dot_general x1, matrix products, on_device(): base_part = jnp.dot(tokens, base_weight, preferred_element_type=jnp.float32)  6.68 us
    ppermute x6, starting transfers between devices, shift_parts(): return lax.ppermute(x, ('parts', 'tp'), pairs)  6.32 us
    unnamed x18, local copies, waits for them, and re-layouts  2.52 us
  transfers between devices with their start and end apart: 13, of which 7 were waited for; matrix products, arithmetic and copies ran while one was open for 20% of the time, Pallas kernels for 2%

profile of v8, /device:TPU:0, one launch (start us, length us, event | category | flops | bytes accessed | tf_op | source)
XLA Modules:
  0.0 118.3 jit_solution(7826528612090427725)
XLA Ops:
  6.5 4.1 %shard_map.73 = (bf16[64,512]{1,0:T(8,128)(2,1)}, bf16[64,512]{1,0:T(8,128)(2,1)}, bf16[64,4096]{1,0:T(8,128)(2,1)}, bf16[64,4096]{1,0:T(8,128)(2,1)}, bf16[64,4...) custom-call(s32[32]{0:T(128)} %home_ref.3, s32[8,8]{1,0:T(8,128)} %fetch_ref.3, bf16[4,64,4096]{2,1,0:T(8,128)(2,1)} %bitcast.41, ...), custom_call_target="tpu_custom_call" | custom-call | bytes 4718592 | tf_op jit(solution)/shard_map/pallas_call | solution.py:50
  10.7 4.1 %collective-permute-start.1 = (bf16[64,512]{1,0:T(8,128)(2,1)}, bf16[64,512]{1,0:T(8,128)(2,1)S(1)}, u32[]{:S(2)}, u32[]{:S(2)}) collective-permute-start(bf16[64,512]{1,0:T(8,128)(2,1)} %get-tuple-element.42), channel_id=1, source_target_pairs={{0,8},{2,10},{4,12},{6,14},{8,0},{10,2},{12,4},{14,6},{16,28},{18,... | collective-permute-start | bytes 196616 | tf_op jit(solution)/shard_map/ppermute | solution.py:90
  14.8 1.5 %collective-permute-start.2 = (bf16[64,512]{1,0:T(8,128)(2,1)}, bf16[64,512]{1,0:T(8,128)(2,1)S(1)}, u32[]{:S(2)}, u32[]{:S(2)}) collective-permute-start(bf16[64,512]{1,0:T(8,128)(2,1)} %get-tuple-element.43), channel_id=1, source_target_pairs={{0,10},{2,8},{4,14},{6,12},{8,2},{10,0},{12,6},{14,4},{16,30},{18,... | collective-permute-start | bytes 196616 | tf_op jit(solution)/shard_map/ppermute | solution.py:90
  16.3 2.4 %collective-permute-start.7 = (bf16[64,4096]{1,0:T(8,128)(2,1)}, bf16[64,4096]{1,0:T(8,128)(2,1)S(1)}, u32[]{:S(2)}, u32[]{:S(2)}) collective-permute-start(bf16[64,4096]{1,0:T(8,128)(2,1)} %get-tuple-element.52), channel_id=1, source_target_pairs={{0,8},{2,10},{4,12},{6,14},{8,0},{10,2},{12,4},{14,6},{16,28},{18,... | collective-permute-start | bytes 1572872 | tf_op jit(solution)/shard_map/ppermute | solution.py:90
  18.7 3.7 %collective-permute-start = (bf16[256,4096]{1,0:T(8,128)(2,1)S(1)}, bf16[256,4096]{1,0:T(8,128)(2,1)}, u32[]{:S(2)}, u32[]{:S(2)}) collective-permute-start(bf16[256,4096]{1,0:T(8,128)(2,1)S(1)} %copy-done.1), channel_id=1, source_target_pairs={{0,16},{1,17},{16,0},{17,1},{2,18},{3,19},{18,2},{19,3},{4,20},{5,... | collective-permute-start | bytes 6291464 | tf_op jit(solution)/shard_map/ppermute | solution.py:98
  22.4 6.7 %fusion.12 = f32[256,1024]{1,0:T(8,128)} fusion(bf16[256,4096]{1,0:T(8,128)(2,1)S(1)} %copy-done.1, bf16[4096,1024]{1,0:T(8,128)(2,1)} %param.8), kind=kOutput, calls=%fused_computation.73 | convolution fusion | flops 2147483648 | bytes 11534336 | tf_op jit(solution)/shard_map/dot_general | solution.py:112
  29.1 0.7 fusion.8
  29.8 15.8 %collective-permute-done.2 = bf16[64,512]{1,0:T(8,128)(2,1)S(1)} collective-permute-done((bf16[64,512]{1,0:T(8,128)(2,1)}, bf16[64,512]{1,0:T(8,128)(2,1)S(1)}, u32[]{:S(2)}, u32[]{:S(2)}) %collective-permute-start.2) | collective-permute-done | bytes 65568 | tf_op jit(solution)/shard_map/ppermute | solution.py:90
  45.6 1.5 %collective-permute-start.3 = (bf16[64,4608]{1,0:T(8,128)(2,1)}, bf16[64,4608]{1,0:T(8,128)(2,1)}, u32[]{:S(2)}, u32[]{:S(2)}) collective-permute-start(bf16[64,4608]{1,0:T(8,128)(2,1)} %get-tuple-element.44), channel_id=1, source_target_pairs={{0,2},{2,0},{4,6},{6,4},{8,10},{10,8},{12,14},{14,12},{16,18},{18,... | collective-permute-start | bytes 1769480 | tf_op jit(solution)/shard_map/ppermute | solution.py:90
  47.1 0.6 gather_fusion
  47.7 2.8 %shard_map.74 = bf16[64,4608]{1,0:T(8,128)(2,1)} custom-call(s32[32]{0:T(128)} %home_ref.3, s32[8,8]{1,0:T(8,128)} %fetch_ref.3, bf16[4,64,4096]{2,1,0:T(8,128)(2,1)} %bitcast.42, bf16[4,64,1024]{2,1,0:T(8,128)(2,1)} %expand_ref.3), custom_call_target="tpu_custom_call" | custom-call | bytes 1179648 | tf_op jit(solution)/shard_map/pallas_call | solution.py:50
  50.8 0.7 fusion.10
  51.5 0.8 slice_dynamic-update-slice_fusion.1
  52.3 19.4 %collective-permute-done.3 = bf16[64,4608]{1,0:T(8,128)(2,1)} collective-permute-done((bf16[64,4608]{1,0:T(8,128)(2,1)}, bf16[64,4608]{1,0:T(8,128)(2,1)}, u32[]{:S(2)}, u32[]{:S(2)}) %collective-permute-start.3) | collective-permute-done | bytes 589856 | tf_op jit(solution)/shard_map/ppermute | solution.py:90
  71.7 0.8 slice_dynamic-update-slice_fusion
  72.5 6.8 %collective-permute-done.4 = bf16[64,4608]{1,0:T(8,128)(2,1)S(1)} collective-permute-done((bf16[64,4608]{1,0:T(8,128)(2,1)S(1)}, bf16[64,4608]{1,0:T(8,128)(2,1)S(1)}, u32[]{:S(2)}, u32[]{:S(2)}) %collective-permute-start.4) | collective-permute-done | bytes 589856 | tf_op jit(solution)/shard_map/ppermute | solution.py:90
  79.5 6.8 %collective-permute-done.6 = bf16[192,512]{1,0:T(8,128)(2,1)S(1)} collective-permute-done((bf16[192,512]{1,0:T(8,128)(2,1)S(1)}, bf16[192,512]{1,0:T(8,128)(2,1)S(1)}, u32[]{:S(2)}, u32[]{:S(2)}) %collective-permute-start.6) | collective-permute-done | bytes 196640 | tf_op jit(solution)/shard_map/ppermute | solution.py:98
  86.3 0.8 copy-done.2
  87.4 3.3 %collective-permute-done.5 = s32[1,8]{1,0:T(1,128)S(1)} collective-permute-done((s32[1,8]{1,0:T(1,128)S(1)}, s32[1,8]{1,0:T(1,128)S(1)}, u32[]{:S(2)}, u32[]{:S(2)}) %collective-permute-start.5) | collective-permute-done | bytes 64 | tf_op jit(solution)/shard_map/ppermute | solution.py:98
  90.9 1.8 %convolution_select_fusion.7 = f32[256,64]{0,1:T(8,128)S(1)} fusion(bf16[256,4096]{1,0:T(8,128)(2,1)S(1)} %copy-done.1, bf16[64,4608]{1,0:T(8,128)(2,1)} %shard_map.74, pred[256]{0:T(512)(128)(4,1)S(1)} %get-tuple-element.70), kind=kOutput, calls=%fused_computation.11 | convolution fusion | flops 134234112 | bytes 2687232 | tf_op jit(solution)/shard_map/dot_general | solution.py:150
  92.7 1.8 %fusion.1 = f32[256,64]{0,1:T(8,128)S(1)} fusion(f32[256,64]{0,1:T(8,128)S(1)} %convolution_select_fusion.7, bf16[256,4096]{1,0:T(8,128)(2,1)S(1)} %copy-done.1, bf16[64,4608]{1,0:T(8,128)(2,1)} %collective-permute-done.3, pred[256]{0:T(512)(128)(4,1)S(1)} %get-tuple-element.69), kind=kOutput, calls=%fused_computation.10 | convolution fusion | flops 134250496 | bytes 2752768 | tf_op jit(solution)/shard_map/dot_general | solution.py:150
  94.5 0.8 fusion
  95.3 2.4 %convolution_select_fusion.4 = f32[256,64]{0,1:T(8,128)S(1)} fusion(bf16[256,4096]{1,0:T(8,128)(2,1)} %collective-permute-done, bf16[64,4608]{1,0:T(8,128)(2,1)S(1)} %collective-permute-done.4, pred[256]{0:T(512)(128)(4,1)S(1)} %get-tuple-element.73), kind=kOutput, calls=%fused_computation.6 | convolution fusion | flops 134234112 | bytes 2687488 | tf_op jit(solution)/shard_map/dot_general | solution.py:150
  97.7 0.8 convolution_select_fusion.3
  98.4 0.8 add_add_fusion.2
  99.3 2.4 %convolution_select_fusion.1 = f32[256,64]{0,1:T(8,128)S(1)} fusion(bf16[256,4096]{1,0:T(8,128)(2,1)} %collective-permute-done, bf16[64,4096]{1,0:T(8,128)(2,1)S(1)} %collective-permute-done.7, pred[256]{0:T(512)(128)(4,1)S(1)} %get-tuple-element.72), kind=kOutput, calls=%fused_computation.3 | convolution fusion | flops 134234112 | bytes 2687232 | tf_op jit(solution)/shard_map/dot_general | solution.py:150
  101.6 2.4 %add_add_fusion.1 = f32[256,64]{0,1:T(8,128)S(1)} fusion(f32[256,64]{0,1:T(8,128)S(1)} %convolution_select_fusion.4, f32[256,64]{0,1:T(8,128)S(1)} %convolution_select_fusion.1, bf16[256,4096]{1,0:T(8,128)(2,1)} %collective-permute-done, bf16[64,4096]{1,0:T(8,128)(2,1)S(1)} %collective-permute-done.8, pred[256]{0:T(512)(128)(4,1)S(1)} %get-tuple-element.71), kind=kOutput, calls=%fused_computation.29 | convolution fusion | flops 134266880 | bytes 2818304 | tf_op jit(solution)/shard_map/dot_general | solution.py:150
  104.5 1.7 %collective-permute-start.9 = (f32[256,64]{0,1:T(8,128)S(1)}, f32[256,64]{0,1:T(8,128)S(1)}, u32[]{:S(2)}, u32[]{:S(2)}) collective-permute-start(f32[256,64]{0,1:T(8,128)S(1)} %add_add_fusion.1), channel_id=1, source_target_pairs={{0,16},{1,17},{16,0},{17,1},{2,18},{3,19},{18,2},{19,3},{4,20},{5,... | collective-permute-start | bytes 196616 | tf_op jit(solution)/shard_map/ppermute | solution.py:98
  106.3 1.6 %collective-permute-done.11 = f32[256,64]{0,1:T(8,128)S(1)} collective-permute-done((f32[256,64]{0,1:T(8,128)S(1)}, f32[256,64]{0,1:T(8,128)S(1)}, u32[]{:S(2)}, u32[]{:S(2)}) %collective-permute-start.11) | collective-permute-done | bytes 65568 | tf_op jit(solution)/shard_map/ppermute | solution.py:98
  107.9 2.0 %collective-permute-done.9 = f32[256,64]{0,1:T(8,128)S(1)} collective-permute-done((f32[256,64]{0,1:T(8,128)S(1)}, f32[256,64]{0,1:T(8,128)S(1)}, u32[]{:S(2)}, u32[]{:S(2)}) %collective-permute-start.9) | collective-permute-done | bytes 65568 | tf_op jit(solution)/shard_map/ppermute | solution.py:98
  110.1 0.6 convolution_multiply_fusion
  110.7 0.8 add_convert_fusion
  (47 shorter events, 1.5 us)
Async XLA Ops:
  6.5 12.1 %copy-start.1 = (bf16[256,4096]{1,0:T(8,128)(2,1)S(1)}, bf16[256,4096]{1,0:T(8,128)(2,1)}, u32[]{:S(2)}) copy-start(bf16[256,4096]{1,0:T(8,128)(2,1)} %param.7) | copy-start | bytes 6291460
  6.5 91.1 %reduce-scatter.2.cloned.1.call-start = ((), (), s32[]{:S(2)}) async-start(), calls=%async_computation.1 | async-start | bytes 1572864 | tf_op jit(solution)/shard_map/reduce_scatter | solution.py:113
  10.6 36.4 %copy-start = (s32[32]{0:T(128)S(1)}, s32[32]{0:T(128)}, u32[]{:S(2)}) copy-start(s32[32]{0:T(128)} %home_ref.3) | copy-start | bytes 388
  10.7 19.1 %collective-permute-start.1 = (bf16[64,512]{1,0:T(8,128)(2,1)}, bf16[64,512]{1,0:T(8,128)(2,1)S(1)}, u32[]{:S(2)}, u32[]{:S(2)}) collective-permute-start(bf16[64,512]{1,0:T(8,128)(2,1)} %get-tuple-element.42), channel_id=1, source_target_pairs={{0,8},{2,10},{4,12},{6,14},{8,0},{10,2},{12,4},{14,6},{16,28},{18,... | collective-permute-start | bytes 196616 | tf_op jit(solution)/shard_map/ppermute | solution.py:90
  14.8 30.9 %collective-permute-start.2 = (bf16[64,512]{1,0:T(8,128)(2,1)}, bf16[64,512]{1,0:T(8,128)(2,1)S(1)}, u32[]{:S(2)}, u32[]{:S(2)}) collective-permute-start(bf16[64,512]{1,0:T(8,128)(2,1)} %get-tuple-element.43), channel_id=1, source_target_pairs={{0,10},{2,8},{4,14},{6,12},{8,2},{10,0},{12,6},{14,4},{16,30},{18,... | collective-permute-start | bytes 196616 | tf_op jit(solution)/shard_map/ppermute | solution.py:90
  16.3 81.4 %collective-permute-start.7 = (bf16[64,4096]{1,0:T(8,128)(2,1)}, bf16[64,4096]{1,0:T(8,128)(2,1)S(1)}, u32[]{:S(2)}, u32[]{:S(2)}) collective-permute-start(bf16[64,4096]{1,0:T(8,128)(2,1)} %get-tuple-element.52), channel_id=1, source_target_pairs={{0,8},{2,10},{4,12},{6,14},{8,0},{10,2},{12,4},{14,6},{16,28},{18,... | collective-permute-start | bytes 1572872 | tf_op jit(solution)/shard_map/ppermute | solution.py:90
  18.6 79.8 %collective-permute-start.8 = (bf16[64,4096]{1,0:T(8,128)(2,1)}, bf16[64,4096]{1,0:T(8,128)(2,1)S(1)}, u32[]{:S(2)}, u32[]{:S(2)}) collective-permute-start(bf16[64,4096]{1,0:T(8,128)(2,1)} %get-tuple-element.53), channel_id=1, source_target_pairs={{0,10},{2,8},{4,14},{6,12},{8,2},{10,0},{12,6},{14,4},{16,30},{18,... | collective-permute-start | bytes 1572872 | tf_op jit(solution)/shard_map/ppermute | solution.py:90
  18.7 67.7 %collective-permute-start = (bf16[256,4096]{1,0:T(8,128)(2,1)S(1)}, bf16[256,4096]{1,0:T(8,128)(2,1)}, u32[]{:S(2)}, u32[]{:S(2)}) collective-permute-start(bf16[256,4096]{1,0:T(8,128)(2,1)S(1)} %copy-done.1), channel_id=1, source_target_pairs={{0,16},{1,17},{16,0},{17,1},{2,18},{3,19},{18,2},{19,3},{4,20},{5,... | collective-permute-start | bytes 6291464 | tf_op jit(solution)/shard_map/ppermute | solution.py:98
  29.1 21.5 %copy-start.5 = (s32[1,8]{1,0:T(1,128)S(1)}, s32[1,8]{1,0:T(1,128)}, u32[]{:S(2)}) copy-start(s32[1,8]{1,0:T(1,128)} %param.13) | copy-start | bytes 100
  45.6 26.1 %collective-permute-start.3 = (bf16[64,4608]{1,0:T(8,128)(2,1)}, bf16[64,4608]{1,0:T(8,128)(2,1)}, u32[]{:S(2)}, u32[]{:S(2)}) collective-permute-start(bf16[64,4608]{1,0:T(8,128)(2,1)} %get-tuple-element.44), channel_id=1, source_target_pairs={{0,2},{2,0},{4,6},{6,4},{8,10},{10,8},{12,14},{14,12},{16,18},{18,... | collective-permute-start | bytes 1769480 | tf_op jit(solution)/shard_map/ppermute | solution.py:90
  47.7 3.0 %copy-start.6 = (bf16[64,4608]{1,0:T(8,128)(2,1)S(1)}, bf16[64,4608]{1,0:T(8,128)(2,1)}, u32[]{:S(2)}) copy-start(bf16[64,4608]{1,0:T(8,128)(2,1)} %get-tuple-element.45) | copy-start | bytes 1769476
  50.7 28.7 %collective-permute-start.4 = (bf16[64,4608]{1,0:T(8,128)(2,1)S(1)}, bf16[64,4608]{1,0:T(8,128)(2,1)S(1)}, u32[]{:S(2)}, u32[]{:S(2)}) collective-permute-start(bf16[64,4608]{1,0:T(8,128)(2,1)S(1)} %copy-done.6), channel_id=1, source_target_pairs={{0,4},{2,6},{4,0},{6,2},{8,12},{10,14},{12,8},{14,10},{16,22},{18,... | collective-permute-start | bytes 1769480 | tf_op jit(solution)/shard_map/ppermute | solution.py:90
  79.4 6.9 %collective-permute-start.6 = (bf16[192,512]{1,0:T(8,128)(2,1)S(1)}, bf16[192,512]{1,0:T(8,128)(2,1)S(1)}, u32[]{:S(2)}, u32[]{:S(2)}) collective-permute-start(bf16[192,512]{1,0:T(8,128)(2,1)S(1)} %pad_maximum_fusion), channel_id=1, source_target_pairs={{0,16},{1,17},{16,0},{17,1},{2,18},{3,19},{18,2},{19,3},{4,20},{5,... | collective-permute-start | bytes 589832 | tf_op jit(solution)/shard_map/ppermute | solution.py:98
  86.3 0.8 copy-start.2
  87.1 3.5 %collective-permute-start.5 = (s32[1,8]{1,0:T(1,128)S(1)}, s32[1,8]{1,0:T(1,128)S(1)}, u32[]{:S(2)}, u32[]{:S(2)}) collective-permute-start(s32[1,8]{1,0:T(1,128)S(1)} %copy-done.5), channel_id=1, source_target_pairs={{0,16},{1,17},{16,0},{17,1},{2,18},{3,19},{18,2},{19,3},{4,20},{5,... | collective-permute-start | bytes 104 | tf_op jit(solution)/shard_map/ppermute | solution.py:98
  99.2 7.1 %collective-permute-start.10 = (f32[256,64]{0,1:T(8,128)S(1)}, f32[256,64]{0,1:T(8,128)S(1)}, u32[]{:S(2)}, u32[]{:S(2)}) collective-permute-start(f32[256,64]{0,1:T(8,128)S(1)} %add_add_fusion.2), channel_id=1, source_target_pairs={{0,1},{1,0},{16,17},{17,16},{2,3},{3,2},{18,19},{19,18},{4,5},{5,4... | collective-permute-start | bytes 196616 | tf_op jit(solution)/shard_map/ppermute | solution.py:98
  101.6 8.4 %copy-start.3 = (bf16[512,512]{1,0:T(8,128)(2,1)S(1)}, bf16[512,512]{1,0:T(8,128)(2,1)}, u32[]{:S(2)}) copy-start(bf16[512,512]{1,0:T(8,128)(2,1)} %copy-done.2) | copy-start | bytes 1572868
  104.1 6.7 %copy-start.4 = (f32[256,512]{1,0:T(8,128)S(1)}, f32[256,512]{1,0:T(8,128)}, u32[]{:S(2)}) copy-start(f32[256,512]{1,0:T(8,128)} %reduce-scatter.2.cloned.1.call-done) | copy-start | bytes 1572868
  104.1 3.8 %collective-permute-start.11 = (f32[256,64]{0,1:T(8,128)S(1)}, f32[256,64]{0,1:T(8,128)S(1)}, u32[]{:S(2)}, u32[]{:S(2)}) collective-permute-start(f32[256,64]{0,1:T(8,128)S(1)} %add_add_fusion.1), channel_id=1, source_target_pairs={{0,17},{1,16},{16,1},{17,0},{2,19},{3,18},{18,3},{19,2},{4,21},{5,... | collective-permute-start | bytes 196616 | tf_op jit(solution)/shard_map/ppermute | solution.py:98
  104.5 5.4 %collective-permute-start.9 = (f32[256,64]{0,1:T(8,128)S(1)}, f32[256,64]{0,1:T(8,128)S(1)}, u32[]{:S(2)}, u32[]{:S(2)}) collective-permute-start(f32[256,64]{0,1:T(8,128)S(1)} %add_add_fusion.1), channel_id=1, source_target_pairs={{0,16},{1,17},{16,0},{17,1},{2,18},{3,19},{18,2},{19,3},{4,20},{5,... | collective-permute-start | bytes 196616 | tf_op jit(solution)/shard_map/ppermute | solution.py:98
Sparse Core Ops, SparseCore 0:
  29.2 8.7 reduce-scatter.1

commit v9 on v8

--- a/solution.py
+++ b/solution.py
@@ -89,31 +89,33 @@
         ]
         return lax.ppermute(x, ("parts", "rep"), pairs)
 
-    def shift_parts(x, shift, turn=0):
-        pairs = [
-            (p * cores + t, ((p + shift) % parts) * cores + (t + turn) % cores)
-            for p in range(parts)
-            for t in range(cores)
-        ]
-        return lax.ppermute(x, ("parts", "tp"), pairs)
+    def shift_parts(x, shift):
+        return lax.ppermute(x, "parts", [(i, (i + shift) % parts) for i in range(parts)])
+
+    def trade(x):
+        for shift in range(1, cores):
+            x = x + lax.ppermute(x, "tp", [(i, (i + shift) % cores) for i in range(cores)])
+        return x
 
     rank = panels.shape[1]
-    others = near + solo
-    blocks = [(group, False, True) for group in far] + [(group, True, False) for group in far]
-    blocks += [(group, True, True) for group in others]
+    groups = far + near + solo
+    blocks = [(group, True, True) for group in groups]
     send = pack(blocks, columns, adapter_home, fetch_list, panels, expand_panels)
     tokens, send = tie((tokens, send))
-    count = len(far)
-    far_expand = [hop(x, group) for x, group in zip(send, far)]
-    far_recv = [hop(x, group) for x, group in zip(send[count:], far)]
+    recv = [hop(x, group) for x, group in zip(send, groups)]
     tokens_of = [tokens] + [shift_parts(tokens, shift) for shift in range(1, parts)]
-    other_send, far_expand = tie((send[2 * count :], far_expand))
-    recv = [hop(x, group) for x, group in zip(other_send, others)]
     base_part = jnp.dot(tokens, base_weight, preferred_element_type=jnp.float32)
     base = lax.psum_scatter(base_part, "tp", scatter_dimension=1, tiled=True)
-    panels, base_part = tie((panels, base_part))
-    tables = (columns, adapter_home, fetch_list, panels, expand_panels)
-    (own,) = pack([((0,) * parts, True, True)], *tables)
+
+    stored = jnp.take(adapter_home, lax.dynamic_index_in_dim(fetch_list, me, 0, keepdims=False))
+    steps = (stored // per_home) ^ me
+    slot = jnp.sum(jnp.where(steps == 0, stored % per_home, 0))
+    own = lax.dynamic_index_in_dim(panels, slot, 0, keepdims=False)
+    left = lax.axis_index("tp") * columns
+    own_expand = lax.dynamic_slice(expand_panels, (slot, 0, left), (1, rank, columns))[0]
+    far_recv, near_recv = recv[: len(far)], recv[len(far) : len(far) + len(near)]
+    solo_recv = recv[len(far) + len(near) :]
+    early, early_groups = near_recv + far_recv[:-1], near + far[:-1]
 
     def step_of(group, shift=0):
         step = jnp.int32(0)
@@ -121,61 +123,63 @@
             step = jnp.where(part == p, group[(p - shift) % parts], step)
         return step
 
-    mine = [x[:, depth:] for x in recv[: len(near)]] + far_expand
-    expands = [own[:, depth:]] + [x[:, depth:] for x in recv[len(near) :]] + mine
-    expand_steps = [0] + [group[0] for group in solo] + [step_of(group) for group in near + far]
-    sent = jnp.concatenate(mine, axis=0)
+    expands = [own_expand] + [x[:, depth:] for x in solo_recv + early]
+    expand_steps = [0] + [group[0] for group in solo] + [step_of(group) for group in early_groups]
+    sent = jnp.concatenate([x[:, depth:] for x in early], axis=0)
     for shift in range(1, parts):
         expands.append(shift_parts(sent, shift))
-        expand_steps += [step_of(group, shift) for group in near + far]
+        expand_steps += [step_of(group, shift) for group in early_groups]
     expand = jnp.concatenate(expands, axis=0)
+
     lengths_of = [seg_len[0]]
     for shift in range(1, parts):
         seg_len, tokens_of[shift] = tie((seg_len, tokens_of[shift]))
         lengths_of.append(shift_parts(seg_len, shift)[0])
-
-    stored = jnp.take(adapter_home, lax.dynamic_index_in_dim(fetch_list, me, 0, keepdims=False))
-    steps = (stored // per_home) ^ me
     rows = jnp.arange(tok_count, dtype=jnp.int32)
 
     def steps_of_rows(lengths):
         ordinal = jnp.arange(lengths.shape[0])
         starts = jnp.sum(jnp.where(ordinal[None, :] < ordinal[:, None], lengths[None, :], 0), axis=1)
         member = (rows[:, None] >= starts[None, :]) & (rows[:, None] < (starts + lengths)[None, :])
-        return jnp.sum(jnp.where(member, steps[None, :], 0), axis=1)[:, None]
+        return jnp.sum(jnp.where(member, steps[None, :], 0), axis=1)[None, :]
 
     row_steps = [steps_of_rows(lengths) for lengths in lengths_of]
 
     def score(block, step, shift):
         product = lax.dot_general(
+            block[:, :depth],
             tokens_of[shift],
-            block[:, :depth],
             (((1,), (1,)), ((), ())),
             preferred_element_type=jnp.float32,
         )
         return jnp.where(row_steps[shift] == step, product, 0.0)
 
     scores = [score(own, 0, 0)] + [0.0] * (parts - 1)
-    for block, group in zip(recv[len(near) :], solo):
+    for block, group in zip(solo_recv, solo):
         scores[0] = scores[0] + score(block, group[0], 0)
-    for block, group in zip(recv, near):
+    for block, group in zip(early, early_groups):
         for shift in range(parts):
             scores[shift] = scores[shift] + score(block, step_of(group), shift)
-    tokens_of, scores, expand, base = tie((tokens_of, scores, expand, base))
-    for block, group in zip(far_recv, far):
-        for shift in range(parts):
-            scores[shift] = scores[shift] + score(block, step_of(group), shift)
-    shrink = scores[0]
-    for turn in range(cores):
-        for shift in range(parts):
-            if shift or turn:
-                shrink = shrink + shift_parts(scores[shift], -shift, turn)
+    tokens_of, scores, expand, base, far_recv[-1] = tie(
+        (tokens_of, scores, expand, base, far_recv[-1])
+    )
+    last_expand = far_recv[-1][:, depth:]
+    expands = [expand, last_expand] + [shift_parts(last_expand, shift) for shift in range(1, parts)]
+    expand_steps += [step_of(far[-1], shift) for shift in range(parts)]
+    for shift in range(parts):
+        scores[shift] = scores[shift] + score(far_recv[-1], step_of(far[-1]), shift)
+    scores, expands = tie((scores, expands))
+    scores = trade(jnp.concatenate(scores, axis=1))
+    shrink = scores[:, :tok_count]
+    for shift in range(1, parts):
+        shrink = shrink + shift_parts(scores[:, shift * tok_count : (shift + 1) * tok_count], -shift)
     wide = jnp.concatenate(
-        [jnp.where(row_steps[0] == step, shrink, 0.0) for step in expand_steps], axis=1
-    )
-    lora = jnp.dot(
+        [jnp.where(row_steps[0] == step, shrink, 0.0) for step in expand_steps], axis=0
+    )
+    lora = lax.dot_general(
         wide,
-        expand.astype(jnp.float32),
+        jnp.concatenate(expands, axis=0).astype(jnp.float32),
+        (((0,), (0,)), ((), ())),
         precision=lax.Precision.HIGHEST,
         preferred_element_type=jnp.float32,
     )

time: 119 us -> 102 us (0.86)
  waiting for transfers between devices: 55.8 us -> 38.8 us
  Pallas kernels: 6.93 us -> 4.11 us
  starting transfers between devices: 15.9 us -> 13.6 us
  between operations: 13.7 us -> 15.7 us
  other arithmetic: 2.63 us -> 4.01 us
  matrix products: 20.3 us -> 21.5 us
    ppermute x6 -> x4, waiting for transfers between devices: 42 us -> 24.3 us  [hop(): return lax.ppermute(x, ('parts', 'rep'), pairs)]
    pallas_call x2 -> x1, Pallas kernels: 6.93 us -> 4.11 us  [pack(): pl.pallas_call(functools.partial(pack_kernel, blocks), out_shape=[jax.Sha...]
    reduce_sum x1 -> x2, other arithmetic: 0.09 us -> 1.44 us  [the longest x1 1.35 us: on_device(): slot = jnp.sum(jnp.where(steps == 0, stored % per_home, 0))]
    ppermute x6 -> x4, starting transfers between devices: 9.53 us -> 8.25 us  [hop(): return lax.ppermute(x, ('parts', 'rep'), pairs)]
    dot_general x9, matrix products: 13.6 us -> 14.8 us  [the longest x8 14.2 us: score(): lax.dot_general(block[:, :depth], tokens_of[shift], (((1,), (1,)), ((), (...]
    unnamed x18 -> x15, local copies, waits for them, and re-layouts: 2.52 us -> 1.74 us
  transfers between devices with their start and end apart: 13 -> 11, of which waited for: 7 -> 6; matrix products, arithmetic and copies ran while one was open for 20% -> 27% of each run, Pallas kernels for 2% -> 0%
where the time goes in v9:
time: 102 us; the launch traced here: 101 us
  waiting for transfers between devices  38.8 us (38%)
  matrix products  21.5 us (21%)
  between operations  15.7 us (15%)
  starting transfers between devices  13.6 us (13%)
  Pallas kernels  4.11 us (4%)
  other arithmetic  4.01 us (4%)
  local copies, waits for them, and re-layouts  3.27 us (3%)
    ppermute x4, waiting for transfers between devices, hop(): return lax.ppermute(x, ('parts', 'rep'), pairs)  24.3 us
    dot_general x8, matrix products, score(): lax.dot_general(block[:, :depth], tokens_of[shift], (((1,), (1,)), ((), (...  14.2 us
    ppermute x5, waiting for transfers between devices, shift_parts(): lax.ppermute(x, 'parts', [(i, (i + shift) % parts) for i in range(parts)])  13.1 us
    ppermute x4, starting transfers between devices, hop(): return lax.ppermute(x, ('parts', 'rep'), pairs)  8.25 us
    dot_general x1, matrix products, on_device(): base_part = jnp.dot(tokens, base_weight, preferred_element_type=jnp.float32)  6.69 us
    ppermute x5, starting transfers between devices, shift_parts(): lax.ppermute(x, 'parts', [(i, (i + shift) % parts) for i in range(parts)])  5.3 us
    pallas_call x1, Pallas kernels, pack(): pl.pallas_call(functools.partial(pack_kernel, blocks), out_shape=[jax.Sha...  4.11 us
  transfers between devices with their start and end apart: 11, of which 6 were waited for; matrix products, arithmetic and copies ran while one was open for 27% of the time, Pallas kernels for 0%

profile of v9, /device:TPU:0, one launch (start us, length us, event | category | flops | bytes accessed | tf_op | source)
XLA Modules:
  0.0 101.0 jit_solution(7853839248914995183)
XLA Ops:
  6.5 4.1 %shard_map.73 = (bf16[64,4608]{1,0:T(8,128)(2,1)}, bf16[64,4608]{1,0:T(8,128)(2,1)}, bf16[64,4608]{1,0:T(8,128)(2,1)}, bf16[64,4608]{1,0:T(8,128)(2,1)}) custom-call(s32[32]{0:T(128)} %home_ref.1, s32[8,8]{1,0:T(8,128)} %fetch_ref.1, bf16[4,64,4096]{2,1,0:T(8,128)(2,1)} %bitcast.47, bf16[4,64,1024]{2,1,0:T(8,128)(2,1)} %expand_ref.1), custom_call_target="tpu_custom_call" | custom-call | bytes 4718592 | tf_op jit(solution)/shard_map/pallas_call | solution.py:50
  10.7 2.9 %collective-permute-start.1 = (bf16[64,4608]{1,0:T(8,128)(2,1)}, bf16[64,4608]{1,0:T(8,128)(2,1)}, u32[]{:S(2)}, u32[]{:S(2)}) collective-permute-start(bf16[64,4608]{1,0:T(8,128)(2,1)} %get-tuple-element.34), channel_id=1, source_target_pairs={{0,2},{2,0},{4,6},{6,4},{8,10},{10,8},{12,14},{14,12},{16,18},{18,... | collective-permute-start | bytes 1769480 | tf_op jit(solution)/shard_map/ppermute | solution.py:90
  13.6 1.6 %collective-permute-start.2 = (bf16[64,4608]{1,0:T(8,128)(2,1)}, bf16[64,4608]{1,0:T(8,128)(2,1)S(1)}, u32[]{:S(2)}, u32[]{:S(2)}) collective-permute-start(bf16[64,4608]{1,0:T(8,128)(2,1)} %get-tuple-element.35), channel_id=1, source_target_pairs={{0,4},{2,6},{4,0},{6,2},{8,12},{10,14},{12,8},{14,10},{16,22},{18,... | collective-permute-start | bytes 1769480 | tf_op jit(solution)/shard_map/ppermute | solution.py:90
  15.2 2.6 %collective-permute-start.3 = (bf16[64,4608]{1,0:T(8,128)(2,1)}, bf16[64,4608]{1,0:T(8,128)(2,1)}, u32[]{:S(2)}, u32[]{:S(2)}) collective-permute-start(bf16[64,4608]{1,0:T(8,128)(2,1)} %get-tuple-element.36), channel_id=1, source_target_pairs={{0,8},{2,10},{4,12},{6,14},{8,0},{10,2},{12,4},{14,6},{16,28},{18,... | collective-permute-start | bytes 1769480 | tf_op jit(solution)/shard_map/ppermute | solution.py:90
  17.8 1.3 %collective-permute-start = (bf16[256,4096]{1,0:T(8,128)(2,1)S(1)}, bf16[256,4096]{1,0:T(8,128)(2,1)}, u32[]{:S(2)}, u32[]{:S(2)}) collective-permute-start(bf16[256,4096]{1,0:T(8,128)(2,1)S(1)} %copy-done.1), channel_id=1, source_target_pairs={{0,16},{16,0},{1,17},{17,1},{2,18},{18,2},{3,19},{19,3},{4,20},{20... | collective-permute-start | bytes 6291464 | tf_op jit(solution)/shard_map/ppermute | solution.py:93
  19.1 6.7 %fusion.28 = f32[256,1024]{1,0:T(8,128)} fusion(bf16[256,4096]{1,0:T(8,128)(2,1)S(1)} %copy-done.1, bf16[4096,1024]{1,0:T(8,128)(2,1)} %param.8), kind=kOutput, calls=%fused_computation.96 | convolution fusion | flops 2147483648 | bytes 11534336 | tf_op jit(solution)/shard_map/dot_general | solution.py:107
  25.8 1.1 %collective-permute-start.6 = (bf16[64,4608]{1,0:T(8,128)(2,1)}, bf16[64,4608]{1,0:T(8,128)(2,1)S(1)}, u32[]{:S(2)}, u32[]{:S(2)}) collective-permute-start(bf16[64,4608]{1,0:T(8,128)(2,1)} %get-tuple-element.38), channel_id=1, source_target_pairs={{0,10},{2,8},{4,14},{6,12},{8,2},{10,0},{12,6},{14,4},{16,30},{18,... | collective-permute-start | bytes 1769480 | tf_op jit(solution)/shard_map/ppermute | solution.py:90
  27.0 0.7 fusion.21
  28.3 1.3 %fusion.24 = s32[]{:T(128)} fusion(s32[8]{0:T(128)S(1)} %gather_fusion, s32[]{:T(128)S(6)} %axis_index.33, s32[8,8]{1,0:T(8,128)} %fetch_ref.1, s32[]{:T(128)S(6)} %select_n.169), kind=kLoop, calls=%fused_computation.90 | loop fusion | flops 239 | bytes 76 | tf_op jit(solution)/shard_map/reduce_sum | solution.py:112
  31.8 0.9 bitcast_dynamic-update-slice_fusion
  32.6 0.8 slice_dynamic-update-slice_fusion
  33.5 7.8 %collective-permute-done.2 = bf16[64,4608]{1,0:T(8,128)(2,1)S(1)} collective-permute-done((bf16[64,4608]{1,0:T(8,128)(2,1)}, bf16[64,4608]{1,0:T(8,128)(2,1)S(1)}, u32[]{:S(2)}, u32[]{:S(2)}) %collective-permute-start.2) | collective-permute-done | bytes 589856 | tf_op jit(solution)/shard_map/ppermute | solution.py:90
  41.2 16.6 %collective-permute-done.3 = bf16[64,4608]{1,0:T(8,128)(2,1)} collective-permute-done((bf16[64,4608]{1,0:T(8,128)(2,1)}, bf16[64,4608]{1,0:T(8,128)(2,1)}, u32[]{:S(2)}, u32[]{:S(2)}) %collective-permute-start.3) | collective-permute-done | bytes 589856 | tf_op jit(solution)/shard_map/ppermute | solution.py:90
  57.8 0.8 fusion.27
  58.8 0.7 fusion.23
  59.5 7.7 %collective-permute-done.5 = bf16[128,512]{1,0:T(8,128)(2,1)S(1)} collective-permute-done((bf16[128,512]{1,0:T(8,128)(2,1)S(1)}, bf16[128,512]{1,0:T(8,128)(2,1)S(1)}, u32[]{:S(2)}, u32[]{:S(2)}) %collective-permute-start.5) | collective-permute-done | bytes 131104 | tf_op jit(solution)/shard_map/ppermute | solution.py:93
  67.2 1.4 %collective-permute-start.4 = (s32[1,8]{1,0:T(1,128)S(1)}, s32[1,8]{1,0:T(1,128)S(1)}, u32[]{:S(2)}, u32[]{:S(2)}) collective-permute-start(s32[1,8]{1,0:T(1,128)S(1)} %copy-done.5), channel_id=1, source_target_pairs={{0,16},{16,0},{1,17},{17,1},{2,18},{18,2},{3,19},{19,3},{4,20},{20... | collective-permute-start | bytes 104 | tf_op jit(solution)/shard_map/ppermute | solution.py:93
  68.6 2.2 %collective-permute-done.4 = s32[1,8]{1,0:T(1,128)S(1)} collective-permute-done((s32[1,8]{1,0:T(1,128)S(1)}, s32[1,8]{1,0:T(1,128)S(1)}, u32[]{:S(2)}, u32[]{:S(2)}) %collective-permute-start.4) | collective-permute-done | bytes 64 | tf_op jit(solution)/shard_map/ppermute | solution.py:93
  71.0 1.8 %convolution_select_fusion.4 = f32[64,256]{1,0:T(8,128)S(1)} fusion(bf16[256,4096]{1,0:T(8,128)(2,1)S(1)} %copy-done.1, bf16[64,4608]{1,0:T(8,128)(2,1)} %collective-permute-done.3, pred[256]{0:T(512)(128)(4,1)S(1)} %get-tuple-element.63), kind=kOutput, calls=%fused_computation.7 | convolution fusion | flops 134234112 | bytes 2687232 | tf_op jit(solution)/shard_map/dot_general | solution.py:149
  72.8 2.5 %convolution_select_fusion.2 = f32[64,256]{1,0:T(8,128)S(1)} fusion(bf16[256,4096]{1,0:T(8,128)(2,1)} %collective-permute-done, bf16[64,4608]{1,0:T(8,128)(2,1)} %collective-permute-done.3, pred[256]{0:T(512)(128)(4,1)S(1)} %get-tuple-element.68), kind=kOutput, calls=%fused_computation.4 | convolution fusion | flops 134234112 | bytes 2687232 | tf_op jit(solution)/shard_map/dot_general | solution.py:149
  75.4 2.4 %fusion = f32[64,256]{1,0:T(8,128)S(1)} fusion(f32[64,256]{1,0:T(8,128)S(1)} %convolution_select_fusion.2, bf16[256,4096]{1,0:T(8,128)(2,1)} %collective-permute-done, bf16[64,4608]{1,0:T(8,128)(2,1)S(1)} %collective-permute-done.2, pred[256]{0:T(512)(128)(4,1)S(1)} %get-tuple-element.69), kind=kOutput, calls=%fused_computation.6 | convolution fusion | flops 134250496 | bytes 2753024 | tf_op jit(solution)/shard_map/dot_general | solution.py:149
  77.7 1.8 %convolution_select_fusion.7 = f32[64,256]{1,0:T(8,128)S(1)} fusion(bf16[256,4096]{1,0:T(8,128)(2,1)S(1)} %copy-done.1, bf16[4,4096,64]{1,2,0:T(8,128)(2,1)} %param.9, s32[]{:T(128)S(6)} %select_n.180, pred[256]{0:T(512)(128)(4,1)S(1)} %get-tuple-element.66), kind=kOutput, calls=%fused_computation.13 | convolution fusion | flops 134234112 | bytes 2687236 | tf_op jit(solution)/shard_map/dot_general | solution.py:149
  79.5 1.8 %fusion.3 = f32[64,256]{1,0:T(8,128)S(1)} fusion(f32[64,256]{1,0:T(8,128)S(1)} %convolution_select_fusion.7, bf16[256,4096]{1,0:T(8,128)(2,1)S(1)} %copy-done.1, bf16[64,4608]{1,0:T(8,128)(2,1)} %collective-permute-done.1, pred[256]{0:T(512)(128)(4,1)S(1)} %get-tuple-element.65), kind=kOutput, calls=%fused_computation.12 | convolution fusion | flops 134250496 | bytes 2752768 | tf_op jit(solution)/shard_map/dot_general | solution.py:149
  81.3 0.8 fusion.2
  82.2 1.4 %collective-permute-start.7 = (bf16[64,512]{1,0:T(8,128)(2,1)S(1)}, bf16[64,512]{1,0:T(8,128)(2,1)S(1)}, u32[]{:S(2)}, u32[]{:S(2)}) collective-permute-start(bf16[64,512]{1,0:T(8,128)(2,1)S(1)} %slice.42), channel_id=1, source_target_pairs={{0,16},{16,0},{1,17},{17,1},{2,18},{18,2},{3,19},{19,3},{4,20},{20... | collective-permute-start | bytes 196616 | tf_op jit(solution)/shard_map/ppermute | solution.py:93
  83.5 2.4 %convolution_select_fusion = f32[64,256]{1,0:T(8,128)S(1)} fusion(bf16[256,4096]{1,0:T(8,128)(2,1)} %collective-permute-done, bf16[64,4608]{1,0:T(8,128)(2,1)S(1)} %collective-permute-done.6, pred[256]{0:T(512)(128)(4,1)S(1)} %get-tuple-element.67), kind=kOutput, calls=%fused_computation.2 | convolution fusion | flops 134234112 | bytes 2687488 | tf_op jit(solution)/shard_map/dot_general | solution.py:149
  85.9 0.8 convolution_select_fusion.1
  86.8 1.3 %collective-permute-done.8 = f32[64,512]{1,0:T(8,128)S(1)} collective-permute-done((f32[64,512]{1,0:T(8,128)S(1)}, f32[64,512]{1,0:T(8,128)S(1)}, u32[]{:S(2)}, u32[]{:S(2)}) %collective-permute-start.8) | collective-permute-done | bytes 131104 | tf_op jit(solution)/shard_map/ppermute | solution.py:97
  88.2 1.1 %collective-permute-start.9 = (f32[64,256]{1,0:T(8,128)S(1)}, f32[64,256]{1,0:T(8,128)S(1)}, u32[]{:S(2)}, u32[]{:S(2)}) collective-permute-start(f32[64,256]{1,0:T(8,128)S(1)} %slice.54), channel_id=1, source_target_pairs={{0,16},{16,0},{1,17},{17,1},{2,18},{18,2},{3,19},{19,3},{4,20},{20... | collective-permute-start | bytes 196616 | tf_op jit(solution)/shard_map/ppermute | solution.py:93
  89.3 3.2 %collective-permute-done.9 = f32[64,256]{1,0:T(8,128)S(1)} collective-permute-done((f32[64,256]{1,0:T(8,128)S(1)}, f32[64,256]{1,0:T(8,128)S(1)}, u32[]{:S(2)}, u32[]{:S(2)}) %collective-permute-start.9) | collective-permute-done | bytes 65568 | tf_op jit(solution)/shard_map/ppermute | solution.py:93
  92.7 0.7 convolution_multiply_fusion
  93.4 0.8 add_convert_fusion
  (47 shorter events, 1.4 us)
Async XLA Ops:
  6.5 11.3 %copy-start.1 = (bf16[256,4096]{1,0:T(8,128)(2,1)S(1)}, bf16[256,4096]{1,0:T(8,128)(2,1)}, u32[]{:S(2)}) copy-start(bf16[256,4096]{1,0:T(8,128)(2,1)} %param.7) | copy-start | bytes 6291460
  6.5 75.6 %reduce-scatter.2.cloned.1.call-start = ((), (), s32[]{:S(2)}) async-start(), calls=%async_computation.1 | async-start | bytes 1572864 | tf_op jit(solution)/shard_map/reduce_scatter | solution.py:108
  10.7 17.0 %copy-start = (s32[32]{0:T(128)S(1)}, s32[32]{0:T(128)}, u32[]{:S(2)}) copy-start(s32[32]{0:T(128)} %home_ref.1) | copy-start | bytes 388
  10.7 19.0 %copy-start.5 = (s32[1,8]{1,0:T(1,128)S(1)}, s32[1,8]{1,0:T(1,128)}, u32[]{:S(2)}) copy-start(s32[1,8]{1,0:T(1,128)} %param.13) | copy-start | bytes 100
  10.7 21.9 %collective-permute-start.1 = (bf16[64,4608]{1,0:T(8,128)(2,1)}, bf16[64,4608]{1,0:T(8,128)(2,1)}, u32[]{:S(2)}, u32[]{:S(2)}) collective-permute-start(bf16[64,4608]{1,0:T(8,128)(2,1)} %get-tuple-element.34), channel_id=1, source_target_pairs={{0,2},{2,0},{4,6},{6,4},{8,10},{10,8},{12,14},{14,12},{16,18},{18,... | collective-permute-start | bytes 1769480 | tf_op jit(solution)/shard_map/ppermute | solution.py:90
  13.6 27.6 %collective-permute-start.2 = (bf16[64,4608]{1,0:T(8,128)(2,1)}, bf16[64,4608]{1,0:T(8,128)(2,1)S(1)}, u32[]{:S(2)}, u32[]{:S(2)}) collective-permute-start(bf16[64,4608]{1,0:T(8,128)(2,1)} %get-tuple-element.35), channel_id=1, source_target_pairs={{0,4},{2,6},{4,0},{6,2},{8,12},{10,14},{12,8},{14,10},{16,22},{18,... | collective-permute-start | bytes 1769480 | tf_op jit(solution)/shard_map/ppermute | solution.py:90
  15.2 42.6 %collective-permute-start.3 = (bf16[64,4608]{1,0:T(8,128)(2,1)}, bf16[64,4608]{1,0:T(8,128)(2,1)}, u32[]{:S(2)}, u32[]{:S(2)}) collective-permute-start(bf16[64,4608]{1,0:T(8,128)(2,1)} %get-tuple-element.36), channel_id=1, source_target_pairs={{0,8},{2,10},{4,12},{6,14},{8,0},{10,2},{12,4},{14,6},{16,28},{18,... | collective-permute-start | bytes 1769480 | tf_op jit(solution)/shard_map/ppermute | solution.py:90
  17.8 49.4 %collective-permute-start = (bf16[256,4096]{1,0:T(8,128)(2,1)S(1)}, bf16[256,4096]{1,0:T(8,128)(2,1)}, u32[]{:S(2)}, u32[]{:S(2)}) collective-permute-start(bf16[256,4096]{1,0:T(8,128)(2,1)S(1)} %copy-done.1), channel_id=1, source_target_pairs={{0,16},{16,0},{1,17},{17,1},{2,18},{18,2},{3,19},{19,3},{4,20},{20... | collective-permute-start | bytes 6291464 | tf_op jit(solution)/shard_map/ppermute | solution.py:93
  25.8 56.3 %collective-permute-start.6 = (bf16[64,4608]{1,0:T(8,128)(2,1)}, bf16[64,4608]{1,0:T(8,128)(2,1)S(1)}, u32[]{:S(2)}, u32[]{:S(2)}) collective-permute-start(bf16[64,4608]{1,0:T(8,128)(2,1)} %get-tuple-element.38), channel_id=1, source_target_pairs={{0,10},{2,8},{4,14},{6,12},{8,2},{10,0},{12,6},{14,4},{16,30},{18,... | collective-permute-start | bytes 1769480 | tf_op jit(solution)/shard_map/ppermute | solution.py:90
  58.7 8.5 %collective-permute-start.5 = (bf16[128,512]{1,0:T(8,128)(2,1)S(1)}, bf16[128,512]{1,0:T(8,128)(2,1)S(1)}, u32[]{:S(2)}, u32[]{:S(2)}) collective-permute-start(bf16[128,512]{1,0:T(8,128)(2,1)S(1)} %pad_maximum_fusion), channel_id=1, source_target_pairs={{0,16},{16,0},{1,17},{17,1},{2,18},{18,2},{3,19},{19,3},{4,20},{20... | collective-permute-start | bytes 393224 | tf_op jit(solution)/shard_map/ppermute | solution.py:93
  67.2 3.9 %copy-start.3 = (bf16[384,512]{1,0:T(8,128)(2,1)}, bf16[384,512]{1,0:T(8,128)(2,1)S(1)}, u32[]{:S(2)}) copy-start(bf16[384,512]{1,0:T(8,128)(2,1)S(1)} %constant_dynamic-update-slice_fusion) | copy-start | bytes 1179652
  67.2 3.6 %collective-permute-start.4 = (s32[1,8]{1,0:T(1,128)S(1)}, s32[1,8]{1,0:T(1,128)S(1)}, u32[]{:S(2)}, u32[]{:S(2)}) collective-permute-start(s32[1,8]{1,0:T(1,128)S(1)} %copy-done.5), channel_id=1, source_target_pairs={{0,16},{16,0},{1,17},{17,1},{2,18},{18,2},{3,19},{19,3},{4,20},{20... | collective-permute-start | bytes 104 | tf_op jit(solution)/shard_map/ppermute | solution.py:93
  82.2 4.5 %collective-permute-start.7 = (bf16[64,512]{1,0:T(8,128)(2,1)S(1)}, bf16[64,512]{1,0:T(8,128)(2,1)S(1)}, u32[]{:S(2)}, u32[]{:S(2)}) collective-permute-start(bf16[64,512]{1,0:T(8,128)(2,1)S(1)} %slice.42), channel_id=1, source_target_pairs={{0,16},{16,0},{1,17},{17,1},{2,18},{18,2},{3,19},{19,3},{4,20},{20... | collective-permute-start | bytes 196616 | tf_op jit(solution)/shard_map/ppermute | solution.py:93
  85.9 6.8 %copy-start.4 = (bf16[384,512]{1,0:T(8,128)(2,1)S(1)}, bf16[384,512]{1,0:T(8,128)(2,1)}, u32[]{:S(2)}) copy-start(bf16[384,512]{1,0:T(8,128)(2,1)} %copy-done.3) | copy-start | bytes 1179652
  86.7 6.7 %copy-start.2 = (f32[256,512]{1,0:T(8,128)S(1)}, f32[256,512]{1,0:T(8,128)}, u32[]{:S(2)}) copy-start(f32[256,512]{1,0:T(8,128)} %reduce-scatter.2.cloned.1.call-done) | copy-start | bytes 1572868
  86.8 1.4 %collective-permute-start.8 = (f32[64,512]{1,0:T(8,128)S(1)}, f32[64,512]{1,0:T(8,128)S(1)}, u32[]{:S(2)}, u32[]{:S(2)}) collective-permute-start(f32[64,512]{1,0:T(8,128)S(1)} %constant_dynamic-update-slice_fusion.3), channel_id=1, source_target_pairs={{0,1},{1,0},{2,3},{3,2},{4,5},{5,4},{6,7},{7,6},{8,9},{9,8},{10,11... | collective-permute-start | bytes 393224 | tf_op jit(solution)/shard_map/ppermute | solution.py:97
  88.2 4.3 %collective-permute-start.9 = (f32[64,256]{1,0:T(8,128)S(1)}, f32[64,256]{1,0:T(8,128)S(1)}, u32[]{:S(2)}, u32[]{:S(2)}) collective-permute-start(f32[64,256]{1,0:T(8,128)S(1)} %slice.54), channel_id=1, source_target_pairs={{0,16},{16,0},{1,17},{17,1},{2,18},{18,2},{3,19},{19,3},{4,20},{20... | collective-permute-start | bytes 196616 | tf_op jit(solution)/shard_map/ppermute | solution.py:93
Sparse Core Ops, SparseCore 0:
  26.0 6.6 reduce-scatter.1

commit v10 on v9

--- a/solution.py
+++ b/solution.py
@@ -61,6 +61,70 @@
     )
 
 
+def score_kernel(parts, shared, alone, scalars, *refs):
+    row_steps = refs[0]
+    tokens, panels = refs[1 : 1 + parts], refs[1 + parts : 1 + parts + shared + alone]
+    out, sums = refs[1 + parts + shared + alone], refs[2 + parts + shared + alone :]
+    at = pl.program_id(0)
+    blocks = [x[...] if len(x.shape) == 2 else x[0] for x in panels]
+    stack = jnp.concatenate(blocks, axis=0)
+    rank, count = blocks[0].shape[0], out.shape[1] // parts
+    for shift in range(parts):
+        left = stack if shift == 0 else stack[: shared * rank]
+        product = lax.dot_general(
+            left, tokens[shift][...], (((1,), (1,)), ((), ())), preferred_element_type=jnp.float32
+        )
+
+        @pl.when(at == 0)
+        def _(shift=shift, product=product):
+            sums[shift][...] = product
+
+        @pl.when(at > 0)
+        def _(shift=shift, product=product):
+            sums[shift][...] += product
+
+    @pl.when(at == pl.num_programs(0) - 1)
+    def _():
+        for shift in range(parts):
+            used = row_steps[pl.ds(shift, 1), :]
+            total = jnp.zeros((rank, count), jnp.float32)
+            for n in range(shared + (alone if shift == 0 else 0)):
+                term = sums[shift][pl.ds(n * rank, rank), :]
+                total = total + jnp.where(used == scalars[1 + n], term, 0.0)
+            out[:, pl.ds(shift * count, count)] = total
+
+
+def score(tokens_of, shared, solo, panels, slot, steps, row_steps):
+    parts, count = len(tokens_of), tokens_of[0].shape[0]
+    _, rank, depth = panels.shape
+    chunk = 1024
+    alone = len(solo) + 1
+    panel_spec = pl.BlockSpec((rank, chunk), lambda k, scalars: (0, k))
+    heights = [(len(shared) + (alone if shift == 0 else 0)) * rank for shift in range(parts)]
+    return pl.pallas_call(
+        functools.partial(score_kernel, parts, len(shared), alone),
+        grid_spec=pltpu.PrefetchScalarGridSpec(
+            num_scalar_prefetch=1,
+            grid=(depth // chunk,),
+            in_specs=[pl.BlockSpec(row_steps.shape, lambda k, scalars: (0, 0))]
+            + [pl.BlockSpec((count, chunk), lambda k, scalars: (0, k))] * parts
+            + [panel_spec] * (len(shared) + len(solo))
+            + [pl.BlockSpec((1, rank, chunk), lambda k, scalars: (scalars[0], 0, k))],
+            out_specs=pl.BlockSpec((rank, parts * count), lambda k, scalars: (0, 0)),
+            scratch_shapes=[pltpu.VMEM((height, count), jnp.float32) for height in heights],
+        ),
+        out_shape=jax.ShapeDtypeStruct((rank, parts * count), jnp.float32),
+        compiler_params=pltpu.CompilerParams(
+            dimension_semantics=("arbitrary",), vmem_limit_bytes=32 << 20
+        ),
+        cost_estimate=pl.CostEstimate(
+            flops=2 * depth * count * sum(heights),
+            bytes_accessed=2 * depth * (parts * count + heights[0]),
+            transcendentals=0,
+        ),
+    )(jnp.stack([slot] + steps), row_steps, *tokens_of, *shared, *solo, panels)
+
+
 def on_device(tokens, base_weight, shrink_panels, expand_panels, adapter_home, fetch_list, seg_len):
     per_home, depth, _ = shrink_panels.shape
     replicas, parts, cores = lax.axis_size("rep"), lax.axis_size("parts"), lax.axis_size("tp")
@@ -110,7 +174,6 @@
     stored = jnp.take(adapter_home, lax.dynamic_index_in_dim(fetch_list, me, 0, keepdims=False))
     steps = (stored // per_home) ^ me
     slot = jnp.sum(jnp.where(steps == 0, stored % per_home, 0))
-    own = lax.dynamic_index_in_dim(panels, slot, 0, keepdims=False)
     left = lax.axis_index("tp") * columns
     own_expand = lax.dynamic_slice(expand_panels, (slot, 0, left), (1, rank, columns))[0]
     far_recv, near_recv = recv[: len(far)], recv[len(far) : len(far) + len(near)]
@@ -132,8 +195,8 @@
     expand = jnp.concatenate(expands, axis=0)
 
     lengths_of = [seg_len[0]]
+    seg_len, solo_recv = tie((seg_len, solo_recv))
     for shift in range(1, parts):
-        seg_len, tokens_of[shift] = tie((seg_len, tokens_of[shift]))
         lengths_of.append(shift_parts(seg_len, shift)[0])
     rows = jnp.arange(tok_count, dtype=jnp.int32)
 
@@ -143,38 +206,24 @@
         member = (rows[:, None] >= starts[None, :]) & (rows[:, None] < (starts + lengths)[None, :])
         return jnp.sum(jnp.where(member, steps[None, :], 0), axis=1)[None, :]
 
-    row_steps = [steps_of_rows(lengths) for lengths in lengths_of]
-
-    def score(block, step, shift):
-        product = lax.dot_general(
-            block[:, :depth],
-            tokens_of[shift],
-            (((1,), (1,)), ((), ())),
-            preferred_element_type=jnp.float32,
-        )
-        return jnp.where(row_steps[shift] == step, product, 0.0)
-
-    scores = [score(own, 0, 0)] + [0.0] * (parts - 1)
-    for block, group in zip(solo_recv, solo):
-        scores[0] = scores[0] + score(block, group[0], 0)
-    for block, group in zip(early, early_groups):
-        for shift in range(parts):
-            scores[shift] = scores[shift] + score(block, step_of(group), shift)
-    tokens_of, scores, expand, base, far_recv[-1] = tie(
-        (tokens_of, scores, expand, base, far_recv[-1])
-    )
+    row_steps = jnp.concatenate([steps_of_rows(lengths) for lengths in lengths_of], axis=0)
+
+    row_steps, expand, base, far_recv[-1] = tie((row_steps, expand, base, far_recv[-1]))
     last_expand = far_recv[-1][:, depth:]
     expands = [expand, last_expand] + [shift_parts(last_expand, shift) for shift in range(1, parts)]
     expand_steps += [step_of(far[-1], shift) for shift in range(parts)]
-    for shift in range(parts):
-        scores[shift] = scores[shift] + score(far_recv[-1], step_of(far[-1]), shift)
+    shared_steps = [step_of(group) for group in far + near]
+    alone_steps = [jnp.int32(group[0]) for group in solo] + [jnp.int32(0)]
+    scores = score(
+        tokens_of, far_recv + near_recv, solo_recv, panels, slot, shared_steps + alone_steps, row_steps
+    )
     scores, expands = tie((scores, expands))
-    scores = trade(jnp.concatenate(scores, axis=1))
+    scores = trade(scores)
     shrink = scores[:, :tok_count]
     for shift in range(1, parts):
         shrink = shrink + shift_parts(scores[:, shift * tok_count : (shift + 1) * tok_count], -shift)
     wide = jnp.concatenate(
-        [jnp.where(row_steps[0] == step, shrink, 0.0) for step in expand_steps], axis=0
+        [jnp.where(row_steps[:1] == step, shrink, 0.0) for step in expand_steps], axis=0
     )
     lora = lax.dot_general(
         wide,

time: 102 us -> 92.5 us (0.907)
  matrix products: 21.5 us -> 8.94 us
  Pallas kernels: 4.11 us -> 10.2 us
  waiting for transfers between devices: 38.8 us -> 34.7 us
  local copies, waits for them, and re-layouts: 3.27 us -> 4.67 us
    dot_general x8 -> x0, matrix products: 14.2 us -> none  [score(): lax.dot_general(block[:, :depth], tokens_of[shift], (((1,), (1,)), ((), (...]
    pallas_call x0 -> x1, Pallas kernels: none -> 6.28 us  [score(): pl.pallas_call(functools.partial(score_kernel, parts, len(shared), alone)...]
    ppermute x5, waiting for transfers between devices: 13.1 us -> 10.1 us  [shift_parts(): lax.ppermute(x, 'parts', [(i, (i + shift) % parts) for i in range(parts)])]
  transfers between devices with their start and end apart: 11 -> 11, of which waited for: 6 -> 6; matrix products, arithmetic and copies ran while one was open for 27% -> 16% of each run, Pallas kernels for 0% -> 7%
where the time goes in v10:
time: 92.5 us; the launch traced here: 92 us
  waiting for transfers between devices  34.7 us (38%)
  between operations  15.5 us (17%)
  starting transfers between devices  13.9 us (15%)
  Pallas kernels  10.2 us (11%)
  matrix products  8.94 us (10%)
  local copies, waits for them, and re-layouts  4.67 us (5%)
  other arithmetic  4.05 us (4%)
    ppermute x4, waiting for transfers between devices, hop(): return lax.ppermute(x, ('parts', 'rep'), pairs)  23.3 us
    ppermute x5, waiting for transfers between devices, shift_parts(): lax.ppermute(x, 'parts', [(i, (i + shift) % parts) for i in range(parts)])  10.1 us
    ppermute x4, starting transfers between devices, hop(): return lax.ppermute(x, ('parts', 'rep'), pairs)  8.36 us
    dot_general x1, matrix products, on_device(): base_part = jnp.dot(tokens, base_weight, preferred_element_type=jnp.float32)  7.32 us
    pallas_call x1, Pallas kernels, score(): pl.pallas_call(functools.partial(score_kernel, parts, len(shared), alone)...  6.28 us
    ppermute x5, starting transfers between devices, shift_parts(): lax.ppermute(x, 'parts', [(i, (i + shift) % parts) for i in range(parts)])  5.48 us
    pallas_call x1, Pallas kernels, pack(): pl.pallas_call(functools.partial(pack_kernel, blocks), out_shape=[jax.Sha...  3.93 us
  transfers between devices with their start and end apart: 11, of which 6 were waited for; matrix products, arithmetic and copies ran while one was open for 16% of the time, Pallas kernels for 7%

profile of v10, /device:TPU:0, one launch (start us, length us, event | category | flops | bytes accessed | tf_op | source)
XLA Modules:
  0.0 92.0 jit_solution(9077935597131310697)
XLA Ops:
  6.5 3.9 %shard_map.73 = (bf16[64,4608]{1,0:T(8,128)(2,1)}, bf16[64,4608]{1,0:T(8,128)(2,1)}, bf16[64,4608]{1,0:T(8,128)(2,1)}, bf16[64,4608]{1,0:T(8,128)(2,1)}) custom-call(s32[32]{0:T(128)} %home_ref.1, s32[8,8]{1,0:T(8,128)} %fetch_ref.1, bf16[4,64,4096]{2,1,0:T(8,128)(2,1)} %bitcast.40, bf16[4,64,1024]{2,1,0:T(8,128)(2,1)} %expand_ref.1), custom_call_target="tpu_custom_call" | custom-call | bytes 4718592 | tf_op jit(solution)/shard_map/pallas_call | solution.py:50
  10.5 3.0 %collective-permute-start = (bf16[64,4608]{1,0:T(8,128)(2,1)}, bf16[64,4608]{1,0:T(8,128)(2,1)S(1)}, u32[]{:S(2)}, u32[]{:S(2)}) collective-permute-start(bf16[64,4608]{1,0:T(8,128)(2,1)} %get-tuple-element.28), channel_id=1, source_target_pairs={{0,2},{2,0},{4,6},{6,4},{8,10},{10,8},{12,14},{14,12},{16,18},{18,... | collective-permute-start | bytes 1769480 | tf_op jit(solution)/shard_map/ppermute | solution.py:154
  13.5 1.6 %collective-permute-start.2 = (bf16[64,4608]{1,0:T(8,128)(2,1)}, bf16[64,4608]{1,0:T(8,128)(2,1)S(1)}, u32[]{:S(2)}, u32[]{:S(2)}) collective-permute-start(bf16[64,4608]{1,0:T(8,128)(2,1)} %get-tuple-element.30), channel_id=1, source_target_pairs={{0,4},{2,6},{4,0},{6,2},{8,12},{10,14},{12,8},{14,10},{16,22},{18,... | collective-permute-start | bytes 1769480 | tf_op jit(solution)/shard_map/ppermute | solution.py:154
  15.1 2.6 %collective-permute-start.3 = (bf16[64,4608]{1,0:T(8,128)(2,1)}, bf16[64,4608]{1,0:T(8,128)(2,1)}, u32[]{:S(2)}, u32[]{:S(2)}) collective-permute-start(bf16[64,4608]{1,0:T(8,128)(2,1)} %get-tuple-element.31), channel_id=1, source_target_pairs={{0,8},{2,10},{4,12},{6,14},{8,0},{10,2},{12,4},{14,6},{16,28},{18,... | collective-permute-start | bytes 1769480 | tf_op jit(solution)/shard_map/ppermute | solution.py:154
  17.7 1.3 %collective-permute-start.6 = (bf16[256,4096]{1,0:T(8,128)(2,1)}, bf16[256,4096]{1,0:T(8,128)(2,1)}, u32[]{:S(2)}, u32[]{:S(2)}) collective-permute-start(bf16[256,4096]{1,0:T(8,128)(2,1)} %refs_1_), channel_id=1, source_target_pairs={{0,16},{16,0},{1,17},{17,1},{2,18},{18,2},{3,19},{19,3},{4,20},{20... | collective-permute-start | bytes 6291464 | tf_op jit(solution)/shard_map/ppermute | solution.py:157
  19.0 7.3 %fusion.14 = f32[256,1024]{1,0:T(8,128)} fusion(bf16[256,4096]{1,0:T(8,128)(2,1)} %refs_1_, bf16[4096,1024]{1,0:T(8,128)(2,1)} %param.8), kind=kOutput, calls=%fused_computation.70 | convolution fusion | flops 2147483648 | bytes 11534336 | tf_op jit(solution)/shard_map/dot_general | solution.py:171
  26.4 1.1 %collective-permute-start.5 = (bf16[64,4608]{1,0:T(8,128)(2,1)}, bf16[64,4608]{1,0:T(8,128)(2,1)}, u32[]{:S(2)}, u32[]{:S(2)}) collective-permute-start(bf16[64,4608]{1,0:T(8,128)(2,1)} %get-tuple-element.33), channel_id=1, source_target_pairs={{0,10},{2,8},{4,14},{6,12},{8,2},{10,0},{12,6},{14,4},{16,30},{18,... | collective-permute-start | bytes 1769480 | tf_op jit(solution)/shard_map/ppermute | solution.py:154
  27.5 0.7 fusion.7
  28.2 0.6 gather_fusion
  28.9 0.1 select_reduce_fusion.3
  29.0 0.7 fusion.9
  29.7 1.4 %fusion.10 = s32[]{:T(128)} fusion(s32[8]{0:T(128)S(1)} %gather_fusion, s32[]{:T(128)S(6)} %axis_index.33, s32[8,8]{1,0:T(8,128)} %fetch_ref.1, s32[]{:T(128)S(6)} %select_n.137), kind=kLoop, calls=%fused_computation.64 | loop fusion | flops 239 | bytes 76 | tf_op jit(solution)/shard_map/reduce_sum | solution.py:176
  32.9 0.7 stack.19.scalars
  33.6 0.8 bitcast_dynamic-update-slice_fusion
  34.5 6.6 %collective-permute-done.2.refs_5_ = bf16[64,4608]{1,0:T(8,128)(2,1)S(1)} collective-permute-done((bf16[64,4608]{1,0:T(8,128)(2,1)}, bf16[64,4608]{1,0:T(8,128)(2,1)S(1)}, u32[]{:S(2)}, u32[]{:S(2)}) %collective-permute-start.2) | collective-permute-done | bytes 589856 | tf_op jit(solution)/shard_map/ppermute | solution.py:154
  41.1 16.3 %collective-permute-done.3.refs_3_ = bf16[64,4608]{1,0:T(8,128)(2,1)} collective-permute-done((bf16[64,4608]{1,0:T(8,128)(2,1)}, bf16[64,4608]{1,0:T(8,128)(2,1)}, u32[]{:S(2)}, u32[]{:S(2)}) %collective-permute-start.3) | collective-permute-done | bytes 589856 | tf_op jit(solution)/shard_map/ppermute | solution.py:154
  57.4 0.8 fusion.13
  58.4 2.0 %collective-permute-start.1 = (s32[1,8]{1,0:T(1,128)S(1)}, s32[1,8]{1,0:T(1,128)S(1)}, u32[]{:S(2)}, u32[]{:S(2)}) collective-permute-start(s32[1,8]{1,0:T(1,128)S(1)} %copy-done.4), channel_id=1, source_target_pairs={{0,16},{16,0},{1,17},{17,1},{2,18},{18,2},{3,19},{19,3},{4,20},{20... | collective-permute-start | bytes 104 | tf_op jit(solution)/shard_map/ppermute | solution.py:157
  60.4 6.9 %collective-permute-done.1 = s32[1,8]{1,0:T(1,128)S(1)} collective-permute-done((s32[1,8]{1,0:T(1,128)S(1)}, s32[1,8]{1,0:T(1,128)S(1)}, u32[]{:S(2)}, u32[]{:S(2)}) %collective-permute-start.1) | collective-permute-done | bytes 64 | tf_op jit(solution)/shard_map/ppermute | solution.py:157
  67.3 0.1 select_reduce_fusion.2
  67.4 0.1 select_reduce_fusion.1
  67.6 0.7 copy-done.3
  68.3 0.4 collective-permute-done.5.refs_4_
  68.7 0.8 slice.34
  69.6 0.9 collective-permute-start.7
  70.5 6.3 %shard_map.74 = f32[64,512]{1,0:T(8,128)S(1)} custom-call(s32[6]{0:T(128)S(1)} %stack.19.scalars, s32[2,256]{1,0:T(2,128)S(1)} %pad_add_fusion.refs_0_, bf16[256,4096]{1,0:T(8,128)(2,1)} %refs_1_, bf16[256,4096]{1,0:T(8,128)(2,1)} %collective-permute-done.6.refs_2_, bf16[64,4608]{1,0:T(8,128)(2,1)} %collective-permute-done.3.refs_3_, ...), custom_call_target="tpu_custom_call" | custom-call | flops 1073741824 | bytes 6815744 | tf_op jit(solution)/shard_map/pallas_call | solution.py:104
  76.8 0.1 collective-permute-start.8
  76.9 1.3 %collective-permute-done.8 = f32[64,512]{1,0:T(8,128)S(1)} collective-permute-done((f32[64,512]{1,0:T(8,128)S(1)}, f32[64,512]{1,0:T(8,128)S(1)}, u32[]{:S(2)}, u32[]{:S(2)}) %collective-permute-start.8) | collective-permute-done | bytes 131104 | tf_op jit(solution)/shard_map/ppermute | solution.py:161
  78.3 1.2 %collective-permute-start.9 = (f32[64,256]{1,0:T(8,128)S(1)}, f32[64,256]{1,0:T(8,128)S(1)}, u32[]{:S(2)}, u32[]{:S(2)}) collective-permute-start(f32[64,256]{1,0:T(8,128)S(1)} %slice.43), channel_id=1, source_target_pairs={{0,16},{16,0},{1,17},{17,1},{2,18},{18,2},{3,19},{19,3},{4,20},{20... | collective-permute-start | bytes 196616 | tf_op jit(solution)/shard_map/ppermute | solution.py:157
  79.5 3.1 %collective-permute-done.9 = f32[64,256]{1,0:T(8,128)S(1)} collective-permute-done((f32[64,256]{1,0:T(8,128)S(1)}, f32[64,256]{1,0:T(8,128)S(1)}, u32[]{:S(2)}, u32[]{:S(2)}) %collective-permute-start.9) | collective-permute-done | bytes 65568 | tf_op jit(solution)/shard_map/ppermute | solution.py:157
  82.7 1.6 %convolution_multiply_fusion = f32[256,512]{1,0:T(8,128)S(1)} fusion(f32[512,256]{1,0:T(8,128)S(1)} %select_dynamic-update-slice_fusion, bf16[64,512]{1,0:T(8,128)(2,1)S(1)} %collective-permute-done.7, bf16[64,512]{1,0:T(8,128)(2,1)S(1)} %slice.34, bf16[384,512]{1,0:T(8,128)(2,1)} %copy-done.3), kind=kOutput, calls=%fused_computation.1 | convolution fusion | flops 807010304 | bytes 1572864 | tf_op jit(solution)/shard_map/dot_general | solution.py:228
  84.4 0.8 add_convert_fusion
  (35 shorter events, 0.3 us)
Async XLA Ops:
  6.5 62.2 %reduce-scatter.2.cloned.1.call-start = ((), (), s32[]{:S(2)}) async-start(), calls=%async_computation.1 | async-start | bytes 1572864 | tf_op jit(solution)/shard_map/reduce_scatter | solution.py:172
  10.5 17.7 %copy-start.1 = (s32[32]{0:T(128)S(1)}, s32[32]{0:T(128)}, u32[]{:S(2)}) copy-start(s32[32]{0:T(128)} %home_ref.1) | copy-start | bytes 388
  10.5 18.4 %copy-start.4 = (s32[1,8]{1,0:T(1,128)S(1)}, s32[1,8]{1,0:T(1,128)}, u32[]{:S(2)}) copy-start(s32[1,8]{1,0:T(1,128)} %param.13) | copy-start | bytes 100
  10.5 24.0 %collective-permute-start = (bf16[64,4608]{1,0:T(8,128)(2,1)}, bf16[64,4608]{1,0:T(8,128)(2,1)S(1)}, u32[]{:S(2)}, u32[]{:S(2)}) collective-permute-start(bf16[64,4608]{1,0:T(8,128)(2,1)} %get-tuple-element.28), channel_id=1, source_target_pairs={{0,2},{2,0},{4,6},{6,4},{8,10},{10,8},{12,14},{14,12},{16,18},{18,... | collective-permute-start | bytes 1769480 | tf_op jit(solution)/shard_map/ppermute | solution.py:154
  13.5 27.5 %collective-permute-start.2 = (bf16[64,4608]{1,0:T(8,128)(2,1)}, bf16[64,4608]{1,0:T(8,128)(2,1)S(1)}, u32[]{:S(2)}, u32[]{:S(2)}) collective-permute-start(bf16[64,4608]{1,0:T(8,128)(2,1)} %get-tuple-element.30), channel_id=1, source_target_pairs={{0,4},{2,6},{4,0},{6,2},{8,12},{10,14},{12,8},{14,10},{16,22},{18,... | collective-permute-start | bytes 1769480 | tf_op jit(solution)/shard_map/ppermute | solution.py:154
  15.1 42.3 %collective-permute-start.3 = (bf16[64,4608]{1,0:T(8,128)(2,1)}, bf16[64,4608]{1,0:T(8,128)(2,1)}, u32[]{:S(2)}, u32[]{:S(2)}) collective-permute-start(bf16[64,4608]{1,0:T(8,128)(2,1)} %get-tuple-element.31), channel_id=1, source_target_pairs={{0,8},{2,10},{4,12},{6,14},{8,0},{10,2},{12,4},{14,6},{16,28},{18,... | collective-permute-start | bytes 1769480 | tf_op jit(solution)/shard_map/ppermute | solution.py:154
  17.7 52.8 %collective-permute-start.6 = (bf16[256,4096]{1,0:T(8,128)(2,1)}, bf16[256,4096]{1,0:T(8,128)(2,1)}, u32[]{:S(2)}, u32[]{:S(2)}) collective-permute-start(bf16[256,4096]{1,0:T(8,128)(2,1)} %refs_1_), channel_id=1, source_target_pairs={{0,16},{16,0},{1,17},{17,1},{2,18},{18,2},{3,19},{19,3},{4,20},{20... | collective-permute-start | bytes 6291464 | tf_op jit(solution)/shard_map/ppermute | solution.py:157
  26.3 44.2 %copy-start = (bf16[4,4096,64]{1,2,0:T(8,128)(2,1)S(1)}, bf16[4,4096,64]{1,2,0:T(8,128)(2,1)}, u32[]{:S(2)}) copy-start(bf16[4,4096,64]{1,2,0:T(8,128)(2,1)} %param.9) | copy-start | bytes 6291460
  26.4 42.4 %collective-permute-start.5 = (bf16[64,4608]{1,0:T(8,128)(2,1)}, bf16[64,4608]{1,0:T(8,128)(2,1)}, u32[]{:S(2)}, u32[]{:S(2)}) collective-permute-start(bf16[64,4608]{1,0:T(8,128)(2,1)} %get-tuple-element.33), channel_id=1, source_target_pairs={{0,10},{2,8},{4,14},{6,12},{8,2},{10,0},{12,6},{14,4},{16,30},{18,... | collective-permute-start | bytes 1769480 | tf_op jit(solution)/shard_map/ppermute | solution.py:154
  58.3 9.3 %collective-permute-start.4 = (bf16[128,512]{1,0:T(8,128)(2,1)S(1)}, bf16[128,512]{1,0:T(8,128)(2,1)S(1)}, u32[]{:S(2)}, u32[]{:S(2)}) collective-permute-start(bf16[128,512]{1,0:T(8,128)(2,1)S(1)} %pad_maximum_fusion), channel_id=1, source_target_pairs={{0,16},{16,0},{1,17},{17,1},{2,18},{18,2},{3,19},{19,3},{4,20},{20... | collective-permute-start | bytes 393224 | tf_op jit(solution)/shard_map/ppermute | solution.py:157
  58.4 9.0 %collective-permute-start.1 = (s32[1,8]{1,0:T(1,128)S(1)}, s32[1,8]{1,0:T(1,128)S(1)}, u32[]{:S(2)}, u32[]{:S(2)}) collective-permute-start(s32[1,8]{1,0:T(1,128)S(1)} %copy-done.4), channel_id=1, source_target_pairs={{0,16},{16,0},{1,17},{17,1},{2,18},{18,2},{3,19},{19,3},{4,20},{20... | collective-permute-start | bytes 104 | tf_op jit(solution)/shard_map/ppermute | solution.py:157
  67.6 0.7 copy-start.3
  69.6 7.2 %collective-permute-start.7 = (bf16[64,512]{1,0:T(8,128)(2,1)S(1)}, bf16[64,512]{1,0:T(8,128)(2,1)S(1)}, u32[]{:S(2)}, u32[]{:S(2)}) collective-permute-start(bf16[64,512]{1,0:T(8,128)(2,1)S(1)} %slice.34), channel_id=1, source_target_pairs={{0,16},{16,0},{1,17},{17,1},{2,18},{18,2},{3,19},{19,3},{4,20},{20... | collective-permute-start | bytes 196616 | tf_op jit(solution)/shard_map/ppermute | solution.py:157
  76.8 7.6 %copy-start.2 = (f32[256,512]{1,0:T(8,128)S(1)}, f32[256,512]{1,0:T(8,128)}, u32[]{:S(2)}) copy-start(f32[256,512]{1,0:T(8,128)} %reduce-scatter.2.cloned.1.call-done) | copy-start | bytes 1572868
  76.8 1.4 %collective-permute-start.8 = (f32[64,512]{1,0:T(8,128)S(1)}, f32[64,512]{1,0:T(8,128)S(1)}, u32[]{:S(2)}, u32[]{:S(2)}) collective-permute-start(f32[64,512]{1,0:T(8,128)S(1)} %shard_map.74), channel_id=1, source_target_pairs={{0,1},{1,0},{2,3},{3,2},{4,5},{5,4},{6,7},{7,6},{8,9},{9,8},{10,11... | collective-permute-start | bytes 393224 | tf_op jit(solution)/shard_map/ppermute | solution.py:161
  78.3 4.3 %collective-permute-start.9 = (f32[64,256]{1,0:T(8,128)S(1)}, f32[64,256]{1,0:T(8,128)S(1)}, u32[]{:S(2)}, u32[]{:S(2)}) collective-permute-start(f32[64,256]{1,0:T(8,128)S(1)} %slice.43), channel_id=1, source_target_pairs={{0,16},{16,0},{1,17},{17,1},{2,18},{18,2},{3,19},{19,3},{4,20},{20... | collective-permute-start | bytes 196616 | tf_op jit(solution)/shard_map/ppermute | solution.py:157
Sparse Core Ops, SparseCore 0:
  26.5 6.6 reduce-scatter.1

commit v11 on v9

--- a/solution.py
+++ b/solution.py
@@ -61,6 +61,78 @@
     )
 
 
+def score_kernel(plan, rows_of, chunks, has_prior, scalars, row_steps, *refs):
+    prior = refs[0] if has_prior else None
+    refs = refs[1:] if has_prior else refs
+    sets = len(plan)
+    count_panels = len(refs) - sets - 4
+    tokens, panels = refs[:sets], refs[sets : sets + count_panels]
+    out, held_tokens, held_panels, sems = refs[sets + count_panels :]
+    rank, count = out.shape[0], held_tokens.shape[1]
+    width = held_tokens.shape[2] // chunks
+    copies = []
+    for c in range(chunks):
+        cols = pl.ds(c * width, width)
+        pairs = []
+        for n, ref in enumerate(panels):
+            source = ref.at[:, cols] if len(ref.shape) == 2 else ref.at[scalars[0], :, cols]
+            pairs.append((source, held_panels.at[pl.ds(n * rank, rank), cols]))
+        pairs += [(ref.at[:, cols], held_tokens.at[n, :, cols]) for n, ref in enumerate(tokens)]
+        copies.append([])
+        for n, (source, target) in enumerate(pairs):
+            copies[-1].append(pltpu.make_async_copy(source, target, sems.at[c, n]))
+            copies[-1][-1].start()
+    sums = [None] * sets
+    for c in range(chunks):
+        for copy in copies[c]:
+            copy.wait()
+        cols = pl.ds(c * width, width)
+        for t, used in enumerate(plan):
+            product = lax.dot_general(
+                held_panels[pl.ds(used[0] * rank, len(used) * rank), cols],
+                held_tokens[t, :, cols],
+                (((1,), (1,)), ((), ())),
+                preferred_element_type=jnp.float32,
+            )
+            sums[t] = product if c == 0 else sums[t] + product
+    for t, used in enumerate(plan):
+        mine = row_steps[pl.ds(rows_of[t], 1), :]
+        total = prior[...] if has_prior and t == 0 else jnp.zeros((rank, count), jnp.float32)
+        for n, panel in enumerate(used):
+            term = sums[t][n * rank : (n + 1) * rank]
+            total = total + jnp.where(mine == scalars[1 + panel], term, 0.0)
+        out[:, pl.ds(t * count, count)] = total
+
+
+def score(plan, rows_of, tokens_of, panels, scalars, row_steps, prior=None):
+    count, depth = tokens_of[0].shape
+    rank = panels[0].shape[0]
+    chunks = 4
+    shape = (rank, len(plan) * count)
+    prior = [] if prior is None else [prior]
+    whole = pl.BlockSpec(memory_space=pltpu.VMEM)
+    copied = len(tokens_of) + len(panels)
+    return pl.pallas_call(
+        functools.partial(score_kernel, plan, rows_of, chunks, bool(prior)),
+        out_shape=jax.ShapeDtypeStruct(shape, jnp.float32),
+        in_specs=[pl.BlockSpec(memory_space=pltpu.SMEM)]
+        + [whole] * (1 + len(prior))
+        + [pl.BlockSpec(memory_space=pl.ANY)] * copied,
+        out_specs=whole,
+        scratch_shapes=[
+            pltpu.VMEM((len(tokens_of), count, depth), tokens_of[0].dtype),
+            pltpu.VMEM((len(panels) * rank, depth), tokens_of[0].dtype),
+            pltpu.SemaphoreType.DMA((chunks, copied)),
+        ],
+        compiler_params=pltpu.CompilerParams(vmem_limit_bytes=40 << 20),
+        cost_estimate=pl.CostEstimate(
+            flops=2 * depth * count * rank * sum(len(used) for used in plan),
+            bytes_accessed=2 * depth * (len(plan) * count + len(panels) * rank),
+            transcendentals=0,
+        ),
+    )(scalars, row_steps, *prior, *tokens_of, *panels)
+
+
 def on_device(tokens, base_weight, shrink_panels, expand_panels, adapter_home, fetch_list, seg_len):
     per_home, depth, _ = shrink_panels.shape
     replicas, parts, cores = lax.axis_size("rep"), lax.axis_size("parts"), lax.axis_size("tp")
@@ -104,17 +176,18 @@
     tokens, send = tie((tokens, send))
     recv = [hop(x, group) for x, group in zip(send, groups)]
     tokens_of = [tokens] + [shift_parts(tokens, shift) for shift in range(1, parts)]
+    solo_recv = recv[len(far) + len(near) :]
+    base_weight, fetch_list, seg_len, solo_recv = tie((base_weight, fetch_list, seg_len, solo_recv))
     base_part = jnp.dot(tokens, base_weight, preferred_element_type=jnp.float32)
+    base_part, recv[: len(far) - 1] = tie((base_part, recv[: len(far) - 1]))
     base = lax.psum_scatter(base_part, "tp", scatter_dimension=1, tiled=True)
 
     stored = jnp.take(adapter_home, lax.dynamic_index_in_dim(fetch_list, me, 0, keepdims=False))
     steps = (stored // per_home) ^ me
     slot = jnp.sum(jnp.where(steps == 0, stored % per_home, 0))
-    own = lax.dynamic_index_in_dim(panels, slot, 0, keepdims=False)
     left = lax.axis_index("tp") * columns
     own_expand = lax.dynamic_slice(expand_panels, (slot, 0, left), (1, rank, columns))[0]
     far_recv, near_recv = recv[: len(far)], recv[len(far) : len(far) + len(near)]
-    solo_recv = recv[len(far) + len(near) :]
     early, early_groups = near_recv + far_recv[:-1], near + far[:-1]
 
     def step_of(group, shift=0):
@@ -133,7 +206,6 @@
 
     lengths_of = [seg_len[0]]
     for shift in range(1, parts):
-        seg_len, tokens_of[shift] = tie((seg_len, tokens_of[shift]))
         lengths_of.append(shift_parts(seg_len, shift)[0])
     rows = jnp.arange(tok_count, dtype=jnp.int32)
 
@@ -143,45 +215,52 @@
         member = (rows[:, None] >= starts[None, :]) & (rows[:, None] < (starts + lengths)[None, :])
         return jnp.sum(jnp.where(member, steps[None, :], 0), axis=1)[None, :]
 
-    row_steps = [steps_of_rows(lengths) for lengths in lengths_of]
-
-    def score(block, step, shift):
-        product = lax.dot_general(
-            block[:, :depth],
-            tokens_of[shift],
-            (((1,), (1,)), ((), ())),
-            preferred_element_type=jnp.float32,
-        )
-        return jnp.where(row_steps[shift] == step, product, 0.0)
-
-    scores = [score(own, 0, 0)] + [0.0] * (parts - 1)
-    for block, group in zip(solo_recv, solo):
-        scores[0] = scores[0] + score(block, group[0], 0)
-    for block, group in zip(early, early_groups):
-        for shift in range(parts):
-            scores[shift] = scores[shift] + score(block, step_of(group), shift)
-    tokens_of, scores, expand, base, far_recv[-1] = tie(
-        (tokens_of, scores, expand, base, far_recv[-1])
-    )
+    row_steps = jnp.concatenate([steps_of_rows(lengths) for lengths in lengths_of], axis=0)
+
+    slot_and = lambda values: jnp.stack([slot] + [jnp.int32(value) for value in values])
+    early_steps = [step_of(group) for group in early_groups]
+    alone_steps = [group[0] for group in solo] + [0]
+    first = score(
+        [tuple(range(len(early) + len(solo) + 1))],
+        [0],
+        [tokens],
+        early + solo_recv + [panels],
+        slot_and(early_steps + alone_steps),
+        row_steps[:1],
+    )
+    row_steps, expand, base, first, tokens_of[1:], far_recv[-1] = tie(
+        (row_steps, expand, base, first, tokens_of[1:], far_recv[-1])
+    )
+    scores = score(
+        [(0,)] + [tuple(range(len(early) + 1))] * (parts - 1),
+        list(range(parts)),
+        tokens_of,
+        [far_recv[-1]] + early,
+        slot_and([step_of(far[-1])] + early_steps),
+        row_steps,
+        first,
+    )
+    scores, far_recv[-1] = tie((scores, far_recv[-1]))
     last_expand = far_recv[-1][:, depth:]
     expands = [expand, last_expand] + [shift_parts(last_expand, shift) for shift in range(1, parts)]
     expand_steps += [step_of(far[-1], shift) for shift in range(parts)]
-    for shift in range(parts):
-        scores[shift] = scores[shift] + score(far_recv[-1], step_of(far[-1]), shift)
-    scores, expands = tie((scores, expands))
-    scores = trade(jnp.concatenate(scores, axis=1))
+    scores = trade(scores)
     shrink = scores[:, :tok_count]
     for shift in range(1, parts):
         shrink = shrink + shift_parts(scores[:, shift * tok_count : (shift + 1) * tok_count], -shift)
+    high = lax.reduce_precision(shrink, 8, 7)
+    terms = [high.astype(jnp.bfloat16), (shrink - high).astype(jnp.bfloat16)]
     wide = jnp.concatenate(
-        [jnp.where(row_steps[0] == step, shrink, 0.0) for step in expand_steps], axis=0
-    )
+        [
+            jnp.where(row_steps[:1] == step, term, jnp.zeros((), jnp.bfloat16))
+            for term in terms
+            for step in expand_steps
+        ],
+        axis=0,
+    )
+    expand = jnp.concatenate(expands * 2, axis=0)
     lora = lax.dot_general(
-        wide,
-        jnp.concatenate(expands, axis=0).astype(jnp.float32),
-        (((0,), (0,)), ((), ())),
-        precision=lax.Precision.HIGHEST,
-        preferred_element_type=jnp.float32,
+        wide, expand, (((0,), (0,)), ((), ())), preferred_element_type=jnp.float32
     )
     return (base + adapter_scale * lora).astype(jnp.bfloat16)
 

time: 102 us -> 99 us (0.971)
  waiting for transfers between devices: 38.8 us -> 17.9 us
  starting transfers between devices: 13.6 us -> 28.9 us
  matrix products: 21.5 us -> 7.93 us
  local copies, waits for them, and re-layouts: 3.27 us -> 11.1 us
  Pallas kernels: 4.11 us -> 11.6 us
  other arithmetic: 4.01 us -> 5.49 us
    ppermute x5, starting transfers between devices: 5.3 us -> 21.4 us  [shift_parts(): lax.ppermute(x, 'parts', [(i, (i + shift) % parts) for i in range(parts)])]
    dot_general x9 -> x1, matrix products: 14.8 us -> 0.45 us  [on_device(): lax.dot_general(wide, expand, (((0,), (0,)), ((), ())), preferred_element...]
    ppermute x4, waiting for transfers between devices: 24.3 us -> 10.6 us  [hop(): return lax.ppermute(x, ('parts', 'rep'), pairs)]
    pallas_call x0 -> x2, Pallas kernels: none -> 7.44 us  [score(): pl.pallas_call(functools.partial(score_kernel, plan, rows_of, chunks, boo...]
    ppermute x5, waiting for transfers between devices: 13.1 us -> 7.25 us  [shift_parts(): lax.ppermute(x, 'parts', [(i, (i + shift) % parts) for i in range(parts)])]
    unnamed x15 -> x18, local copies, waits for them, and re-layouts: 1.74 us -> 6.96 us
    ppermute x1, waiting for transfers between devices: 1.33 us -> 0.01 us  [trade(): lax.ppermute(x, 'tp', [(i, (i + shift) % cores) for i in range(cores)])]
  transfers between devices with their start and end apart: 11 -> 11, of which waited for: 6 -> 5; matrix products, arithmetic and copies ran while one was open for 27% -> 22% of each run, Pallas kernels for 0% -> 4%
where the time goes in v11:
time: 99 us; the launch traced here: 98.3 us
  starting transfers between devices  28.9 us (29%)
  waiting for transfers between devices  17.9 us (18%)
  between operations  15.5 us (16%)
  Pallas kernels  11.6 us (12%)
  local copies, waits for them, and re-layouts  11.1 us (11%)
  matrix products  7.93 us (8%)
  other arithmetic  5.49 us (6%)
    ppermute x5, starting transfers between devices, shift_parts(): lax.ppermute(x, 'parts', [(i, (i + shift) % parts) for i in range(parts)])  21.4 us
    ppermute x4, waiting for transfers between devices, hop(): return lax.ppermute(x, ('parts', 'rep'), pairs)  10.6 us
    dot_general x1, matrix products, on_device(): base_part = jnp.dot(tokens, base_weight, preferred_element_type=jnp.float32)  7.47 us
    pallas_call x2, Pallas kernels, score(): pl.pallas_call(functools.partial(score_kernel, plan, rows_of, chunks, boo...  7.44 us
    ppermute x4, starting transfers between devices, hop(): return lax.ppermute(x, ('parts', 'rep'), pairs)  7.4 us
    ppermute x5, waiting for transfers between devices, shift_parts(): lax.ppermute(x, 'parts', [(i, (i + shift) % parts) for i in range(parts)])  7.25 us
    unnamed x18, local copies, waits for them, and re-layouts  6.96 us
    pallas_call x1, Pallas kernels, pack(): pl.pallas_call(functools.partial(pack_kernel, blocks), out_shape=[jax.Sha...  4.11 us
  transfers between devices with their start and end apart: 11, of which 5 were waited for; matrix products, arithmetic and copies ran while one was open for 22% of the time, Pallas kernels for 4%

profile of v11, /device:TPU:0, one launch (start us, length us, event | category | flops | bytes accessed | tf_op | source)
XLA Modules:
  0.0 98.3 jit_solution(12111656888980720144)
XLA Ops:
  6.5 4.1 %shard_map.73 = (bf16[64,4608]{1,0:T(8,128)(2,1)}, bf16[64,4608]{1,0:T(8,128)(2,1)}, bf16[64,4608]{1,0:T(8,128)(2,1)}, bf16[64,4608]{1,0:T(8,128)(2,1)}) custom-call(s32[32]{0:T(128)} %home_ref.1, s32[8,8]{1,0:T(8,128)} %fetch_ref.1, bf16[4,64,4096]{2,1,0:T(8,128)(2,1)} %bitcast.41, bf16[4,64,1024]{2,1,0:T(8,128)(2,1)} %expand_ref.1), custom_call_target="tpu_custom_call" | custom-call | bytes 4718592 | tf_op jit(solution)/shard_map/pallas_call | solution.py:50
  10.7 3.0 %collective-permute-start = (bf16[64,4608]{1,0:T(8,128)(2,1)}, bf16[64,4608]{1,0:T(8,128)(2,1)S(1)}, u32[]{:S(2)}, u32[]{:S(2)}) collective-permute-start(bf16[64,4608]{1,0:T(8,128)(2,1)} %get-tuple-element.32), channel_id=1, source_target_pairs={{0,2},{2,0},{4,6},{6,4},{8,10},{10,8},{12,14},{14,12},{16,18},{18,... | collective-permute-start | bytes 1769480 | tf_op jit(solution)/shard_map/ppermute | solution.py:162
  13.6 1.6 %collective-permute-start.2 = (bf16[64,4608]{1,0:T(8,128)(2,1)}, bf16[64,4608]{1,0:T(8,128)(2,1)S(1)}, u32[]{:S(2)}, u32[]{:S(2)}) collective-permute-start(bf16[64,4608]{1,0:T(8,128)(2,1)} %get-tuple-element.36), channel_id=1, source_target_pairs={{0,4},{2,6},{4,0},{6,2},{8,12},{10,14},{12,8},{14,10},{16,22},{18,... | collective-permute-start | bytes 1769480 | tf_op jit(solution)/shard_map/ppermute | solution.py:162
  15.2 2.5 %collective-permute-start.3 = (bf16[64,4608]{1,0:T(8,128)(2,1)}, bf16[64,4608]{1,0:T(8,128)(2,1)S(1)}, u32[]{:S(2)}, u32[]{:S(2)}) collective-permute-start(bf16[64,4608]{1,0:T(8,128)(2,1)} %get-tuple-element.39), channel_id=1, source_target_pairs={{0,8},{2,10},{4,12},{6,14},{8,0},{10,2},{12,4},{14,6},{16,28},{18,... | collective-permute-start | bytes 1769480 | tf_op jit(solution)/shard_map/ppermute | solution.py:162
  18.1 3.3 %collective-permute-start.5 = (bf16[256,4096]{1,0:T(8,128)(2,1)}, bf16[256,4096]{1,0:T(8,128)(2,1)}, u32[]{:S(2)}, u32[]{:S(2)}) collective-permute-start(bf16[256,4096]{1,0:T(8,128)(2,1)} %refs_1_), channel_id=1, source_target_pairs={{0,16},{16,0},{1,17},{17,1},{2,18},{18,2},{3,19},{19,3},{4,20},{20... | collective-permute-start | bytes 6291464 | tf_op jit(solution)/shard_map/ppermute | solution.py:165
  21.4 5.7 %collective-permute-done.refs_3_ = bf16[64,4608]{1,0:T(8,128)(2,1)S(1)} collective-permute-done((bf16[64,4608]{1,0:T(8,128)(2,1)}, bf16[64,4608]{1,0:T(8,128)(2,1)S(1)}, u32[]{:S(2)}, u32[]{:S(2)}) %collective-permute-start) | collective-permute-done | bytes 589856 | tf_op jit(solution)/shard_map/ppermute | solution.py:162
  27.2 0.7 fusion.3
  27.9 0.6 gather_fusion
  28.5 1.4 %fusion.6 = s32[]{:T(128)} fusion(s32[8]{0:T(128)S(1)} %gather_fusion, s32[]{:T(128)S(6)} %axis_index.33, s32[8,8]{1,0:T(8,128)} %fetch_ref.1, s32[]{:T(128)S(6)} %select_n.161), kind=kLoop, calls=%fused_computation.77 | loop fusion | flops 239 | bytes 76 | tf_op jit(solution)/shard_map/reduce_sum | solution.py:187
  31.2 14.4 %collective-permute-start.1 = (s32[1,8]{1,0:T(1,128)S(1)}, s32[1,8]{1,0:T(1,128)S(1)}, u32[]{:S(2)}, u32[]{:S(2)}) collective-permute-start(s32[1,8]{1,0:T(1,128)S(1)} %copy-done.5), channel_id=1, source_target_pairs={{0,16},{16,0},{1,17},{17,1},{2,18},{18,2},{3,19},{19,3},{4,20},{20... | collective-permute-start | bytes 104 | tf_op jit(solution)/shard_map/ppermute | solution.py:165
  45.6 7.5 %fusion.11 = f32[256,1024]{1,0:T(8,128)} fusion(bf16[256,4096]{1,0:T(8,128)(2,1)} %refs_1_, bf16[4096,1024]{1,0:T(8,128)(2,1)} %param.8), kind=kOutput, calls=%fused_computation.83 | convolution fusion | flops 2147483648 | bytes 11534336 | tf_op jit(solution)/shard_map/dot_general | solution.py:181
  53.0 4.8 %collective-permute-done.3.refs_2_.refs_5_ = bf16[64,4608]{1,0:T(8,128)(2,1)S(1)} collective-permute-done((bf16[64,4608]{1,0:T(8,128)(2,1)}, bf16[64,4608]{1,0:T(8,128)(2,1)S(1)}, u32[]{:S(2)}, u32[]{:S(2)}) %collective-permute-start.3) | collective-permute-done | bytes 589856 | tf_op jit(solution)/shard_map/ppermute | solution.py:162
  58.5 1.5 %bitcast_dynamic-update-slice_fusion = bf16[384,512]{1,0:T(8,128)(2,1)} fusion(bf16[4,64,1024]{2,1,0:T(8,128)(2,1)} %expand_ref.1, s32[]{:T(128)S(6)} %select_n.174, s32[]{:T(128)S(6)} %select_n.175), kind=kLoop, calls=%fused_computation.8 | loop fusion | bytes 131080
  60.0 1.5 %slice_dynamic-update-slice_fusion = bf16[384,512]{1,0:T(8,128)(2,1)} fusion(bf16[384,512]{1,0:T(8,128)(2,1)} %bitcast_dynamic-update-slice_fusion, bf16[64,4608]{1,0:T(8,128)(2,1)} %copy-done.1), kind=kLoop, calls=%fused_computation.9 | loop fusion | bytes 131072
  62.7 0.7 pad_maximum_fusion
  63.4 0.7 stack.24.scalars
  64.1 0.7 pad_add_fusion.1.scalars
  64.9 0.7 fusion.5
  65.6 2.0 %collective-permute-done.1 = s32[1,8]{1,0:T(1,128)S(1)} collective-permute-done((s32[1,8]{1,0:T(1,128)S(1)}, s32[1,8]{1,0:T(1,128)S(1)}, u32[]{:S(2)}, u32[]{:S(2)}) %collective-permute-start.1) | collective-permute-done | bytes 64 | tf_op jit(solution)/shard_map/ppermute | solution.py:165
  67.9 1.1 %copy-done.2 = bf16[64,4608]{1,0:T(8,128)(2,1)S(1)} copy-done((bf16[64,4608]{1,0:T(8,128)(2,1)S(1)}, bf16[64,4608]{1,0:T(8,128)(2,1)}, u32[]{:S(2)}) %copy-start.2) | copy-done | bytes 589848
  68.9 3.6 %shard_map.74.refs_0_ = f32[64,256]{1,0:T(8,128)S(1)} custom-call(s32[5]{0:T(128)S(1)} %stack.24.scalars, s32[1,256]{1,0:T(1,128)S(1)} %bitcast.43, bf16[256,4096]{1,0:T(8,128)(2,1)} %refs_1_, bf16[64,4608]{1,0:T(8,128)(2,1)S(1)} %collective-permute-done.2.refs_1_.refs_4_, bf16[64,4608]{1,0:T(8,128)(2,1)S(1)} %collective-permute-done.3.refs_2_.refs_5_, ...), custom_call_target="tpu_custom_call" | custom-call | flops 536870912 | bytes 4194304 | tf_op jit(solution)/shard_map/pallas_call | solution.py:115
  72.5 0.7 constant_dynamic-update-slice_fusion
  73.2 3.9 %shard_map.75 = f32[64,512]{1,0:T(8,128)S(1)} custom-call(s32[4]{0:T(128)S(1)} %pad_add_fusion.1.scalars, s32[2,256]{1,0:T(2,128)S(1)} %pad_add_fusion.row_steps, f32[64,256]{1,0:T(8,128)S(1)} %shard_map.74.refs_0_, bf16[256,4096]{1,0:T(8,128)(2,1)} %refs_1_, bf16[256,4096]{1,0:T(8,128)(2,1)} %collective-permute-done.5.refs_2_, ...), custom_call_target="tpu_custom_call" | custom-call | flops 536870912 | bytes 5767168 | tf_op jit(solution)/shard_map/pallas_call | solution.py:115
  77.2 1.0 %constant_dynamic-update-slice_fusion.24 = bf16[1024,512]{1,0:T(8,128)(2,1)S(1)} fusion(bf16[384,512]{1,0:T(8,128)(2,1)} %constant_dynamic-update-slice_fusion), kind=kLoop, calls=%fused_computation.34 | loop fusion | bytes 786432
  78.2 0.9 fusion.8
  79.0 1.8 %collective-permute-start.9 = (bf16[64,512]{1,0:T(8,128)(2,1)S(1)}, bf16[64,512]{1,0:T(8,128)(2,1)S(1)}, u32[]{:S(2)}, u32[]{:S(2)}) collective-permute-start(bf16[64,512]{1,0:T(8,128)(2,1)S(1)} %get-tuple-element.65), channel_id=1, source_target_pairs={{0,16},{16,0},{1,17},{17,1},{2,18},{18,2},{3,19},{19,3},{4,20},{20... | collective-permute-start | bytes 196616 | tf_op jit(solution)/shard_map/ppermute | solution.py:165
  80.9 2.7 %collective-permute-done.9 = bf16[64,512]{1,0:T(8,128)(2,1)S(1)} collective-permute-done((bf16[64,512]{1,0:T(8,128)(2,1)S(1)}, bf16[64,512]{1,0:T(8,128)(2,1)S(1)}, u32[]{:S(2)}, u32[]{:S(2)}) %collective-permute-start.9) | collective-permute-done | bytes 65568 | tf_op jit(solution)/shard_map/ppermute | solution.py:165
  83.6 1.0 %constant_dynamic-update-slice_fusion.21 = bf16[1024,512]{1,0:T(8,128)(2,1)S(1)} fusion(bf16[1024,512]{1,0:T(8,128)(2,1)S(1)} %constant_dynamic-update-slice_fusion.22, bf16[384,512]{1,0:T(8,128)(2,1)} %constant_dynamic-update-slice_fusion), kind=kLoop, calls=%fused_computation.31 | loop fusion | bytes 786432
  84.6 0.9 constant_dynamic-update-slice_fusion.20
  85.6 1.8 %collective-permute-start.8 = (f32[64,256]{1,0:T(8,128)S(1)}, f32[64,256]{1,0:T(8,128)S(1)}, u32[]{:S(2)}, u32[]{:S(2)}) collective-permute-start(f32[64,256]{1,0:T(8,128)S(1)} %slice.49), channel_id=1, source_target_pairs={{0,16},{16,0},{1,17},{17,1},{2,18},{18,2},{3,19},{19,3},{4,20},{20... | collective-permute-start | bytes 196616 | tf_op jit(solution)/shard_map/ppermute | solution.py:165
  87.4 2.5 %collective-permute-done.8 = f32[64,256]{1,0:T(8,128)S(1)} collective-permute-done((f32[64,256]{1,0:T(8,128)S(1)}, f32[64,256]{1,0:T(8,128)S(1)}, u32[]{:S(2)}, u32[]{:S(2)}) %collective-permute-start.8) | collective-permute-done | bytes 65568 | tf_op jit(solution)/shard_map/ppermute | solution.py:165
  90.7 0.8 add_convert_fusion
  (52 shorter events, 2.7 us)
Async XLA Ops:
  6.5 21.3 %copy-start.3 = (s32[32]{0:T(128)S(1)}, s32[32]{0:T(128)}, u32[]{:S(2)}) copy-start(s32[32]{0:T(128)} %home_ref.1) | copy-start | bytes 388
  6.5 24.6 %copy-start.5 = (s32[1,8]{1,0:T(1,128)S(1)}, s32[1,8]{1,0:T(1,128)}, u32[]{:S(2)}) copy-start(s32[1,8]{1,0:T(1,128)} %param.13) | copy-start | bytes 100
  6.5 66.6 %reduce-scatter.2.cloned.1.call-start = ((), (), s32[]{:S(2)}) async-start(), calls=%async_computation.1 | async-start | bytes 1572864 | tf_op jit(solution)/shard_map/reduce_scatter | solution.py:183
  10.7 16.5 %collective-permute-start = (bf16[64,4608]{1,0:T(8,128)(2,1)}, bf16[64,4608]{1,0:T(8,128)(2,1)S(1)}, u32[]{:S(2)}, u32[]{:S(2)}) collective-permute-start(bf16[64,4608]{1,0:T(8,128)(2,1)} %get-tuple-element.32), channel_id=1, source_target_pairs={{0,2},{2,0},{4,6},{6,4},{8,10},{10,8},{12,14},{14,12},{16,18},{18,... | collective-permute-start | bytes 1769480 | tf_op jit(solution)/shard_map/ppermute | solution.py:162
  13.6 47.9 %collective-permute-start.2 = (bf16[64,4608]{1,0:T(8,128)(2,1)}, bf16[64,4608]{1,0:T(8,128)(2,1)S(1)}, u32[]{:S(2)}, u32[]{:S(2)}) collective-permute-start(bf16[64,4608]{1,0:T(8,128)(2,1)} %get-tuple-element.36), channel_id=1, source_target_pairs={{0,4},{2,6},{4,0},{6,2},{8,12},{10,14},{12,8},{14,10},{16,22},{18,... | collective-permute-start | bytes 1769480 | tf_op jit(solution)/shard_map/ppermute | solution.py:162
  15.2 42.7 %collective-permute-start.3 = (bf16[64,4608]{1,0:T(8,128)(2,1)}, bf16[64,4608]{1,0:T(8,128)(2,1)S(1)}, u32[]{:S(2)}, u32[]{:S(2)}) collective-permute-start(bf16[64,4608]{1,0:T(8,128)(2,1)} %get-tuple-element.39), channel_id=1, source_target_pairs={{0,8},{2,10},{4,12},{6,14},{8,0},{10,2},{12,4},{14,6},{16,28},{18,... | collective-permute-start | bytes 1769480 | tf_op jit(solution)/shard_map/ppermute | solution.py:162
  17.8 55.4 %collective-permute-start.6 = (bf16[64,4608]{1,0:T(8,128)(2,1)}, bf16[64,4608]{1,0:T(8,128)(2,1)}, u32[]{:S(2)}, u32[]{:S(2)}) collective-permute-start(bf16[64,4608]{1,0:T(8,128)(2,1)} %get-tuple-element.42), channel_id=1, source_target_pairs={{0,10},{2,8},{4,14},{6,12},{8,2},{10,0},{12,6},{14,4},{16,30},{18,... | collective-permute-start | bytes 1769480 | tf_op jit(solution)/shard_map/ppermute | solution.py:162
  18.1 55.1 %collective-permute-start.5 = (bf16[256,4096]{1,0:T(8,128)(2,1)}, bf16[256,4096]{1,0:T(8,128)(2,1)}, u32[]{:S(2)}, u32[]{:S(2)}) collective-permute-start(bf16[256,4096]{1,0:T(8,128)(2,1)} %refs_1_), channel_id=1, source_target_pairs={{0,16},{16,0},{1,17},{17,1},{2,18},{18,2},{3,19},{19,3},{4,20},{20... | collective-permute-start | bytes 6291464 | tf_op jit(solution)/shard_map/ppermute | solution.py:165
  27.2 4.0 %copy-start.1 = (bf16[64,4608]{1,0:T(8,128)(2,1)}, bf16[64,4608]{1,0:T(8,128)(2,1)S(1)}, u32[]{:S(2)}) copy-start(bf16[64,4608]{1,0:T(8,128)(2,1)S(1)} %collective-permute-done.refs_3_) | copy-start | bytes 1769476
  31.2 36.5 %collective-permute-start.1 = (s32[1,8]{1,0:T(1,128)S(1)}, s32[1,8]{1,0:T(1,128)S(1)}, u32[]{:S(2)}, u32[]{:S(2)}) collective-permute-start(s32[1,8]{1,0:T(1,128)S(1)} %copy-done.5), channel_id=1, source_target_pairs={{0,16},{16,0},{1,17},{17,1},{2,18},{18,2},{3,19},{19,3},{4,20},{20... | collective-permute-start | bytes 104 | tf_op jit(solution)/shard_map/ppermute | solution.py:165
  45.6 22.3 %copy-start = (bf16[4,4096,64]{1,2,0:T(8,128)(2,1)S(1)}, bf16[4,4096,64]{1,2,0:T(8,128)(2,1)}, u32[]{:S(2)}) copy-start(bf16[4,4096,64]{1,2,0:T(8,128)(2,1)} %param.9) | copy-start | bytes 6291460
  63.4 9.1 %collective-permute-start.4 = (bf16[128,512]{1,0:T(8,128)(2,1)}, bf16[128,512]{1,0:T(8,128)(2,1)S(1)}, u32[]{:S(2)}, u32[]{:S(2)}) collective-permute-start(bf16[128,512]{1,0:T(8,128)(2,1)} %pad_maximum_fusion), channel_id=1, source_target_pairs={{0,16},{16,0},{1,17},{17,1},{2,18},{18,2},{3,19},{19,3},{4,20},{20... | collective-permute-start | bytes 393224 | tf_op jit(solution)/shard_map/ppermute | solution.py:165
  67.9 1.1 %copy-start.2 = (bf16[64,4608]{1,0:T(8,128)(2,1)S(1)}, bf16[64,4608]{1,0:T(8,128)(2,1)}, u32[]{:S(2)}) copy-start(bf16[64,4608]{1,0:T(8,128)(2,1)} %copy-done.1) | copy-start | bytes 1769476
  77.1 8.5 %collective-permute-start.7 = (f32[64,512]{1,0:T(8,128)S(1)}, f32[64,512]{1,0:T(8,128)S(1)}, u32[]{:S(2)}, u32[]{:S(2)}) collective-permute-start(f32[64,512]{1,0:T(8,128)S(1)} %shard_map.75), channel_id=1, source_target_pairs={{0,1},{1,0},{2,3},{3,2},{4,5},{5,4},{6,7},{7,6},{8,9},{9,8},{10,11... | collective-permute-start | bytes 393224 | tf_op jit(solution)/shard_map/ppermute | solution.py:169
  79.0 4.6 %collective-permute-start.9 = (bf16[64,512]{1,0:T(8,128)(2,1)S(1)}, bf16[64,512]{1,0:T(8,128)(2,1)S(1)}, u32[]{:S(2)}, u32[]{:S(2)}) collective-permute-start(bf16[64,512]{1,0:T(8,128)(2,1)S(1)} %get-tuple-element.65), channel_id=1, source_target_pairs={{0,16},{16,0},{1,17},{17,1},{2,18},{18,2},{3,19},{19,3},{4,20},{20... | collective-permute-start | bytes 196616 | tf_op jit(solution)/shard_map/ppermute | solution.py:165
  84.6 6.1 %copy-start.4 = (f32[256,512]{1,0:T(8,128)S(1)}, f32[256,512]{1,0:T(8,128)}, u32[]{:S(2)}) copy-start(f32[256,512]{1,0:T(8,128)} %reduce-scatter.2.cloned.1.call-done) | copy-start | bytes 1572868
  85.6 4.3 %collective-permute-start.8 = (f32[64,256]{1,0:T(8,128)S(1)}, f32[64,256]{1,0:T(8,128)S(1)}, u32[]{:S(2)}, u32[]{:S(2)}) collective-permute-start(f32[64,256]{1,0:T(8,128)S(1)} %slice.49), channel_id=1, source_target_pairs={{0,16},{16,0},{1,17},{17,1},{2,18},{18,2},{3,19},{19,3},{4,20},{20... | collective-permute-start | bytes 196616 | tf_op jit(solution)/shard_map/ppermute | solution.py:165
Sparse Core Ops, SparseCore 0:
  58.0 8.0 reduce-scatter.1

commit v12 on v11

v12 whole, which is shorter than its diff:
```python
import functools
import jax
import jax.numpy as jnp
from jax import lax
from jax.experimental import pallas as pl
from jax.experimental.pallas import tpu as pltpu
from jax.sharding import PartitionSpec as P

adapter_scale = 2.0


def by_part(values):
    part = lax.axis_index("parts")
    chosen = jnp.int32(values[0])
    for p, value in enumerate(values):
        chosen = jnp.where(part == p, value, chosen)
    return chosen


def turned(group, shift):
    return tuple(group[(p - shift) % len(group)] for p in range(len(group)))


def slot_for(peer, me, per_home, home_ref, fetch_ref):
    first = me * per_home

    def look(j, slot):
        local = home_ref[fetch_ref[peer, j]] - first
        return jnp.where((local >= 0) & (local < per_home), local, slot)

    listed = fetch_ref.shape[1]
    return lax.fori_loop(0, listed, look, jnp.int32(0), unroll=listed <= 8)


def steps_of_rows(lengths_ref, count, me, per_home, home_ref, fetch_ref):
    rows = lax.broadcasted_iota(jnp.int32, (1, count), 1)
    result = jnp.zeros((1, count), jnp.int32)
    start = jnp.int32(0)
    for j in range(fetch_ref.shape[1]):
        step = lax.div(home_ref[fetch_ref[me, j]], jnp.int32(per_home)) ^ me
        result = jnp.where(rows >= start, step, result)
        start = start + lengths_ref[0, j]
    return result


def pack_kernel(groups, home_ref, fetch_ref, shrink_ref, expand_ref, *refs):
    outs, sems = refs[:-1], refs[-1]
    me = lax.axis_index("rep")
    per_home, _, depth = shrink_ref.shape
    columns = expand_ref.shape[2] // lax.axis_size("tp")
    left = pl.multiple_of(lax.axis_index("tp") * columns, 128)
    copies = []
    for at, group in enumerate(groups):
        slot = slot_for(me ^ by_part(group), me, per_home, home_ref, fetch_ref)
        pieces = (
            (shrink_ref.at[slot], outs[at].at[:, pl.ds(0, depth)]),
            (expand_ref.at[slot, :, pl.ds(left, columns)], outs[at].at[:, pl.ds(depth, columns)]),
        )
        for n, (source, target) in enumerate(pieces):
            copies.append(pltpu.make_async_copy(source, target, sems.at[at, n]))
            copies[-1].start()
    for copy in copies:
        copy.wait()


def pack(groups, columns, adapter_home, fetch_list, panels, expand_panels):
    rank, depth = panels.shape[1:]
    shape = (rank, depth + columns)
    return list(
        pl.pallas_call(
            functools.partial(pack_kernel, groups),
            out_shape=[jax.ShapeDtypeStruct(shape, panels.dtype)] * len(groups),
            in_specs=[pl.BlockSpec(memory_space=pltpu.SMEM)] * 2 + [pl.BlockSpec(memory_space=pl.ANY)] * 2,
            out_specs=[pl.BlockSpec(memory_space=pltpu.VMEM)] * len(groups),
            scratch_shapes=[pltpu.SemaphoreType.DMA((len(groups), 2))],
            compiler_params=pltpu.CompilerParams(vmem_limit_bytes=56 << 20),
            cost_estimate=pl.CostEstimate(
                flops=0, bytes_accessed=4 * len(groups) * shape[0] * shape[1], transcendentals=0
            ),
        )(adapter_home, fetch_list, panels, expand_panels)
    )


def score_kernel(plan, groups, kept, chunks, has_prior, per_home, home_ref, fetch_ref, *refs):
    sets, many = len(plan), len(groups)
    lengths, refs = refs[:sets], refs[sets:]
    prior, refs = (refs[0], refs[1:]) if has_prior else (None, refs)
    tokens, panels = refs[:sets], refs[sets : sets + many]
    out, out_expand, held_tokens, held_panels, sems = refs[sets + many :]
    me = lax.axis_index("rep")
    rank, count, depth = out.shape[0], held_tokens.shape[1], held_tokens.shape[2]
    width = depth // chunks
    slot = slot_for(me, me, per_home, home_ref, fetch_ref)
    copies = []
    for c in range(chunks):
        cols = pl.ds(c * width, width)
        pairs = []
        for n, ref in enumerate(panels):
            source = ref.at[:, cols] if len(ref.shape) == 2 else ref.at[slot, :, cols]
            pairs.append((source, held_panels.at[pl.ds(n * rank, rank), cols]))
        pairs += [(ref.at[:, cols], held_tokens.at[n, :, cols]) for n, ref in enumerate(tokens)]
        if c == chunks - 1:
            pairs += [
                (panels[n].at[:, pl.ds(depth, out_expand.shape[1])], out_expand.at[pl.ds(i * rank, rank)])
                for i, n in enumerate(kept)
            ]
        copies.append([])
        for n, (source, target) in enumerate(pairs):
            copies[-1].append(pltpu.make_async_copy(source, target, sems.at[c, n]))
            copies[-1][-1].start()
    row_steps = [steps_of_rows(x, count, me, per_home, home_ref, fetch_ref) for x in lengths]
    sums = [None] * sets
    for c in range(chunks):
        for copy in copies[c]:
            copy.wait()
        cols = pl.ds(c * width, width)
        for t, used in enumerate(plan):
            product = lax.dot_general(
                held_panels[pl.ds(used[0] * rank, len(used) * rank), cols],
                held_tokens[t, :, cols],
                (((1,), (1,)), ((), ())),
                preferred_element_type=jnp.float32,
            )
            sums[t] = product if c == 0 else sums[t] + product
    for t, used in enumerate(plan):
        total = prior[...] if has_prior and t == 0 else jnp.zeros((rank, count), jnp.float32)
        for n, panel in enumerate(used):
            term = sums[t][n * rank : (n + 1) * rank]
            total = total + jnp.where(row_steps[t] == by_part(groups[panel]), term, 0.0)
        out[:, pl.ds(t * count, count)] = total


def score(plan, groups, kept, tables, columns, lengths_of, tokens_of, panels, prior=None):
    count, depth = tokens_of[0].shape
    per_home, rank, _ = tables[2].shape
    chunks = 4
    prior = [] if prior is None else [prior]
    smem, vmem = pl.BlockSpec(memory_space=pltpu.SMEM), pl.BlockSpec(memory_space=pltpu.VMEM)
    copied = len(tokens_of) + len(panels)
    return pl.pallas_call(
        functools.partial(score_kernel, plan, groups, kept, chunks, bool(prior), per_home),
        out_shape=[
            jax.ShapeDtypeStruct((rank, len(plan) * count), jnp.float32),
            jax.ShapeDtypeStruct((len(kept) * rank, columns), panels[0].dtype),
        ],
        in_specs=[smem] * (2 + len(lengths_of))
        + [vmem] * len(prior)
        + [pl.BlockSpec(memory_space=pl.ANY)] * copied,
        out_specs=[vmem, vmem],
        scratch_shapes=[
            pltpu.VMEM((len(tokens_of), count, depth), tokens_of[0].dtype),
            pltpu.VMEM((len(panels) * rank, depth), tokens_of[0].dtype),
            pltpu.SemaphoreType.DMA((chunks, copied + len(kept))),
        ],
        compiler_params=pltpu.CompilerParams(vmem_limit_bytes=40 << 20),
        cost_estimate=pl.CostEstimate(flops=0, bytes_accessed=0, transcendentals=0),
    )(tables[0], tables[1], *lengths_of, *prior, *tokens_of, *panels)


def base_kernel(chunks, tokens_ref, weight_ref, *refs):
    outs, (held_tokens, held_weight, sems) = refs[:-3], refs[-3:]
    cores, half = len(outs), lax.axis_index("tp")
    columns = outs[0].shape[1]
    height = tokens_ref.shape[1] // chunks
    copies = []
    for c in range(chunks):
        rows = pl.ds(c * height, height)
        pairs = [(tokens_ref.at[:, rows], held_tokens.at[:, rows])]
        for shift in range(cores):
            left = pl.multiple_of(lax.rem(half + shift, cores) * columns, 128)
            pairs.append((weight_ref.at[rows, pl.ds(left, columns)], held_weight.at[shift, rows, :]))
        copies.append([])
        for n, (source, target) in enumerate(pairs):
            copies[-1].append(pltpu.make_async_copy(source, target, sems.at[c, n]))
            copies[-1][-1].start()
    for c in range(chunks):
        for copy in copies[c]:
            copy.wait()
        rows = pl.ds(c * height, height)
        for shift, out in enumerate(outs):
            product = jnp.dot(
                held_tokens[:, rows], held_weight[shift, rows, :], preferred_element_type=jnp.float32
            )
            if c == 0:
                out[...] = product
            else:
                out[...] += product


def base_terms(tokens, weight, cores):
    count, depth = tokens.shape
    columns = weight.shape[1] // cores
    chunks = 4
    return list(
        pl.pallas_call(
            functools.partial(base_kernel, chunks),
            out_shape=[jax.ShapeDtypeStruct((count, columns), jnp.float32)] * cores,
            in_specs=[pl.BlockSpec(memory_space=pl.ANY)] * 2,
            out_specs=[pl.BlockSpec(memory_space=pltpu.VMEM)] * cores,
            scratch_shapes=[
                pltpu.VMEM((count, depth), tokens.dtype),
                pltpu.VMEM((cores, depth, columns), weight.dtype),
                pltpu.SemaphoreType.DMA((chunks, 1 + cores)),
            ],
            compiler_params=pltpu.CompilerParams(vmem_limit_bytes=40 << 20),
            cost_estimate=pl.CostEstimate(flops=0, bytes_accessed=0, transcendentals=0),
        )(tokens, weight)
    )


def finish_kernel(pieces, added, came, bases, per_home, home_ref, fetch_ref, lengths_ref, *refs):
    scores, others = refs[:added], refs[added : added + came]
    base, refs = refs[added + came : added + came + bases], refs[added + came + bases :]
    expand_ref, arrays, (out, held, sems) = refs[0], refs[1:-3], refs[-3:]
    me = lax.axis_index("rep")
    count, columns = out.shape
    rank = scores[0].shape[0]
    left = pl.multiple_of(lax.axis_index("tp") * columns, 128)
    slot = slot_for(me, me, per_home, home_ref, fetch_ref)
    copies = []
    for n, (at, row, _) in enumerate(pieces):
        if at is None:
            source = expand_ref.at[slot, :, pl.ds(left, columns)]
        else:
            source = arrays[at].at[pl.ds(row, rank), pl.ds(arrays[at].shape[1] - columns, columns)]
        copies.append(pltpu.make_async_copy(source, held.at[pl.ds(n * rank, rank)], sems.at[n]))
        copies[-1].start()
    row_steps = steps_of_rows(lengths_ref, count, me, per_home, home_ref, fetch_ref)
    shrink = scores[0][:, pl.ds(0, count)]
    for x in scores[1:]:
        shrink = shrink + x[:, pl.ds(0, count)]
    for x in others:
        shrink = shrink + x[...]
    shrink = adapter_scale * shrink
    high = shrink.astype(jnp.bfloat16).astype(jnp.float32)
    terms = [high, shrink - high]
    masks = [row_steps == by_part(group) for _, _, group in pieces]
    for copy in copies:
        copy.wait()
    total = base[0][...]
    for x in base[1:]:
        total = total + x[...]
    for term in terms:
        wide = jnp.concatenate([jnp.where(mask, term, 0.0) for mask in masks], axis=0)
        total = total + lax.dot_general(
            wide.astype(jnp.bfloat16),
            held[...],
            (((0,), (0,)), ((), ())),
            preferred_element_type=jnp.float32,
        )
    out[...] = total.astype(out.dtype)


def finish(pieces, tables, lengths, scores, others, base, arrays):
    count, columns = base[0].shape
    per_home, rank, _ = tables[2].shape
    smem, vmem = pl.BlockSpec(memory_space=pltpu.SMEM), pl.BlockSpec(memory_space=pltpu.VMEM)
    height = len(pieces) * rank
    return pl.pallas_call(
        functools.partial(finish_kernel, pieces, len(scores), len(others), len(base), per_home),
        out_shape=jax.ShapeDtypeStruct((count, columns), jnp.bfloat16),
        in_specs=[smem] * 3
        + [vmem] * (len(scores) + len(others) + len(base))
        + [pl.BlockSpec(memory_space=pl.ANY)] * (1 + len(arrays)),
        out_specs=vmem,
        scratch_shapes=[
            pltpu.VMEM((height, columns), jnp.bfloat16),
            pltpu.SemaphoreType.DMA((len(pieces),)),
        ],
        compiler_params=pltpu.CompilerParams(vmem_limit_bytes=24 << 20),
        cost_estimate=pl.CostEstimate(
            flops=4 * count * columns * height,
            bytes_accessed=2 * columns * height + 6 * count * columns,
            transcendentals=0,
        ),
    )(tables[0], tables[1], lengths, *scores, *others, *base, tables[3], *arrays)


def on_device(tokens, base_weight, shrink_panels, expand_panels, adapter_home, fetch_list, seg_len):
    replicas, parts, cores = lax.axis_size("rep"), lax.axis_size("parts"), lax.axis_size("tp")
    tok_count = tokens.shape[0]
    columns = expand_panels.shape[2] // cores
    panels = jnp.swapaxes(shrink_panels, 1, 2)
    rank = panels.shape[1]
    tie = lax.optimization_barrier

    alone, half = max(2, parts), replicas // 2

    def grouped(steps):
        size = len(steps) // parts
        return [tuple(steps[p * size + g] for p in range(parts)) for g in range(size)]

    far = grouped(list(range(half, replicas)))
    near = grouped(list(range(alone, half)))
    groups = far + near
    solo = [(step,) * parts for step in range(1, alone)]

    def hop(x, group):
        pairs = [
            (p * replicas + i, p * replicas + (i ^ group[p]))
            for p in range(parts)
            for i in range(replicas)
        ]
        return lax.ppermute(x, ("parts", "rep"), pairs)

    def shift_parts(x, shift):
        return lax.ppermute(x, "parts", [(i, (i + shift) % parts) for i in range(parts)])

    def shift_cores(x, shift):
        return lax.ppermute(x, "tp", [(i, (i + shift) % cores) for i in range(cores)])

    tables = (adapter_home, fetch_list, panels, expand_panels)
    groups = far + near + solo
    send = pack(groups, columns, *tables)
    tokens, send = tie((tokens, send))
    recv = [hop(x, group) for x, group in zip(send, groups)]
    tokens_of = [tokens] + [shift_parts(tokens, shift) for shift in range(1, parts)]
    solo_recv = recv[len(far) + len(near) :]
    base_weight, seg_len, solo_recv = tie((base_weight, seg_len, solo_recv))
    base = base_terms(tokens, base_weight, cores)
    base, recv[: len(far) - 1] = tie((base, recv[: len(far) - 1]))
    base = base[:1] + [shift_cores(x, shift + 1) for shift, x in enumerate(base[1:])]
    lengths_of = [seg_len] + [shift_parts(seg_len, shift) for shift in range(1, parts)]
    early, early_groups = recv[len(far) : len(far) + len(near)] + recv[: len(far) - 1], near + far[:-1]
    last, last_group, own_group = recv[len(far) - 1], far[-1], (0,) * parts

    count = len(early)
    first, sent = score(
        [tuple(range(count + len(solo) + 1))],
        early_groups + solo + [own_group],
        tuple(range(count)),
        tables,
        columns,
        lengths_of[:1],
        [tokens],
        early + solo_recv + [panels],
    )
    passed = [shift_parts(sent, shift) for shift in range(1, parts)]
    base, first, tokens_of[1:], last = tie((base, first, tokens_of[1:], last))
    scores, sent = score(
        [(0,)] + [tuple(range(count + 1))] * (parts - 1),
        [last_group] + early_groups,
        (0,),
        tables,
        columns,
        lengths_of,
        tokens_of,
        [last] + early,
        first,
    )
    last_passed = [shift_parts(sent, shift) for shift in range(1, parts)]
    halves = [scores] + [shift_cores(scores, shift) for shift in range(1, cores)]
    whole = halves[0]
    for x in halves[1:]:
        whole = whole + x
    came = [
        shift_parts(whole[:, shift * tok_count : (shift + 1) * tok_count], -shift)
        for shift in range(1, parts)
    ]
    arrays = early + solo_recv + [last] + passed + last_passed
    pieces = [(None, 0, own_group)]
    pieces += [(n, 0, group) for n, group in enumerate(early_groups + solo + [last_group])]
    at = len(pieces) - 1
    for shift in range(1, parts):
        pieces += [(at, n * rank, turned(group, shift)) for n, group in enumerate(early_groups)]
        pieces.append((at + parts - 1, 0, turned(last_group, shift)))
        at += 1
    return finish(pieces, tables, seg_len, halves, came, base, arrays)


def solution(mesh):
    return jax.shard_map(
        on_device,
        mesh=mesh,
        in_specs=(
            P(("parts", "rep"), "tp"),
            P("tp", None),
            P("rep", "tp", None),
            P("rep", None, None),
            P(),
            P(),
            P(("parts", "rep"), None),
        ),
        out_specs=P(("parts", "rep"), "tp"),
        check_vma=False,
    )
```

time: 99 us -> 76.6 us (0.77)
  waiting for transfers between devices: 17.9 us -> 45.1 us
  starting transfers between devices: 28.9 us -> 11.3 us
  between operations: 15.5 us -> 0.15 us
  matrix products: 7.93 us -> 0 us
  local copies, waits for them, and re-layouts: 11.1 us -> 3.41 us
  other arithmetic: 5.49 us -> 0.01 us
  Pallas kernels: 11.6 us -> 16.4 us
    ppermute x4, waiting for transfers between devices: 10.6 us -> 38.7 us  [hop(): return lax.ppermute(x, ('parts', 'rep'), pairs)]
    ppermute x5, starting transfers between devices: 21.4 us -> 5.25 us  [shift_parts(): lax.ppermute(x, 'parts', [(i, (i + shift) % parts) for i in range(parts)])]
    dot_general x2 -> x0, matrix products: 7.93 us -> none  [the longest x1 7.47 us: on_device(): base_part = jnp.dot(tokens, base_weight, preferred_element_type=jnp.float32)]
    pallas_call x3 -> x5, Pallas kernels: 11.6 us -> 16.4 us  [the longest x2 6.27 us: score(): pl.pallas_call(functools.partial(score_kernel, plan, groups, kept, chunks...]
    unnamed x18 -> x14, local copies, waits for them, and re-layouts: 6.96 us -> 3.41 us
    slice x4 -> x0, local copies, waits for them, and re-layouts: 2.11 us -> none  [the longest x2 1.25 us: on_device(): expands = [own_expand] + [x[:, depth:] for x in solo_recv + early]]
    reduce_sum x4 -> x0, other arithmetic: 1.68 us -> none  [the longest x1 1.36 us: on_device(): slot = jnp.sum(jnp.where(steps == 0, stored % per_home, 0))]
    ppermute x4, starting transfers between devices: 7.4 us -> 5.96 us  [hop(): return lax.ppermute(x, ('parts', 'rep'), pairs)]
  transfers between devices with their start and end apart: 11 -> 11, of which waited for: 5 -> 6; matrix products, arithmetic and copies ran while one was open for 22% -> 0% of each run, Pallas kernels for 4% -> 9%
where the time goes in v12:
time: 76.6 us; the launch traced here: 76.4 us
  waiting for transfers between devices  45.1 us (59%)
  Pallas kernels  16.4 us (21%)
  starting transfers between devices  11.3 us (15%)
  local copies, waits for them, and re-layouts  3.41 us (4%)
    ppermute x4, waiting for transfers between devices, hop(): return lax.ppermute(x, ('parts', 'rep'), pairs)  38.7 us
    ppermute x5, waiting for transfers between devices, shift_parts(): lax.ppermute(x, 'parts', [(i, (i + shift) % parts) for i in range(parts)])  6.46 us
    pallas_call x2, Pallas kernels, score(): pl.pallas_call(functools.partial(score_kernel, plan, groups, kept, chunks...  6.27 us
    ppermute x4, starting transfers between devices, hop(): return lax.ppermute(x, ('parts', 'rep'), pairs)  5.96 us
    ppermute x5, starting transfers between devices, shift_parts(): lax.ppermute(x, 'parts', [(i, (i + shift) % parts) for i in range(parts)])  5.25 us
    pallas_call x1, Pallas kernels, base_terms(): pl.pallas_call(functools.partial(base_kernel, chunks), out_shape=[jax.Sha...  3.95 us
    pallas_call x1, Pallas kernels, pack(): pl.pallas_call(functools.partial(pack_kernel, groups), out_shape=[jax.Sha...  3.93 us
    unnamed x14, local copies, waits for them, and re-layouts  3.41 us
  transfers between devices with their start and end apart: 11, of which 6 were waited for; matrix products, arithmetic and copies ran while one was open for 0% of the time, Pallas kernels for 9%

profile of v12, /device:TPU:0, one launch (start us, length us, event | category | flops | bytes accessed | tf_op | source)
XLA Modules:
  0.0 76.4 jit_solution(12237169228416616172)
XLA Ops:
  0.0 3.9 %shard_map.73 = (bf16[64,4608]{1,0:T(8,128)(2,1)}, bf16[64,4608]{1,0:T(8,128)(2,1)}, bf16[64,4608]{1,0:T(8,128)(2,1)}, bf16[64,4608]{1,0:T(8,128)(2,1)}) custom-call(s32[32]{0:T(128)} %home_ref.7, s32[8,8]{1,0:T(8,128)} %fetch_ref.7, bf16[4,64,4096]{2,1,0:T(8,128)(2,1)} %bitcast.1, bf16[4,64,1024]{2,1,0:T(8,128)(2,1)} %refs_5_.1), custom_call_target="tpu_custom_call" | custom-call | bytes 4718592 | tf_op jit(solution)/shard_map/pallas_call | solution.py:70
  3.9 0.0 copy-start.4
  4.0 0.0 copy-start.6
  4.0 0.0 copy-start.5
  4.0 3.0 %collective-permute-start.5 = (bf16[256,4096]{1,0:T(8,128)(2,1)S(1)}, bf16[256,4096]{1,0:T(8,128)(2,1)S(1)}, u32[]{:S(2)}, u32[]{:S(2)}) collective-permute-start(bf16[256,4096]{1,0:T(8,128)(2,1)S(1)} %copy-done), channel_id=1, source_target_pairs={{0,16},{16,0},{1,17},{17,1},{2,18},{18,2},{3,19},{19,3},{4,20},{20... | collective-permute-start | bytes 6291464 | tf_op jit(solution)/shard_map/ppermute | solution.py:307
  7.0 1.6 %collective-permute-start = (bf16[64,4608]{1,0:T(8,128)(2,1)}, bf16[64,4608]{1,0:T(8,128)(2,1)S(1)}, u32[]{:S(2)}, u32[]{:S(2)}) collective-permute-start(bf16[64,4608]{1,0:T(8,128)(2,1)} %get-tuple-element.35), channel_id=1, source_target_pairs={{0,2},{2,0},{4,6},{6,4},{8,10},{10,8},{12,14},{14,12},{16,18},{18,... | collective-permute-start | bytes 1769480 | tf_op jit(solution)/shard_map/ppermute | solution.py:304
  8.6 2.5 %collective-permute-start.2 = (bf16[64,4608]{1,0:T(8,128)(2,1)}, bf16[64,4608]{1,0:T(8,128)(2,1)S(1)}, u32[]{:S(2)}, u32[]{:S(2)}) collective-permute-start(bf16[64,4608]{1,0:T(8,128)(2,1)} %get-tuple-element.41), channel_id=1, source_target_pairs={{0,8},{2,10},{4,12},{6,14},{8,0},{10,2},{12,4},{14,6},{16,28},{18,... | collective-permute-start | bytes 1769480 | tf_op jit(solution)/shard_map/ppermute | solution.py:304
  11.1 1.6 %collective-permute-start.4 = (bf16[64,4608]{1,0:T(8,128)(2,1)}, bf16[64,4608]{1,0:T(8,128)(2,1)S(1)}, u32[]{:S(2)}, u32[]{:S(2)}) collective-permute-start(bf16[64,4608]{1,0:T(8,128)(2,1)} %get-tuple-element.44), channel_id=1, source_target_pairs={{0,4},{2,6},{4,0},{6,2},{8,12},{10,14},{12,8},{14,10},{16,22},{18,... | collective-permute-start | bytes 1769480 | tf_op jit(solution)/shard_map/ppermute | solution.py:304
  12.7 0.3 collective-permute-start.6
  13.0 9.0 %collective-permute-done.refs_4_.refs_8_ = bf16[64,4608]{1,0:T(8,128)(2,1)S(1)} collective-permute-done((bf16[64,4608]{1,0:T(8,128)(2,1)}, bf16[64,4608]{1,0:T(8,128)(2,1)S(1)}, u32[]{:S(2)}, u32[]{:S(2)}) %collective-permute-start) | collective-permute-done | bytes 589856 | tf_op jit(solution)/shard_map/ppermute | solution.py:304
  22.0 3.4 %copy-done.1 = bf16[4096,1024]{1,0:T(8,128)(2,1)S(1)} copy-done((bf16[4096,1024]{1,0:T(8,128)(2,1)S(1)}, bf16[4096,1024]{1,0:T(8,128)(2,1)}, u32[]{:S(2)}) %copy-start.1) | copy-done | bytes 8388632
  25.4 3.9 %shard_map.74 = (f32[256,512]{1,0:T(8,128)S(1)}, f32[256,512]{1,0:T(8,128)S(1)}) custom-call(bf16[256,4096]{1,0:T(8,128)(2,1)S(1)} %copy-done, bf16[4096,1024]{1,0:T(8,128)(2,1)S(1)} %copy-done.1), custom_call_target="tpu_custom_call" | custom-call | tf_op jit(solution)/shard_map/pallas_call | solution.py:195
  29.3 21.4 %collective-permute-done.2.refs_3_.refs_7_ = bf16[64,4608]{1,0:T(8,128)(2,1)S(1)} collective-permute-done((bf16[64,4608]{1,0:T(8,128)(2,1)}, bf16[64,4608]{1,0:T(8,128)(2,1)S(1)}, u32[]{:S(2)}, u32[]{:S(2)}) %collective-permute-start.2) | collective-permute-done | bytes 589856 | tf_op jit(solution)/shard_map/ppermute | solution.py:304
  50.7 0.0 collective-permute-start.3
  50.7 0.0 copy-done.6
  50.7 0.0 collective-permute-start.1
  50.7 0.0 collective-permute-done.4.refs_2_.refs_6_
  50.8 3.1 %shard_map.75 = (f32[64,256]{1,0:T(8,128)S(1)}, bf16[128,512]{1,0:T(8,128)(2,1)S(1)}) custom-call(s32[32]{0:T(128)S(1)} %copy-done.5, s32[8,8]{1,0:T(8,128)S(1)} %copy-done.4, s32[1,8]{1,0:T(1,128)S(1)} %copy-done.6, bf16[256,4096]{1,0:T(8,128)(2,1)S(1)} %copy-done, bf16[64,4608]{1,0:T(8,128)(2,1)S(1)} %collective-permute-done.4.refs_2_.refs_6_, ...), custom_call_target="tpu_custom_call" | custom-call | tf_op jit(solution)/shard_map/pallas_call | solution.py:140
  53.9 8.2 %collective-permute-done.6.refs_5_.refs_9_ = bf16[64,4608]{1,0:T(8,128)(2,1)S(1)} collective-permute-done((bf16[64,4608]{1,0:T(8,128)(2,1)}, bf16[64,4608]{1,0:T(8,128)(2,1)S(1)}, u32[]{:S(2)}, u32[]{:S(2)}) %collective-permute-start.6) | collective-permute-done | bytes 589856 | tf_op jit(solution)/shard_map/ppermute | solution.py:304
  62.1 0.0 collective-permute-done.3.refs_4_
  62.1 0.0 collective-permute-done.5.refs_4_
  62.1 0.0 collective-permute-done.1.refs_1_
  62.1 3.2 %shard_map.76 = (f32[64,512]{1,0:T(8,128)S(1)}, bf16[64,512]{1,0:T(8,128)(2,1)S(1)}) custom-call(s32[32]{0:T(128)S(1)} %copy-done.5, s32[8,8]{1,0:T(8,128)S(1)} %copy-done.4, s32[1,8]{1,0:T(1,128)S(1)} %copy-done.6, s32[1,8]{1,0:T(1,128)S(1)} %collective-permute-done.1.refs_1_, f32[64,256]{1,0:T(8,128)S(1)} %get-tuple-element.49.refs_2_, ...), custom_call_target="tpu_custom_call" | custom-call | tf_op jit(solution)/shard_map/pallas_call | solution.py:140
  65.3 0.1 collective-permute-start.7
  65.4 0.1 collective-permute-start.9
  65.5 2.0 %collective-permute-start.10 = (bf16[64,512]{1,0:T(8,128)(2,1)S(1)}, bf16[64,512]{1,0:T(8,128)(2,1)S(1)}, u32[]{:S(2)}, u32[]{:S(2)}) collective-permute-start(bf16[64,512]{1,0:T(8,128)(2,1)S(1)} %get-tuple-element.56), channel_id=1, source_target_pairs={{0,16},{16,0},{1,17},{17,1},{2,18},{18,2},{3,19},{19,3},{4,20},{20... | collective-permute-start | bytes 196616 | tf_op jit(solution)/shard_map/ppermute | solution.py:307
  67.5 0.0 collective-permute-done.7.refs_1_
  67.5 0.2 collective-permute-start.8
  67.7 4.1 %collective-permute-done.9.refs_10_ = bf16[128,512]{1,0:T(8,128)(2,1)S(1)} collective-permute-done((bf16[128,512]{1,0:T(8,128)(2,1)S(1)}, bf16[128,512]{1,0:T(8,128)(2,1)S(1)}, u32[]{:S(2)}, u32[]{:S(2)}) %collective-permute-start.9) | collective-permute-done | bytes 131104 | tf_op jit(solution)/shard_map/ppermute | solution.py:307
  71.8 1.4 %collective-permute-done.10.refs_11_ = bf16[64,512]{1,0:T(8,128)(2,1)S(1)} collective-permute-done((bf16[64,512]{1,0:T(8,128)(2,1)S(1)}, bf16[64,512]{1,0:T(8,128)(2,1)S(1)}, u32[]{:S(2)}, u32[]{:S(2)}) %collective-permute-start.10) | collective-permute-done | bytes 65568 | tf_op jit(solution)/shard_map/ppermute | solution.py:307
  73.2 1.0 %collective-permute-done.8.refs_2_ = f32[64,256]{1,0:T(8,128)S(1)} collective-permute-done((f32[64,256]{1,0:T(8,128)S(1)}, f32[64,256]{1,0:T(8,128)S(1)}, u32[]{:S(2)}, u32[]{:S(2)}) %collective-permute-start.8) | collective-permute-done | bytes 65568 | tf_op jit(solution)/shard_map/ppermute | solution.py:307
  74.1 2.2 %shard_map.77 = bf16[256,512]{1,0:T(8,128)(2,1)} custom-call(s32[32]{0:T(128)S(1)} %copy-done.5, s32[8,8]{1,0:T(8,128)S(1)} %copy-done.4, s32[1,8]{1,0:T(1,128)S(1)} %copy-done.6, f32[64,512]{1,0:T(8,128)S(1)} %get-tuple-element.52.refs_0_, f32[64,512]{1,0:T(8,128)S(1)} %collective-permute-done.7.refs_1_, f32[64,256]{1,0:T(8,128)S(1)} %collective-permute-done.8.refs_2_, ...), custom_call_target="tpu_custom_call" | custom-call | flops 268435456 | bytes 1310720 | tf_op jit(solution)/shard_map/pallas_call | solution.py:259
  (10 shorter events, 0.0 us)
Async XLA Ops:
  0.0 4.0 %copy-start = (bf16[256,4096]{1,0:T(8,128)(2,1)S(1)}, bf16[256,4096]{1,0:T(8,128)(2,1)}, u32[]{:S(2)}) copy-start(bf16[256,4096]{1,0:T(8,128)(2,1)} %refs_3_) | copy-start | bytes 6291460
  3.9 46.8 %copy-start.4 = (s32[8,8]{1,0:T(8,128)S(1)}, s32[8,8]{1,0:T(8,128)}, u32[]{:S(2)}) copy-start(s32[8,8]{1,0:T(8,128)} %fetch_ref.7) | copy-start | bytes 772
  4.0 46.8 %copy-start.6 = (s32[1,8]{1,0:T(1,128)S(1)}, s32[1,8]{1,0:T(1,128)}, u32[]{:S(2)}) copy-start(s32[1,8]{1,0:T(1,128)} %lengths_ref) | copy-start | bytes 100
  4.0 46.8 %copy-start.5 = (s32[32]{0:T(128)S(1)}, s32[32]{0:T(128)}, u32[]{:S(2)}) copy-start(s32[32]{0:T(128)} %home_ref.7) | copy-start | bytes 388
  4.0 58.1 %collective-permute-start.5 = (bf16[256,4096]{1,0:T(8,128)(2,1)S(1)}, bf16[256,4096]{1,0:T(8,128)(2,1)S(1)}, u32[]{:S(2)}, u32[]{:S(2)}) collective-permute-start(bf16[256,4096]{1,0:T(8,128)(2,1)S(1)} %copy-done), channel_id=1, source_target_pairs={{0,16},{16,0},{1,17},{17,1},{2,18},{18,2},{3,19},{19,3},{4,20},{20... | collective-permute-start | bytes 6291464 | tf_op jit(solution)/shard_map/ppermute | solution.py:307
  7.0 15.0 %collective-permute-start = (bf16[64,4608]{1,0:T(8,128)(2,1)}, bf16[64,4608]{1,0:T(8,128)(2,1)S(1)}, u32[]{:S(2)}, u32[]{:S(2)}) collective-permute-start(bf16[64,4608]{1,0:T(8,128)(2,1)} %get-tuple-element.35), channel_id=1, source_target_pairs={{0,2},{2,0},{4,6},{6,4},{8,10},{10,8},{12,14},{14,12},{16,18},{18,... | collective-permute-start | bytes 1769480 | tf_op jit(solution)/shard_map/ppermute | solution.py:304
  8.6 42.1 %collective-permute-start.2 = (bf16[64,4608]{1,0:T(8,128)(2,1)}, bf16[64,4608]{1,0:T(8,128)(2,1)S(1)}, u32[]{:S(2)}, u32[]{:S(2)}) collective-permute-start(bf16[64,4608]{1,0:T(8,128)(2,1)} %get-tuple-element.41), channel_id=1, source_target_pairs={{0,8},{2,10},{4,12},{6,14},{8,0},{10,2},{12,4},{14,6},{16,28},{18,... | collective-permute-start | bytes 1769480 | tf_op jit(solution)/shard_map/ppermute | solution.py:304
  11.1 39.6 %collective-permute-start.4 = (bf16[64,4608]{1,0:T(8,128)(2,1)}, bf16[64,4608]{1,0:T(8,128)(2,1)S(1)}, u32[]{:S(2)}, u32[]{:S(2)}) collective-permute-start(bf16[64,4608]{1,0:T(8,128)(2,1)} %get-tuple-element.44), channel_id=1, source_target_pairs={{0,4},{2,6},{4,0},{6,2},{8,12},{10,14},{12,8},{14,10},{16,22},{18,... | collective-permute-start | bytes 1769480 | tf_op jit(solution)/shard_map/ppermute | solution.py:304
  12.7 49.4 %collective-permute-start.6 = (bf16[64,4608]{1,0:T(8,128)(2,1)}, bf16[64,4608]{1,0:T(8,128)(2,1)S(1)}, u32[]{:S(2)}, u32[]{:S(2)}) collective-permute-start(bf16[64,4608]{1,0:T(8,128)(2,1)} %get-tuple-element.48), channel_id=1, source_target_pairs={{0,10},{2,8},{4,14},{6,12},{8,2},{10,0},{12,6},{14,4},{16,30},{18,... | collective-permute-start | bytes 1769480 | tf_op jit(solution)/shard_map/ppermute | solution.py:304
  22.0 3.4 %copy-start.1 = (bf16[4096,1024]{1,0:T(8,128)(2,1)S(1)}, bf16[4096,1024]{1,0:T(8,128)(2,1)}, u32[]{:S(2)}) copy-start(bf16[4096,1024]{1,0:T(8,128)(2,1)} %weight_ref) | copy-start | bytes 25165828
  25.4 25.4 %copy-start.2 = (bf16[4,4096,64]{1,2,0:T(8,128)(2,1)S(1)}, bf16[4,4096,64]{1,2,0:T(8,128)(2,1)}, u32[]{:S(2)}) copy-start(bf16[4,4096,64]{1,2,0:T(8,128)(2,1)} %param.9) | copy-start | bytes 6291460
  50.7 11.4 %collective-permute-start.3 = (f32[256,512]{1,0:T(8,128)S(1)}, f32[256,512]{1,0:T(8,128)S(1)}, u32[]{:S(2)}, u32[]{:S(2)}) collective-permute-start(f32[256,512]{1,0:T(8,128)S(1)} %get-tuple-element.43), channel_id=1, source_target_pairs={{0,1},{1,0},{2,3},{3,2},{4,5},{5,4},{6,7},{7,6},{8,9},{9,8},{10,11... | collective-permute-start | bytes 1572872 | tf_op jit(solution)/shard_map/ppermute | solution.py:310
  50.7 11.4 %collective-permute-start.1 = (s32[1,8]{1,0:T(1,128)S(1)}, s32[1,8]{1,0:T(1,128)S(1)}, u32[]{:S(2)}, u32[]{:S(2)}) collective-permute-start(s32[1,8]{1,0:T(1,128)S(1)} %copy-done.6), channel_id=1, source_target_pairs={{0,16},{16,0},{1,17},{17,1},{2,18},{18,2},{3,19},{19,3},{4,20},{20... | collective-permute-start | bytes 104 | tf_op jit(solution)/shard_map/ppermute | solution.py:307
  62.1 12.0 %copy-start.3 = (bf16[4,64,1024]{2,1,0:T(8,128)(2,1)S(1)}, bf16[4,64,1024]{2,1,0:T(8,128)(2,1)}, u32[]{:S(2)}) copy-start(bf16[4,64,1024]{2,1,0:T(8,128)(2,1)} %refs_5_.1) | copy-start | bytes 1572868
  65.3 2.2 %collective-permute-start.7 = (f32[64,512]{1,0:T(8,128)S(1)}, f32[64,512]{1,0:T(8,128)S(1)}, u32[]{:S(2)}, u32[]{:S(2)}) collective-permute-start(f32[64,512]{1,0:T(8,128)S(1)} %get-tuple-element.52.refs_0_), channel_id=1, source_target_pairs={{0,1},{1,0},{2,3},{3,2},{4,5},{5,4},{6,7},{7,6},{8,9},{9,8},{10,11... | collective-permute-start | bytes 393224 | tf_op jit(solution)/shard_map/ppermute | solution.py:310
  65.4 6.4 %collective-permute-start.9 = (bf16[128,512]{1,0:T(8,128)(2,1)S(1)}, bf16[128,512]{1,0:T(8,128)(2,1)S(1)}, u32[]{:S(2)}, u32[]{:S(2)}) collective-permute-start(bf16[128,512]{1,0:T(8,128)(2,1)S(1)} %get-tuple-element.55), channel_id=1, source_target_pairs={{0,16},{16,0},{1,17},{17,1},{2,18},{18,2},{3,19},{19,3},{4,20},{20... | collective-permute-start | bytes 393224 | tf_op jit(solution)/shard_map/ppermute | solution.py:307
  65.5 7.7 %collective-permute-start.10 = (bf16[64,512]{1,0:T(8,128)(2,1)S(1)}, bf16[64,512]{1,0:T(8,128)(2,1)S(1)}, u32[]{:S(2)}, u32[]{:S(2)}) collective-permute-start(bf16[64,512]{1,0:T(8,128)(2,1)S(1)} %get-tuple-element.56), channel_id=1, source_target_pairs={{0,16},{16,0},{1,17},{17,1},{2,18},{18,2},{3,19},{19,3},{4,20},{20... | collective-permute-start | bytes 196616 | tf_op jit(solution)/shard_map/ppermute | solution.py:307
  67.5 6.6 %collective-permute-start.8 = (f32[64,256]{1,0:T(8,128)S(1)}, f32[64,256]{1,0:T(8,128)S(1)}, u32[]{:S(2)}, u32[]{:S(2)}) collective-permute-start(f32[64,256]{1,0:T(8,128)S(1)} %slice_add_fusion), channel_id=1, source_target_pairs={{0,16},{16,0},{1,17},{17,1},{2,18},{18,2},{3,19},{19,3},{4,20},{20... | collective-permute-start | bytes 196616 | tf_op jit(solution)/shard_map/ppermute | solution.py:307

commit v13 on v12

--- a/solution.py
+++ b/solution.py
@@ -44,39 +44,46 @@
 
 
 def pack_kernel(groups, home_ref, fetch_ref, shrink_ref, expand_ref, *refs):
-    outs, sems = refs[:-1], refs[-1]
+    count = len(groups)
+    outs, held, in_sems, out_sems = refs[:count], refs[count], refs[count + 1], refs[count + 2]
     me = lax.axis_index("rep")
     per_home, _, depth = shrink_ref.shape
     columns = expand_ref.shape[2] // lax.axis_size("tp")
     left = pl.multiple_of(lax.axis_index("tp") * columns, 128)
-    copies = []
+    cuts = in_sems.shape[1] - 1
+    width = depth // cuts
+    arriving = []
     for at, group in enumerate(groups):
         slot = slot_for(me ^ by_part(group), me, per_home, home_ref, fetch_ref)
-        pieces = (
-            (shrink_ref.at[slot], outs[at].at[:, pl.ds(0, depth)]),
-            (expand_ref.at[slot, :, pl.ds(left, columns)], outs[at].at[:, pl.ds(depth, columns)]),
-        )
-        for n, (source, target) in enumerate(pieces):
-            copies.append(pltpu.make_async_copy(source, target, sems.at[at, n]))
-            copies[-1].start()
-    for copy in copies:
+        pieces = [(shrink_ref.at[slot, :, pl.ds(n * width, width)], n * width, width) for n in range(cuts)]
+        pieces.append((expand_ref.at[slot, :, pl.ds(left, columns)], depth, columns))
+        for n, (source, start, size) in enumerate(pieces):
+            target = held.at[at, :, pl.ds(start, size)]
+            copy = pltpu.make_async_copy(source, target, in_sems.at[at, n])
+            copy.start()
+            leave = pltpu.make_async_copy(target, outs[at].at[:, pl.ds(start, size)], out_sems.at[at, n])
+            arriving.append((copy, leave))
+    for copy, leave in arriving:
         copy.wait()
+        leave.start()
+    for _, leave in arriving:
+        leave.wait()
 
 
 def pack(groups, columns, adapter_home, fetch_list, panels, expand_panels):
     rank, depth = panels.shape[1:]
     shape = (rank, depth + columns)
+    cuts = 2
     return list(
         pl.pallas_call(
             functools.partial(pack_kernel, groups),
             out_shape=[jax.ShapeDtypeStruct(shape, panels.dtype)] * len(groups),
             in_specs=[pl.BlockSpec(memory_space=pltpu.SMEM)] * 2 + [pl.BlockSpec(memory_space=pl.ANY)] * 2,
-            out_specs=[pl.BlockSpec(memory_space=pltpu.VMEM)] * len(groups),
-            scratch_shapes=[pltpu.SemaphoreType.DMA((len(groups), 2))],
+            out_specs=[pl.BlockSpec(memory_space=pl.ANY)] * len(groups),
+            scratch_shapes=[pltpu.VMEM((len(groups),) + shape, panels.dtype)]
+            + [pltpu.SemaphoreType.DMA((len(groups), cuts + 1))] * 2,
             compiler_params=pltpu.CompilerParams(vmem_limit_bytes=56 << 20),
-            cost_estimate=pl.CostEstimate(
-                flops=0, bytes_accessed=4 * len(groups) * shape[0] * shape[1], transcendentals=0
-            ),
+            cost_estimate=pl.CostEstimate(flops=0, bytes_accessed=0, transcendentals=0),
         )(adapter_home, fetch_list, panels, expand_panels)
     )
 
@@ -316,12 +323,13 @@
     recv = [hop(x, group) for x, group in zip(send, groups)]
     tokens_of = [tokens] + [shift_parts(tokens, shift) for shift in range(1, parts)]
     solo_recv = recv[len(far) + len(near) :]
-    base_weight, seg_len, solo_recv = tie((base_weight, seg_len, solo_recv))
+    near_recv = recv[len(far) : len(far) + len(near)]
+    base_weight, seg_len, near_recv = tie((base_weight, seg_len, near_recv))
     base = base_terms(tokens, base_weight, cores)
     base, recv[: len(far) - 1] = tie((base, recv[: len(far) - 1]))
     base = base[:1] + [shift_cores(x, shift + 1) for shift, x in enumerate(base[1:])]
     lengths_of = [seg_len] + [shift_parts(seg_len, shift) for shift in range(1, parts)]
-    early, early_groups = recv[len(far) : len(far) + len(near)] + recv[: len(far) - 1], near + far[:-1]
+    early, early_groups = near_recv + recv[: len(far) - 1], near + far[:-1]
     last, last_group, own_group = recv[len(far) - 1], far[-1], (0,) * parts
 
     count = len(early)
@@ -336,7 +344,7 @@
         early + solo_recv + [panels],
     )
     passed = [shift_parts(sent, shift) for shift in range(1, parts)]
-    base, first, tokens_of[1:], last = tie((base, first, tokens_of[1:], last))
+    base, first, passed, tokens_of[1:], last = tie((base, first, passed, tokens_of[1:], last))
     scores, sent = score(
         [(0,)] + [tuple(range(count + 1))] * (parts - 1),
         [last_group] + early_groups,

time: 76.6 us -> 74.3 us (0.970)
  waiting for transfers between devices: 45.1 us -> 42.6 us
  starting transfers between devices: 11.3 us -> 12.1 us
    ppermute x5, waiting for transfers between devices: 6.46 us -> 3.75 us  [shift_parts(): lax.ppermute(x, 'parts', [(i, (i + shift) % parts) for i in range(parts)])]
    ppermute x2, waiting for transfers between devices: 0.01 us -> 1.26 us  [shift_cores(): lax.ppermute(x, 'tp', [(i, (i + shift) % cores) for i in range(cores)])]
    ppermute x4, waiting for transfers between devices: 38.7 us -> 37.6 us  [hop(): return lax.ppermute(x, ('parts', 'rep'), pairs)]
where the time goes in v13:
time: 74.3 us; the launch traced here: 74.1 us
  waiting for transfers between devices  42.6 us (57%)
  Pallas kernels  16 us (22%)
  starting transfers between devices  12.1 us (16%)
  local copies, waits for them, and re-layouts  3.41 us (5%)
    ppermute x4, waiting for transfers between devices, hop(): return lax.ppermute(x, ('parts', 'rep'), pairs)  37.6 us
    pallas_call x2, Pallas kernels, score(): pl.pallas_call(functools.partial(score_kernel, plan, groups, kept, chunks...  6.27 us
    ppermute x4, starting transfers between devices, hop(): return lax.ppermute(x, ('parts', 'rep'), pairs)  5.99 us
    ppermute x5, starting transfers between devices, shift_parts(): lax.ppermute(x, 'parts', [(i, (i + shift) % parts) for i in range(parts)])  5.98 us
    pallas_call x1, Pallas kernels, base_terms(): pl.pallas_call(functools.partial(base_kernel, chunks), out_shape=[jax.Sha...  3.95 us
    ppermute x5, waiting for transfers between devices, shift_parts(): lax.ppermute(x, 'parts', [(i, (i + shift) % parts) for i in range(parts)])  3.75 us
    pallas_call x1, Pallas kernels, pack(): pl.pallas_call(functools.partial(pack_kernel, groups), out_shape=[jax.Sha...  3.5 us
    unnamed x14, local copies, waits for them, and re-layouts  3.41 us
  transfers between devices with their start and end apart: 11, of which 6 were waited for; matrix products, arithmetic and copies ran while one was open for 0% of the time, Pallas kernels for 9%

profile of v13, /device:TPU:0, one launch (start us, length us, event | category | flops | bytes accessed | tf_op | source)
XLA Modules:
  0.0 74.1 jit_solution(5813029782889393997)
XLA Ops:
  0.0 3.5 %shard_map.73 = (bf16[64,4608]{1,0:T(8,128)(2,1)}, bf16[64,4608]{1,0:T(8,128)(2,1)}, bf16[64,4608]{1,0:T(8,128)(2,1)}, bf16[64,4608]{1,0:T(8,128)(2,1)}) custom-call(s32[32]{0:T(128)} %home_ref.7, s32[8,8]{1,0:T(8,128)} %fetch_ref.7, bf16[4,64,4096]{2,1,0:T(8,128)(2,1)} %bitcast.1, bf16[4,64,1024]{2,1,0:T(8,128)(2,1)} %refs_5_.1), custom_call_target="tpu_custom_call" | custom-call | tf_op jit(solution)/shard_map/pallas_call | solution.py:78
  3.5 0.0 copy-start.4
  3.5 0.0 copy-start.5
  3.5 0.0 copy-start.6
  3.6 3.0 %collective-permute-start.6 = (bf16[256,4096]{1,0:T(8,128)(2,1)S(1)}, bf16[256,4096]{1,0:T(8,128)(2,1)S(1)}, u32[]{:S(2)}, u32[]{:S(2)}) collective-permute-start(bf16[256,4096]{1,0:T(8,128)(2,1)S(1)} %copy-done), channel_id=1, source_target_pairs={{0,16},{16,0},{1,17},{17,1},{2,18},{18,2},{3,19},{19,3},{4,20},{20... | collective-permute-start | bytes 6291464 | tf_op jit(solution)/shard_map/ppermute | solution.py:314
  6.6 1.6 %collective-permute-start = (bf16[64,4608]{1,0:T(8,128)(2,1)}, bf16[64,4608]{1,0:T(8,128)(2,1)S(1)}, u32[]{:S(2)}, u32[]{:S(2)}) collective-permute-start(bf16[64,4608]{1,0:T(8,128)(2,1)} %get-tuple-element.36), channel_id=1, source_target_pairs={{0,4},{2,6},{4,0},{6,2},{8,12},{10,14},{12,8},{14,10},{16,22},{18,... | collective-permute-start | bytes 1769480 | tf_op jit(solution)/shard_map/ppermute | solution.py:311
  8.2 2.6 %collective-permute-start.2 = (bf16[64,4608]{1,0:T(8,128)(2,1)}, bf16[64,4608]{1,0:T(8,128)(2,1)S(1)}, u32[]{:S(2)}, u32[]{:S(2)}) collective-permute-start(bf16[64,4608]{1,0:T(8,128)(2,1)} %get-tuple-element.42), channel_id=1, source_target_pairs={{0,8},{2,10},{4,12},{6,14},{8,0},{10,2},{12,4},{14,6},{16,28},{18,... | collective-permute-start | bytes 1769480 | tf_op jit(solution)/shard_map/ppermute | solution.py:311
  10.7 1.5 %collective-permute-start.4 = (bf16[64,4608]{1,0:T(8,128)(2,1)}, bf16[64,4608]{1,0:T(8,128)(2,1)S(1)}, u32[]{:S(2)}, u32[]{:S(2)}) collective-permute-start(bf16[64,4608]{1,0:T(8,128)(2,1)} %get-tuple-element.47), channel_id=1, source_target_pairs={{0,2},{2,0},{4,6},{6,4},{8,10},{10,8},{12,14},{14,12},{16,18},{18,... | collective-permute-start | bytes 1769480 | tf_op jit(solution)/shard_map/ppermute | solution.py:311
  12.3 0.3 collective-permute-start.7
  12.6 21.5 %collective-permute-done.refs_2_.refs_6_ = bf16[64,4608]{1,0:T(8,128)(2,1)S(1)} collective-permute-done((bf16[64,4608]{1,0:T(8,128)(2,1)}, bf16[64,4608]{1,0:T(8,128)(2,1)S(1)}, u32[]{:S(2)}, u32[]{:S(2)}) %collective-permute-start) | collective-permute-done | bytes 589856 | tf_op jit(solution)/shard_map/ppermute | solution.py:311
  34.0 3.4 %copy-done.1 = bf16[4096,1024]{1,0:T(8,128)(2,1)S(1)} copy-done((bf16[4096,1024]{1,0:T(8,128)(2,1)S(1)}, bf16[4096,1024]{1,0:T(8,128)(2,1)}, u32[]{:S(2)}) %copy-start.1) | copy-done | bytes 8388632
  37.4 3.9 %shard_map.74 = (f32[256,512]{1,0:T(8,128)S(1)}, f32[256,512]{1,0:T(8,128)S(1)}) custom-call(bf16[256,4096]{1,0:T(8,128)(2,1)S(1)} %copy-done, bf16[4096,1024]{1,0:T(8,128)(2,1)S(1)} %copy-done.1), custom_call_target="tpu_custom_call" | custom-call | tf_op jit(solution)/shard_map/pallas_call | solution.py:202
  41.4 9.4 %collective-permute-done.2.refs_3_.refs_7_ = bf16[64,4608]{1,0:T(8,128)(2,1)S(1)} collective-permute-done((bf16[64,4608]{1,0:T(8,128)(2,1)}, bf16[64,4608]{1,0:T(8,128)(2,1)S(1)}, u32[]{:S(2)}, u32[]{:S(2)}) %collective-permute-start.2) | collective-permute-done | bytes 589856 | tf_op jit(solution)/shard_map/ppermute | solution.py:311
  50.8 0.0 collective-permute-start.3
  50.8 0.0 collective-permute-done.4.refs_4_.refs_8_
  50.9 3.1 %shard_map.75 = (f32[64,256]{1,0:T(8,128)S(1)}, bf16[128,512]{1,0:T(8,128)(2,1)S(1)}) custom-call(s32[32]{0:T(128)S(1)} %copy-done.5, s32[8,8]{1,0:T(8,128)S(1)} %copy-done.4, s32[1,8]{1,0:T(1,128)S(1)} %copy-done.6, bf16[256,4096]{1,0:T(8,128)(2,1)S(1)} %copy-done, bf16[64,4608]{1,0:T(8,128)(2,1)S(1)} %collective-permute-done.refs_2_.refs_6_, ...), custom_call_target="tpu_custom_call" | custom-call | tf_op jit(solution)/shard_map/pallas_call | solution.py:147
  54.0 0.1 collective-permute-start.5
  54.0 2.0 %collective-permute-start.1 = (s32[1,8]{1,0:T(1,128)S(1)}, s32[1,8]{1,0:T(1,128)S(1)}, u32[]{:S(2)}, u32[]{:S(2)}) collective-permute-start(s32[1,8]{1,0:T(1,128)S(1)} %copy-done.6), channel_id=1, source_target_pairs={{0,16},{16,0},{1,17},{17,1},{2,18},{18,2},{3,19},{19,3},{4,20},{20... | collective-permute-start | bytes 104 | tf_op jit(solution)/shard_map/ppermute | solution.py:314
  56.1 6.6 %collective-permute-done.7.refs_5_.refs_9_ = bf16[64,4608]{1,0:T(8,128)(2,1)S(1)} collective-permute-done((bf16[64,4608]{1,0:T(8,128)(2,1)}, bf16[64,4608]{1,0:T(8,128)(2,1)S(1)}, u32[]{:S(2)}, u32[]{:S(2)}) %collective-permute-start.7) | collective-permute-done | bytes 589856 | tf_op jit(solution)/shard_map/ppermute | solution.py:311
  62.7 0.0 collective-permute-done.5.refs_10_
  62.7 0.0 collective-permute-done.3.refs_4_
  62.7 0.0 collective-permute-done.6.refs_4_
  62.7 0.0 copy-start.3
  62.7 0.0 collective-permute-done.1.refs_1_
  62.7 3.2 %shard_map.76 = (f32[64,512]{1,0:T(8,128)S(1)}, bf16[64,512]{1,0:T(8,128)(2,1)S(1)}) custom-call(s32[32]{0:T(128)S(1)} %copy-done.5, s32[8,8]{1,0:T(8,128)S(1)} %copy-done.4, s32[1,8]{1,0:T(1,128)S(1)} %copy-done.6, s32[1,8]{1,0:T(1,128)S(1)} %collective-permute-done.1.refs_1_, f32[64,256]{1,0:T(8,128)S(1)} %get-tuple-element.51.refs_2_, ...), custom_call_target="tpu_custom_call" | custom-call | tf_op jit(solution)/shard_map/pallas_call | solution.py:147
  65.9 0.1 collective-permute-start.8
  66.0 0.1 collective-permute-start.10
  66.1 1.3 %collective-permute-done.8.refs_1_ = f32[64,512]{1,0:T(8,128)S(1)} collective-permute-done((f32[64,512]{1,0:T(8,128)S(1)}, f32[64,512]{1,0:T(8,128)S(1)}, u32[]{:S(2)}, u32[]{:S(2)}) %collective-permute-start.8) | collective-permute-done | bytes 131104 | tf_op jit(solution)/shard_map/ppermute | solution.py:317
  67.3 0.8 %collective-permute-start.9 = (f32[64,256]{1,0:T(8,128)S(1)}, f32[64,256]{1,0:T(8,128)S(1)}, u32[]{:S(2)}, u32[]{:S(2)}) collective-permute-start(f32[64,256]{1,0:T(8,128)S(1)} %slice_add_fusion), channel_id=1, source_target_pairs={{0,16},{16,0},{1,17},{17,1},{2,18},{18,2},{3,19},{19,3},{4,20},{20... | collective-permute-start | bytes 196616 | tf_op jit(solution)/shard_map/ppermute | solution.py:314
  68.2 2.8 %collective-permute-done.10.refs_11_ = bf16[64,512]{1,0:T(8,128)(2,1)S(1)} collective-permute-done((bf16[64,512]{1,0:T(8,128)(2,1)S(1)}, bf16[64,512]{1,0:T(8,128)(2,1)S(1)}, u32[]{:S(2)}, u32[]{:S(2)}) %collective-permute-start.10) | collective-permute-done | bytes 65568 | tf_op jit(solution)/shard_map/ppermute | solution.py:314
  70.9 1.0 %collective-permute-done.9.refs_2_ = f32[64,256]{1,0:T(8,128)S(1)} collective-permute-done((f32[64,256]{1,0:T(8,128)S(1)}, f32[64,256]{1,0:T(8,128)S(1)}, u32[]{:S(2)}, u32[]{:S(2)}) %collective-permute-start.9) | collective-permute-done | bytes 65568 | tf_op jit(solution)/shard_map/ppermute | solution.py:314
  71.9 2.2 %shard_map.77 = bf16[256,512]{1,0:T(8,128)(2,1)} custom-call(s32[32]{0:T(128)S(1)} %copy-done.5, s32[8,8]{1,0:T(8,128)S(1)} %copy-done.4, s32[1,8]{1,0:T(1,128)S(1)} %copy-done.6, f32[64,512]{1,0:T(8,128)S(1)} %get-tuple-element.54.refs_0_, f32[64,512]{1,0:T(8,128)S(1)} %collective-permute-done.8.refs_1_, f32[64,256]{1,0:T(8,128)S(1)} %collective-permute-done.9.refs_2_, ...), custom_call_target="tpu_custom_call" | custom-call | flops 268435456 | bytes 1310720 | tf_op jit(solution)/shard_map/pallas_call | solution.py:266
  (10 shorter events, 0.0 us)
Async XLA Ops:
  0.0 3.6 %copy-start = (bf16[256,4096]{1,0:T(8,128)(2,1)S(1)}, bf16[256,4096]{1,0:T(8,128)(2,1)}, u32[]{:S(2)}) copy-start(bf16[256,4096]{1,0:T(8,128)(2,1)} %refs_3_) | copy-start | bytes 6291460
  3.5 47.3 %copy-start.4 = (s32[8,8]{1,0:T(8,128)S(1)}, s32[8,8]{1,0:T(8,128)}, u32[]{:S(2)}) copy-start(s32[8,8]{1,0:T(8,128)} %fetch_ref.7) | copy-start | bytes 772
  3.5 47.3 %copy-start.5 = (s32[32]{0:T(128)S(1)}, s32[32]{0:T(128)}, u32[]{:S(2)}) copy-start(s32[32]{0:T(128)} %home_ref.7) | copy-start | bytes 388
  3.5 47.3 %copy-start.6 = (s32[1,8]{1,0:T(1,128)S(1)}, s32[1,8]{1,0:T(1,128)}, u32[]{:S(2)}) copy-start(s32[1,8]{1,0:T(1,128)} %lengths_ref) | copy-start | bytes 100
  3.6 59.1 %collective-permute-start.6 = (bf16[256,4096]{1,0:T(8,128)(2,1)S(1)}, bf16[256,4096]{1,0:T(8,128)(2,1)S(1)}, u32[]{:S(2)}, u32[]{:S(2)}) collective-permute-start(bf16[256,4096]{1,0:T(8,128)(2,1)S(1)} %copy-done), channel_id=1, source_target_pairs={{0,16},{16,0},{1,17},{17,1},{2,18},{18,2},{3,19},{19,3},{4,20},{20... | collective-permute-start | bytes 6291464 | tf_op jit(solution)/shard_map/ppermute | solution.py:314
  6.6 27.5 %collective-permute-start = (bf16[64,4608]{1,0:T(8,128)(2,1)}, bf16[64,4608]{1,0:T(8,128)(2,1)S(1)}, u32[]{:S(2)}, u32[]{:S(2)}) collective-permute-start(bf16[64,4608]{1,0:T(8,128)(2,1)} %get-tuple-element.36), channel_id=1, source_target_pairs={{0,4},{2,6},{4,0},{6,2},{8,12},{10,14},{12,8},{14,10},{16,22},{18,... | collective-permute-start | bytes 1769480 | tf_op jit(solution)/shard_map/ppermute | solution.py:311
  8.2 42.7 %collective-permute-start.2 = (bf16[64,4608]{1,0:T(8,128)(2,1)}, bf16[64,4608]{1,0:T(8,128)(2,1)S(1)}, u32[]{:S(2)}, u32[]{:S(2)}) collective-permute-start(bf16[64,4608]{1,0:T(8,128)(2,1)} %get-tuple-element.42), channel_id=1, source_target_pairs={{0,8},{2,10},{4,12},{6,14},{8,0},{10,2},{12,4},{14,6},{16,28},{18,... | collective-permute-start | bytes 1769480 | tf_op jit(solution)/shard_map/ppermute | solution.py:311
  10.7 40.1 %collective-permute-start.4 = (bf16[64,4608]{1,0:T(8,128)(2,1)}, bf16[64,4608]{1,0:T(8,128)(2,1)S(1)}, u32[]{:S(2)}, u32[]{:S(2)}) collective-permute-start(bf16[64,4608]{1,0:T(8,128)(2,1)} %get-tuple-element.47), channel_id=1, source_target_pairs={{0,2},{2,0},{4,6},{6,4},{8,10},{10,8},{12,14},{14,12},{16,18},{18,... | collective-permute-start | bytes 1769480 | tf_op jit(solution)/shard_map/ppermute | solution.py:311
  12.3 50.4 %collective-permute-start.7 = (bf16[64,4608]{1,0:T(8,128)(2,1)}, bf16[64,4608]{1,0:T(8,128)(2,1)S(1)}, u32[]{:S(2)}, u32[]{:S(2)}) collective-permute-start(bf16[64,4608]{1,0:T(8,128)(2,1)} %get-tuple-element.50), channel_id=1, source_target_pairs={{0,10},{2,8},{4,14},{6,12},{8,2},{10,0},{12,6},{14,4},{16,30},{18,... | collective-permute-start | bytes 1769480 | tf_op jit(solution)/shard_map/ppermute | solution.py:311
  34.0 3.4 %copy-start.1 = (bf16[4096,1024]{1,0:T(8,128)(2,1)S(1)}, bf16[4096,1024]{1,0:T(8,128)(2,1)}, u32[]{:S(2)}) copy-start(bf16[4096,1024]{1,0:T(8,128)(2,1)} %weight_ref) | copy-start | bytes 25165828
  37.4 13.4 %copy-start.2 = (bf16[4,4096,64]{1,2,0:T(8,128)(2,1)S(1)}, bf16[4,4096,64]{1,2,0:T(8,128)(2,1)}, u32[]{:S(2)}) copy-start(bf16[4,4096,64]{1,2,0:T(8,128)(2,1)} %param.9) | copy-start | bytes 6291460
  50.8 11.9 %collective-permute-start.3 = (f32[256,512]{1,0:T(8,128)S(1)}, f32[256,512]{1,0:T(8,128)S(1)}, u32[]{:S(2)}, u32[]{:S(2)}) collective-permute-start(f32[256,512]{1,0:T(8,128)S(1)} %get-tuple-element.44), channel_id=1, source_target_pairs={{0,1},{1,0},{2,3},{3,2},{4,5},{5,4},{6,7},{7,6},{8,9},{9,8},{10,11... | collective-permute-start | bytes 1572872 | tf_op jit(solution)/shard_map/ppermute | solution.py:317
  54.0 8.7 %collective-permute-start.5 = (bf16[128,512]{1,0:T(8,128)(2,1)S(1)}, bf16[128,512]{1,0:T(8,128)(2,1)S(1)}, u32[]{:S(2)}, u32[]{:S(2)}) collective-permute-start(bf16[128,512]{1,0:T(8,128)(2,1)S(1)} %get-tuple-element.49), channel_id=1, source_target_pairs={{0,16},{16,0},{1,17},{17,1},{2,18},{18,2},{3,19},{19,3},{4,20},{20... | collective-permute-start | bytes 393224 | tf_op jit(solution)/shard_map/ppermute | solution.py:314
  54.0 8.7 %collective-permute-start.1 = (s32[1,8]{1,0:T(1,128)S(1)}, s32[1,8]{1,0:T(1,128)S(1)}, u32[]{:S(2)}, u32[]{:S(2)}) collective-permute-start(s32[1,8]{1,0:T(1,128)S(1)} %copy-done.6), channel_id=1, source_target_pairs={{0,16},{16,0},{1,17},{17,1},{2,18},{18,2},{3,19},{19,3},{4,20},{20... | collective-permute-start | bytes 104 | tf_op jit(solution)/shard_map/ppermute | solution.py:314
  62.7 9.2 %copy-start.3 = (bf16[4,64,1024]{2,1,0:T(8,128)(2,1)S(1)}, bf16[4,64,1024]{2,1,0:T(8,128)(2,1)}, u32[]{:S(2)}) copy-start(bf16[4,64,1024]{2,1,0:T(8,128)(2,1)} %refs_5_.1) | copy-start | bytes 1572868
  65.9 1.4 %collective-permute-start.8 = (f32[64,512]{1,0:T(8,128)S(1)}, f32[64,512]{1,0:T(8,128)S(1)}, u32[]{:S(2)}, u32[]{:S(2)}) collective-permute-start(f32[64,512]{1,0:T(8,128)S(1)} %get-tuple-element.54.refs_0_), channel_id=1, source_target_pairs={{0,1},{1,0},{2,3},{3,2},{4,5},{5,4},{6,7},{7,6},{8,9},{9,8},{10,11... | collective-permute-start | bytes 393224 | tf_op jit(solution)/shard_map/ppermute | solution.py:317
  66.0 4.9 %collective-permute-start.10 = (bf16[64,512]{1,0:T(8,128)(2,1)S(1)}, bf16[64,512]{1,0:T(8,128)(2,1)S(1)}, u32[]{:S(2)}, u32[]{:S(2)}) collective-permute-start(bf16[64,512]{1,0:T(8,128)(2,1)S(1)} %get-tuple-element.58), channel_id=1, source_target_pairs={{0,16},{16,0},{1,17},{17,1},{2,18},{18,2},{3,19},{19,3},{4,20},{20... | collective-permute-start | bytes 196616 | tf_op jit(solution)/shard_map/ppermute | solution.py:314
  67.3 4.6 %collective-permute-start.9 = (f32[64,256]{1,0:T(8,128)S(1)}, f32[64,256]{1,0:T(8,128)S(1)}, u32[]{:S(2)}, u32[]{:S(2)}) collective-permute-start(f32[64,256]{1,0:T(8,128)S(1)} %slice_add_fusion), channel_id=1, source_target_pairs={{0,16},{16,0},{1,17},{17,1},{2,18},{18,2},{3,19},{19,3},{4,20},{20... | collective-permute-start | bytes 196616 | tf_op jit(solution)/shard_map/ppermute | solution.py:314

commit v14 on v13

--- a/solution.py
+++ b/solution.py
@@ -88,12 +88,12 @@
     )
 
 
-def score_kernel(plan, groups, kept, chunks, has_prior, per_home, home_ref, fetch_ref, *refs):
+def score_kernel(plan, groups, chunks, has_prior, per_home, home_ref, fetch_ref, *refs):
     sets, many = len(plan), len(groups)
     lengths, refs = refs[:sets], refs[sets:]
     prior, refs = (refs[0], refs[1:]) if has_prior else (None, refs)
     tokens, panels = refs[:sets], refs[sets : sets + many]
-    out, out_expand, held_tokens, held_panels, sems = refs[sets + many :]
+    out, held_tokens, held_panels, sems = refs[sets + many :]
     me = lax.axis_index("rep")
     rank, count, depth = out.shape[0], held_tokens.shape[1], held_tokens.shape[2]
     width = depth // chunks
@@ -106,11 +106,6 @@
             source = ref.at[:, cols] if len(ref.shape) == 2 else ref.at[slot, :, cols]
             pairs.append((source, held_panels.at[pl.ds(n * rank, rank), cols]))
         pairs += [(ref.at[:, cols], held_tokens.at[n, :, cols]) for n, ref in enumerate(tokens)]
-        if c == chunks - 1:
-            pairs += [
-                (panels[n].at[:, pl.ds(depth, out_expand.shape[1])], out_expand.at[pl.ds(i * rank, rank)])
-                for i, n in enumerate(kept)
-            ]
         copies.append([])
         for n, (source, target) in enumerate(pairs):
             copies[-1].append(pltpu.make_async_copy(source, target, sems.at[c, n]))
@@ -130,14 +125,15 @@
             )
             sums[t] = product if c == 0 else sums[t] + product
     for t, used in enumerate(plan):
-        total = prior[...] if has_prior and t == 0 else jnp.zeros((rank, count), jnp.float32)
+        mine = pl.ds(t * count, count)
+        total = prior[:, mine] if has_prior else jnp.zeros((rank, count), jnp.float32)
         for n, panel in enumerate(used):
             term = sums[t][n * rank : (n + 1) * rank]
             total = total + jnp.where(row_steps[t] == by_part(groups[panel]), term, 0.0)
-        out[:, pl.ds(t * count, count)] = total
-
-
-def score(plan, groups, kept, tables, columns, lengths_of, tokens_of, panels, prior=None):
+        out[:, mine] = total
+
+
+def score(plan, groups, tables, lengths_of, tokens_of, panels, prior=None):
     count, depth = tokens_of[0].shape
     per_home, rank, _ = tables[2].shape
     chunks = 4
@@ -145,23 +141,46 @@
     smem, vmem = pl.BlockSpec(memory_space=pltpu.SMEM), pl.BlockSpec(memory_space=pltpu.VMEM)
     copied = len(tokens_of) + len(panels)
     return pl.pallas_call(
-        functools.partial(score_kernel, plan, groups, kept, chunks, bool(prior), per_home),
-        out_shape=[
-            jax.ShapeDtypeStruct((rank, len(plan) * count), jnp.float32),
-            jax.ShapeDtypeStruct((len(kept) * rank, columns), panels[0].dtype),
-        ],
+        functools.partial(score_kernel, plan, groups, chunks, bool(prior), per_home),
+        out_shape=jax.ShapeDtypeStruct((rank, len(plan) * count), jnp.float32),
         in_specs=[smem] * (2 + len(lengths_of))
         + [vmem] * len(prior)
         + [pl.BlockSpec(memory_space=pl.ANY)] * copied,
-        out_specs=[vmem, vmem],
+        out_specs=vmem,
         scratch_shapes=[
             pltpu.VMEM((len(tokens_of), count, depth), tokens_of[0].dtype),
             pltpu.VMEM((len(panels) * rank, depth), tokens_of[0].dtype),
-            pltpu.SemaphoreType.DMA((chunks, copied + len(kept))),
+            pltpu.SemaphoreType.DMA((chunks, copied)),
         ],
         compiler_params=pltpu.CompilerParams(vmem_limit_bytes=40 << 20),
         cost_estimate=pl.CostEstimate(flops=0, bytes_accessed=0, transcendentals=0),
     )(tables[0], tables[1], *lengths_of, *prior, *tokens_of, *panels)
+
+
+def gather_kernel(*refs):
+    blocks, out, sems = refs[:-2], refs[-2], refs[-1]
+    columns = out.shape[1]
+    copies, first = [], 0
+    for n, block in enumerate(blocks):
+        rows, width = block.shape
+        source = block.at[:, pl.ds(width - columns, columns)]
+        copies.append(pltpu.make_async_copy(source, out.at[pl.ds(first, rows)], sems.at[n]))
+        copies[-1].start()
+        first += rows
+    for copy in copies:
+        copy.wait()
+
+
+def gather(blocks, columns):
+    rows = sum(block.shape[0] for block in blocks)
+    return pl.pallas_call(
+        gather_kernel,
+        out_shape=jax.ShapeDtypeStruct((rows, columns), blocks[0].dtype),
+        in_specs=[pl.BlockSpec(memory_space=pl.ANY)] * len(blocks),
+        out_specs=pl.BlockSpec(memory_space=pltpu.VMEM),
+        scratch_shapes=[pltpu.SemaphoreType.DMA((len(blocks),))],
+        cost_estimate=pl.CostEstimate(flops=0, bytes_accessed=0, transcendentals=0),
+    )(*blocks)
 
 
 def base_kernel(chunks, tokens_ref, weight_ref, *refs):
@@ -216,38 +235,39 @@
 
 
 def finish_kernel(pieces, added, came, bases, per_home, home_ref, fetch_ref, lengths_ref, *refs):
-    scores, others = refs[:added], refs[added : added + came]
-    base, refs = refs[added + came : added + came + bases], refs[added + came + bases :]
-    expand_ref, arrays, (out, held, sems) = refs[0], refs[1:-3], refs[-3:]
+    scores, refs = refs[: added + came], refs[added + came :]
+    base, expand_ref, refs = refs[:bases], refs[bases], refs[bases + 1 :]
+    arrays, (out, held, held_scores, held_base, sems) = refs[:-5], refs[-5:]
     me = lax.axis_index("rep")
     count, columns = out.shape
     rank = scores[0].shape[0]
     left = pl.multiple_of(lax.axis_index("tp") * columns, 128)
     slot = slot_for(me, me, per_home, home_ref, fetch_ref)
-    copies = []
+    pairs = [(x.at[:, pl.ds(0, count)], held_scores.at[n]) for n, x in enumerate(scores)]
+    pairs += [(x, held_base.at[n]) for n, x in enumerate(base)]
     for n, (at, row, _) in enumerate(pieces):
         if at is None:
             source = expand_ref.at[slot, :, pl.ds(left, columns)]
         else:
             source = arrays[at].at[pl.ds(row, rank), pl.ds(arrays[at].shape[1] - columns, columns)]
-        copies.append(pltpu.make_async_copy(source, held.at[pl.ds(n * rank, rank)], sems.at[n]))
+        pairs.append((source, held.at[pl.ds(n * rank, rank)]))
+    copies = []
+    for n, (source, target) in enumerate(pairs):
+        copies.append(pltpu.make_async_copy(source, target, sems.at[n]))
         copies[-1].start()
     row_steps = steps_of_rows(lengths_ref, count, me, per_home, home_ref, fetch_ref)
-    shrink = scores[0][:, pl.ds(0, count)]
-    for x in scores[1:]:
-        shrink = shrink + x[:, pl.ds(0, count)]
-    for x in others:
-        shrink = shrink + x[...]
-    shrink = adapter_scale * shrink
-    high = shrink.astype(jnp.bfloat16).astype(jnp.float32)
-    terms = [high, shrink - high]
     masks = [row_steps == by_part(group) for _, _, group in pieces]
     for copy in copies:
         copy.wait()
-    total = base[0][...]
-    for x in base[1:]:
-        total = total + x[...]
-    for term in terms:
+    shrink = held_scores[0]
+    for n in range(1, added + came):
+        shrink = shrink + held_scores[n]
+    shrink = adapter_scale * shrink
+    high = shrink.astype(jnp.bfloat16).astype(jnp.float32)
+    total = held_base[0]
+    for n in range(1, bases):
+        total = total + held_base[n]
+    for term in (high, shrink - high):
         wide = jnp.concatenate([jnp.where(mask, term, 0.0) for mask in masks], axis=0)
         total = total + lax.dot_general(
             wide.astype(jnp.bfloat16),
@@ -261,26 +281,22 @@
 def finish(pieces, tables, lengths, scores, others, base, arrays):
     count, columns = base[0].shape
     per_home, rank, _ = tables[2].shape
-    smem, vmem = pl.BlockSpec(memory_space=pltpu.SMEM), pl.BlockSpec(memory_space=pltpu.VMEM)
-    height = len(pieces) * rank
+    smem, anywhere = pl.BlockSpec(memory_space=pltpu.SMEM), pl.BlockSpec(memory_space=pl.ANY)
+    copied = list(scores) + list(others) + list(base)
     return pl.pallas_call(
         functools.partial(finish_kernel, pieces, len(scores), len(others), len(base), per_home),
         out_shape=jax.ShapeDtypeStruct((count, columns), jnp.bfloat16),
-        in_specs=[smem] * 3
-        + [vmem] * (len(scores) + len(others) + len(base))
-        + [pl.BlockSpec(memory_space=pl.ANY)] * (1 + len(arrays)),
-        out_specs=vmem,
+        in_specs=[smem] * 3 + [anywhere] * (len(copied) + 1 + len(arrays)),
+        out_specs=pl.BlockSpec(memory_space=pltpu.VMEM),
         scratch_shapes=[
-            pltpu.VMEM((height, columns), jnp.bfloat16),
-            pltpu.SemaphoreType.DMA((len(pieces),)),
+            pltpu.VMEM((len(pieces) * rank, columns), jnp.bfloat16),
+            pltpu.VMEM((len(scores) + len(others), rank, count), jnp.float32),
+            pltpu.VMEM((len(base), count, columns), jnp.float32),
+            pltpu.SemaphoreType.DMA((len(copied) + len(pieces),)),
         ],
         compiler_params=pltpu.CompilerParams(vmem_limit_bytes=24 << 20),
-        cost_estimate=pl.CostEstimate(
-            flops=4 * count * columns * height,
-            bytes_accessed=2 * columns * height + 6 * count * columns,
-            transcendentals=0,
-        ),
-    )(tables[0], tables[1], lengths, *scores, *others, *base, tables[3], *arrays)
+        cost_estimate=pl.CostEstimate(flops=0, bytes_accessed=0, transcendentals=0),
+    )(tables[0], tables[1], lengths, *copied, tables[3], *arrays)
 
 
 def on_device(tokens, base_weight, shrink_panels, expand_panels, adapter_home, fetch_list, seg_len):
@@ -333,30 +349,19 @@
     last, last_group, own_group = recv[len(far) - 1], far[-1], (0,) * parts
 
     count = len(early)
-    first, sent = score(
-        [tuple(range(count + len(solo) + 1))],
+    sent = gather(early, columns)
+    passed = [shift_parts(sent, shift) for shift in range(1, parts)]
+    first = score(
+        [tuple(range(count + len(solo) + 1))] + [tuple(range(count))] * (parts - 1),
         early_groups + solo + [own_group],
-        tuple(range(count)),
         tables,
-        columns,
-        lengths_of[:1],
-        [tokens],
+        lengths_of,
+        tokens_of,
         early + solo_recv + [panels],
     )
-    passed = [shift_parts(sent, shift) for shift in range(1, parts)]
-    base, first, passed, tokens_of[1:], last = tie((base, first, passed, tokens_of[1:], last))
-    scores, sent = score(
-        [(0,)] + [tuple(range(count + 1))] * (parts - 1),
-        [last_group] + early_groups,
-        (0,),
-        tables,
-        columns,
-        lengths_of,
-        tokens_of,
-        [last] + early,
-        first,
-    )
-    last_passed = [shift_parts(sent, shift) for shift in range(1, parts)]
+    base, first, passed, last = tie((base, first, passed, last))
+    scores = score([(0,)] * parts, [last_group], tables, lengths_of, tokens_of, [last], first)
+    last_passed = [shift_parts(gather([last], columns), shift) for shift in range(1, parts)]
     halves = [scores] + [shift_cores(scores, shift) for shift in range(1, cores)]
     whole = halves[0]
     for x in halves[1:]:

time: 74.3 us -> 86.7 us (1.17)
  the two profiles are of different devices: /device:TPU:0 before, /device:TPU:26 now
where the time goes in v14:
time: 86.7 us; the launch traced here: 86.2 us
  waiting for transfers between devices  41.9 us (48%)
  Pallas kernels  21.6 us (25%)
  starting transfers between devices  11.6 us (13%)
  local copies, waits for them, and re-layouts  10.8 us (12%)
    ppermute x4, waiting for transfers between devices, hop(): return lax.ppermute(x, ('parts', 'rep'), pairs)  34.6 us
    unnamed x30, local copies, waits for them, and re-layouts  10.8 us
    ppermute x5, waiting for transfers between devices, shift_parts(): lax.ppermute(x, 'parts', [(i, (i + shift) % parts) for i in range(parts)])  7.34 us
    pallas_call x2, Pallas kernels, score(): pl.pallas_call(functools.partial(score_kernel, plan, groups, chunks, bool...  7.24 us
    ppermute x4, starting transfers between devices, hop(): return lax.ppermute(x, ('parts', 'rep'), pairs)  6.65 us
    ppermute x5, starting transfers between devices, shift_parts(): lax.ppermute(x, 'parts', [(i, (i + shift) % parts) for i in range(parts)])  4.87 us
    pallas_call x1, Pallas kernels, base_terms(): pl.pallas_call(functools.partial(base_kernel, chunks), out_shape=[jax.Sha...  4.72 us
    pallas_call x1, Pallas kernels, pack(): pl.pallas_call(functools.partial(pack_kernel, groups), out_shape=[jax.Sha...  3.5 us
  transfers between devices with their start and end apart: 11, of which 4 were waited for; matrix products, arithmetic and copies ran while one was open for 0% of the time, Pallas kernels for 13%

profile of v14, /device:TPU:26, one launch (start us, length us, event | category | flops | bytes accessed | tf_op | source)
XLA Modules:
  0.0 86.2 jit_solution(811616552814745372)
XLA Ops:
  0.0 3.5 %shard_map.73 = (bf16[64,4608]{1,0:T(8,128)(2,1)}, bf16[64,4608]{1,0:T(8,128)(2,1)}, bf16[64,4608]{1,0:T(8,128)(2,1)}, bf16[64,4608]{1,0:T(8,128)(2,1)}) custom-call(s32[32]{0:T(128)} %home_ref.7, s32[8,8]{1,0:T(8,128)} %fetch_ref.7, bf16[4,64,4096]{2,1,0:T(8,128)(2,1)} %bitcast.1, bf16[4,64,1024]{2,1,0:T(8,128)(2,1)} %refs_5_.1), custom_call_target="tpu_custom_call" | custom-call | tf_op jit(solution)/shard_map/pallas_call | solution.py:78
  3.5 0.0 copy-start.12
  3.5 0.0 copy-start.14
  3.5 0.0 copy-start.13
  3.6 0.6 collective-permute-start.4
  4.2 1.4 %collective-permute-start = (bf16[64,4608]{1,0:T(8,128)(2,1)}, bf16[64,4608]{1,0:T(8,128)(2,1)S(1)}, u32[]{:S(2)}, u32[]{:S(2)}) collective-permute-start(bf16[64,4608]{1,0:T(8,128)(2,1)} %get-tuple-element.31), channel_id=1, source_target_pairs={{0,4},{2,6},{4,0},{6,2},{8,12},{10,14},{12,8},{14,10},{16,22},{18,... | collective-permute-start | bytes 1769480 | tf_op jit(solution)/shard_map/ppermute | solution.py:327
  5.6 1.3 %collective-permute-start.2 = (bf16[64,4608]{1,0:T(8,128)(2,1)}, bf16[64,4608]{1,0:T(8,128)(2,1)S(1)}, u32[]{:S(2)}, u32[]{:S(2)}) collective-permute-start(bf16[64,4608]{1,0:T(8,128)(2,1)} %get-tuple-element.37), channel_id=1, source_target_pairs={{0,8},{2,10},{4,12},{6,14},{8,0},{10,2},{12,4},{14,6},{16,28},{18,... | collective-permute-start | bytes 1769480 | tf_op jit(solution)/shard_map/ppermute | solution.py:327
  6.9 0.5 collective-permute-start.5
  7.4 3.4 %collective-permute-start.7 = (bf16[64,4608]{1,0:T(8,128)(2,1)}, bf16[64,4608]{1,0:T(8,128)(2,1)}, u32[]{:S(2)}, u32[]{:S(2)}) collective-permute-start(bf16[64,4608]{1,0:T(8,128)(2,1)} %get-tuple-element.43), channel_id=1, source_target_pairs={{0,10},{2,8},{4,14},{6,12},{8,2},{10,0},{12,6},{14,4},{16,30},{18,... | collective-permute-start | bytes 1769480 | tf_op jit(solution)/shard_map/ppermute | solution.py:327
  10.8 34.6 %collective-permute-done.refs_4_.refs_0_.refs_6_ = bf16[64,4608]{1,0:T(8,128)(2,1)S(1)} collective-permute-done((bf16[64,4608]{1,0:T(8,128)(2,1)}, bf16[64,4608]{1,0:T(8,128)(2,1)S(1)}, u32[]{:S(2)}, u32[]{:S(2)}) %collective-permute-start) | collective-permute-done | bytes 589856 | tf_op jit(solution)/shard_map/ppermute | solution.py:327
  45.4 3.4 %copy-done.1 = bf16[4096,1024]{1,0:T(8,128)(2,1)S(1)} copy-done((bf16[4096,1024]{1,0:T(8,128)(2,1)S(1)}, bf16[4096,1024]{1,0:T(8,128)(2,1)}, u32[]{:S(2)}) %copy-start.1) | copy-done | bytes 8388632
  48.8 4.7 %shard_map.74 = (f32[256,512]{1,0:T(8,128)S(1)}, f32[256,512]{1,0:T(8,128)}) custom-call(bf16[256,4096]{1,0:T(8,128)(2,1)S(1)} %copy-done, bf16[4096,1024]{1,0:T(8,128)(2,1)S(1)} %copy-done.1), custom_call_target="tpu_custom_call" | custom-call | tf_op jit(solution)/shard_map/pallas_call | solution.py:221
  53.5 0.8 copy-done.10
  54.4 0.8 copy-done.6
  55.2 1.5 %shard_map.76 = bf16[128,512]{1,0:T(8,128)(2,1)} custom-call(bf16[64,4608]{1,0:T(8,128)(2,1)} %copy-done.3, bf16[64,4608]{1,0:T(8,128)(2,1)} %copy-done.6), custom_call_target="tpu_custom_call" | custom-call | tf_op jit(solution)/shard_map/pallas_call | solution.py:176
  56.7 0.1 collective-permute-start.6
  56.8 2.0 %collective-permute-start.1 = (s32[1,8]{1,0:T(1,128)S(1)}, s32[1,8]{1,0:T(1,128)S(1)}, u32[]{:S(2)}, u32[]{:S(2)}) collective-permute-start(s32[1,8]{1,0:T(1,128)S(1)} %copy-done.14), channel_id=1, source_target_pairs={{0,16},{16,0},{1,17},{17,1},{2,18},{18,2},{3,19},{19,3},{4,20},{20... | collective-permute-start | bytes 104 | tf_op jit(solution)/shard_map/ppermute | solution.py:330
  58.8 3.3 %collective-permute-done.1.refs_1_ = s32[1,8]{1,0:T(1,128)S(1)} collective-permute-done((s32[1,8]{1,0:T(1,128)S(1)}, s32[1,8]{1,0:T(1,128)S(1)}, u32[]{:S(2)}, u32[]{:S(2)}) %collective-permute-start.1) | collective-permute-done | bytes 64 | tf_op jit(solution)/shard_map/ppermute | solution.py:330
  62.2 1.6 %copy-done.2 = bf16[4,4096,64]{1,2,0:T(8,128)(2,1)S(1)} copy-done((bf16[4,4096,64]{1,2,0:T(8,128)(2,1)S(1)}, bf16[4,4096,64]{1,2,0:T(8,128)(2,1)}, u32[]{:S(2)}) %copy-start.2) | copy-done | bytes 2097176
  63.8 1.1 %copy-done.4 = bf16[64,4608]{1,0:T(8,128)(2,1)S(1)} copy-done((bf16[64,4608]{1,0:T(8,128)(2,1)S(1)}, bf16[64,4608]{1,0:T(8,128)(2,1)}, u32[]{:S(2)}) %copy-start.4) | copy-done | bytes 589848
  64.8 1.1 %copy-done.7 = bf16[64,4608]{1,0:T(8,128)(2,1)S(1)} copy-done((bf16[64,4608]{1,0:T(8,128)(2,1)S(1)}, bf16[64,4608]{1,0:T(8,128)(2,1)}, u32[]{:S(2)}) %copy-start.7) | copy-done | bytes 589848
  65.9 3.8 %shard_map.75.refs_2_ = f32[64,512]{1,0:T(8,128)S(1)} custom-call(s32[32]{0:T(128)S(1)} %copy-done.13, s32[8,8]{1,0:T(8,128)S(1)} %copy-done.12, s32[1,8]{1,0:T(1,128)S(1)} %copy-done.14, s32[1,8]{1,0:T(1,128)S(1)} %collective-permute-done.1.refs_1_, bf16[256,4096]{1,0:T(8,128)(2,1)S(1)} %copy-done, ...), custom_call_target="tpu_custom_call" | custom-call | tf_op jit(solution)/shard_map/pallas_call | solution.py:143
  69.7 3.5 %shard_map.77.refs_0_ = f32[64,512]{1,0:T(8,128)S(1)} custom-call(s32[32]{0:T(128)S(1)} %copy-done.13, s32[8,8]{1,0:T(8,128)S(1)} %copy-done.12, s32[1,8]{1,0:T(1,128)S(1)} %copy-done.14, s32[1,8]{1,0:T(1,128)S(1)} %collective-permute-done.1.refs_1_, f32[64,512]{1,0:T(8,128)S(1)} %shard_map.75.refs_2_, bf16[256,4096]{1,0:T(8,128)(2,1)S(1)} %copy-done, ...), custom_call_target="tpu_custom_call" | custom-call | tf_op jit(solution)/shard_map/pallas_call | solution.py:143
  73.2 0.1 collective-permute-start.8
  73.3 1.5 %shard_map.78 = bf16[64,512]{1,0:T(8,128)(2,1)} custom-call(bf16[64,4608]{1,0:T(8,128)(2,1)} %collective-permute-done.7.refs_5_.refs_0_.refs_9_), custom_call_target="tpu_custom_call" | custom-call | tf_op jit(solution)/shard_map/pallas_call | solution.py:176
  74.8 0.3 collective-permute-start.10
  75.1 1.8 %collective-permute-start.9 = (f32[64,256]{1,0:T(8,128)S(1)}, f32[64,256]{1,0:T(8,128)S(1)}, u32[]{:S(2)}, u32[]{:S(2)}) collective-permute-start(f32[64,256]{1,0:T(8,128)S(1)} %slice_add_fusion), channel_id=1, source_target_pairs={{0,16},{16,0},{1,17},{17,1},{2,18},{18,2},{3,19},{19,3},{4,20},{20... | collective-permute-start | bytes 196616 | tf_op jit(solution)/shard_map/ppermute | solution.py:330
  76.9 3.0 %collective-permute-done.10.refs_11_ = bf16[64,512]{1,0:T(8,128)(2,1)S(1)} collective-permute-done((bf16[64,512]{1,0:T(8,128)(2,1)}, bf16[64,512]{1,0:T(8,128)(2,1)S(1)}, u32[]{:S(2)}, u32[]{:S(2)}) %collective-permute-start.10) | collective-permute-done | bytes 65568 | tf_op jit(solution)/shard_map/ppermute | solution.py:330
  79.9 1.0 %collective-permute-done.9.refs_2_ = f32[64,256]{1,0:T(8,128)S(1)} collective-permute-done((f32[64,256]{1,0:T(8,128)S(1)}, f32[64,256]{1,0:T(8,128)S(1)}, u32[]{:S(2)}, u32[]{:S(2)}) %collective-permute-start.9) | collective-permute-done | bytes 65568 | tf_op jit(solution)/shard_map/ppermute | solution.py:330
  81.0 1.0 %copy-done.9 = bf16[4,64,1024]{2,1,0:T(8,128)(2,1)S(1)} copy-done((bf16[4,64,1024]{2,1,0:T(8,128)(2,1)S(1)}, bf16[4,64,1024]{2,1,0:T(8,128)(2,1)}, u32[]{:S(2)}) %copy-start.9) | copy-done | bytes 524312
  82.0 1.0 %copy-done.11 = f32[256,512]{1,0:T(8,128)S(1)} copy-done((f32[256,512]{1,0:T(8,128)S(1)}, f32[256,512]{1,0:T(8,128)}, u32[]{:S(2)}) %copy-start.11) | copy-done | bytes 524312
  83.0 3.1 %shard_map.79 = bf16[256,512]{1,0:T(8,128)(2,1)} custom-call(s32[32]{0:T(128)S(1)} %copy-done.13, s32[8,8]{1,0:T(8,128)S(1)} %copy-done.12, s32[1,8]{1,0:T(1,128)S(1)} %copy-done.14, f32[64,512]{1,0:T(8,128)S(1)} %shard_map.77.refs_0_, f32[64,512]{1,0:T(8,128)S(1)} %collective-permute-done.8.refs_1_, f32[64,256]{1,0:T(8,128)S(1)} %collective-permute-done.9.refs_2_, ...), custom_call_target="tpu_custom_call" | custom-call | tf_op jit(solution)/shard_map/pallas_call | solution.py:286
  (28 shorter events, 0.1 us)
Async XLA Ops:
  0.0 3.5 %copy-start = (bf16[256,4096]{1,0:T(8,128)(2,1)S(1)}, bf16[256,4096]{1,0:T(8,128)(2,1)}, u32[]{:S(2)}) copy-start(bf16[256,4096]{1,0:T(8,128)(2,1)} %refs_3_) | copy-start | bytes 6291460
  3.5 58.7 %copy-start.12 = (s32[8,8]{1,0:T(8,128)S(1)}, s32[8,8]{1,0:T(8,128)}, u32[]{:S(2)}) copy-start(s32[8,8]{1,0:T(8,128)} %fetch_ref.7) | copy-start | bytes 772
  3.5 53.3 %copy-start.14 = (s32[1,8]{1,0:T(1,128)S(1)}, s32[1,8]{1,0:T(1,128)}, u32[]{:S(2)}) copy-start(s32[1,8]{1,0:T(1,128)} %lengths_ref) | copy-start | bytes 100
  3.5 58.6 %copy-start.13 = (s32[32]{0:T(128)S(1)}, s32[32]{0:T(128)}, u32[]{:S(2)}) copy-start(s32[32]{0:T(128)} %home_ref.7) | copy-start | bytes 388
  3.6 58.6 %collective-permute-start.4 = (bf16[256,4096]{1,0:T(8,128)(2,1)S(1)}, bf16[256,4096]{1,0:T(8,128)(2,1)}, u32[]{:S(2)}, u32[]{:S(2)}) collective-permute-start(bf16[256,4096]{1,0:T(8,128)(2,1)S(1)} %copy-done), channel_id=1, source_target_pairs={{0,16},{16,0},{1,17},{17,1},{2,18},{18,2},{3,19},{19,3},{4,20},{20... | collective-permute-start | bytes 6291464 | tf_op jit(solution)/shard_map/ppermute | solution.py:330
  4.2 41.2 %collective-permute-start = (bf16[64,4608]{1,0:T(8,128)(2,1)}, bf16[64,4608]{1,0:T(8,128)(2,1)S(1)}, u32[]{:S(2)}, u32[]{:S(2)}) collective-permute-start(bf16[64,4608]{1,0:T(8,128)(2,1)} %get-tuple-element.31), channel_id=1, source_target_pairs={{0,4},{2,6},{4,0},{6,2},{8,12},{10,14},{12,8},{14,10},{16,22},{18,... | collective-permute-start | bytes 1769480 | tf_op jit(solution)/shard_map/ppermute | solution.py:327
  5.6 48.8 %collective-permute-start.2 = (bf16[64,4608]{1,0:T(8,128)(2,1)}, bf16[64,4608]{1,0:T(8,128)(2,1)S(1)}, u32[]{:S(2)}, u32[]{:S(2)}) collective-permute-start(bf16[64,4608]{1,0:T(8,128)(2,1)} %get-tuple-element.37), channel_id=1, source_target_pairs={{0,8},{2,10},{4,12},{6,14},{8,0},{10,2},{12,4},{14,6},{16,28},{18,... | collective-permute-start | bytes 1769480 | tf_op jit(solution)/shard_map/ppermute | solution.py:327
  6.9 49.9 %collective-permute-start.5 = (bf16[64,4608]{1,0:T(8,128)(2,1)}, bf16[64,4608]{1,0:T(8,128)(2,1)}, u32[]{:S(2)}, u32[]{:S(2)}) collective-permute-start(bf16[64,4608]{1,0:T(8,128)(2,1)} %get-tuple-element.42), channel_id=1, source_target_pairs={{0,2},{2,0},{4,6},{6,4},{8,10},{10,8},{12,14},{14,12},{16,18},{18,... | collective-permute-start | bytes 1769480 | tf_op jit(solution)/shard_map/ppermute | solution.py:327
  7.4 62.3 %collective-permute-start.7 = (bf16[64,4608]{1,0:T(8,128)(2,1)}, bf16[64,4608]{1,0:T(8,128)(2,1)}, u32[]{:S(2)}, u32[]{:S(2)}) collective-permute-start(bf16[64,4608]{1,0:T(8,128)(2,1)} %get-tuple-element.43), channel_id=1, source_target_pairs={{0,10},{2,8},{4,14},{6,12},{8,2},{10,0},{12,6},{14,4},{16,30},{18,... | collective-permute-start | bytes 1769480 | tf_op jit(solution)/shard_map/ppermute | solution.py:327
  45.4 3.4 %copy-start.1 = (bf16[4096,1024]{1,0:T(8,128)(2,1)S(1)}, bf16[4096,1024]{1,0:T(8,128)(2,1)}, u32[]{:S(2)}) copy-start(bf16[4096,1024]{1,0:T(8,128)(2,1)} %weight_ref) | copy-start | bytes 25165828
  48.8 4.7 %copy-start.3 = (bf16[64,4608]{1,0:T(8,128)(2,1)}, bf16[64,4608]{1,0:T(8,128)(2,1)S(1)}, u32[]{:S(2)}) copy-start(bf16[64,4608]{1,0:T(8,128)(2,1)S(1)} %collective-permute-done.refs_4_.refs_0_.refs_6_) | copy-start | bytes 1769476
  53.5 0.8 copy-start.10
  54.4 0.8 copy-start.6
  54.4 15.4 %collective-permute-start.3 = (f32[256,512]{1,0:T(8,128)}, f32[256,512]{1,0:T(8,128)}, u32[]{:S(2)}, u32[]{:S(2)}) collective-permute-start(f32[256,512]{1,0:T(8,128)} %get-tuple-element.39), channel_id=1, source_target_pairs={{0,1},{1,0},{2,3},{3,2},{4,5},{5,4},{6,7},{7,6},{8,9},{9,8},{10,11... | collective-permute-start | bytes 1572872 | tf_op jit(solution)/shard_map/ppermute | solution.py:333
  56.7 13.0 %collective-permute-start.6 = (bf16[128,512]{1,0:T(8,128)(2,1)}, bf16[128,512]{1,0:T(8,128)(2,1)S(1)}, u32[]{:S(2)}, u32[]{:S(2)}) collective-permute-start(bf16[128,512]{1,0:T(8,128)(2,1)} %shard_map.76), channel_id=1, source_target_pairs={{0,16},{16,0},{1,17},{17,1},{2,18},{18,2},{3,19},{19,3},{4,20},{20... | collective-permute-start | bytes 393224 | tf_op jit(solution)/shard_map/ppermute | solution.py:330
  56.8 5.3 %collective-permute-start.1 = (s32[1,8]{1,0:T(1,128)S(1)}, s32[1,8]{1,0:T(1,128)S(1)}, u32[]{:S(2)}, u32[]{:S(2)}) collective-permute-start(s32[1,8]{1,0:T(1,128)S(1)} %copy-done.14), channel_id=1, source_target_pairs={{0,16},{16,0},{1,17},{17,1},{2,18},{18,2},{3,19},{19,3},{4,20},{20... | collective-permute-start | bytes 104 | tf_op jit(solution)/shard_map/ppermute | solution.py:330
  62.2 1.6 %copy-start.2 = (bf16[4,4096,64]{1,2,0:T(8,128)(2,1)S(1)}, bf16[4,4096,64]{1,2,0:T(8,128)(2,1)}, u32[]{:S(2)}) copy-start(bf16[4,4096,64]{1,2,0:T(8,128)(2,1)} %param.9) | copy-start | bytes 6291460
  63.8 1.1 %copy-start.4 = (bf16[64,4608]{1,0:T(8,128)(2,1)S(1)}, bf16[64,4608]{1,0:T(8,128)(2,1)}, u32[]{:S(2)}) copy-start(bf16[64,4608]{1,0:T(8,128)(2,1)} %copy-done.3) | copy-start | bytes 1769476
  64.8 1.1 %copy-start.7 = (bf16[64,4608]{1,0:T(8,128)(2,1)S(1)}, bf16[64,4608]{1,0:T(8,128)(2,1)}, u32[]{:S(2)}) copy-start(bf16[64,4608]{1,0:T(8,128)(2,1)} %copy-done.6) | copy-start | bytes 1769476
  69.7 11.3 %copy-start.5 = (bf16[64,4608]{1,0:T(8,128)(2,1)S(1)}, bf16[64,4608]{1,0:T(8,128)(2,1)}, u32[]{:S(2)}) copy-start(bf16[64,4608]{1,0:T(8,128)(2,1)} %copy-done.3) | copy-start | bytes 1769476
  69.7 11.3 %copy-start.8 = (bf16[64,4608]{1,0:T(8,128)(2,1)S(1)}, bf16[64,4608]{1,0:T(8,128)(2,1)}, u32[]{:S(2)}) copy-start(bf16[64,4608]{1,0:T(8,128)(2,1)} %copy-done.6) | copy-start | bytes 1769476
  73.2 1.9 %collective-permute-start.8 = (f32[64,512]{1,0:T(8,128)S(1)}, f32[64,512]{1,0:T(8,128)S(1)}, u32[]{:S(2)}, u32[]{:S(2)}) collective-permute-start(f32[64,512]{1,0:T(8,128)S(1)} %shard_map.77.refs_0_), channel_id=1, source_target_pairs={{0,1},{1,0},{2,3},{3,2},{4,5},{5,4},{6,7},{7,6},{8,9},{9,8},{10,11... | collective-permute-start | bytes 393224 | tf_op jit(solution)/shard_map/ppermute | solution.py:333
  74.8 5.2 %collective-permute-start.10 = (bf16[64,512]{1,0:T(8,128)(2,1)}, bf16[64,512]{1,0:T(8,128)(2,1)S(1)}, u32[]{:S(2)}, u32[]{:S(2)}) collective-permute-start(bf16[64,512]{1,0:T(8,128)(2,1)} %shard_map.78), channel_id=1, source_target_pairs={{0,16},{16,0},{1,17},{17,1},{2,18},{18,2},{3,19},{19,3},{4,20},{20... | collective-permute-start | bytes 196616 | tf_op jit(solution)/shard_map/ppermute | solution.py:330
  75.1 5.8 %collective-permute-start.9 = (f32[64,256]{1,0:T(8,128)S(1)}, f32[64,256]{1,0:T(8,128)S(1)}, u32[]{:S(2)}, u32[]{:S(2)}) collective-permute-start(f32[64,256]{1,0:T(8,128)S(1)} %slice_add_fusion), channel_id=1, source_target_pairs={{0,16},{16,0},{1,17},{17,1},{2,18},{18,2},{3,19},{19,3},{4,20},{20... | collective-permute-start | bytes 196616 | tf_op jit(solution)/shard_map/ppermute | solution.py:330
  80.9 1.0 %copy-start.9 = (bf16[4,64,1024]{2,1,0:T(8,128)(2,1)S(1)}, bf16[4,64,1024]{2,1,0:T(8,128)(2,1)}, u32[]{:S(2)}) copy-start(bf16[4,64,1024]{2,1,0:T(8,128)(2,1)} %refs_5_.1) | copy-start | bytes 1572868
  82.0 1.0 %copy-start.11 = (f32[256,512]{1,0:T(8,128)S(1)}, f32[256,512]{1,0:T(8,128)}, u32[]{:S(2)}) copy-start(f32[256,512]{1,0:T(8,128)} %copy-done.10) | copy-start | bytes 1572868

commit v15 on v13

--- a/solution.py
+++ b/solution.py
@@ -43,9 +43,10 @@
     return result
 
 
-def pack_kernel(groups, home_ref, fetch_ref, shrink_ref, expand_ref, *refs):
+def pack_kernel(groups, home_ref, fetch_ref, lengths_ref, shrink_ref, expand_ref, *refs):
     count = len(groups)
-    outs, held, in_sems, out_sems = refs[:count], refs[count], refs[count + 1], refs[count + 2]
+    outs, steps_out, refs = refs[:count], refs[count], refs[count + 1 :]
+    held, in_sems, out_sems = refs
     me = lax.axis_index("rep")
     per_home, _, depth = shrink_ref.shape
     columns = expand_ref.shape[2] // lax.axis_size("tp")
@@ -63,6 +64,8 @@
             copy.start()
             leave = pltpu.make_async_copy(target, outs[at].at[:, pl.ds(start, size)], out_sems.at[at, n])
             arriving.append((copy, leave))
+    steps = steps_of_rows(lengths_ref, steps_out.shape[1], me, per_home, home_ref, fetch_ref)
+    steps_out[...] = jnp.broadcast_to(steps, steps_out.shape)
     for copy, leave in arriving:
         copy.wait()
         leave.start()
@@ -70,34 +73,41 @@
         leave.wait()
 
 
-def pack(groups, columns, adapter_home, fetch_list, panels, expand_panels):
+def pack(groups, columns, count, lengths, adapter_home, fetch_list, panels, expand_panels):
     rank, depth = panels.shape[1:]
     shape = (rank, depth + columns)
     cuts = 2
     return list(
         pl.pallas_call(
             functools.partial(pack_kernel, groups),
-            out_shape=[jax.ShapeDtypeStruct(shape, panels.dtype)] * len(groups),
-            in_specs=[pl.BlockSpec(memory_space=pltpu.SMEM)] * 2 + [pl.BlockSpec(memory_space=pl.ANY)] * 2,
-            out_specs=[pl.BlockSpec(memory_space=pl.ANY)] * len(groups),
+            out_shape=[jax.ShapeDtypeStruct(shape, panels.dtype)] * len(groups)
+            + [jax.ShapeDtypeStruct((8, count), jnp.int32)],
+            in_specs=[pl.BlockSpec(memory_space=pltpu.SMEM)] * 3 + [pl.BlockSpec(memory_space=pl.ANY)] * 2,
+            out_specs=[pl.BlockSpec(memory_space=pl.ANY)] * len(groups)
+            + [pl.BlockSpec(memory_space=pltpu.VMEM)],
             scratch_shapes=[pltpu.VMEM((len(groups),) + shape, panels.dtype)]
             + [pltpu.SemaphoreType.DMA((len(groups), cuts + 1))] * 2,
             compiler_params=pltpu.CompilerParams(vmem_limit_bytes=56 << 20),
             cost_estimate=pl.CostEstimate(flops=0, bytes_accessed=0, transcendentals=0),
-        )(adapter_home, fetch_list, panels, expand_panels)
-    )
-
-
-def score_kernel(plan, groups, kept, chunks, has_prior, per_home, home_ref, fetch_ref, *refs):
+        )(adapter_home, fetch_list, lengths, panels, expand_panels)
+    )
+
+
+def score_kernel(plan, groups, kept, own, chunks, has_prior, *refs):
     sets, many = len(plan), len(groups)
-    lengths, refs = refs[:sets], refs[sets:]
+    tables, refs = (refs[:2], refs[2:]) if own else (None, refs)
+    row_steps, refs = refs[:sets], refs[sets:]
     prior, refs = (refs[0], refs[1:]) if has_prior else (None, refs)
-    tokens, panels = refs[:sets], refs[sets : sets + many]
-    out, out_expand, held_tokens, held_panels, sems = refs[sets + many :]
-    me = lax.axis_index("rep")
+    tokens, panels, refs = refs[:sets], refs[sets : sets + many], refs[sets + many :]
+    expand_ref, refs = (refs[0], refs[1:]) if own else (None, refs)
+    out, out_expand, refs = refs[0], refs[1], refs[2:]
+    out_own, refs = (refs[0], refs[1:]) if own else (None, refs)
+    held_tokens, held_panels, sems = refs
     rank, count, depth = out.shape[0], held_tokens.shape[1], held_tokens.shape[2]
-    width = depth // chunks
-    slot = slot_for(me, me, per_home, home_ref, fetch_ref)
+    width, columns = depth // chunks, out_expand.shape[1]
+    if own:
+        me = lax.axis_index("rep")
+        slot = slot_for(me, me, panels[-1].shape[0], *tables)
     copies = []
     for c in range(chunks):
         cols = pl.ds(c * width, width)
@@ -108,14 +118,16 @@
         pairs += [(ref.at[:, cols], held_tokens.at[n, :, cols]) for n, ref in enumerate(tokens)]
         if c == chunks - 1:
             pairs += [
-                (panels[n].at[:, pl.ds(depth, out_expand.shape[1])], out_expand.at[pl.ds(i * rank, rank)])
+                (panels[n].at[:, pl.ds(depth, columns)], out_expand.at[pl.ds(i * rank, rank)])
                 for i, n in enumerate(kept)
             ]
+            if own:
+                left = pl.multiple_of(lax.axis_index("tp") * columns, 128)
+                pairs.append((expand_ref.at[slot, :, pl.ds(left, columns)], out_own))
         copies.append([])
         for n, (source, target) in enumerate(pairs):
             copies[-1].append(pltpu.make_async_copy(source, target, sems.at[c, n]))
             copies[-1][-1].start()
-    row_steps = [steps_of_rows(x, count, me, per_home, home_ref, fetch_ref) for x in lengths]
     sums = [None] * sets
     for c in range(chunks):
         for copy in copies[c]:
@@ -130,38 +142,41 @@
             )
             sums[t] = product if c == 0 else sums[t] + product
     for t, used in enumerate(plan):
+        mine = row_steps[t][pl.ds(0, 1), :]
         total = prior[...] if has_prior and t == 0 else jnp.zeros((rank, count), jnp.float32)
         for n, panel in enumerate(used):
             term = sums[t][n * rank : (n + 1) * rank]
-            total = total + jnp.where(row_steps[t] == by_part(groups[panel]), term, 0.0)
+            total = total + jnp.where(mine == by_part(groups[panel]), term, 0.0)
         out[:, pl.ds(t * count, count)] = total
 
 
-def score(plan, groups, kept, tables, columns, lengths_of, tokens_of, panels, prior=None):
+def score(plan, groups, kept, columns, row_steps, tokens_of, panels, prior=None, tables=None):
     count, depth = tokens_of[0].shape
-    per_home, rank, _ = tables[2].shape
+    rank = panels[0].shape[0]
     chunks = 4
+    own = tables is not None
     prior = [] if prior is None else [prior]
     smem, vmem = pl.BlockSpec(memory_space=pltpu.SMEM), pl.BlockSpec(memory_space=pltpu.VMEM)
-    copied = len(tokens_of) + len(panels)
+    copied = list(tokens_of) + list(panels) + ([tables[3]] if own else [])
+    outs = [(rank, len(plan) * count), (len(kept) * rank, columns)] + [(rank, columns)] * own
     return pl.pallas_call(
-        functools.partial(score_kernel, plan, groups, kept, chunks, bool(prior), per_home),
+        functools.partial(score_kernel, plan, groups, kept, own, chunks, bool(prior)),
         out_shape=[
-            jax.ShapeDtypeStruct((rank, len(plan) * count), jnp.float32),
-            jax.ShapeDtypeStruct((len(kept) * rank, columns), panels[0].dtype),
+            jax.ShapeDtypeStruct(shape, panels[0].dtype if n else jnp.float32)
+            for n, shape in enumerate(outs)
         ],
-        in_specs=[smem] * (2 + len(lengths_of))
-        + [vmem] * len(prior)
-        + [pl.BlockSpec(memory_space=pl.ANY)] * copied,
-        out_specs=[vmem, vmem],
+        in_specs=[smem] * (2 * own)
+        + [vmem] * (len(row_steps) + len(prior))
+        + [pl.BlockSpec(memory_space=pl.ANY)] * len(copied),
+        out_specs=[vmem] * len(outs),
         scratch_shapes=[
             pltpu.VMEM((len(tokens_of), count, depth), tokens_of[0].dtype),
             pltpu.VMEM((len(panels) * rank, depth), tokens_of[0].dtype),
-            pltpu.SemaphoreType.DMA((chunks, copied + len(kept))),
+            pltpu.SemaphoreType.DMA((chunks, len(copied) + len(kept))),
         ],
         compiler_params=pltpu.CompilerParams(vmem_limit_bytes=40 << 20),
         cost_estimate=pl.CostEstimate(flops=0, bytes_accessed=0, transcendentals=0),
-    )(tables[0], tables[1], *lengths_of, *prior, *tokens_of, *panels)
+    )(*(tables[:2] if own else ()), *row_steps, *prior, *copied)
 
 
 def base_kernel(chunks, tokens_ref, weight_ref, *refs):
@@ -215,39 +230,28 @@
     )
 
 
-def finish_kernel(pieces, added, came, bases, per_home, home_ref, fetch_ref, lengths_ref, *refs):
-    scores, others = refs[:added], refs[added : added + came]
-    base, refs = refs[added + came : added + came + bases], refs[added + came + bases :]
-    expand_ref, arrays, (out, held, sems) = refs[0], refs[1:-3], refs[-3:]
-    me = lax.axis_index("rep")
+def end_kernel(pieces, added, bases, row_steps, *refs):
+    scores, base, refs = refs[:added], refs[added : added + bases], refs[added + bases :]
+    arrays, (out, held, sems) = refs[:-3], refs[-3:]
     count, columns = out.shape
     rank = scores[0].shape[0]
-    left = pl.multiple_of(lax.axis_index("tp") * columns, 128)
-    slot = slot_for(me, me, per_home, home_ref, fetch_ref)
     copies = []
     for n, (at, row, _) in enumerate(pieces):
-        if at is None:
-            source = expand_ref.at[slot, :, pl.ds(left, columns)]
-        else:
-            source = arrays[at].at[pl.ds(row, rank), pl.ds(arrays[at].shape[1] - columns, columns)]
+        source = arrays[at].at[pl.ds(row, rank), pl.ds(arrays[at].shape[1] - columns, columns)]
         copies.append(pltpu.make_async_copy(source, held.at[pl.ds(n * rank, rank)], sems.at[n]))
         copies[-1].start()
-    row_steps = steps_of_rows(lengths_ref, count, me, per_home, home_ref, fetch_ref)
     shrink = scores[0][:, pl.ds(0, count)]
     for x in scores[1:]:
         shrink = shrink + x[:, pl.ds(0, count)]
-    for x in others:
-        shrink = shrink + x[...]
     shrink = adapter_scale * shrink
     high = shrink.astype(jnp.bfloat16).astype(jnp.float32)
-    terms = [high, shrink - high]
-    masks = [row_steps == by_part(group) for _, _, group in pieces]
-    for copy in copies:
-        copy.wait()
+    masks = [row_steps[pl.ds(0, 1), :] == by_part(group) for _, _, group in pieces]
     total = base[0][...]
     for x in base[1:]:
         total = total + x[...]
-    for term in terms:
+    for copy in copies:
+        copy.wait()
+    for term in (high, shrink - high):
         wide = jnp.concatenate([jnp.where(mask, term, 0.0) for mask in masks], axis=0)
         total = total + lax.dot_general(
             wide.astype(jnp.bfloat16),
@@ -258,29 +262,23 @@
     out[...] = total.astype(out.dtype)
 
 
-def finish(pieces, tables, lengths, scores, others, base, arrays):
+def end(pieces, row_steps, scores, base, arrays, kind, cost):
     count, columns = base[0].shape
-    per_home, rank, _ = tables[2].shape
-    smem, vmem = pl.BlockSpec(memory_space=pltpu.SMEM), pl.BlockSpec(memory_space=pltpu.VMEM)
-    height = len(pieces) * rank
+    rank = scores[0].shape[0]
+    vmem = pl.BlockSpec(memory_space=pltpu.VMEM)
     return pl.pallas_call(
-        functools.partial(finish_kernel, pieces, len(scores), len(others), len(base), per_home),
-        out_shape=jax.ShapeDtypeStruct((count, columns), jnp.bfloat16),
-        in_specs=[smem] * 3
-        + [vmem] * (len(scores) + len(others) + len(base))
-        + [pl.BlockSpec(memory_space=pl.ANY)] * (1 + len(arrays)),
+        functools.partial(end_kernel, pieces, len(scores), len(base)),
+        out_shape=jax.ShapeDtypeStruct((count, columns), kind),
+        in_specs=[vmem] * (1 + len(scores) + len(base))
+        + [pl.BlockSpec(memory_space=pl.ANY)] * len(arrays),
         out_specs=vmem,
         scratch_shapes=[
-            pltpu.VMEM((height, columns), jnp.bfloat16),
+            pltpu.VMEM((len(pieces) * rank, columns), jnp.bfloat16),
             pltpu.SemaphoreType.DMA((len(pieces),)),
         ],
         compiler_params=pltpu.CompilerParams(vmem_limit_bytes=24 << 20),
-        cost_estimate=pl.CostEstimate(
-            flops=4 * count * columns * height,
-            bytes_accessed=2 * columns * height + 6 * count * columns,
-            transcendentals=0,
-        ),
-    )(tables[0], tables[1], lengths, *scores, *others, *base, tables[3], *arrays)
+        cost_estimate=pl.CostEstimate(flops=0, bytes_accessed=cost, transcendentals=0),
+    )(row_steps, *scores, *base, *arrays)
 
 
 def on_device(tokens, base_weight, shrink_panels, expand_panels, adapter_home, fetch_list, seg_len):
@@ -318,30 +316,30 @@
 
     tables = (adapter_home, fetch_list, panels, expand_panels)
     groups = far + near + solo
-    send = pack(groups, columns, *tables)
+    *send, row_steps = pack(groups, columns, tok_count, seg_len, *tables)
     tokens, send = tie((tokens, send))
     recv = [hop(x, group) for x, group in zip(send, groups)]
     tokens_of = [tokens] + [shift_parts(tokens, shift) for shift in range(1, parts)]
     solo_recv = recv[len(far) + len(near) :]
     near_recv = recv[len(far) : len(far) + len(near)]
-    base_weight, seg_len, near_recv = tie((base_weight, seg_len, near_recv))
+    base_weight, row_steps, near_recv = tie((base_weight, row_steps, near_recv))
     base = base_terms(tokens, base_weight, cores)
     base, recv[: len(far) - 1] = tie((base, recv[: len(far) - 1]))
     base = base[:1] + [shift_cores(x, shift + 1) for shift, x in enumerate(base[1:])]
-    lengths_of = [seg_len] + [shift_parts(seg_len, shift) for shift in range(1, parts)]
+    steps_of = [row_steps] + [shift_parts(row_steps, shift) for shift in range(1, parts)]
     early, early_groups = near_recv + recv[: len(far) - 1], near + far[:-1]
     last, last_group, own_group = recv[len(far) - 1], far[-1], (0,) * parts
 
     count = len(early)
-    first, sent = score(
+    first, sent, own_expand = score(
         [tuple(range(count + len(solo) + 1))],
         early_groups + solo + [own_group],
         tuple(range(count)),
-        tables,
         columns,
-        lengths_of[:1],
+        steps_of[:1],
         [tokens],
         early + solo_recv + [panels],
+        tables=tables,
     )
     passed = [shift_parts(sent, shift) for shift in range(1, parts)]
     base, first, passed, tokens_of[1:], last = tie((base, first, passed, tokens_of[1:], last))
@@ -349,9 +347,8 @@
         [(0,)] + [tuple(range(count + 1))] * (parts - 1),
         [last_group] + early_groups,
         (0,),
-        tables,
         columns,
-        lengths_of,
+        steps_of,
         tokens_of,
         [last] + early,
         first,
@@ -365,15 +362,15 @@
         shift_parts(whole[:, shift * tok_count : (shift + 1) * tok_count], -shift)
         for shift in range(1, parts)
     ]
-    arrays = early + solo_recv + [last] + passed + last_passed
-    pieces = [(None, 0, own_group)]
-    pieces += [(n, 0, group) for n, group in enumerate(early_groups + solo + [last_group])]
-    at = len(pieces) - 1
+    arrays = [own_expand] + early + solo_recv + [last]
+    pieces = [(n, 0, group) for n, group in enumerate([own_group] + early_groups + solo + [last_group])]
+    result = end(pieces, row_steps, halves, base, arrays, jnp.float32, 1 << 24)
+    pieces = []
     for shift in range(1, parts):
+        at = shift - 1
         pieces += [(at, n * rank, turned(group, shift)) for n, group in enumerate(early_groups)]
         pieces.append((at + parts - 1, 0, turned(last_group, shift)))
-        at += 1
-    return finish(pieces, tables, seg_len, halves, came, base, arrays)
+    return end(pieces, row_steps, came, [result], passed + last_passed, jnp.bfloat16, 0)
 
 
 def solution(mesh):

time: 74.3 us -> 73.3 us (0.987)
  waiting for transfers between devices: 42.6 us -> 41.8 us
    pallas_call x3 -> x4, Pallas kernels: 8.52 us -> 7.63 us  [the longest x2 5.63 us: score(): pl.pallas_call(functools.partial(score_kernel, plan, groups, kept, own, c...]
  transfers between devices with their start and end apart: 11 -> 11, of which waited for: 6 -> 6; matrix products, arithmetic and copies ran while one was open for 0% -> 0% of each run, Pallas kernels for 9% -> 11%
where the time goes in v15:
time: 73.3 us; the launch traced here: 73.1 us
  waiting for transfers between devices  41.8 us (57%)
  Pallas kernels  15.7 us (21%)
  starting transfers between devices  12 us (16%)
  local copies, waits for them, and re-layouts  3.41 us (5%)
    ppermute x4, waiting for transfers between devices, hop(): return lax.ppermute(x, ('parts', 'rep'), pairs)  37.5 us
    ppermute x4, starting transfers between devices, hop(): return lax.ppermute(x, ('parts', 'rep'), pairs)  5.99 us
    ppermute x5, starting transfers between devices, shift_parts(): lax.ppermute(x, 'parts', [(i, (i + shift) % parts) for i in range(parts)])  5.98 us
    pallas_call x2, Pallas kernels, score(): pl.pallas_call(functools.partial(score_kernel, plan, groups, kept, own, c...  5.63 us
    pallas_call x1, Pallas kernels, pack(): pl.pallas_call(functools.partial(pack_kernel, groups), out_shape=[jax.Sha...  4.11 us
    pallas_call x1, Pallas kernels, base_terms(): pl.pallas_call(functools.partial(base_kernel, chunks), out_shape=[jax.Sha...  3.96 us
    unnamed x14, local copies, waits for them, and re-layouts  3.41 us
    ppermute x5, waiting for transfers between devices, shift_parts(): lax.ppermute(x, 'parts', [(i, (i + shift) % parts) for i in range(parts)])  3.07 us
  transfers between devices with their start and end apart: 11, of which 6 were waited for; matrix products, arithmetic and copies ran while one was open for 0% of the time, Pallas kernels for 11%

profile of v15, /device:TPU:0, one launch (start us, length us, event | category | flops | bytes accessed | tf_op | source)
XLA Modules:
  0.0 73.1 jit_solution(8188365880887743937)
XLA Ops:
  0.0 4.1 %shard_map.73 = (bf16[64,4608]{1,0:T(8,128)(2,1)}, bf16[64,4608]{1,0:T(8,128)(2,1)}, bf16[64,4608]{1,0:T(8,128)(2,1)}, bf16[64,4608]{1,0:T(8,128)(2,1)}, s32[8,256]{1,0:T(8,128)}) custom-call(s32[32]{0:T(128)} %refs_0_.1, s32[8,8]{1,0:T(8,128)} %refs_1_.1, s32[1,8]{1,0:T(1,128)} %lengths_ref.1, bf16[4,64,4096]{2,1,0:T(8,128)(2,1)} %bitcast.1, ...), custom_call_target="tpu_custom_call" | custom-call | tf_op jit(solution)/shard_map/pallas_call | solution.py:81
  4.1 0.0 copy-done
  4.1 3.0 %collective-permute-start.6 = (bf16[256,4096]{1,0:T(8,128)(2,1)S(1)}, bf16[256,4096]{1,0:T(8,128)(2,1)S(1)}, u32[]{:S(2)}, u32[]{:S(2)}) collective-permute-start(bf16[256,4096]{1,0:T(8,128)(2,1)S(1)} %copy-done), channel_id=1, source_target_pairs={{0,16},{16,0},{1,17},{17,1},{2,18},{18,2},{3,19},{19,3},{4,20},{20... | collective-permute-start | bytes 6291464 | tf_op jit(solution)/shard_map/ppermute | solution.py:312
  7.1 1.6 %collective-permute-start = (bf16[64,4608]{1,0:T(8,128)(2,1)}, bf16[64,4608]{1,0:T(8,128)(2,1)S(1)}, u32[]{:S(2)}, u32[]{:S(2)}) collective-permute-start(bf16[64,4608]{1,0:T(8,128)(2,1)} %get-tuple-element.39), channel_id=1, source_target_pairs={{0,4},{2,6},{4,0},{6,2},{8,12},{10,14},{12,8},{14,10},{16,22},{18,... | collective-permute-start | bytes 1769480 | tf_op jit(solution)/shard_map/ppermute | solution.py:309
  8.7 2.6 %collective-permute-start.2 = (bf16[64,4608]{1,0:T(8,128)(2,1)}, bf16[64,4608]{1,0:T(8,128)(2,1)S(1)}, u32[]{:S(2)}, u32[]{:S(2)}) collective-permute-start(bf16[64,4608]{1,0:T(8,128)(2,1)} %get-tuple-element.45), channel_id=1, source_target_pairs={{0,8},{2,10},{4,12},{6,14},{8,0},{10,2},{12,4},{14,6},{16,28},{18,... | collective-permute-start | bytes 1769480 | tf_op jit(solution)/shard_map/ppermute | solution.py:309
  11.3 1.5 %collective-permute-start.4 = (bf16[64,4608]{1,0:T(8,128)(2,1)}, bf16[64,4608]{1,0:T(8,128)(2,1)S(1)}, u32[]{:S(2)}, u32[]{:S(2)}) collective-permute-start(bf16[64,4608]{1,0:T(8,128)(2,1)} %get-tuple-element.50), channel_id=1, source_target_pairs={{0,2},{2,0},{4,6},{6,4},{8,10},{10,8},{12,14},{14,12},{16,18},{18,... | collective-permute-start | bytes 1769480 | tf_op jit(solution)/shard_map/ppermute | solution.py:309
  12.8 0.3 collective-permute-start.7
  13.1 21.5 %collective-permute-done.refs_4_.refs_6_.refs_5_ = bf16[64,4608]{1,0:T(8,128)(2,1)S(1)} collective-permute-done((bf16[64,4608]{1,0:T(8,128)(2,1)}, bf16[64,4608]{1,0:T(8,128)(2,1)S(1)}, u32[]{:S(2)}, u32[]{:S(2)}) %collective-permute-start) | collective-permute-done | bytes 589856 | tf_op jit(solution)/shard_map/ppermute | solution.py:309
  34.6 3.4 %copy-done.1 = bf16[4096,1024]{1,0:T(8,128)(2,1)S(1)} copy-done((bf16[4096,1024]{1,0:T(8,128)(2,1)S(1)}, bf16[4096,1024]{1,0:T(8,128)(2,1)}, u32[]{:S(2)}) %copy-start.1) | copy-done | bytes 8388632
  38.0 0.0 copy-start.6
  38.0 4.0 %shard_map.74 = (f32[256,512]{1,0:T(8,128)S(1)}, f32[256,512]{1,0:T(8,128)S(1)}) custom-call(bf16[256,4096]{1,0:T(8,128)(2,1)S(1)} %copy-done, bf16[4096,1024]{1,0:T(8,128)(2,1)S(1)} %copy-done.1), custom_call_target="tpu_custom_call" | custom-call | tf_op jit(solution)/shard_map/pallas_call | solution.py:217
  42.0 9.4 %collective-permute-done.2.refs_5_.refs_7_.refs_6_ = bf16[64,4608]{1,0:T(8,128)(2,1)S(1)} collective-permute-done((bf16[64,4608]{1,0:T(8,128)(2,1)}, bf16[64,4608]{1,0:T(8,128)(2,1)S(1)}, u32[]{:S(2)}, u32[]{:S(2)}) %collective-permute-start.2) | collective-permute-done | bytes 589856 | tf_op jit(solution)/shard_map/ppermute | solution.py:309
  51.4 0.0 collective-permute-start.3
  51.4 0.0 collective-permute-done.4.refs_6_.refs_7_
  51.4 0.0 copy-done.2
  51.4 3.1 %shard_map.75 = (f32[64,256]{1,0:T(8,128)S(1)}, bf16[128,512]{1,0:T(8,128)(2,1)S(1)}, bf16[64,512]{1,0:T(8,128)(2,1)S(1)}) custom-call(s32[32]{0:T(128)S(1)} %copy-done.6, s32[8,8]{1,0:T(8,128)S(1)} %copy-done.5, s32[8,256]{1,0:T(8,128)S(1)} %copy-done.4, bf16[256,4096]{1,0:T(8,128)(2,1)S(1)} %copy-done, ...), custom_call_target="tpu_custom_call" | custom-call | tf_op jit(solution)/shard_map/pallas_call | solution.py:162
  54.6 0.1 collective-permute-start.5
  54.6 2.0 %collective-permute-start.1 = (s32[8,256]{1,0:T(8,128)S(1)}, s32[8,256]{1,0:T(8,128)S(1)}, u32[]{:S(2)}, u32[]{:S(2)}) collective-permute-start(s32[8,256]{1,0:T(8,128)S(1)} %copy-done.4), channel_id=1, source_target_pairs={{0,16},{16,0},{1,17},{17,1},{2,18},{18,2},{3,19},{19,3},{4,20},{20... | collective-permute-start | bytes 24584 | tf_op jit(solution)/shard_map/ppermute | solution.py:312
  56.6 6.6 %collective-permute-done.7.refs_5_.refs_8_ = bf16[64,4608]{1,0:T(8,128)(2,1)S(1)} collective-permute-done((bf16[64,4608]{1,0:T(8,128)(2,1)}, bf16[64,4608]{1,0:T(8,128)(2,1)S(1)}, u32[]{:S(2)}, u32[]{:S(2)}) %collective-permute-start.7) | collective-permute-done | bytes 589856 | tf_op jit(solution)/shard_map/ppermute | solution.py:309
  63.2 0.0 collective-permute-done.5.refs_2_
  63.3 0.0 collective-permute-done.3.refs_3_
  63.3 0.0 collective-permute-done.6.refs_4_
  63.3 0.0 collective-permute-done.1.refs_1_
  63.3 2.5 %shard_map.76 = (f32[64,512]{1,0:T(8,128)S(1)}, bf16[64,512]{1,0:T(8,128)(2,1)S(1)}) custom-call(s32[8,256]{1,0:T(8,128)S(1)} %copy-done.4, s32[8,256]{1,0:T(8,128)S(1)} %collective-permute-done.1.refs_1_, f32[64,256]{1,0:T(8,128)S(1)} %get-tuple-element.54.refs_2_, bf16[256,4096]{1,0:T(8,128)(2,1)S(1)} %copy-done, ...), custom_call_target="tpu_custom_call" | custom-call | tf_op jit(solution)/shard_map/pallas_call | solution.py:162
  65.8 0.1 collective-permute-start.8
  65.9 0.1 collective-permute-start.10
  66.0 1.3 %collective-permute-done.8.refs_1_ = f32[64,512]{1,0:T(8,128)S(1)} collective-permute-done((f32[64,512]{1,0:T(8,128)S(1)}, f32[64,512]{1,0:T(8,128)S(1)}, u32[]{:S(2)}, u32[]{:S(2)}) %collective-permute-start.8) | collective-permute-done | bytes 131104 | tf_op jit(solution)/shard_map/ppermute | solution.py:315
  67.2 0.8 %collective-permute-start.9 = (f32[64,256]{1,0:T(8,128)S(1)}, f32[64,256]{1,0:T(8,128)S(1)}, u32[]{:S(2)}, u32[]{:S(2)}) collective-permute-start(f32[64,256]{1,0:T(8,128)S(1)} %slice_add_fusion), channel_id=1, source_target_pairs={{0,16},{16,0},{1,17},{17,1},{2,18},{18,2},{3,19},{19,3},{4,20},{20... | collective-permute-start | bytes 196616 | tf_op jit(solution)/shard_map/ppermute | solution.py:312
  68.1 0.7 shard_map.77.refs_1_
  68.7 2.1 %collective-permute-done.10.refs_3_ = bf16[64,512]{1,0:T(8,128)(2,1)S(1)} collective-permute-done((bf16[64,512]{1,0:T(8,128)(2,1)S(1)}, bf16[64,512]{1,0:T(8,128)(2,1)S(1)}, u32[]{:S(2)}, u32[]{:S(2)}) %collective-permute-start.10) | collective-permute-done | bytes 65568 | tf_op jit(solution)/shard_map/ppermute | solution.py:312
  70.8 1.0 %collective-permute-done.9.refs_0_ = f32[64,256]{1,0:T(8,128)S(1)} collective-permute-done((f32[64,256]{1,0:T(8,128)S(1)}, f32[64,256]{1,0:T(8,128)S(1)}, u32[]{:S(2)}, u32[]{:S(2)}) %collective-permute-start.9) | collective-permute-done | bytes 65568 | tf_op jit(solution)/shard_map/ppermute | solution.py:312
  71.8 1.3 %shard_map.78 = bf16[256,512]{1,0:T(8,128)(2,1)} custom-call(s32[8,256]{1,0:T(8,128)S(1)} %copy-done.4, f32[64,256]{1,0:T(8,128)S(1)} %collective-permute-done.9.refs_0_, f32[256,512]{1,0:T(8,128)S(1)} %shard_map.77.refs_1_, bf16[128,512]{1,0:T(8,128)(2,1)S(1)} %collective-permute-done.5.refs_2_, bf16[64,512]{1,0:T(8,128)(2,1)S(1)} %collective-permute-done.10.refs_3_), custom_call_target="tpu_custom_call" | custom-call | tf_op jit(solution)/shard_map/pallas_call | solution.py:269
  (11 shorter events, 0.0 us)
Async XLA Ops:
  0.0 4.1 %copy-start = (bf16[256,4096]{1,0:T(8,128)(2,1)S(1)}, bf16[256,4096]{1,0:T(8,128)(2,1)}, u32[]{:S(2)}) copy-start(bf16[256,4096]{1,0:T(8,128)(2,1)} %refs_3_.1) | copy-start | bytes 6291460
  4.1 59.1 %collective-permute-start.6 = (bf16[256,4096]{1,0:T(8,128)(2,1)S(1)}, bf16[256,4096]{1,0:T(8,128)(2,1)S(1)}, u32[]{:S(2)}, u32[]{:S(2)}) collective-permute-start(bf16[256,4096]{1,0:T(8,128)(2,1)S(1)} %copy-done), channel_id=1, source_target_pairs={{0,16},{16,0},{1,17},{17,1},{2,18},{18,2},{3,19},{19,3},{4,20},{20... | collective-permute-start | bytes 6291464 | tf_op jit(solution)/shard_map/ppermute | solution.py:312
  7.1 27.5 %collective-permute-start = (bf16[64,4608]{1,0:T(8,128)(2,1)}, bf16[64,4608]{1,0:T(8,128)(2,1)S(1)}, u32[]{:S(2)}, u32[]{:S(2)}) collective-permute-start(bf16[64,4608]{1,0:T(8,128)(2,1)} %get-tuple-element.39), channel_id=1, source_target_pairs={{0,4},{2,6},{4,0},{6,2},{8,12},{10,14},{12,8},{14,10},{16,22},{18,... | collective-permute-start | bytes 1769480 | tf_op jit(solution)/shard_map/ppermute | solution.py:309
  8.7 42.7 %collective-permute-start.2 = (bf16[64,4608]{1,0:T(8,128)(2,1)}, bf16[64,4608]{1,0:T(8,128)(2,1)S(1)}, u32[]{:S(2)}, u32[]{:S(2)}) collective-permute-start(bf16[64,4608]{1,0:T(8,128)(2,1)} %get-tuple-element.45), channel_id=1, source_target_pairs={{0,8},{2,10},{4,12},{6,14},{8,0},{10,2},{12,4},{14,6},{16,28},{18,... | collective-permute-start | bytes 1769480 | tf_op jit(solution)/shard_map/ppermute | solution.py:309
  11.3 40.1 %collective-permute-start.4 = (bf16[64,4608]{1,0:T(8,128)(2,1)}, bf16[64,4608]{1,0:T(8,128)(2,1)S(1)}, u32[]{:S(2)}, u32[]{:S(2)}) collective-permute-start(bf16[64,4608]{1,0:T(8,128)(2,1)} %get-tuple-element.50), channel_id=1, source_target_pairs={{0,2},{2,0},{4,6},{6,4},{8,10},{10,8},{12,14},{14,12},{16,18},{18,... | collective-permute-start | bytes 1769480 | tf_op jit(solution)/shard_map/ppermute | solution.py:309
  12.8 50.4 %collective-permute-start.7 = (bf16[64,4608]{1,0:T(8,128)(2,1)}, bf16[64,4608]{1,0:T(8,128)(2,1)S(1)}, u32[]{:S(2)}, u32[]{:S(2)}) collective-permute-start(bf16[64,4608]{1,0:T(8,128)(2,1)} %get-tuple-element.53), channel_id=1, source_target_pairs={{0,10},{2,8},{4,14},{6,12},{8,2},{10,0},{12,6},{14,4},{16,30},{18,... | collective-permute-start | bytes 1769480 | tf_op jit(solution)/shard_map/ppermute | solution.py:309
  34.6 3.4 %copy-start.1 = (bf16[4096,1024]{1,0:T(8,128)(2,1)S(1)}, bf16[4096,1024]{1,0:T(8,128)(2,1)}, u32[]{:S(2)}) copy-start(bf16[4096,1024]{1,0:T(8,128)(2,1)} %weight_ref) | copy-start | bytes 25165828
  38.0 13.4 %copy-start.2 = (bf16[4,4096,64]{1,2,0:T(8,128)(2,1)S(1)}, bf16[4,4096,64]{1,2,0:T(8,128)(2,1)}, u32[]{:S(2)}) copy-start(bf16[4,4096,64]{1,2,0:T(8,128)(2,1)} %param.9) | copy-start | bytes 6291460
  38.0 13.4 %copy-start.3 = (bf16[4,64,1024]{2,1,0:T(8,128)(2,1)S(1)}, bf16[4,64,1024]{2,1,0:T(8,128)(2,1)}, u32[]{:S(2)}) copy-start(bf16[4,64,1024]{2,1,0:T(8,128)(2,1)} %refs_8_.1) | copy-start | bytes 1572868
  38.0 13.4 %copy-start.4 = (s32[8,256]{1,0:T(8,128)S(1)}, s32[8,256]{1,0:T(8,128)}, u32[]{:S(2)}) copy-start(s32[8,256]{1,0:T(8,128)} %get-tuple-element.40.refs_2_.refs_0_.row_steps) | copy-start | bytes 24580
  38.0 13.4 %copy-start.5 = (s32[8,8]{1,0:T(8,128)S(1)}, s32[8,8]{1,0:T(8,128)}, u32[]{:S(2)}) copy-start(s32[8,8]{1,0:T(8,128)} %refs_1_.1) | copy-start | bytes 772
  38.0 13.4 %copy-start.6 = (s32[32]{0:T(128)S(1)}, s32[32]{0:T(128)}, u32[]{:S(2)}) copy-start(s32[32]{0:T(128)} %refs_0_.1) | copy-start | bytes 388
  51.4 11.9 %collective-permute-start.3 = (f32[256,512]{1,0:T(8,128)S(1)}, f32[256,512]{1,0:T(8,128)S(1)}, u32[]{:S(2)}, u32[]{:S(2)}) collective-permute-start(f32[256,512]{1,0:T(8,128)S(1)} %get-tuple-element.47), channel_id=1, source_target_pairs={{0,1},{1,0},{2,3},{3,2},{4,5},{5,4},{6,7},{7,6},{8,9},{9,8},{10,11... | collective-permute-start | bytes 1572872 | tf_op jit(solution)/shard_map/ppermute | solution.py:315
  54.6 8.7 %collective-permute-start.5 = (bf16[128,512]{1,0:T(8,128)(2,1)S(1)}, bf16[128,512]{1,0:T(8,128)(2,1)S(1)}, u32[]{:S(2)}, u32[]{:S(2)}) collective-permute-start(bf16[128,512]{1,0:T(8,128)(2,1)S(1)} %get-tuple-element.52), channel_id=1, source_target_pairs={{0,16},{16,0},{1,17},{17,1},{2,18},{18,2},{3,19},{19,3},{4,20},{20... | collective-permute-start | bytes 393224 | tf_op jit(solution)/shard_map/ppermute | solution.py:312
  54.6 8.6 %collective-permute-start.1 = (s32[8,256]{1,0:T(8,128)S(1)}, s32[8,256]{1,0:T(8,128)S(1)}, u32[]{:S(2)}, u32[]{:S(2)}) collective-permute-start(s32[8,256]{1,0:T(8,128)S(1)} %copy-done.4), channel_id=1, source_target_pairs={{0,16},{16,0},{1,17},{17,1},{2,18},{18,2},{3,19},{19,3},{4,20},{20... | collective-permute-start | bytes 24584 | tf_op jit(solution)/shard_map/ppermute | solution.py:312
  65.8 1.4 %collective-permute-start.8 = (f32[64,512]{1,0:T(8,128)S(1)}, f32[64,512]{1,0:T(8,128)S(1)}, u32[]{:S(2)}, u32[]{:S(2)}) collective-permute-start(f32[64,512]{1,0:T(8,128)S(1)} %get-tuple-element.57.refs_0_), channel_id=1, source_target_pairs={{0,1},{1,0},{2,3},{3,2},{4,5},{5,4},{6,7},{7,6},{8,9},{9,8},{10,11... | collective-permute-start | bytes 393224 | tf_op jit(solution)/shard_map/ppermute | solution.py:315
  65.9 4.9 %collective-permute-start.10 = (bf16[64,512]{1,0:T(8,128)(2,1)S(1)}, bf16[64,512]{1,0:T(8,128)(2,1)S(1)}, u32[]{:S(2)}, u32[]{:S(2)}) collective-permute-start(bf16[64,512]{1,0:T(8,128)(2,1)S(1)} %get-tuple-element.62), channel_id=1, source_target_pairs={{0,16},{16,0},{1,17},{17,1},{2,18},{18,2},{3,19},{19,3},{4,20},{20... | collective-permute-start | bytes 196616 | tf_op jit(solution)/shard_map/ppermute | solution.py:312
  67.2 4.6 %collective-permute-start.9 = (f32[64,256]{1,0:T(8,128)S(1)}, f32[64,256]{1,0:T(8,128)S(1)}, u32[]{:S(2)}, u32[]{:S(2)}) collective-permute-start(f32[64,256]{1,0:T(8,128)S(1)} %slice_add_fusion), channel_id=1, source_target_pairs={{0,16},{16,0},{1,17},{17,1},{2,18},{18,2},{3,19},{19,3},{4,20},{20... | collective-permute-start | bytes 196616 | tf_op jit(solution)/shard_map/ppermute | solution.py:312

commit v16 on v15

--- a/solution.py
+++ b/solution.py
@@ -32,21 +32,30 @@
     return lax.fori_loop(0, listed, look, jnp.int32(0), unroll=listed <= 8)
 
 
-def steps_of_rows(lengths_ref, count, me, per_home, home_ref, fetch_ref):
-    rows = lax.broadcasted_iota(jnp.int32, (1, count), 1)
-    result = jnp.zeros((1, count), jnp.int32)
+def steps_kernel(per_home, home_ref, fetch_ref, lengths_ref, out):
+    me = lax.axis_index("rep")
+    rows = lax.broadcasted_iota(jnp.int32, out.shape, 1)
+    result = jnp.zeros(out.shape, jnp.int32)
     start = jnp.int32(0)
     for j in range(fetch_ref.shape[1]):
         step = lax.div(home_ref[fetch_ref[me, j]], jnp.int32(per_home)) ^ me
         result = jnp.where(rows >= start, step, result)
         start = start + lengths_ref[0, j]
-    return result
-
-
-def pack_kernel(groups, home_ref, fetch_ref, lengths_ref, shrink_ref, expand_ref, *refs):
-    count = len(groups)
-    outs, steps_out, refs = refs[:count], refs[count], refs[count + 1 :]
-    held, in_sems, out_sems = refs
+    out[...] = result
+
+
+def steps_of_rows(count, per_home, adapter_home, fetch_list, seg_len):
+    return pl.pallas_call(
+        functools.partial(steps_kernel, per_home),
+        out_shape=jax.ShapeDtypeStruct((8, count), jnp.int32),
+        in_specs=[pl.BlockSpec(memory_space=pltpu.SMEM)] * 3,
+        out_specs=pl.BlockSpec(memory_space=pltpu.VMEM),
+        cost_estimate=pl.CostEstimate(flops=0, bytes_accessed=0, transcendentals=0),
+    )(adapter_home, fetch_list, seg_len)
+
+
+def pack_kernel(groups, home_ref, fetch_ref, shrink_ref, expand_ref, *refs):
+    outs, (held, in_sems, out_sems) = refs[:-3], refs[-3:]
     me = lax.axis_index("rep")
     per_home, _, depth = shrink_ref.shape
     columns = expand_ref.shape[2] // lax.axis_size("tp")
@@ -64,8 +73,6 @@
             copy.start()
             leave = pltpu.make_async_copy(target, outs[at].at[:, pl.ds(start, size)], out_sems.at[at, n])
             arriving.append((copy, leave))
-    steps = steps_of_rows(lengths_ref, steps_out.shape[1], me, per_home, home_ref, fetch_ref)
-    steps_out[...] = jnp.broadcast_to(steps, steps_out.shape)
     for copy, leave in arriving:
         copy.wait()
         leave.start()
@@ -73,23 +80,21 @@
         leave.wait()
 
 
-def pack(groups, columns, count, lengths, adapter_home, fetch_list, panels, expand_panels):
+def pack(groups, columns, adapter_home, fetch_list, panels, expand_panels):
     rank, depth = panels.shape[1:]
     shape = (rank, depth + columns)
     cuts = 2
     return list(
         pl.pallas_call(
             functools.partial(pack_kernel, groups),
-            out_shape=[jax.ShapeDtypeStruct(shape, panels.dtype)] * len(groups)
-            + [jax.ShapeDtypeStruct((8, count), jnp.int32)],
-            in_specs=[pl.BlockSpec(memory_space=pltpu.SMEM)] * 3 + [pl.BlockSpec(memory_space=pl.ANY)] * 2,
-            out_specs=[pl.BlockSpec(memory_space=pl.ANY)] * len(groups)
-            + [pl.BlockSpec(memory_space=pltpu.VMEM)],
+            out_shape=[jax.ShapeDtypeStruct(shape, panels.dtype)] * len(groups),
+            in_specs=[pl.BlockSpec(memory_space=pltpu.SMEM)] * 2 + [pl.BlockSpec(memory_space=pl.ANY)] * 2,
+            out_specs=[pl.BlockSpec(memory_space=pl.ANY)] * len(groups),
             scratch_shapes=[pltpu.VMEM((len(groups),) + shape, panels.dtype)]
             + [pltpu.SemaphoreType.DMA((len(groups), cuts + 1))] * 2,
             compiler_params=pltpu.CompilerParams(vmem_limit_bytes=56 << 20),
             cost_estimate=pl.CostEstimate(flops=0, bytes_accessed=0, transcendentals=0),
-        )(adapter_home, fetch_list, lengths, panels, expand_panels)
+        )(adapter_home, fetch_list, panels, expand_panels)
     )
 
 
@@ -316,16 +321,17 @@
 
     tables = (adapter_home, fetch_list, panels, expand_panels)
     groups = far + near + solo
-    *send, row_steps = pack(groups, columns, tok_count, seg_len, *tables)
+    send = pack(groups, columns, *tables)
     tokens, send = tie((tokens, send))
     recv = [hop(x, group) for x, group in zip(send, groups)]
     tokens_of = [tokens] + [shift_parts(tokens, shift) for shift in range(1, parts)]
     solo_recv = recv[len(far) + len(near) :]
     near_recv = recv[len(far) : len(far) + len(near)]
-    base_weight, row_steps, near_recv = tie((base_weight, row_steps, near_recv))
+    seg_len, base_weight, solo_recv = tie((seg_len, base_weight, solo_recv))
     base = base_terms(tokens, base_weight, cores)
     base, recv[: len(far) - 1] = tie((base, recv[: len(far) - 1]))
     base = base[:1] + [shift_cores(x, shift + 1) for shift, x in enumerate(base[1:])]
+    row_steps = steps_of_rows(tok_count, panels.shape[0], adapter_home, fetch_list, seg_len)
     steps_of = [row_steps] + [shift_parts(row_steps, shift) for shift in range(1, parts)]
     early, early_groups = near_recv + recv[: len(far) - 1], near + far[:-1]
     last, last_group, own_group = recv[len(far) - 1], far[-1], (0,) * parts

time: 73.3 us -> 77 us (1.050)
  waiting for transfers between devices: 41.8 us -> 34.3 us
  local copies, waits for them, and re-layouts: 3.41 us -> 8.76 us
  Pallas kernels: 15.7 us -> 21 us
    ppermute x4, waiting for transfers between devices: 37.5 us -> 29.1 us  [hop(): return lax.ppermute(x, ('parts', 'rep'), pairs)]
    unnamed x14 -> x20, local copies, waits for them, and re-layouts: 3.41 us -> 8.76 us
    pallas_call x2, Pallas kernels: 2 us -> 4.5 us  [end(): pl.pallas_call(functools.partial(end_kernel, pieces, len(scores), len(bas...]
    pallas_call x0 -> x1, Pallas kernels: none -> 1.37 us  [steps_of_rows(): pl.pallas_call(functools.partial(steps_kernel, per_home), out_shape=jax.S...]
    pallas_call x2, Pallas kernels: 5.63 us -> 6.97 us  [score(): pl.pallas_call(functools.partial(score_kernel, plan, groups, kept, own, c...]
    ppermute x5, waiting for transfers between devices: 3.07 us -> 4.19 us  [shift_parts(): lax.ppermute(x, 'parts', [(i, (i + shift) % parts) for i in range(parts)])]
  transfers between devices with their start and end apart: 11 -> 11, of which waited for: 6 -> 8; matrix products, arithmetic and copies ran while one was open for 0% -> 0% of each run, Pallas kernels for 11% -> 15%
where the time goes in v16:
time: 77 us; the launch traced here: 76.5 us
  waiting for transfers between devices  34.3 us (45%)
  Pallas kernels  21 us (27%)
  starting transfers between devices  12.3 us (16%)
  local copies, waits for them, and re-layouts  8.76 us (11%)
    ppermute x4, waiting for transfers between devices, hop(): return lax.ppermute(x, ('parts', 'rep'), pairs)  29.1 us
    unnamed x20, local copies, waits for them, and re-layouts  8.76 us
    pallas_call x2, Pallas kernels, score(): pl.pallas_call(functools.partial(score_kernel, plan, groups, kept, own, c...  6.97 us
    ppermute x5, starting transfers between devices, shift_parts(): lax.ppermute(x, 'parts', [(i, (i + shift) % parts) for i in range(parts)])  6.25 us
    ppermute x4, starting transfers between devices, hop(): return lax.ppermute(x, ('parts', 'rep'), pairs)  5.96 us
    pallas_call x1, Pallas kernels, base_terms(): pl.pallas_call(functools.partial(base_kernel, chunks), out_shape=[jax.Sha...  4.63 us
    pallas_call x2, Pallas kernels, end(): pl.pallas_call(functools.partial(end_kernel, pieces, len(scores), len(bas...  4.5 us
    ppermute x5, waiting for transfers between devices, shift_parts(): lax.ppermute(x, 'parts', [(i, (i + shift) % parts) for i in range(parts)])  4.19 us
  transfers between devices with their start and end apart: 11, of which 8 were waited for; matrix products, arithmetic and copies ran while one was open for 0% of the time, Pallas kernels for 15%

profile of v16, /device:TPU:0, one launch (start us, length us, event | category | flops | bytes accessed | tf_op | source)
XLA Modules:
  0.0 76.5 jit_solution(16202585219199250578)
XLA Ops:
  0.0 3.5 %shard_map.73 = (bf16[64,4608]{1,0:T(8,128)(2,1)}, bf16[64,4608]{1,0:T(8,128)(2,1)}, bf16[64,4608]{1,0:T(8,128)(2,1)}, bf16[64,4608]{1,0:T(8,128)(2,1)}) custom-call(s32[32]{0:T(128)} %refs_0_.1, s32[8,8]{1,0:T(8,128)} %refs_1_.1, bf16[4,64,4096]{2,1,0:T(8,128)(2,1)} %bitcast.1, bf16[4,64,1024]{2,1,0:T(8,128)(2,1)} %refs_8_.1), custom_call_target="tpu_custom_call" | custom-call | tf_op jit(solution)/shard_map/pallas_call | solution.py:88
  3.5 0.0 copy-start.8
  3.6 3.0 %collective-permute-start.6 = (bf16[256,4096]{1,0:T(8,128)(2,1)S(1)}, bf16[256,4096]{1,0:T(8,128)(2,1)}, u32[]{:S(2)}, u32[]{:S(2)}) collective-permute-start(bf16[256,4096]{1,0:T(8,128)(2,1)S(1)} %copy-done), channel_id=1, source_target_pairs={{0,16},{16,0},{1,17},{17,1},{2,18},{18,2},{3,19},{19,3},{4,20},{20... | collective-permute-start | bytes 6291464 | tf_op jit(solution)/shard_map/ppermute | solution.py:317
  6.6 1.5 %collective-permute-start = (bf16[64,4608]{1,0:T(8,128)(2,1)}, bf16[64,4608]{1,0:T(8,128)(2,1)S(1)}, u32[]{:S(2)}, u32[]{:S(2)}) collective-permute-start(bf16[64,4608]{1,0:T(8,128)(2,1)} %get-tuple-element.37), channel_id=1, source_target_pairs={{0,2},{2,0},{4,6},{6,4},{8,10},{10,8},{12,14},{14,12},{16,18},{18,... | collective-permute-start | bytes 1769480 | tf_op jit(solution)/shard_map/ppermute | solution.py:314
  8.1 2.6 %collective-permute-start.2 = (bf16[64,4608]{1,0:T(8,128)(2,1)}, bf16[64,4608]{1,0:T(8,128)(2,1)S(1)}, u32[]{:S(2)}, u32[]{:S(2)}) collective-permute-start(bf16[64,4608]{1,0:T(8,128)(2,1)} %get-tuple-element.43), channel_id=1, source_target_pairs={{0,8},{2,10},{4,12},{6,14},{8,0},{10,2},{12,4},{14,6},{16,28},{18,... | collective-permute-start | bytes 1769480 | tf_op jit(solution)/shard_map/ppermute | solution.py:314
  10.7 1.6 %collective-permute-start.4 = (bf16[64,4608]{1,0:T(8,128)(2,1)}, bf16[64,4608]{1,0:T(8,128)(2,1)S(1)}, u32[]{:S(2)}, u32[]{:S(2)}) collective-permute-start(bf16[64,4608]{1,0:T(8,128)(2,1)} %get-tuple-element.46), channel_id=1, source_target_pairs={{0,4},{2,6},{4,0},{6,2},{8,12},{10,14},{12,8},{14,10},{16,22},{18,... | collective-permute-start | bytes 1769480 | tf_op jit(solution)/shard_map/ppermute | solution.py:314
  12.2 0.3 collective-permute-start.7
  12.5 9.0 %collective-permute-done.refs_6_.refs_7_ = bf16[64,4608]{1,0:T(8,128)(2,1)S(1)} collective-permute-done((bf16[64,4608]{1,0:T(8,128)(2,1)}, bf16[64,4608]{1,0:T(8,128)(2,1)S(1)}, u32[]{:S(2)}, u32[]{:S(2)}) %collective-permute-start) | collective-permute-done | bytes 589856 | tf_op jit(solution)/shard_map/ppermute | solution.py:314
  21.6 0.8 %copy-done.3 = bf16[64,4608]{1,0:T(8,128)(2,1)} copy-done((bf16[64,4608]{1,0:T(8,128)(2,1)}, bf16[64,4608]{1,0:T(8,128)(2,1)S(1)}, u32[]{:S(2)}) %copy-start.3) | copy-done | bytes 589848
  22.4 3.4 %copy-done.1 = bf16[4096,1024]{1,0:T(8,128)(2,1)S(1)} copy-done((bf16[4096,1024]{1,0:T(8,128)(2,1)S(1)}, bf16[4096,1024]{1,0:T(8,128)(2,1)}, u32[]{:S(2)}) %copy-start.1) | copy-done | bytes 8388632
  25.8 4.6 %shard_map.75 = (f32[256,512]{1,0:T(8,128)S(1)}, f32[256,512]{1,0:T(8,128)}) custom-call(bf16[256,4096]{1,0:T(8,128)(2,1)S(1)} %copy-done, bf16[4096,1024]{1,0:T(8,128)(2,1)S(1)} %copy-done.1), custom_call_target="tpu_custom_call" | custom-call | tf_op jit(solution)/shard_map/pallas_call | solution.py:222
  30.4 0.8 %copy-done.6 = f32[256,512]{1,0:T(8,128)} copy-done((f32[256,512]{1,0:T(8,128)}, f32[256,512]{1,0:T(8,128)S(1)}, u32[]{:S(2)}) %copy-start.6) | copy-done | bytes 524312
  31.3 19.0 %collective-permute-done.2.refs_5_.refs_7_.refs_6_ = bf16[64,4608]{1,0:T(8,128)(2,1)S(1)} collective-permute-done((bf16[64,4608]{1,0:T(8,128)(2,1)}, bf16[64,4608]{1,0:T(8,128)(2,1)S(1)}, u32[]{:S(2)}, u32[]{:S(2)}) %collective-permute-start.2) | collective-permute-done | bytes 589856 | tf_op jit(solution)/shard_map/ppermute | solution.py:314
  50.3 1.4 %shard_map.74.refs_2_.refs_0_.row_steps = s32[8,256]{1,0:T(8,128)} custom-call(s32[32]{0:T(128)} %refs_0_.1, s32[8,8]{1,0:T(8,128)} %refs_1_.1, s32[1,8]{1,0:T(1,128)} %lengths_ref), custom_call_target="tpu_custom_call" | custom-call | tf_op jit(solution)/shard_map/pallas_call | solution.py:48
  51.6 1.6 %copy-done.2 = bf16[4,4096,64]{1,2,0:T(8,128)(2,1)S(1)} copy-done((bf16[4,4096,64]{1,2,0:T(8,128)(2,1)S(1)}, bf16[4,4096,64]{1,2,0:T(8,128)(2,1)}, u32[]{:S(2)}) %copy-start.2) | copy-done | bytes 2097176
  53.2 1.1 %copy-done.4 = bf16[64,4608]{1,0:T(8,128)(2,1)S(1)} copy-done((bf16[64,4608]{1,0:T(8,128)(2,1)S(1)}, bf16[64,4608]{1,0:T(8,128)(2,1)}, u32[]{:S(2)}) %copy-start.4) | copy-done | bytes 589848
  54.3 1.0 %copy-done.5 = bf16[4,64,1024]{2,1,0:T(8,128)(2,1)S(1)} copy-done((bf16[4,64,1024]{2,1,0:T(8,128)(2,1)S(1)}, bf16[4,64,1024]{2,1,0:T(8,128)(2,1)}, u32[]{:S(2)}) %copy-start.5) | copy-done | bytes 524312
  55.3 3.2 %shard_map.76 = (f32[64,256]{1,0:T(8,128)S(1)}, bf16[128,512]{1,0:T(8,128)(2,1)S(1)}, bf16[64,512]{1,0:T(8,128)(2,1)S(1)}) custom-call(s32[32]{0:T(128)S(1)} %copy-done.9, s32[8,8]{1,0:T(8,128)S(1)} %copy-done.8, s32[8,256]{1,0:T(8,128)} %shard_map.74.refs_2_.refs_0_.row_steps, bf16[256,4096]{1,0:T(8,128)(2,1)S(1)} %copy-done, ...), custom_call_target="tpu_custom_call" | custom-call | tf_op jit(solution)/shard_map/pallas_call | solution.py:167
  58.5 0.1 collective-permute-start.5
  58.6 2.0 %collective-permute-start.1 = (s32[8,256]{1,0:T(8,128)}, s32[8,256]{1,0:T(8,128)S(1)}, u32[]{:S(2)}, u32[]{:S(2)}) collective-permute-start(s32[8,256]{1,0:T(8,128)} %shard_map.74.refs_2_.refs_0_.row_steps), channel_id=1, source_target_pairs={{0,16},{16,0},{1,17},{17,1},{2,18},{18,2},{3,19},{19,3},{4,20},{20... | collective-permute-start | bytes 24584 | tf_op jit(solution)/shard_map/ppermute | solution.py:317
  60.6 1.1 %collective-permute-done.7.refs_5_.refs_8_ = bf16[64,4608]{1,0:T(8,128)(2,1)} collective-permute-done((bf16[64,4608]{1,0:T(8,128)(2,1)}, bf16[64,4608]{1,0:T(8,128)(2,1)}, u32[]{:S(2)}, u32[]{:S(2)}) %collective-permute-start.7) | collective-permute-done | bytes 589856 | tf_op jit(solution)/shard_map/ppermute | solution.py:314
  61.7 2.9 %collective-permute-done.5.refs_2_ = bf16[128,512]{1,0:T(8,128)(2,1)S(1)} collective-permute-done((bf16[128,512]{1,0:T(8,128)(2,1)S(1)}, bf16[128,512]{1,0:T(8,128)(2,1)S(1)}, u32[]{:S(2)}, u32[]{:S(2)}) %collective-permute-start.5) | collective-permute-done | bytes 131104 | tf_op jit(solution)/shard_map/ppermute | solution.py:317
  64.6 0.1 collective-permute-done.1.refs_1_
  64.7 3.8 %shard_map.77 = (f32[64,512]{1,0:T(8,128)S(1)}, bf16[64,512]{1,0:T(8,128)(2,1)S(1)}) custom-call(s32[8,256]{1,0:T(8,128)} %shard_map.74.refs_2_.refs_0_.row_steps, s32[8,256]{1,0:T(8,128)S(1)} %collective-permute-done.1.refs_1_, f32[64,256]{1,0:T(8,128)S(1)} %get-tuple-element.52.refs_2_, bf16[256,4096]{1,0:T(8,128)(2,1)S(1)} %copy-done, ...), custom_call_target="tpu_custom_call" | custom-call | tf_op jit(solution)/shard_map/pallas_call | solution.py:167
  68.5 0.1 collective-permute-start.8
  68.6 0.3 collective-permute-start.10
  68.9 1.0 %collective-permute-done.8.refs_1_ = f32[64,512]{1,0:T(8,128)S(1)} collective-permute-done((f32[64,512]{1,0:T(8,128)S(1)}, f32[64,512]{1,0:T(8,128)S(1)}, u32[]{:S(2)}, u32[]{:S(2)}) %collective-permute-start.8) | collective-permute-done | bytes 131104 | tf_op jit(solution)/shard_map/ppermute | solution.py:320
  69.9 0.8 %collective-permute-start.9 = (f32[64,256]{1,0:T(8,128)S(1)}, f32[64,256]{1,0:T(8,128)S(1)}, u32[]{:S(2)}, u32[]{:S(2)}) collective-permute-start(f32[64,256]{1,0:T(8,128)S(1)} %slice_add_fusion), channel_id=1, source_target_pairs={{0,16},{16,0},{1,17},{17,1},{2,18},{18,2},{3,19},{19,3},{4,20},{20... | collective-permute-start | bytes 196616 | tf_op jit(solution)/shard_map/ppermute | solution.py:317
  70.7 2.5 %shard_map.78.refs_1_ = f32[256,512]{1,0:T(8,128)S(1)} custom-call(s32[8,256]{1,0:T(8,128)} %shard_map.74.refs_2_.refs_0_.row_steps, f32[64,512]{1,0:T(8,128)S(1)} %get-tuple-element.55.refs_0_, f32[64,512]{1,0:T(8,128)S(1)} %collective-permute-done.8.refs_1_, f32[256,512]{1,0:T(8,128)S(1)} %copy-done.7, f32[256,512]{1,0:T(8,128)} %collective-permute-done.3.refs_3_, ...), custom_call_target="tpu_custom_call" | custom-call | bytes 16777216 | tf_op jit(solution)/shard_map/pallas_call | solution.py:274
  73.2 0.3 collective-permute-done.10.refs_3_
  73.5 1.0 %collective-permute-done.9.refs_0_ = f32[64,256]{1,0:T(8,128)S(1)} collective-permute-done((f32[64,256]{1,0:T(8,128)S(1)}, f32[64,256]{1,0:T(8,128)S(1)}, u32[]{:S(2)}, u32[]{:S(2)}) %collective-permute-start.9) | collective-permute-done | bytes 65568 | tf_op jit(solution)/shard_map/ppermute | solution.py:317
  74.5 2.0 %shard_map.79 = bf16[256,512]{1,0:T(8,128)(2,1)} custom-call(s32[8,256]{1,0:T(8,128)} %shard_map.74.refs_2_.refs_0_.row_steps, f32[64,256]{1,0:T(8,128)S(1)} %collective-permute-done.9.refs_0_, f32[256,512]{1,0:T(8,128)S(1)} %shard_map.78.refs_1_, bf16[128,512]{1,0:T(8,128)(2,1)S(1)} %collective-permute-done.5.refs_2_, ...), custom_call_target="tpu_custom_call" | custom-call | tf_op jit(solution)/shard_map/pallas_call | solution.py:274
  (18 shorter events, 0.0 us)
Async XLA Ops:
  0.0 3.5 %copy-start = (bf16[256,4096]{1,0:T(8,128)(2,1)S(1)}, bf16[256,4096]{1,0:T(8,128)(2,1)}, u32[]{:S(2)}) copy-start(bf16[256,4096]{1,0:T(8,128)(2,1)} %refs_3_.1) | copy-start | bytes 6291460
  3.5 48.1 %copy-start.8 = (s32[8,8]{1,0:T(8,128)S(1)}, s32[8,8]{1,0:T(8,128)}, u32[]{:S(2)}) copy-start(s32[8,8]{1,0:T(8,128)} %refs_1_.1) | copy-start | bytes 772
  3.5 48.1 %copy-start.9 = (s32[32]{0:T(128)S(1)}, s32[32]{0:T(128)}, u32[]{:S(2)}) copy-start(s32[32]{0:T(128)} %refs_0_.1) | copy-start | bytes 388
  3.6 61.0 %collective-permute-start.6 = (bf16[256,4096]{1,0:T(8,128)(2,1)S(1)}, bf16[256,4096]{1,0:T(8,128)(2,1)}, u32[]{:S(2)}, u32[]{:S(2)}) collective-permute-start(bf16[256,4096]{1,0:T(8,128)(2,1)S(1)} %copy-done), channel_id=1, source_target_pairs={{0,16},{16,0},{1,17},{17,1},{2,18},{18,2},{3,19},{19,3},{4,20},{20... | collective-permute-start | bytes 6291464 | tf_op jit(solution)/shard_map/ppermute | solution.py:317
  6.6 15.0 %collective-permute-start = (bf16[64,4608]{1,0:T(8,128)(2,1)}, bf16[64,4608]{1,0:T(8,128)(2,1)S(1)}, u32[]{:S(2)}, u32[]{:S(2)}) collective-permute-start(bf16[64,4608]{1,0:T(8,128)(2,1)} %get-tuple-element.37), channel_id=1, source_target_pairs={{0,2},{2,0},{4,6},{6,4},{8,10},{10,8},{12,14},{14,12},{16,18},{18,... | collective-permute-start | bytes 1769480 | tf_op jit(solution)/shard_map/ppermute | solution.py:314
  8.1 42.2 %collective-permute-start.2 = (bf16[64,4608]{1,0:T(8,128)(2,1)}, bf16[64,4608]{1,0:T(8,128)(2,1)S(1)}, u32[]{:S(2)}, u32[]{:S(2)}) collective-permute-start(bf16[64,4608]{1,0:T(8,128)(2,1)} %get-tuple-element.43), channel_id=1, source_target_pairs={{0,8},{2,10},{4,12},{6,14},{8,0},{10,2},{12,4},{14,6},{16,28},{18,... | collective-permute-start | bytes 1769480 | tf_op jit(solution)/shard_map/ppermute | solution.py:314
  10.7 41.0 %collective-permute-start.4 = (bf16[64,4608]{1,0:T(8,128)(2,1)}, bf16[64,4608]{1,0:T(8,128)(2,1)S(1)}, u32[]{:S(2)}, u32[]{:S(2)}) collective-permute-start(bf16[64,4608]{1,0:T(8,128)(2,1)} %get-tuple-element.46), channel_id=1, source_target_pairs={{0,4},{2,6},{4,0},{6,2},{8,12},{10,14},{12,8},{14,10},{16,22},{18,... | collective-permute-start | bytes 1769480 | tf_op jit(solution)/shard_map/ppermute | solution.py:314
  12.2 49.5 %collective-permute-start.7 = (bf16[64,4608]{1,0:T(8,128)(2,1)}, bf16[64,4608]{1,0:T(8,128)(2,1)}, u32[]{:S(2)}, u32[]{:S(2)}) collective-permute-start(bf16[64,4608]{1,0:T(8,128)(2,1)} %get-tuple-element.51), channel_id=1, source_target_pairs={{0,10},{2,8},{4,14},{6,12},{8,2},{10,0},{12,6},{14,4},{16,30},{18,... | collective-permute-start | bytes 1769480 | tf_op jit(solution)/shard_map/ppermute | solution.py:314
  21.6 0.8 %copy-start.3 = (bf16[64,4608]{1,0:T(8,128)(2,1)}, bf16[64,4608]{1,0:T(8,128)(2,1)S(1)}, u32[]{:S(2)}) copy-start(bf16[64,4608]{1,0:T(8,128)(2,1)S(1)} %collective-permute-done.refs_6_.refs_7_) | copy-start | bytes 1769476
  22.4 3.4 %copy-start.1 = (bf16[4096,1024]{1,0:T(8,128)(2,1)S(1)}, bf16[4096,1024]{1,0:T(8,128)(2,1)}, u32[]{:S(2)}) copy-start(bf16[4096,1024]{1,0:T(8,128)(2,1)} %weight_ref) | copy-start | bytes 25165828
  30.4 0.8 %copy-start.6 = (f32[256,512]{1,0:T(8,128)}, f32[256,512]{1,0:T(8,128)S(1)}, u32[]{:S(2)}) copy-start(f32[256,512]{1,0:T(8,128)S(1)} %get-tuple-element.56.refs_2_) | copy-start | bytes 1572868
  50.2 14.3 %collective-permute-start.3 = (f32[256,512]{1,0:T(8,128)}, f32[256,512]{1,0:T(8,128)}, u32[]{:S(2)}, u32[]{:S(2)}) collective-permute-start(f32[256,512]{1,0:T(8,128)} %get-tuple-element.45), channel_id=1, source_target_pairs={{0,1},{1,0},{2,3},{3,2},{4,5},{5,4},{6,7},{7,6},{8,9},{9,8},{10,11... | collective-permute-start | bytes 1572872 | tf_op jit(solution)/shard_map/ppermute | solution.py:320
  51.6 1.6 %copy-start.2 = (bf16[4,4096,64]{1,2,0:T(8,128)(2,1)S(1)}, bf16[4,4096,64]{1,2,0:T(8,128)(2,1)}, u32[]{:S(2)}) copy-start(bf16[4,4096,64]{1,2,0:T(8,128)(2,1)} %param.9) | copy-start | bytes 6291460
  53.2 1.1 %copy-start.4 = (bf16[64,4608]{1,0:T(8,128)(2,1)S(1)}, bf16[64,4608]{1,0:T(8,128)(2,1)}, u32[]{:S(2)}) copy-start(bf16[64,4608]{1,0:T(8,128)(2,1)} %copy-done.3) | copy-start | bytes 1769476
  54.3 1.0 %copy-start.5 = (bf16[4,64,1024]{2,1,0:T(8,128)(2,1)S(1)}, bf16[4,64,1024]{2,1,0:T(8,128)(2,1)}, u32[]{:S(2)}) copy-start(bf16[4,64,1024]{2,1,0:T(8,128)(2,1)} %refs_8_.1) | copy-start | bytes 1572868
  58.5 6.1 %collective-permute-start.5 = (bf16[128,512]{1,0:T(8,128)(2,1)S(1)}, bf16[128,512]{1,0:T(8,128)(2,1)S(1)}, u32[]{:S(2)}, u32[]{:S(2)}) collective-permute-start(bf16[128,512]{1,0:T(8,128)(2,1)S(1)} %get-tuple-element.50), channel_id=1, source_target_pairs={{0,16},{16,0},{1,17},{17,1},{2,18},{18,2},{3,19},{19,3},{4,20},{20... | collective-permute-start | bytes 393224 | tf_op jit(solution)/shard_map/ppermute | solution.py:317
  58.6 6.1 %collective-permute-start.1 = (s32[8,256]{1,0:T(8,128)}, s32[8,256]{1,0:T(8,128)S(1)}, u32[]{:S(2)}, u32[]{:S(2)}) collective-permute-start(s32[8,256]{1,0:T(8,128)} %shard_map.74.refs_2_.refs_0_.row_steps), channel_id=1, source_target_pairs={{0,16},{16,0},{1,17},{17,1},{2,18},{18,2},{3,19},{19,3},{4,20},{20... | collective-permute-start | bytes 24584 | tf_op jit(solution)/shard_map/ppermute | solution.py:317
  64.6 6.2 %copy-start.7 = (f32[256,512]{1,0:T(8,128)S(1)}, f32[256,512]{1,0:T(8,128)}, u32[]{:S(2)}) copy-start(f32[256,512]{1,0:T(8,128)} %copy-done.6) | copy-start | bytes 1572868
  68.5 1.4 %collective-permute-start.8 = (f32[64,512]{1,0:T(8,128)S(1)}, f32[64,512]{1,0:T(8,128)S(1)}, u32[]{:S(2)}, u32[]{:S(2)}) collective-permute-start(f32[64,512]{1,0:T(8,128)S(1)} %get-tuple-element.55.refs_0_), channel_id=1, source_target_pairs={{0,1},{1,0},{2,3},{3,2},{4,5},{5,4},{6,7},{7,6},{8,9},{9,8},{10,11... | collective-permute-start | bytes 393224 | tf_op jit(solution)/shard_map/ppermute | solution.py:320
  68.6 4.9 %collective-permute-start.10 = (bf16[64,512]{1,0:T(8,128)(2,1)S(1)}, bf16[64,512]{1,0:T(8,128)(2,1)S(1)}, u32[]{:S(2)}, u32[]{:S(2)}) collective-permute-start(bf16[64,512]{1,0:T(8,128)(2,1)S(1)} %get-tuple-element.60), channel_id=1, source_target_pairs={{0,16},{16,0},{1,17},{17,1},{2,18},{18,2},{3,19},{19,3},{4,20},{20... | collective-permute-start | bytes 196616 | tf_op jit(solution)/shard_map/ppermute | solution.py:317
  69.9 4.6 %collective-permute-start.9 = (f32[64,256]{1,0:T(8,128)S(1)}, f32[64,256]{1,0:T(8,128)S(1)}, u32[]{:S(2)}, u32[]{:S(2)}) collective-permute-start(f32[64,256]{1,0:T(8,128)S(1)} %slice_add_fusion), channel_id=1, source_target_pairs={{0,16},{16,0},{1,17},{17,1},{2,18},{18,2},{3,19},{19,3},{4,20},{20... | collective-permute-start | bytes 196616 | tf_op jit(solution)/shard_map/ppermute | solution.py:317

commit v17 on v16

--- a/solution.py
+++ b/solution.py
@@ -50,6 +50,7 @@
         out_shape=jax.ShapeDtypeStruct((8, count), jnp.int32),
         in_specs=[pl.BlockSpec(memory_space=pltpu.SMEM)] * 3,
         out_specs=pl.BlockSpec(memory_space=pltpu.VMEM),
+        compiler_params=pltpu.CompilerParams(vmem_limit_bytes=2 << 20),
         cost_estimate=pl.CostEstimate(flops=0, bytes_accessed=0, transcendentals=0),
     )(adapter_home, fetch_list, seg_len)
 
@@ -106,42 +107,32 @@
     tokens, panels, refs = refs[:sets], refs[sets : sets + many], refs[sets + many :]
     expand_ref, refs = (refs[0], refs[1:]) if own else (None, refs)
     out, out_expand, refs = refs[0], refs[1], refs[2:]
-    out_own, refs = (refs[0], refs[1:]) if own else (None, refs)
-    held_tokens, held_panels, sems = refs
-    rank, count, depth = out.shape[0], held_tokens.shape[1], held_tokens.shape[2]
-    width, columns = depth // chunks, out_expand.shape[1]
+    rank, (count, depth) = out.shape[0], tokens[0].shape
+    columns = out_expand.shape[1]
+    copies = []
     if own:
+        out_own, held, sems = refs
         me = lax.axis_index("rep")
         slot = slot_for(me, me, panels[-1].shape[0], *tables)
-    copies = []
-    for c in range(chunks):
-        cols = pl.ds(c * width, width)
-        pairs = []
-        for n, ref in enumerate(panels):
-            source = ref.at[:, cols] if len(ref.shape) == 2 else ref.at[slot, :, cols]
-            pairs.append((source, held_panels.at[pl.ds(n * rank, rank), cols]))
-        pairs += [(ref.at[:, cols], held_tokens.at[n, :, cols]) for n, ref in enumerate(tokens)]
-        if c == chunks - 1:
-            pairs += [
-                (panels[n].at[:, pl.ds(depth, columns)], out_expand.at[pl.ds(i * rank, rank)])
-                for i, n in enumerate(kept)
-            ]
-            if own:
-                left = pl.multiple_of(lax.axis_index("tp") * columns, 128)
-                pairs.append((expand_ref.at[slot, :, pl.ds(left, columns)], out_own))
-        copies.append([])
-        for n, (source, target) in enumerate(pairs):
-            copies[-1].append(pltpu.make_async_copy(source, target, sems.at[c, n]))
-            copies[-1][-1].start()
+        left = pl.multiple_of(lax.axis_index("tp") * columns, 128)
+        for n, (source, target) in enumerate(
+            ((panels[-1].at[slot], held), (expand_ref.at[slot, :, pl.ds(left, columns)], out_own))
+        ):
+            copies.append(pltpu.make_async_copy(source, target, sems.at[n]))
+            copies[-1].start()
+        panels = panels[:-1] + (held,)
+    for i, n in enumerate(kept):
+        out_expand[pl.ds(i * rank, rank), :] = panels[n][:, pl.ds(depth, columns)]
+    for copy in copies:
+        copy.wait()
+    width = depth // chunks
     sums = [None] * sets
     for c in range(chunks):
-        for copy in copies[c]:
-            copy.wait()
         cols = pl.ds(c * width, width)
         for t, used in enumerate(plan):
             product = lax.dot_general(
-                held_panels[pl.ds(used[0] * rank, len(used) * rank), cols],
-                held_tokens[t, :, cols],
+                jnp.concatenate([panels[n][:, cols] for n in used], axis=0),
+                tokens[t][:, cols],
                 (((1,), (1,)), ((), ())),
                 preferred_element_type=jnp.float32,
             )
@@ -162,8 +153,10 @@
     own = tables is not None
     prior = [] if prior is None else [prior]
     smem, vmem = pl.BlockSpec(memory_space=pltpu.SMEM), pl.BlockSpec(memory_space=pltpu.VMEM)
-    copied = list(tokens_of) + list(panels) + ([tables[3]] if own else [])
+    anywhere = pl.BlockSpec(memory_space=pl.ANY)
     outs = [(rank, len(plan) * count), (len(kept) * rank, columns)] + [(rank, columns)] * own
+    arrays = list(row_steps) + prior + list(tokens_of) + list(panels)
+    need = 4 * len(plan) * count * (rank * len(panels) + depth) + 4 * len(panels) * rank * (depth + columns)
     return pl.pallas_call(
         functools.partial(score_kernel, plan, groups, kept, own, chunks, bool(prior)),
         out_shape=[
@@ -171,17 +164,13 @@
             for n, shape in enumerate(outs)
         ],
         in_specs=[smem] * (2 * own)
-        + [vmem] * (len(row_steps) + len(prior))
-        + [pl.BlockSpec(memory_space=pl.ANY)] * len(copied),
+        + [vmem] * (len(arrays) - own)
+        + [anywhere] * (2 * own),
         out_specs=[vmem] * len(outs),
-        scratch_shapes=[
-            pltpu.VMEM((len(tokens_of), count, depth), tokens_of[0].dtype),
-            pltpu.VMEM((len(panels) * rank, depth), tokens_of[0].dtype),
-            pltpu.SemaphoreType.DMA((chunks, len(copied) + len(kept))),
-        ],
-        compiler_params=pltpu.CompilerParams(vmem_limit_bytes=40 << 20),
+        scratch_shapes=[pltpu.VMEM((rank, depth), tokens_of[0].dtype), pltpu.SemaphoreType.DMA((2,))] * own,
+        compiler_params=pltpu.CompilerParams(vmem_limit_bytes=need + (2 << 20)),
         cost_estimate=pl.CostEstimate(flops=0, bytes_accessed=0, transcendentals=0),
-    )(*(tables[:2] if own else ()), *row_steps, *prior, *copied)
+    )(*(tables[:2] if own else ()), *arrays, *([tables[3]] if own else ()))
 
 
 def base_kernel(chunks, tokens_ref, weight_ref, *refs):
@@ -229,7 +218,7 @@
                 pltpu.VMEM((cores, depth, columns), weight.dtype),
                 pltpu.SemaphoreType.DMA((chunks, 1 + cores)),
             ],
-            compiler_params=pltpu.CompilerParams(vmem_limit_bytes=40 << 20),
+            compiler_params=pltpu.CompilerParams(vmem_limit_bytes=20 << 20),
             cost_estimate=pl.CostEstimate(flops=0, bytes_accessed=0, transcendentals=0),
         )(tokens, weight)
     )
@@ -281,7 +270,7 @@
             pltpu.VMEM((len(pieces) * rank, columns), jnp.bfloat16),
             pltpu.SemaphoreType.DMA((len(pieces),)),
         ],
-        compiler_params=pltpu.CompilerParams(vmem_limit_bytes=24 << 20),
+        compiler_params=pltpu.CompilerParams(vmem_limit_bytes=16 << 20),
         cost_estimate=pl.CostEstimate(flops=0, bytes_accessed=cost, transcendentals=0),
     )(row_steps, *scores, *base, *arrays)
 

time: 77 us -> 70.5 us (0.916)
  Pallas kernels: 21 us -> 13 us
  waiting for transfers between devices: 34.3 us -> 41.8 us
  local copies, waits for them, and re-layouts: 8.76 us -> 3.41 us
    ppermute x4, waiting for transfers between devices: 29.1 us -> 37.5 us  [hop(): return lax.ppermute(x, ('parts', 'rep'), pairs)]
    unnamed x20 -> x14, local copies, waits for them, and re-layouts: 8.76 us -> 3.41 us
    pallas_call x2, Pallas kernels: 6.97 us -> 2.84 us  [score(): pl.pallas_call(functools.partial(score_kernel, plan, groups, kept, own, c...]
    pallas_call x2, Pallas kernels: 4.5 us -> 2.01 us  [end(): pl.pallas_call(functools.partial(end_kernel, pieces, len(scores), len(bas...]
    ppermute x5, waiting for transfers between devices: 4.19 us -> 3.05 us  [shift_parts(): lax.ppermute(x, 'parts', [(i, (i + shift) % parts) for i in range(parts)])]
  transfers between devices with their start and end apart: 11 -> 11, of which waited for: 8 -> 6; matrix products, arithmetic and copies ran while one was open for 0% -> 0% of each run, Pallas kernels for 15% -> 10%
where the time goes in v17:
time: 70.5 us; the launch traced here: 70.4 us
  waiting for transfers between devices  41.8 us (59%)
  Pallas kernels  13 us (18%)
  starting transfers between devices  12 us (17%)
  local copies, waits for them, and re-layouts  3.41 us (5%)
    ppermute x4, waiting for transfers between devices, hop(): return lax.ppermute(x, ('parts', 'rep'), pairs)  37.5 us
    ppermute x5, starting transfers between devices, shift_parts(): lax.ppermute(x, 'parts', [(i, (i + shift) % parts) for i in range(parts)])  5.98 us
    ppermute x4, starting transfers between devices, hop(): return lax.ppermute(x, ('parts', 'rep'), pairs)  5.96 us
    pallas_call x1, Pallas kernels, base_terms(): pl.pallas_call(functools.partial(base_kernel, chunks), out_shape=[jax.Sha...  3.95 us
    pallas_call x1, Pallas kernels, pack(): pl.pallas_call(functools.partial(pack_kernel, groups), out_shape=[jax.Sha...  3.5 us
    unnamed x14, local copies, waits for them, and re-layouts  3.41 us
    ppermute x5, waiting for transfers between devices, shift_parts(): lax.ppermute(x, 'parts', [(i, (i + shift) % parts) for i in range(parts)])  3.05 us
    pallas_call x2, Pallas kernels, score(): pl.pallas_call(functools.partial(score_kernel, plan, groups, kept, own, c...  2.84 us
  transfers between devices with their start and end apart: 11, of which 6 were waited for; matrix products, arithmetic and copies ran while one was open for 0% of the time, Pallas kernels for 10%

profile of v17, /device:TPU:0, one launch (start us, length us, event | category | flops | bytes accessed | tf_op | source)
XLA Modules:
  0.0 70.4 jit_solution(11199648573478587911)
XLA Ops:
  0.0 3.5 %shard_map.73 = (bf16[64,4608]{1,0:T(8,128)(2,1)}, bf16[64,4608]{1,0:T(8,128)(2,1)}, bf16[64,4608]{1,0:T(8,128)(2,1)}, bf16[64,4608]{1,0:T(8,128)(2,1)}) custom-call(s32[32]{0:T(128)} %refs_0_.1, s32[8,8]{1,0:T(8,128)} %refs_1_.1, bf16[4,64,4096]{2,1,0:T(8,128)(2,1)} %bitcast.1, bf16[4,64,1024]{2,1,0:T(8,128)(2,1)} %refs_8_.1), custom_call_target="tpu_custom_call" | custom-call | tf_op jit(solution)/shard_map/pallas_call | solution.py:89
  3.5 0.0 copy-start.4
  3.5 0.0 copy-start.5
  3.5 0.0 copy-start.6
  3.6 3.0 %collective-permute-start.6 = (bf16[256,4096]{1,0:T(8,128)(2,1)S(1)}, bf16[256,4096]{1,0:T(8,128)(2,1)S(1)}, u32[]{:S(2)}, u32[]{:S(2)}) collective-permute-start(bf16[256,4096]{1,0:T(8,128)(2,1)S(1)} %copy-done), channel_id=1, source_target_pairs={{0,16},{16,0},{1,17},{17,1},{2,18},{18,2},{3,19},{19,3},{4,20},{20... | collective-permute-start | bytes 6291464 | tf_op jit(solution)/shard_map/ppermute | solution.py:306
  6.6 1.5 %collective-permute-start = (bf16[64,4608]{1,0:T(8,128)(2,1)}, bf16[64,4608]{1,0:T(8,128)(2,1)S(1)}, u32[]{:S(2)}, u32[]{:S(2)}) collective-permute-start(bf16[64,4608]{1,0:T(8,128)(2,1)} %get-tuple-element.37), channel_id=1, source_target_pairs={{0,2},{2,0},{4,6},{6,4},{8,10},{10,8},{12,14},{14,12},{16,18},{18,... | collective-permute-start | bytes 1769480 | tf_op jit(solution)/shard_map/ppermute | solution.py:303
  8.1 2.6 %collective-permute-start.2 = (bf16[64,4608]{1,0:T(8,128)(2,1)}, bf16[64,4608]{1,0:T(8,128)(2,1)S(1)}, u32[]{:S(2)}, u32[]{:S(2)}) collective-permute-start(bf16[64,4608]{1,0:T(8,128)(2,1)} %get-tuple-element.43), channel_id=1, source_target_pairs={{0,8},{2,10},{4,12},{6,14},{8,0},{10,2},{12,4},{14,6},{16,28},{18,... | collective-permute-start | bytes 1769480 | tf_op jit(solution)/shard_map/ppermute | solution.py:303
  10.7 1.6 %collective-permute-start.4 = (bf16[64,4608]{1,0:T(8,128)(2,1)}, bf16[64,4608]{1,0:T(8,128)(2,1)S(1)}, u32[]{:S(2)}, u32[]{:S(2)}) collective-permute-start(bf16[64,4608]{1,0:T(8,128)(2,1)} %get-tuple-element.46), channel_id=1, source_target_pairs={{0,4},{2,6},{4,0},{6,2},{8,12},{10,14},{12,8},{14,10},{16,22},{18,... | collective-permute-start | bytes 1769480 | tf_op jit(solution)/shard_map/ppermute | solution.py:303
  12.3 0.3 collective-permute-start.7
  12.5 9.0 %collective-permute-done.refs_6_.refs_7_ = bf16[64,4608]{1,0:T(8,128)(2,1)S(1)} collective-permute-done((bf16[64,4608]{1,0:T(8,128)(2,1)}, bf16[64,4608]{1,0:T(8,128)(2,1)S(1)}, u32[]{:S(2)}, u32[]{:S(2)}) %collective-permute-start) | collective-permute-done | bytes 589856 | tf_op jit(solution)/shard_map/ppermute | solution.py:303
  21.6 3.4 %copy-done.1 = bf16[4096,1024]{1,0:T(8,128)(2,1)S(1)} copy-done((bf16[4096,1024]{1,0:T(8,128)(2,1)S(1)}, bf16[4096,1024]{1,0:T(8,128)(2,1)}, u32[]{:S(2)}) %copy-start.1) | copy-done | bytes 8388632
  24.9 3.9 %shard_map.75 = (f32[256,512]{1,0:T(8,128)S(1)}, f32[256,512]{1,0:T(8,128)S(1)}) custom-call(bf16[256,4096]{1,0:T(8,128)(2,1)S(1)} %copy-done, bf16[4096,1024]{1,0:T(8,128)(2,1)S(1)} %copy-done.1), custom_call_target="tpu_custom_call" | custom-call | tf_op jit(solution)/shard_map/pallas_call | solution.py:211
  28.9 21.3 %collective-permute-done.2.refs_5_.refs_7_.refs_6_ = bf16[64,4608]{1,0:T(8,128)(2,1)S(1)} collective-permute-done((bf16[64,4608]{1,0:T(8,128)(2,1)}, bf16[64,4608]{1,0:T(8,128)(2,1)S(1)}, u32[]{:S(2)}, u32[]{:S(2)}) %collective-permute-start.2) | collective-permute-done | bytes 589856 | tf_op jit(solution)/shard_map/ppermute | solution.py:303
  50.2 0.0 collective-permute-start.3
  50.2 0.6 shard_map.74.refs_2_.refs_0_.row_steps
  50.9 0.0 collective-permute-done.4.refs_4_.refs_6_.refs_5_
  50.9 1.5 %shard_map.76 = (f32[64,256]{1,0:T(8,128)S(1)}, bf16[128,512]{1,0:T(8,128)(2,1)S(1)}, bf16[64,512]{1,0:T(8,128)(2,1)S(1)}) custom-call(s32[32]{0:T(128)S(1)} %copy-done.5, s32[8,8]{1,0:T(8,128)S(1)} %copy-done.4, s32[8,256]{1,0:T(8,128)S(1)} %shard_map.74.refs_2_.refs_0_.row_steps, bf16[256,4096]{1,0:T(8,128)(2,1)S(1)} %copy-done, ...), custom_call_target="tpu_custom_call" | custom-call | tf_op jit(solution)/shard_map/pallas_call | solution.py:160
  52.4 0.1 collective-permute-start.5
  52.5 2.0 %collective-permute-start.1 = (s32[8,256]{1,0:T(8,128)S(1)}, s32[8,256]{1,0:T(8,128)S(1)}, u32[]{:S(2)}, u32[]{:S(2)}) collective-permute-start(s32[8,256]{1,0:T(8,128)S(1)} %shard_map.74.refs_2_.refs_0_.row_steps), channel_id=1, source_target_pairs={{0,16},{16,0},{1,17},{17,1},{2,18},{18,2},{3,19},{19,3},{4,20},{20... | collective-permute-start | bytes 24584 | tf_op jit(solution)/shard_map/ppermute | solution.py:306
  54.5 7.1 %collective-permute-done.7.refs_5_.refs_8_ = bf16[64,4608]{1,0:T(8,128)(2,1)S(1)} collective-permute-done((bf16[64,4608]{1,0:T(8,128)(2,1)}, bf16[64,4608]{1,0:T(8,128)(2,1)S(1)}, u32[]{:S(2)}, u32[]{:S(2)}) %collective-permute-start.7) | collective-permute-done | bytes 589856 | tf_op jit(solution)/shard_map/ppermute | solution.py:303
  61.6 0.0 collective-permute-done.5.refs_2_
  61.6 0.0 collective-permute-done.3.refs_3_
  61.6 0.0 collective-permute-done.6.refs_4_
  61.6 1.4 %shard_map.77 = (f32[64,512]{1,0:T(8,128)S(1)}, bf16[64,512]{1,0:T(8,128)(2,1)S(1)}) custom-call(s32[8,256]{1,0:T(8,128)S(1)} %shard_map.74.refs_2_.refs_0_.row_steps, s32[8,256]{1,0:T(8,128)S(1)} %collective-permute-done.1.refs_1_, f32[64,256]{1,0:T(8,128)S(1)} %get-tuple-element.52.refs_2_, bf16[256,4096]{1,0:T(8,128)(2,1)S(1)} %copy-done, ...), custom_call_target="tpu_custom_call" | custom-call | tf_op jit(solution)/shard_map/pallas_call | solution.py:160
  63.0 0.1 collective-permute-start.8
  63.1 0.1 collective-permute-start.10
  63.2 1.3 %collective-permute-done.8.refs_1_ = f32[64,512]{1,0:T(8,128)S(1)} collective-permute-done((f32[64,512]{1,0:T(8,128)S(1)}, f32[64,512]{1,0:T(8,128)S(1)}, u32[]{:S(2)}, u32[]{:S(2)}) %collective-permute-start.8) | collective-permute-done | bytes 131104 | tf_op jit(solution)/shard_map/ppermute | solution.py:309
  64.5 0.8 %collective-permute-start.9 = (f32[64,256]{1,0:T(8,128)S(1)}, f32[64,256]{1,0:T(8,128)S(1)}, u32[]{:S(2)}, u32[]{:S(2)}) collective-permute-start(f32[64,256]{1,0:T(8,128)S(1)} %slice_add_fusion), channel_id=1, source_target_pairs={{0,16},{16,0},{1,17},{17,1},{2,18},{18,2},{3,19},{19,3},{4,20},{20... | collective-permute-start | bytes 196616 | tf_op jit(solution)/shard_map/ppermute | solution.py:306
  65.3 0.7 shard_map.78.refs_1_
  66.0 2.1 %collective-permute-done.10.refs_3_ = bf16[64,512]{1,0:T(8,128)(2,1)S(1)} collective-permute-done((bf16[64,512]{1,0:T(8,128)(2,1)S(1)}, bf16[64,512]{1,0:T(8,128)(2,1)S(1)}, u32[]{:S(2)}, u32[]{:S(2)}) %collective-permute-start.10) | collective-permute-done | bytes 65568 | tf_op jit(solution)/shard_map/ppermute | solution.py:306
  68.0 1.0 %collective-permute-done.9.refs_0_ = f32[64,256]{1,0:T(8,128)S(1)} collective-permute-done((f32[64,256]{1,0:T(8,128)S(1)}, f32[64,256]{1,0:T(8,128)S(1)}, u32[]{:S(2)}, u32[]{:S(2)}) %collective-permute-start.9) | collective-permute-done | bytes 65568 | tf_op jit(solution)/shard_map/ppermute | solution.py:306
  69.0 1.3 %shard_map.79 = bf16[256,512]{1,0:T(8,128)(2,1)} custom-call(s32[8,256]{1,0:T(8,128)S(1)} %shard_map.74.refs_2_.refs_0_.row_steps, f32[64,256]{1,0:T(8,128)S(1)} %collective-permute-done.9.refs_0_, f32[256,512]{1,0:T(8,128)S(1)} %shard_map.78.refs_1_, bf16[128,512]{1,0:T(8,128)(2,1)S(1)} %collective-permute-done.5.refs_2_, ...), custom_call_target="tpu_custom_call" | custom-call | tf_op jit(solution)/shard_map/pallas_call | solution.py:263
  (12 shorter events, 0.0 us)
Async XLA Ops:
  0.0 3.6 %copy-start = (bf16[256,4096]{1,0:T(8,128)(2,1)S(1)}, bf16[256,4096]{1,0:T(8,128)(2,1)}, u32[]{:S(2)}) copy-start(bf16[256,4096]{1,0:T(8,128)(2,1)} %refs_3_.1) | copy-start | bytes 6291460
  0.0 50.9 %copy-start.3 = (bf16[4,64,1024]{2,1,0:T(8,128)(2,1)S(1)}, bf16[4,64,1024]{2,1,0:T(8,128)(2,1)}, u32[]{:S(2)}) copy-start(bf16[4,64,1024]{2,1,0:T(8,128)(2,1)} %refs_8_.1) | copy-start | bytes 1572868
  3.5 46.7 %copy-start.4 = (s32[8,8]{1,0:T(8,128)S(1)}, s32[8,8]{1,0:T(8,128)}, u32[]{:S(2)}) copy-start(s32[8,8]{1,0:T(8,128)} %refs_1_.1) | copy-start | bytes 772
  3.5 46.7 %copy-start.5 = (s32[32]{0:T(128)S(1)}, s32[32]{0:T(128)}, u32[]{:S(2)}) copy-start(s32[32]{0:T(128)} %refs_0_.1) | copy-start | bytes 388
  3.5 46.7 %copy-start.6 = (s32[1,8]{1,0:T(1,128)S(1)}, s32[1,8]{1,0:T(1,128)}, u32[]{:S(2)}) copy-start(s32[1,8]{1,0:T(1,128)} %lengths_ref) | copy-start | bytes 100
  3.6 58.1 %collective-permute-start.6 = (bf16[256,4096]{1,0:T(8,128)(2,1)S(1)}, bf16[256,4096]{1,0:T(8,128)(2,1)S(1)}, u32[]{:S(2)}, u32[]{:S(2)}) collective-permute-start(bf16[256,4096]{1,0:T(8,128)(2,1)S(1)} %copy-done), channel_id=1, source_target_pairs={{0,16},{16,0},{1,17},{17,1},{2,18},{18,2},{3,19},{19,3},{4,20},{20... | collective-permute-start | bytes 6291464 | tf_op jit(solution)/shard_map/ppermute | solution.py:306
  6.6 15.0 %collective-permute-start = (bf16[64,4608]{1,0:T(8,128)(2,1)}, bf16[64,4608]{1,0:T(8,128)(2,1)S(1)}, u32[]{:S(2)}, u32[]{:S(2)}) collective-permute-start(bf16[64,4608]{1,0:T(8,128)(2,1)} %get-tuple-element.37), channel_id=1, source_target_pairs={{0,2},{2,0},{4,6},{6,4},{8,10},{10,8},{12,14},{14,12},{16,18},{18,... | collective-permute-start | bytes 1769480 | tf_op jit(solution)/shard_map/ppermute | solution.py:303
  8.1 42.1 %collective-permute-start.2 = (bf16[64,4608]{1,0:T(8,128)(2,1)}, bf16[64,4608]{1,0:T(8,128)(2,1)S(1)}, u32[]{:S(2)}, u32[]{:S(2)}) collective-permute-start(bf16[64,4608]{1,0:T(8,128)(2,1)} %get-tuple-element.43), channel_id=1, source_target_pairs={{0,8},{2,10},{4,12},{6,14},{8,0},{10,2},{12,4},{14,6},{16,28},{18,... | collective-permute-start | bytes 1769480 | tf_op jit(solution)/shard_map/ppermute | solution.py:303
  10.7 40.2 %collective-permute-start.4 = (bf16[64,4608]{1,0:T(8,128)(2,1)}, bf16[64,4608]{1,0:T(8,128)(2,1)S(1)}, u32[]{:S(2)}, u32[]{:S(2)}) collective-permute-start(bf16[64,4608]{1,0:T(8,128)(2,1)} %get-tuple-element.46), channel_id=1, source_target_pairs={{0,4},{2,6},{4,0},{6,2},{8,12},{10,14},{12,8},{14,10},{16,22},{18,... | collective-permute-start | bytes 1769480 | tf_op jit(solution)/shard_map/ppermute | solution.py:303
  12.3 49.4 %collective-permute-start.7 = (bf16[64,4608]{1,0:T(8,128)(2,1)}, bf16[64,4608]{1,0:T(8,128)(2,1)S(1)}, u32[]{:S(2)}, u32[]{:S(2)}) collective-permute-start(bf16[64,4608]{1,0:T(8,128)(2,1)} %get-tuple-element.51), channel_id=1, source_target_pairs={{0,10},{2,8},{4,14},{6,12},{8,2},{10,0},{12,6},{14,4},{16,30},{18,... | collective-permute-start | bytes 1769480 | tf_op jit(solution)/shard_map/ppermute | solution.py:303
  21.6 3.4 %copy-start.1 = (bf16[4096,1024]{1,0:T(8,128)(2,1)S(1)}, bf16[4096,1024]{1,0:T(8,128)(2,1)}, u32[]{:S(2)}) copy-start(bf16[4096,1024]{1,0:T(8,128)(2,1)} %weight_ref) | copy-start | bytes 25165828
  24.9 26.0 %copy-start.2 = (bf16[4,4096,64]{1,2,0:T(8,128)(2,1)S(1)}, bf16[4,4096,64]{1,2,0:T(8,128)(2,1)}, u32[]{:S(2)}) copy-start(bf16[4,4096,64]{1,2,0:T(8,128)(2,1)} %param.9) | copy-start | bytes 6291460
  50.2 11.4 %collective-permute-start.3 = (f32[256,512]{1,0:T(8,128)S(1)}, f32[256,512]{1,0:T(8,128)S(1)}, u32[]{:S(2)}, u32[]{:S(2)}) collective-permute-start(f32[256,512]{1,0:T(8,128)S(1)} %get-tuple-element.45), channel_id=1, source_target_pairs={{0,1},{1,0},{2,3},{3,2},{4,5},{5,4},{6,7},{7,6},{8,9},{9,8},{10,11... | collective-permute-start | bytes 1572872 | tf_op jit(solution)/shard_map/ppermute | solution.py:309
  52.4 9.2 %collective-permute-start.5 = (bf16[128,512]{1,0:T(8,128)(2,1)S(1)}, bf16[128,512]{1,0:T(8,128)(2,1)S(1)}, u32[]{:S(2)}, u32[]{:S(2)}) collective-permute-start(bf16[128,512]{1,0:T(8,128)(2,1)S(1)} %get-tuple-element.50), channel_id=1, source_target_pairs={{0,16},{16,0},{1,17},{17,1},{2,18},{18,2},{3,19},{19,3},{4,20},{20... | collective-permute-start | bytes 393224 | tf_op jit(solution)/shard_map/ppermute | solution.py:306
  52.5 9.2 %collective-permute-start.1 = (s32[8,256]{1,0:T(8,128)S(1)}, s32[8,256]{1,0:T(8,128)S(1)}, u32[]{:S(2)}, u32[]{:S(2)}) collective-permute-start(s32[8,256]{1,0:T(8,128)S(1)} %shard_map.74.refs_2_.refs_0_.row_steps), channel_id=1, source_target_pairs={{0,16},{16,0},{1,17},{17,1},{2,18},{18,2},{3,19},{19,3},{4,20},{20... | collective-permute-start | bytes 24584 | tf_op jit(solution)/shard_map/ppermute | solution.py:306
  63.0 1.4 %collective-permute-start.8 = (f32[64,512]{1,0:T(8,128)S(1)}, f32[64,512]{1,0:T(8,128)S(1)}, u32[]{:S(2)}, u32[]{:S(2)}) collective-permute-start(f32[64,512]{1,0:T(8,128)S(1)} %get-tuple-element.55.refs_0_), channel_id=1, source_target_pairs={{0,1},{1,0},{2,3},{3,2},{4,5},{5,4},{6,7},{7,6},{8,9},{9,8},{10,11... | collective-permute-start | bytes 393224 | tf_op jit(solution)/shard_map/ppermute | solution.py:309
  63.1 4.9 %collective-permute-start.10 = (bf16[64,512]{1,0:T(8,128)(2,1)S(1)}, bf16[64,512]{1,0:T(8,128)(2,1)S(1)}, u32[]{:S(2)}, u32[]{:S(2)}) collective-permute-start(bf16[64,512]{1,0:T(8,128)(2,1)S(1)} %get-tuple-element.60), channel_id=1, source_target_pairs={{0,16},{16,0},{1,17},{17,1},{2,18},{18,2},{3,19},{19,3},{4,20},{20... | collective-permute-start | bytes 196616 | tf_op jit(solution)/shard_map/ppermute | solution.py:306
  64.5 4.6 %collective-permute-start.9 = (f32[64,256]{1,0:T(8,128)S(1)}, f32[64,256]{1,0:T(8,128)S(1)}, u32[]{:S(2)}, u32[]{:S(2)}) collective-permute-start(f32[64,256]{1,0:T(8,128)S(1)} %slice_add_fusion), channel_id=1, source_target_pairs={{0,16},{16,0},{1,17},{17,1},{2,18},{18,2},{3,19},{19,3},{4,20},{20... | collective-permute-start | bytes 196616 | tf_op jit(solution)/shard_map/ppermute | solution.py:306

commit v18 on v17

--- a/solution.py
+++ b/solution.py
@@ -84,7 +84,7 @@
 def pack(groups, columns, adapter_home, fetch_list, panels, expand_panels):
     rank, depth = panels.shape[1:]
     shape = (rank, depth + columns)
-    cuts = 2
+    cuts = 4
     return list(
         pl.pallas_call(
             functools.partial(pack_kernel, groups),
@@ -316,7 +316,6 @@
     tokens_of = [tokens] + [shift_parts(tokens, shift) for shift in range(1, parts)]
     solo_recv = recv[len(far) + len(near) :]
     near_recv = recv[len(far) : len(far) + len(near)]
-    seg_len, base_weight, solo_recv = tie((seg_len, base_weight, solo_recv))
     base = base_terms(tokens, base_weight, cores)
     base, recv[: len(far) - 1] = tie((base, recv[: len(far) - 1]))
     base = base[:1] + [shift_cores(x, shift + 1) for shift, x in enumerate(base[1:])]

time: 70.5 us -> 70.5 us (level)
  transfers between devices with their start and end apart: 11 -> 11, of which waited for: 6 -> 5; matrix products, arithmetic and copies ran while one was open for 0% -> 0% of each run, Pallas kernels for 10% -> 10%
where the time goes in v18:
time: 70.5 us; the launch traced here: 70.3 us
  waiting for transfers between devices  41.5 us (59%)
  Pallas kernels  13.2 us (19%)
  starting transfers between devices  12 us (17%)
  local copies, waits for them, and re-layouts  3.41 us (5%)
    ppermute x4, waiting for transfers between devices, hop(): return lax.ppermute(x, ('parts', 'rep'), pairs)  37.2 us
    ppermute x5, starting transfers between devices, shift_parts(): lax.ppermute(x, 'parts', [(i, (i + shift) % parts) for i in range(parts)])  5.99 us
    ppermute x4, starting transfers between devices, hop(): return lax.ppermute(x, ('parts', 'rep'), pairs)  5.96 us
    pallas_call x1, Pallas kernels, base_terms(): pl.pallas_call(functools.partial(base_kernel, chunks), out_shape=[jax.Sha...  3.96 us
    pallas_call x1, Pallas kernels, pack(): pl.pallas_call(functools.partial(pack_kernel, groups), out_shape=[jax.Sha...  3.69 us
    unnamed x14, local copies, waits for them, and re-layouts  3.41 us
    ppermute x5, waiting for transfers between devices, shift_parts(): lax.ppermute(x, 'parts', [(i, (i + shift) % parts) for i in range(parts)])  3.05 us
    pallas_call x2, Pallas kernels, score(): pl.pallas_call(functools.partial(score_kernel, plan, groups, kept, own, c...  2.84 us
  transfers between devices with their start and end apart: 11, of which 5 were waited for; matrix products, arithmetic and copies ran while one was open for 0% of the time, Pallas kernels for 10%

profile of v18, /device:TPU:0, one launch (start us, length us, event | category | flops | bytes accessed | tf_op | source)
XLA Modules:
  0.0 70.3 jit_solution(12134866676620498986)
XLA Ops:
  0.0 3.7 %shard_map.74 = (bf16[64,4608]{1,0:T(8,128)(2,1)}, bf16[64,4608]{1,0:T(8,128)(2,1)}, bf16[64,4608]{1,0:T(8,128)(2,1)}, bf16[64,4608]{1,0:T(8,128)(2,1)}) custom-call(s32[32]{0:T(128)} %refs_0_.1, s32[8,8]{1,0:T(8,128)} %refs_1_.1, bf16[4,64,4096]{2,1,0:T(8,128)(2,1)} %bitcast.1, bf16[4,64,1024]{2,1,0:T(8,128)(2,1)} %refs_8_.1), custom_call_target="tpu_custom_call" | custom-call | tf_op jit(solution)/shard_map/pallas_call | solution.py:89
  3.7 0.0 copy-start.4
  3.7 0.0 copy-start.5
  3.7 0.0 copy-start.6
  3.8 3.0 %collective-permute-start.6 = (bf16[256,4096]{1,0:T(8,128)(2,1)S(1)}, bf16[256,4096]{1,0:T(8,128)(2,1)S(1)}, u32[]{:S(2)}, u32[]{:S(2)}) collective-permute-start(bf16[256,4096]{1,0:T(8,128)(2,1)S(1)} %copy-done), channel_id=1, source_target_pairs={{0,16},{16,0},{1,17},{17,1},{2,18},{18,2},{3,19},{19,3},{4,20},{20... | collective-permute-start | bytes 6291464 | tf_op jit(solution)/shard_map/ppermute | solution.py:306
  6.8 2.6 %collective-permute-start.1 = (bf16[64,4608]{1,0:T(8,128)(2,1)}, bf16[64,4608]{1,0:T(8,128)(2,1)S(1)}, u32[]{:S(2)}, u32[]{:S(2)}) collective-permute-start(bf16[64,4608]{1,0:T(8,128)(2,1)} %get-tuple-element.37), channel_id=1, source_target_pairs={{0,8},{2,10},{4,12},{6,14},{8,0},{10,2},{12,4},{14,6},{16,28},{18,... | collective-permute-start | bytes 1769480 | tf_op jit(solution)/shard_map/ppermute | solution.py:303
  9.3 1.6 %collective-permute-start.3 = (bf16[64,4608]{1,0:T(8,128)(2,1)}, bf16[64,4608]{1,0:T(8,128)(2,1)S(1)}, u32[]{:S(2)}, u32[]{:S(2)}) collective-permute-start(bf16[64,4608]{1,0:T(8,128)(2,1)} %get-tuple-element.40), channel_id=1, source_target_pairs={{0,4},{2,6},{4,0},{6,2},{8,12},{10,14},{12,8},{14,10},{16,22},{18,... | collective-permute-start | bytes 1769480 | tf_op jit(solution)/shard_map/ppermute | solution.py:303
  10.9 1.5 %collective-permute-start.4 = (bf16[64,4608]{1,0:T(8,128)(2,1)}, bf16[64,4608]{1,0:T(8,128)(2,1)S(1)}, u32[]{:S(2)}, u32[]{:S(2)}) collective-permute-start(bf16[64,4608]{1,0:T(8,128)(2,1)} %get-tuple-element.42), channel_id=1, source_target_pairs={{0,2},{2,0},{4,6},{6,4},{8,10},{10,8},{12,14},{14,12},{16,18},{18,... | collective-permute-start | bytes 1769480 | tf_op jit(solution)/shard_map/ppermute | solution.py:303
  12.4 0.3 collective-permute-start.7
  12.7 3.4 %copy-done.1 = bf16[4096,1024]{1,0:T(8,128)(2,1)S(1)} copy-done((bf16[4096,1024]{1,0:T(8,128)(2,1)S(1)}, bf16[4096,1024]{1,0:T(8,128)(2,1)}, u32[]{:S(2)}) %copy-start.1) | copy-done | bytes 8388632
  16.1 4.0 %shard_map.75 = (f32[256,512]{1,0:T(8,128)S(1)}, f32[256,512]{1,0:T(8,128)S(1)}) custom-call(bf16[256,4096]{1,0:T(8,128)(2,1)S(1)} %copy-done, bf16[4096,1024]{1,0:T(8,128)(2,1)S(1)} %copy-done.1), custom_call_target="tpu_custom_call" | custom-call | tf_op jit(solution)/shard_map/pallas_call | solution.py:211
  20.1 29.1 %collective-permute-done.1.refs_5_.refs_7_.refs_6_ = bf16[64,4608]{1,0:T(8,128)(2,1)S(1)} collective-permute-done((bf16[64,4608]{1,0:T(8,128)(2,1)}, bf16[64,4608]{1,0:T(8,128)(2,1)S(1)}, u32[]{:S(2)}, u32[]{:S(2)}) %collective-permute-start.1) | collective-permute-done | bytes 589856 | tf_op jit(solution)/shard_map/ppermute | solution.py:303
  49.1 0.0 collective-permute-start.2
  49.2 0.6 shard_map.73.refs_2_.refs_0_.row_steps
  49.8 0.0 collective-permute-done.3.refs_4_.refs_6_.refs_5_
  49.8 0.0 collective-permute-done.4.refs_6_.refs_7_
  49.9 1.5 %shard_map.76 = (f32[64,256]{1,0:T(8,128)S(1)}, bf16[128,512]{1,0:T(8,128)(2,1)S(1)}, bf16[64,512]{1,0:T(8,128)(2,1)S(1)}) custom-call(s32[32]{0:T(128)S(1)} %copy-done.5, s32[8,8]{1,0:T(8,128)S(1)} %copy-done.4, s32[8,256]{1,0:T(8,128)S(1)} %shard_map.73.refs_2_.refs_0_.row_steps, bf16[256,4096]{1,0:T(8,128)(2,1)S(1)} %copy-done, ...), custom_call_target="tpu_custom_call" | custom-call | tf_op jit(solution)/shard_map/pallas_call | solution.py:160
  51.3 1.3 %collective-permute-start.5 = (bf16[128,512]{1,0:T(8,128)(2,1)S(1)}, bf16[128,512]{1,0:T(8,128)(2,1)S(1)}, u32[]{:S(2)}, u32[]{:S(2)}) collective-permute-start(bf16[128,512]{1,0:T(8,128)(2,1)S(1)} %get-tuple-element.44), channel_id=1, source_target_pairs={{0,16},{16,0},{1,17},{17,1},{2,18},{18,2},{3,19},{19,3},{4,20},{20... | collective-permute-start | bytes 393224 | tf_op jit(solution)/shard_map/ppermute | solution.py:306
  52.7 0.8 %collective-permute-start = (s32[8,256]{1,0:T(8,128)S(1)}, s32[8,256]{1,0:T(8,128)S(1)}, u32[]{:S(2)}, u32[]{:S(2)}) collective-permute-start(s32[8,256]{1,0:T(8,128)S(1)} %shard_map.73.refs_2_.refs_0_.row_steps), channel_id=1, source_target_pairs={{0,16},{16,0},{1,17},{17,1},{2,18},{18,2},{3,19},{19,3},{4,20},{20... | collective-permute-start | bytes 24584 | tf_op jit(solution)/shard_map/ppermute | solution.py:306
  53.4 8.2 %collective-permute-done.7.refs_5_.refs_8_ = bf16[64,4608]{1,0:T(8,128)(2,1)S(1)} collective-permute-done((bf16[64,4608]{1,0:T(8,128)(2,1)}, bf16[64,4608]{1,0:T(8,128)(2,1)S(1)}, u32[]{:S(2)}, u32[]{:S(2)}) %collective-permute-start.7) | collective-permute-done | bytes 589856 | tf_op jit(solution)/shard_map/ppermute | solution.py:303
  61.6 0.0 collective-permute-done.5.refs_2_
  61.6 0.0 collective-permute-done.2.refs_3_
  61.6 0.0 collective-permute-done.6.refs_4_
  61.6 1.4 %shard_map.77 = (f32[64,512]{1,0:T(8,128)S(1)}, bf16[64,512]{1,0:T(8,128)(2,1)S(1)}) custom-call(s32[8,256]{1,0:T(8,128)S(1)} %shard_map.73.refs_2_.refs_0_.row_steps, s32[8,256]{1,0:T(8,128)S(1)} %collective-permute-done.refs_1_, f32[64,256]{1,0:T(8,128)S(1)} %get-tuple-element.46.refs_2_, bf16[256,4096]{1,0:T(8,128)(2,1)S(1)} %copy-done, ...), custom_call_target="tpu_custom_call" | custom-call | tf_op jit(solution)/shard_map/pallas_call | solution.py:160
  63.0 0.1 collective-permute-start.8
  63.1 0.1 collective-permute-start.10
  63.1 1.3 %collective-permute-done.8.refs_1_ = f32[64,512]{1,0:T(8,128)S(1)} collective-permute-done((f32[64,512]{1,0:T(8,128)S(1)}, f32[64,512]{1,0:T(8,128)S(1)}, u32[]{:S(2)}, u32[]{:S(2)}) %collective-permute-start.8) | collective-permute-done | bytes 131104 | tf_op jit(solution)/shard_map/ppermute | solution.py:309
  64.4 0.8 %collective-permute-start.9 = (f32[64,256]{1,0:T(8,128)S(1)}, f32[64,256]{1,0:T(8,128)S(1)}, u32[]{:S(2)}, u32[]{:S(2)}) collective-permute-start(f32[64,256]{1,0:T(8,128)S(1)} %slice_add_fusion), channel_id=1, source_target_pairs={{0,16},{16,0},{1,17},{17,1},{2,18},{18,2},{3,19},{19,3},{4,20},{20... | collective-permute-start | bytes 196616 | tf_op jit(solution)/shard_map/ppermute | solution.py:306
  65.2 0.7 shard_map.78.refs_1_
  65.9 2.1 %collective-permute-done.10.refs_3_ = bf16[64,512]{1,0:T(8,128)(2,1)S(1)} collective-permute-done((bf16[64,512]{1,0:T(8,128)(2,1)S(1)}, bf16[64,512]{1,0:T(8,128)(2,1)S(1)}, u32[]{:S(2)}, u32[]{:S(2)}) %collective-permute-start.10) | collective-permute-done | bytes 65568 | tf_op jit(solution)/shard_map/ppermute | solution.py:306
  68.0 1.0 %collective-permute-done.9.refs_0_ = f32[64,256]{1,0:T(8,128)S(1)} collective-permute-done((f32[64,256]{1,0:T(8,128)S(1)}, f32[64,256]{1,0:T(8,128)S(1)}, u32[]{:S(2)}, u32[]{:S(2)}) %collective-permute-start.9) | collective-permute-done | bytes 65568 | tf_op jit(solution)/shard_map/ppermute | solution.py:306
  69.0 1.3 %shard_map.79 = bf16[256,512]{1,0:T(8,128)(2,1)} custom-call(s32[8,256]{1,0:T(8,128)S(1)} %shard_map.73.refs_2_.refs_0_.row_steps, f32[64,256]{1,0:T(8,128)S(1)} %collective-permute-done.9.refs_0_, f32[256,512]{1,0:T(8,128)S(1)} %shard_map.78.refs_1_, bf16[128,512]{1,0:T(8,128)(2,1)S(1)} %collective-permute-done.5.refs_2_, ...), custom_call_target="tpu_custom_call" | custom-call | tf_op jit(solution)/shard_map/pallas_call | solution.py:263
  (12 shorter events, 0.0 us)
Async XLA Ops:
  0.0 3.7 %copy-start = (bf16[256,4096]{1,0:T(8,128)(2,1)S(1)}, bf16[256,4096]{1,0:T(8,128)(2,1)}, u32[]{:S(2)}) copy-start(bf16[256,4096]{1,0:T(8,128)(2,1)} %refs_3_.1) | copy-start | bytes 6291460
  3.7 45.4 %copy-start.4 = (s32[8,8]{1,0:T(8,128)S(1)}, s32[8,8]{1,0:T(8,128)}, u32[]{:S(2)}) copy-start(s32[8,8]{1,0:T(8,128)} %refs_1_.1) | copy-start | bytes 772
  3.7 45.4 %copy-start.5 = (s32[32]{0:T(128)S(1)}, s32[32]{0:T(128)}, u32[]{:S(2)}) copy-start(s32[32]{0:T(128)} %refs_0_.1) | copy-start | bytes 388
  3.7 45.4 %copy-start.6 = (s32[1,8]{1,0:T(1,128)S(1)}, s32[1,8]{1,0:T(1,128)}, u32[]{:S(2)}) copy-start(s32[1,8]{1,0:T(1,128)} %lengths_ref.1) | copy-start | bytes 100
  3.8 57.8 %collective-permute-start.6 = (bf16[256,4096]{1,0:T(8,128)(2,1)S(1)}, bf16[256,4096]{1,0:T(8,128)(2,1)S(1)}, u32[]{:S(2)}, u32[]{:S(2)}) collective-permute-start(bf16[256,4096]{1,0:T(8,128)(2,1)S(1)} %copy-done), channel_id=1, source_target_pairs={{0,16},{16,0},{1,17},{17,1},{2,18},{18,2},{3,19},{19,3},{4,20},{20... | collective-permute-start | bytes 6291464 | tf_op jit(solution)/shard_map/ppermute | solution.py:306
  6.8 42.4 %collective-permute-start.1 = (bf16[64,4608]{1,0:T(8,128)(2,1)}, bf16[64,4608]{1,0:T(8,128)(2,1)S(1)}, u32[]{:S(2)}, u32[]{:S(2)}) collective-permute-start(bf16[64,4608]{1,0:T(8,128)(2,1)} %get-tuple-element.37), channel_id=1, source_target_pairs={{0,8},{2,10},{4,12},{6,14},{8,0},{10,2},{12,4},{14,6},{16,28},{18,... | collective-permute-start | bytes 1769480 | tf_op jit(solution)/shard_map/ppermute | solution.py:303
  9.3 40.5 %collective-permute-start.3 = (bf16[64,4608]{1,0:T(8,128)(2,1)}, bf16[64,4608]{1,0:T(8,128)(2,1)S(1)}, u32[]{:S(2)}, u32[]{:S(2)}) collective-permute-start(bf16[64,4608]{1,0:T(8,128)(2,1)} %get-tuple-element.40), channel_id=1, source_target_pairs={{0,4},{2,6},{4,0},{6,2},{8,12},{10,14},{12,8},{14,10},{16,22},{18,... | collective-permute-start | bytes 1769480 | tf_op jit(solution)/shard_map/ppermute | solution.py:303
  10.9 38.9 %collective-permute-start.4 = (bf16[64,4608]{1,0:T(8,128)(2,1)}, bf16[64,4608]{1,0:T(8,128)(2,1)S(1)}, u32[]{:S(2)}, u32[]{:S(2)}) collective-permute-start(bf16[64,4608]{1,0:T(8,128)(2,1)} %get-tuple-element.42), channel_id=1, source_target_pairs={{0,2},{2,0},{4,6},{6,4},{8,10},{10,8},{12,14},{14,12},{16,18},{18,... | collective-permute-start | bytes 1769480 | tf_op jit(solution)/shard_map/ppermute | solution.py:303
  12.4 49.1 %collective-permute-start.7 = (bf16[64,4608]{1,0:T(8,128)(2,1)}, bf16[64,4608]{1,0:T(8,128)(2,1)S(1)}, u32[]{:S(2)}, u32[]{:S(2)}) collective-permute-start(bf16[64,4608]{1,0:T(8,128)(2,1)} %get-tuple-element.45), channel_id=1, source_target_pairs={{0,10},{2,8},{4,14},{6,12},{8,2},{10,0},{12,6},{14,4},{16,30},{18,... | collective-permute-start | bytes 1769480 | tf_op jit(solution)/shard_map/ppermute | solution.py:303
  12.7 3.4 %copy-start.1 = (bf16[4096,1024]{1,0:T(8,128)(2,1)S(1)}, bf16[4096,1024]{1,0:T(8,128)(2,1)}, u32[]{:S(2)}) copy-start(bf16[4096,1024]{1,0:T(8,128)(2,1)} %weight_ref.1) | copy-start | bytes 25165828
  16.1 33.7 %copy-start.2 = (bf16[4,4096,64]{1,2,0:T(8,128)(2,1)S(1)}, bf16[4,4096,64]{1,2,0:T(8,128)(2,1)}, u32[]{:S(2)}) copy-start(bf16[4,4096,64]{1,2,0:T(8,128)(2,1)} %param.9) | copy-start | bytes 6291460
  16.1 33.7 %copy-start.3 = (bf16[4,64,1024]{2,1,0:T(8,128)(2,1)S(1)}, bf16[4,64,1024]{2,1,0:T(8,128)(2,1)}, u32[]{:S(2)}) copy-start(bf16[4,64,1024]{2,1,0:T(8,128)(2,1)} %refs_8_.1) | copy-start | bytes 1572868
  49.1 12.4 %collective-permute-start.2 = (f32[256,512]{1,0:T(8,128)S(1)}, f32[256,512]{1,0:T(8,128)S(1)}, u32[]{:S(2)}, u32[]{:S(2)}) collective-permute-start(f32[256,512]{1,0:T(8,128)S(1)} %get-tuple-element.39), channel_id=1, source_target_pairs={{0,1},{1,0},{2,3},{3,2},{4,5},{5,4},{6,7},{7,6},{8,9},{9,8},{10,11... | collective-permute-start | bytes 1572872 | tf_op jit(solution)/shard_map/ppermute | solution.py:309
  51.3 10.3 %collective-permute-start.5 = (bf16[128,512]{1,0:T(8,128)(2,1)S(1)}, bf16[128,512]{1,0:T(8,128)(2,1)S(1)}, u32[]{:S(2)}, u32[]{:S(2)}) collective-permute-start(bf16[128,512]{1,0:T(8,128)(2,1)S(1)} %get-tuple-element.44), channel_id=1, source_target_pairs={{0,16},{16,0},{1,17},{17,1},{2,18},{18,2},{3,19},{19,3},{4,20},{20... | collective-permute-start | bytes 393224 | tf_op jit(solution)/shard_map/ppermute | solution.py:306
  52.7 8.9 %collective-permute-start = (s32[8,256]{1,0:T(8,128)S(1)}, s32[8,256]{1,0:T(8,128)S(1)}, u32[]{:S(2)}, u32[]{:S(2)}) collective-permute-start(s32[8,256]{1,0:T(8,128)S(1)} %shard_map.73.refs_2_.refs_0_.row_steps), channel_id=1, source_target_pairs={{0,16},{16,0},{1,17},{17,1},{2,18},{18,2},{3,19},{19,3},{4,20},{20... | collective-permute-start | bytes 24584 | tf_op jit(solution)/shard_map/ppermute | solution.py:306
  63.0 1.4 %collective-permute-start.8 = (f32[64,512]{1,0:T(8,128)S(1)}, f32[64,512]{1,0:T(8,128)S(1)}, u32[]{:S(2)}, u32[]{:S(2)}) collective-permute-start(f32[64,512]{1,0:T(8,128)S(1)} %get-tuple-element.49.refs_0_), channel_id=1, source_target_pairs={{0,1},{1,0},{2,3},{3,2},{4,5},{5,4},{6,7},{7,6},{8,9},{9,8},{10,11... | collective-permute-start | bytes 393224 | tf_op jit(solution)/shard_map/ppermute | solution.py:309
  63.1 4.9 %collective-permute-start.10 = (bf16[64,512]{1,0:T(8,128)(2,1)S(1)}, bf16[64,512]{1,0:T(8,128)(2,1)S(1)}, u32[]{:S(2)}, u32[]{:S(2)}) collective-permute-start(bf16[64,512]{1,0:T(8,128)(2,1)S(1)} %get-tuple-element.54), channel_id=1, source_target_pairs={{0,16},{16,0},{1,17},{17,1},{2,18},{18,2},{3,19},{19,3},{4,20},{20... | collective-permute-start | bytes 196616 | tf_op jit(solution)/shard_map/ppermute | solution.py:306
  64.4 4.6 %collective-permute-start.9 = (f32[64,256]{1,0:T(8,128)S(1)}, f32[64,256]{1,0:T(8,128)S(1)}, u32[]{:S(2)}, u32[]{:S(2)}) collective-permute-start(f32[64,256]{1,0:T(8,128)S(1)} %slice_add_fusion), channel_id=1, source_target_pairs={{0,16},{16,0},{1,17},{17,1},{2,18},{18,2},{3,19},{19,3},{4,20},{20... | collective-permute-start | bytes 196616 | tf_op jit(solution)/shard_map/ppermute | solution.py:306

commit v19 on v18

--- a/solution.py
+++ b/solution.py
@@ -99,32 +99,15 @@
     )
 
 
-def score_kernel(plan, groups, kept, own, chunks, has_prior, *refs):
+def score_kernel(plan, groups, kept, chunks, has_prior, *refs):
     sets, many = len(plan), len(groups)
-    tables, refs = (refs[:2], refs[2:]) if own else (None, refs)
     row_steps, refs = refs[:sets], refs[sets:]
     prior, refs = (refs[0], refs[1:]) if has_prior else (None, refs)
-    tokens, panels, refs = refs[:sets], refs[sets : sets + many], refs[sets + many :]
-    expand_ref, refs = (refs[0], refs[1:]) if own else (None, refs)
-    out, out_expand, refs = refs[0], refs[1], refs[2:]
+    tokens, panels = refs[:sets], refs[sets : sets + many]
+    out, out_expand = refs[sets + many :]
     rank, (count, depth) = out.shape[0], tokens[0].shape
-    columns = out_expand.shape[1]
-    copies = []
-    if own:
-        out_own, held, sems = refs
-        me = lax.axis_index("rep")
-        slot = slot_for(me, me, panels[-1].shape[0], *tables)
-        left = pl.multiple_of(lax.axis_index("tp") * columns, 128)
-        for n, (source, target) in enumerate(
-            ((panels[-1].at[slot], held), (expand_ref.at[slot, :, pl.ds(left, columns)], out_own))
-        ):
-            copies.append(pltpu.make_async_copy(source, target, sems.at[n]))
-            copies[-1].start()
-        panels = panels[:-1] + (held,)
     for i, n in enumerate(kept):
-        out_expand[pl.ds(i * rank, rank), :] = panels[n][:, pl.ds(depth, columns)]
-    for copy in copies:
-        copy.wait()
+        out_expand[pl.ds(i * rank, rank), :] = panels[n][:, pl.ds(depth, out_expand.shape[1])]
     width = depth // chunks
     sums = [None] * sets
     for c in range(chunks):
@@ -146,31 +129,26 @@
         out[:, pl.ds(t * count, count)] = total
 
 
-def score(plan, groups, kept, columns, row_steps, tokens_of, panels, prior=None, tables=None):
+def score(plan, groups, kept, columns, row_steps, tokens_of, panels, prior=None):
     count, depth = tokens_of[0].shape
     rank = panels[0].shape[0]
     chunks = 4
-    own = tables is not None
     prior = [] if prior is None else [prior]
-    smem, vmem = pl.BlockSpec(memory_space=pltpu.SMEM), pl.BlockSpec(memory_space=pltpu.VMEM)
-    anywhere = pl.BlockSpec(memory_space=pl.ANY)
-    outs = [(rank, len(plan) * count), (len(kept) * rank, columns)] + [(rank, columns)] * own
+    vmem = pl.BlockSpec(memory_space=pltpu.VMEM)
+    outs = [(rank, len(plan) * count), (len(kept) * rank, columns)]
     arrays = list(row_steps) + prior + list(tokens_of) + list(panels)
     need = 4 * len(plan) * count * (rank * len(panels) + depth) + 4 * len(panels) * rank * (depth + columns)
     return pl.pallas_call(
-        functools.partial(score_kernel, plan, groups, kept, own, chunks, bool(prior)),
+        functools.partial(score_kernel, plan, groups, kept, chunks, bool(prior)),
         out_shape=[
             jax.ShapeDtypeStruct(shape, panels[0].dtype if n else jnp.float32)
             for n, shape in enumerate(outs)
         ],
-        in_specs=[smem] * (2 * own)
-        + [vmem] * (len(arrays) - own)
-        + [anywhere] * (2 * own),
+        in_specs=[vmem] * len(arrays),
         out_specs=[vmem] * len(outs),
-        scratch_shapes=[pltpu.VMEM((rank, depth), tokens_of[0].dtype), pltpu.SemaphoreType.DMA((2,))] * own,
         compiler_params=pltpu.CompilerParams(vmem_limit_bytes=need + (2 << 20)),
         cost_estimate=pl.CostEstimate(flops=0, bytes_accessed=0, transcendentals=0),
-    )(*(tables[:2] if own else ()), *arrays, *([tables[3]] if own else ()))
+    )(*arrays)
 
 
 def base_kernel(chunks, tokens_ref, weight_ref, *refs):
@@ -283,16 +261,14 @@
     rank = panels.shape[1]
     tie = lax.optimization_barrier
 
-    alone, half = max(2, parts), replicas // 2
+    half = replicas // 2
 
     def grouped(steps):
         size = len(steps) // parts
         return [tuple(steps[p * size + g] for p in range(parts)) for g in range(size)]
 
     far = grouped(list(range(half, replicas)))
-    near = grouped(list(range(alone, half)))
-    groups = far + near
-    solo = [(step,) * parts for step in range(1, alone)]
+    near = grouped(list(range(parts, half))) + [tuple(reversed(range(parts)))]
 
     def hop(x, group):
         pairs = [
@@ -309,31 +285,28 @@
         return lax.ppermute(x, "tp", [(i, (i + shift) % cores) for i in range(cores)])
 
     tables = (adapter_home, fetch_list, panels, expand_panels)
-    groups = far + near + solo
+    groups = far + near
     send = pack(groups, columns, *tables)
     tokens, send = tie((tokens, send))
     recv = [hop(x, group) for x, group in zip(send, groups)]
     tokens_of = [tokens] + [shift_parts(tokens, shift) for shift in range(1, parts)]
-    solo_recv = recv[len(far) + len(near) :]
-    near_recv = recv[len(far) : len(far) + len(near)]
     base = base_terms(tokens, base_weight, cores)
     base, recv[: len(far) - 1] = tie((base, recv[: len(far) - 1]))
     base = base[:1] + [shift_cores(x, shift + 1) for shift, x in enumerate(base[1:])]
     row_steps = steps_of_rows(tok_count, panels.shape[0], adapter_home, fetch_list, seg_len)
     steps_of = [row_steps] + [shift_parts(row_steps, shift) for shift in range(1, parts)]
-    early, early_groups = near_recv + recv[: len(far) - 1], near + far[:-1]
-    last, last_group, own_group = recv[len(far) - 1], far[-1], (0,) * parts
+    early, early_groups = recv[len(far) :] + recv[: len(far) - 1], near + far[:-1]
+    last, last_group = recv[len(far) - 1], far[-1]
 
     count = len(early)
-    first, sent, own_expand = score(
-        [tuple(range(count + len(solo) + 1))],
-        early_groups + solo + [own_group],
+    first, sent = score(
+        [tuple(range(count))],
+        early_groups,
         tuple(range(count)),
         columns,
         steps_of[:1],
         [tokens],
-        early + solo_recv + [panels],
-        tables=tables,
+        early,
     )
     passed = [shift_parts(sent, shift) for shift in range(1, parts)]
     base, first, passed, tokens_of[1:], last = tie((base, first, passed, tokens_of[1:], last))
@@ -356,9 +329,8 @@
         shift_parts(whole[:, shift * tok_count : (shift + 1) * tok_count], -shift)
         for shift in range(1, parts)
     ]
-    arrays = [own_expand] + early + solo_recv + [last]
-    pieces = [(n, 0, group) for n, group in enumerate([own_group] + early_groups + solo + [last_group])]
-    result = end(pieces, row_steps, halves, base, arrays, jnp.float32, 1 << 24)
+    pieces = [(n, 0, group) for n, group in enumerate(early_groups + [last_group])]
+    result = end(pieces, row_steps, halves, base, early + [last], jnp.float32, 1 << 24)
     pieces = []
     for shift in range(1, parts):
         at = shift - 1

time: 70.5 us -> 70.5 us (level)
  starting transfers between devices: 12 us -> 14 us
  waiting for transfers between devices: 41.5 us -> 40.5 us
  Pallas kernels: 13.2 us -> 12.3 us
    ppermute x4, starting transfers between devices: 5.96 us -> 7.92 us  [hop(): return lax.ppermute(x, ('parts', 'rep'), pairs)]
    ppermute x4, waiting for transfers between devices: 37.2 us -> 35.9 us  [hop(): return lax.ppermute(x, ('parts', 'rep'), pairs)]
    unnamed x14 -> x10, local copies, waits for them, and re-layouts: 3.41 us -> 3.4 us
  transfers between devices with their start and end apart: 11 -> 11, of which waited for: 5 -> 5; matrix products, arithmetic and copies ran while one was open for 0% -> 0% of each run, Pallas kernels for 10% -> 8%
where the time goes in v19:
time: 70.5 us; the launch traced here: 70.3 us
  waiting for transfers between devices  40.5 us (57%)
  starting transfers between devices  14 us (20%)
  Pallas kernels  12.3 us (17%)
  local copies, waits for them, and re-layouts  3.4 us (5%)
    ppermute x4, waiting for transfers between devices, hop(): return lax.ppermute(x, ('parts', 'rep'), pairs)  35.9 us
    ppermute x4, starting transfers between devices, hop(): return lax.ppermute(x, ('parts', 'rep'), pairs)  7.92 us
    ppermute x5, starting transfers between devices, shift_parts(): lax.ppermute(x, 'parts', [(i, (i + shift) % parts) for i in range(parts)])  5.98 us
    pallas_call x1, Pallas kernels, base_terms(): pl.pallas_call(functools.partial(base_kernel, chunks), out_shape=[jax.Sha...  3.92 us
    pallas_call x1, Pallas kernels, pack(): pl.pallas_call(functools.partial(pack_kernel, groups), out_shape=[jax.Sha...  3.7 us
    unnamed x10, local copies, waits for them, and re-layouts  3.4 us
    ppermute x5, waiting for transfers between devices, shift_parts(): lax.ppermute(x, 'parts', [(i, (i + shift) % parts) for i in range(parts)])  3.27 us
    pallas_call x2, Pallas kernels, score(): pl.pallas_call(functools.partial(score_kernel, plan, groups, kept, chunks...  2.15 us
  transfers between devices with their start and end apart: 11, of which 5 were waited for; matrix products, arithmetic and copies ran while one was open for 0% of the time, Pallas kernels for 8%

profile of v19, /device:TPU:0, one launch (start us, length us, event | category | flops | bytes accessed | tf_op | source)
XLA Modules:
  0.0 70.3 jit_solution(14954898168000958781)
XLA Ops:
  0.0 3.7 %shard_map.74 = (bf16[64,4608]{1,0:T(8,128)(2,1)}, bf16[64,4608]{1,0:T(8,128)(2,1)}, bf16[64,4608]{1,0:T(8,128)(2,1)}, bf16[64,4608]{1,0:T(8,128)(2,1)}) custom-call(s32[32]{0:T(128)} %home_ref.3, s32[8,8]{1,0:T(8,128)} %fetch_ref.3, bf16[4,64,4096]{2,1,0:T(8,128)(2,1)} %bitcast.1, bf16[4,64,1024]{2,1,0:T(8,128)(2,1)} %expand_ref.1), custom_call_target="tpu_custom_call" | custom-call | tf_op jit(solution)/shard_map/pallas_call | solution.py:89
  3.7 0.0 copy-start.2
  3.7 0.0 copy-start.3
  3.7 0.0 copy-start.4
  3.8 3.0 %collective-permute-start.6 = (bf16[256,4096]{1,0:T(8,128)(2,1)S(1)}, bf16[256,4096]{1,0:T(8,128)(2,1)S(1)}, u32[]{:S(2)}, u32[]{:S(2)}) collective-permute-start(bf16[256,4096]{1,0:T(8,128)(2,1)S(1)} %copy-done), channel_id=1, source_target_pairs={{0,16},{16,0},{1,17},{17,1},{2,18},{18,2},{3,19},{19,3},{4,20},{20... | collective-permute-start | bytes 6291464 | tf_op jit(solution)/shard_map/ppermute | solution.py:282
  6.8 2.6 %collective-permute-start.1 = (bf16[64,4608]{1,0:T(8,128)(2,1)}, bf16[64,4608]{1,0:T(8,128)(2,1)S(1)}, u32[]{:S(2)}, u32[]{:S(2)}) collective-permute-start(bf16[64,4608]{1,0:T(8,128)(2,1)} %get-tuple-element.36), channel_id=1, source_target_pairs={{0,8},{2,10},{4,12},{6,14},{8,0},{10,2},{12,4},{14,6},{16,28},{18,... | collective-permute-start | bytes 1769480 | tf_op jit(solution)/shard_map/ppermute | solution.py:279
  9.3 1.6 %collective-permute-start.3 = (bf16[64,4608]{1,0:T(8,128)(2,1)}, bf16[64,4608]{1,0:T(8,128)(2,1)S(1)}, u32[]{:S(2)}, u32[]{:S(2)}) collective-permute-start(bf16[64,4608]{1,0:T(8,128)(2,1)} %get-tuple-element.39), channel_id=1, source_target_pairs={{0,4},{2,6},{4,0},{6,2},{8,12},{10,14},{12,8},{14,10},{16,22},{18,... | collective-permute-start | bytes 1769480 | tf_op jit(solution)/shard_map/ppermute | solution.py:279
  10.9 3.4 %collective-permute-start.4 = (bf16[64,4608]{1,0:T(8,128)(2,1)}, bf16[64,4608]{1,0:T(8,128)(2,1)S(1)}, u32[]{:S(2)}, u32[]{:S(2)}) collective-permute-start(bf16[64,4608]{1,0:T(8,128)(2,1)} %get-tuple-element.40), channel_id=1, source_target_pairs={{0,2},{2,0},{4,6},{6,4},{8,10},{10,8},{12,14},{14,12},{16,16},{18,... | collective-permute-start | bytes 1769480 | tf_op jit(solution)/shard_map/ppermute | solution.py:279
  14.3 0.3 collective-permute-start.7
  14.7 3.4 %copy-done.1 = bf16[4096,1024]{1,0:T(8,128)(2,1)S(1)} copy-done((bf16[4096,1024]{1,0:T(8,128)(2,1)S(1)}, bf16[4096,1024]{1,0:T(8,128)(2,1)}, u32[]{:S(2)}) %copy-start.1) | copy-done | bytes 8388632
  18.1 3.9 %shard_map.75 = (f32[256,512]{1,0:T(8,128)S(1)}, f32[256,512]{1,0:T(8,128)S(1)}) custom-call(bf16[256,4096]{1,0:T(8,128)(2,1)S(1)} %copy-done, bf16[4096,1024]{1,0:T(8,128)(2,1)S(1)} %copy-done.1), custom_call_target="tpu_custom_call" | custom-call | tf_op jit(solution)/shard_map/pallas_call | solution.py:189
  22.0 27.1 %collective-permute-done.1.refs_4_.refs_8_.refs_6_ = bf16[64,4608]{1,0:T(8,128)(2,1)S(1)} collective-permute-done((bf16[64,4608]{1,0:T(8,128)(2,1)}, bf16[64,4608]{1,0:T(8,128)(2,1)S(1)}, u32[]{:S(2)}, u32[]{:S(2)}) %collective-permute-start.1) | collective-permute-done | bytes 589856 | tf_op jit(solution)/shard_map/ppermute | solution.py:279
  49.1 0.0 collective-permute-start.2
  49.2 0.6 shard_map.73.refs_0_.row_steps
  49.8 0.0 collective-permute-done.3.refs_2_.refs_6_.refs_4_
  49.8 0.0 collective-permute-done.4.refs_3_.refs_7_.refs_5_
  49.8 0.8 %shard_map.76 = (f32[64,256]{1,0:T(8,128)S(1)}, bf16[192,512]{1,0:T(8,128)(2,1)S(1)}) custom-call(s32[8,256]{1,0:T(8,128)S(1)} %shard_map.73.refs_0_.row_steps, bf16[256,4096]{1,0:T(8,128)(2,1)S(1)} %copy-done, bf16[64,4608]{1,0:T(8,128)(2,1)S(1)} %collective-permute-done.3.refs_2_.refs_6_.refs_4_, ...), custom_call_target="tpu_custom_call" | custom-call | tf_op jit(solution)/shard_map/pallas_call | solution.py:141
  50.7 0.1 collective-permute-start.5
  50.8 2.0 %collective-permute-start = (s32[8,256]{1,0:T(8,128)S(1)}, s32[8,256]{1,0:T(8,128)S(1)}, u32[]{:S(2)}, u32[]{:S(2)}) collective-permute-start(s32[8,256]{1,0:T(8,128)S(1)} %shard_map.73.refs_0_.row_steps), channel_id=1, source_target_pairs={{0,16},{16,0},{1,17},{17,1},{2,18},{18,2},{3,19},{19,3},{4,20},{20... | collective-permute-start | bytes 24584 | tf_op jit(solution)/shard_map/ppermute | solution.py:282
  52.8 8.8 %collective-permute-done.7.refs_5_.refs_7_ = bf16[64,4608]{1,0:T(8,128)(2,1)S(1)} collective-permute-done((bf16[64,4608]{1,0:T(8,128)(2,1)}, bf16[64,4608]{1,0:T(8,128)(2,1)S(1)}, u32[]{:S(2)}, u32[]{:S(2)}) %collective-permute-start.7) | collective-permute-done | bytes 589856 | tf_op jit(solution)/shard_map/ppermute | solution.py:279
  61.6 0.0 collective-permute-done.5.refs_2_
  61.6 0.0 collective-permute-done.2.refs_3_
  61.6 0.0 collective-permute-done.6.refs_4_
  61.6 1.3 %shard_map.77 = (f32[64,512]{1,0:T(8,128)S(1)}, bf16[64,512]{1,0:T(8,128)(2,1)S(1)}) custom-call(s32[8,256]{1,0:T(8,128)S(1)} %shard_map.73.refs_0_.row_steps, s32[8,256]{1,0:T(8,128)S(1)} %collective-permute-done.refs_1_, f32[64,256]{1,0:T(8,128)S(1)} %get-tuple-element.45.refs_2_, bf16[256,4096]{1,0:T(8,128)(2,1)S(1)} %copy-done, ...), custom_call_target="tpu_custom_call" | custom-call | tf_op jit(solution)/shard_map/pallas_call | solution.py:141
  62.9 0.1 collective-permute-start.8
  63.0 0.1 collective-permute-start.10
  63.1 1.3 %collective-permute-done.8.refs_1_ = f32[64,512]{1,0:T(8,128)S(1)} collective-permute-done((f32[64,512]{1,0:T(8,128)S(1)}, f32[64,512]{1,0:T(8,128)S(1)}, u32[]{:S(2)}, u32[]{:S(2)}) %collective-permute-start.8) | collective-permute-done | bytes 131104 | tf_op jit(solution)/shard_map/ppermute | solution.py:285
  64.3 0.8 %collective-permute-start.9 = (f32[64,256]{1,0:T(8,128)S(1)}, f32[64,256]{1,0:T(8,128)S(1)}, u32[]{:S(2)}, u32[]{:S(2)}) collective-permute-start(f32[64,256]{1,0:T(8,128)S(1)} %slice_add_fusion), channel_id=1, source_target_pairs={{0,16},{16,0},{1,17},{17,1},{2,18},{18,2},{3,19},{19,3},{4,20},{20... | collective-permute-start | bytes 196616 | tf_op jit(solution)/shard_map/ppermute | solution.py:282
  65.2 0.5 shard_map.78.refs_1_
  65.6 2.3 %collective-permute-done.10.refs_3_ = bf16[64,512]{1,0:T(8,128)(2,1)S(1)} collective-permute-done((bf16[64,512]{1,0:T(8,128)(2,1)S(1)}, bf16[64,512]{1,0:T(8,128)(2,1)S(1)}, u32[]{:S(2)}, u32[]{:S(2)}) %collective-permute-start.10) | collective-permute-done | bytes 65568 | tf_op jit(solution)/shard_map/ppermute | solution.py:282
  67.9 1.0 %collective-permute-done.9.refs_0_ = f32[64,256]{1,0:T(8,128)S(1)} collective-permute-done((f32[64,256]{1,0:T(8,128)S(1)}, f32[64,256]{1,0:T(8,128)S(1)}, u32[]{:S(2)}, u32[]{:S(2)}) %collective-permute-start.9) | collective-permute-done | bytes 65568 | tf_op jit(solution)/shard_map/ppermute | solution.py:282
  68.9 1.4 %shard_map.79 = bf16[256,512]{1,0:T(8,128)(2,1)} custom-call(s32[8,256]{1,0:T(8,128)S(1)} %shard_map.73.refs_0_.row_steps, f32[64,256]{1,0:T(8,128)S(1)} %collective-permute-done.9.refs_0_, f32[256,512]{1,0:T(8,128)S(1)} %shard_map.78.refs_1_, bf16[192,512]{1,0:T(8,128)(2,1)S(1)} %collective-permute-done.5.refs_2_, ...), custom_call_target="tpu_custom_call" | custom-call | tf_op jit(solution)/shard_map/pallas_call | solution.py:241
  (8 shorter events, 0.0 us)
Async XLA Ops:
  0.0 3.7 %copy-start = (bf16[256,4096]{1,0:T(8,128)(2,1)S(1)}, bf16[256,4096]{1,0:T(8,128)(2,1)}, u32[]{:S(2)}) copy-start(bf16[256,4096]{1,0:T(8,128)(2,1)} %refs_3_) | copy-start | bytes 6291460
  3.7 45.4 %copy-start.2 = (s32[8,8]{1,0:T(8,128)S(1)}, s32[8,8]{1,0:T(8,128)}, u32[]{:S(2)}) copy-start(s32[8,8]{1,0:T(8,128)} %fetch_ref.3) | copy-start | bytes 772
  3.7 45.4 %copy-start.3 = (s32[32]{0:T(128)S(1)}, s32[32]{0:T(128)}, u32[]{:S(2)}) copy-start(s32[32]{0:T(128)} %home_ref.3) | copy-start | bytes 388
  3.7 45.4 %copy-start.4 = (s32[1,8]{1,0:T(1,128)S(1)}, s32[1,8]{1,0:T(1,128)}, u32[]{:S(2)}) copy-start(s32[1,8]{1,0:T(1,128)} %lengths_ref.1) | copy-start | bytes 100
  3.8 57.8 %collective-permute-start.6 = (bf16[256,4096]{1,0:T(8,128)(2,1)S(1)}, bf16[256,4096]{1,0:T(8,128)(2,1)S(1)}, u32[]{:S(2)}, u32[]{:S(2)}) collective-permute-start(bf16[256,4096]{1,0:T(8,128)(2,1)S(1)} %copy-done), channel_id=1, source_target_pairs={{0,16},{16,0},{1,17},{17,1},{2,18},{18,2},{3,19},{19,3},{4,20},{20... | collective-permute-start | bytes 6291464 | tf_op jit(solution)/shard_map/ppermute | solution.py:282
  6.8 42.4 %collective-permute-start.1 = (bf16[64,4608]{1,0:T(8,128)(2,1)}, bf16[64,4608]{1,0:T(8,128)(2,1)S(1)}, u32[]{:S(2)}, u32[]{:S(2)}) collective-permute-start(bf16[64,4608]{1,0:T(8,128)(2,1)} %get-tuple-element.36), channel_id=1, source_target_pairs={{0,8},{2,10},{4,12},{6,14},{8,0},{10,2},{12,4},{14,6},{16,28},{18,... | collective-permute-start | bytes 1769480 | tf_op jit(solution)/shard_map/ppermute | solution.py:279
  9.3 40.5 %collective-permute-start.3 = (bf16[64,4608]{1,0:T(8,128)(2,1)}, bf16[64,4608]{1,0:T(8,128)(2,1)S(1)}, u32[]{:S(2)}, u32[]{:S(2)}) collective-permute-start(bf16[64,4608]{1,0:T(8,128)(2,1)} %get-tuple-element.39), channel_id=1, source_target_pairs={{0,4},{2,6},{4,0},{6,2},{8,12},{10,14},{12,8},{14,10},{16,22},{18,... | collective-permute-start | bytes 1769480 | tf_op jit(solution)/shard_map/ppermute | solution.py:279
  10.9 38.9 %collective-permute-start.4 = (bf16[64,4608]{1,0:T(8,128)(2,1)}, bf16[64,4608]{1,0:T(8,128)(2,1)S(1)}, u32[]{:S(2)}, u32[]{:S(2)}) collective-permute-start(bf16[64,4608]{1,0:T(8,128)(2,1)} %get-tuple-element.40), channel_id=1, source_target_pairs={{0,2},{2,0},{4,6},{6,4},{8,10},{10,8},{12,14},{14,12},{16,16},{18,... | collective-permute-start | bytes 1769480 | tf_op jit(solution)/shard_map/ppermute | solution.py:279
  14.3 47.2 %collective-permute-start.7 = (bf16[64,4608]{1,0:T(8,128)(2,1)}, bf16[64,4608]{1,0:T(8,128)(2,1)S(1)}, u32[]{:S(2)}, u32[]{:S(2)}) collective-permute-start(bf16[64,4608]{1,0:T(8,128)(2,1)} %get-tuple-element.44), channel_id=1, source_target_pairs={{0,10},{2,8},{4,14},{6,12},{8,2},{10,0},{12,6},{14,4},{16,30},{18,... | collective-permute-start | bytes 1769480 | tf_op jit(solution)/shard_map/ppermute | solution.py:279
  14.7 3.4 %copy-start.1 = (bf16[4096,1024]{1,0:T(8,128)(2,1)S(1)}, bf16[4096,1024]{1,0:T(8,128)(2,1)}, u32[]{:S(2)}) copy-start(bf16[4096,1024]{1,0:T(8,128)(2,1)} %weight_ref.1) | copy-start | bytes 25165828
  49.1 12.4 %collective-permute-start.2 = (f32[256,512]{1,0:T(8,128)S(1)}, f32[256,512]{1,0:T(8,128)S(1)}, u32[]{:S(2)}, u32[]{:S(2)}) collective-permute-start(f32[256,512]{1,0:T(8,128)S(1)} %get-tuple-element.38), channel_id=1, source_target_pairs={{0,1},{1,0},{2,3},{3,2},{4,5},{5,4},{6,7},{7,6},{8,9},{9,8},{10,11... | collective-permute-start | bytes 1572872 | tf_op jit(solution)/shard_map/ppermute | solution.py:285
  50.7 10.9 %collective-permute-start.5 = (bf16[192,512]{1,0:T(8,128)(2,1)S(1)}, bf16[192,512]{1,0:T(8,128)(2,1)S(1)}, u32[]{:S(2)}, u32[]{:S(2)}) collective-permute-start(bf16[192,512]{1,0:T(8,128)(2,1)S(1)} %get-tuple-element.43), channel_id=1, source_target_pairs={{0,16},{16,0},{1,17},{17,1},{2,18},{18,2},{3,19},{19,3},{4,20},{20... | collective-permute-start | bytes 589832 | tf_op jit(solution)/shard_map/ppermute | solution.py:282
  50.8 10.8 %collective-permute-start = (s32[8,256]{1,0:T(8,128)S(1)}, s32[8,256]{1,0:T(8,128)S(1)}, u32[]{:S(2)}, u32[]{:S(2)}) collective-permute-start(s32[8,256]{1,0:T(8,128)S(1)} %shard_map.73.refs_0_.row_steps), channel_id=1, source_target_pairs={{0,16},{16,0},{1,17},{17,1},{2,18},{18,2},{3,19},{19,3},{4,20},{20... | collective-permute-start | bytes 24584 | tf_op jit(solution)/shard_map/ppermute | solution.py:282
  62.9 1.4 %collective-permute-start.8 = (f32[64,512]{1,0:T(8,128)S(1)}, f32[64,512]{1,0:T(8,128)S(1)}, u32[]{:S(2)}, u32[]{:S(2)}) collective-permute-start(f32[64,512]{1,0:T(8,128)S(1)} %get-tuple-element.48.refs_0_), channel_id=1, source_target_pairs={{0,1},{1,0},{2,3},{3,2},{4,5},{5,4},{6,7},{7,6},{8,9},{9,8},{10,11... | collective-permute-start | bytes 393224 | tf_op jit(solution)/shard_map/ppermute | solution.py:285
  63.0 4.9 %collective-permute-start.10 = (bf16[64,512]{1,0:T(8,128)(2,1)S(1)}, bf16[64,512]{1,0:T(8,128)(2,1)S(1)}, u32[]{:S(2)}, u32[]{:S(2)}) collective-permute-start(bf16[64,512]{1,0:T(8,128)(2,1)S(1)} %get-tuple-element.52), channel_id=1, source_target_pairs={{0,16},{16,0},{1,17},{17,1},{2,18},{18,2},{3,19},{19,3},{4,20},{20... | collective-permute-start | bytes 196616 | tf_op jit(solution)/shard_map/ppermute | solution.py:282
  64.3 4.6 %collective-permute-start.9 = (f32[64,256]{1,0:T(8,128)S(1)}, f32[64,256]{1,0:T(8,128)S(1)}, u32[]{:S(2)}, u32[]{:S(2)}) collective-permute-start(f32[64,256]{1,0:T(8,128)S(1)} %slice_add_fusion), channel_id=1, source_target_pairs={{0,16},{16,0},{1,17},{17,1},{2,18},{18,2},{3,19},{19,3},{4,20},{20... | collective-permute-start | bytes 196616 | tf_op jit(solution)/shard_map/ppermute | solution.py:282

commit v20 on v19

--- a/solution.py
+++ b/solution.py
@@ -9,16 +9,24 @@
 adapter_scale = 2.0
 
 
-def by_part(values):
+def upper(replicas):
+    return (lax.axis_index("rep") >= replicas // 2).astype(jnp.int32)
+
+
+def step_of(group, high):
+    steps, moves = group
     part = lax.axis_index("parts")
-    chosen = jnp.int32(values[0])
-    for p, value in enumerate(values):
-        chosen = jnp.where(part == p, value, chosen)
+    if moves:
+        part = lax.rem(part + high, jnp.int32(len(steps)))
+    chosen = jnp.int32(steps[0])
+    for p, step in enumerate(steps):
+        chosen = jnp.where(part == p, step, chosen)
     return chosen
 
 
 def turned(group, shift):
-    return tuple(group[(p - shift) % len(group)] for p in range(len(group)))
+    steps, moves = group
+    return (tuple(steps[(p - shift) % len(steps)] for p in range(len(steps))), moves)
 
 
 def slot_for(peer, me, per_home, home_ref, fetch_ref):
@@ -58,6 +66,7 @@
 def pack_kernel(groups, home_ref, fetch_ref, shrink_ref, expand_ref, *refs):
     outs, (held, in_sems, out_sems) = refs[:-3], refs[-3:]
     me = lax.axis_index("rep")
+    other = 1 - upper(fetch_ref.shape[0])
     per_home, _, depth = shrink_ref.shape
     columns = expand_ref.shape[2] // lax.axis_size("tp")
     left = pl.multiple_of(lax.axis_index("tp") * columns, 128)
@@ -65,7 +74,7 @@
     width = depth // cuts
     arriving = []
     for at, group in enumerate(groups):
-        slot = slot_for(me ^ by_part(group), me, per_home, home_ref, fetch_ref)
+        slot = slot_for(me ^ step_of(group, other), me, per_home, home_ref, fetch_ref)
         pieces = [(shrink_ref.at[slot, :, pl.ds(n * width, width)], n * width, width) for n in range(cuts)]
         pieces.append((expand_ref.at[slot, :, pl.ds(left, columns)], depth, columns))
         for n, (source, start, size) in enumerate(pieces):
@@ -99,7 +108,7 @@
     )
 
 
-def score_kernel(plan, groups, kept, chunks, has_prior, *refs):
+def score_kernel(plan, groups, kept, chunks, has_prior, replicas, *refs):
     sets, many = len(plan), len(groups)
     row_steps, refs = refs[:sets], refs[sets:]
     prior, refs = (refs[0], refs[1:]) if has_prior else (None, refs)
@@ -108,6 +117,7 @@
     rank, (count, depth) = out.shape[0], tokens[0].shape
     for i, n in enumerate(kept):
         out_expand[pl.ds(i * rank, rank), :] = panels[n][:, pl.ds(depth, out_expand.shape[1])]
+    high = upper(replicas)
     width = depth // chunks
     sums = [None] * sets
     for c in range(chunks):
@@ -125,7 +135,7 @@
         total = prior[...] if has_prior and t == 0 else jnp.zeros((rank, count), jnp.float32)
         for n, panel in enumerate(used):
             term = sums[t][n * rank : (n + 1) * rank]
-            total = total + jnp.where(mine == by_part(groups[panel]), term, 0.0)
+            total = total + jnp.where(mine == step_of(groups[panel], high), term, 0.0)
         out[:, pl.ds(t * count, count)] = total
 
 
@@ -139,7 +149,9 @@
     arrays = list(row_steps) + prior + list(tokens_of) + list(panels)
     need = 4 * len(plan) * count * (rank * len(panels) + depth) + 4 * len(panels) * rank * (depth + columns)
     return pl.pallas_call(
-        functools.partial(score_kernel, plan, groups, kept, chunks, bool(prior)),
+        functools.partial(
+            score_kernel, plan, groups, kept, chunks, bool(prior), lax.axis_size("rep")
+        ),
         out_shape=[
             jax.ShapeDtypeStruct(shape, panels[0].dtype if n else jnp.float32)
             for n, shape in enumerate(outs)
@@ -202,7 +214,7 @@
     )
 
 
-def end_kernel(pieces, added, bases, row_steps, *refs):
+def end_kernel(pieces, added, bases, replicas, row_steps, *refs):
     scores, base, refs = refs[:added], refs[added : added + bases], refs[added + bases :]
     arrays, (out, held, sems) = refs[:-3], refs[-3:]
     count, columns = out.shape
@@ -217,7 +229,8 @@
         shrink = shrink + x[:, pl.ds(0, count)]
     shrink = adapter_scale * shrink
     high = shrink.astype(jnp.bfloat16).astype(jnp.float32)
-    masks = [row_steps[pl.ds(0, 1), :] == by_part(group) for _, _, group in pieces]
+    place = upper(replicas)
+    masks = [row_steps[pl.ds(0, 1), :] == step_of(group, place) for _, _, group in pieces]
     total = base[0][...]
     for x in base[1:]:
         total = total + x[...]
@@ -239,7 +252,7 @@
     rank = scores[0].shape[0]
     vmem = pl.BlockSpec(memory_space=pltpu.VMEM)
     return pl.pallas_call(
-        functools.partial(end_kernel, pieces, len(scores), len(base)),
+        functools.partial(end_kernel, pieces, len(scores), len(base), lax.axis_size("rep")),
         out_shape=jax.ShapeDtypeStruct((count, columns), kind),
         in_specs=[vmem] * (1 + len(scores) + len(base))
         + [pl.BlockSpec(memory_space=pl.ANY)] * len(arrays),
@@ -262,20 +275,18 @@
     tie = lax.optimization_barrier
 
     half = replicas // 2
-
-    def grouped(steps):
-        size = len(steps) // parts
-        return [tuple(steps[p * size + g] for p in range(parts)) for g in range(size)]
-
-    far = grouped(list(range(half, replicas)))
-    near = grouped(list(range(parts, half))) + [tuple(reversed(range(parts)))]
+    far = [(tuple(range(step, step + parts)), True) for step in range(half, replicas, parts)]
+    size = half // parts - 1
+    near = [(tuple(parts + p * size + g for p in range(parts)), False) for g in range(size)]
+    near.append((tuple(reversed(range(parts))), False))
 
     def hop(x, group):
-        pairs = [
-            (p * replicas + i, p * replicas + (i ^ group[p]))
-            for p in range(parts)
-            for i in range(replicas)
-        ]
+        steps, moves = group
+        pairs = []
+        for p in range(parts):
+            for i in range(replicas):
+                step = steps[(p + (moves and i >= half)) % parts]
+                pairs.append((p * replicas + (i ^ step), p * replicas + i))
         return lax.ppermute(x, ("parts", "rep"), pairs)
 
     def shift_parts(x, shift):

time: 70.5 us -> 69 us (0.979)
  the two profiles are of different devices: /device:TPU:0 before, /device:TPU:16 now
where the time goes in v20:
time: 69 us; the launch traced here: 68.8 us
  waiting for transfers between devices  41.4 us (60%)
  Pallas kernels  12.3 us (18%)
  starting transfers between devices  11.5 us (17%)
  local copies, waits for them, and re-layouts  3.4 us (5%)
    ppermute x4, waiting for transfers between devices, hop(): return lax.ppermute(x, ('parts', 'rep'), pairs)  36.9 us
    ppermute x4, starting transfers between devices, hop(): return lax.ppermute(x, ('parts', 'rep'), pairs)  6.9 us
    ppermute x5, starting transfers between devices, shift_parts(): lax.ppermute(x, 'parts', [(i, (i + shift) % parts) for i in range(parts)])  4.54 us
    pallas_call x1, Pallas kernels, base_terms(): pl.pallas_call(functools.partial(base_kernel, chunks), out_shape=[jax.Sha...  3.94 us
    pallas_call x1, Pallas kernels, pack(): pl.pallas_call(functools.partial(pack_kernel, groups), out_shape=[jax.Sha...  3.7 us
    unnamed x10, local copies, waits for them, and re-layouts  3.4 us
    ppermute x5, waiting for transfers between devices, shift_parts(): lax.ppermute(x, 'parts', [(i, (i + shift) % parts) for i in range(parts)])  3.26 us
    pallas_call x2, Pallas kernels, score(): pl.pallas_call(functools.partial(score_kernel, plan, groups, kept, chunks...  2.15 us
  transfers between devices with their start and end apart: 11, of which 7 were waited for; matrix products, arithmetic and copies ran while one was open for 0% of the time, Pallas kernels for 9%

profile of v20, /device:TPU:16, one launch (start us, length us, event | category | flops | bytes accessed | tf_op | source)
XLA Modules:
  0.0 68.8 jit_solution(3499942455255223500)
XLA Ops:
  0.0 3.7 %shard_map.74 = (bf16[64,4608]{1,0:T(8,128)(2,1)}, bf16[64,4608]{1,0:T(8,128)(2,1)}, bf16[64,4608]{1,0:T(8,128)(2,1)}, bf16[64,4608]{1,0:T(8,128)(2,1)}) custom-call(s32[32]{0:T(128)} %home_ref.3, s32[8,8]{1,0:T(8,128)} %fetch_ref.3, bf16[4,64,4096]{2,1,0:T(8,128)(2,1)} %bitcast.1, bf16[4,64,1024]{2,1,0:T(8,128)(2,1)} %expand_ref.1), custom_call_target="tpu_custom_call" | custom-call | tf_op jit(solution)/shard_map/pallas_call | solution.py:98
  3.7 0.0 copy-start.2
  3.7 0.0 copy-start.3
  3.7 0.0 copy-start.4
  3.8 1.6 %collective-permute-start.6 = (bf16[256,4096]{1,0:T(8,128)(2,1)S(1)}, bf16[256,4096]{1,0:T(8,128)(2,1)S(1)}, u32[]{:S(2)}, u32[]{:S(2)}) collective-permute-start(bf16[256,4096]{1,0:T(8,128)(2,1)S(1)} %copy-done), channel_id=1, source_target_pairs={{0,16},{16,0},{1,17},{17,1},{2,18},{18,2},{3,19},{19,3},{4,20},{20... | collective-permute-start | bytes 6291464 | tf_op jit(solution)/shard_map/ppermute | solution.py:293
  5.3 0.3 collective-permute-start.1
  5.7 1.6 %collective-permute-start.3 = (bf16[64,4608]{1,0:T(8,128)(2,1)}, bf16[64,4608]{1,0:T(8,128)(2,1)S(1)}, u32[]{:S(2)}, u32[]{:S(2)}) collective-permute-start(bf16[64,4608]{1,0:T(8,128)(2,1)} %get-tuple-element.39), channel_id=1, source_target_pairs={{4,0},{6,2},{0,4},{2,6},{12,8},{14,10},{8,12},{10,14},{22,16},{20,... | collective-permute-start | bytes 1769480 | tf_op jit(solution)/shard_map/ppermute | solution.py:290
  7.2 3.4 %collective-permute-start.4 = (bf16[64,4608]{1,0:T(8,128)(2,1)}, bf16[64,4608]{1,0:T(8,128)(2,1)S(1)}, u32[]{:S(2)}, u32[]{:S(2)}) collective-permute-start(bf16[64,4608]{1,0:T(8,128)(2,1)} %get-tuple-element.40), channel_id=1, source_target_pairs={{2,0},{0,2},{6,4},{4,6},{10,8},{8,10},{14,12},{12,14},{16,16},{18,... | collective-permute-start | bytes 1769480 | tf_op jit(solution)/shard_map/ppermute | solution.py:290
  10.7 1.6 %collective-permute-start.7 = (bf16[64,4608]{1,0:T(8,128)(2,1)}, bf16[64,4608]{1,0:T(8,128)(2,1)S(1)}, u32[]{:S(2)}, u32[]{:S(2)}) collective-permute-start(bf16[64,4608]{1,0:T(8,128)(2,1)} %get-tuple-element.44), channel_id=1, source_target_pairs={{12,0},{14,2},{8,4},{10,6},{6,8},{4,10},{2,12},{0,14},{30,16},{28,... | collective-permute-start | bytes 1769480 | tf_op jit(solution)/shard_map/ppermute | solution.py:290
  12.2 3.4 %copy-done.1 = bf16[4096,1024]{1,0:T(8,128)(2,1)S(1)} copy-done((bf16[4096,1024]{1,0:T(8,128)(2,1)S(1)}, bf16[4096,1024]{1,0:T(8,128)(2,1)}, u32[]{:S(2)}) %copy-start.1) | copy-done | bytes 8388632
  15.6 3.9 %shard_map.75 = (f32[256,512]{1,0:T(8,128)S(1)}, f32[256,512]{1,0:T(8,128)S(1)}) custom-call(bf16[256,4096]{1,0:T(8,128)(2,1)S(1)} %copy-done, bf16[4096,1024]{1,0:T(8,128)(2,1)S(1)} %copy-done.1), custom_call_target="tpu_custom_call" | custom-call | tf_op jit(solution)/shard_map/pallas_call | solution.py:201
  19.6 13.6 %collective-permute-done.1.refs_4_.refs_8_.refs_6_ = bf16[64,4608]{1,0:T(8,128)(2,1)S(1)} collective-permute-done((bf16[64,4608]{1,0:T(8,128)(2,1)}, bf16[64,4608]{1,0:T(8,128)(2,1)S(1)}, u32[]{:S(2)}, u32[]{:S(2)}) %collective-permute-start.1) | collective-permute-done | bytes 589856 | tf_op jit(solution)/shard_map/ppermute | solution.py:290
  33.2 0.0 collective-permute-start.2
  33.2 0.6 shard_map.73.refs_0_.row_steps
  33.9 0.4 collective-permute-done.3.refs_2_.refs_6_.refs_4_
  34.3 0.5 collective-permute-done.4.refs_3_.refs_7_.refs_5_
  34.9 0.8 %shard_map.76 = (f32[64,256]{1,0:T(8,128)S(1)}, bf16[192,512]{1,0:T(8,128)(2,1)S(1)}) custom-call(s32[8,256]{1,0:T(8,128)S(1)} %shard_map.73.refs_0_.row_steps, bf16[256,4096]{1,0:T(8,128)(2,1)S(1)} %copy-done, bf16[64,4608]{1,0:T(8,128)(2,1)S(1)} %collective-permute-done.3.refs_2_.refs_6_.refs_4_, ...), custom_call_target="tpu_custom_call" | custom-call | tf_op jit(solution)/shard_map/pallas_call | solution.py:151
  35.7 1.0 %collective-permute-start.5 = (bf16[192,512]{1,0:T(8,128)(2,1)S(1)}, bf16[192,512]{1,0:T(8,128)(2,1)S(1)}, u32[]{:S(2)}, u32[]{:S(2)}) collective-permute-start(bf16[192,512]{1,0:T(8,128)(2,1)S(1)} %get-tuple-element.43), channel_id=1, source_target_pairs={{0,16},{16,0},{1,17},{17,1},{2,18},{18,2},{3,19},{19,3},{4,20},{20... | collective-permute-start | bytes 589832 | tf_op jit(solution)/shard_map/ppermute | solution.py:293
  36.7 1.1 %collective-permute-start = (s32[8,256]{1,0:T(8,128)S(1)}, s32[8,256]{1,0:T(8,128)S(1)}, u32[]{:S(2)}, u32[]{:S(2)}) collective-permute-start(s32[8,256]{1,0:T(8,128)S(1)} %shard_map.73.refs_0_.row_steps), channel_id=1, source_target_pairs={{0,16},{16,0},{1,17},{17,1},{2,18},{18,2},{3,19},{19,3},{4,20},{20... | collective-permute-start | bytes 24584 | tf_op jit(solution)/shard_map/ppermute | solution.py:293
  37.8 22.2 %collective-permute-done.7.refs_5_.refs_7_ = bf16[64,4608]{1,0:T(8,128)(2,1)S(1)} collective-permute-done((bf16[64,4608]{1,0:T(8,128)(2,1)}, bf16[64,4608]{1,0:T(8,128)(2,1)S(1)}, u32[]{:S(2)}, u32[]{:S(2)}) %collective-permute-start.7) | collective-permute-done | bytes 589856 | tf_op jit(solution)/shard_map/ppermute | solution.py:290
  60.0 0.0 collective-permute-done.5.refs_2_
  60.0 0.0 collective-permute-done.2.refs_3_
  60.0 0.0 collective-permute-done.6.refs_4_
  60.1 1.3 %shard_map.77 = (f32[64,512]{1,0:T(8,128)S(1)}, bf16[64,512]{1,0:T(8,128)(2,1)S(1)}) custom-call(s32[8,256]{1,0:T(8,128)S(1)} %shard_map.73.refs_0_.row_steps, s32[8,256]{1,0:T(8,128)S(1)} %collective-permute-done.refs_1_, f32[64,256]{1,0:T(8,128)S(1)} %get-tuple-element.45.refs_2_, bf16[256,4096]{1,0:T(8,128)(2,1)S(1)} %copy-done, ...), custom_call_target="tpu_custom_call" | custom-call | tf_op jit(solution)/shard_map/pallas_call | solution.py:151
  61.4 0.1 collective-permute-start.8
  61.5 0.1 collective-permute-start.10
  61.5 1.3 %collective-permute-done.8.refs_1_ = f32[64,512]{1,0:T(8,128)S(1)} collective-permute-done((f32[64,512]{1,0:T(8,128)S(1)}, f32[64,512]{1,0:T(8,128)S(1)}, u32[]{:S(2)}, u32[]{:S(2)}) %collective-permute-start.8) | collective-permute-done | bytes 131104 | tf_op jit(solution)/shard_map/ppermute | solution.py:296
  62.8 0.8 %collective-permute-start.9 = (f32[64,256]{1,0:T(8,128)S(1)}, f32[64,256]{1,0:T(8,128)S(1)}, u32[]{:S(2)}, u32[]{:S(2)}) collective-permute-start(f32[64,256]{1,0:T(8,128)S(1)} %slice_add_fusion), channel_id=1, source_target_pairs={{0,16},{16,0},{1,17},{17,1},{2,18},{18,2},{3,19},{19,3},{4,20},{20... | collective-permute-start | bytes 196616 | tf_op jit(solution)/shard_map/ppermute | solution.py:293
  63.6 0.5 shard_map.78.refs_1_
  64.1 2.3 %collective-permute-done.10.refs_3_ = bf16[64,512]{1,0:T(8,128)(2,1)S(1)} collective-permute-done((bf16[64,512]{1,0:T(8,128)(2,1)S(1)}, bf16[64,512]{1,0:T(8,128)(2,1)S(1)}, u32[]{:S(2)}, u32[]{:S(2)}) %collective-permute-start.10) | collective-permute-done | bytes 65568 | tf_op jit(solution)/shard_map/ppermute | solution.py:293
  66.4 1.0 %collective-permute-done.9.refs_0_ = f32[64,256]{1,0:T(8,128)S(1)} collective-permute-done((f32[64,256]{1,0:T(8,128)S(1)}, f32[64,256]{1,0:T(8,128)S(1)}, u32[]{:S(2)}, u32[]{:S(2)}) %collective-permute-start.9) | collective-permute-done | bytes 65568 | tf_op jit(solution)/shard_map/ppermute | solution.py:293
  67.4 1.4 %shard_map.79 = bf16[256,512]{1,0:T(8,128)(2,1)} custom-call(s32[8,256]{1,0:T(8,128)S(1)} %shard_map.73.refs_0_.row_steps, f32[64,256]{1,0:T(8,128)S(1)} %collective-permute-done.9.refs_0_, f32[256,512]{1,0:T(8,128)S(1)} %shard_map.78.refs_1_, bf16[192,512]{1,0:T(8,128)(2,1)S(1)} %collective-permute-done.5.refs_2_, ...), custom_call_target="tpu_custom_call" | custom-call | tf_op jit(solution)/shard_map/pallas_call | solution.py:254
  (8 shorter events, 0.0 us)
Async XLA Ops:
  0.0 3.8 %copy-start = (bf16[256,4096]{1,0:T(8,128)(2,1)S(1)}, bf16[256,4096]{1,0:T(8,128)(2,1)}, u32[]{:S(2)}) copy-start(bf16[256,4096]{1,0:T(8,128)(2,1)} %refs_3_) | copy-start | bytes 6291460
  3.7 29.5 %copy-start.2 = (s32[8,8]{1,0:T(8,128)S(1)}, s32[8,8]{1,0:T(8,128)}, u32[]{:S(2)}) copy-start(s32[8,8]{1,0:T(8,128)} %fetch_ref.3) | copy-start | bytes 772
  3.7 29.5 %copy-start.3 = (s32[32]{0:T(128)S(1)}, s32[32]{0:T(128)}, u32[]{:S(2)}) copy-start(s32[32]{0:T(128)} %home_ref.3) | copy-start | bytes 388
  3.7 29.5 %copy-start.4 = (s32[1,8]{1,0:T(1,128)S(1)}, s32[1,8]{1,0:T(1,128)}, u32[]{:S(2)}) copy-start(s32[1,8]{1,0:T(1,128)} %lengths_ref.1) | copy-start | bytes 100
  3.8 56.3 %collective-permute-start.6 = (bf16[256,4096]{1,0:T(8,128)(2,1)S(1)}, bf16[256,4096]{1,0:T(8,128)(2,1)S(1)}, u32[]{:S(2)}, u32[]{:S(2)}) collective-permute-start(bf16[256,4096]{1,0:T(8,128)(2,1)S(1)} %copy-done), channel_id=1, source_target_pairs={{0,16},{16,0},{1,17},{17,1},{2,18},{18,2},{3,19},{19,3},{4,20},{20... | collective-permute-start | bytes 6291464 | tf_op jit(solution)/shard_map/ppermute | solution.py:293
  5.3 27.9 %collective-permute-start.1 = (bf16[64,4608]{1,0:T(8,128)(2,1)}, bf16[64,4608]{1,0:T(8,128)(2,1)S(1)}, u32[]{:S(2)}, u32[]{:S(2)}) collective-permute-start(bf16[64,4608]{1,0:T(8,128)(2,1)} %get-tuple-element.36), channel_id=1, source_target_pairs={{8,0},{10,2},{12,4},{14,6},{2,8},{0,10},{6,12},{4,14},{26,16},{24,... | collective-permute-start | bytes 1769480 | tf_op jit(solution)/shard_map/ppermute | solution.py:290
  5.7 28.7 %collective-permute-start.3 = (bf16[64,4608]{1,0:T(8,128)(2,1)}, bf16[64,4608]{1,0:T(8,128)(2,1)S(1)}, u32[]{:S(2)}, u32[]{:S(2)}) collective-permute-start(bf16[64,4608]{1,0:T(8,128)(2,1)} %get-tuple-element.39), channel_id=1, source_target_pairs={{4,0},{6,2},{0,4},{2,6},{12,8},{14,10},{8,12},{10,14},{22,16},{20,... | collective-permute-start | bytes 1769480 | tf_op jit(solution)/shard_map/ppermute | solution.py:290
  7.2 27.6 %collective-permute-start.4 = (bf16[64,4608]{1,0:T(8,128)(2,1)}, bf16[64,4608]{1,0:T(8,128)(2,1)S(1)}, u32[]{:S(2)}, u32[]{:S(2)}) collective-permute-start(bf16[64,4608]{1,0:T(8,128)(2,1)} %get-tuple-element.40), channel_id=1, source_target_pairs={{2,0},{0,2},{6,4},{4,6},{10,8},{8,10},{14,12},{12,14},{16,16},{18,... | collective-permute-start | bytes 1769480 | tf_op jit(solution)/shard_map/ppermute | solution.py:290
  10.7 49.4 %collective-permute-start.7 = (bf16[64,4608]{1,0:T(8,128)(2,1)}, bf16[64,4608]{1,0:T(8,128)(2,1)S(1)}, u32[]{:S(2)}, u32[]{:S(2)}) collective-permute-start(bf16[64,4608]{1,0:T(8,128)(2,1)} %get-tuple-element.44), channel_id=1, source_target_pairs={{12,0},{14,2},{8,4},{10,6},{6,8},{4,10},{2,12},{0,14},{30,16},{28,... | collective-permute-start | bytes 1769480 | tf_op jit(solution)/shard_map/ppermute | solution.py:290
  12.2 3.4 %copy-start.1 = (bf16[4096,1024]{1,0:T(8,128)(2,1)S(1)}, bf16[4096,1024]{1,0:T(8,128)(2,1)}, u32[]{:S(2)}) copy-start(bf16[4096,1024]{1,0:T(8,128)(2,1)} %weight_ref.1) | copy-start | bytes 25165828
  33.2 26.8 %collective-permute-start.2 = (f32[256,512]{1,0:T(8,128)S(1)}, f32[256,512]{1,0:T(8,128)S(1)}, u32[]{:S(2)}, u32[]{:S(2)}) collective-permute-start(f32[256,512]{1,0:T(8,128)S(1)} %get-tuple-element.38), channel_id=1, source_target_pairs={{0,1},{1,0},{2,3},{3,2},{4,5},{5,4},{6,7},{7,6},{8,9},{9,8},{10,11... | collective-permute-start | bytes 1572872 | tf_op jit(solution)/shard_map/ppermute | solution.py:296
  35.7 24.3 %collective-permute-start.5 = (bf16[192,512]{1,0:T(8,128)(2,1)S(1)}, bf16[192,512]{1,0:T(8,128)(2,1)S(1)}, u32[]{:S(2)}, u32[]{:S(2)}) collective-permute-start(bf16[192,512]{1,0:T(8,128)(2,1)S(1)} %get-tuple-element.43), channel_id=1, source_target_pairs={{0,16},{16,0},{1,17},{17,1},{2,18},{18,2},{3,19},{19,3},{4,20},{20... | collective-permute-start | bytes 589832 | tf_op jit(solution)/shard_map/ppermute | solution.py:293
  36.7 23.4 %collective-permute-start = (s32[8,256]{1,0:T(8,128)S(1)}, s32[8,256]{1,0:T(8,128)S(1)}, u32[]{:S(2)}, u32[]{:S(2)}) collective-permute-start(s32[8,256]{1,0:T(8,128)S(1)} %shard_map.73.refs_0_.row_steps), channel_id=1, source_target_pairs={{0,16},{16,0},{1,17},{17,1},{2,18},{18,2},{3,19},{19,3},{4,20},{20... | collective-permute-start | bytes 24584 | tf_op jit(solution)/shard_map/ppermute | solution.py:293
  61.4 1.4 %collective-permute-start.8 = (f32[64,512]{1,0:T(8,128)S(1)}, f32[64,512]{1,0:T(8,128)S(1)}, u32[]{:S(2)}, u32[]{:S(2)}) collective-permute-start(f32[64,512]{1,0:T(8,128)S(1)} %get-tuple-element.48.refs_0_), channel_id=1, source_target_pairs={{0,1},{1,0},{2,3},{3,2},{4,5},{5,4},{6,7},{7,6},{8,9},{9,8},{10,11... | collective-permute-start | bytes 393224 | tf_op jit(solution)/shard_map/ppermute | solution.py:296
  61.5 4.9 %collective-permute-start.10 = (bf16[64,512]{1,0:T(8,128)(2,1)S(1)}, bf16[64,512]{1,0:T(8,128)(2,1)S(1)}, u32[]{:S(2)}, u32[]{:S(2)}) collective-permute-start(bf16[64,512]{1,0:T(8,128)(2,1)S(1)} %get-tuple-element.52), channel_id=1, source_target_pairs={{0,16},{16,0},{1,17},{17,1},{2,18},{18,2},{3,19},{19,3},{4,20},{20... | collective-permute-start | bytes 196616 | tf_op jit(solution)/shard_map/ppermute | solution.py:293
  62.8 4.6 %collective-permute-start.9 = (f32[64,256]{1,0:T(8,128)S(1)}, f32[64,256]{1,0:T(8,128)S(1)}, u32[]{:S(2)}, u32[]{:S(2)}) collective-permute-start(f32[64,256]{1,0:T(8,128)S(1)} %slice_add_fusion), channel_id=1, source_target_pairs={{0,16},{16,0},{1,17},{17,1},{2,18},{18,2},{3,19},{19,3},{4,20},{20... | collective-permute-start | bytes 196616 | tf_op jit(solution)/shard_map/ppermute | solution.py:293

commit v21 on v20

--- a/solution.py
+++ b/solution.py
@@ -63,7 +63,7 @@
     )(adapter_home, fetch_list, seg_len)
 
 
-def pack_kernel(groups, home_ref, fetch_ref, shrink_ref, expand_ref, *refs):
+def pack_kernel(blocks, home_ref, fetch_ref, shrink_ref, expand_ref, *refs):
     outs, (held, in_sems, out_sems) = refs[:-3], refs[-3:]
     me = lax.axis_index("rep")
     other = 1 - upper(fetch_ref.shape[0])
@@ -73,12 +73,14 @@
     cuts = in_sems.shape[1] - 1
     width = depth // cuts
     arriving = []
-    for at, group in enumerate(groups):
-        slot = slot_for(me ^ step_of(group, other), me, per_home, home_ref, fetch_ref)
-        pieces = [(shrink_ref.at[slot, :, pl.ds(n * width, width)], n * width, width) for n in range(cuts)]
-        pieces.append((expand_ref.at[slot, :, pl.ds(left, columns)], depth, columns))
+    for at, (group, first, rows) in enumerate(blocks):
+        step = jnp.maximum(step_of(group, other), 0)
+        slot = slot_for(me ^ step, me, per_home, home_ref, fetch_ref)
+        rows = pl.ds(first, rows)
+        pieces = [(shrink_ref.at[slot, rows, pl.ds(n * width, width)], n * width, width) for n in range(cuts)]
+        pieces.append((expand_ref.at[slot, rows, pl.ds(left, columns)], depth, columns))
         for n, (source, start, size) in enumerate(pieces):
-            target = held.at[at, :, pl.ds(start, size)]
+            target = held.at[at, rows, pl.ds(start, size)]
             copy = pltpu.make_async_copy(source, target, in_sems.at[at, n])
             copy.start()
             leave = pltpu.make_async_copy(target, outs[at].at[:, pl.ds(start, size)], out_sems.at[at, n])
@@ -90,33 +92,36 @@
         leave.wait()
 
 
-def pack(groups, columns, adapter_home, fetch_list, panels, expand_panels):
+def pack(blocks, columns, adapter_home, fetch_list, panels, expand_panels):
     rank, depth = panels.shape[1:]
-    shape = (rank, depth + columns)
+    width = depth + columns
     cuts = 4
     return list(
         pl.pallas_call(
-            functools.partial(pack_kernel, groups),
-            out_shape=[jax.ShapeDtypeStruct(shape, panels.dtype)] * len(groups),
+            functools.partial(pack_kernel, blocks),
+            out_shape=[jax.ShapeDtypeStruct((rows, width), panels.dtype) for _, _, rows in blocks],
             in_specs=[pl.BlockSpec(memory_space=pltpu.SMEM)] * 2 + [pl.BlockSpec(memory_space=pl.ANY)] * 2,
-            out_specs=[pl.BlockSpec(memory_space=pl.ANY)] * len(groups),
-            scratch_shapes=[pltpu.VMEM((len(groups),) + shape, panels.dtype)]
-            + [pltpu.SemaphoreType.DMA((len(groups), cuts + 1))] * 2,
+            out_specs=[pl.BlockSpec(memory_space=pl.ANY)] * len(blocks),
+            scratch_shapes=[pltpu.VMEM((len(blocks), rank, width), panels.dtype)]
+            + [pltpu.SemaphoreType.DMA((len(blocks), cuts + 1))] * 2,
             compiler_params=pltpu.CompilerParams(vmem_limit_bytes=56 << 20),
             cost_estimate=pl.CostEstimate(flops=0, bytes_accessed=0, transcendentals=0),
         )(adapter_home, fetch_list, panels, expand_panels)
     )
 
 
-def score_kernel(plan, groups, kept, chunks, has_prior, replicas, *refs):
-    sets, many = len(plan), len(groups)
+def score_kernel(plan, blocks, kept, chunks, has_prior, replicas, *refs):
+    sets, many = len(plan), len(blocks)
     row_steps, refs = refs[:sets], refs[sets:]
     prior, refs = (refs[0], refs[1:]) if has_prior else (None, refs)
     tokens, panels = refs[:sets], refs[sets : sets + many]
     out, out_expand = refs[sets + many :]
     rank, (count, depth) = out.shape[0], tokens[0].shape
-    for i, n in enumerate(kept):
-        out_expand[pl.ds(i * rank, rank), :] = panels[n][:, pl.ds(depth, out_expand.shape[1])]
+    filled = 0
+    for n in kept:
+        rows = blocks[n][2]
+        out_expand[pl.ds(filled, rows), :] = panels[n][:, pl.ds(depth, out_expand.shape[1])]
+        filled += rows
     high = upper(replicas)
     width = depth // chunks
     sums = [None] * sets
@@ -133,24 +138,28 @@
     for t, used in enumerate(plan):
         mine = row_steps[t][pl.ds(0, 1), :]
         total = prior[...] if has_prior and t == 0 else jnp.zeros((rank, count), jnp.float32)
-        for n, panel in enumerate(used):
-            term = sums[t][n * rank : (n + 1) * rank]
-            total = total + jnp.where(mine == step_of(groups[panel], high), term, 0.0)
+        filled = 0
+        for panel in used:
+            group, first, rows = blocks[panel]
+            term = jnp.where(mine == step_of(group, high), sums[t][filled : filled + rows], 0.0)
+            filled += rows
+            ends = [jnp.zeros((size, count), jnp.float32) for size in (first, rank - first - rows)]
+            term = [x for x in (ends[0], term, ends[1]) if x.shape[0]]
+            total = total + (jnp.concatenate(term, axis=0) if len(term) > 1 else term[0])
         out[:, pl.ds(t * count, count)] = total
 
 
-def score(plan, groups, kept, columns, row_steps, tokens_of, panels, prior=None):
+def score(plan, blocks, kept, rank, columns, row_steps, tokens_of, panels, prior=None):
     count, depth = tokens_of[0].shape
-    rank = panels[0].shape[0]
     chunks = 4
     prior = [] if prior is None else [prior]
     vmem = pl.BlockSpec(memory_space=pltpu.VMEM)
-    outs = [(rank, len(plan) * count), (len(kept) * rank, columns)]
+    outs = [(rank, len(plan) * count), (sum(blocks[n][2] for n in kept), columns)]
     arrays = list(row_steps) + prior + list(tokens_of) + list(panels)
     need = 4 * len(plan) * count * (rank * len(panels) + depth) + 4 * len(panels) * rank * (depth + columns)
     return pl.pallas_call(
         functools.partial(
-            score_kernel, plan, groups, kept, chunks, bool(prior), lax.axis_size("rep")
+            score_kernel, plan, blocks, kept, chunks, bool(prior), lax.axis_size("rep")
         ),
         out_shape=[
             jax.ShapeDtypeStruct(shape, panels[0].dtype if n else jnp.float32)
@@ -218,26 +227,30 @@
     scores, base, refs = refs[:added], refs[added : added + bases], refs[added + bases :]
     arrays, (out, held, sems) = refs[:-3], refs[-3:]
     count, columns = out.shape
-    rank = scores[0].shape[0]
-    copies = []
-    for n, (at, row, _) in enumerate(pieces):
-        source = arrays[at].at[pl.ds(row, rank), pl.ds(arrays[at].shape[1] - columns, columns)]
-        copies.append(pltpu.make_async_copy(source, held.at[pl.ds(n * rank, rank)], sems.at[n]))
+    copies, filled = [], 0
+    for n, (at, row, (_, _, rows)) in enumerate(pieces):
+        source = arrays[at].at[pl.ds(row, rows), pl.ds(arrays[at].shape[1] - columns, columns)]
+        copies.append(pltpu.make_async_copy(source, held.at[pl.ds(filled, rows)], sems.at[n]))
         copies[-1].start()
+        filled += rows
     shrink = scores[0][:, pl.ds(0, count)]
     for x in scores[1:]:
         shrink = shrink + x[:, pl.ds(0, count)]
     shrink = adapter_scale * shrink
     high = shrink.astype(jnp.bfloat16).astype(jnp.float32)
     place = upper(replicas)
-    masks = [row_steps[pl.ds(0, 1), :] == step_of(group, place) for _, _, group in pieces]
+    masks = [row_steps[pl.ds(0, 1), :] == step_of(block[0], place) for _, _, block in pieces]
     total = base[0][...]
     for x in base[1:]:
         total = total + x[...]
     for copy in copies:
         copy.wait()
     for term in (high, shrink - high):
-        wide = jnp.concatenate([jnp.where(mask, term, 0.0) for mask in masks], axis=0)
+        wide = [
+            jnp.where(mask, term[first : first + rows], 0.0)
+            for mask, (_, _, (_, first, rows)) in zip(masks, pieces)
+        ]
+        wide = jnp.concatenate(wide, axis=0)
         total = total + lax.dot_general(
             wide.astype(jnp.bfloat16),
             held[...],
@@ -249,7 +262,6 @@
 
 def end(pieces, row_steps, scores, base, arrays, kind, cost):
     count, columns = base[0].shape
-    rank = scores[0].shape[0]
     vmem = pl.BlockSpec(memory_space=pltpu.VMEM)
     return pl.pallas_call(
         functools.partial(end_kernel, pieces, len(scores), len(base), lax.axis_size("rep")),
@@ -258,7 +270,7 @@
         + [pl.BlockSpec(memory_space=pl.ANY)] * len(arrays),
         out_specs=vmem,
         scratch_shapes=[
-            pltpu.VMEM((len(pieces) * rank, columns), jnp.bfloat16),
+            pltpu.VMEM((sum(rows for _, _, (_, _, rows) in pieces), columns), jnp.bfloat16),
             pltpu.SemaphoreType.DMA((len(pieces),)),
         ],
         compiler_params=pltpu.CompilerParams(vmem_limit_bytes=16 << 20),
@@ -286,6 +298,8 @@
         for p in range(parts):
             for i in range(replicas):
                 step = steps[(p + (moves and i >= half)) % parts]
+                if step < 0:
+                    continue
                 pairs.append((p * replicas + (i ^ step), p * replicas + i))
         return lax.ppermute(x, ("parts", "rep"), pairs)
 
@@ -296,39 +310,45 @@
         return lax.ppermute(x, "tp", [(i, (i + shift) % cores) for i in range(cores)])
 
     tables = (adapter_home, fetch_list, panels, expand_panels)
-    groups = far + near
-    send = pack(groups, columns, *tables)
-    tokens, send = tie((tokens, send))
-    recv = [hop(x, group) for x, group in zip(send, groups)]
+    low = rank - 16
+    steps, moves = far[0]
+    keep = (tuple(step if p % 2 == 0 else -1 for p, step in enumerate(steps)), moves)
+    take = (tuple(steps[p + 1] if p % 2 == 0 else -1 for p in range(parts)), moves)
+    blocks = [(group, 0, rank) for group in near + far[1:-1]]
+    blocks += [(far[0], 0, low), (keep, low, rank - low), (take, low, rank - low)]
+    last_blocks = [(far[-1], 0, rank)]
+    *send, keep_send, take_send, last_send = pack(blocks + last_blocks, columns, *tables)
+    tokens, send, last_send = tie((tokens, send, last_send))
+    early = [hop(x, block[0]) for x, block in zip(send, blocks)]
+    last = [hop(last_send, far[-1])]
     tokens_of = [tokens] + [shift_parts(tokens, shift) for shift in range(1, parts)]
+    at = len(near) - 1
+    keep_send, early[at] = tie((keep_send, early[at]))
+    early.append(hop(keep_send, keep))
+    take_send, base_weight, seg_len, early[-1] = tie((take_send, base_weight, seg_len, early[-1]))
+    early.append(hop(take_send, take))
     base = base_terms(tokens, base_weight, cores)
-    base, recv[: len(far) - 1] = tie((base, recv[: len(far) - 1]))
+    base, early[len(near) : -2] = tie((base, early[len(near) : -2]))
     base = base[:1] + [shift_cores(x, shift + 1) for shift, x in enumerate(base[1:])]
     row_steps = steps_of_rows(tok_count, panels.shape[0], adapter_home, fetch_list, seg_len)
     steps_of = [row_steps] + [shift_parts(row_steps, shift) for shift in range(1, parts)]
-    early, early_groups = recv[len(far) :] + recv[: len(far) - 1], near + far[:-1]
-    last, last_group = recv[len(far) - 1], far[-1]
 
     count = len(early)
     first, sent = score(
-        [tuple(range(count))],
-        early_groups,
-        tuple(range(count)),
-        columns,
-        steps_of[:1],
-        [tokens],
-        early,
+        [tuple(range(count))], blocks, tuple(range(count)), rank, columns, steps_of[:1], [tokens], early
     )
     passed = [shift_parts(sent, shift) for shift in range(1, parts)]
     base, first, passed, tokens_of[1:], last = tie((base, first, passed, tokens_of[1:], last))
+    ends = tuple(range(len(last)))
     scores, sent = score(
-        [(0,)] + [tuple(range(count + 1))] * (parts - 1),
-        [last_group] + early_groups,
-        (0,),
+        [ends] + [tuple(range(len(last) + count))] * (parts - 1),
+        last_blocks + blocks,
+        ends,
+        rank,
         columns,
         steps_of,
         tokens_of,
-        [last] + early,
+        last + early,
         first,
     )
     last_passed = [shift_parts(sent, shift) for shift in range(1, parts)]
@@ -340,13 +360,15 @@
         shift_parts(whole[:, shift * tok_count : (shift + 1) * tok_count], -shift)
         for shift in range(1, parts)
     ]
-    pieces = [(n, 0, group) for n, group in enumerate(early_groups + [last_group])]
-    result = end(pieces, row_steps, halves, base, early + [last], jnp.float32, 1 << 24)
+    pieces = [(n, 0, block) for n, block in enumerate(blocks + last_blocks)]
+    result = end(pieces, row_steps, halves, base, early + last, jnp.float32, 1 << 24)
     pieces = []
-    for shift in range(1, parts):
-        at = shift - 1
-        pieces += [(at, n * rank, turned(group, shift)) for n, group in enumerate(early_groups)]
-        pieces.append((at + parts - 1, 0, turned(last_group, shift)))
+    for at in range(parts - 1):
+        for number, many in ((at, blocks), (at + parts - 1, last_blocks)):
+            row = 0
+            for group, top, rows in many:
+                pieces.append((number, row, (turned(group, at + 1), top, rows)))
+                row += rows
     return end(pieces, row_steps, came, [result], passed + last_passed, jnp.bfloat16, 0)
 
 

time: 69 us -> 91.3 us (1.32)
  the two profiles are of different devices: /device:TPU:16 before, /device:TPU:0 now
where the time goes in v21:
time: 91.3 us; the launch traced here: 91.1 us
  waiting for transfers between devices  44 us (48%)
  starting transfers between devices  30.7 us (34%)
  Pallas kernels  12.9 us (14%)
  local copies, waits for them, and re-layouts  3.4 us (4%)
    ppermute x6, waiting for transfers between devices, hop(): return lax.ppermute(x, ('parts', 'rep'), pairs)  34.9 us
    ppermute x6, starting transfers between devices, hop(): return lax.ppermute(x, ('parts', 'rep'), pairs)  24.2 us
    ppermute x5, waiting for transfers between devices, shift_parts(): lax.ppermute(x, 'parts', [(i, (i + shift) % parts) for i in range(parts)])  8.17 us
    ppermute x5, starting transfers between devices, shift_parts(): lax.ppermute(x, 'parts', [(i, (i + shift) % parts) for i in range(parts)])  6.28 us
    pallas_call x1, Pallas kernels, base_terms(): pl.pallas_call(functools.partial(base_kernel, chunks), out_shape=[jax.Sha...  3.94 us
    pallas_call x1, Pallas kernels, pack(): pl.pallas_call(functools.partial(pack_kernel, blocks), out_shape=[jax.Sha...  3.86 us
    unnamed x12, local copies, waits for them, and re-layouts  3.4 us
    pallas_call x2, Pallas kernels, end(): pl.pallas_call(functools.partial(end_kernel, pieces, len(scores), len(bas...  2.27 us
  transfers between devices with their start and end apart: 13, of which 8 were waited for; matrix products, arithmetic and copies ran while one was open for 0% of the time, Pallas kernels for 7%

profile of v21, /device:TPU:0, one launch (start us, length us, event | category | flops | bytes accessed | tf_op | source)
XLA Modules:
  0.0 91.1 jit_solution(8570215764585136917)
XLA Ops:
  0.0 3.9 %shard_map.73 = (bf16[64,4608]{1,0:T(8,128)(2,1)}, bf16[64,4608]{1,0:T(8,128)(2,1)}, bf16[48,4608]{1,0:T(8,128)(2,1)}, bf16[16,4608]{1,0:T(8,128)(2,1)}, bf16[16...) custom-call(s32[32]{0:T(128)} %home_ref.3, s32[8,8]{1,0:T(8,128)} %fetch_ref.3, bf16[4,64,4096]{2,1,0:T(8,128)(2,1)} %bitcast.1, ...), custom_call_target="tpu_custom_call" | custom-call | tf_op jit(solution)/shard_map/pallas_call | solution.py:100
  3.9 3.0 %collective-permute-start.8 = (bf16[256,4096]{1,0:T(8,128)(2,1)S(1)}, bf16[256,4096]{1,0:T(8,128)(2,1)S(1)}, u32[]{:S(2)}, u32[]{:S(2)}) collective-permute-start(bf16[256,4096]{1,0:T(8,128)(2,1)S(1)} %copy-done), channel_id=1, source_target_pairs={{0,16},{16,0},{1,17},{17,1},{2,18},{18,2},{3,19},{19,3},{4,20},{20... | collective-permute-start | bytes 6291464 | tf_op jit(solution)/shard_map/ppermute | solution.py:307
  6.9 3.4 %collective-permute-start = (bf16[64,4608]{1,0:T(8,128)(2,1)}, bf16[64,4608]{1,0:T(8,128)(2,1)S(1)}, u32[]{:S(2)}, u32[]{:S(2)}) collective-permute-start(bf16[64,4608]{1,0:T(8,128)(2,1)} %get-tuple-element.43), channel_id=1, source_target_pairs={{2,0},{0,2},{6,4},{4,6},{10,8},{8,10},{14,12},{12,14},{16,16},{18,... | collective-permute-start | bytes 1769480 | tf_op jit(solution)/shard_map/ppermute | solution.py:304
  10.3 2.6 %collective-permute-start.3 = (bf16[48,4608]{1,0:T(8,128)(2,1)}, bf16[48,4608]{1,0:T(8,128)(2,1)S(1)}, u32[]{:S(2)}, u32[]{:S(2)}) collective-permute-start(bf16[48,4608]{1,0:T(8,128)(2,1)} %get-tuple-element.50), channel_id=1, source_target_pairs={{8,0},{10,2},{12,4},{14,6},{2,8},{0,10},{6,12},{4,14},{26,16},{24,... | collective-permute-start | bytes 1327112 | tf_op jit(solution)/shard_map/ppermute | solution.py:304
  12.9 1.6 %collective-permute-start.5 = (bf16[64,4608]{1,0:T(8,128)(2,1)}, bf16[64,4608]{1,0:T(8,128)(2,1)S(1)}, u32[]{:S(2)}, u32[]{:S(2)}) collective-permute-start(bf16[64,4608]{1,0:T(8,128)(2,1)} %get-tuple-element.53), channel_id=1, source_target_pairs={{4,0},{6,2},{0,4},{2,6},{12,8},{14,10},{8,12},{10,14},{22,16},{20,... | collective-permute-start | bytes 1769480 | tf_op jit(solution)/shard_map/ppermute | solution.py:304
  14.5 9.3 %collective-permute-done.refs_3_.refs_7_.refs_5_ = bf16[64,4608]{1,0:T(8,128)(2,1)S(1)} collective-permute-done((bf16[64,4608]{1,0:T(8,128)(2,1)}, bf16[64,4608]{1,0:T(8,128)(2,1)S(1)}, u32[]{:S(2)}, u32[]{:S(2)}) %collective-permute-start) | collective-permute-done | bytes 589856 | tf_op jit(solution)/shard_map/ppermute | solution.py:304
  23.8 1.3 %collective-permute-start.1 = (bf16[16,4608]{1,0:T(8,128)(2,1)}, bf16[16,4608]{1,0:T(8,128)(2,1)S(1)}, u32[]{:S(2)}, u32[]{:S(2)}) collective-permute-start(bf16[16,4608]{1,0:T(8,128)(2,1)} %get-tuple-element.44), channel_id=1, source_target_pairs={{8,0},{10,2},{12,4},{14,6},{16,24},{18,26},{20,28},{22,30},{9,1},{... | collective-permute-start | bytes 442376 | tf_op jit(solution)/shard_map/ppermute | solution.py:304
  25.0 14.1 %collective-permute-start.9 = (bf16[64,4608]{1,0:T(8,128)(2,1)}, bf16[64,4608]{1,0:T(8,128)(2,1)S(1)}, u32[]{:S(2)}, u32[]{:S(2)}) collective-permute-start(bf16[64,4608]{1,0:T(8,128)(2,1)} %get-tuple-element.60), channel_id=1, source_target_pairs={{12,0},{14,2},{8,4},{10,6},{6,8},{4,10},{2,12},{0,14},{30,16},{28,... | collective-permute-start | bytes 1769480 | tf_op jit(solution)/shard_map/ppermute | solution.py:304
  39.1 16.5 %collective-permute-done.1.refs_5_.refs_9_.refs_7_ = bf16[16,4608]{1,0:T(8,128)(2,1)S(1)} collective-permute-done((bf16[16,4608]{1,0:T(8,128)(2,1)}, bf16[16,4608]{1,0:T(8,128)(2,1)S(1)}, u32[]{:S(2)}, u32[]{:S(2)}) %collective-permute-start.1) | collective-permute-done | bytes 147488 | tf_op jit(solution)/shard_map/ppermute | solution.py:304
  55.6 3.4 %copy-done.1 = bf16[4096,1024]{1,0:T(8,128)(2,1)S(1)} copy-done((bf16[4096,1024]{1,0:T(8,128)(2,1)S(1)}, bf16[4096,1024]{1,0:T(8,128)(2,1)}, u32[]{:S(2)}) %copy-start.1) | copy-done | bytes 8388632
  59.0 3.9 %shard_map.75 = (f32[256,512]{1,0:T(8,128)S(1)}, f32[256,512]{1,0:T(8,128)S(1)}) custom-call(bf16[256,4096]{1,0:T(8,128)(2,1)S(1)} %copy-done, bf16[4096,1024]{1,0:T(8,128)(2,1)S(1)} %copy-done.1), custom_call_target="tpu_custom_call" | custom-call | tf_op jit(solution)/shard_map/pallas_call | solution.py:210
  63.0 0.0 collective-permute-done.3.refs_4_.refs_8_.refs_6_
  63.0 0.1 collective-permute-start.4
  63.1 1.3 %collective-permute-start.6 = (bf16[16,4608]{1,0:T(8,128)(2,1)S(1)}, bf16[16,4608]{1,0:T(8,128)(2,1)S(1)}, u32[]{:S(2)}, u32[]{:S(2)}) collective-permute-start(bf16[16,4608]{1,0:T(8,128)(2,1)S(1)} %copy-done.5), channel_id=1, source_target_pairs={{10,0},{8,2},{14,4},{12,6},{18,24},{16,26},{22,28},{20,30},{11,1},... | collective-permute-start | bytes 442376 | tf_op jit(solution)/shard_map/ppermute | solution.py:304
  64.4 0.6 shard_map.74.refs_0_.row_steps
  65.1 0.0 collective-permute-done.5.refs_2_.refs_6_.refs_4_
  65.1 9.1 %collective-permute-done.6.refs_6_.refs_10_.refs_8_ = bf16[16,4608]{1,0:T(8,128)(2,1)S(1)} collective-permute-done((bf16[16,4608]{1,0:T(8,128)(2,1)S(1)}, bf16[16,4608]{1,0:T(8,128)(2,1)S(1)}, u32[]{:S(2)}, u32[]{:S(2)}) %collective-permute-start.6) | collective-permute-done | bytes 147488 | tf_op jit(solution)/shard_map/ppermute | solution.py:304
  74.2 0.8 shard_map.76
  75.0 0.1 collective-permute-start.7
  75.1 2.0 %collective-permute-start.2 = (s32[8,256]{1,0:T(8,128)S(1)}, s32[8,256]{1,0:T(8,128)S(1)}, u32[]{:S(2)}, u32[]{:S(2)}) collective-permute-start(s32[8,256]{1,0:T(8,128)S(1)} %shard_map.74.refs_0_.row_steps), channel_id=1, source_target_pairs={{0,16},{16,0},{1,17},{17,1},{2,18},{18,2},{3,19},{19,3},{4,20},{20... | collective-permute-start | bytes 24584 | tf_op jit(solution)/shard_map/ppermute | solution.py:307
  77.1 0.0 collective-permute-done.9.refs_5_.refs_9_
  77.1 5.0 %collective-permute-done.7.refs_2_ = bf16[208,512]{1,0:T(8,128)(2,1)S(1)} collective-permute-done((bf16[208,512]{1,0:T(8,128)(2,1)S(1)}, bf16[208,512]{1,0:T(8,128)(2,1)S(1)}, u32[]{:S(2)}, u32[]{:S(2)}) %collective-permute-start.7) | collective-permute-done | bytes 213024 | tf_op jit(solution)/shard_map/ppermute | solution.py:307
  82.1 0.1 collective-permute-done.2.refs_1_
  82.2 1.3 %shard_map.77 = (f32[64,512]{1,0:T(8,128)S(1)}, bf16[64,512]{1,0:T(8,128)(2,1)S(1)}) custom-call(s32[8,256]{1,0:T(8,128)S(1)} %shard_map.74.refs_0_.row_steps, s32[8,256]{1,0:T(8,128)S(1)} %collective-permute-done.2.refs_1_, f32[64,256]{1,0:T(8,128)S(1)} %get-tuple-element.61.refs_2_, bf16[256,4096]{1,0:T(8,128)(2,1)S(1)} %copy-done, ...), custom_call_target="tpu_custom_call" | custom-call | tf_op jit(solution)/shard_map/pallas_call | solution.py:160
  83.6 0.1 collective-permute-start.10
  83.6 0.4 collective-permute-start.12
  84.0 1.0 %collective-permute-done.10.refs_1_ = f32[64,512]{1,0:T(8,128)S(1)} collective-permute-done((f32[64,512]{1,0:T(8,128)S(1)}, f32[64,512]{1,0:T(8,128)S(1)}, u32[]{:S(2)}, u32[]{:S(2)}) %collective-permute-start.10) | collective-permute-done | bytes 131104 | tf_op jit(solution)/shard_map/ppermute | solution.py:310
  85.0 0.8 collective-permute-start.11
  85.8 0.7 shard_map.78.refs_1_
  86.5 2.1 %collective-permute-done.12.refs_3_ = bf16[64,512]{1,0:T(8,128)(2,1)S(1)} collective-permute-done((bf16[64,512]{1,0:T(8,128)(2,1)S(1)}, bf16[64,512]{1,0:T(8,128)(2,1)S(1)}, u32[]{:S(2)}, u32[]{:S(2)}) %collective-permute-start.12) | collective-permute-done | bytes 65568 | tf_op jit(solution)/shard_map/ppermute | solution.py:307
  88.6 1.0 %collective-permute-done.11.refs_0_ = f32[64,256]{1,0:T(8,128)S(1)} collective-permute-done((f32[64,256]{1,0:T(8,128)S(1)}, f32[64,256]{1,0:T(8,128)S(1)}, u32[]{:S(2)}, u32[]{:S(2)}) %collective-permute-start.11) | collective-permute-done | bytes 65568 | tf_op jit(solution)/shard_map/ppermute | solution.py:307
  89.5 1.6 %shard_map.79 = bf16[256,512]{1,0:T(8,128)(2,1)} custom-call(s32[8,256]{1,0:T(8,128)S(1)} %shard_map.74.refs_0_.row_steps, f32[64,256]{1,0:T(8,128)S(1)} %collective-permute-done.11.refs_0_, f32[256,512]{1,0:T(8,128)S(1)} %shard_map.78.refs_1_, bf16[208,512]{1,0:T(8,128)(2,1)S(1)} %collective-permute-done.7.refs_2_, ...), custom_call_target="tpu_custom_call" | custom-call | tf_op jit(solution)/shard_map/pallas_call | solution.py:266
  (14 shorter events, 0.0 us)
Async XLA Ops:
  0.0 3.9 %copy-start = (bf16[256,4096]{1,0:T(8,128)(2,1)S(1)}, bf16[256,4096]{1,0:T(8,128)(2,1)}, u32[]{:S(2)}) copy-start(bf16[256,4096]{1,0:T(8,128)(2,1)} %refs_3_) | copy-start | bytes 6291460
  3.9 78.3 %collective-permute-start.8 = (bf16[256,4096]{1,0:T(8,128)(2,1)S(1)}, bf16[256,4096]{1,0:T(8,128)(2,1)S(1)}, u32[]{:S(2)}, u32[]{:S(2)}) collective-permute-start(bf16[256,4096]{1,0:T(8,128)(2,1)S(1)} %copy-done), channel_id=1, source_target_pairs={{0,16},{16,0},{1,17},{17,1},{2,18},{18,2},{3,19},{19,3},{4,20},{20... | collective-permute-start | bytes 6291464 | tf_op jit(solution)/shard_map/ppermute | solution.py:307
  6.9 16.9 %collective-permute-start = (bf16[64,4608]{1,0:T(8,128)(2,1)}, bf16[64,4608]{1,0:T(8,128)(2,1)S(1)}, u32[]{:S(2)}, u32[]{:S(2)}) collective-permute-start(bf16[64,4608]{1,0:T(8,128)(2,1)} %get-tuple-element.43), channel_id=1, source_target_pairs={{2,0},{0,2},{6,4},{4,6},{10,8},{8,10},{14,12},{12,14},{16,16},{18,... | collective-permute-start | bytes 1769480 | tf_op jit(solution)/shard_map/ppermute | solution.py:304
  10.3 52.7 %collective-permute-start.3 = (bf16[48,4608]{1,0:T(8,128)(2,1)}, bf16[48,4608]{1,0:T(8,128)(2,1)S(1)}, u32[]{:S(2)}, u32[]{:S(2)}) collective-permute-start(bf16[48,4608]{1,0:T(8,128)(2,1)} %get-tuple-element.50), channel_id=1, source_target_pairs={{8,0},{10,2},{12,4},{14,6},{2,8},{0,10},{6,12},{4,14},{26,16},{24,... | collective-permute-start | bytes 1327112 | tf_op jit(solution)/shard_map/ppermute | solution.py:304
  12.9 52.2 %collective-permute-start.5 = (bf16[64,4608]{1,0:T(8,128)(2,1)}, bf16[64,4608]{1,0:T(8,128)(2,1)S(1)}, u32[]{:S(2)}, u32[]{:S(2)}) collective-permute-start(bf16[64,4608]{1,0:T(8,128)(2,1)} %get-tuple-element.53), channel_id=1, source_target_pairs={{4,0},{6,2},{0,4},{2,6},{12,8},{14,10},{8,12},{10,14},{22,16},{20,... | collective-permute-start | bytes 1769480 | tf_op jit(solution)/shard_map/ppermute | solution.py:304
  23.8 31.9 %collective-permute-start.1 = (bf16[16,4608]{1,0:T(8,128)(2,1)}, bf16[16,4608]{1,0:T(8,128)(2,1)S(1)}, u32[]{:S(2)}, u32[]{:S(2)}) collective-permute-start(bf16[16,4608]{1,0:T(8,128)(2,1)} %get-tuple-element.44), channel_id=1, source_target_pairs={{8,0},{10,2},{12,4},{14,6},{16,24},{18,26},{20,28},{22,30},{9,1},{... | collective-permute-start | bytes 442376 | tf_op jit(solution)/shard_map/ppermute | solution.py:304
  25.0 52.1 %collective-permute-start.9 = (bf16[64,4608]{1,0:T(8,128)(2,1)}, bf16[64,4608]{1,0:T(8,128)(2,1)S(1)}, u32[]{:S(2)}, u32[]{:S(2)}) collective-permute-start(bf16[64,4608]{1,0:T(8,128)(2,1)} %get-tuple-element.60), channel_id=1, source_target_pairs={{12,0},{14,2},{8,4},{10,6},{6,8},{4,10},{2,12},{0,14},{30,16},{28,... | collective-permute-start | bytes 1769480 | tf_op jit(solution)/shard_map/ppermute | solution.py:304
  55.6 3.4 %copy-start.1 = (bf16[4096,1024]{1,0:T(8,128)(2,1)S(1)}, bf16[4096,1024]{1,0:T(8,128)(2,1)}, u32[]{:S(2)}) copy-start(bf16[4096,1024]{1,0:T(8,128)(2,1)} %weight_ref) | copy-start | bytes 25165828
  59.0 4.1 %copy-start.5 = (bf16[16,4608]{1,0:T(8,128)(2,1)S(1)}, bf16[16,4608]{1,0:T(8,128)(2,1)}, u32[]{:S(2)}) copy-start(bf16[16,4608]{1,0:T(8,128)(2,1)} %get-tuple-element.57) | copy-start | bytes 442372
  59.0 5.4 %copy-start.2 = (s32[8,8]{1,0:T(8,128)S(1)}, s32[8,8]{1,0:T(8,128)}, u32[]{:S(2)}) copy-start(s32[8,8]{1,0:T(8,128)} %fetch_ref.3) | copy-start | bytes 772
  59.0 5.4 %copy-start.3 = (s32[32]{0:T(128)S(1)}, s32[32]{0:T(128)}, u32[]{:S(2)}) copy-start(s32[32]{0:T(128)} %home_ref.3) | copy-start | bytes 388
  59.0 5.4 %copy-start.4 = (s32[1,8]{1,0:T(1,128)S(1)}, s32[1,8]{1,0:T(1,128)}, u32[]{:S(2)}) copy-start(s32[1,8]{1,0:T(1,128)} %lengths_ref) | copy-start | bytes 100
  63.0 19.2 %collective-permute-start.4 = (f32[256,512]{1,0:T(8,128)S(1)}, f32[256,512]{1,0:T(8,128)S(1)}, u32[]{:S(2)}, u32[]{:S(2)}) collective-permute-start(f32[256,512]{1,0:T(8,128)S(1)} %get-tuple-element.52), channel_id=1, source_target_pairs={{0,1},{1,0},{2,3},{3,2},{4,5},{5,4},{6,7},{7,6},{8,9},{9,8},{10,11... | collective-permute-start | bytes 1572872 | tf_op jit(solution)/shard_map/ppermute | solution.py:310
  63.1 11.1 %collective-permute-start.6 = (bf16[16,4608]{1,0:T(8,128)(2,1)S(1)}, bf16[16,4608]{1,0:T(8,128)(2,1)S(1)}, u32[]{:S(2)}, u32[]{:S(2)}) collective-permute-start(bf16[16,4608]{1,0:T(8,128)(2,1)S(1)} %copy-done.5), channel_id=1, source_target_pairs={{10,0},{8,2},{14,4},{12,6},{18,24},{16,26},{22,28},{20,30},{11,1},... | collective-permute-start | bytes 442376 | tf_op jit(solution)/shard_map/ppermute | solution.py:304
  75.0 7.1 %collective-permute-start.7 = (bf16[208,512]{1,0:T(8,128)(2,1)S(1)}, bf16[208,512]{1,0:T(8,128)(2,1)S(1)}, u32[]{:S(2)}, u32[]{:S(2)}) collective-permute-start(bf16[208,512]{1,0:T(8,128)(2,1)S(1)} %get-tuple-element.59), channel_id=1, source_target_pairs={{0,16},{16,0},{1,17},{17,1},{2,18},{18,2},{3,19},{19,3},{4,20},{20... | collective-permute-start | bytes 638984 | tf_op jit(solution)/shard_map/ppermute | solution.py:307
  75.1 7.1 %collective-permute-start.2 = (s32[8,256]{1,0:T(8,128)S(1)}, s32[8,256]{1,0:T(8,128)S(1)}, u32[]{:S(2)}, u32[]{:S(2)}) collective-permute-start(s32[8,256]{1,0:T(8,128)S(1)} %shard_map.74.refs_0_.row_steps), channel_id=1, source_target_pairs={{0,16},{16,0},{1,17},{17,1},{2,18},{18,2},{3,19},{19,3},{4,20},{20... | collective-permute-start | bytes 24584 | tf_op jit(solution)/shard_map/ppermute | solution.py:307
  83.6 1.4 %collective-permute-start.10 = (f32[64,512]{1,0:T(8,128)S(1)}, f32[64,512]{1,0:T(8,128)S(1)}, u32[]{:S(2)}, u32[]{:S(2)}) collective-permute-start(f32[64,512]{1,0:T(8,128)S(1)} %get-tuple-element.64.refs_0_), channel_id=1, source_target_pairs={{0,1},{1,0},{2,3},{3,2},{4,5},{5,4},{6,7},{7,6},{8,9},{9,8},{10,11... | collective-permute-start | bytes 393224 | tf_op jit(solution)/shard_map/ppermute | solution.py:310
  83.6 4.9 %collective-permute-start.12 = (bf16[64,512]{1,0:T(8,128)(2,1)S(1)}, bf16[64,512]{1,0:T(8,128)(2,1)S(1)}, u32[]{:S(2)}, u32[]{:S(2)}) collective-permute-start(bf16[64,512]{1,0:T(8,128)(2,1)S(1)} %get-tuple-element.68), channel_id=1, source_target_pairs={{0,16},{16,0},{1,17},{17,1},{2,18},{18,2},{3,19},{19,3},{4,20},{20... | collective-permute-start | bytes 196616 | tf_op jit(solution)/shard_map/ppermute | solution.py:307
  85.0 4.6 %collective-permute-start.11 = (f32[64,256]{1,0:T(8,128)S(1)}, f32[64,256]{1,0:T(8,128)S(1)}, u32[]{:S(2)}, u32[]{:S(2)}) collective-permute-start(f32[64,256]{1,0:T(8,128)S(1)} %slice_add_fusion), channel_id=1, source_target_pairs={{0,16},{16,0},{1,17},{17,1},{2,18},{18,2},{3,19},{19,3},{4,20},{20... | collective-permute-start | bytes 196616 | tf_op jit(solution)/shard_map/ppermute | solution.py:307

commit v22 on v20

--- a/solution.py
+++ b/solution.py
@@ -275,7 +275,7 @@
     tie = lax.optimization_barrier
 
     half = replicas // 2
-    far = [(tuple(range(step, step + parts)), True) for step in range(half, replicas, parts)]
+    far = [(tuple(range(step, step + parts)), True) for step in range(half, replicas, parts)][::-1]
     size = half // parts - 1
     near = [(tuple(parts + p * size + g for p in range(parts)), False) for g in range(size)]
     near.append((tuple(reversed(range(parts))), False))

time: 69 us -> 81.5 us (1.18)
  the two profiles are of different devices: /device:TPU:16 before, /device:TPU:0 now
where the time goes in v22:
time: 81.5 us; the launch traced here: 81.3 us
  starting transfers between devices  35.2 us (43%)
  waiting for transfers between devices  30.2 us (37%)
  Pallas kernels  12.3 us (15%)
  local copies, waits for them, and re-layouts  3.4 us (4%)
    ppermute x4, waiting for transfers between devices, hop(): return lax.ppermute(x, ('parts', 'rep'), pairs)  27.7 us
    ppermute x5, starting transfers between devices, shift_parts(): lax.ppermute(x, 'parts', [(i, (i + shift) % parts) for i in range(parts)])  27.3 us
    ppermute x4, starting transfers between devices, hop(): return lax.ppermute(x, ('parts', 'rep'), pairs)  7.8 us
    pallas_call x1, Pallas kernels, base_terms(): pl.pallas_call(functools.partial(base_kernel, chunks), out_shape=[jax.Sha...  3.93 us
    pallas_call x1, Pallas kernels, pack(): pl.pallas_call(functools.partial(pack_kernel, groups), out_shape=[jax.Sha...  3.7 us
    unnamed x10, local copies, waits for them, and re-layouts  3.4 us
    ppermute x5, waiting for transfers between devices, shift_parts(): lax.ppermute(x, 'parts', [(i, (i + shift) % parts) for i in range(parts)])  2.52 us
    pallas_call x2, Pallas kernels, score(): pl.pallas_call(functools.partial(score_kernel, plan, groups, kept, chunks...  2.15 us
  transfers between devices with their start and end apart: 11, of which 5 were waited for; matrix products, arithmetic and copies ran while one was open for 0% of the time, Pallas kernels for 7%

profile of v22, /device:TPU:0, one launch (start us, length us, event | category | flops | bytes accessed | tf_op | source)
XLA Modules:
  0.0 81.3 jit_solution(1766121336224184453)
XLA Ops:
  0.0 3.7 %shard_map.74 = (bf16[64,4608]{1,0:T(8,128)(2,1)}, bf16[64,4608]{1,0:T(8,128)(2,1)}, bf16[64,4608]{1,0:T(8,128)(2,1)}, bf16[64,4608]{1,0:T(8,128)(2,1)}) custom-call(s32[32]{0:T(128)} %home_ref.3, s32[8,8]{1,0:T(8,128)} %fetch_ref.3, bf16[4,64,4096]{2,1,0:T(8,128)(2,1)} %bitcast.1, bf16[4,64,1024]{2,1,0:T(8,128)(2,1)} %expand_ref.1), custom_call_target="tpu_custom_call" | custom-call | tf_op jit(solution)/shard_map/pallas_call | solution.py:98
  3.7 0.0 copy-start.2
  3.7 0.0 copy-start.3
  3.7 0.0 copy-start.4
  3.8 3.0 %collective-permute-start.6 = (bf16[256,4096]{1,0:T(8,128)(2,1)S(1)}, bf16[256,4096]{1,0:T(8,128)(2,1)S(1)}, u32[]{:S(2)}, u32[]{:S(2)}) collective-permute-start(bf16[256,4096]{1,0:T(8,128)(2,1)S(1)} %copy-done), channel_id=1, source_target_pairs={{0,16},{16,0},{1,17},{17,1},{2,18},{18,2},{3,19},{19,3},{4,20},{20... | collective-permute-start | bytes 6291464 | tf_op jit(solution)/shard_map/ppermute | solution.py:293
  6.8 4.6 %collective-permute-start.1 = (bf16[64,4608]{1,0:T(8,128)(2,1)}, bf16[64,4608]{1,0:T(8,128)(2,1)S(1)}, u32[]{:S(2)}, u32[]{:S(2)}) collective-permute-start(bf16[64,4608]{1,0:T(8,128)(2,1)} %get-tuple-element.36), channel_id=1, source_target_pairs={{12,0},{14,2},{8,4},{10,6},{6,8},{4,10},{2,12},{0,14},{30,16},{28,... | collective-permute-start | bytes 1769480 | tf_op jit(solution)/shard_map/ppermute | solution.py:290
  11.3 0.0 collective-permute-start.3
  11.3 2.4 %collective-permute-start.4 = (bf16[64,4608]{1,0:T(8,128)(2,1)}, bf16[64,4608]{1,0:T(8,128)(2,1)S(1)}, u32[]{:S(2)}, u32[]{:S(2)}) collective-permute-start(bf16[64,4608]{1,0:T(8,128)(2,1)} %get-tuple-element.40), channel_id=1, source_target_pairs={{2,0},{0,2},{6,4},{4,6},{10,8},{8,10},{14,12},{12,14},{16,16},{18,... | collective-permute-start | bytes 1769480 | tf_op jit(solution)/shard_map/ppermute | solution.py:290
  13.7 0.8 %collective-permute-start.7 = (bf16[64,4608]{1,0:T(8,128)(2,1)}, bf16[64,4608]{1,0:T(8,128)(2,1)S(1)}, u32[]{:S(2)}, u32[]{:S(2)}) collective-permute-start(bf16[64,4608]{1,0:T(8,128)(2,1)} %get-tuple-element.44), channel_id=1, source_target_pairs={{8,0},{10,2},{12,4},{14,6},{2,8},{0,10},{6,12},{4,14},{26,16},{24,... | collective-permute-start | bytes 1769480 | tf_op jit(solution)/shard_map/ppermute | solution.py:290
  14.6 3.4 %copy-done.1 = bf16[4096,1024]{1,0:T(8,128)(2,1)S(1)} copy-done((bf16[4096,1024]{1,0:T(8,128)(2,1)S(1)}, bf16[4096,1024]{1,0:T(8,128)(2,1)}, u32[]{:S(2)}) %copy-start.1) | copy-done | bytes 8388632
  18.0 3.9 %shard_map.75 = (f32[256,512]{1,0:T(8,128)S(1)}, f32[256,512]{1,0:T(8,128)S(1)}) custom-call(bf16[256,4096]{1,0:T(8,128)(2,1)S(1)} %copy-done, bf16[4096,1024]{1,0:T(8,128)(2,1)S(1)} %copy-done.1), custom_call_target="tpu_custom_call" | custom-call | tf_op jit(solution)/shard_map/pallas_call | solution.py:201
  21.9 3.5 %collective-permute-done.1.refs_4_.refs_8_.refs_6_ = bf16[64,4608]{1,0:T(8,128)(2,1)S(1)} collective-permute-done((bf16[64,4608]{1,0:T(8,128)(2,1)}, bf16[64,4608]{1,0:T(8,128)(2,1)S(1)}, u32[]{:S(2)}, u32[]{:S(2)}) %collective-permute-start.1) | collective-permute-done | bytes 589856 | tf_op jit(solution)/shard_map/ppermute | solution.py:290
  25.4 0.0 collective-permute-start.2
  25.4 0.6 shard_map.73.refs_0_.row_steps
  26.1 12.0 %collective-permute-done.3.refs_2_.refs_6_.refs_4_ = bf16[64,4608]{1,0:T(8,128)(2,1)S(1)} collective-permute-done((bf16[64,4608]{1,0:T(8,128)(2,1)}, bf16[64,4608]{1,0:T(8,128)(2,1)S(1)}, u32[]{:S(2)}, u32[]{:S(2)}) %collective-permute-start.3) | collective-permute-done | bytes 589856 | tf_op jit(solution)/shard_map/ppermute | solution.py:290
  38.1 0.0 collective-permute-done.4.refs_3_.refs_7_.refs_5_
  38.1 0.8 %shard_map.76 = (f32[64,256]{1,0:T(8,128)S(1)}, bf16[192,512]{1,0:T(8,128)(2,1)S(1)}) custom-call(s32[8,256]{1,0:T(8,128)S(1)} %shard_map.73.refs_0_.row_steps, bf16[256,4096]{1,0:T(8,128)(2,1)S(1)} %copy-done, bf16[64,4608]{1,0:T(8,128)(2,1)S(1)} %collective-permute-done.3.refs_2_.refs_6_.refs_4_, ...), custom_call_target="tpu_custom_call" | custom-call | tf_op jit(solution)/shard_map/pallas_call | solution.py:151
  38.9 9.5 %collective-permute-start.5 = (bf16[192,512]{1,0:T(8,128)(2,1)S(1)}, bf16[192,512]{1,0:T(8,128)(2,1)S(1)}, u32[]{:S(2)}, u32[]{:S(2)}) collective-permute-start(bf16[192,512]{1,0:T(8,128)(2,1)S(1)} %get-tuple-element.43), channel_id=1, source_target_pairs={{0,16},{16,0},{1,17},{17,1},{2,18},{18,2},{3,19},{19,3},{4,20},{20... | collective-permute-start | bytes 589832 | tf_op jit(solution)/shard_map/ppermute | solution.py:293
  48.4 0.1 collective-permute-start
  48.5 12.2 %collective-permute-done.7.refs_5_.refs_7_ = bf16[64,4608]{1,0:T(8,128)(2,1)S(1)} collective-permute-done((bf16[64,4608]{1,0:T(8,128)(2,1)}, bf16[64,4608]{1,0:T(8,128)(2,1)S(1)}, u32[]{:S(2)}, u32[]{:S(2)}) %collective-permute-start.7) | collective-permute-done | bytes 589856 | tf_op jit(solution)/shard_map/ppermute | solution.py:290
  60.7 0.0 collective-permute-done.5.refs_2_
  60.7 0.0 collective-permute-done.2.refs_3_
  60.7 0.0 collective-permute-done.6.refs_4_
  60.7 1.3 %shard_map.77 = (f32[64,512]{1,0:T(8,128)S(1)}, bf16[64,512]{1,0:T(8,128)(2,1)S(1)}) custom-call(s32[8,256]{1,0:T(8,128)S(1)} %shard_map.73.refs_0_.row_steps, s32[8,256]{1,0:T(8,128)S(1)} %collective-permute-done.refs_1_, f32[64,256]{1,0:T(8,128)S(1)} %get-tuple-element.45.refs_2_, bf16[256,4096]{1,0:T(8,128)(2,1)S(1)} %copy-done, ...), custom_call_target="tpu_custom_call" | custom-call | tf_op jit(solution)/shard_map/pallas_call | solution.py:151
  62.0 0.1 collective-permute-start.8
  62.1 13.4 %collective-permute-start.10 = (bf16[64,512]{1,0:T(8,128)(2,1)S(1)}, bf16[64,512]{1,0:T(8,128)(2,1)S(1)}, u32[]{:S(2)}, u32[]{:S(2)}) collective-permute-start(bf16[64,512]{1,0:T(8,128)(2,1)S(1)} %get-tuple-element.52), channel_id=1, source_target_pairs={{0,16},{16,0},{1,17},{17,1},{2,18},{18,2},{3,19},{19,3},{4,20},{20... | collective-permute-start | bytes 196616 | tf_op jit(solution)/shard_map/ppermute | solution.py:293
  75.5 0.0 collective-permute-done.8.refs_1_
  75.5 1.3 %collective-permute-start.9 = (f32[64,256]{1,0:T(8,128)S(1)}, f32[64,256]{1,0:T(8,128)S(1)}, u32[]{:S(2)}, u32[]{:S(2)}) collective-permute-start(f32[64,256]{1,0:T(8,128)S(1)} %slice_add_fusion), channel_id=1, source_target_pairs={{0,16},{16,0},{1,17},{17,1},{2,18},{18,2},{3,19},{19,3},{4,20},{20... | collective-permute-start | bytes 196616 | tf_op jit(solution)/shard_map/ppermute | solution.py:293
  76.8 0.5 shard_map.78.refs_1_
  77.3 0.9 %collective-permute-done.10.refs_3_ = bf16[64,512]{1,0:T(8,128)(2,1)S(1)} collective-permute-done((bf16[64,512]{1,0:T(8,128)(2,1)S(1)}, bf16[64,512]{1,0:T(8,128)(2,1)S(1)}, u32[]{:S(2)}, u32[]{:S(2)}) %collective-permute-start.10) | collective-permute-done | bytes 65568 | tf_op jit(solution)/shard_map/ppermute | solution.py:293
  78.2 1.7 %collective-permute-done.9.refs_0_ = f32[64,256]{1,0:T(8,128)S(1)} collective-permute-done((f32[64,256]{1,0:T(8,128)S(1)}, f32[64,256]{1,0:T(8,128)S(1)}, u32[]{:S(2)}, u32[]{:S(2)}) %collective-permute-start.9) | collective-permute-done | bytes 65568 | tf_op jit(solution)/shard_map/ppermute | solution.py:293
  79.8 1.4 %shard_map.79 = bf16[256,512]{1,0:T(8,128)(2,1)} custom-call(s32[8,256]{1,0:T(8,128)S(1)} %shard_map.73.refs_0_.row_steps, f32[64,256]{1,0:T(8,128)S(1)} %collective-permute-done.9.refs_0_, f32[256,512]{1,0:T(8,128)S(1)} %shard_map.78.refs_1_, bf16[192,512]{1,0:T(8,128)(2,1)S(1)} %collective-permute-done.5.refs_2_, ...), custom_call_target="tpu_custom_call" | custom-call | tf_op jit(solution)/shard_map/pallas_call | solution.py:254
  (8 shorter events, 0.0 us)
Async XLA Ops:
  0.0 3.8 %copy-start = (bf16[256,4096]{1,0:T(8,128)(2,1)S(1)}, bf16[256,4096]{1,0:T(8,128)(2,1)}, u32[]{:S(2)}) copy-start(bf16[256,4096]{1,0:T(8,128)(2,1)} %refs_3_) | copy-start | bytes 6291460
  3.7 21.7 %copy-start.2 = (s32[8,8]{1,0:T(8,128)S(1)}, s32[8,8]{1,0:T(8,128)}, u32[]{:S(2)}) copy-start(s32[8,8]{1,0:T(8,128)} %fetch_ref.3) | copy-start | bytes 772
  3.7 21.7 %copy-start.3 = (s32[32]{0:T(128)S(1)}, s32[32]{0:T(128)}, u32[]{:S(2)}) copy-start(s32[32]{0:T(128)} %home_ref.3) | copy-start | bytes 388
  3.7 21.7 %copy-start.4 = (s32[1,8]{1,0:T(1,128)S(1)}, s32[1,8]{1,0:T(1,128)}, u32[]{:S(2)}) copy-start(s32[1,8]{1,0:T(1,128)} %lengths_ref.1) | copy-start | bytes 100
  3.8 56.9 %collective-permute-start.6 = (bf16[256,4096]{1,0:T(8,128)(2,1)S(1)}, bf16[256,4096]{1,0:T(8,128)(2,1)S(1)}, u32[]{:S(2)}, u32[]{:S(2)}) collective-permute-start(bf16[256,4096]{1,0:T(8,128)(2,1)S(1)} %copy-done), channel_id=1, source_target_pairs={{0,16},{16,0},{1,17},{17,1},{2,18},{18,2},{3,19},{19,3},{4,20},{20... | collective-permute-start | bytes 6291464 | tf_op jit(solution)/shard_map/ppermute | solution.py:293
  6.8 18.6 %collective-permute-start.1 = (bf16[64,4608]{1,0:T(8,128)(2,1)}, bf16[64,4608]{1,0:T(8,128)(2,1)S(1)}, u32[]{:S(2)}, u32[]{:S(2)}) collective-permute-start(bf16[64,4608]{1,0:T(8,128)(2,1)} %get-tuple-element.36), channel_id=1, source_target_pairs={{12,0},{14,2},{8,4},{10,6},{6,8},{4,10},{2,12},{0,14},{30,16},{28,... | collective-permute-start | bytes 1769480 | tf_op jit(solution)/shard_map/ppermute | solution.py:290
  11.3 26.7 %collective-permute-start.3 = (bf16[64,4608]{1,0:T(8,128)(2,1)}, bf16[64,4608]{1,0:T(8,128)(2,1)S(1)}, u32[]{:S(2)}, u32[]{:S(2)}) collective-permute-start(bf16[64,4608]{1,0:T(8,128)(2,1)} %get-tuple-element.39), channel_id=1, source_target_pairs={{4,0},{6,2},{0,4},{2,6},{12,8},{14,10},{8,12},{10,14},{22,16},{20,... | collective-permute-start | bytes 1769480 | tf_op jit(solution)/shard_map/ppermute | solution.py:290
  11.3 26.7 %collective-permute-start.4 = (bf16[64,4608]{1,0:T(8,128)(2,1)}, bf16[64,4608]{1,0:T(8,128)(2,1)S(1)}, u32[]{:S(2)}, u32[]{:S(2)}) collective-permute-start(bf16[64,4608]{1,0:T(8,128)(2,1)} %get-tuple-element.40), channel_id=1, source_target_pairs={{2,0},{0,2},{6,4},{4,6},{10,8},{8,10},{14,12},{12,14},{16,16},{18,... | collective-permute-start | bytes 1769480 | tf_op jit(solution)/shard_map/ppermute | solution.py:290
  13.7 47.0 %collective-permute-start.7 = (bf16[64,4608]{1,0:T(8,128)(2,1)}, bf16[64,4608]{1,0:T(8,128)(2,1)S(1)}, u32[]{:S(2)}, u32[]{:S(2)}) collective-permute-start(bf16[64,4608]{1,0:T(8,128)(2,1)} %get-tuple-element.44), channel_id=1, source_target_pairs={{8,0},{10,2},{12,4},{14,6},{2,8},{0,10},{6,12},{4,14},{26,16},{24,... | collective-permute-start | bytes 1769480 | tf_op jit(solution)/shard_map/ppermute | solution.py:290
  14.6 3.4 %copy-start.1 = (bf16[4096,1024]{1,0:T(8,128)(2,1)S(1)}, bf16[4096,1024]{1,0:T(8,128)(2,1)}, u32[]{:S(2)}) copy-start(bf16[4096,1024]{1,0:T(8,128)(2,1)} %weight_ref.1) | copy-start | bytes 25165828
  25.4 35.3 %collective-permute-start.2 = (f32[256,512]{1,0:T(8,128)S(1)}, f32[256,512]{1,0:T(8,128)S(1)}, u32[]{:S(2)}, u32[]{:S(2)}) collective-permute-start(f32[256,512]{1,0:T(8,128)S(1)} %get-tuple-element.38), channel_id=1, source_target_pairs={{0,1},{1,0},{2,3},{3,2},{4,5},{5,4},{6,7},{7,6},{8,9},{9,8},{10,11... | collective-permute-start | bytes 1572872 | tf_op jit(solution)/shard_map/ppermute | solution.py:296
  38.9 21.8 %collective-permute-start.5 = (bf16[192,512]{1,0:T(8,128)(2,1)S(1)}, bf16[192,512]{1,0:T(8,128)(2,1)S(1)}, u32[]{:S(2)}, u32[]{:S(2)}) collective-permute-start(bf16[192,512]{1,0:T(8,128)(2,1)S(1)} %get-tuple-element.43), channel_id=1, source_target_pairs={{0,16},{16,0},{1,17},{17,1},{2,18},{18,2},{3,19},{19,3},{4,20},{20... | collective-permute-start | bytes 589832 | tf_op jit(solution)/shard_map/ppermute | solution.py:293
  48.4 12.3 %collective-permute-start = (s32[8,256]{1,0:T(8,128)S(1)}, s32[8,256]{1,0:T(8,128)S(1)}, u32[]{:S(2)}, u32[]{:S(2)}) collective-permute-start(s32[8,256]{1,0:T(8,128)S(1)} %shard_map.73.refs_0_.row_steps), channel_id=1, source_target_pairs={{0,16},{16,0},{1,17},{17,1},{2,18},{18,2},{3,19},{19,3},{4,20},{20... | collective-permute-start | bytes 24584 | tf_op jit(solution)/shard_map/ppermute | solution.py:293
  62.0 13.5 %collective-permute-start.8 = (f32[64,512]{1,0:T(8,128)S(1)}, f32[64,512]{1,0:T(8,128)S(1)}, u32[]{:S(2)}, u32[]{:S(2)}) collective-permute-start(f32[64,512]{1,0:T(8,128)S(1)} %get-tuple-element.48.refs_0_), channel_id=1, source_target_pairs={{0,1},{1,0},{2,3},{3,2},{4,5},{5,4},{6,7},{7,6},{8,9},{9,8},{10,11... | collective-permute-start | bytes 393224 | tf_op jit(solution)/shard_map/ppermute | solution.py:296
  62.1 16.1 %collective-permute-start.10 = (bf16[64,512]{1,0:T(8,128)(2,1)S(1)}, bf16[64,512]{1,0:T(8,128)(2,1)S(1)}, u32[]{:S(2)}, u32[]{:S(2)}) collective-permute-start(bf16[64,512]{1,0:T(8,128)(2,1)S(1)} %get-tuple-element.52), channel_id=1, source_target_pairs={{0,16},{16,0},{1,17},{17,1},{2,18},{18,2},{3,19},{19,3},{4,20},{20... | collective-permute-start | bytes 196616 | tf_op jit(solution)/shard_map/ppermute | solution.py:293
  75.5 4.3 %collective-permute-start.9 = (f32[64,256]{1,0:T(8,128)S(1)}, f32[64,256]{1,0:T(8,128)S(1)}, u32[]{:S(2)}, u32[]{:S(2)}) collective-permute-start(f32[64,256]{1,0:T(8,128)S(1)} %slice_add_fusion), channel_id=1, source_target_pairs={{0,16},{16,0},{1,17},{17,1},{2,18},{18,2},{3,19},{19,3},{4,20},{20... | collective-permute-start | bytes 196616 | tf_op jit(solution)/shard_map/ppermute | solution.py:293

commit v23 on v20

--- a/solution.py
+++ b/solution.py
@@ -276,6 +276,7 @@
 
     half = replicas // 2
     far = [(tuple(range(step, step + parts)), True) for step in range(half, replicas, parts)]
+    far[-1] = (far[-1][0][::-1], True)
     size = half // parts - 1
     near = [(tuple(parts + p * size + g for p in range(parts)), False) for g in range(size)]
     near.append((tuple(reversed(range(parts))), False))

time: 69 us -> 69.1 us (level)
  starting transfers between devices: 11.5 us -> 13.1 us
  waiting for transfers between devices: 41.4 us -> 39.9 us
    ppermute x4, starting transfers between devices: 6.9 us -> 7.85 us  [hop(): return lax.ppermute(x, ('parts', 'rep'), pairs)]
    ppermute x4, waiting for transfers between devices: 36.9 us -> 36 us  [hop(): return lax.ppermute(x, ('parts', 'rep'), pairs)]
where the time goes in v23:
time: 69.1 us; the launch traced here: 68.8 us
  waiting for transfers between devices  39.9 us (58%)
  starting transfers between devices  13.1 us (19%)
  Pallas kernels  12.3 us (18%)
  local copies, waits for them, and re-layouts  3.4 us (5%)
    ppermute x4, waiting for transfers between devices, hop(): return lax.ppermute(x, ('parts', 'rep'), pairs)  36 us
    ppermute x4, starting transfers between devices, hop(): return lax.ppermute(x, ('parts', 'rep'), pairs)  7.85 us
    ppermute x5, starting transfers between devices, shift_parts(): lax.ppermute(x, 'parts', [(i, (i + shift) % parts) for i in range(parts)])  5.12 us
    pallas_call x1, Pallas kernels, base_terms(): pl.pallas_call(functools.partial(base_kernel, chunks), out_shape=[jax.Sha...  3.93 us
    pallas_call x1, Pallas kernels, pack(): pl.pallas_call(functools.partial(pack_kernel, groups), out_shape=[jax.Sha...  3.7 us
    unnamed x10, local copies, waits for them, and re-layouts  3.4 us
    ppermute x5, waiting for transfers between devices, shift_parts(): lax.ppermute(x, 'parts', [(i, (i + shift) % parts) for i in range(parts)])  3.26 us
    pallas_call x2, Pallas kernels, score(): pl.pallas_call(functools.partial(score_kernel, plan, groups, kept, chunks...  2.15 us
  transfers between devices with their start and end apart: 11, of which 7 were waited for; matrix products, arithmetic and copies ran while one was open for 0% of the time, Pallas kernels for 9%

profile of v23, /device:TPU:16, one launch (start us, length us, event | category | flops | bytes accessed | tf_op | source)
XLA Modules:
  0.0 68.8 jit_solution(8437983238413513901)
XLA Ops:
  0.0 3.7 %shard_map.74 = (bf16[64,4608]{1,0:T(8,128)(2,1)}, bf16[64,4608]{1,0:T(8,128)(2,1)}, bf16[64,4608]{1,0:T(8,128)(2,1)}, bf16[64,4608]{1,0:T(8,128)(2,1)}) custom-call(s32[32]{0:T(128)} %home_ref.3, s32[8,8]{1,0:T(8,128)} %fetch_ref.3, bf16[4,64,4096]{2,1,0:T(8,128)(2,1)} %bitcast.1, bf16[4,64,1024]{2,1,0:T(8,128)(2,1)} %expand_ref.1), custom_call_target="tpu_custom_call" | custom-call | tf_op jit(solution)/shard_map/pallas_call | solution.py:98
  3.7 0.0 copy-start.2
  3.7 0.0 copy-start.3
  3.7 0.0 copy-start.4
  3.8 1.6 %collective-permute-start.6 = (bf16[256,4096]{1,0:T(8,128)(2,1)S(1)}, bf16[256,4096]{1,0:T(8,128)(2,1)S(1)}, u32[]{:S(2)}, u32[]{:S(2)}) collective-permute-start(bf16[256,4096]{1,0:T(8,128)(2,1)S(1)} %copy-done), channel_id=1, source_target_pairs={{0,16},{16,0},{1,17},{17,1},{2,18},{18,2},{3,19},{19,3},{4,20},{20... | collective-permute-start | bytes 6291464 | tf_op jit(solution)/shard_map/ppermute | solution.py:294
  5.3 0.3 collective-permute-start.1
  5.7 1.6 %collective-permute-start.3 = (bf16[64,4608]{1,0:T(8,128)(2,1)}, bf16[64,4608]{1,0:T(8,128)(2,1)S(1)}, u32[]{:S(2)}, u32[]{:S(2)}) collective-permute-start(bf16[64,4608]{1,0:T(8,128)(2,1)} %get-tuple-element.39), channel_id=1, source_target_pairs={{4,0},{6,2},{0,4},{2,6},{12,8},{14,10},{8,12},{10,14},{22,16},{20,... | collective-permute-start | bytes 1769480 | tf_op jit(solution)/shard_map/ppermute | solution.py:291
  7.2 3.4 %collective-permute-start.4 = (bf16[64,4608]{1,0:T(8,128)(2,1)}, bf16[64,4608]{1,0:T(8,128)(2,1)S(1)}, u32[]{:S(2)}, u32[]{:S(2)}) collective-permute-start(bf16[64,4608]{1,0:T(8,128)(2,1)} %get-tuple-element.40), channel_id=1, source_target_pairs={{2,0},{0,2},{6,4},{4,6},{10,8},{8,10},{14,12},{12,14},{16,16},{18,... | collective-permute-start | bytes 1769480 | tf_op jit(solution)/shard_map/ppermute | solution.py:291
  10.7 2.5 %collective-permute-start.7 = (bf16[64,4608]{1,0:T(8,128)(2,1)}, bf16[64,4608]{1,0:T(8,128)(2,1)S(1)}, u32[]{:S(2)}, u32[]{:S(2)}) collective-permute-start(bf16[64,4608]{1,0:T(8,128)(2,1)} %get-tuple-element.44), channel_id=1, source_target_pairs={{14,0},{12,2},{10,4},{8,6},{4,8},{6,10},{0,12},{2,14},{28,16},{30,... | collective-permute-start | bytes 1769480 | tf_op jit(solution)/shard_map/ppermute | solution.py:291
  13.2 3.4 %copy-done.1 = bf16[4096,1024]{1,0:T(8,128)(2,1)S(1)} copy-done((bf16[4096,1024]{1,0:T(8,128)(2,1)S(1)}, bf16[4096,1024]{1,0:T(8,128)(2,1)}, u32[]{:S(2)}) %copy-start.1) | copy-done | bytes 8388632
  16.6 3.9 %shard_map.75 = (f32[256,512]{1,0:T(8,128)S(1)}, f32[256,512]{1,0:T(8,128)S(1)}) custom-call(bf16[256,4096]{1,0:T(8,128)(2,1)S(1)} %copy-done, bf16[4096,1024]{1,0:T(8,128)(2,1)S(1)} %copy-done.1), custom_call_target="tpu_custom_call" | custom-call | tf_op jit(solution)/shard_map/pallas_call | solution.py:201
  20.5 12.7 %collective-permute-done.1.refs_4_.refs_8_.refs_6_ = bf16[64,4608]{1,0:T(8,128)(2,1)S(1)} collective-permute-done((bf16[64,4608]{1,0:T(8,128)(2,1)}, bf16[64,4608]{1,0:T(8,128)(2,1)S(1)}, u32[]{:S(2)}, u32[]{:S(2)}) %collective-permute-start.1) | collective-permute-done | bytes 589856 | tf_op jit(solution)/shard_map/ppermute | solution.py:291
  33.2 0.0 collective-permute-start.2
  33.2 0.6 shard_map.73.refs_0_.row_steps
  33.9 0.4 collective-permute-done.3.refs_2_.refs_6_.refs_4_
  34.3 0.5 collective-permute-done.4.refs_3_.refs_7_.refs_5_
  34.9 0.8 %shard_map.76 = (f32[64,256]{1,0:T(8,128)S(1)}, bf16[192,512]{1,0:T(8,128)(2,1)S(1)}) custom-call(s32[8,256]{1,0:T(8,128)S(1)} %shard_map.73.refs_0_.row_steps, bf16[256,4096]{1,0:T(8,128)(2,1)S(1)} %copy-done, bf16[64,4608]{1,0:T(8,128)(2,1)S(1)} %collective-permute-done.3.refs_2_.refs_6_.refs_4_, ...), custom_call_target="tpu_custom_call" | custom-call | tf_op jit(solution)/shard_map/pallas_call | solution.py:151
  35.7 1.0 %collective-permute-start.5 = (bf16[192,512]{1,0:T(8,128)(2,1)S(1)}, bf16[192,512]{1,0:T(8,128)(2,1)S(1)}, u32[]{:S(2)}, u32[]{:S(2)}) collective-permute-start(bf16[192,512]{1,0:T(8,128)(2,1)S(1)} %get-tuple-element.43), channel_id=1, source_target_pairs={{0,16},{16,0},{1,17},{17,1},{2,18},{18,2},{3,19},{19,3},{4,20},{20... | collective-permute-start | bytes 589832 | tf_op jit(solution)/shard_map/ppermute | solution.py:294
  36.7 1.1 %collective-permute-start = (s32[8,256]{1,0:T(8,128)S(1)}, s32[8,256]{1,0:T(8,128)S(1)}, u32[]{:S(2)}, u32[]{:S(2)}) collective-permute-start(s32[8,256]{1,0:T(8,128)S(1)} %shard_map.73.refs_0_.row_steps), channel_id=1, source_target_pairs={{0,16},{16,0},{1,17},{17,1},{2,18},{18,2},{3,19},{19,3},{4,20},{20... | collective-permute-start | bytes 24584 | tf_op jit(solution)/shard_map/ppermute | solution.py:294
  37.8 22.3 %collective-permute-done.7.refs_5_.refs_7_ = bf16[64,4608]{1,0:T(8,128)(2,1)S(1)} collective-permute-done((bf16[64,4608]{1,0:T(8,128)(2,1)}, bf16[64,4608]{1,0:T(8,128)(2,1)S(1)}, u32[]{:S(2)}, u32[]{:S(2)}) %collective-permute-start.7) | collective-permute-done | bytes 589856 | tf_op jit(solution)/shard_map/ppermute | solution.py:291
  60.1 0.0 collective-permute-done.5.refs_2_
  60.1 0.0 collective-permute-done.2.refs_3_
  60.1 0.0 collective-permute-done.refs_1_
  60.1 1.3 %shard_map.77 = (f32[64,512]{1,0:T(8,128)S(1)}, bf16[64,512]{1,0:T(8,128)(2,1)S(1)}) custom-call(s32[8,256]{1,0:T(8,128)S(1)} %shard_map.73.refs_0_.row_steps, s32[8,256]{1,0:T(8,128)S(1)} %collective-permute-done.refs_1_, f32[64,256]{1,0:T(8,128)S(1)} %get-tuple-element.45.refs_2_, bf16[256,4096]{1,0:T(8,128)(2,1)S(1)} %copy-done, ...), custom_call_target="tpu_custom_call" | custom-call | tf_op jit(solution)/shard_map/pallas_call | solution.py:151
  61.4 0.1 collective-permute-start.8
  61.5 0.6 collective-permute-start.10
  62.2 0.7 collective-permute-done.8.refs_1_
  62.9 0.8 %collective-permute-start.9 = (f32[64,256]{1,0:T(8,128)S(1)}, f32[64,256]{1,0:T(8,128)S(1)}, u32[]{:S(2)}, u32[]{:S(2)}) collective-permute-start(f32[64,256]{1,0:T(8,128)S(1)} %slice_add_fusion), channel_id=1, source_target_pairs={{0,16},{16,0},{1,17},{17,1},{2,18},{18,2},{3,19},{19,3},{4,20},{20... | collective-permute-start | bytes 196616 | tf_op jit(solution)/shard_map/ppermute | solution.py:294
  63.7 0.5 shard_map.78.refs_1_
  64.2 2.3 %collective-permute-done.10.refs_3_ = bf16[64,512]{1,0:T(8,128)(2,1)S(1)} collective-permute-done((bf16[64,512]{1,0:T(8,128)(2,1)S(1)}, bf16[64,512]{1,0:T(8,128)(2,1)S(1)}, u32[]{:S(2)}, u32[]{:S(2)}) %collective-permute-start.10) | collective-permute-done | bytes 65568 | tf_op jit(solution)/shard_map/ppermute | solution.py:294
  66.4 1.0 %collective-permute-done.9.refs_0_ = f32[64,256]{1,0:T(8,128)S(1)} collective-permute-done((f32[64,256]{1,0:T(8,128)S(1)}, f32[64,256]{1,0:T(8,128)S(1)}, u32[]{:S(2)}, u32[]{:S(2)}) %collective-permute-start.9) | collective-permute-done | bytes 65568 | tf_op jit(solution)/shard_map/ppermute | solution.py:294
  67.4 1.4 %shard_map.79 = bf16[256,512]{1,0:T(8,128)(2,1)} custom-call(s32[8,256]{1,0:T(8,128)S(1)} %shard_map.73.refs_0_.row_steps, f32[64,256]{1,0:T(8,128)S(1)} %collective-permute-done.9.refs_0_, f32[256,512]{1,0:T(8,128)S(1)} %shard_map.78.refs_1_, bf16[192,512]{1,0:T(8,128)(2,1)S(1)} %collective-permute-done.5.refs_2_, ...), custom_call_target="tpu_custom_call" | custom-call | tf_op jit(solution)/shard_map/pallas_call | solution.py:254
  (8 shorter events, 0.0 us)
Async XLA Ops:
  0.0 3.8 %copy-start = (bf16[256,4096]{1,0:T(8,128)(2,1)S(1)}, bf16[256,4096]{1,0:T(8,128)(2,1)}, u32[]{:S(2)}) copy-start(bf16[256,4096]{1,0:T(8,128)(2,1)} %refs_3_) | copy-start | bytes 6291460
  3.7 29.5 %copy-start.2 = (s32[8,8]{1,0:T(8,128)S(1)}, s32[8,8]{1,0:T(8,128)}, u32[]{:S(2)}) copy-start(s32[8,8]{1,0:T(8,128)} %fetch_ref.3) | copy-start | bytes 772
  3.7 29.5 %copy-start.3 = (s32[32]{0:T(128)S(1)}, s32[32]{0:T(128)}, u32[]{:S(2)}) copy-start(s32[32]{0:T(128)} %home_ref.3) | copy-start | bytes 388
  3.7 29.5 %copy-start.4 = (s32[1,8]{1,0:T(1,128)S(1)}, s32[1,8]{1,0:T(1,128)}, u32[]{:S(2)}) copy-start(s32[1,8]{1,0:T(1,128)} %lengths_ref.1) | copy-start | bytes 100
  3.8 56.3 %collective-permute-start.6 = (bf16[256,4096]{1,0:T(8,128)(2,1)S(1)}, bf16[256,4096]{1,0:T(8,128)(2,1)S(1)}, u32[]{:S(2)}, u32[]{:S(2)}) collective-permute-start(bf16[256,4096]{1,0:T(8,128)(2,1)S(1)} %copy-done), channel_id=1, source_target_pairs={{0,16},{16,0},{1,17},{17,1},{2,18},{18,2},{3,19},{19,3},{4,20},{20... | collective-permute-start | bytes 6291464 | tf_op jit(solution)/shard_map/ppermute | solution.py:294
  5.3 27.9 %collective-permute-start.1 = (bf16[64,4608]{1,0:T(8,128)(2,1)}, bf16[64,4608]{1,0:T(8,128)(2,1)S(1)}, u32[]{:S(2)}, u32[]{:S(2)}) collective-permute-start(bf16[64,4608]{1,0:T(8,128)(2,1)} %get-tuple-element.36), channel_id=1, source_target_pairs={{8,0},{10,2},{12,4},{14,6},{2,8},{0,10},{6,12},{4,14},{26,16},{24,... | collective-permute-start | bytes 1769480 | tf_op jit(solution)/shard_map/ppermute | solution.py:291
  5.7 28.7 %collective-permute-start.3 = (bf16[64,4608]{1,0:T(8,128)(2,1)}, bf16[64,4608]{1,0:T(8,128)(2,1)S(1)}, u32[]{:S(2)}, u32[]{:S(2)}) collective-permute-start(bf16[64,4608]{1,0:T(8,128)(2,1)} %get-tuple-element.39), channel_id=1, source_target_pairs={{4,0},{6,2},{0,4},{2,6},{12,8},{14,10},{8,12},{10,14},{22,16},{20,... | collective-permute-start | bytes 1769480 | tf_op jit(solution)/shard_map/ppermute | solution.py:291
  7.2 27.6 %collective-permute-start.4 = (bf16[64,4608]{1,0:T(8,128)(2,1)}, bf16[64,4608]{1,0:T(8,128)(2,1)S(1)}, u32[]{:S(2)}, u32[]{:S(2)}) collective-permute-start(bf16[64,4608]{1,0:T(8,128)(2,1)} %get-tuple-element.40), channel_id=1, source_target_pairs={{2,0},{0,2},{6,4},{4,6},{10,8},{8,10},{14,12},{12,14},{16,16},{18,... | collective-permute-start | bytes 1769480 | tf_op jit(solution)/shard_map/ppermute | solution.py:291
  10.7 49.4 %collective-permute-start.7 = (bf16[64,4608]{1,0:T(8,128)(2,1)}, bf16[64,4608]{1,0:T(8,128)(2,1)S(1)}, u32[]{:S(2)}, u32[]{:S(2)}) collective-permute-start(bf16[64,4608]{1,0:T(8,128)(2,1)} %get-tuple-element.44), channel_id=1, source_target_pairs={{14,0},{12,2},{10,4},{8,6},{4,8},{6,10},{0,12},{2,14},{28,16},{30,... | collective-permute-start | bytes 1769480 | tf_op jit(solution)/shard_map/ppermute | solution.py:291
  13.2 3.4 %copy-start.1 = (bf16[4096,1024]{1,0:T(8,128)(2,1)S(1)}, bf16[4096,1024]{1,0:T(8,128)(2,1)}, u32[]{:S(2)}) copy-start(bf16[4096,1024]{1,0:T(8,128)(2,1)} %weight_ref.1) | copy-start | bytes 25165828
  33.2 26.9 %collective-permute-start.2 = (f32[256,512]{1,0:T(8,128)S(1)}, f32[256,512]{1,0:T(8,128)S(1)}, u32[]{:S(2)}, u32[]{:S(2)}) collective-permute-start(f32[256,512]{1,0:T(8,128)S(1)} %get-tuple-element.38), channel_id=1, source_target_pairs={{0,1},{1,0},{2,3},{3,2},{4,5},{5,4},{6,7},{7,6},{8,9},{9,8},{10,11... | collective-permute-start | bytes 1572872 | tf_op jit(solution)/shard_map/ppermute | solution.py:297
  35.7 24.4 %collective-permute-start.5 = (bf16[192,512]{1,0:T(8,128)(2,1)S(1)}, bf16[192,512]{1,0:T(8,128)(2,1)S(1)}, u32[]{:S(2)}, u32[]{:S(2)}) collective-permute-start(bf16[192,512]{1,0:T(8,128)(2,1)S(1)} %get-tuple-element.43), channel_id=1, source_target_pairs={{0,16},{16,0},{1,17},{17,1},{2,18},{18,2},{3,19},{19,3},{4,20},{20... | collective-permute-start | bytes 589832 | tf_op jit(solution)/shard_map/ppermute | solution.py:294
  36.7 23.4 %collective-permute-start = (s32[8,256]{1,0:T(8,128)S(1)}, s32[8,256]{1,0:T(8,128)S(1)}, u32[]{:S(2)}, u32[]{:S(2)}) collective-permute-start(s32[8,256]{1,0:T(8,128)S(1)} %shard_map.73.refs_0_.row_steps), channel_id=1, source_target_pairs={{0,16},{16,0},{1,17},{17,1},{2,18},{18,2},{3,19},{19,3},{4,20},{20... | collective-permute-start | bytes 24584 | tf_op jit(solution)/shard_map/ppermute | solution.py:294
  61.4 1.4 %collective-permute-start.8 = (f32[64,512]{1,0:T(8,128)S(1)}, f32[64,512]{1,0:T(8,128)S(1)}, u32[]{:S(2)}, u32[]{:S(2)}) collective-permute-start(f32[64,512]{1,0:T(8,128)S(1)} %get-tuple-element.48.refs_0_), channel_id=1, source_target_pairs={{0,1},{1,0},{2,3},{3,2},{4,5},{5,4},{6,7},{7,6},{8,9},{9,8},{10,11... | collective-permute-start | bytes 393224 | tf_op jit(solution)/shard_map/ppermute | solution.py:297
  61.5 4.9 %collective-permute-start.10 = (bf16[64,512]{1,0:T(8,128)(2,1)S(1)}, bf16[64,512]{1,0:T(8,128)(2,1)S(1)}, u32[]{:S(2)}, u32[]{:S(2)}) collective-permute-start(bf16[64,512]{1,0:T(8,128)(2,1)S(1)} %get-tuple-element.52), channel_id=1, source_target_pairs={{0,16},{16,0},{1,17},{17,1},{2,18},{18,2},{3,19},{19,3},{4,20},{20... | collective-permute-start | bytes 196616 | tf_op jit(solution)/shard_map/ppermute | solution.py:294
  62.9 4.6 %collective-permute-start.9 = (f32[64,256]{1,0:T(8,128)S(1)}, f32[64,256]{1,0:T(8,128)S(1)}, u32[]{:S(2)}, u32[]{:S(2)}) collective-permute-start(f32[64,256]{1,0:T(8,128)S(1)} %slice_add_fusion), channel_id=1, source_target_pairs={{0,16},{16,0},{1,17},{17,1},{2,18},{18,2},{3,19},{19,3},{4,20},{20... | collective-permute-start | bytes 196616 | tf_op jit(solution)/shard_map/ppermute | solution.py:294

commit v24 on v20

--- a/solution.py
+++ b/solution.py
@@ -93,7 +93,7 @@
 def pack(groups, columns, adapter_home, fetch_list, panels, expand_panels):
     rank, depth = panels.shape[1:]
     shape = (rank, depth + columns)
-    cuts = 4
+    cuts = 2
     return list(
         pl.pallas_call(
             functools.partial(pack_kernel, groups),
@@ -277,8 +277,8 @@
     half = replicas // 2
     far = [(tuple(range(step, step + parts)), True) for step in range(half, replicas, parts)]
     size = half // parts - 1
-    near = [(tuple(parts + p * size + g for p in range(parts)), False) for g in range(size)]
-    near.append((tuple(reversed(range(parts))), False))
+    near = [(tuple(parts + p * size + g for p in reversed(range(parts))), False) for g in range(size)]
+    near.append((tuple(range(parts)), False))
 
     def hop(x, group):
         steps, moves = group

time: 69 us -> 68.9 us (level)
  the two profiles are of different devices: /device:TPU:16 before, /device:TPU:20 now
where the time goes in v24:
time: 68.9 us; the launch traced here: 68.6 us
  waiting for transfers between devices  42.2 us (61%)
  Pallas kernels  12.1 us (18%)
  starting transfers between devices  10.8 us (16%)
  local copies, waits for them, and re-layouts  3.4 us (5%)
    ppermute x4, waiting for transfers between devices, hop(): return lax.ppermute(x, ('parts', 'rep'), pairs)  37.6 us
    ppermute x4, starting transfers between devices, hop(): return lax.ppermute(x, ('parts', 'rep'), pairs)  6.1 us
    ppermute x5, starting transfers between devices, shift_parts(): lax.ppermute(x, 'parts', [(i, (i + shift) % parts) for i in range(parts)])  4.6 us
    pallas_call x1, Pallas kernels, base_terms(): pl.pallas_call(functools.partial(base_kernel, chunks), out_shape=[jax.Sha...  3.94 us
    pallas_call x1, Pallas kernels, pack(): pl.pallas_call(functools.partial(pack_kernel, groups), out_shape=[jax.Sha...  3.51 us
    unnamed x10, local copies, waits for them, and re-layouts  3.4 us
    ppermute x5, waiting for transfers between devices, shift_parts(): lax.ppermute(x, 'parts', [(i, (i + shift) % parts) for i in range(parts)])  3.26 us
    pallas_call x2, Pallas kernels, score(): pl.pallas_call(functools.partial(score_kernel, plan, groups, kept, chunks...  2.14 us
  transfers between devices with their start and end apart: 11, of which 6 were waited for; matrix products, arithmetic and copies ran while one was open for 0% of the time, Pallas kernels for 9%

profile of v24, /device:TPU:20, one launch (start us, length us, event | category | flops | bytes accessed | tf_op | source)
XLA Modules:
  0.0 68.6 jit_solution(7933940768625581671)
XLA Ops:
  0.0 3.5 %shard_map.74 = (bf16[64,4608]{1,0:T(8,128)(2,1)}, bf16[64,4608]{1,0:T(8,128)(2,1)}, bf16[64,4608]{1,0:T(8,128)(2,1)}, bf16[64,4608]{1,0:T(8,128)(2,1)}) custom-call(s32[32]{0:T(128)} %home_ref.3, s32[8,8]{1,0:T(8,128)} %fetch_ref.3, bf16[4,64,4096]{2,1,0:T(8,128)(2,1)} %bitcast.1, bf16[4,64,1024]{2,1,0:T(8,128)(2,1)} %expand_ref.1), custom_call_target="tpu_custom_call" | custom-call | tf_op jit(solution)/shard_map/pallas_call | solution.py:98
  3.5 0.0 copy-start.2
  3.5 0.0 copy-start.3
  3.5 0.0 copy-start.4
  3.6 1.6 %collective-permute-start.6 = (bf16[256,4096]{1,0:T(8,128)(2,1)S(1)}, bf16[256,4096]{1,0:T(8,128)(2,1)S(1)}, u32[]{:S(2)}, u32[]{:S(2)}) collective-permute-start(bf16[256,4096]{1,0:T(8,128)(2,1)S(1)} %copy-done), channel_id=1, source_target_pairs={{0,16},{16,0},{1,17},{17,1},{2,18},{18,2},{3,19},{19,3},{4,20},{20... | collective-permute-start | bytes 6291464 | tf_op jit(solution)/shard_map/ppermute | solution.py:293
  5.2 0.3 collective-permute-start.1
  5.5 1.7 %collective-permute-start.3 = (bf16[64,4608]{1,0:T(8,128)(2,1)}, bf16[64,4608]{1,0:T(8,128)(2,1)S(1)}, u32[]{:S(2)}, u32[]{:S(2)}) collective-permute-start(bf16[64,4608]{1,0:T(8,128)(2,1)} %get-tuple-element.39), channel_id=1, source_target_pairs={{6,0},{4,2},{2,4},{0,6},{14,8},{12,10},{10,12},{8,14},{20,16},{22,... | collective-permute-start | bytes 1769480 | tf_op jit(solution)/shard_map/ppermute | solution.py:290
  7.2 1.7 %collective-permute-start.4 = (bf16[64,4608]{1,0:T(8,128)(2,1)}, bf16[64,4608]{1,0:T(8,128)(2,1)S(1)}, u32[]{:S(2)}, u32[]{:S(2)}) collective-permute-start(bf16[64,4608]{1,0:T(8,128)(2,1)} %get-tuple-element.40), channel_id=1, source_target_pairs={{0,0},{2,2},{4,4},{6,6},{8,8},{10,10},{12,12},{14,14},{18,16},{16,... | collective-permute-start | bytes 1769480 | tf_op jit(solution)/shard_map/ppermute | solution.py:290
  8.9 2.4 %collective-permute-start.7 = (bf16[64,4608]{1,0:T(8,128)(2,1)}, bf16[64,4608]{1,0:T(8,128)(2,1)S(1)}, u32[]{:S(2)}, u32[]{:S(2)}) collective-permute-start(bf16[64,4608]{1,0:T(8,128)(2,1)} %get-tuple-element.44), channel_id=1, source_target_pairs={{12,0},{14,2},{8,4},{10,6},{6,8},{4,10},{2,12},{0,14},{30,16},{28,... | collective-permute-start | bytes 1769480 | tf_op jit(solution)/shard_map/ppermute | solution.py:290
  11.3 3.4 %copy-done.1 = bf16[4096,1024]{1,0:T(8,128)(2,1)S(1)} copy-done((bf16[4096,1024]{1,0:T(8,128)(2,1)S(1)}, bf16[4096,1024]{1,0:T(8,128)(2,1)}, u32[]{:S(2)}) %copy-start.1) | copy-done | bytes 8388632
  14.7 3.9 %shard_map.75 = (f32[256,512]{1,0:T(8,128)S(1)}, f32[256,512]{1,0:T(8,128)S(1)}) custom-call(bf16[256,4096]{1,0:T(8,128)(2,1)S(1)} %copy-done, bf16[4096,1024]{1,0:T(8,128)(2,1)S(1)} %copy-done.1), custom_call_target="tpu_custom_call" | custom-call | tf_op jit(solution)/shard_map/pallas_call | solution.py:201
  18.6 13.4 %collective-permute-done.1.refs_4_.refs_8_.refs_6_ = bf16[64,4608]{1,0:T(8,128)(2,1)S(1)} collective-permute-done((bf16[64,4608]{1,0:T(8,128)(2,1)}, bf16[64,4608]{1,0:T(8,128)(2,1)S(1)}, u32[]{:S(2)}, u32[]{:S(2)}) %collective-permute-start.1) | collective-permute-done | bytes 589856 | tf_op jit(solution)/shard_map/ppermute | solution.py:290
  32.1 0.0 collective-permute-start.2
  32.1 0.6 shard_map.73.refs_0_.row_steps
  32.7 3.4 %collective-permute-done.3.refs_2_.refs_6_.refs_4_ = bf16[64,4608]{1,0:T(8,128)(2,1)S(1)} collective-permute-done((bf16[64,4608]{1,0:T(8,128)(2,1)}, bf16[64,4608]{1,0:T(8,128)(2,1)S(1)}, u32[]{:S(2)}, u32[]{:S(2)}) %collective-permute-start.3) | collective-permute-done | bytes 589856 | tf_op jit(solution)/shard_map/ppermute | solution.py:290
  36.1 0.0 collective-permute-done.4.refs_3_.refs_7_.refs_5_
  36.2 0.8 %shard_map.76 = (f32[64,256]{1,0:T(8,128)S(1)}, bf16[192,512]{1,0:T(8,128)(2,1)S(1)}) custom-call(s32[8,256]{1,0:T(8,128)S(1)} %shard_map.73.refs_0_.row_steps, bf16[256,4096]{1,0:T(8,128)(2,1)S(1)} %copy-done, bf16[64,4608]{1,0:T(8,128)(2,1)S(1)} %collective-permute-done.3.refs_2_.refs_6_.refs_4_, ...), custom_call_target="tpu_custom_call" | custom-call | tf_op jit(solution)/shard_map/pallas_call | solution.py:151
  37.0 0.1 collective-permute-start.5
  37.1 2.0 %collective-permute-start = (s32[8,256]{1,0:T(8,128)S(1)}, s32[8,256]{1,0:T(8,128)S(1)}, u32[]{:S(2)}, u32[]{:S(2)}) collective-permute-start(s32[8,256]{1,0:T(8,128)S(1)} %shard_map.73.refs_0_.row_steps), channel_id=1, source_target_pairs={{0,16},{16,0},{1,17},{17,1},{2,18},{18,2},{3,19},{19,3},{4,20},{20... | collective-permute-start | bytes 24584 | tf_op jit(solution)/shard_map/ppermute | solution.py:293
  39.1 20.8 %collective-permute-done.7.refs_5_.refs_7_ = bf16[64,4608]{1,0:T(8,128)(2,1)S(1)} collective-permute-done((bf16[64,4608]{1,0:T(8,128)(2,1)}, bf16[64,4608]{1,0:T(8,128)(2,1)S(1)}, u32[]{:S(2)}, u32[]{:S(2)}) %collective-permute-start.7) | collective-permute-done | bytes 589856 | tf_op jit(solution)/shard_map/ppermute | solution.py:290
  59.9 0.0 collective-permute-done.5.refs_2_
  59.9 0.0 collective-permute-done.2.refs_3_
  59.9 0.0 collective-permute-done.6.refs_4_
  59.9 1.3 %shard_map.77 = (f32[64,512]{1,0:T(8,128)S(1)}, bf16[64,512]{1,0:T(8,128)(2,1)S(1)}) custom-call(s32[8,256]{1,0:T(8,128)S(1)} %shard_map.73.refs_0_.row_steps, s32[8,256]{1,0:T(8,128)S(1)} %collective-permute-done.refs_1_, f32[64,256]{1,0:T(8,128)S(1)} %get-tuple-element.45.refs_2_, bf16[256,4096]{1,0:T(8,128)(2,1)S(1)} %copy-done, ...), custom_call_target="tpu_custom_call" | custom-call | tf_op jit(solution)/shard_map/pallas_call | solution.py:151
  61.2 0.1 collective-permute-start.8
  61.3 0.1 collective-permute-start.10
  61.4 1.3 %collective-permute-done.8.refs_1_ = f32[64,512]{1,0:T(8,128)S(1)} collective-permute-done((f32[64,512]{1,0:T(8,128)S(1)}, f32[64,512]{1,0:T(8,128)S(1)}, u32[]{:S(2)}, u32[]{:S(2)}) %collective-permute-start.8) | collective-permute-done | bytes 131104 | tf_op jit(solution)/shard_map/ppermute | solution.py:296
  62.7 0.8 %collective-permute-start.9 = (f32[64,256]{1,0:T(8,128)S(1)}, f32[64,256]{1,0:T(8,128)S(1)}, u32[]{:S(2)}, u32[]{:S(2)}) collective-permute-start(f32[64,256]{1,0:T(8,128)S(1)} %slice_add_fusion), channel_id=1, source_target_pairs={{0,16},{16,0},{1,17},{17,1},{2,18},{18,2},{3,19},{19,3},{4,20},{20... | collective-permute-start | bytes 196616 | tf_op jit(solution)/shard_map/ppermute | solution.py:293
  63.5 0.5 shard_map.78.refs_1_
  64.0 2.3 %collective-permute-done.10.refs_3_ = bf16[64,512]{1,0:T(8,128)(2,1)S(1)} collective-permute-done((bf16[64,512]{1,0:T(8,128)(2,1)S(1)}, bf16[64,512]{1,0:T(8,128)(2,1)S(1)}, u32[]{:S(2)}, u32[]{:S(2)}) %collective-permute-start.10) | collective-permute-done | bytes 65568 | tf_op jit(solution)/shard_map/ppermute | solution.py:293
  66.2 1.0 %collective-permute-done.9.refs_0_ = f32[64,256]{1,0:T(8,128)S(1)} collective-permute-done((f32[64,256]{1,0:T(8,128)S(1)}, f32[64,256]{1,0:T(8,128)S(1)}, u32[]{:S(2)}, u32[]{:S(2)}) %collective-permute-start.9) | collective-permute-done | bytes 65568 | tf_op jit(solution)/shard_map/ppermute | solution.py:293
  67.2 1.4 %shard_map.79 = bf16[256,512]{1,0:T(8,128)(2,1)} custom-call(s32[8,256]{1,0:T(8,128)S(1)} %shard_map.73.refs_0_.row_steps, f32[64,256]{1,0:T(8,128)S(1)} %collective-permute-done.9.refs_0_, f32[256,512]{1,0:T(8,128)S(1)} %shard_map.78.refs_1_, bf16[192,512]{1,0:T(8,128)(2,1)S(1)} %collective-permute-done.5.refs_2_, ...), custom_call_target="tpu_custom_call" | custom-call | tf_op jit(solution)/shard_map/pallas_call | solution.py:254
  (8 shorter events, 0.0 us)
Async XLA Ops:
  0.0 3.6 %copy-start = (bf16[256,4096]{1,0:T(8,128)(2,1)S(1)}, bf16[256,4096]{1,0:T(8,128)(2,1)}, u32[]{:S(2)}) copy-start(bf16[256,4096]{1,0:T(8,128)(2,1)} %refs_3_) | copy-start | bytes 6291460
  3.5 28.5 %copy-start.2 = (s32[8,8]{1,0:T(8,128)S(1)}, s32[8,8]{1,0:T(8,128)}, u32[]{:S(2)}) copy-start(s32[8,8]{1,0:T(8,128)} %fetch_ref.3) | copy-start | bytes 772
  3.5 28.5 %copy-start.3 = (s32[32]{0:T(128)S(1)}, s32[32]{0:T(128)}, u32[]{:S(2)}) copy-start(s32[32]{0:T(128)} %home_ref.3) | copy-start | bytes 388
  3.5 28.5 %copy-start.4 = (s32[1,8]{1,0:T(1,128)S(1)}, s32[1,8]{1,0:T(1,128)}, u32[]{:S(2)}) copy-start(s32[1,8]{1,0:T(1,128)} %lengths_ref.1) | copy-start | bytes 100
  3.6 56.3 %collective-permute-start.6 = (bf16[256,4096]{1,0:T(8,128)(2,1)S(1)}, bf16[256,4096]{1,0:T(8,128)(2,1)S(1)}, u32[]{:S(2)}, u32[]{:S(2)}) collective-permute-start(bf16[256,4096]{1,0:T(8,128)(2,1)S(1)} %copy-done), channel_id=1, source_target_pairs={{0,16},{16,0},{1,17},{17,1},{2,18},{18,2},{3,19},{19,3},{4,20},{20... | collective-permute-start | bytes 6291464 | tf_op jit(solution)/shard_map/ppermute | solution.py:293
  5.2 26.9 %collective-permute-start.1 = (bf16[64,4608]{1,0:T(8,128)(2,1)}, bf16[64,4608]{1,0:T(8,128)(2,1)S(1)}, u32[]{:S(2)}, u32[]{:S(2)}) collective-permute-start(bf16[64,4608]{1,0:T(8,128)(2,1)} %get-tuple-element.36), channel_id=1, source_target_pairs={{8,0},{10,2},{12,4},{14,6},{2,8},{0,10},{6,12},{4,14},{26,16},{24,... | collective-permute-start | bytes 1769480 | tf_op jit(solution)/shard_map/ppermute | solution.py:290
  5.5 30.7 %collective-permute-start.3 = (bf16[64,4608]{1,0:T(8,128)(2,1)}, bf16[64,4608]{1,0:T(8,128)(2,1)S(1)}, u32[]{:S(2)}, u32[]{:S(2)}) collective-permute-start(bf16[64,4608]{1,0:T(8,128)(2,1)} %get-tuple-element.39), channel_id=1, source_target_pairs={{6,0},{4,2},{2,4},{0,6},{14,8},{12,10},{10,12},{8,14},{20,16},{22,... | collective-permute-start | bytes 1769480 | tf_op jit(solution)/shard_map/ppermute | solution.py:290
  7.2 29.0 %collective-permute-start.4 = (bf16[64,4608]{1,0:T(8,128)(2,1)}, bf16[64,4608]{1,0:T(8,128)(2,1)S(1)}, u32[]{:S(2)}, u32[]{:S(2)}) collective-permute-start(bf16[64,4608]{1,0:T(8,128)(2,1)} %get-tuple-element.40), channel_id=1, source_target_pairs={{0,0},{2,2},{4,4},{6,6},{8,8},{10,10},{12,12},{14,14},{18,16},{16,... | collective-permute-start | bytes 1769480 | tf_op jit(solution)/shard_map/ppermute | solution.py:290
  8.9 51.0 %collective-permute-start.7 = (bf16[64,4608]{1,0:T(8,128)(2,1)}, bf16[64,4608]{1,0:T(8,128)(2,1)S(1)}, u32[]{:S(2)}, u32[]{:S(2)}) collective-permute-start(bf16[64,4608]{1,0:T(8,128)(2,1)} %get-tuple-element.44), channel_id=1, source_target_pairs={{12,0},{14,2},{8,4},{10,6},{6,8},{4,10},{2,12},{0,14},{30,16},{28,... | collective-permute-start | bytes 1769480 | tf_op jit(solution)/shard_map/ppermute | solution.py:290
  11.3 3.4 %copy-start.1 = (bf16[4096,1024]{1,0:T(8,128)(2,1)S(1)}, bf16[4096,1024]{1,0:T(8,128)(2,1)}, u32[]{:S(2)}) copy-start(bf16[4096,1024]{1,0:T(8,128)(2,1)} %weight_ref.1) | copy-start | bytes 25165828
  32.1 27.8 %collective-permute-start.2 = (f32[256,512]{1,0:T(8,128)S(1)}, f32[256,512]{1,0:T(8,128)S(1)}, u32[]{:S(2)}, u32[]{:S(2)}) collective-permute-start(f32[256,512]{1,0:T(8,128)S(1)} %get-tuple-element.38), channel_id=1, source_target_pairs={{0,1},{1,0},{2,3},{3,2},{4,5},{5,4},{6,7},{7,6},{8,9},{9,8},{10,11... | collective-permute-start | bytes 1572872 | tf_op jit(solution)/shard_map/ppermute | solution.py:296
  37.0 22.9 %collective-permute-start.5 = (bf16[192,512]{1,0:T(8,128)(2,1)S(1)}, bf16[192,512]{1,0:T(8,128)(2,1)S(1)}, u32[]{:S(2)}, u32[]{:S(2)}) collective-permute-start(bf16[192,512]{1,0:T(8,128)(2,1)S(1)} %get-tuple-element.43), channel_id=1, source_target_pairs={{0,16},{16,0},{1,17},{17,1},{2,18},{18,2},{3,19},{19,3},{4,20},{20... | collective-permute-start | bytes 589832 | tf_op jit(solution)/shard_map/ppermute | solution.py:293
  37.1 22.8 %collective-permute-start = (s32[8,256]{1,0:T(8,128)S(1)}, s32[8,256]{1,0:T(8,128)S(1)}, u32[]{:S(2)}, u32[]{:S(2)}) collective-permute-start(s32[8,256]{1,0:T(8,128)S(1)} %shard_map.73.refs_0_.row_steps), channel_id=1, source_target_pairs={{0,16},{16,0},{1,17},{17,1},{2,18},{18,2},{3,19},{19,3},{4,20},{20... | collective-permute-start | bytes 24584 | tf_op jit(solution)/shard_map/ppermute | solution.py:293
  61.2 1.4 %collective-permute-start.8 = (f32[64,512]{1,0:T(8,128)S(1)}, f32[64,512]{1,0:T(8,128)S(1)}, u32[]{:S(2)}, u32[]{:S(2)}) collective-permute-start(f32[64,512]{1,0:T(8,128)S(1)} %get-tuple-element.48.refs_0_), channel_id=1, source_target_pairs={{0,1},{1,0},{2,3},{3,2},{4,5},{5,4},{6,7},{7,6},{8,9},{9,8},{10,11... | collective-permute-start | bytes 393224 | tf_op jit(solution)/shard_map/ppermute | solution.py:296
  61.3 4.9 %collective-permute-start.10 = (bf16[64,512]{1,0:T(8,128)(2,1)S(1)}, bf16[64,512]{1,0:T(8,128)(2,1)S(1)}, u32[]{:S(2)}, u32[]{:S(2)}) collective-permute-start(bf16[64,512]{1,0:T(8,128)(2,1)S(1)} %get-tuple-element.52), channel_id=1, source_target_pairs={{0,16},{16,0},{1,17},{17,1},{2,18},{18,2},{3,19},{19,3},{4,20},{20... | collective-permute-start | bytes 196616 | tf_op jit(solution)/shard_map/ppermute | solution.py:293
  62.7 4.6 %collective-permute-start.9 = (f32[64,256]{1,0:T(8,128)S(1)}, f32[64,256]{1,0:T(8,128)S(1)}, u32[]{:S(2)}, u32[]{:S(2)}) collective-permute-start(f32[64,256]{1,0:T(8,128)S(1)} %slice_add_fusion), channel_id=1, source_target_pairs={{0,16},{16,0},{1,17},{17,1},{2,18},{18,2},{3,19},{19,3},{4,20},{20... | collective-permute-start | bytes 196616 | tf_op jit(solution)/shard_map/ppermute | solution.py:293

commit v25 on v24

--- a/solution.py
+++ b/solution.py
@@ -275,7 +275,7 @@
     tie = lax.optimization_barrier
 
     half = replicas // 2
-    far = [(tuple(range(step, step + parts)), True) for step in range(half, replicas, parts)]
+    far = [(tuple(range(step, step + parts))[::-1], True) for step in range(half, replicas, parts)]
     size = half // parts - 1
     near = [(tuple(parts + p * size + g for p in reversed(range(parts))), False) for g in range(size)]
     near.append((tuple(range(parts)), False))

time: 68.9 us -> 68 us (0.987)
  the two profiles are of different devices: /device:TPU:20 before, /device:TPU:0 now
where the time goes in v25:
time: 68 us; the launch traced here: 67.7 us
  waiting for transfers between devices  38.7 us (57%)
  starting transfers between devices  13.3 us (20%)
  Pallas kernels  12.1 us (18%)
  local copies, waits for them, and re-layouts  3.4 us (5%)
    ppermute x4, waiting for transfers between devices, hop(): return lax.ppermute(x, ('parts', 'rep'), pairs)  29 us
    ppermute x5, waiting for transfers between devices, shift_parts(): lax.ppermute(x, 'parts', [(i, (i + shift) % parts) for i in range(parts)])  8.72 us
    ppermute x4, starting transfers between devices, hop(): return lax.ppermute(x, ('parts', 'rep'), pairs)  7 us
    ppermute x5, starting transfers between devices, shift_parts(): lax.ppermute(x, 'parts', [(i, (i + shift) % parts) for i in range(parts)])  6.25 us
    pallas_call x1, Pallas kernels, base_terms(): pl.pallas_call(functools.partial(base_kernel, chunks), out_shape=[jax.Sha...  3.94 us
    pallas_call x1, Pallas kernels, pack(): pl.pallas_call(functools.partial(pack_kernel, groups), out_shape=[jax.Sha...  3.51 us
    unnamed x10, local copies, waits for them, and re-layouts  3.4 us
    pallas_call x2, Pallas kernels, score(): pl.pallas_call(functools.partial(score_kernel, plan, groups, kept, chunks...  2.14 us
  transfers between devices with their start and end apart: 11, of which 6 were waited for; matrix products, arithmetic and copies ran while one was open for 0% of the time, Pallas kernels for 9%

profile of v25, /device:TPU:0, one launch (start us, length us, event | category | flops | bytes accessed | tf_op | source)
XLA Modules:
  0.0 67.7 jit_solution(17181916734478795587)
XLA Ops:
  0.0 3.5 %shard_map.74 = (bf16[64,4608]{1,0:T(8,128)(2,1)}, bf16[64,4608]{1,0:T(8,128)(2,1)}, bf16[64,4608]{1,0:T(8,128)(2,1)}, bf16[64,4608]{1,0:T(8,128)(2,1)}) custom-call(s32[32]{0:T(128)} %home_ref.3, s32[8,8]{1,0:T(8,128)} %fetch_ref.3, bf16[4,64,4096]{2,1,0:T(8,128)(2,1)} %bitcast.1, bf16[4,64,1024]{2,1,0:T(8,128)(2,1)} %expand_ref.1), custom_call_target="tpu_custom_call" | custom-call | tf_op jit(solution)/shard_map/pallas_call | solution.py:98
  3.5 0.0 copy-start.2
  3.5 0.0 copy-start.3
  3.5 0.0 copy-start.4
  3.6 3.0 %collective-permute-start.6 = (bf16[256,4096]{1,0:T(8,128)(2,1)S(1)}, bf16[256,4096]{1,0:T(8,128)(2,1)S(1)}, u32[]{:S(2)}, u32[]{:S(2)}) collective-permute-start(bf16[256,4096]{1,0:T(8,128)(2,1)S(1)} %copy-done), channel_id=1, source_target_pairs={{0,16},{16,0},{1,17},{17,1},{2,18},{18,2},{3,19},{19,3},{4,20},{20... | collective-permute-start | bytes 6291464 | tf_op jit(solution)/shard_map/ppermute | solution.py:293
  6.6 2.6 %collective-permute-start.1 = (bf16[64,4608]{1,0:T(8,128)(2,1)}, bf16[64,4608]{1,0:T(8,128)(2,1)S(1)}, u32[]{:S(2)}, u32[]{:S(2)}) collective-permute-start(bf16[64,4608]{1,0:T(8,128)(2,1)} %get-tuple-element.36), channel_id=1, source_target_pairs={{10,0},{8,2},{14,4},{12,6},{0,8},{2,10},{4,12},{6,14},{24,16},{26,... | collective-permute-start | bytes 1769480 | tf_op jit(solution)/shard_map/ppermute | solution.py:290
  9.2 2.5 %collective-permute-start.3 = (bf16[64,4608]{1,0:T(8,128)(2,1)}, bf16[64,4608]{1,0:T(8,128)(2,1)S(1)}, u32[]{:S(2)}, u32[]{:S(2)}) collective-permute-start(bf16[64,4608]{1,0:T(8,128)(2,1)} %get-tuple-element.39), channel_id=1, source_target_pairs={{6,0},{4,2},{2,4},{0,6},{14,8},{12,10},{10,12},{8,14},{20,16},{22,... | collective-permute-start | bytes 1769480 | tf_op jit(solution)/shard_map/ppermute | solution.py:290
  11.7 1.7 %collective-permute-start.4 = (bf16[64,4608]{1,0:T(8,128)(2,1)}, bf16[64,4608]{1,0:T(8,128)(2,1)S(1)}, u32[]{:S(2)}, u32[]{:S(2)}) collective-permute-start(bf16[64,4608]{1,0:T(8,128)(2,1)} %get-tuple-element.40), channel_id=1, source_target_pairs={{0,0},{2,2},{4,4},{6,6},{8,8},{10,10},{12,12},{14,14},{18,16},{16,... | collective-permute-start | bytes 1769480 | tf_op jit(solution)/shard_map/ppermute | solution.py:290
  13.4 0.2 collective-permute-start.7
  13.6 3.4 %copy-done.1 = bf16[4096,1024]{1,0:T(8,128)(2,1)S(1)} copy-done((bf16[4096,1024]{1,0:T(8,128)(2,1)S(1)}, bf16[4096,1024]{1,0:T(8,128)(2,1)}, u32[]{:S(2)}) %copy-start.1) | copy-done | bytes 8388632
  17.0 3.9 %shard_map.75 = (f32[256,512]{1,0:T(8,128)S(1)}, f32[256,512]{1,0:T(8,128)S(1)}) custom-call(bf16[256,4096]{1,0:T(8,128)(2,1)S(1)} %copy-done, bf16[4096,1024]{1,0:T(8,128)(2,1)S(1)} %copy-done.1), custom_call_target="tpu_custom_call" | custom-call | tf_op jit(solution)/shard_map/pallas_call | solution.py:201
  20.9 29.0 %collective-permute-done.1.refs_4_.refs_8_.refs_6_ = bf16[64,4608]{1,0:T(8,128)(2,1)S(1)} collective-permute-done((bf16[64,4608]{1,0:T(8,128)(2,1)}, bf16[64,4608]{1,0:T(8,128)(2,1)S(1)}, u32[]{:S(2)}, u32[]{:S(2)}) %collective-permute-start.1) | collective-permute-done | bytes 589856 | tf_op jit(solution)/shard_map/ppermute | solution.py:290
  49.9 0.0 collective-permute-start.2
  49.9 0.6 shard_map.73.refs_0_.row_steps
  50.5 0.0 collective-permute-done.3.refs_2_.refs_6_.refs_4_
  50.5 0.0 collective-permute-done.4.refs_3_.refs_7_.refs_5_
  50.6 0.8 %shard_map.76 = (f32[64,256]{1,0:T(8,128)S(1)}, bf16[192,512]{1,0:T(8,128)(2,1)S(1)}) custom-call(s32[8,256]{1,0:T(8,128)S(1)} %shard_map.73.refs_0_.row_steps, bf16[256,4096]{1,0:T(8,128)(2,1)S(1)} %copy-done, bf16[64,4608]{1,0:T(8,128)(2,1)S(1)} %collective-permute-done.3.refs_2_.refs_6_.refs_4_, ...), custom_call_target="tpu_custom_call" | custom-call | tf_op jit(solution)/shard_map/pallas_call | solution.py:151
  51.4 0.1 collective-permute-start.5
  51.5 2.0 %collective-permute-start = (s32[8,256]{1,0:T(8,128)S(1)}, s32[8,256]{1,0:T(8,128)S(1)}, u32[]{:S(2)}, u32[]{:S(2)}) collective-permute-start(s32[8,256]{1,0:T(8,128)S(1)} %shard_map.73.refs_0_.row_steps), channel_id=1, source_target_pairs={{0,16},{16,0},{1,17},{17,1},{2,18},{18,2},{3,19},{19,3},{4,20},{20... | collective-permute-start | bytes 24584 | tf_op jit(solution)/shard_map/ppermute | solution.py:293
  53.5 5.4 %collective-permute-done.5.refs_2_ = bf16[192,512]{1,0:T(8,128)(2,1)S(1)} collective-permute-done((bf16[192,512]{1,0:T(8,128)(2,1)S(1)}, bf16[192,512]{1,0:T(8,128)(2,1)S(1)}, u32[]{:S(2)}, u32[]{:S(2)}) %collective-permute-start.5) | collective-permute-done | bytes 196640 | tf_op jit(solution)/shard_map/ppermute | solution.py:293
  58.9 0.0 collective-permute-done.2.refs_3_
  58.9 0.0 collective-permute-done.6.refs_4_
  58.9 0.1 collective-permute-done.refs_1_
  59.0 1.3 %shard_map.77 = (f32[64,512]{1,0:T(8,128)S(1)}, bf16[64,512]{1,0:T(8,128)(2,1)S(1)}) custom-call(s32[8,256]{1,0:T(8,128)S(1)} %shard_map.73.refs_0_.row_steps, s32[8,256]{1,0:T(8,128)S(1)} %collective-permute-done.refs_1_, f32[64,256]{1,0:T(8,128)S(1)} %get-tuple-element.45.refs_2_, bf16[256,4096]{1,0:T(8,128)(2,1)S(1)} %copy-done, ...), custom_call_target="tpu_custom_call" | custom-call | tf_op jit(solution)/shard_map/pallas_call | solution.py:151
  60.3 0.1 collective-permute-start.8
  60.4 0.3 collective-permute-start.10
  60.7 1.0 %collective-permute-done.8.refs_1_ = f32[64,512]{1,0:T(8,128)S(1)} collective-permute-done((f32[64,512]{1,0:T(8,128)S(1)}, f32[64,512]{1,0:T(8,128)S(1)}, u32[]{:S(2)}, u32[]{:S(2)}) %collective-permute-start.8) | collective-permute-done | bytes 131104 | tf_op jit(solution)/shard_map/ppermute | solution.py:296
  61.7 0.8 %collective-permute-start.9 = (f32[64,256]{1,0:T(8,128)S(1)}, f32[64,256]{1,0:T(8,128)S(1)}, u32[]{:S(2)}, u32[]{:S(2)}) collective-permute-start(f32[64,256]{1,0:T(8,128)S(1)} %slice_add_fusion), channel_id=1, source_target_pairs={{0,16},{16,0},{1,17},{17,1},{2,18},{18,2},{3,19},{19,3},{4,20},{20... | collective-permute-start | bytes 196616 | tf_op jit(solution)/shard_map/ppermute | solution.py:293
  62.5 0.5 shard_map.78.refs_1_
  63.0 2.3 %collective-permute-done.10.refs_3_ = bf16[64,512]{1,0:T(8,128)(2,1)S(1)} collective-permute-done((bf16[64,512]{1,0:T(8,128)(2,1)S(1)}, bf16[64,512]{1,0:T(8,128)(2,1)S(1)}, u32[]{:S(2)}, u32[]{:S(2)}) %collective-permute-start.10) | collective-permute-done | bytes 65568 | tf_op jit(solution)/shard_map/ppermute | solution.py:293
  65.3 1.0 %collective-permute-done.9.refs_0_ = f32[64,256]{1,0:T(8,128)S(1)} collective-permute-done((f32[64,256]{1,0:T(8,128)S(1)}, f32[64,256]{1,0:T(8,128)S(1)}, u32[]{:S(2)}, u32[]{:S(2)}) %collective-permute-start.9) | collective-permute-done | bytes 65568 | tf_op jit(solution)/shard_map/ppermute | solution.py:293
  66.3 1.4 %shard_map.79 = bf16[256,512]{1,0:T(8,128)(2,1)} custom-call(s32[8,256]{1,0:T(8,128)S(1)} %shard_map.73.refs_0_.row_steps, f32[64,256]{1,0:T(8,128)S(1)} %collective-permute-done.9.refs_0_, f32[256,512]{1,0:T(8,128)S(1)} %shard_map.78.refs_1_, bf16[192,512]{1,0:T(8,128)(2,1)S(1)} %collective-permute-done.5.refs_2_, ...), custom_call_target="tpu_custom_call" | custom-call | tf_op jit(solution)/shard_map/pallas_call | solution.py:254
  (8 shorter events, 0.0 us)
Async XLA Ops:
  0.0 3.6 %copy-start = (bf16[256,4096]{1,0:T(8,128)(2,1)S(1)}, bf16[256,4096]{1,0:T(8,128)(2,1)}, u32[]{:S(2)}) copy-start(bf16[256,4096]{1,0:T(8,128)(2,1)} %refs_3_) | copy-start | bytes 6291460
  3.5 46.3 %copy-start.2 = (s32[8,8]{1,0:T(8,128)S(1)}, s32[8,8]{1,0:T(8,128)}, u32[]{:S(2)}) copy-start(s32[8,8]{1,0:T(8,128)} %fetch_ref.3) | copy-start | bytes 772
  3.5 46.3 %copy-start.3 = (s32[32]{0:T(128)S(1)}, s32[32]{0:T(128)}, u32[]{:S(2)}) copy-start(s32[32]{0:T(128)} %home_ref.3) | copy-start | bytes 388
  3.5 46.3 %copy-start.4 = (s32[1,8]{1,0:T(1,128)S(1)}, s32[1,8]{1,0:T(1,128)}, u32[]{:S(2)}) copy-start(s32[1,8]{1,0:T(1,128)} %lengths_ref.1) | copy-start | bytes 100
  3.6 55.3 %collective-permute-start.6 = (bf16[256,4096]{1,0:T(8,128)(2,1)S(1)}, bf16[256,4096]{1,0:T(8,128)(2,1)S(1)}, u32[]{:S(2)}, u32[]{:S(2)}) collective-permute-start(bf16[256,4096]{1,0:T(8,128)(2,1)S(1)} %copy-done), channel_id=1, source_target_pairs={{0,16},{16,0},{1,17},{17,1},{2,18},{18,2},{3,19},{19,3},{4,20},{20... | collective-permute-start | bytes 6291464 | tf_op jit(solution)/shard_map/ppermute | solution.py:293
  6.6 43.3 %collective-permute-start.1 = (bf16[64,4608]{1,0:T(8,128)(2,1)}, bf16[64,4608]{1,0:T(8,128)(2,1)S(1)}, u32[]{:S(2)}, u32[]{:S(2)}) collective-permute-start(bf16[64,4608]{1,0:T(8,128)(2,1)} %get-tuple-element.36), channel_id=1, source_target_pairs={{10,0},{8,2},{14,4},{12,6},{0,8},{2,10},{4,12},{6,14},{24,16},{26,... | collective-permute-start | bytes 1769480 | tf_op jit(solution)/shard_map/ppermute | solution.py:290
  9.2 41.4 %collective-permute-start.3 = (bf16[64,4608]{1,0:T(8,128)(2,1)}, bf16[64,4608]{1,0:T(8,128)(2,1)S(1)}, u32[]{:S(2)}, u32[]{:S(2)}) collective-permute-start(bf16[64,4608]{1,0:T(8,128)(2,1)} %get-tuple-element.39), channel_id=1, source_target_pairs={{6,0},{4,2},{2,4},{0,6},{14,8},{12,10},{10,12},{8,14},{20,16},{22,... | collective-permute-start | bytes 1769480 | tf_op jit(solution)/shard_map/ppermute | solution.py:290
  11.7 38.8 %collective-permute-start.4 = (bf16[64,4608]{1,0:T(8,128)(2,1)}, bf16[64,4608]{1,0:T(8,128)(2,1)S(1)}, u32[]{:S(2)}, u32[]{:S(2)}) collective-permute-start(bf16[64,4608]{1,0:T(8,128)(2,1)} %get-tuple-element.40), channel_id=1, source_target_pairs={{0,0},{2,2},{4,4},{6,6},{8,8},{10,10},{12,12},{14,14},{18,16},{16,... | collective-permute-start | bytes 1769480 | tf_op jit(solution)/shard_map/ppermute | solution.py:290
  13.4 40.1 %collective-permute-start.7 = (bf16[64,4608]{1,0:T(8,128)(2,1)}, bf16[64,4608]{1,0:T(8,128)(2,1)S(1)}, u32[]{:S(2)}, u32[]{:S(2)}) collective-permute-start(bf16[64,4608]{1,0:T(8,128)(2,1)} %get-tuple-element.44), channel_id=1, source_target_pairs={{14,0},{12,2},{10,4},{8,6},{4,8},{6,10},{0,12},{2,14},{28,16},{30,... | collective-permute-start | bytes 1769480 | tf_op jit(solution)/shard_map/ppermute | solution.py:290
  13.6 3.4 %copy-start.1 = (bf16[4096,1024]{1,0:T(8,128)(2,1)S(1)}, bf16[4096,1024]{1,0:T(8,128)(2,1)}, u32[]{:S(2)}) copy-start(bf16[4096,1024]{1,0:T(8,128)(2,1)} %weight_ref.1) | copy-start | bytes 25165828
  49.9 9.0 %collective-permute-start.2 = (f32[256,512]{1,0:T(8,128)S(1)}, f32[256,512]{1,0:T(8,128)S(1)}, u32[]{:S(2)}, u32[]{:S(2)}) collective-permute-start(f32[256,512]{1,0:T(8,128)S(1)} %get-tuple-element.38), channel_id=1, source_target_pairs={{0,1},{1,0},{2,3},{3,2},{4,5},{5,4},{6,7},{7,6},{8,9},{9,8},{10,11... | collective-permute-start | bytes 1572872 | tf_op jit(solution)/shard_map/ppermute | solution.py:296
  51.4 7.5 %collective-permute-start.5 = (bf16[192,512]{1,0:T(8,128)(2,1)S(1)}, bf16[192,512]{1,0:T(8,128)(2,1)S(1)}, u32[]{:S(2)}, u32[]{:S(2)}) collective-permute-start(bf16[192,512]{1,0:T(8,128)(2,1)S(1)} %get-tuple-element.43), channel_id=1, source_target_pairs={{0,16},{16,0},{1,17},{17,1},{2,18},{18,2},{3,19},{19,3},{4,20},{20... | collective-permute-start | bytes 589832 | tf_op jit(solution)/shard_map/ppermute | solution.py:293
  51.5 7.5 %collective-permute-start = (s32[8,256]{1,0:T(8,128)S(1)}, s32[8,256]{1,0:T(8,128)S(1)}, u32[]{:S(2)}, u32[]{:S(2)}) collective-permute-start(s32[8,256]{1,0:T(8,128)S(1)} %shard_map.73.refs_0_.row_steps), channel_id=1, source_target_pairs={{0,16},{16,0},{1,17},{17,1},{2,18},{18,2},{3,19},{19,3},{4,20},{20... | collective-permute-start | bytes 24584 | tf_op jit(solution)/shard_map/ppermute | solution.py:293
  60.3 1.4 %collective-permute-start.8 = (f32[64,512]{1,0:T(8,128)S(1)}, f32[64,512]{1,0:T(8,128)S(1)}, u32[]{:S(2)}, u32[]{:S(2)}) collective-permute-start(f32[64,512]{1,0:T(8,128)S(1)} %get-tuple-element.48.refs_0_), channel_id=1, source_target_pairs={{0,1},{1,0},{2,3},{3,2},{4,5},{5,4},{6,7},{7,6},{8,9},{9,8},{10,11... | collective-permute-start | bytes 393224 | tf_op jit(solution)/shard_map/ppermute | solution.py:296
  60.4 4.9 %collective-permute-start.10 = (bf16[64,512]{1,0:T(8,128)(2,1)S(1)}, bf16[64,512]{1,0:T(8,128)(2,1)S(1)}, u32[]{:S(2)}, u32[]{:S(2)}) collective-permute-start(bf16[64,512]{1,0:T(8,128)(2,1)S(1)} %get-tuple-element.52), channel_id=1, source_target_pairs={{0,16},{16,0},{1,17},{17,1},{2,18},{18,2},{3,19},{19,3},{4,20},{20... | collective-permute-start | bytes 196616 | tf_op jit(solution)/shard_map/ppermute | solution.py:293
  61.7 4.6 %collective-permute-start.9 = (f32[64,256]{1,0:T(8,128)S(1)}, f32[64,256]{1,0:T(8,128)S(1)}, u32[]{:S(2)}, u32[]{:S(2)}) collective-permute-start(f32[64,256]{1,0:T(8,128)S(1)} %slice_add_fusion), channel_id=1, source_target_pairs={{0,16},{16,0},{1,17},{17,1},{2,18},{18,2},{3,19},{19,3},{4,20},{20... | collective-permute-start | bytes 196616 | tf_op jit(solution)/shard_map/ppermute | solution.py:293

commit v26 on v25

--- a/solution.py
+++ b/solution.py
@@ -142,7 +142,7 @@
 def score(plan, groups, kept, columns, row_steps, tokens_of, panels, prior=None):
     count, depth = tokens_of[0].shape
     rank = panels[0].shape[0]
-    chunks = 4
+    chunks = 2
     prior = [] if prior is None else [prior]
     vmem = pl.BlockSpec(memory_space=pltpu.VMEM)
     outs = [(rank, len(plan) * count), (len(kept) * rank, columns)]
@@ -216,14 +216,16 @@
 
 def end_kernel(pieces, added, bases, replicas, row_steps, *refs):
     scores, base, refs = refs[:added], refs[added : added + bases], refs[added + bases :]
-    arrays, (out, held, sems) = refs[:-3], refs[-3:]
+    arrays, out = refs[:-1], refs[-1]
     count, columns = out.shape
     rank = scores[0].shape[0]
-    copies = []
-    for n, (at, row, _) in enumerate(pieces):
-        source = arrays[at].at[pl.ds(row, rank), pl.ds(arrays[at].shape[1] - columns, columns)]
-        copies.append(pltpu.make_async_copy(source, held.at[pl.ds(n * rank, rank)], sems.at[n]))
-        copies[-1].start()
+    expand = jnp.concatenate(
+        [
+            arrays[at][pl.ds(row, rank), pl.ds(arrays[at].shape[1] - columns, columns)]
+            for at, row, _ in pieces
+        ],
+        axis=0,
+    )
     shrink = scores[0][:, pl.ds(0, count)]
     for x in scores[1:]:
         shrink = shrink + x[:, pl.ds(0, count)]
@@ -234,13 +236,11 @@
     total = base[0][...]
     for x in base[1:]:
         total = total + x[...]
-    for copy in copies:
-        copy.wait()
     for term in (high, shrink - high):
         wide = jnp.concatenate([jnp.where(mask, term, 0.0) for mask in masks], axis=0)
         total = total + lax.dot_general(
             wide.astype(jnp.bfloat16),
-            held[...],
+            expand,
             (((0,), (0,)), ((), ())),
             preferred_element_type=jnp.float32,
         )
@@ -249,18 +249,12 @@
 
 def end(pieces, row_steps, scores, base, arrays, kind, cost):
     count, columns = base[0].shape
-    rank = scores[0].shape[0]
     vmem = pl.BlockSpec(memory_space=pltpu.VMEM)
     return pl.pallas_call(
         functools.partial(end_kernel, pieces, len(scores), len(base), lax.axis_size("rep")),
         out_shape=jax.ShapeDtypeStruct((count, columns), kind),
-        in_specs=[vmem] * (1 + len(scores) + len(base))
-        + [pl.BlockSpec(memory_space=pl.ANY)] * len(arrays),
+        in_specs=[vmem] * (1 + len(scores) + len(base) + len(arrays)),
         out_specs=vmem,
-        scratch_shapes=[
-            pltpu.VMEM((len(pieces) * rank, columns), jnp.bfloat16),
-            pltpu.SemaphoreType.DMA((len(pieces),)),
-        ],
         compiler_params=pltpu.CompilerParams(vmem_limit_bytes=16 << 20),
         cost_estimate=pl.CostEstimate(flops=0, bytes_accessed=cost, transcendentals=0),
     )(row_steps, *scores, *base, *arrays)

time: 68 us -> 67.6 us (level)
  no operation moved by 1% of the time
where the time goes in v26:
time: 67.6 us; the launch traced here: 67.3 us
  waiting for transfers between devices  38.8 us (57%)
  starting transfers between devices  13.3 us (20%)
  Pallas kernels  11.6 us (17%)
  local copies, waits for them, and re-layouts  3.4 us (5%)
    ppermute x4, waiting for transfers between devices, hop(): return lax.ppermute(x, ('parts', 'rep'), pairs)  29 us
    ppermute x5, waiting for transfers between devices, shift_parts(): lax.ppermute(x, 'parts', [(i, (i + shift) % parts) for i in range(parts)])  8.85 us
    ppermute x4, starting transfers between devices, hop(): return lax.ppermute(x, ('parts', 'rep'), pairs)  7 us
    ppermute x5, starting transfers between devices, shift_parts(): lax.ppermute(x, 'parts', [(i, (i + shift) % parts) for i in range(parts)])  6.25 us
    pallas_call x1, Pallas kernels, base_terms(): pl.pallas_call(functools.partial(base_kernel, chunks), out_shape=[jax.Sha...  3.94 us
    pallas_call x1, Pallas kernels, pack(): pl.pallas_call(functools.partial(pack_kernel, groups), out_shape=[jax.Sha...  3.51 us
    unnamed x10, local copies, waits for them, and re-layouts  3.4 us
    pallas_call x2, Pallas kernels, score(): pl.pallas_call(functools.partial(score_kernel, plan, groups, kept, chunks...  2.14 us
  transfers between devices with their start and end apart: 11, of which 6 were waited for; matrix products, arithmetic and copies ran while one was open for 0% of the time, Pallas kernels for 9%

profile of v26, /device:TPU:0, one launch (start us, length us, event | category | flops | bytes accessed | tf_op | source)
XLA Modules:
  0.0 67.3 jit_solution(15511165299121764654)
XLA Ops:
  0.0 3.5 %shard_map.74 = (bf16[64,4608]{1,0:T(8,128)(2,1)}, bf16[64,4608]{1,0:T(8,128)(2,1)}, bf16[64,4608]{1,0:T(8,128)(2,1)}, bf16[64,4608]{1,0:T(8,128)(2,1)}) custom-call(s32[32]{0:T(128)} %home_ref.3, s32[8,8]{1,0:T(8,128)} %fetch_ref.3, bf16[4,64,4096]{2,1,0:T(8,128)(2,1)} %bitcast.1, bf16[4,64,1024]{2,1,0:T(8,128)(2,1)} %expand_ref.1), custom_call_target="tpu_custom_call" | custom-call | tf_op jit(solution)/shard_map/pallas_call | solution.py:98
  3.5 0.0 copy-start.2
  3.5 0.0 copy-start.3
  3.5 0.0 copy-start.4
  3.6 3.0 %collective-permute-start.6 = (bf16[256,4096]{1,0:T(8,128)(2,1)S(1)}, bf16[256,4096]{1,0:T(8,128)(2,1)S(1)}, u32[]{:S(2)}, u32[]{:S(2)}) collective-permute-start(bf16[256,4096]{1,0:T(8,128)(2,1)S(1)} %copy-done), channel_id=1, source_target_pairs={{0,16},{16,0},{1,17},{17,1},{2,18},{18,2},{3,19},{19,3},{4,20},{20... | collective-permute-start | bytes 6291464 | tf_op jit(solution)/shard_map/ppermute | solution.py:287
  6.6 2.6 %collective-permute-start.1 = (bf16[64,4608]{1,0:T(8,128)(2,1)}, bf16[64,4608]{1,0:T(8,128)(2,1)S(1)}, u32[]{:S(2)}, u32[]{:S(2)}) collective-permute-start(bf16[64,4608]{1,0:T(8,128)(2,1)} %get-tuple-element.36), channel_id=1, source_target_pairs={{10,0},{8,2},{14,4},{12,6},{0,8},{2,10},{4,12},{6,14},{24,16},{26,... | collective-permute-start | bytes 1769480 | tf_op jit(solution)/shard_map/ppermute | solution.py:284
  9.2 2.5 %collective-permute-start.3 = (bf16[64,4608]{1,0:T(8,128)(2,1)}, bf16[64,4608]{1,0:T(8,128)(2,1)S(1)}, u32[]{:S(2)}, u32[]{:S(2)}) collective-permute-start(bf16[64,4608]{1,0:T(8,128)(2,1)} %get-tuple-element.39), channel_id=1, source_target_pairs={{6,0},{4,2},{2,4},{0,6},{14,8},{12,10},{10,12},{8,14},{20,16},{22,... | collective-permute-start | bytes 1769480 | tf_op jit(solution)/shard_map/ppermute | solution.py:284
  11.7 1.7 %collective-permute-start.4 = (bf16[64,4608]{1,0:T(8,128)(2,1)}, bf16[64,4608]{1,0:T(8,128)(2,1)S(1)}, u32[]{:S(2)}, u32[]{:S(2)}) collective-permute-start(bf16[64,4608]{1,0:T(8,128)(2,1)} %get-tuple-element.40), channel_id=1, source_target_pairs={{0,0},{2,2},{4,4},{6,6},{8,8},{10,10},{12,12},{14,14},{18,16},{16,... | collective-permute-start | bytes 1769480 | tf_op jit(solution)/shard_map/ppermute | solution.py:284
  13.4 0.2 collective-permute-start.7
  13.6 3.4 %copy-done.1 = bf16[4096,1024]{1,0:T(8,128)(2,1)S(1)} copy-done((bf16[4096,1024]{1,0:T(8,128)(2,1)S(1)}, bf16[4096,1024]{1,0:T(8,128)(2,1)}, u32[]{:S(2)}) %copy-start.1) | copy-done | bytes 8388632
  17.0 3.9 %shard_map.75 = (f32[256,512]{1,0:T(8,128)S(1)}, f32[256,512]{1,0:T(8,128)S(1)}) custom-call(bf16[256,4096]{1,0:T(8,128)(2,1)S(1)} %copy-done, bf16[4096,1024]{1,0:T(8,128)(2,1)S(1)} %copy-done.1), custom_call_target="tpu_custom_call" | custom-call | tf_op jit(solution)/shard_map/pallas_call | solution.py:201
  20.9 29.0 %collective-permute-done.1.refs_4_.refs_8_.refs_6_ = bf16[64,4608]{1,0:T(8,128)(2,1)S(1)} collective-permute-done((bf16[64,4608]{1,0:T(8,128)(2,1)}, bf16[64,4608]{1,0:T(8,128)(2,1)S(1)}, u32[]{:S(2)}, u32[]{:S(2)}) %collective-permute-start.1) | collective-permute-done | bytes 589856 | tf_op jit(solution)/shard_map/ppermute | solution.py:284
  49.9 0.0 collective-permute-start.2
  49.9 0.6 shard_map.73.refs_0_.row_steps
  50.5 0.0 collective-permute-done.3.refs_2_.refs_6_.refs_4_
  50.6 0.0 collective-permute-done.4.refs_3_.refs_7_.refs_5_
  50.6 0.8 %shard_map.76 = (f32[64,256]{1,0:T(8,128)S(1)}, bf16[192,512]{1,0:T(8,128)(2,1)S(1)}) custom-call(s32[8,256]{1,0:T(8,128)S(1)} %shard_map.73.refs_0_.row_steps, bf16[256,4096]{1,0:T(8,128)(2,1)S(1)} %copy-done, bf16[64,4608]{1,0:T(8,128)(2,1)S(1)} %collective-permute-done.3.refs_2_.refs_6_.refs_4_, ...), custom_call_target="tpu_custom_call" | custom-call | tf_op jit(solution)/shard_map/pallas_call | solution.py:151
  51.4 0.1 collective-permute-start.5
  51.5 2.0 %collective-permute-start = (s32[8,256]{1,0:T(8,128)S(1)}, s32[8,256]{1,0:T(8,128)S(1)}, u32[]{:S(2)}, u32[]{:S(2)}) collective-permute-start(s32[8,256]{1,0:T(8,128)S(1)} %shard_map.73.refs_0_.row_steps), channel_id=1, source_target_pairs={{0,16},{16,0},{1,17},{17,1},{2,18},{18,2},{3,19},{19,3},{4,20},{20... | collective-permute-start | bytes 24584 | tf_op jit(solution)/shard_map/ppermute | solution.py:287
  53.5 0.0 collective-permute-done.7.refs_5_.refs_7_
  53.5 5.4 %collective-permute-done.5.refs_2_ = bf16[192,512]{1,0:T(8,128)(2,1)S(1)} collective-permute-done((bf16[192,512]{1,0:T(8,128)(2,1)S(1)}, bf16[192,512]{1,0:T(8,128)(2,1)S(1)}, u32[]{:S(2)}, u32[]{:S(2)}) %collective-permute-start.5) | collective-permute-done | bytes 196640 | tf_op jit(solution)/shard_map/ppermute | solution.py:287
  58.9 0.0 collective-permute-done.6.refs_4_
  58.9 0.1 collective-permute-done.refs_1_
  59.0 1.3 %shard_map.77 = (f32[64,512]{1,0:T(8,128)S(1)}, bf16[64,512]{1,0:T(8,128)(2,1)S(1)}) custom-call(s32[8,256]{1,0:T(8,128)S(1)} %shard_map.73.refs_0_.row_steps, s32[8,256]{1,0:T(8,128)S(1)} %collective-permute-done.refs_1_, f32[64,256]{1,0:T(8,128)S(1)} %get-tuple-element.45.refs_2_, bf16[256,4096]{1,0:T(8,128)(2,1)S(1)} %copy-done, ...), custom_call_target="tpu_custom_call" | custom-call | tf_op jit(solution)/shard_map/pallas_call | solution.py:151
  60.3 0.1 collective-permute-start.8
  60.4 0.3 collective-permute-start.10
  60.7 1.0 %collective-permute-done.8.refs_1_ = f32[64,512]{1,0:T(8,128)S(1)} collective-permute-done((f32[64,512]{1,0:T(8,128)S(1)}, f32[64,512]{1,0:T(8,128)S(1)}, u32[]{:S(2)}, u32[]{:S(2)}) %collective-permute-start.8) | collective-permute-done | bytes 131104 | tf_op jit(solution)/shard_map/ppermute | solution.py:290
  61.7 0.8 %collective-permute-start.9 = (f32[64,256]{1,0:T(8,128)S(1)}, f32[64,256]{1,0:T(8,128)S(1)}, u32[]{:S(2)}, u32[]{:S(2)}) collective-permute-start(f32[64,256]{1,0:T(8,128)S(1)} %slice_add_fusion), channel_id=1, source_target_pairs={{0,16},{16,0},{1,17},{17,1},{2,18},{18,2},{3,19},{19,3},{4,20},{20... | collective-permute-start | bytes 196616 | tf_op jit(solution)/shard_map/ppermute | solution.py:287
  62.5 0.3 shard_map.78.refs_1_
  62.9 2.4 %collective-permute-done.10.refs_3_ = bf16[64,512]{1,0:T(8,128)(2,1)S(1)} collective-permute-done((bf16[64,512]{1,0:T(8,128)(2,1)S(1)}, bf16[64,512]{1,0:T(8,128)(2,1)S(1)}, u32[]{:S(2)}, u32[]{:S(2)}) %collective-permute-start.10) | collective-permute-done | bytes 65568 | tf_op jit(solution)/shard_map/ppermute | solution.py:287
  65.3 1.0 %collective-permute-done.9.refs_0_ = f32[64,256]{1,0:T(8,128)S(1)} collective-permute-done((f32[64,256]{1,0:T(8,128)S(1)}, f32[64,256]{1,0:T(8,128)S(1)}, u32[]{:S(2)}, u32[]{:S(2)}) %collective-permute-start.9) | collective-permute-done | bytes 65568 | tf_op jit(solution)/shard_map/ppermute | solution.py:287
  66.3 1.1 %shard_map.79 = bf16[256,512]{1,0:T(8,128)(2,1)} custom-call(s32[8,256]{1,0:T(8,128)S(1)} %shard_map.73.refs_0_.row_steps, f32[64,256]{1,0:T(8,128)S(1)} %collective-permute-done.9.refs_0_, f32[256,512]{1,0:T(8,128)S(1)} %shard_map.78.refs_1_, bf16[192,512]{1,0:T(8,128)(2,1)S(1)} %collective-permute-done.5.refs_2_, ...), custom_call_target="tpu_custom_call" | custom-call | tf_op jit(solution)/shard_map/pallas_call | solution.py:253
  (8 shorter events, 0.0 us)
Async XLA Ops:
  0.0 3.6 %copy-start = (bf16[256,4096]{1,0:T(8,128)(2,1)S(1)}, bf16[256,4096]{1,0:T(8,128)(2,1)}, u32[]{:S(2)}) copy-start(bf16[256,4096]{1,0:T(8,128)(2,1)} %refs_3_) | copy-start | bytes 6291460
  3.5 46.3 %copy-start.2 = (s32[8,8]{1,0:T(8,128)S(1)}, s32[8,8]{1,0:T(8,128)}, u32[]{:S(2)}) copy-start(s32[8,8]{1,0:T(8,128)} %fetch_ref.3) | copy-start | bytes 772
  3.5 46.3 %copy-start.3 = (s32[32]{0:T(128)S(1)}, s32[32]{0:T(128)}, u32[]{:S(2)}) copy-start(s32[32]{0:T(128)} %home_ref.3) | copy-start | bytes 388
  3.5 46.3 %copy-start.4 = (s32[1,8]{1,0:T(1,128)S(1)}, s32[1,8]{1,0:T(1,128)}, u32[]{:S(2)}) copy-start(s32[1,8]{1,0:T(1,128)} %lengths_ref.1) | copy-start | bytes 100
  3.6 55.3 %collective-permute-start.6 = (bf16[256,4096]{1,0:T(8,128)(2,1)S(1)}, bf16[256,4096]{1,0:T(8,128)(2,1)S(1)}, u32[]{:S(2)}, u32[]{:S(2)}) collective-permute-start(bf16[256,4096]{1,0:T(8,128)(2,1)S(1)} %copy-done), channel_id=1, source_target_pairs={{0,16},{16,0},{1,17},{17,1},{2,18},{18,2},{3,19},{19,3},{4,20},{20... | collective-permute-start | bytes 6291464 | tf_op jit(solution)/shard_map/ppermute | solution.py:287
  6.6 43.3 %collective-permute-start.1 = (bf16[64,4608]{1,0:T(8,128)(2,1)}, bf16[64,4608]{1,0:T(8,128)(2,1)S(1)}, u32[]{:S(2)}, u32[]{:S(2)}) collective-permute-start(bf16[64,4608]{1,0:T(8,128)(2,1)} %get-tuple-element.36), channel_id=1, source_target_pairs={{10,0},{8,2},{14,4},{12,6},{0,8},{2,10},{4,12},{6,14},{24,16},{26,... | collective-permute-start | bytes 1769480 | tf_op jit(solution)/shard_map/ppermute | solution.py:284
  9.2 41.4 %collective-permute-start.3 = (bf16[64,4608]{1,0:T(8,128)(2,1)}, bf16[64,4608]{1,0:T(8,128)(2,1)S(1)}, u32[]{:S(2)}, u32[]{:S(2)}) collective-permute-start(bf16[64,4608]{1,0:T(8,128)(2,1)} %get-tuple-element.39), channel_id=1, source_target_pairs={{6,0},{4,2},{2,4},{0,6},{14,8},{12,10},{10,12},{8,14},{20,16},{22,... | collective-permute-start | bytes 1769480 | tf_op jit(solution)/shard_map/ppermute | solution.py:284
  11.7 38.9 %collective-permute-start.4 = (bf16[64,4608]{1,0:T(8,128)(2,1)}, bf16[64,4608]{1,0:T(8,128)(2,1)S(1)}, u32[]{:S(2)}, u32[]{:S(2)}) collective-permute-start(bf16[64,4608]{1,0:T(8,128)(2,1)} %get-tuple-element.40), channel_id=1, source_target_pairs={{0,0},{2,2},{4,4},{6,6},{8,8},{10,10},{12,12},{14,14},{18,16},{16,... | collective-permute-start | bytes 1769480 | tf_op jit(solution)/shard_map/ppermute | solution.py:284
  13.4 40.1 %collective-permute-start.7 = (bf16[64,4608]{1,0:T(8,128)(2,1)}, bf16[64,4608]{1,0:T(8,128)(2,1)S(1)}, u32[]{:S(2)}, u32[]{:S(2)}) collective-permute-start(bf16[64,4608]{1,0:T(8,128)(2,1)} %get-tuple-element.44), channel_id=1, source_target_pairs={{14,0},{12,2},{10,4},{8,6},{4,8},{6,10},{0,12},{2,14},{28,16},{30,... | collective-permute-start | bytes 1769480 | tf_op jit(solution)/shard_map/ppermute | solution.py:284
  13.6 3.4 %copy-start.1 = (bf16[4096,1024]{1,0:T(8,128)(2,1)S(1)}, bf16[4096,1024]{1,0:T(8,128)(2,1)}, u32[]{:S(2)}) copy-start(bf16[4096,1024]{1,0:T(8,128)(2,1)} %weight_ref.1) | copy-start | bytes 25165828
  49.9 9.0 %collective-permute-start.2 = (f32[256,512]{1,0:T(8,128)S(1)}, f32[256,512]{1,0:T(8,128)S(1)}, u32[]{:S(2)}, u32[]{:S(2)}) collective-permute-start(f32[256,512]{1,0:T(8,128)S(1)} %get-tuple-element.38), channel_id=1, source_target_pairs={{0,1},{1,0},{2,3},{3,2},{4,5},{5,4},{6,7},{7,6},{8,9},{9,8},{10,11... | collective-permute-start | bytes 1572872 | tf_op jit(solution)/shard_map/ppermute | solution.py:290
  51.4 7.5 %collective-permute-start.5 = (bf16[192,512]{1,0:T(8,128)(2,1)S(1)}, bf16[192,512]{1,0:T(8,128)(2,1)S(1)}, u32[]{:S(2)}, u32[]{:S(2)}) collective-permute-start(bf16[192,512]{1,0:T(8,128)(2,1)S(1)} %get-tuple-element.43), channel_id=1, source_target_pairs={{0,16},{16,0},{1,17},{17,1},{2,18},{18,2},{3,19},{19,3},{4,20},{20... | collective-permute-start | bytes 589832 | tf_op jit(solution)/shard_map/ppermute | solution.py:287
  51.5 7.5 %collective-permute-start = (s32[8,256]{1,0:T(8,128)S(1)}, s32[8,256]{1,0:T(8,128)S(1)}, u32[]{:S(2)}, u32[]{:S(2)}) collective-permute-start(s32[8,256]{1,0:T(8,128)S(1)} %shard_map.73.refs_0_.row_steps), channel_id=1, source_target_pairs={{0,16},{16,0},{1,17},{17,1},{2,18},{18,2},{3,19},{19,3},{4,20},{20... | collective-permute-start | bytes 24584 | tf_op jit(solution)/shard_map/ppermute | solution.py:287
  60.3 1.4 %collective-permute-start.8 = (f32[64,512]{1,0:T(8,128)S(1)}, f32[64,512]{1,0:T(8,128)S(1)}, u32[]{:S(2)}, u32[]{:S(2)}) collective-permute-start(f32[64,512]{1,0:T(8,128)S(1)} %get-tuple-element.48.refs_0_), channel_id=1, source_target_pairs={{0,1},{1,0},{2,3},{3,2},{4,5},{5,4},{6,7},{7,6},{8,9},{9,8},{10,11... | collective-permute-start | bytes 393224 | tf_op jit(solution)/shard_map/ppermute | solution.py:290
  60.4 4.9 %collective-permute-start.10 = (bf16[64,512]{1,0:T(8,128)(2,1)S(1)}, bf16[64,512]{1,0:T(8,128)(2,1)S(1)}, u32[]{:S(2)}, u32[]{:S(2)}) collective-permute-start(bf16[64,512]{1,0:T(8,128)(2,1)S(1)} %get-tuple-element.52), channel_id=1, source_target_pairs={{0,16},{16,0},{1,17},{17,1},{2,18},{18,2},{3,19},{19,3},{4,20},{20... | collective-permute-start | bytes 196616 | tf_op jit(solution)/shard_map/ppermute | solution.py:287
  61.7 4.6 %collective-permute-start.9 = (f32[64,256]{1,0:T(8,128)S(1)}, f32[64,256]{1,0:T(8,128)S(1)}, u32[]{:S(2)}, u32[]{:S(2)}) collective-permute-start(f32[64,256]{1,0:T(8,128)S(1)} %slice_add_fusion), channel_id=1, source_target_pairs={{0,16},{16,0},{1,17},{17,1},{2,18},{18,2},{3,19},{19,3},{4,20},{20... | collective-permute-start | bytes 196616 | tf_op jit(solution)/shard_map/ppermute | solution.py:287

commit v27 on v26

--- a/solution.py
+++ b/solution.py
@@ -142,7 +142,7 @@
 def score(plan, groups, kept, columns, row_steps, tokens_of, panels, prior=None):
     count, depth = tokens_of[0].shape
     rank = panels[0].shape[0]
-    chunks = 2
+    chunks = 1
     prior = [] if prior is None else [prior]
     vmem = pl.BlockSpec(memory_space=pltpu.VMEM)
     outs = [(rank, len(plan) * count), (len(kept) * rank, columns)]

time: 67.6 us -> 67.6 us (level)
  no operation moved by 1% of the time
where the time goes in v27:
time: 67.6 us; the launch traced here: 67.3 us
  waiting for transfers between devices  38.8 us (57%)
  starting transfers between devices  13.3 us (20%)
  Pallas kernels  11.7 us (17%)
  local copies, waits for them, and re-layouts  3.4 us (5%)
    ppermute x4, waiting for transfers between devices, hop(): return lax.ppermute(x, ('parts', 'rep'), pairs)  29 us
    ppermute x5, waiting for transfers between devices, shift_parts(): lax.ppermute(x, 'parts', [(i, (i + shift) % parts) for i in range(parts)])  8.85 us
    ppermute x4, starting transfers between devices, hop(): return lax.ppermute(x, ('parts', 'rep'), pairs)  7 us
    ppermute x5, starting transfers between devices, shift_parts(): lax.ppermute(x, 'parts', [(i, (i + shift) % parts) for i in range(parts)])  6.23 us
    pallas_call x1, Pallas kernels, base_terms(): pl.pallas_call(functools.partial(base_kernel, chunks), out_shape=[jax.Sha...  3.94 us
    pallas_call x1, Pallas kernels, pack(): pl.pallas_call(functools.partial(pack_kernel, groups), out_shape=[jax.Sha...  3.54 us
    unnamed x10, local copies, waits for them, and re-layouts  3.4 us
    pallas_call x2, Pallas kernels, score(): pl.pallas_call(functools.partial(score_kernel, plan, groups, kept, chunks...  2.14 us
  transfers between devices with their start and end apart: 11, of which 6 were waited for; matrix products, arithmetic and copies ran while one was open for 0% of the time, Pallas kernels for 9%

profile of v27, /device:TPU:0, one launch (start us, length us, event | category | flops | bytes accessed | tf_op | source)
XLA Modules:
  0.0 67.3 jit_solution(10797526174409853847)
XLA Ops:
  0.0 3.5 %shard_map.74 = (bf16[64,4608]{1,0:T(8,128)(2,1)}, bf16[64,4608]{1,0:T(8,128)(2,1)}, bf16[64,4608]{1,0:T(8,128)(2,1)}, bf16[64,4608]{1,0:T(8,128)(2,1)}) custom-call(s32[32]{0:T(128)} %home_ref.3, s32[8,8]{1,0:T(8,128)} %fetch_ref.3, bf16[4,64,4096]{2,1,0:T(8,128)(2,1)} %bitcast.1, bf16[4,64,1024]{2,1,0:T(8,128)(2,1)} %expand_ref.1), custom_call_target="tpu_custom_call" | custom-call | tf_op jit(solution)/shard_map/pallas_call | solution.py:98
  3.5 0.0 copy-start.2
  3.6 0.0 copy-start.3
  3.6 0.0 copy-start.4
  3.6 3.0 %collective-permute-start.6 = (bf16[256,4096]{1,0:T(8,128)(2,1)S(1)}, bf16[256,4096]{1,0:T(8,128)(2,1)S(1)}, u32[]{:S(2)}, u32[]{:S(2)}) collective-permute-start(bf16[256,4096]{1,0:T(8,128)(2,1)S(1)} %copy-done), channel_id=1, source_target_pairs={{0,16},{16,0},{1,17},{17,1},{2,18},{18,2},{3,19},{19,3},{4,20},{20... | collective-permute-start | bytes 6291464 | tf_op jit(solution)/shard_map/ppermute | solution.py:287
  6.6 2.6 %collective-permute-start.1 = (bf16[64,4608]{1,0:T(8,128)(2,1)}, bf16[64,4608]{1,0:T(8,128)(2,1)S(1)}, u32[]{:S(2)}, u32[]{:S(2)}) collective-permute-start(bf16[64,4608]{1,0:T(8,128)(2,1)} %get-tuple-element.36), channel_id=1, source_target_pairs={{10,0},{8,2},{14,4},{12,6},{0,8},{2,10},{4,12},{6,14},{24,16},{26,... | collective-permute-start | bytes 1769480 | tf_op jit(solution)/shard_map/ppermute | solution.py:284
  9.2 2.5 %collective-permute-start.3 = (bf16[64,4608]{1,0:T(8,128)(2,1)}, bf16[64,4608]{1,0:T(8,128)(2,1)S(1)}, u32[]{:S(2)}, u32[]{:S(2)}) collective-permute-start(bf16[64,4608]{1,0:T(8,128)(2,1)} %get-tuple-element.39), channel_id=1, source_target_pairs={{6,0},{4,2},{2,4},{0,6},{14,8},{12,10},{10,12},{8,14},{20,16},{22,... | collective-permute-start | bytes 1769480 | tf_op jit(solution)/shard_map/ppermute | solution.py:284
  11.7 1.7 %collective-permute-start.4 = (bf16[64,4608]{1,0:T(8,128)(2,1)}, bf16[64,4608]{1,0:T(8,128)(2,1)S(1)}, u32[]{:S(2)}, u32[]{:S(2)}) collective-permute-start(bf16[64,4608]{1,0:T(8,128)(2,1)} %get-tuple-element.40), channel_id=1, source_target_pairs={{0,0},{2,2},{4,4},{6,6},{8,8},{10,10},{12,12},{14,14},{18,16},{16,... | collective-permute-start | bytes 1769480 | tf_op jit(solution)/shard_map/ppermute | solution.py:284
  13.4 0.2 collective-permute-start.7
  13.6 3.4 %copy-done.1 = bf16[4096,1024]{1,0:T(8,128)(2,1)S(1)} copy-done((bf16[4096,1024]{1,0:T(8,128)(2,1)S(1)}, bf16[4096,1024]{1,0:T(8,128)(2,1)}, u32[]{:S(2)}) %copy-start.1) | copy-done | bytes 8388632
  17.0 3.9 %shard_map.75 = (f32[256,512]{1,0:T(8,128)S(1)}, f32[256,512]{1,0:T(8,128)S(1)}) custom-call(bf16[256,4096]{1,0:T(8,128)(2,1)S(1)} %copy-done, bf16[4096,1024]{1,0:T(8,128)(2,1)S(1)} %copy-done.1), custom_call_target="tpu_custom_call" | custom-call | tf_op jit(solution)/shard_map/pallas_call | solution.py:201
  20.9 29.0 %collective-permute-done.1.refs_4_.refs_8_.refs_6_ = bf16[64,4608]{1,0:T(8,128)(2,1)S(1)} collective-permute-done((bf16[64,4608]{1,0:T(8,128)(2,1)}, bf16[64,4608]{1,0:T(8,128)(2,1)S(1)}, u32[]{:S(2)}, u32[]{:S(2)}) %collective-permute-start.1) | collective-permute-done | bytes 589856 | tf_op jit(solution)/shard_map/ppermute | solution.py:284
  49.9 0.0 collective-permute-start.2
  49.9 0.6 shard_map.73.refs_0_.row_steps
  50.5 0.0 collective-permute-done.3.refs_2_.refs_6_.refs_4_
  50.6 0.8 %shard_map.76 = (f32[64,256]{1,0:T(8,128)S(1)}, bf16[192,512]{1,0:T(8,128)(2,1)S(1)}) custom-call(s32[8,256]{1,0:T(8,128)S(1)} %shard_map.73.refs_0_.row_steps, bf16[256,4096]{1,0:T(8,128)(2,1)S(1)} %copy-done, bf16[64,4608]{1,0:T(8,128)(2,1)S(1)} %collective-permute-done.3.refs_2_.refs_6_.refs_4_, ...), custom_call_target="tpu_custom_call" | custom-call | tf_op jit(solution)/shard_map/pallas_call | solution.py:151
  51.4 0.1 collective-permute-start.5
  51.5 2.0 %collective-permute-start = (s32[8,256]{1,0:T(8,128)S(1)}, s32[8,256]{1,0:T(8,128)S(1)}, u32[]{:S(2)}, u32[]{:S(2)}) collective-permute-start(s32[8,256]{1,0:T(8,128)S(1)} %shard_map.73.refs_0_.row_steps), channel_id=1, source_target_pairs={{0,16},{16,0},{1,17},{17,1},{2,18},{18,2},{3,19},{19,3},{4,20},{20... | collective-permute-start | bytes 24584 | tf_op jit(solution)/shard_map/ppermute | solution.py:287
  53.5 0.0 collective-permute-done.7.refs_5_.refs_7_
  53.5 5.4 %collective-permute-done.5.refs_2_ = bf16[192,512]{1,0:T(8,128)(2,1)S(1)} collective-permute-done((bf16[192,512]{1,0:T(8,128)(2,1)S(1)}, bf16[192,512]{1,0:T(8,128)(2,1)S(1)}, u32[]{:S(2)}, u32[]{:S(2)}) %collective-permute-start.5) | collective-permute-done | bytes 196640 | tf_op jit(solution)/shard_map/ppermute | solution.py:287
  58.9 0.0 collective-permute-done.2.refs_3_
  58.9 0.0 collective-permute-done.6.refs_4_
  58.9 0.1 collective-permute-done.refs_1_
  59.0 1.3 %shard_map.77 = (f32[64,512]{1,0:T(8,128)S(1)}, bf16[64,512]{1,0:T(8,128)(2,1)S(1)}) custom-call(s32[8,256]{1,0:T(8,128)S(1)} %shard_map.73.refs_0_.row_steps, s32[8,256]{1,0:T(8,128)S(1)} %collective-permute-done.refs_1_, f32[64,256]{1,0:T(8,128)S(1)} %get-tuple-element.45.refs_2_, bf16[256,4096]{1,0:T(8,128)(2,1)S(1)} %copy-done, ...), custom_call_target="tpu_custom_call" | custom-call | tf_op jit(solution)/shard_map/pallas_call | solution.py:151
  60.3 0.1 collective-permute-start.8
  60.4 0.3 collective-permute-start.10
  60.7 1.0 %collective-permute-done.8.refs_1_ = f32[64,512]{1,0:T(8,128)S(1)} collective-permute-done((f32[64,512]{1,0:T(8,128)S(1)}, f32[64,512]{1,0:T(8,128)S(1)}, u32[]{:S(2)}, u32[]{:S(2)}) %collective-permute-start.8) | collective-permute-done | bytes 131104 | tf_op jit(solution)/shard_map/ppermute | solution.py:290
  61.7 0.8 %collective-permute-start.9 = (f32[64,256]{1,0:T(8,128)S(1)}, f32[64,256]{1,0:T(8,128)S(1)}, u32[]{:S(2)}, u32[]{:S(2)}) collective-permute-start(f32[64,256]{1,0:T(8,128)S(1)} %slice_add_fusion), channel_id=1, source_target_pairs={{0,16},{16,0},{1,17},{17,1},{2,18},{18,2},{3,19},{19,3},{4,20},{20... | collective-permute-start | bytes 196616 | tf_op jit(solution)/shard_map/ppermute | solution.py:287
  62.5 0.3 shard_map.78.refs_1_
  62.9 2.4 %collective-permute-done.10.refs_3_ = bf16[64,512]{1,0:T(8,128)(2,1)S(1)} collective-permute-done((bf16[64,512]{1,0:T(8,128)(2,1)S(1)}, bf16[64,512]{1,0:T(8,128)(2,1)S(1)}, u32[]{:S(2)}, u32[]{:S(2)}) %collective-permute-start.10) | collective-permute-done | bytes 65568 | tf_op jit(solution)/shard_map/ppermute | solution.py:287
  65.3 1.0 %collective-permute-done.9.refs_0_ = f32[64,256]{1,0:T(8,128)S(1)} collective-permute-done((f32[64,256]{1,0:T(8,128)S(1)}, f32[64,256]{1,0:T(8,128)S(1)}, u32[]{:S(2)}, u32[]{:S(2)}) %collective-permute-start.9) | collective-permute-done | bytes 65568 | tf_op jit(solution)/shard_map/ppermute | solution.py:287
  66.3 1.1 %shard_map.79 = bf16[256,512]{1,0:T(8,128)(2,1)} custom-call(s32[8,256]{1,0:T(8,128)S(1)} %shard_map.73.refs_0_.row_steps, f32[64,256]{1,0:T(8,128)S(1)} %collective-permute-done.9.refs_0_, f32[256,512]{1,0:T(8,128)S(1)} %shard_map.78.refs_1_, bf16[192,512]{1,0:T(8,128)(2,1)S(1)} %collective-permute-done.5.refs_2_, ...), custom_call_target="tpu_custom_call" | custom-call | tf_op jit(solution)/shard_map/pallas_call | solution.py:253
  (8 shorter events, 0.0 us)
Async XLA Ops:
  0.0 3.6 %copy-start = (bf16[256,4096]{1,0:T(8,128)(2,1)S(1)}, bf16[256,4096]{1,0:T(8,128)(2,1)}, u32[]{:S(2)}) copy-start(bf16[256,4096]{1,0:T(8,128)(2,1)} %refs_3_) | copy-start | bytes 6291460
  3.5 46.3 %copy-start.2 = (s32[8,8]{1,0:T(8,128)S(1)}, s32[8,8]{1,0:T(8,128)}, u32[]{:S(2)}) copy-start(s32[8,8]{1,0:T(8,128)} %fetch_ref.3) | copy-start | bytes 772
  3.6 46.3 %copy-start.3 = (s32[32]{0:T(128)S(1)}, s32[32]{0:T(128)}, u32[]{:S(2)}) copy-start(s32[32]{0:T(128)} %home_ref.3) | copy-start | bytes 388
  3.6 46.3 %copy-start.4 = (s32[1,8]{1,0:T(1,128)S(1)}, s32[1,8]{1,0:T(1,128)}, u32[]{:S(2)}) copy-start(s32[1,8]{1,0:T(1,128)} %lengths_ref.1) | copy-start | bytes 100
  3.6 55.3 %collective-permute-start.6 = (bf16[256,4096]{1,0:T(8,128)(2,1)S(1)}, bf16[256,4096]{1,0:T(8,128)(2,1)S(1)}, u32[]{:S(2)}, u32[]{:S(2)}) collective-permute-start(bf16[256,4096]{1,0:T(8,128)(2,1)S(1)} %copy-done), channel_id=1, source_target_pairs={{0,16},{16,0},{1,17},{17,1},{2,18},{18,2},{3,19},{19,3},{4,20},{20... | collective-permute-start | bytes 6291464 | tf_op jit(solution)/shard_map/ppermute | solution.py:287
  6.6 43.3 %collective-permute-start.1 = (bf16[64,4608]{1,0:T(8,128)(2,1)}, bf16[64,4608]{1,0:T(8,128)(2,1)S(1)}, u32[]{:S(2)}, u32[]{:S(2)}) collective-permute-start(bf16[64,4608]{1,0:T(8,128)(2,1)} %get-tuple-element.36), channel_id=1, source_target_pairs={{10,0},{8,2},{14,4},{12,6},{0,8},{2,10},{4,12},{6,14},{24,16},{26,... | collective-permute-start | bytes 1769480 | tf_op jit(solution)/shard_map/ppermute | solution.py:284
  9.2 41.4 %collective-permute-start.3 = (bf16[64,4608]{1,0:T(8,128)(2,1)}, bf16[64,4608]{1,0:T(8,128)(2,1)S(1)}, u32[]{:S(2)}, u32[]{:S(2)}) collective-permute-start(bf16[64,4608]{1,0:T(8,128)(2,1)} %get-tuple-element.39), channel_id=1, source_target_pairs={{6,0},{4,2},{2,4},{0,6},{14,8},{12,10},{10,12},{8,14},{20,16},{22,... | collective-permute-start | bytes 1769480 | tf_op jit(solution)/shard_map/ppermute | solution.py:284
  11.7 38.9 %collective-permute-start.4 = (bf16[64,4608]{1,0:T(8,128)(2,1)}, bf16[64,4608]{1,0:T(8,128)(2,1)S(1)}, u32[]{:S(2)}, u32[]{:S(2)}) collective-permute-start(bf16[64,4608]{1,0:T(8,128)(2,1)} %get-tuple-element.40), channel_id=1, source_target_pairs={{0,0},{2,2},{4,4},{6,6},{8,8},{10,10},{12,12},{14,14},{18,16},{16,... | collective-permute-start | bytes 1769480 | tf_op jit(solution)/shard_map/ppermute | solution.py:284
  13.4 40.1 %collective-permute-start.7 = (bf16[64,4608]{1,0:T(8,128)(2,1)}, bf16[64,4608]{1,0:T(8,128)(2,1)S(1)}, u32[]{:S(2)}, u32[]{:S(2)}) collective-permute-start(bf16[64,4608]{1,0:T(8,128)(2,1)} %get-tuple-element.44), channel_id=1, source_target_pairs={{14,0},{12,2},{10,4},{8,6},{4,8},{6,10},{0,12},{2,14},{28,16},{30,... | collective-permute-start | bytes 1769480 | tf_op jit(solution)/shard_map/ppermute | solution.py:284
  13.6 3.4 %copy-start.1 = (bf16[4096,1024]{1,0:T(8,128)(2,1)S(1)}, bf16[4096,1024]{1,0:T(8,128)(2,1)}, u32[]{:S(2)}) copy-start(bf16[4096,1024]{1,0:T(8,128)(2,1)} %weight_ref.1) | copy-start | bytes 25165828
  49.9 9.0 %collective-permute-start.2 = (f32[256,512]{1,0:T(8,128)S(1)}, f32[256,512]{1,0:T(8,128)S(1)}, u32[]{:S(2)}, u32[]{:S(2)}) collective-permute-start(f32[256,512]{1,0:T(8,128)S(1)} %get-tuple-element.38), channel_id=1, source_target_pairs={{0,1},{1,0},{2,3},{3,2},{4,5},{5,4},{6,7},{7,6},{8,9},{9,8},{10,11... | collective-permute-start | bytes 1572872 | tf_op jit(solution)/shard_map/ppermute | solution.py:290
  51.4 7.5 %collective-permute-start.5 = (bf16[192,512]{1,0:T(8,128)(2,1)S(1)}, bf16[192,512]{1,0:T(8,128)(2,1)S(1)}, u32[]{:S(2)}, u32[]{:S(2)}) collective-permute-start(bf16[192,512]{1,0:T(8,128)(2,1)S(1)} %get-tuple-element.43), channel_id=1, source_target_pairs={{0,16},{16,0},{1,17},{17,1},{2,18},{18,2},{3,19},{19,3},{4,20},{20... | collective-permute-start | bytes 589832 | tf_op jit(solution)/shard_map/ppermute | solution.py:287
  51.5 7.5 %collective-permute-start = (s32[8,256]{1,0:T(8,128)S(1)}, s32[8,256]{1,0:T(8,128)S(1)}, u32[]{:S(2)}, u32[]{:S(2)}) collective-permute-start(s32[8,256]{1,0:T(8,128)S(1)} %shard_map.73.refs_0_.row_steps), channel_id=1, source_target_pairs={{0,16},{16,0},{1,17},{17,1},{2,18},{18,2},{3,19},{19,3},{4,20},{20... | collective-permute-start | bytes 24584 | tf_op jit(solution)/shard_map/ppermute | solution.py:287
  60.3 1.4 %collective-permute-start.8 = (f32[64,512]{1,0:T(8,128)S(1)}, f32[64,512]{1,0:T(8,128)S(1)}, u32[]{:S(2)}, u32[]{:S(2)}) collective-permute-start(f32[64,512]{1,0:T(8,128)S(1)} %get-tuple-element.48.refs_0_), channel_id=1, source_target_pairs={{0,1},{1,0},{2,3},{3,2},{4,5},{5,4},{6,7},{7,6},{8,9},{9,8},{10,11... | collective-permute-start | bytes 393224 | tf_op jit(solution)/shard_map/ppermute | solution.py:290
  60.4 4.9 %collective-permute-start.10 = (bf16[64,512]{1,0:T(8,128)(2,1)S(1)}, bf16[64,512]{1,0:T(8,128)(2,1)S(1)}, u32[]{:S(2)}, u32[]{:S(2)}) collective-permute-start(bf16[64,512]{1,0:T(8,128)(2,1)S(1)} %get-tuple-element.52), channel_id=1, source_target_pairs={{0,16},{16,0},{1,17},{17,1},{2,18},{18,2},{3,19},{19,3},{4,20},{20... | collective-permute-start | bytes 196616 | tf_op jit(solution)/shard_map/ppermute | solution.py:287
  61.7 4.6 %collective-permute-start.9 = (f32[64,256]{1,0:T(8,128)S(1)}, f32[64,256]{1,0:T(8,128)S(1)}, u32[]{:S(2)}, u32[]{:S(2)}) collective-permute-start(f32[64,256]{1,0:T(8,128)S(1)} %slice_add_fusion), channel_id=1, source_target_pairs={{0,16},{16,0},{1,17},{17,1},{2,18},{18,2},{3,19},{19,3},{4,20},{20... | collective-permute-start | bytes 196616 | tf_op jit(solution)/shard_map/ppermute | solution.py:287
